TPU v7x, 32 devices: a whole 2x2x4 slice. The times are simulated.
32 devices in a mesh: grp: 2 (over x), blk: 8 (over z, y), cls: 2 (over core).
Axes of the slice: x: 2, y: 2, z: 4, core: 2. Of those that a mesh axis runs over, the one named last changes fastest.
Arguments:
- particles: bfloat16 [32768, 8192], P(('grp', 'blk', 'cls')), parts along dimension 0, may hold values from -11 to 11
- significant: int32 [16, 32768], P(None, ('grp', 'blk', 'cls')), parts along dimension 1, may hold values from 0 to 511, as said below
- templates: bfloat16 [1024, 8192], P(('grp', 'blk')), parts along dimension 0, may hold values from -0.2 to 0.2
- template_class: int32 [1024], P(('grp', 'blk')), parts along dimension 0, may hold values from 0 to 7
- class_counts: int32 [16], P('grp'), parts along dimension 0, may hold values from 1024 to 4096
- inv_noise: float32 [8192], replicated, may hold values from 0.3 to 3
Outputs:
- loglik: float32 [32768], P(('grp', 'blk', 'cls')), parts along dimension 0
- class_avg: float32 [16, 8192], P(('grp', 'cls'), 'blk'), parts along dimension 0
There are 2 independent parts, one for each index of `grp`. A program takes and returns all parts, laid end to end along the dimension named above; an argument that names none is the same for every part. Nothing has to cross between parts.
Inputs may be any that keep to these rules, and one draw needn't show every extreme that they name: `significant`: the 16 templates of a particle are distinct; taking template ids around a circle of 512 from an offset of the particle's own, its k-th template lies in the k-th of 16 equal arcs.
All inputs are finite; a program needn't handle non-finite values.
Results may differ from a plain program's by a relative error of at most 0.0012.
Values may be sent and summed in bfloat16 or wider, within the bound.
No kernel may reach another device: no remote copies, remote signals or barrier semaphores. Data moves between devices by JAX's collectives and lax.ppermute only.
A program may use at most 128 MiB of HBM per device.

v0:
```python
import jax
import jax.numpy as jnp
from jax import lax
from jax.sharding import PartitionSpec as P


def score_block(state, piece, particles, significant, inv_noise, log_counts):
    run_max, run_sum, picked, picked_class = state
    tmpl_rows, tmpl_tags = piece
    row_count = tmpl_rows.shape[0]
    widened = tmpl_rows.astype(jnp.float32)
    weighted = (widened * inv_noise[None, :]).astype(jnp.bfloat16)
    energy = 0.5 * jnp.sum(inv_noise[None, :] * widened * widened, axis=1)
    tag_index = tmpl_tags.astype(jnp.int32)
    class_ids = jnp.arange(log_counts.shape[0], dtype=jnp.int32)
    prior = jnp.sum(
        jnp.where(tag_index[:, None] == class_ids[None, :], log_counts[None, :], jnp.float32(0.0)),
        axis=1,
    )
    scores = lax.dot_general(
        weighted, particles, (((1,), (1,)), ((), ())), preferred_element_type=jnp.float32
    )
    scores = scores - energy[:, None] + prior[:, None]
    new_max = jnp.maximum(run_max, jnp.max(scores, axis=0))
    run_sum = jnp.sum(jnp.exp(scores - new_max[None, :]), axis=0)
    tmpl_ids = jnp.arange(row_count, dtype=jnp.int32)
    matched = significant[:, None, :] == tmpl_ids[None, :, None]
    picked = jnp.sum(jnp.where(matched, scores[None, :, :], jnp.float32(0.0)), axis=1)
    picked_class = jnp.sum(jnp.where(matched, tag_index[None, :, None], jnp.int32(0)), axis=1)
    return (new_max, run_sum, picked, picked_class)


def body(particles, significant, templates, template_class, class_counts, inv_noise):
    per_device = particles.shape[0]
    log_counts = jnp.log(class_counts.astype(jnp.float32))
    starting = (
        jnp.full((per_device,), -1e30, jnp.float32),
        jnp.zeros((per_device,), jnp.float32),
        jnp.zeros(significant.shape, jnp.float32),
        jnp.zeros(significant.shape, jnp.int32),
    )
    class_tags = template_class.astype(jnp.bfloat16)
    state = score_block(
        starting,
        (
            lax.all_gather(templates, "blk", axis=0, tiled=True),
            lax.all_gather(class_tags, "blk", axis=0, tiled=True),
        ),
        particles,
        significant,
        inv_noise,
        log_counts,
    )
    run_max, run_sum, picked, picked_class = state
    loglik = run_max + jnp.log(run_sum)
    sig_max = jnp.max(picked, axis=0)
    sig_exp = jnp.exp(picked - sig_max[None, :])
    posterior = sig_exp / jnp.sum(sig_exp, axis=0)[None, :]
    classes = class_counts.shape[0]
    class_ids = jnp.arange(classes, dtype=jnp.int32)
    hits = picked_class[:, None, :] == class_ids[None, :, None]
    class_weights = jnp.sum(jnp.where(hits, posterior[:, None, :], jnp.float32(0.0)), axis=0)
    rounded = class_weights.astype(jnp.bfloat16)
    partial_sums = jnp.dot(rounded, particles, preferred_element_type=jnp.float32)
    partial_totals = jnp.sum(class_weights, axis=1)
    blocks = lax.axis_size("blk")
    owners = lax.axis_size("cls")
    per_owner = classes // owners
    half_sums, half_totals = (
        lax.psum_scatter(partial_sums, "cls", scatter_dimension=0, tiled=True),
        lax.psum_scatter(partial_totals, "cls", scatter_dimension=0, tiled=True),
    )
    repeated = jnp.broadcast_to(half_totals[:, None], (per_owner, blocks))
    owner_sums, column_totals = (
        lax.psum_scatter(half_sums, "blk", scatter_dimension=1, tiled=True),
        lax.psum_scatter(repeated, "blk", scatter_dimension=1, tiled=True),
    )
    owner_totals = column_totals[:, 0]
    own_counts = lax.dynamic_slice_in_dim(
        class_counts, lax.axis_index("cls") * per_owner, per_owner, 0
    )
    class_avg = owner_sums / (owner_totals + own_counts.astype(jnp.float32))[:, None]
    return (loglik, class_avg)


def solution(mesh):
    placed = (
        P(("grp", "blk", "cls"), None),
        P(None, ("grp", "blk", "cls")),
        P(("grp", "blk"), None),
        P(("grp", "blk")),
        P("grp"),
        P(),
    )
    return jax.shard_map(
        body,
        mesh=mesh,
        in_specs=placed,
        out_specs=(P(("grp", "blk", "cls")), P(("grp", "cls"), "blk")),
        check_vma=False,
    )
```

profile of v0, /device:TPU:0, one launch (start us, length us, event | category | flops | bytes accessed | tf_op | source)
XLA Modules:
  0.0 292.3 jit_solution(2283772560687802993)
XLA Ops:
  7.2 0.7 all-gather.2.cloned.1.call-update
  8.0 0.7 convert_element_type.23
  8.6 1.2 dynamic-slice.1
  9.8 1.3 fusion.9
  11.8 0.2 dynamic-update-slice
  12.1 23.7 %all-reduce = bf16[512]{0:T(512)(128)(2,1)S(1)} all-reduce(bf16[512]{0:T(512)(128)(2,1)S(1)} %dynamic-update-slice), channel_id=1, replica_groups=mesh['grp'=2,'blk'=8,'cls'=2] {'blk'}, use_global_device_ids=true, to_apply=%add | all-reduce | flops 512 | bytes 2048
  36.4 0.7 convert_log_fusion
  37.1 5.2 %select_reduce_fusion.1 = s32[16,1024]{1,0:T(8,128)S(1)} fusion(s32[512]{0:T(512)S(1)} %convert_element_type.24, s32[16,1024]{1,0:T(8,128)} %param.7), kind=kLoop, calls=%fused_computation.1 | loop fusion | flops 25149440 | bytes 133120 | tf_op jit(solution)/shard_map/reduce_sum | solution.py:29
  42.3 95.8 %all-gather.2.cloned.1.call-done = bf16[512,8192]{1,0:T(8,128)(2,1)} async-done(((bf16[64,8192]{1,0:T(8,128)(2,1)}), bf16[512,8192]{1,0:T(8,128)(2,1)}) %all-gather.2.cloned.1.call-update) | async-done | bytes 8388624 | tf_op jit(solution)/shard_map/all_gather | solution.py:46
  138.2 5.6 %fusion = f32[512]{0:T(512)S(1)} fusion(bf16[512,8192]{1,0:T(8,128)(2,1)} %all-gather.2.cloned.1.call-done, f32[8192]{0:T(1024)} %param.11), kind=kLoop, calls=%fused_computation.5 | loop fusion | flops 16776704 | bytes 8423424 | tf_op jit(solution)/shard_map/reduce_sum | solution.py:13
  143.8 15.4 %fusion.10 = (f32[1024]{0:T(1024)S(1)}, f32[512,1024]{1,0:T(8,128)S(1)}) fusion(f32[512]{0:T(512)S(1)} %select_reduce_fusion.4, f32[512]{0:T(512)S(1)} %broadcast_multiply_fusion, bf16[1024,8192]{1,0:T(8,128)(2,1)} %param.6, bf16[512,8192]{1,0:T(8,128)(2,1)} %all-gather.2.cloned.1.call-done, f32[8192]{0:T(1024)} %param.11), kind=kOutput, calls=%fused_computation.30 | convolution fusion | flops 8604089344 | bytes 27303936 | tf_op jit(solution)/shard_map/dot_general | solution.py:20
  159.2 5.0 %select_reduce_fusion = f32[16,1024]{1,0:T(8,128)S(1)} fusion(f32[512,1024]{1,0:T(8,128)S(1)} %get-tuple-element.7, s32[16,1024]{1,0:T(8,128)S(1)} %copy-done), kind=kLoop, calls=%fused_computation | loop fusion | flops 25149440 | bytes 2228224 | tf_op jit(solution)/shard_map/reduce_sum | solution.py:28
  164.4 0.3 select_reduce_fusion.2
  164.6 8.8 %fusion.11 = f32[8,8192]{1,0:T(8,128)} fusion(bf16[8,1024]{1,0:T(8,128)(2,1)S(1)} %get-tuple-element.3, bf16[1024,8192]{1,0:T(8,128)(2,1)} %param.6), kind=kOutput, calls=%fused_computation.31 | convolution fusion | flops 134217728 | bytes 17055744 | tf_op jit(solution)/shard_map/dot_general | solution.py:64
  173.4 2.5 all-reduce.2
  176.0 18.4 %all-reduce.3 = f32[4,8]{0,1:T(8,128)S(1)} all-reduce(f32[4,8]{0,1:T(8,128)S(1)} %broadcast_in_dim.84), channel_id=5, replica_groups=mesh['grp'=2,'blk'=8,'cls'=2] {'blk'}, use_global_device_ids=true, to_apply=%region_13.14.clone | all-reduce | flops 32 | bytes 256
  194.4 0.3 exponential_reduce_fusion
  194.8 1.0 constant_dynamic-slice_fusion.1
  195.8 2.6 copy.8
  198.4 0.7 fusion.8
  199.1 0.6 log_add_fusion
  199.7 84.1 %reduce-scatter.4.cloned.1.call-done = f32[1024,4]{1,0:T(8,128)} async-done(((f32[8192,4]{1,0:T(8,128)}), f32[1024,4]{1,0:T(8,128)}) %reduce-scatter.4.cloned.1.call-update) | async-done | bytes 16400
  283.8 1.2 copy.9
  285.1 0.7 broadcast_divide_fusion
  (20 shorter events, 0.4 us)
Async XLA Ops:
  7.2 131.0 %all-gather.2.cloned.1.call-start = ((), (), s32[]{:S(2)}) async-start(), calls=%async_computation.1 | async-start | bytes 9437184 | tf_op jit(solution)/shard_map/all_gather | solution.py:46
  7.9 186.9 %all-reduce.6.cloned.1.call-start = ((), (), s32[]{:S(2)}) async-start(), calls=%async_computation.3 | async-start | bytes 524288
  143.8 15.4 %copy-start = (s32[16,1024]{1,0:T(8,128)S(1)}, s32[16,1024]{1,0:T(8,128)}, u32[]{:S(2)}) copy-start(s32[16,1024]{1,0:T(8,128)} %param.7) | copy-start | bytes 196612
  164.3 34.2 %copy-start.1 = (s32[8]{0:T(128)S(1)}, s32[8]{0:T(128)}, u32[]{:S(2)}) copy-start(s32[8]{0:T(128)} %param.10) | copy-start | bytes 100
  173.4 110.4 %reduce-scatter.4.cloned.1.call-start = ((), (), s32[]{:S(2)}) async-start(), calls=%async_computation.2 | async-start | bytes 4718592
Sparse Core Ops, SparseCore 0:
  10.1 127.9 all-gather.1
  173.5 16.4 all-reduce.5
  198.5 85.2 reduce-scatter.3
where the time goes:
time: 293 us; the launch traced here: 292 us
  waiting for transfers between devices  181 us (62%)
  blocking collectives  44.6 us (15%)
  matrix products  24.1 us (8%)
  other arithmetic  20 us (7%)
  between operations  15.1 us (5%)
  local copies, waits for them, and re-layouts  7.7 us (3%)
    all_gather x1, waiting for transfers between devices, body(): lax.all_gather(templates, 'blk', axis=0, tiled=True)  95.8 us
    unnamed x5, waiting for transfers between devices  84.8 us
    unnamed x3, blocking collectives  44.6 us
    dot_general x1, matrix products, score_block(): lax.dot_general(weighted, particles, (((1,), (1,)), ((), ())), preferred_...  15.4 us
    dot_general x1, matrix products, body(): jnp.dot(rounded, particles, preferred_element_type=jnp.float32)  8.75 us
    unnamed x12, local copies, waits for them, and re-layouts  7.69 us
  transfers between devices with their start and end apart: 3, of which 2 were waited for; matrix products, arithmetic and copies ran while one was open for 4% of the time, Pallas kernels for 0%

commit v1 on v0

v1 whole, which is shorter than its diff:
```python
import functools

import jax
import jax.numpy as jnp
from jax import lax
from jax.experimental import pallas as pl
from jax.experimental.pallas import tpu as pltpu
from jax.sharding import PartitionSpec as P

LOWEST = -1e30
STEPS = 8
SUBS = 2
LANES = 128
STATE_ROWS = 8
VMEM_LIMIT = 48 * 1024 * 1024


def ring_order(blocks):
    if blocks <= 8:
        return list(range(0, blocks, 2)) + list(range(blocks - 1, 0, -2))
    return list(range(blocks))


def score_kernel(layout, base_ref, logs_ref, sig_ref, state_ref, noise_ref, part_ref, *rest):
    groups = []
    at = 0
    for subs in layout:
        groups.append((rest[at], rest[at + 1 : at + 1 + subs]))
        at += 1 + subs
    out_ref, acc, energy = rest[at:]
    step = pl.program_id(0)
    steps = pl.num_programs(0)

    @pl.when(step == 0)
    def _():
        acc[...] = jnp.zeros_like(acc)
        energy[...] = jnp.zeros_like(energy)

    def add(which):
        rows = [refs[which if len(refs) > 1 else 0][...] for _, refs in groups]
        widened = jnp.concatenate(rows, axis=0).astype(jnp.float32)
        product = widened * noise_ref[...]
        square = product * widened
        folded = square[:, :LANES]
        for lane in range(LANES, square.shape[1], LANES):
            folded = folded + square[:, lane : lane + LANES]
        energy[...] += folded
        acc[...] += lax.dot_general(
            product.astype(jnp.bfloat16),
            part_ref[...],
            (((1,), (1,)), ((), ())),
            preferred_element_type=jnp.float32,
        )

    most = max(layout)
    for which in range(most):
        pl.when(step * most // steps == which)(functools.partial(add, which))

    @pl.when(step == steps - 1)
    def _():
        classes = logs_ref.shape[0]
        tags = jnp.concatenate([ref[...] for ref, _ in groups], axis=0).astype(jnp.float32)
        row_ids = []
        for group, (ref, _) in enumerate(groups):
            row_ids.append(
                base_ref[group] + lax.broadcasted_iota(jnp.int32, (ref.shape[0], 1), 0)
            )
        ids = jnp.concatenate(row_ids, axis=0)
        prior = jnp.zeros_like(tags[:, :1])
        for tag in range(classes):
            prior = jnp.where(tags[:, :1] == tag, logs_ref[tag], prior)
        bias = prior - 0.5 * jnp.sum(energy[...], axis=1, keepdims=True)
        scores = acc[...] + bias
        old_max = state_ref[0:1, :]
        old_sum = state_ref[1:2, :]
        new_max = jnp.maximum(old_max, jnp.max(scores, axis=0, keepdims=True))
        new_sum = old_sum * jnp.exp(old_max - new_max) + jnp.sum(
            jnp.exp(scores - new_max), axis=0, keepdims=True
        )
        hit = sig_ref[0:1, :] == ids
        for pick in range(1, sig_ref.shape[0]):
            hit = hit | (sig_ref[pick : pick + 1, :] == ids)
        old_top = state_ref[2:3, :]
        new_top = jnp.maximum(
            old_top, jnp.max(jnp.where(hit, scores, LOWEST), axis=0, keepdims=True)
        )
        value = jnp.where(hit, jnp.exp(scores - new_top), 0.0)
        lane = lax.broadcasted_iota(jnp.int32, tags.shape, 1).astype(jnp.float32)
        onehot = jnp.transpose(jnp.where(tags == lane, 1.0, 0.0))[:classes, :].astype(jnp.bfloat16)
        weights = state_ref[STATE_ROWS:, :] * jnp.exp(old_top - new_top)
        left = value
        for _ in range(3):
            piece = left.astype(jnp.bfloat16)
            left = left - piece.astype(jnp.float32)
            weights = weights + jnp.dot(onehot, piece, preferred_element_type=jnp.float32)
        out_ref[0:1, :] = new_max
        out_ref[1:2, :] = new_sum
        out_ref[2:3, :] = new_top
        out_ref[3:STATE_ROWS, :] = jnp.zeros_like(out_ref[3:STATE_ROWS, :])
        out_ref[STATE_ROWS:, :] = weights


def score_groups(groups, bases, logs, significant, state, noise, particles):
    per_device, freqs = particles.shape
    width = freqs // STEPS
    specs = [
        pl.BlockSpec(memory_space=pltpu.SMEM),
        pl.BlockSpec(memory_space=pltpu.SMEM),
        pl.BlockSpec(significant.shape, lambda j: (0, 0)),
        pl.BlockSpec(state.shape, lambda j: (0, 0)),
        pl.BlockSpec((1, width), lambda j: (0, j)),
        pl.BlockSpec((per_device, width), lambda j: (0, j)),
    ]
    arrays = [bases, logs, significant, state, noise, particles]
    layout = []
    rows = 0
    for tags, column, parts in groups:
        height = parts[0].shape[0]
        rows += height
        layout.append(len(parts))
        specs.append(pl.BlockSpec((height, LANES), lambda j, column=column: (0, column)))
        arrays.append(tags)
        share = STEPS // len(parts)
        for index, part in enumerate(parts):
            specs.append(
                pl.BlockSpec(
                    (height, width),
                    lambda j, low=index * share, share=share: (
                        0,
                        jnp.clip(j - low, 0, share - 1),
                    ),
                )
            )
            arrays.append(part)
    return pl.pallas_call(
        functools.partial(score_kernel, tuple(layout)),
        grid=(STEPS,),
        in_specs=specs,
        out_specs=pl.BlockSpec(state.shape, lambda j: (0, 0)),
        out_shape=jax.ShapeDtypeStruct(state.shape, jnp.float32),
        scratch_shapes=[
            pltpu.VMEM((rows, per_device), jnp.float32),
            pltpu.VMEM((rows, LANES), jnp.float32),
        ],
        compiler_params=pltpu.CompilerParams(vmem_limit_bytes=VMEM_LIMIT),
        cost_estimate=pl.CostEstimate(
            flops=4 * 128 * per_device * freqs,
            bytes_accessed=2 * per_device * freqs,
            transcendentals=0,
        ),
    )(*arrays)


def sums_kernel(own_ref, state_ref, part_ref, loglik_ref, mine_ref, theirs_ref, rounded, totals):
    classes, per_owner = rounded.shape[0], mine_ref.shape[1]
    width = part_ref.shape[1]

    @pl.when(pl.program_id(0) == 0)
    def _():
        loglik_ref[...] = state_ref[0:1, :] + jnp.log(state_ref[1:2, :])
        weights = state_ref[STATE_ROWS:, :]
        weights = weights / jnp.sum(weights, axis=0, keepdims=True)
        turned = jnp.concatenate([weights[per_owner:], weights[:per_owner]], axis=0)
        weights = jnp.where(own_ref[0] == 0, weights, turned)
        rounded[...] = weights.astype(jnp.bfloat16)
        total = jnp.sum(weights, axis=1, keepdims=True)
        totals[...] = jnp.broadcast_to(total, totals.shape)

    sums = jnp.dot(rounded[...], part_ref[...], preferred_element_type=jnp.float32)
    mine_ref[0, :, :width] = sums[:per_owner]
    theirs_ref[0, :, :width] = sums[per_owner:classes]
    mine_ref[0, :, width:] = totals[:per_owner]
    theirs_ref[0, :, width:] = totals[per_owner:classes]


def class_sums(own, state, particles, blocks, classes, owners):
    per_device, freqs = particles.shape
    width = freqs // blocks
    per_owner = classes // owners
    piece = jax.ShapeDtypeStruct((blocks, per_owner, width + LANES), jnp.float32)
    piece_spec = pl.BlockSpec((1, per_owner, width + LANES), lambda j: (j, 0, 0))
    return pl.pallas_call(
        sums_kernel,
        grid=(blocks,),
        in_specs=[
            pl.BlockSpec(memory_space=pltpu.SMEM),
            pl.BlockSpec(state.shape, lambda j: (0, 0)),
            pl.BlockSpec((per_device, width), lambda j: (0, j)),
        ],
        out_specs=[pl.BlockSpec((1, per_device), lambda j: (0, 0)), piece_spec, piece_spec],
        out_shape=[jax.ShapeDtypeStruct((1, per_device), jnp.float32), piece, piece],
        scratch_shapes=[
            pltpu.VMEM((classes, per_device), jnp.bfloat16),
            pltpu.VMEM((classes, LANES), jnp.float32),
        ],
        compiler_params=pltpu.CompilerParams(vmem_limit_bytes=VMEM_LIMIT),
        cost_estimate=pl.CostEstimate(
            flops=2 * 128 * per_device * freqs,
            bytes_accessed=2 * per_device * freqs,
            transcendentals=0,
        ),
    )(own, state, particles)


def body(particles, significant, templates, template_class, class_counts, inv_noise):
    per_device, freqs = particles.shape
    height = templates.shape[0]
    classes = class_counts.shape[0]
    blocks = lax.axis_size("blk")
    owners = lax.axis_size("cls")
    half = height // owners
    order = ring_order(blocks)
    place = [order.index(block) for block in range(blocks)]
    block_id = lax.axis_index("blk")
    core = lax.axis_index("cls")
    at = jnp.asarray(place, jnp.int32)[block_id]
    order_table = jnp.asarray(order, jnp.int32)
    forward = [(order[i], order[(i + 1) % blocks]) for i in range(blocks)]
    backward = [(order[(i + 1) % blocks], order[i]) for i in range(blocks)]
    swap = [(i, owners - 1 - i) for i in range(owners)]

    noise = inv_noise[None, :]
    logs = jnp.log(class_counts.astype(jnp.float32))
    tags = jnp.broadcast_to(
        template_class.astype(jnp.bfloat16)[:, None], (height, LANES)
    )
    own_rows = lax.dynamic_slice_in_dim(templates, core * half, half, 0)
    own_tags = lax.dynamic_slice_in_dim(tags, core * half, half, 0)
    span = freqs // SUBS
    first = []
    for sub in range(SUBS):
        first.append(
            jnp.concatenate([own_rows[:, sub * span : (sub + 1) * span], own_tags], axis=1)
        )

    score = functools.partial(
        score_groups,
        logs=logs,
        significant=significant,
        noise=noise,
        particles=particles,
    )
    column = span // LANES

    state = jnp.concatenate(
        [
            jnp.full((1, per_device), LOWEST, jnp.float32),
            jnp.zeros((1, per_device), jnp.float32),
            jnp.full((1, per_device), LOWEST, jnp.float32),
            jnp.zeros((STATE_ROWS - 3 + classes, per_device), jnp.float32),
        ],
        axis=0,
    )
    last = blocks // 2
    held = {1: first, -1: first}
    for distance in range(last + 1):
        if distance == 0:
            groups = [(tags, 0, [templates])]
            bases = [block_id * height]
        else:
            groups, bases = [], []
            for way, pairs in ((1, forward), (-1, backward)):
                taken = list(range(SUBS))
                if distance == last:
                    taken = taken[: SUBS // 2] if way == 1 else taken[SUBS // 2 :]
                arrived = {sub: lax.ppermute(held[way][sub], "blk", pairs) for sub in taken}
                passed = {sub: lax.ppermute(arrived[sub], "cls", swap) for sub in taken}
                held[way] = arrived
                source = order_table[lax.rem(at - way * distance + blocks, blocks)]
                if distance == last and way == -1:
                    for sub in taken:
                        groups[0][2].append(arrived[sub])
                        groups[1][2].append(passed[sub])
                    continue
                parts = [arrived[sub] for sub in taken]
                others = [passed[sub] for sub in taken]
                groups.append((parts[0], column, parts))
                groups.append((others[0], column, others))
                bases.append(source * height + core * half)
                bases.append(source * height + (owners - 1 - core) * half)
        state = score(groups, jnp.stack(bases), state=state)

    loglik, mine, theirs = class_sums(
        core[None], state, particles, blocks, classes, owners
    )
    reduced = mine + lax.ppermute(theirs, "cls", swap)
    pieces = lax.all_to_all(reduced, "blk", split_axis=0, concat_axis=0, tiled=True)
    total = jnp.sum(pieces, axis=0)
    width = freqs // blocks
    per_owner = classes // owners
    counts = lax.dynamic_slice_in_dim(class_counts, core * per_owner, per_owner, 0)
    class_avg = total[:, :width] / (total[:, width] + counts.astype(jnp.float32))[:, None]
    return loglik[0], class_avg


def solution(mesh):
    placed = (
        P(("grp", "blk", "cls"), None),
        P(None, ("grp", "blk", "cls")),
        P(("grp", "blk"), None),
        P(("grp", "blk")),
        P("grp"),
        P(),
    )
    return jax.shard_map(
        body,
        mesh=mesh,
        in_specs=placed,
        out_specs=(P(("grp", "blk", "cls")), P(("grp", "cls"), "blk")),
        check_vma=False,
    )
```

time: 293 us -> 138 us (0.47)
  waiting for transfers between devices: 181 us -> 18.9 us
  Pallas kernels: 0 us -> 72.2 us
  blocking collectives: 44.6 us -> 0 us
  starting transfers between devices: 0.12 us -> 24.4 us
  matrix products: 24.1 us -> 0 us
  other arithmetic: 20 us -> 3.19 us
  between operations: 15.1 us -> 9.84 us
    all_gather x1 -> x0, waiting for transfers between devices: 95.8 us -> none  [body(): lax.all_gather(templates, 'blk', axis=0, tiled=True)]
    unnamed x5 -> x0, waiting for transfers between devices: 84.8 us -> none
    pallas_call x0 -> x6, Pallas kernels: none -> 72.2 us  [the longest x5 62.6 us: score_groups(): pl.pallas_call(functools.partial(score_kernel, tuple(layout)), grid=(STEP...]
    unnamed x3 -> x0, blocking collectives: 44.6 us -> none
    dot_general x2 -> x0, matrix products: 24.1 us -> none  [the longest x1 15.4 us: score_block(): lax.dot_general(weighted, particles, (((1,), (1,)), ((), ())), preferred_...]
    ppermute x0 -> x29, starting transfers between devices: none -> 19.6 us  [the longest x14 17.4 us: body(): arrived = {sub: lax.ppermute(held[way][sub], 'blk', pairs) for sub in taken}]
    reduce_sum x7 -> x1, other arithmetic: 16.6 us -> 0.03 us  [body(): total = jnp.sum(pieces, axis=0)]
    ppermute x0 -> x29, waiting for transfers between devices: none -> 11.3 us  [the longest x14 9.9 us: body(): arrived = {sub: lax.ppermute(held[way][sub], 'blk', pairs) for sub in taken}]
  transfers between devices with their start and end apart: 3 -> 30, of which waited for: 2 -> 6; matrix products, arithmetic and copies ran while one was open for 4% -> 3% of each run, Pallas kernels for 0% -> 37%
where the time goes in v1:
time: 138 us; the launch traced here: 136 us
  Pallas kernels  72.2 us (52%)
  starting transfers between devices  24.4 us (18%)
  waiting for transfers between devices  18.9 us (14%)
  between operations  9.84 us (7%)
  local copies, waits for them, and re-layouts  7.92 us (6%)
  other arithmetic  3.19 us (2%)
    pallas_call x5, Pallas kernels, score_groups(): pl.pallas_call(functools.partial(score_kernel, tuple(layout)), grid=(STEP...  62.6 us
    ppermute x14, starting transfers between devices, body(): arrived = {sub: lax.ppermute(held[way][sub], 'blk', pairs) for sub in taken}  17.4 us
    ppermute x14, waiting for transfers between devices, body(): arrived = {sub: lax.ppermute(held[way][sub], 'blk', pairs) for sub in taken}  9.9 us
    pallas_call x1, Pallas kernels, class_sums(): pl.pallas_call(sums_kernel, grid=(blocks,), in_specs=[pl.BlockSpec(memory...  9.56 us
    all_to_all x1, waiting for transfers between devices, body(): lax.all_to_all(reduced, 'blk', split_axis=0, concat_axis=0, tiled=True)  7.54 us
    all_to_all x1, starting transfers between devices, body(): lax.all_to_all(reduced, 'blk', split_axis=0, concat_axis=0, tiled=True)  4.88 us
    unnamed x14, local copies, waits for them, and re-layouts  3.68 us
  transfers between devices with their start and end apart: 30, of which 6 were waited for; matrix products, arithmetic and copies ran while one was open for 3% of the time, Pallas kernels for 37%

profile of v1, /device:TPU:0, one launch (start us, length us, event | category | flops | bytes accessed | tf_op | source)
XLA Modules:
  0.0 136.4 jit_solution(16923139092135948990)
XLA Ops:
  1.4 1.1 fusion
  2.6 3.1 %collective-permute-start = (bf16[32,4224]{1,0:T(8,128)(2,1)S(1)}, bf16[32,4224]{1,0:T(8,128)(2,1)S(1)}, u32[]{:S(2)}, u32[]{:S(2)}) collective-permute-start(bf16[32,4224]{1,0:T(8,128)(2,1)S(1)} %get-tuple-element.11), channel_id=1, source_target_pairs={{0,4},{4,8},{8,12},{12,14},{14,10},{10,6},{6,2},{2,0},{1,5},{5,9},... | collective-permute-start | bytes 811016 | tf_op jit(solution)/shard_map/ppermute | solution.py:266
  5.7 1.6 %collective-permute-start.1 = (bf16[32,4224]{1,0:T(8,128)(2,1)S(1)}, bf16[32,4224]{1,0:T(8,128)(2,1)S(1)}, u32[]{:S(2)}, u32[]{:S(2)}) collective-permute-start(bf16[32,4224]{1,0:T(8,128)(2,1)S(1)} %get-tuple-element.10), channel_id=1, source_target_pairs={{0,4},{4,8},{8,12},{12,14},{14,10},{10,6},{6,2},{2,0},{1,5},{5,9},... | collective-permute-start | bytes 811016 | tf_op jit(solution)/shard_map/ppermute | solution.py:266
  7.7 1.2 dynamic_slice.31
  13.6 1.6 %fusion.1 = (s32[1]{0:T(128)}, s32[1]{0:T(128)}, s32[1]{0:T(128)}, s32[1]{0:T(128)}, s32[1]{0:T(128)}, /*index=5*/s32[1]{0:T(128)}, s32[1]{0:T(128)}) fusion(s32[8]{0:T(128)} %constant.86.clone, s32[]{:T(128)S(6)} %select_n.37, s32[]{:T(128)S(6)} %select_n.36, s32[]{:T(128)S(6)} %select_n.35, s32[]{:T(128)S(6)} %select_n.34, s32[]{:T(128)S(6)} %select_n.33, ...), kind=kLoop, calls=%fused_computation.12 | loop fusion | bytes 84 | tf_op jit(solution)/shard_map/dynamic_slice | solution.py:269
  15.9 2.0 %collective-permute-done.1.rest_2_ = bf16[32,4224]{1,0:T(8,128)(2,1)S(1)} collective-permute-done((bf16[32,4224]{1,0:T(8,128)(2,1)S(1)}, bf16[32,4224]{1,0:T(8,128)(2,1)S(1)}, u32[]{:S(2)}, u32[]{:S(2)}) %collective-permute-start.1) | collective-permute-done | bytes 270368 | tf_op jit(solution)/shard_map/ppermute | solution.py:266
  22.0 1.8 %collective-permute-start.8 = (bf16[32,4224]{1,0:T(8,128)(2,1)S(1)}, bf16[32,4224]{1,0:T(8,128)(2,1)S(1)}, u32[]{:S(2)}, u32[]{:S(2)}) collective-permute-start(bf16[32,4224]{1,0:T(8,128)(2,1)S(1)} %collective-permute-done.rest_0_.rest_1_), channel_id=1, source_target_pairs={{0,4},{4,8},{8,12},{12,14},{14,10},{10,6},{6,2},{2,0},{1,5},{5,9},... | collective-permute-start | bytes 811016 | tf_op jit(solution)/shard_map/ppermute | solution.py:266
  23.8 1.6 %collective-permute-start.9 = (bf16[32,4224]{1,0:T(8,128)(2,1)S(1)}, bf16[32,4224]{1,0:T(8,128)(2,1)S(1)}, u32[]{:S(2)}, u32[]{:S(2)}) collective-permute-start(bf16[32,4224]{1,0:T(8,128)(2,1)S(1)} %collective-permute-done.1.rest_2_), channel_id=1, source_target_pairs={{0,4},{4,8},{8,12},{12,14},{14,10},{10,6},{6,2},{2,0},{1,5},{5,9},... | collective-permute-start | bytes 811016 | tf_op jit(solution)/shard_map/ppermute | solution.py:266
  27.4 3.9 %collective-permute-done.8.rest_0_.rest_1_ = bf16[32,4224]{1,0:T(8,128)(2,1)S(1)} collective-permute-done((bf16[32,4224]{1,0:T(8,128)(2,1)S(1)}, bf16[32,4224]{1,0:T(8,128)(2,1)S(1)}, u32[]{:S(2)}, u32[]{:S(2)}) %collective-permute-start.8) | collective-permute-done | bytes 270368 | tf_op jit(solution)/shard_map/ppermute | solution.py:266
  31.3 1.8 %collective-permute-start.16 = (bf16[32,4224]{1,0:T(8,128)(2,1)S(1)}, bf16[32,4224]{1,0:T(8,128)(2,1)S(1)}, u32[]{:S(2)}, u32[]{:S(2)}) collective-permute-start(bf16[32,4224]{1,0:T(8,128)(2,1)S(1)} %collective-permute-done.8.rest_0_.rest_1_), channel_id=1, source_target_pairs={{0,4},{4,8},{8,12},{12,14},{14,10},{10,6},{6,2},{2,0},{1,5},{5,9},... | collective-permute-start | bytes 811016 | tf_op jit(solution)/shard_map/ppermute | solution.py:266
  33.1 4.0 %collective-permute-done.9.rest_2_ = bf16[32,4224]{1,0:T(8,128)(2,1)S(1)} collective-permute-done((bf16[32,4224]{1,0:T(8,128)(2,1)S(1)}, bf16[32,4224]{1,0:T(8,128)(2,1)S(1)}, u32[]{:S(2)}, u32[]{:S(2)}) %collective-permute-start.9) | collective-permute-done | bytes 270368 | tf_op jit(solution)/shard_map/ppermute | solution.py:266
  37.6 1.2 copy-done
  41.3 11.8 %shard_map.95.state_ref = f32[16,1024]{1,0:T(8,128)S(1)} custom-call(s32[1]{0:T(128)} %bitcast.29.base_ref, f32[8]{0:T(128)S(1)} %convert_log_fusion.logs_ref, s32[16,1024]{1,0:T(8,128)S(1)} %copy-done.1, f32[16,1024]{1,0:T(8,128)S(1)} %copy-done.5, f32[1,8192]{1,0:T(1,128)S(1)} %bitcast.32, bf16[1024,8192]{1,0:T(8,128)(2,1)} %part_ref.11, ...), custom_call_target="tpu_custom_call" | custom-call | flops 4294967296 | bytes 16777216 | tf_op jit(solution)/shard_map/pallas_call | solution.py:135
  53.1 1.9 %collective-permute-start.17 = (bf16[32,4224]{1,0:T(8,128)(2,1)S(1)}, bf16[32,4224]{1,0:T(8,128)(2,1)S(1)}, u32[]{:S(2)}, u32[]{:S(2)}) collective-permute-start(bf16[32,4224]{1,0:T(8,128)(2,1)S(1)} %collective-permute-done.9.rest_2_), channel_id=1, source_target_pairs={{0,4},{4,8},{8,12},{12,14},{14,10},{10,6},{6,2},{2,0},{1,5},{5,9},... | collective-permute-start | bytes 811016 | tf_op jit(solution)/shard_map/ppermute | solution.py:266
  55.2 1.8 %collective-permute-start.21 = (bf16[32,4224]{1,0:T(8,128)(2,1)S(1)}, bf16[32,4224]{1,0:T(8,128)(2,1)S(1)}, u32[]{:S(2)}, u32[]{:S(2)}) collective-permute-start(bf16[32,4224]{1,0:T(8,128)(2,1)S(1)} %collective-permute-done.13.rest_8_), channel_id=1, source_target_pairs={{4,0},{8,4},{12,8},{14,12},{10,14},{6,10},{2,6},{0,2},{5,1},{9,5},... | collective-permute-start | bytes 811016 | tf_op jit(solution)/shard_map/ppermute | solution.py:266
  57.1 13.0 %shard_map.96.state_ref = f32[16,1024]{1,0:T(8,128)S(1)} custom-call(s32[4]{0:T(128)S(1)} %pad_add_fusion.3.base_ref, f32[8]{0:T(128)S(1)} %convert_log_fusion.logs_ref, s32[16,1024]{1,0:T(8,128)S(1)} %copy-done.2, f32[16,1024]{1,0:T(8,128)S(1)} %shard_map.95.state_ref, f32[1,8192]{1,0:T(1,128)S(1)} %bitcast.33, bf16[1024,8192]{1,0:T(8,128)(2,1)} %part_ref.11, ...), custom_call_target="tpu_custom_call" | custom-call | flops 4294967296 | bytes 16777216 | tf_op jit(solution)/shard_map/pallas_call | solution.py:135
  70.6 1.8 %collective-permute-start.25 = (bf16[32,4224]{1,0:T(8,128)(2,1)S(1)}, bf16[32,4224]{1,0:T(8,128)(2,1)S(1)}, u32[]{:S(2)}, u32[]{:S(2)}) collective-permute-start(bf16[32,4224]{1,0:T(8,128)(2,1)S(1)} %collective-permute-done.21.rest_8_), channel_id=1, source_target_pairs={{4,0},{8,4},{12,8},{14,12},{10,14},{6,10},{2,6},{0,2},{5,1},{9,5},... | collective-permute-start | bytes 811016 | tf_op jit(solution)/shard_map/ppermute | solution.py:266
  72.9 13.0 %shard_map.97.state_ref = f32[16,1024]{1,0:T(8,128)S(1)} custom-call(s32[4]{0:T(128)S(1)} %pad_add_fusion.2.base_ref, f32[8]{0:T(128)S(1)} %convert_log_fusion.logs_ref, s32[16,1024]{1,0:T(8,128)S(1)} %copy-done.2, f32[16,1024]{1,0:T(8,128)S(1)} %shard_map.96.state_ref, f32[1,8192]{1,0:T(1,128)S(1)} %bitcast.34, bf16[1024,8192]{1,0:T(8,128)(2,1)} %part_ref.11, ...), custom_call_target="tpu_custom_call" | custom-call | flops 4294967296 | bytes 16777216 | tf_op jit(solution)/shard_map/pallas_call | solution.py:135
  86.5 13.0 %shard_map.98.state_ref = f32[16,1024]{1,0:T(8,128)S(1)} custom-call(s32[4]{0:T(128)S(1)} %pad_add_fusion.1.base_ref, f32[8]{0:T(128)S(1)} %convert_log_fusion.logs_ref, s32[16,1024]{1,0:T(8,128)S(1)} %copy-done.2, f32[16,1024]{1,0:T(8,128)S(1)} %shard_map.97.state_ref, f32[1,8192]{1,0:T(1,128)S(1)} %bitcast.35, bf16[1024,8192]{1,0:T(8,128)(2,1)} %part_ref.11, ...), custom_call_target="tpu_custom_call" | custom-call | flops 4294967296 | bytes 16777216 | tf_op jit(solution)/shard_map/pallas_call | solution.py:135
  99.5 11.9 %shard_map.99.state_ref = f32[16,1024]{1,0:T(8,128)S(1)} custom-call(s32[2]{0:T(128)S(1)} %pad_add_fusion.base_ref, f32[8]{0:T(128)S(1)} %convert_log_fusion.logs_ref, s32[16,1024]{1,0:T(8,128)S(1)} %copy-done.2, f32[16,1024]{1,0:T(8,128)S(1)} %shard_map.98.state_ref, f32[1,8192]{1,0:T(1,128)S(1)} %bitcast.36, bf16[1024,8192]{1,0:T(8,128)(2,1)} %part_ref.11, ...), custom_call_target="tpu_custom_call" | custom-call | flops 4294967296 | bytes 16777216 | tf_op jit(solution)/shard_map/pallas_call | solution.py:135
  111.5 9.6 %shard_map.100 = (f32[1,1024]{1,0:T(1,128)}, f32[8,4,1152]{2,1,0:T(4,128)S(1)}, f32[8,4,1152]{2,1,0:T(4,128)S(1)}) custom-call(s32[1]{0:T(128)} %bitcast.own_ref, f32[16,1024]{1,0:T(8,128)S(1)} %shard_map.99.state_ref, bf16[1024,8192]{1,0:T(8,128)(2,1)} %part_ref.11), custom_call_target="tpu_custom_call" | custom-call | flops 2147483648 | bytes 16777216 | tf_op jit(solution)/shard_map/pallas_call | solution.py:182
  121.1 1.3 collective-permute-done.28
  123.1 4.9 %all-to-all-start = ((f32[8,4,1152]{2,1,0:T(4,128)}), f32[8,4,1152]{2,1,0:T(4,128)S(1)}, u32[]{:S(2)}, u32[]{:S(2)}) async-start(f32[8,4,1152]{2,1,0:T(4,128)} %add.179), calls=%async_computation | async-start | bytes 294912 | tf_op jit(solution)/shard_map/all_to_all | solution.py:287
  128.0 7.5 %all-to-all-done = f32[8,4,1152]{2,1,0:T(4,128)S(1)} async-done(((f32[8,4,1152]{2,1,0:T(4,128)}), f32[8,4,1152]{2,1,0:T(4,128)S(1)}, u32[]{:S(2)}, u32[]{:S(2)}) %all-to-all-start) | async-done | bytes 147488 | tf_op jit(solution)/shard_map/all_to_all | solution.py:287
  (74 shorter events, 10.4 us)
Async XLA Ops:
  2.6 13.2 %collective-permute-start = (bf16[32,4224]{1,0:T(8,128)(2,1)S(1)}, bf16[32,4224]{1,0:T(8,128)(2,1)S(1)}, u32[]{:S(2)}, u32[]{:S(2)}) collective-permute-start(bf16[32,4224]{1,0:T(8,128)(2,1)S(1)} %get-tuple-element.11), channel_id=1, source_target_pairs={{0,4},{4,8},{8,12},{12,14},{14,10},{10,6},{6,2},{2,0},{1,5},{5,9},... | collective-permute-start | bytes 811016 | tf_op jit(solution)/shard_map/ppermute | solution.py:266
  5.7 12.2 %collective-permute-start.1 = (bf16[32,4224]{1,0:T(8,128)(2,1)S(1)}, bf16[32,4224]{1,0:T(8,128)(2,1)S(1)}, u32[]{:S(2)}, u32[]{:S(2)}) collective-permute-start(bf16[32,4224]{1,0:T(8,128)(2,1)S(1)} %get-tuple-element.10), channel_id=1, source_target_pairs={{0,4},{4,8},{8,12},{12,14},{14,10},{10,6},{6,2},{2,0},{1,5},{5,9},... | collective-permute-start | bytes 811016 | tf_op jit(solution)/shard_map/ppermute | solution.py:266
  7.3 16.5 %collective-permute-start.4 = (bf16[32,4224]{1,0:T(8,128)(2,1)S(1)}, bf16[32,4224]{1,0:T(8,128)(2,1)S(1)}, u32[]{:S(2)}, u32[]{:S(2)}) collective-permute-start(bf16[32,4224]{1,0:T(8,128)(2,1)S(1)} %get-tuple-element.11), channel_id=1, source_target_pairs={{4,0},{8,4},{12,8},{14,12},{10,14},{6,10},{2,6},{0,2},{5,1},{9,5},... | collective-permute-start | bytes 811016 | tf_op jit(solution)/shard_map/ppermute | solution.py:266
  7.7 17.6 %collective-permute-start.5 = (bf16[32,4224]{1,0:T(8,128)(2,1)S(1)}, bf16[32,4224]{1,0:T(8,128)(2,1)S(1)}, u32[]{:S(2)}, u32[]{:S(2)}) collective-permute-start(bf16[32,4224]{1,0:T(8,128)(2,1)S(1)} %get-tuple-element.10), channel_id=1, source_target_pairs={{4,0},{8,4},{12,8},{14,12},{10,14},{6,10},{2,6},{0,2},{5,1},{9,5},... | collective-permute-start | bytes 811016 | tf_op jit(solution)/shard_map/ppermute | solution.py:266
  23.8 13.3 %collective-permute-start.9 = (bf16[32,4224]{1,0:T(8,128)(2,1)S(1)}, bf16[32,4224]{1,0:T(8,128)(2,1)S(1)}, u32[]{:S(2)}, u32[]{:S(2)}) collective-permute-start(bf16[32,4224]{1,0:T(8,128)(2,1)S(1)} %collective-permute-done.1.rest_2_), channel_id=1, source_target_pairs={{0,4},{4,8},{8,12},{12,14},{14,10},{10,6},{6,2},{2,0},{1,5},{5,9},... | collective-permute-start | bytes 811016 | tf_op jit(solution)/shard_map/ppermute | solution.py:266
  25.4 11.7 %collective-permute-start.12 = (bf16[32,4224]{1,0:T(8,128)(2,1)S(1)}, bf16[32,4224]{1,0:T(8,128)(2,1)S(1)}, u32[]{:S(2)}, u32[]{:S(2)}) collective-permute-start(bf16[32,4224]{1,0:T(8,128)(2,1)S(1)} %collective-permute-done.4.rest_6_.rest_7_), channel_id=1, source_target_pairs={{4,0},{8,4},{12,8},{14,12},{10,14},{6,10},{2,6},{0,2},{5,1},{9,5},... | collective-permute-start | bytes 811016 | tf_op jit(solution)/shard_map/ppermute | solution.py:266
  26.9 26.2 %collective-permute-start.13 = (bf16[32,4224]{1,0:T(8,128)(2,1)S(1)}, bf16[32,4224]{1,0:T(8,128)(2,1)S(1)}, u32[]{:S(2)}, u32[]{:S(2)}) collective-permute-start(bf16[32,4224]{1,0:T(8,128)(2,1)S(1)} %collective-permute-done.5.rest_8_), channel_id=1, source_target_pairs={{4,0},{8,4},{12,8},{14,12},{10,14},{6,10},{2,6},{0,2},{5,1},{9,5},... | collective-permute-start | bytes 811016 | tf_op jit(solution)/shard_map/ppermute | solution.py:266
  31.3 23.7 %collective-permute-start.10 = (bf16[32,4224]{1,0:T(8,128)(2,1)S(1)}, bf16[32,4224]{1,0:T(8,128)(2,1)S(1)}, u32[]{:S(2)}, u32[]{:S(2)}) collective-permute-start(bf16[32,4224]{1,0:T(8,128)(2,1)S(1)} %collective-permute-done.8.rest_0_.rest_1_), channel_id=1, source_target_pairs={{0,1},{1,0},{2,3},{3,2},{4,5},{5,4},{6,7},{7,6},{8,9},{9,8},{10,11... | collective-permute-start | bytes 811016 | tf_op jit(solution)/shard_map/ppermute | solution.py:267
  31.3 25.7 %collective-permute-start.16 = (bf16[32,4224]{1,0:T(8,128)(2,1)S(1)}, bf16[32,4224]{1,0:T(8,128)(2,1)S(1)}, u32[]{:S(2)}, u32[]{:S(2)}) collective-permute-start(bf16[32,4224]{1,0:T(8,128)(2,1)S(1)} %collective-permute-done.8.rest_0_.rest_1_), channel_id=1, source_target_pairs={{0,4},{4,8},{8,12},{12,14},{14,10},{10,6},{6,2},{2,0},{1,5},{5,9},... | collective-permute-start | bytes 811016 | tf_op jit(solution)/shard_map/ppermute | solution.py:266
  37.1 18.1 %collective-permute-start.11 = (bf16[32,4224]{1,0:T(8,128)(2,1)S(1)}, bf16[32,4224]{1,0:T(8,128)(2,1)S(1)}, u32[]{:S(2)}, u32[]{:S(2)}) collective-permute-start(bf16[32,4224]{1,0:T(8,128)(2,1)S(1)} %collective-permute-done.9.rest_2_), channel_id=1, source_target_pairs={{0,1},{1,0},{2,3},{3,2},{4,5},{5,4},{6,7},{7,6},{8,9},{9,8},{10,11... | collective-permute-start | bytes 811016 | tf_op jit(solution)/shard_map/ppermute | solution.py:267
  37.1 18.1 %collective-permute-start.14 = (bf16[32,4224]{1,0:T(8,128)(2,1)S(1)}, bf16[32,4224]{1,0:T(8,128)(2,1)S(1)}, u32[]{:S(2)}, u32[]{:S(2)}) collective-permute-start(bf16[32,4224]{1,0:T(8,128)(2,1)S(1)} %collective-permute-done.12.rest_6_.rest_7_), channel_id=1, source_target_pairs={{0,1},{1,0},{2,3},{3,2},{4,5},{5,4},{6,7},{7,6},{8,9},{9,8},{10,11... | collective-permute-start | bytes 811016 | tf_op jit(solution)/shard_map/ppermute | solution.py:267
  53.1 17.5 %collective-permute-start.17 = (bf16[32,4224]{1,0:T(8,128)(2,1)S(1)}, bf16[32,4224]{1,0:T(8,128)(2,1)S(1)}, u32[]{:S(2)}, u32[]{:S(2)}) collective-permute-start(bf16[32,4224]{1,0:T(8,128)(2,1)S(1)} %collective-permute-done.9.rest_2_), channel_id=1, source_target_pairs={{0,4},{4,8},{8,12},{12,14},{14,10},{10,6},{6,2},{2,0},{1,5},{5,9},... | collective-permute-start | bytes 811016 | tf_op jit(solution)/shard_map/ppermute | solution.py:266
  54.9 17.5 %collective-permute-start.20 = (bf16[32,4224]{1,0:T(8,128)(2,1)S(1)}, bf16[32,4224]{1,0:T(8,128)(2,1)S(1)}, u32[]{:S(2)}, u32[]{:S(2)}) collective-permute-start(bf16[32,4224]{1,0:T(8,128)(2,1)S(1)} %collective-permute-done.12.rest_6_.rest_7_), channel_id=1, source_target_pairs={{4,0},{8,4},{12,8},{14,12},{10,14},{6,10},{2,6},{0,2},{5,1},{9,5},... | collective-permute-start | bytes 811016 | tf_op jit(solution)/shard_map/ppermute | solution.py:266
  55.2 15.0 %collective-permute-start.15 = (bf16[32,4224]{1,0:T(8,128)(2,1)S(1)}, bf16[32,4224]{1,0:T(8,128)(2,1)S(1)}, u32[]{:S(2)}, u32[]{:S(2)}) collective-permute-start(bf16[32,4224]{1,0:T(8,128)(2,1)S(1)} %collective-permute-done.13.rest_8_), channel_id=1, source_target_pairs={{0,1},{1,0},{2,3},{3,2},{4,5},{5,4},{6,7},{7,6},{8,9},{9,8},{10,11... | collective-permute-start | bytes 811016 | tf_op jit(solution)/shard_map/ppermute | solution.py:267
  55.2 15.4 %collective-permute-start.21 = (bf16[32,4224]{1,0:T(8,128)(2,1)S(1)}, bf16[32,4224]{1,0:T(8,128)(2,1)S(1)}, u32[]{:S(2)}, u32[]{:S(2)}) collective-permute-start(bf16[32,4224]{1,0:T(8,128)(2,1)S(1)} %collective-permute-done.13.rest_8_), channel_id=1, source_target_pairs={{4,0},{8,4},{12,8},{14,12},{10,14},{6,10},{2,6},{0,2},{5,1},{9,5},... | collective-permute-start | bytes 811016 | tf_op jit(solution)/shard_map/ppermute | solution.py:266
  57.0 15.5 %collective-permute-start.18 = (bf16[32,4224]{1,0:T(8,128)(2,1)S(1)}, bf16[32,4224]{1,0:T(8,128)(2,1)S(1)}, u32[]{:S(2)}, u32[]{:S(2)}) collective-permute-start(bf16[32,4224]{1,0:T(8,128)(2,1)S(1)} %collective-permute-done.16.rest_0_.rest_1_), channel_id=1, source_target_pairs={{0,1},{1,0},{2,3},{3,2},{4,5},{5,4},{6,7},{7,6},{8,9},{9,8},{10,11... | collective-permute-start | bytes 811016 | tf_op jit(solution)/shard_map/ppermute | solution.py:267
  70.1 15.8 %collective-permute-start.24 = (bf16[32,4224]{1,0:T(8,128)(2,1)S(1)}, bf16[32,4224]{1,0:T(8,128)(2,1)S(1)}, u32[]{:S(2)}, u32[]{:S(2)}) collective-permute-start(bf16[32,4224]{1,0:T(8,128)(2,1)S(1)} %collective-permute-done.16.rest_0_.rest_1_), channel_id=1, source_target_pairs={{0,4},{4,8},{8,12},{12,14},{14,10},{10,6},{6,2},{2,0},{1,5},{5,9},... | collective-permute-start | bytes 811016 | tf_op jit(solution)/shard_map/ppermute | solution.py:266
  70.6 15.9 %collective-permute-start.23 = (bf16[32,4224]{1,0:T(8,128)(2,1)S(1)}, bf16[32,4224]{1,0:T(8,128)(2,1)S(1)}, u32[]{:S(2)}, u32[]{:S(2)}) collective-permute-start(bf16[32,4224]{1,0:T(8,128)(2,1)S(1)} %collective-permute-done.21.rest_8_), channel_id=1, source_target_pairs={{0,1},{1,0},{2,3},{3,2},{4,5},{5,4},{6,7},{7,6},{8,9},{9,8},{10,11... | collective-permute-start | bytes 811016 | tf_op jit(solution)/shard_map/ppermute | solution.py:267
  70.6 15.5 %collective-permute-start.25 = (bf16[32,4224]{1,0:T(8,128)(2,1)S(1)}, bf16[32,4224]{1,0:T(8,128)(2,1)S(1)}, u32[]{:S(2)}, u32[]{:S(2)}) collective-permute-start(bf16[32,4224]{1,0:T(8,128)(2,1)S(1)} %collective-permute-done.21.rest_8_), channel_id=1, source_target_pairs={{4,0},{8,4},{12,8},{14,12},{10,14},{6,10},{2,6},{0,2},{5,1},{9,5},... | collective-permute-start | bytes 811016 | tf_op jit(solution)/shard_map/ppermute | solution.py:266
  72.4 14.1 %collective-permute-start.19 = (bf16[32,4224]{1,0:T(8,128)(2,1)S(1)}, bf16[32,4224]{1,0:T(8,128)(2,1)S(1)}, u32[]{:S(2)}, u32[]{:S(2)}) collective-permute-start(bf16[32,4224]{1,0:T(8,128)(2,1)S(1)} %collective-permute-done.17.rest_2_), channel_id=1, source_target_pairs={{0,1},{1,0},{2,3},{3,2},{4,5},{5,4},{6,7},{7,6},{8,9},{9,8},{10,11... | collective-permute-start | bytes 811016 | tf_op jit(solution)/shard_map/ppermute | solution.py:267
  72.4 14.1 %collective-permute-start.22 = (bf16[32,4224]{1,0:T(8,128)(2,1)S(1)}, bf16[32,4224]{1,0:T(8,128)(2,1)S(1)}, u32[]{:S(2)}, u32[]{:S(2)}) collective-permute-start(bf16[32,4224]{1,0:T(8,128)(2,1)S(1)} %collective-permute-done.20.rest_6_.rest_7_), channel_id=1, source_target_pairs={{0,1},{1,0},{2,3},{3,2},{4,5},{5,4},{6,7},{7,6},{8,9},{9,8},{10,11... | collective-permute-start | bytes 811016 | tf_op jit(solution)/shard_map/ppermute | solution.py:267
  85.9 13.6 %collective-permute-start.26 = (bf16[32,4224]{1,0:T(8,128)(2,1)S(1)}, bf16[32,4224]{1,0:T(8,128)(2,1)S(1)}, u32[]{:S(2)}, u32[]{:S(2)}) collective-permute-start(bf16[32,4224]{1,0:T(8,128)(2,1)S(1)} %collective-permute-done.24.rest_0_.rest_1_), channel_id=1, source_target_pairs={{0,1},{1,0},{2,3},{3,2},{4,5},{5,4},{6,7},{7,6},{8,9},{9,8},{10,11... | collective-permute-start | bytes 811016 | tf_op jit(solution)/shard_map/ppermute | solution.py:267
  86.1 13.5 %collective-permute-start.27 = (bf16[32,4224]{1,0:T(8,128)(2,1)S(1)}, bf16[32,4224]{1,0:T(8,128)(2,1)S(1)}, u32[]{:S(2)}, u32[]{:S(2)}) collective-permute-start(bf16[32,4224]{1,0:T(8,128)(2,1)S(1)} %collective-permute-done.25.rest_2_), channel_id=1, source_target_pairs={{0,1},{1,0},{2,3},{3,2},{4,5},{5,4},{6,7},{7,6},{8,9},{9,8},{10,11... | collective-permute-start | bytes 811016 | tf_op jit(solution)/shard_map/ppermute | solution.py:267
  123.1 12.4 %all-to-all-start = ((f32[8,4,1152]{2,1,0:T(4,128)}), f32[8,4,1152]{2,1,0:T(4,128)S(1)}, u32[]{:S(2)}, u32[]{:S(2)}) async-start(f32[8,4,1152]{2,1,0:T(4,128)} %add.179), calls=%async_computation | async-start | bytes 294912 | tf_op jit(solution)/shard_map/all_to_all | solution.py:287
  (13 other events, 187.9 us)

commit v2 on v0

v2 whole, which is shorter than its diff:
```python
import functools

import jax
import jax.numpy as jnp
from jax import lax
from jax.experimental import pallas as pl
from jax.experimental.pallas import tpu as pltpu
from jax.sharding import PartitionSpec as P

LOWEST = -1e30
STEPS = 8
SUBS = 2
LANES = 128
STATE_ROWS = 8
VMEM_LIMIT = 16 * 1024 * 1024


def ring_order(blocks):
    if blocks <= 8:
        return list(range(0, blocks, 2)) + list(range(blocks - 1, 0, -2))
    return list(range(blocks))


def message_kernel(core_ref, tags_ref, rows_ref, *message_refs):
    span = message_refs[0].shape[1]
    half = rows_ref.shape[0]
    for index, ref in enumerate(message_refs):
        ref[:, :span] = rows_ref[:, index * span : (index + 1) * span]
    row = lax.broadcasted_iota(jnp.int32, (half, LANES), 0)
    tags = jnp.zeros((half, LANES), jnp.float32)
    for r in range(half):
        tag = tags_ref[core_ref[0] * half + r].astype(jnp.float32)
        tags = jnp.where(row == r, tag, tags)
    message_refs[-1][:, span:] = tags.astype(jnp.bfloat16)


def make_messages(core, template_class, templates, owners):
    height, freqs = templates.shape
    half = height // owners
    span = freqs // SUBS
    widths = [span] * (SUBS - 1) + [span + LANES]
    return pl.pallas_call(
        message_kernel,
        grid_spec=pltpu.PrefetchScalarGridSpec(
            num_scalar_prefetch=2,
            grid=(1,),
            in_specs=[pl.BlockSpec((half, freqs), lambda j, core, tags: (core[0], 0))],
            out_specs=[pl.BlockSpec((half, width), lambda j, core, tags: (0, 0)) for width in widths],
        ),
        out_shape=[jax.ShapeDtypeStruct((half, width), jnp.bfloat16) for width in widths],
        compiler_params=pltpu.CompilerParams(vmem_limit_bytes=VMEM_LIMIT),
    )(core, template_class, templates)


def add_scores(rows, noise, part, acc, energy):
    widened = rows.astype(jnp.float32)
    product = widened * noise
    square = product * widened
    folded = square[:, :LANES]
    for lane in range(LANES, square.shape[1], LANES):
        folded = folded + square[:, lane : lane + LANES]
    energy[...] += folded
    acc[...] += lax.dot_general(
        product.astype(jnp.bfloat16),
        part,
        (((1,), (1,)), ((), ())),
        preferred_element_type=jnp.float32,
    )


def add_rows(tags, ids, logs_ref, sig_ref, state, acc, energy):
    classes = logs_ref.shape[0]
    prior = jnp.zeros_like(tags[:, :1])
    for tag in range(classes):
        prior = jnp.where(tags[:, :1] == tag, logs_ref[tag], prior)
    bias = prior - 0.5 * jnp.sum(energy[...], axis=1, keepdims=True)
    scores = acc[...] + bias
    old_max, old_sum, old_top, weights = state
    new_max = jnp.maximum(old_max, jnp.max(scores, axis=0, keepdims=True))
    new_sum = old_sum * jnp.exp(old_max - new_max) + jnp.sum(
        jnp.exp(scores - new_max), axis=0, keepdims=True
    )
    hit = sig_ref[0:1, :] == ids
    for pick in range(1, sig_ref.shape[0]):
        hit = hit | (sig_ref[pick : pick + 1, :] == ids)
    new_top = jnp.maximum(
        old_top, jnp.max(jnp.where(hit, scores, LOWEST), axis=0, keepdims=True)
    )
    value = jnp.where(hit, jnp.exp(scores - new_top), 0.0)
    lane = lax.broadcasted_iota(jnp.int32, tags.shape, 1).astype(jnp.float32)
    onehot = jnp.transpose(jnp.where(tags == lane, 1.0, 0.0))[:classes, :].astype(jnp.bfloat16)
    weights = weights * jnp.exp(old_top - new_top)
    left = value
    for _ in range(3):
        piece = left.astype(jnp.bfloat16)
        left = left - piece.astype(jnp.float32)
        weights = weights + jnp.dot(onehot, piece, preferred_element_type=jnp.float32)
    return new_max, new_sum, new_top, weights


def put_state(state, out_ref):
    new_max, new_sum, new_top, weights = state
    out_ref[0:1, :] = new_max
    out_ref[1:2, :] = new_sum
    out_ref[2:3, :] = new_top
    out_ref[3:STATE_ROWS, :] = jnp.zeros_like(out_ref[3:STATE_ROWS, :])
    out_ref[STATE_ROWS:, :] = weights


def get_state(state_ref):
    return state_ref[0:1, :], state_ref[1:2, :], state_ref[2:3, :], state_ref[STATE_ROWS:, :]


def own_kernel(
    base_ref, logs_ref, tags_ref, sig_ref, noise_ref, tmpl_ref, far_ref,
    out_ref, near_ref, acc, energy, arrived,
):
    freqs = noise_ref.shape[1]
    height = tmpl_ref.shape[0]
    width = freqs // STEPS

    def copy(step):
        columns = pl.ds(pl.multiple_of(step * width, width), width)
        return pltpu.make_async_copy(
            far_ref.at[:, columns], near_ref.at[:, columns], arrived.at[step]
        )

    for step in range(STEPS):
        copy(step).start()
    acc[...] = jnp.zeros_like(acc)
    energy[...] = jnp.zeros_like(energy)

    @pl.loop(0, STEPS)
    def _(step):
        copy(step).wait()
        columns = pl.ds(pl.multiple_of(step * width, width), width)
        add_scores(
            tmpl_ref[:, columns], noise_ref[:, columns], near_ref[:, columns], acc, energy
        )

    row = lax.broadcasted_iota(jnp.int32, (height, LANES), 0)
    tags = jnp.zeros((height, LANES), jnp.float32)
    for r in range(height):
        tags = jnp.where(row == r, tags_ref[r].astype(jnp.float32), tags)
    ids = base_ref[0] + lax.broadcasted_iota(jnp.int32, (height, 1), 0)
    lowest = jnp.full((1, acc.shape[1]), LOWEST, jnp.float32)
    none = jnp.zeros((1, acc.shape[1]), jnp.float32)
    weights = jnp.zeros((logs_ref.shape[0], acc.shape[1]), jnp.float32)
    state = (lowest, none, lowest, weights)
    put_state(add_rows(tags, ids, logs_ref, sig_ref, state, acc, energy), out_ref)


def in_smem():
    return pl.BlockSpec(memory_space=pltpu.SMEM)


def in_vmem():
    return pl.BlockSpec(memory_space=pltpu.VMEM)


def score_own(base, logs, template_class, significant, noise, templates, particles):
    per_device, freqs = particles.shape
    height = templates.shape[0]
    rows = STATE_ROWS + logs.shape[0]
    return pl.pallas_call(
        own_kernel,
        in_specs=[in_smem()] * 3 + [in_vmem()] * 3 + [pl.BlockSpec(memory_space=pl.ANY)],
        out_specs=[in_vmem(), in_vmem()],
        out_shape=[
            jax.ShapeDtypeStruct((rows, per_device), jnp.float32),
            pltpu.VMEM(particles.shape, particles.dtype),
        ],
        scratch_shapes=[
            pltpu.VMEM((height, per_device), jnp.float32),
            pltpu.VMEM((height, LANES), jnp.float32),
            pltpu.SemaphoreType.DMA((STEPS,)),
        ],
        compiler_params=pltpu.CompilerParams(vmem_limit_bytes=VMEM_LIMIT),
        cost_estimate=pl.CostEstimate(
            flops=4 * 128 * per_device * freqs,
            bytes_accessed=2 * per_device * freqs,
            transcendentals=0,
        ),
    )(
        base, logs, template_class, significant, noise, templates,
        pltpu.with_memory_space_constraint(particles, pltpu.HBM),
    )


def ring_kernel(layout, base_ref, logs_ref, sig_ref, state_ref, noise_ref, part_ref, *rest):
    groups = []
    at = 0
    for subs in layout:
        groups.append(rest[at : at + subs])
        at += subs
    out_ref, acc, energy = rest[at:]
    freqs = noise_ref.shape[1]
    width = freqs // STEPS
    share = STEPS // layout[0]
    acc[...] = jnp.zeros_like(acc)
    energy[...] = jnp.zeros_like(energy)
    for which in range(layout[0]):

        @pl.loop(0, share)
        def _(step):
            near = pl.ds(pl.multiple_of(step * width, width), width)
            columns = pl.ds(pl.multiple_of((which * share + step) * width, width), width)
            rows = jnp.concatenate([refs[which][:, near] for refs in groups], axis=0)
            add_scores(rows, noise_ref[:, columns], part_ref[:, columns], acc, energy)

    span = freqs // layout[0]
    tags = jnp.concatenate([refs[-1][:, span:] for refs in groups], axis=0).astype(jnp.float32)
    row_ids = []
    for group, refs in enumerate(groups):
        height = refs[0].shape[0]
        row_ids.append(base_ref[group] + lax.broadcasted_iota(jnp.int32, (height, 1), 0))
    ids = jnp.concatenate(row_ids, axis=0)
    state = add_rows(tags, ids, logs_ref, sig_ref, get_state(state_ref), acc, energy)
    put_state(state, out_ref)


def score_groups(groups, bases, logs, significant, state, noise, particles):
    per_device, freqs = particles.shape
    parts = [part for group in groups for part in group]
    rows = sum(group[0].shape[0] for group in groups)
    return pl.pallas_call(
        functools.partial(ring_kernel, tuple(len(group) for group in groups)),
        in_specs=[in_smem()] * 2 + [in_vmem()] * (4 + len(parts)),
        out_specs=in_vmem(),
        out_shape=jax.ShapeDtypeStruct(state.shape, jnp.float32),
        scratch_shapes=[
            pltpu.VMEM((rows, per_device), jnp.float32),
            pltpu.VMEM((rows, LANES), jnp.float32),
        ],
        compiler_params=pltpu.CompilerParams(vmem_limit_bytes=VMEM_LIMIT),
        cost_estimate=pl.CostEstimate(
            flops=4 * 128 * per_device * freqs,
            bytes_accessed=2 * per_device * freqs,
            transcendentals=0,
        ),
    )(
        bases, logs, significant, state, noise,
        pltpu.with_memory_space_constraint(particles, pltpu.VMEM), *parts,
    )


def sums_kernel(own_ref, state_ref, part_ref, loglik_ref, mine_ref, theirs_ref):
    blocks, per_owner = mine_ref.shape[:2]
    width = part_ref.shape[1] // blocks
    _, _, _, weights = get_state(state_ref)
    loglik_ref[...] = state_ref[0:1, :] + jnp.log(state_ref[1:2, :])
    weights = weights / jnp.sum(weights, axis=0, keepdims=True)
    turned = jnp.concatenate([weights[per_owner:], weights[:per_owner]], axis=0)
    weights = jnp.where(own_ref[0] == 0, weights, turned)
    rounded = weights.astype(jnp.bfloat16)
    total = jnp.broadcast_to(
        jnp.sum(weights, axis=1, keepdims=True), (weights.shape[0], LANES)
    )

    @pl.loop(0, blocks)
    def _(block):
        columns = pl.ds(pl.multiple_of(block * width, width), width)
        sums = jnp.dot(rounded, part_ref[:, columns], preferred_element_type=jnp.float32)
        mine_ref[block, :, :width] = sums[:per_owner]
        theirs_ref[block, :, :width] = sums[per_owner:]
        mine_ref[block, :, width:] = total[:per_owner]
        theirs_ref[block, :, width:] = total[per_owner:]


def class_sums(own, state, particles, blocks, classes, owners):
    per_device, freqs = particles.shape
    width = freqs // blocks
    per_owner = classes // owners
    piece = jax.ShapeDtypeStruct((blocks, per_owner, width + LANES), jnp.float32)
    return pl.pallas_call(
        sums_kernel,
        in_specs=[in_smem(), in_vmem(), in_vmem()],
        out_specs=[in_vmem()] * 3,
        out_shape=[jax.ShapeDtypeStruct((1, per_device), jnp.float32), piece, piece],
        compiler_params=pltpu.CompilerParams(vmem_limit_bytes=VMEM_LIMIT),
        cost_estimate=pl.CostEstimate(
            flops=2 * 128 * per_device * freqs,
            bytes_accessed=2 * per_device * freqs,
            transcendentals=0,
        ),
    )(own, state, pltpu.with_memory_space_constraint(particles, pltpu.VMEM))


def scatter_sum(pieces, blocks, block_id):
    if blocks & (blocks - 1):
        pieces = lax.all_to_all(pieces, "blk", split_axis=0, concat_axis=0, tiled=True)
        return jnp.sum(pieces, axis=0)
    stride = blocks // 2
    while stride:
        bit = lax.rem(lax.div(block_id, stride), 2)
        keep = lax.dynamic_slice_in_dim(pieces, bit * stride, stride, 0)
        send = lax.dynamic_slice_in_dim(pieces, (1 - bit) * stride, stride, 0)
        pairs = [(i, i ^ stride) for i in range(blocks)]
        pieces = keep + lax.ppermute(send, "blk", pairs)
        stride //= 2
    return pieces[0]


def body(particles, significant, templates, template_class, class_counts, inv_noise):
    per_device, freqs = particles.shape
    height = templates.shape[0]
    classes = class_counts.shape[0]
    blocks = lax.axis_size("blk")
    owners = lax.axis_size("cls")
    half = height // owners
    order = ring_order(blocks)
    place = [order.index(block) for block in range(blocks)]
    block_id = lax.axis_index("blk")
    core = lax.axis_index("cls")
    at = jnp.asarray(place, jnp.int32)[block_id]
    order_table = jnp.asarray(order, jnp.int32)
    forward = [(order[i], order[(i + 1) % blocks]) for i in range(blocks)]
    backward = [(order[(i + 1) % blocks], order[i]) for i in range(blocks)]
    swap = [(i, owners - 1 - i) for i in range(owners)]

    noise = inv_noise[None, :]
    logs = jnp.log(class_counts.astype(jnp.float32))
    first = make_messages(core[None], template_class, templates, owners)
    base = (block_id * height)[None]
    state, near = score_own(
        base, logs, template_class, significant, noise, templates, particles
    )
    last = blocks // 2
    held = {1: first, -1: first}
    for distance in range(1, last + 1):
        groups, bases = [], []
        for way, pairs in ((1, forward), (-1, backward)):
            taken = list(range(SUBS))
            if distance == last:
                taken = taken[: SUBS // 2] if way == 1 else taken[SUBS // 2 :]
            arrived = {sub: lax.ppermute(held[way][sub], "blk", pairs) for sub in taken}
            passed = {sub: lax.ppermute(arrived[sub], "cls", swap) for sub in taken}
            held[way] = arrived
            if distance == last and way == -1:
                for sub in taken:
                    groups[0].append(arrived[sub])
                    groups[1].append(passed[sub])
                continue
            source = order_table[lax.rem(at - way * distance + blocks, blocks)]
            groups.append([arrived[sub] for sub in taken])
            groups.append([passed[sub] for sub in taken])
            bases.append(source * height + core * half)
            bases.append(source * height + (owners - 1 - core) * half)
        state = score_groups(groups, jnp.stack(bases), logs, significant, state, noise, near)

    loglik, mine, theirs = class_sums(core[None], state, near, blocks, classes, owners)
    reduced = mine + lax.ppermute(theirs, "cls", swap)
    total = scatter_sum(reduced, blocks, block_id)
    width = freqs // blocks
    per_owner = classes // owners
    counts = lax.dynamic_slice_in_dim(class_counts, core * per_owner, per_owner, 0)
    class_avg = total[:, :width] / (total[:, width] + counts.astype(jnp.float32))[:, None]
    return loglik[0], class_avg


def solution(mesh):
    placed = (
        P(("grp", "blk", "cls"), None),
        P(None, ("grp", "blk", "cls")),
        P(("grp", "blk"), None),
        P(("grp", "blk")),
        P("grp"),
        P(),
    )
    return jax.shard_map(
        body,
        mesh=mesh,
        in_specs=placed,
        out_specs=(P(("grp", "blk", "cls")), P(("grp", "cls"), "blk")),
        check_vma=False,
    )
```

time: 293 us -> 111 us (0.38)
  waiting for transfers between devices: 181 us -> 18 us
  Pallas kernels: 0 us -> 47.1 us
  blocking collectives: 44.6 us -> 0 us
  starting transfers between devices: 0.12 us -> 25.4 us
  matrix products: 24.1 us -> 0 us
  other arithmetic: 20 us -> 1.81 us
  between operations: 15.1 us -> 9.79 us
    all_gather x1 -> x0, waiting for transfers between devices: 95.8 us -> none  [body(): lax.all_gather(templates, 'blk', axis=0, tiled=True)]
    unnamed x5 -> x0, waiting for transfers between devices: 84.8 us -> none
    pallas_call x0 -> x7, Pallas kernels: none -> 47.1 us  [the longest x4 34 us: score_groups(): pl.pallas_call(functools.partial(ring_kernel, tuple((len(group) for group...]
    unnamed x3 -> x0, blocking collectives: 44.6 us -> none
    ppermute x0 -> x32, starting transfers between devices: none -> 25.4 us  [the longest x14 17.5 us: body(): arrived = {sub: lax.ppermute(held[way][sub], 'blk', pairs) for sub in taken}]
    dot_general x2 -> x0, matrix products: 24.1 us -> none  [the longest x1 15.4 us: score_block(): lax.dot_general(weighted, particles, (((1,), (1,)), ((), ())), preferred_...]
    ppermute x0 -> x32, waiting for transfers between devices: none -> 18 us  [the longest x3 10.2 us: scatter_sum(): pieces = keep + lax.ppermute(send, 'blk', pairs)]
    reduce_sum x7 -> x0, other arithmetic: 16.6 us -> none  [the longest x1 5.64 us: score_block(): energy = 0.5 * jnp.sum(inv_noise[None, :] * widened * widened, axis=1)]
  transfers between devices with their start and end apart: 3 -> 32, of which waited for: 2 -> 6; matrix products, arithmetic and copies ran while one was open for 4% -> 3% of each run, Pallas kernels for 0% -> 32%
where the time goes in v2:
time: 111 us; the launch traced here: 110 us
  Pallas kernels  47.1 us (42%)
  starting transfers between devices  25.4 us (23%)
  waiting for transfers between devices  18 us (16%)
  between operations  9.79 us (9%)
  local copies, waits for them, and re-layouts  8.36 us (8%)
  other arithmetic  1.81 us (2%)
    pallas_call x4, Pallas kernels, score_groups(): pl.pallas_call(functools.partial(ring_kernel, tuple((len(group) for group...  34 us
    ppermute x14, starting transfers between devices, body(): arrived = {sub: lax.ppermute(held[way][sub], 'blk', pairs) for sub in taken}  17.5 us
    ppermute x3, waiting for transfers between devices, scatter_sum(): pieces = keep + lax.ppermute(send, 'blk', pairs)  10.2 us
    pallas_call x1, Pallas kernels, score_own(): pl.pallas_call(own_kernel, in_specs=[in_smem()] * 3 + [in_vmem()] * 3 + [...  9.06 us
    ppermute x14, waiting for transfers between devices, body(): arrived = {sub: lax.ppermute(held[way][sub], 'blk', pairs) for sub in taken}  6.77 us
    unnamed x18, local copies, waits for them, and re-layouts  5.36 us
    ppermute x3, starting transfers between devices, scatter_sum(): pieces = keep + lax.ppermute(send, 'blk', pairs)  4.95 us
    pallas_call x1, Pallas kernels, class_sums(): pl.pallas_call(sums_kernel, in_specs=[in_smem(), in_vmem(), in_vmem()], o...  3.43 us
  transfers between devices with their start and end apart: 32, of which 6 were waited for; matrix products, arithmetic and copies ran while one was open for 3% of the time, Pallas kernels for 32%

profile of v2, /device:TPU:0, one launch (start us, length us, event | category | flops | bytes accessed | tf_op | source)
XLA Modules:
  0.0 110.4 jit_solution(3256924745036440642)
XLA Ops:
  0.6 1.2 %copy-done = bf16[64,8192]{1,0:T(8,128)(2,1)S(1)} copy-done((bf16[64,8192]{1,0:T(8,128)(2,1)S(1)}, bf16[64,8192]{1,0:T(8,128)(2,1)}, u32[]{:S(2)}) %copy-start) | copy-done | bytes 1048600
  3.1 3.1 %collective-permute-start = (bf16[32,4096]{1,0:T(8,128)(2,1)S(1)}, bf16[32,4096]{1,0:T(8,128)(2,1)S(1)}, u32[]{:S(2)}, u32[]{:S(2)}) collective-permute-start(bf16[32,4096]{1,0:T(8,128)(2,1)S(1)} %get-tuple-element.11), channel_id=1, source_target_pairs={{0,4},{4,8},{8,12},{12,14},{14,10},{10,6},{6,2},{2,0},{1,5},{5,9},... | collective-permute-start | bytes 786440 | tf_op jit(solution)/shard_map/ppermute | solution.py:336
  6.2 2.0 %collective-permute-start.1 = (bf16[32,4224]{1,0:T(8,128)(2,1)S(1)}, bf16[32,4224]{1,0:T(8,128)(2,1)S(1)}, u32[]{:S(2)}, u32[]{:S(2)}) collective-permute-start(bf16[32,4224]{1,0:T(8,128)(2,1)S(1)} %get-tuple-element.12), channel_id=1, source_target_pairs={{0,4},{4,8},{8,12},{12,14},{14,10},{10,6},{6,2},{2,0},{1,5},{5,9},... | collective-permute-start | bytes 811016 | tf_op jit(solution)/shard_map/ppermute | solution.py:336
  8.2 1.2 %dynamic_slice.45 = s32[1]{0:T(128)} dynamic-slice(s32[8]{0:T(128)} %constant.93.clone, s32[]{:T(128)S(6)} %select_n.45), dynamic_slice_sizes={1} | dynamic-slice | bytes 12 | tf_op jit(solution)/shard_map/dynamic_slice | solution.py:315
  14.1 1.6 %fusion = (s32[1]{0:T(128)}, s32[1]{0:T(128)}, s32[1]{0:T(128)}, s32[1]{0:T(128)}, s32[1]{0:T(128)}, /*index=5*/s32[1]{0:T(128)}, s32[1]{0:T(128)}) fusion(s32[8]{0:T(128)} %constant.94.clone, s32[]{:T(128)S(6)} %select_n.51, s32[]{:T(128)S(6)} %select_n.50, s32[]{:T(128)S(6)} %select_n.49, s32[]{:T(128)S(6)} %select_n.48, s32[]{:T(128)S(6)} %select_n.47, ...), kind=kLoop, calls=%fused_computation.14 | loop fusion | bytes 84 | tf_op jit(solution)/shard_map/dynamic_slice | solution.py:344
  20.9 2.0 %collective-permute-start.8 = (bf16[32,4096]{1,0:T(8,128)(2,1)S(1)}, bf16[32,4096]{1,0:T(8,128)(2,1)S(1)}, u32[]{:S(2)}, u32[]{:S(2)}) collective-permute-start(bf16[32,4096]{1,0:T(8,128)(2,1)S(1)} %collective-permute-done.rest_0_), channel_id=1, source_target_pairs={{0,4},{4,8},{8,12},{12,14},{14,10},{10,6},{6,2},{2,0},{1,5},{5,9},... | collective-permute-start | bytes 786440 | tf_op jit(solution)/shard_map/ppermute | solution.py:336
  23.0 2.0 %collective-permute-start.9 = (bf16[32,4224]{1,0:T(8,128)(2,1)S(1)}, bf16[32,4224]{1,0:T(8,128)(2,1)S(1)}, u32[]{:S(2)}, u32[]{:S(2)}) collective-permute-start(bf16[32,4224]{1,0:T(8,128)(2,1)S(1)} %collective-permute-done.1.rest_1_), channel_id=1, source_target_pairs={{0,4},{4,8},{8,12},{12,14},{14,10},{10,6},{6,2},{2,0},{1,5},{5,9},... | collective-permute-start | bytes 811016 | tf_op jit(solution)/shard_map/ppermute | solution.py:336
  25.9 4.1 %collective-permute-done.8.rest_0_ = bf16[32,4096]{1,0:T(8,128)(2,1)S(1)} collective-permute-done((bf16[32,4096]{1,0:T(8,128)(2,1)S(1)}, bf16[32,4096]{1,0:T(8,128)(2,1)S(1)}, u32[]{:S(2)}, u32[]{:S(2)}) %collective-permute-start.8) | collective-permute-done | bytes 262176 | tf_op jit(solution)/shard_map/ppermute | solution.py:336
  30.0 2.0 %collective-permute-start.13 = (bf16[32,4224]{1,0:T(8,128)(2,1)S(1)}, bf16[32,4224]{1,0:T(8,128)(2,1)S(1)}, u32[]{:S(2)}, u32[]{:S(2)}) collective-permute-start(bf16[32,4224]{1,0:T(8,128)(2,1)S(1)} %collective-permute-done.5.rest_5_), channel_id=1, source_target_pairs={{4,0},{8,4},{12,8},{14,12},{10,14},{6,10},{2,6},{0,2},{5,1},{9,5},... | collective-permute-start | bytes 811016 | tf_op jit(solution)/shard_map/ppermute | solution.py:336
  32.7 2.6 %collective-permute-done.9.rest_1_ = bf16[32,4224]{1,0:T(8,128)(2,1)S(1)} collective-permute-done((bf16[32,4224]{1,0:T(8,128)(2,1)S(1)}, bf16[32,4224]{1,0:T(8,128)(2,1)S(1)}, u32[]{:S(2)}, u32[]{:S(2)}) %collective-permute-start.9) | collective-permute-done | bytes 270368 | tf_op jit(solution)/shard_map/ppermute | solution.py:336
  35.4 1.7 %collective-permute-start.20 = (bf16[32,4096]{1,0:T(8,128)(2,1)S(1)}, bf16[32,4096]{1,0:T(8,128)(2,1)S(1)}, u32[]{:S(2)}, u32[]{:S(2)}) collective-permute-start(bf16[32,4096]{1,0:T(8,128)(2,1)S(1)} %collective-permute-done.12.rest_4_), channel_id=1, source_target_pairs={{4,0},{8,4},{12,8},{14,12},{10,14},{6,10},{2,6},{0,2},{5,1},{9,5},... | collective-permute-start | bytes 786440 | tf_op jit(solution)/shard_map/ppermute | solution.py:336
  37.1 1.2 %copy-done.1 = bf16[64,8192]{1,0:T(8,128)(2,1)S(1)} copy-done((bf16[64,8192]{1,0:T(8,128)(2,1)S(1)}, bf16[64,8192]{1,0:T(8,128)(2,1)}, u32[]{:S(2)}) %copy-start.1) | copy-done | bytes 1048600
  40.6 9.1 %shard_map.95 = (f32[16,1024]{1,0:T(8,128)S(1)}, bf16[1024,8192]{1,0:T(8,128)(2,1)S(1)}) custom-call(s32[1]{0:T(128)} %bitcast.29.base_ref, f32[8]{0:T(128)S(1)} %convert_log_fusion.logs_ref, s32[64]{0:T(128)S(1)} %copy-done.7, s32[16,1024]{1,0:T(8,128)S(1)} %copy-done.2, f32[1,8192]{1,0:T(1,128)S(1)} %bitcast.34, bf16[64,8192]{1,0:T(8,128)(2,1)S(1)} %copy-done.1, ...), custom_call_target="tpu_custom_call" | custom-call | flops 4294967296 | bytes 16777216 | tf_op jit(solution)/shard_map/pallas_call | solution.py:165
  50.7 1.3 %collective-permute-start.21 = (bf16[32,4224]{1,0:T(8,128)(2,1)S(1)}, bf16[32,4224]{1,0:T(8,128)(2,1)S(1)}, u32[]{:S(2)}, u32[]{:S(2)}) collective-permute-start(bf16[32,4224]{1,0:T(8,128)(2,1)S(1)} %collective-permute-done.13.rest_5_), channel_id=1, source_target_pairs={{4,0},{8,4},{12,8},{14,12},{10,14},{6,10},{2,6},{0,2},{5,1},{9,5},... | collective-permute-start | bytes 811016 | tf_op jit(solution)/shard_map/ppermute | solution.py:336
  52.1 8.8 %shard_map.97.state_ref = f32[16,1024]{1,0:T(8,128)S(1)} custom-call(s32[4]{0:T(128)S(1)} %pad_add_fusion.3.base_ref, f32[8]{0:T(128)S(1)} %convert_log_fusion.logs_ref, s32[16,1024]{1,0:T(8,128)S(1)} %copy-done.3, f32[16,1024]{1,0:T(8,128)S(1)} %get-tuple-element.9.state_ref, f32[1,8192]{1,0:T(1,128)S(1)} %bitcast.35, ...), custom_call_target="tpu_custom_call" | custom-call | flops 4294967296 | bytes 16777216 | tf_op jit(solution)/shard_map/pallas_call | solution.py:226
  63.5 8.8 %shard_map.98.state_ref = f32[16,1024]{1,0:T(8,128)S(1)} custom-call(s32[4]{0:T(128)S(1)} %pad_add_fusion.2.base_ref, f32[8]{0:T(128)S(1)} %convert_log_fusion.logs_ref, s32[16,1024]{1,0:T(8,128)S(1)} %copy-done.3, f32[16,1024]{1,0:T(8,128)S(1)} %shard_map.97.state_ref, f32[1,8192]{1,0:T(1,128)S(1)} %bitcast.36, ...), custom_call_target="tpu_custom_call" | custom-call | flops 4294967296 | bytes 16777216 | tf_op jit(solution)/shard_map/pallas_call | solution.py:226
  73.0 8.8 %shard_map.99.state_ref = f32[16,1024]{1,0:T(8,128)S(1)} custom-call(s32[4]{0:T(128)S(1)} %pad_add_fusion.1.base_ref, f32[8]{0:T(128)S(1)} %convert_log_fusion.logs_ref, s32[16,1024]{1,0:T(8,128)S(1)} %copy-done.3, f32[16,1024]{1,0:T(8,128)S(1)} %shard_map.98.state_ref, f32[1,8192]{1,0:T(1,128)S(1)} %bitcast.37, ...), custom_call_target="tpu_custom_call" | custom-call | flops 4294967296 | bytes 16777216 | tf_op jit(solution)/shard_map/pallas_call | solution.py:226
  81.8 7.6 %shard_map.100.state_ref = f32[16,1024]{1,0:T(8,128)S(1)} custom-call(s32[2]{0:T(128)S(1)} %pad_add_fusion.base_ref, f32[8]{0:T(128)S(1)} %convert_log_fusion.logs_ref, s32[16,1024]{1,0:T(8,128)S(1)} %copy-done.3, f32[16,1024]{1,0:T(8,128)S(1)} %shard_map.99.state_ref, f32[1,8192]{1,0:T(1,128)S(1)} %bitcast.38, ...), custom_call_target="tpu_custom_call" | custom-call | flops 4294967296 | bytes 16777216 | tf_op jit(solution)/shard_map/pallas_call | solution.py:226
  89.4 3.4 %shard_map.101 = (f32[1,1024]{1,0:T(1,128)}, f32[8,4,1152]{2,1,0:T(4,128)S(1)}, f32[8,4,1152]{2,1,0:T(4,128)S(1)}) custom-call(s32[1]{0:T(128)} %bitcast.core_ref.own_ref, f32[16,1024]{1,0:T(8,128)S(1)} %shard_map.100.state_ref, bf16[1024,8192]{1,0:T(8,128)(2,1)S(1)} %get-tuple-element.10.part_ref), custom_call_target="tpu_custom_call" | custom-call | flops 2147483648 | bytes 16777216 | tf_op jit(solution)/shard_map/pallas_call | solution.py:275
  94.3 2.3 %collective-permute-start.29 = (f32[4,4,1152]{2,1,0:T(4,128)S(1)}, f32[4,4,1152]{2,1,0:T(4,128)S(1)}, u32[]{:S(2)}, u32[]{:S(2)}) collective-permute-start(f32[4,4,1152]{2,1,0:T(4,128)S(1)} %constant_dynamic-slice_fusion.2), channel_id=1, source_target_pairs={{0,8},{2,10},{4,12},{6,14},{8,0},{10,2},{12,4},{14,6},{1,9},{3,11}... | collective-permute-start | bytes 221192 | tf_op jit(solution)/shard_map/ppermute | solution.py:299
  96.6 4.8 %collective-permute-done.29 = f32[4,4,1152]{2,1,0:T(4,128)S(1)} collective-permute-done((f32[4,4,1152]{2,1,0:T(4,128)S(1)}, f32[4,4,1152]{2,1,0:T(4,128)S(1)}, u32[]{:S(2)}, u32[]{:S(2)}) %collective-permute-start.29) | collective-permute-done | bytes 73760 | tf_op jit(solution)/shard_map/ppermute | solution.py:299
  101.8 3.6 %collective-permute-done.30 = f32[2,4,1152]{2,1,0:T(4,128)S(1)} collective-permute-done((f32[2,4,1152]{2,1,0:T(4,128)S(1)}, f32[2,4,1152]{2,1,0:T(4,128)S(1)}, u32[]{:S(2)}, u32[]{:S(2)}) %collective-permute-start.30) | collective-permute-done | bytes 36896 | tf_op jit(solution)/shard_map/ppermute | solution.py:299
  105.5 2.3 %collective-permute-start.31 = (f32[1,4,1152]{2,1,0:T(4,128)S(1)}, f32[1,4,1152]{2,1,0:T(4,128)S(1)}, u32[]{:S(2)}, u32[]{:S(2)}) collective-permute-start(f32[1,4,1152]{2,1,0:T(4,128)S(1)} %constant_dynamic-slice_fusion), channel_id=1, source_target_pairs={{0,2},{2,0},{4,6},{6,4},{8,10},{10,8},{12,14},{14,12},{1,3},{3,1},... | collective-permute-start | bytes 55304 | tf_op jit(solution)/shard_map/ppermute | solution.py:299
  107.8 1.7 %collective-permute-done.31 = f32[1,4,1152]{2,1,0:T(4,128)S(1)} collective-permute-done((f32[1,4,1152]{2,1,0:T(4,128)S(1)}, f32[1,4,1152]{2,1,0:T(4,128)S(1)}, u32[]{:S(2)}, u32[]{:S(2)}) %collective-permute-start.31) | collective-permute-done | bytes 18464 | tf_op jit(solution)/shard_map/ppermute | solution.py:299
  (82 shorter events, 13.2 us)
Async XLA Ops:
  3.1 13.3 %collective-permute-start = (bf16[32,4096]{1,0:T(8,128)(2,1)S(1)}, bf16[32,4096]{1,0:T(8,128)(2,1)S(1)}, u32[]{:S(2)}, u32[]{:S(2)}) collective-permute-start(bf16[32,4096]{1,0:T(8,128)(2,1)S(1)} %get-tuple-element.11), channel_id=1, source_target_pairs={{0,4},{4,8},{8,12},{12,14},{14,10},{10,6},{6,2},{2,0},{1,5},{5,9},... | collective-permute-start | bytes 786440 | tf_op jit(solution)/shard_map/ppermute | solution.py:336
  6.2 10.3 %collective-permute-start.4 = (bf16[32,4096]{1,0:T(8,128)(2,1)S(1)}, bf16[32,4096]{1,0:T(8,128)(2,1)S(1)}, u32[]{:S(2)}, u32[]{:S(2)}) collective-permute-start(bf16[32,4096]{1,0:T(8,128)(2,1)S(1)} %get-tuple-element.11), channel_id=1, source_target_pairs={{4,0},{8,4},{12,8},{14,12},{10,14},{6,10},{2,6},{0,2},{5,1},{9,5},... | collective-permute-start | bytes 786440 | tf_op jit(solution)/shard_map/ppermute | solution.py:336
  6.2 16.7 %collective-permute-start.1 = (bf16[32,4224]{1,0:T(8,128)(2,1)S(1)}, bf16[32,4224]{1,0:T(8,128)(2,1)S(1)}, u32[]{:S(2)}, u32[]{:S(2)}) collective-permute-start(bf16[32,4224]{1,0:T(8,128)(2,1)S(1)} %get-tuple-element.12), channel_id=1, source_target_pairs={{0,4},{4,8},{8,12},{12,14},{14,10},{10,6},{6,2},{2,0},{1,5},{5,9},... | collective-permute-start | bytes 811016 | tf_op jit(solution)/shard_map/ppermute | solution.py:336
  8.2 14.7 %collective-permute-start.5 = (bf16[32,4224]{1,0:T(8,128)(2,1)S(1)}, bf16[32,4224]{1,0:T(8,128)(2,1)S(1)}, u32[]{:S(2)}, u32[]{:S(2)}) collective-permute-start(bf16[32,4224]{1,0:T(8,128)(2,1)S(1)} %get-tuple-element.12), channel_id=1, source_target_pairs={{4,0},{8,4},{12,8},{14,12},{10,14},{6,10},{2,6},{0,2},{5,1},{9,5},... | collective-permute-start | bytes 811016 | tf_op jit(solution)/shard_map/ppermute | solution.py:336
  20.9 9.1 %collective-permute-start.8 = (bf16[32,4096]{1,0:T(8,128)(2,1)S(1)}, bf16[32,4096]{1,0:T(8,128)(2,1)S(1)}, u32[]{:S(2)}, u32[]{:S(2)}) collective-permute-start(bf16[32,4096]{1,0:T(8,128)(2,1)S(1)} %collective-permute-done.rest_0_), channel_id=1, source_target_pairs={{0,4},{4,8},{8,12},{12,14},{14,10},{10,6},{6,2},{2,0},{1,5},{5,9},... | collective-permute-start | bytes 786440 | tf_op jit(solution)/shard_map/ppermute | solution.py:336
  22.9 9.1 %collective-permute-start.12 = (bf16[32,4096]{1,0:T(8,128)(2,1)S(1)}, bf16[32,4096]{1,0:T(8,128)(2,1)S(1)}, u32[]{:S(2)}, u32[]{:S(2)}) collective-permute-start(bf16[32,4096]{1,0:T(8,128)(2,1)S(1)} %collective-permute-done.4.rest_4_), channel_id=1, source_target_pairs={{4,0},{8,4},{12,8},{14,12},{10,14},{6,10},{2,6},{0,2},{5,1},{9,5},... | collective-permute-start | bytes 786440 | tf_op jit(solution)/shard_map/ppermute | solution.py:336
  22.9 9.1 %collective-permute-start.3 = (bf16[32,4224]{1,0:T(8,128)(2,1)S(1)}, bf16[32,4224]{1,0:T(8,128)(2,1)S(1)}, u32[]{:S(2)}, u32[]{:S(2)}) collective-permute-start(bf16[32,4224]{1,0:T(8,128)(2,1)S(1)} %collective-permute-done.1.rest_1_), channel_id=1, source_target_pairs={{0,1},{1,0},{2,3},{3,2},{4,5},{5,4},{6,7},{7,6},{8,9},{9,8},{10,11... | collective-permute-start | bytes 811016 | tf_op jit(solution)/shard_map/ppermute | solution.py:337
  23.0 12.4 %collective-permute-start.9 = (bf16[32,4224]{1,0:T(8,128)(2,1)S(1)}, bf16[32,4224]{1,0:T(8,128)(2,1)S(1)}, u32[]{:S(2)}, u32[]{:S(2)}) collective-permute-start(bf16[32,4224]{1,0:T(8,128)(2,1)S(1)} %collective-permute-done.1.rest_1_), channel_id=1, source_target_pairs={{0,4},{4,8},{8,12},{12,14},{14,10},{10,6},{6,2},{2,0},{1,5},{5,9},... | collective-permute-start | bytes 811016 | tf_op jit(solution)/shard_map/ppermute | solution.py:336
  30.0 19.6 %collective-permute-start.13 = (bf16[32,4224]{1,0:T(8,128)(2,1)S(1)}, bf16[32,4224]{1,0:T(8,128)(2,1)S(1)}, u32[]{:S(2)}, u32[]{:S(2)}) collective-permute-start(bf16[32,4224]{1,0:T(8,128)(2,1)S(1)} %collective-permute-done.5.rest_5_), channel_id=1, source_target_pairs={{4,0},{8,4},{12,8},{14,12},{10,14},{6,10},{2,6},{0,2},{5,1},{9,5},... | collective-permute-start | bytes 811016 | tf_op jit(solution)/shard_map/ppermute | solution.py:336
  32.0 17.7 %collective-permute-start.10 = (bf16[32,4096]{1,0:T(8,128)(2,1)S(1)}, bf16[32,4096]{1,0:T(8,128)(2,1)S(1)}, u32[]{:S(2)}, u32[]{:S(2)}) collective-permute-start(bf16[32,4096]{1,0:T(8,128)(2,1)S(1)} %collective-permute-done.8.rest_0_), channel_id=1, source_target_pairs={{0,1},{1,0},{2,3},{3,2},{4,5},{5,4},{6,7},{7,6},{8,9},{9,8},{10,11... | collective-permute-start | bytes 786440 | tf_op jit(solution)/shard_map/ppermute | solution.py:337
  32.0 18.7 %collective-permute-start.16 = (bf16[32,4096]{1,0:T(8,128)(2,1)S(1)}, bf16[32,4096]{1,0:T(8,128)(2,1)S(1)}, u32[]{:S(2)}, u32[]{:S(2)}) collective-permute-start(bf16[32,4096]{1,0:T(8,128)(2,1)S(1)} %collective-permute-done.8.rest_0_), channel_id=1, source_target_pairs={{0,4},{4,8},{8,12},{12,14},{14,10},{10,6},{6,2},{2,0},{1,5},{5,9},... | collective-permute-start | bytes 786440 | tf_op jit(solution)/shard_map/ppermute | solution.py:336
  32.5 18.1 %collective-permute-start.14 = (bf16[32,4096]{1,0:T(8,128)(2,1)S(1)}, bf16[32,4096]{1,0:T(8,128)(2,1)S(1)}, u32[]{:S(2)}, u32[]{:S(2)}) collective-permute-start(bf16[32,4096]{1,0:T(8,128)(2,1)S(1)} %collective-permute-done.12.rest_4_), channel_id=1, source_target_pairs={{0,1},{1,0},{2,3},{3,2},{4,5},{5,4},{6,7},{7,6},{8,9},{9,8},{10,11... | collective-permute-start | bytes 786440 | tf_op jit(solution)/shard_map/ppermute | solution.py:337
  35.4 16.6 %collective-permute-start.20 = (bf16[32,4096]{1,0:T(8,128)(2,1)S(1)}, bf16[32,4096]{1,0:T(8,128)(2,1)S(1)}, u32[]{:S(2)}, u32[]{:S(2)}) collective-permute-start(bf16[32,4096]{1,0:T(8,128)(2,1)S(1)} %collective-permute-done.12.rest_4_), channel_id=1, source_target_pairs={{4,0},{8,4},{12,8},{14,12},{10,14},{6,10},{2,6},{0,2},{5,1},{9,5},... | collective-permute-start | bytes 786440 | tf_op jit(solution)/shard_map/ppermute | solution.py:336
  49.6 11.2 %collective-permute-start.11 = (bf16[32,4224]{1,0:T(8,128)(2,1)S(1)}, bf16[32,4224]{1,0:T(8,128)(2,1)S(1)}, u32[]{:S(2)}, u32[]{:S(2)}) collective-permute-start(bf16[32,4224]{1,0:T(8,128)(2,1)S(1)} %collective-permute-done.9.rest_1_), channel_id=1, source_target_pairs={{0,1},{1,0},{2,3},{3,2},{4,5},{5,4},{6,7},{7,6},{8,9},{9,8},{10,11... | collective-permute-start | bytes 811016 | tf_op jit(solution)/shard_map/ppermute | solution.py:337
  49.7 12.8 %collective-permute-start.17 = (bf16[32,4224]{1,0:T(8,128)(2,1)S(1)}, bf16[32,4224]{1,0:T(8,128)(2,1)S(1)}, u32[]{:S(2)}, u32[]{:S(2)}) collective-permute-start(bf16[32,4224]{1,0:T(8,128)(2,1)S(1)} %collective-permute-done.9.rest_1_), channel_id=1, source_target_pairs={{0,4},{4,8},{8,12},{12,14},{14,10},{10,6},{6,2},{2,0},{1,5},{5,9},... | collective-permute-start | bytes 811016 | tf_op jit(solution)/shard_map/ppermute | solution.py:336
  50.5 11.5 %collective-permute-start.15 = (bf16[32,4224]{1,0:T(8,128)(2,1)S(1)}, bf16[32,4224]{1,0:T(8,128)(2,1)S(1)}, u32[]{:S(2)}, u32[]{:S(2)}) collective-permute-start(bf16[32,4224]{1,0:T(8,128)(2,1)S(1)} %collective-permute-done.13.rest_5_), channel_id=1, source_target_pairs={{0,1},{1,0},{2,3},{3,2},{4,5},{5,4},{6,7},{7,6},{8,9},{9,8},{10,11... | collective-permute-start | bytes 811016 | tf_op jit(solution)/shard_map/ppermute | solution.py:337
  50.7 11.3 %collective-permute-start.21 = (bf16[32,4224]{1,0:T(8,128)(2,1)S(1)}, bf16[32,4224]{1,0:T(8,128)(2,1)S(1)}, u32[]{:S(2)}, u32[]{:S(2)}) collective-permute-start(bf16[32,4224]{1,0:T(8,128)(2,1)S(1)} %collective-permute-done.13.rest_5_), channel_id=1, source_target_pairs={{4,0},{8,4},{12,8},{14,12},{10,14},{6,10},{2,6},{0,2},{5,1},{9,5},... | collective-permute-start | bytes 811016 | tf_op jit(solution)/shard_map/ppermute | solution.py:336
  52.0 11.5 %collective-permute-start.18 = (bf16[32,4096]{1,0:T(8,128)(2,1)S(1)}, bf16[32,4096]{1,0:T(8,128)(2,1)S(1)}, u32[]{:S(2)}, u32[]{:S(2)}) collective-permute-start(bf16[32,4096]{1,0:T(8,128)(2,1)S(1)} %collective-permute-done.16.rest_0_), channel_id=1, source_target_pairs={{0,1},{1,0},{2,3},{3,2},{4,5},{5,4},{6,7},{7,6},{8,9},{9,8},{10,11... | collective-permute-start | bytes 786440 | tf_op jit(solution)/shard_map/ppermute | solution.py:337
  60.9 11.4 %collective-permute-start.24 = (bf16[32,4096]{1,0:T(8,128)(2,1)S(1)}, bf16[32,4096]{1,0:T(8,128)(2,1)S(1)}, u32[]{:S(2)}, u32[]{:S(2)}) collective-permute-start(bf16[32,4096]{1,0:T(8,128)(2,1)S(1)} %collective-permute-done.16.rest_0_), channel_id=1, source_target_pairs={{0,4},{4,8},{8,12},{12,14},{14,10},{10,6},{6,2},{2,0},{1,5},{5,9},... | collective-permute-start | bytes 786440 | tf_op jit(solution)/shard_map/ppermute | solution.py:336
  62.0 10.9 %collective-permute-start.22 = (bf16[32,4096]{1,0:T(8,128)(2,1)S(1)}, bf16[32,4096]{1,0:T(8,128)(2,1)S(1)}, u32[]{:S(2)}, u32[]{:S(2)}) collective-permute-start(bf16[32,4096]{1,0:T(8,128)(2,1)S(1)} %collective-permute-done.20.rest_4_), channel_id=1, source_target_pairs={{0,1},{1,0},{2,3},{3,2},{4,5},{5,4},{6,7},{7,6},{8,9},{9,8},{10,11... | collective-permute-start | bytes 786440 | tf_op jit(solution)/shard_map/ppermute | solution.py:337
  62.1 10.9 %collective-permute-start.23 = (bf16[32,4224]{1,0:T(8,128)(2,1)S(1)}, bf16[32,4224]{1,0:T(8,128)(2,1)S(1)}, u32[]{:S(2)}, u32[]{:S(2)}) collective-permute-start(bf16[32,4224]{1,0:T(8,128)(2,1)S(1)} %collective-permute-done.21.rest_5_), channel_id=1, source_target_pairs={{0,1},{1,0},{2,3},{3,2},{4,5},{5,4},{6,7},{7,6},{8,9},{9,8},{10,11... | collective-permute-start | bytes 811016 | tf_op jit(solution)/shard_map/ppermute | solution.py:337
  62.6 10.3 %collective-permute-start.25 = (bf16[32,4224]{1,0:T(8,128)(2,1)S(1)}, bf16[32,4224]{1,0:T(8,128)(2,1)S(1)}, u32[]{:S(2)}, u32[]{:S(2)}) collective-permute-start(bf16[32,4224]{1,0:T(8,128)(2,1)S(1)} %collective-permute-done.21.rest_5_), channel_id=1, source_target_pairs={{4,0},{8,4},{12,8},{14,12},{10,14},{6,10},{2,6},{0,2},{5,1},{9,5},... | collective-permute-start | bytes 811016 | tf_op jit(solution)/shard_map/ppermute | solution.py:336
  63.5 9.5 %collective-permute-start.19 = (bf16[32,4224]{1,0:T(8,128)(2,1)S(1)}, bf16[32,4224]{1,0:T(8,128)(2,1)S(1)}, u32[]{:S(2)}, u32[]{:S(2)}) collective-permute-start(bf16[32,4224]{1,0:T(8,128)(2,1)S(1)} %collective-permute-done.17.rest_1_), channel_id=1, source_target_pairs={{0,1},{1,0},{2,3},{3,2},{4,5},{5,4},{6,7},{7,6},{8,9},{9,8},{10,11... | collective-permute-start | bytes 811016 | tf_op jit(solution)/shard_map/ppermute | solution.py:337
  72.3 9.5 %collective-permute-start.26 = (bf16[32,4096]{1,0:T(8,128)(2,1)S(1)}, bf16[32,4096]{1,0:T(8,128)(2,1)S(1)}, u32[]{:S(2)}, u32[]{:S(2)}) collective-permute-start(bf16[32,4096]{1,0:T(8,128)(2,1)S(1)} %collective-permute-done.24.rest_0_), channel_id=1, source_target_pairs={{0,1},{1,0},{2,3},{3,2},{4,5},{5,4},{6,7},{7,6},{8,9},{9,8},{10,11... | collective-permute-start | bytes 786440 | tf_op jit(solution)/shard_map/ppermute | solution.py:337
  (17 other events, 180.4 us)

commit v3 on v2

v3 whole, which is shorter than its diff:
```python
import functools

import jax
import jax.numpy as jnp
from jax import lax
from jax.experimental import pallas as pl
from jax.experimental.pallas import tpu as pltpu
from jax.sharding import PartitionSpec as P

LOWEST = -1e30
STEPS = 8
WIDTH = 1024
LANES = 128
STATE_ROWS = 8
VMEM_LIMIT = 16 * 1024 * 1024


def ring_order(blocks):
    if blocks <= 8:
        return list(range(0, blocks, 2)) + list(range(blocks - 1, 0, -2))
    return list(range(blocks))


def message_kernel(tags_ref, rows_ref, first_ref, second_ref, sent):
    height, span = first_ref.shape
    copies = [
        pltpu.make_async_copy(rows_ref.at[:, :span], first_ref, sent.at[0]),
        pltpu.make_async_copy(rows_ref.at[:, span:], second_ref.at[:, :span], sent.at[1]),
    ]
    for copy in copies:
        copy.start()
    second_ref[:, span:] = tag_rows(tags_ref, height).astype(jnp.bfloat16)
    for copy in copies:
        copy.wait()


def make_messages(template_class, templates):
    height, freqs = templates.shape
    span = freqs // 2
    return pl.pallas_call(
        message_kernel,
        in_specs=[in_smem(), pl.BlockSpec(memory_space=pl.ANY)],
        out_specs=[in_vmem(), in_vmem()],
        out_shape=[
            pltpu.VMEM((height, span), jnp.bfloat16),
            pltpu.VMEM((height, span + LANES), jnp.bfloat16),
        ],
        scratch_shapes=[pltpu.SemaphoreType.DMA((2,))],
        compiler_params=pltpu.CompilerParams(vmem_limit_bytes=VMEM_LIMIT),
    )(
        pltpu.with_memory_space_constraint(template_class, pltpu.HBM),
        pltpu.with_memory_space_constraint(templates, pltpu.HBM),
    )


def tag_rows(tags_ref, height):
    row = lax.broadcasted_iota(jnp.int32, (height, LANES), 0)
    tags = jnp.zeros((height, LANES), jnp.float32)
    for r in range(height):
        tags = jnp.where(row == r, tags_ref[r].astype(jnp.float32), tags)
    return tags


def in_smem():
    return pl.BlockSpec(memory_space=pltpu.SMEM)


def in_vmem():
    return pl.BlockSpec(memory_space=pltpu.VMEM)


def add_scores(rows, noise, part, acc, energy):
    widened = rows.astype(jnp.float32)
    product = widened * noise
    square = product * widened
    folded = square[:, :LANES]
    for lane in range(LANES, square.shape[1], LANES):
        folded = folded + square[:, lane : lane + LANES]
    energy[...] += folded
    acc[...] += lax.dot_general(
        part,
        product.astype(jnp.bfloat16),
        (((1,), (1,)), ((), ())),
        preferred_element_type=jnp.float32,
    )


def add_rows(tags, ids, logs_ref, sig_ref, state, acc, energy):
    classes = logs_ref.shape[0]
    prior = jnp.zeros_like(tags[:, :1])
    for tag in range(classes):
        prior = jnp.where(tags[:, :1] == tag, logs_ref[tag], prior)
    bias = prior - 0.5 * jnp.sum(energy[...], axis=1, keepdims=True)
    scores = jnp.transpose(acc[...]) + bias
    old_max, old_sum, old_top, weights = state
    new_max = jnp.maximum(old_max, jnp.max(scores, axis=0, keepdims=True))
    new_sum = old_sum * jnp.exp(old_max - new_max) + jnp.sum(
        jnp.exp(scores - new_max), axis=0, keepdims=True
    )
    hit = sig_ref[0:1, :] == ids
    for pick in range(1, sig_ref.shape[0]):
        hit = hit | (sig_ref[pick : pick + 1, :] == ids)
    new_top = jnp.maximum(
        old_top, jnp.max(jnp.where(hit, scores, LOWEST), axis=0, keepdims=True)
    )
    value = jnp.where(hit, jnp.exp(scores - new_top), 0.0)
    lane = lax.broadcasted_iota(jnp.int32, tags.shape, 1).astype(jnp.float32)
    onehot = jnp.transpose(jnp.where(tags == lane, 1.0, 0.0))[:classes, :].astype(jnp.bfloat16)
    weights = weights * jnp.exp(old_top - new_top)
    left = value
    for _ in range(3):
        piece = left.astype(jnp.bfloat16)
        left = left - piece.astype(jnp.float32)
        weights = weights + jnp.dot(onehot, piece, preferred_element_type=jnp.float32)
    return new_max, new_sum, new_top, weights


def put_state(state, out_ref):
    new_max, new_sum, new_top, weights = state
    out_ref[0:1, :] = new_max
    out_ref[1:2, :] = new_sum
    out_ref[2:3, :] = new_top
    out_ref[3:STATE_ROWS, :] = jnp.zeros_like(out_ref[3:STATE_ROWS, :])
    out_ref[STATE_ROWS:, :] = weights


def get_state(state_ref):
    return state_ref[0:1, :], state_ref[1:2, :], state_ref[2:3, :], state_ref[STATE_ROWS:, :]


def own_kernel(
    where_ref, logs_ref, tags_ref, sig_ref, noise_ref, tmpl_ref, far_ref,
    out_ref, near_ref, acc, energy, arrived,
):
    freqs = noise_ref.shape[1]
    height = tmpl_ref.shape[0]
    width = freqs // STEPS

    def copy(step):
        columns = pl.ds(pl.multiple_of(step * width, width), width)
        return pltpu.make_async_copy(
            far_ref.at[:, columns], near_ref.at[:, columns], arrived.at[step]
        )

    for step in range(STEPS):
        copy(step).start()
    acc[...] = jnp.zeros_like(acc)
    energy[...] = jnp.zeros_like(energy)

    @pl.loop(0, STEPS)
    def _(step):
        copy(step).wait()
        columns = pl.ds(pl.multiple_of(step * width, width), width)
        add_scores(
            tmpl_ref[:, columns], noise_ref[:, columns], near_ref[:, columns], acc, energy
        )

    tags = tag_rows(tags_ref, height)
    ids = where_ref[0] * height + lax.broadcasted_iota(jnp.int32, (height, 1), 0)
    lowest = jnp.full((1, acc.shape[0]), LOWEST, jnp.float32)
    none = jnp.zeros((1, acc.shape[0]), jnp.float32)
    weights = jnp.zeros((logs_ref.shape[0], acc.shape[0]), jnp.float32)
    state = (lowest, none, lowest, weights)
    put_state(add_rows(tags, ids, logs_ref, sig_ref, state, acc, energy), out_ref)


def score_own(where, logs, template_class, significant, noise, templates, particles):
    per_device, freqs = particles.shape
    height = templates.shape[0]
    rows = STATE_ROWS + logs.shape[0]
    return pl.pallas_call(
        own_kernel,
        in_specs=[in_smem()] * 3 + [in_vmem()] * 3 + [pl.BlockSpec(memory_space=pl.ANY)],
        out_specs=[in_vmem(), in_vmem()],
        out_shape=[
            jax.ShapeDtypeStruct((rows, per_device), jnp.float32),
            pltpu.VMEM(particles.shape, particles.dtype),
        ],
        scratch_shapes=[
            pltpu.VMEM((per_device, height), jnp.float32),
            pltpu.VMEM((height, LANES), jnp.float32),
            pltpu.SemaphoreType.DMA((STEPS,)),
        ],
        compiler_params=pltpu.CompilerParams(vmem_limit_bytes=VMEM_LIMIT),
        cost_estimate=pl.CostEstimate(
            flops=4 * 128 * per_device * freqs,
            bytes_accessed=2 * per_device * freqs,
            transcendentals=0,
        ),
    )(
        where,
        logs,
        *(
            pltpu.with_memory_space_constraint(x, pltpu.HBM)
            for x in (template_class, significant, noise, templates, particles)
        ),
    )


def ring_kernel(phase, ends, sources, where_ref, noise_ref, part_ref, own_ref, sib_ref, *rest):
    if phase == 0:
        acc, energy = rest
        acc[...] = jnp.zeros_like(acc)
        energy[...] = jnp.zeros_like(energy)
    else:
        acc_in, energy_in, logs_ref, sig_ref, state_ref, out_ref, acc, energy = rest
        acc[...] = acc_in[...]
        energy[...] = energy_in[...]
    freqs = noise_ref.shape[1]
    span = freqs // 4 if ends else freqs // 2
    core = where_ref[1]
    low = phase * (freqs // 2)
    if ends:
        pieces = [((own_ref,), low + core * span), ((sib_ref,), low + (1 - core) * span)]
    else:
        pieces = [((own_ref, sib_ref), low)]
    for refs, start in pieces:

        @pl.loop(0, span // WIDTH)
        def _(step):
            near = pl.ds(pl.multiple_of(step * WIDTH, WIDTH), WIDTH)
            columns = pl.ds(pl.multiple_of(start + step * WIDTH, WIDTH), WIDTH)
            rows = jnp.concatenate([ref[:, near] for ref in refs], axis=0)
            add_scores(rows, noise_ref[:, columns], part_ref[:, columns], acc, energy)

    if phase == 0:
        return
    height = own_ref.shape[0]
    tags = [ref[:, span:].astype(jnp.float32) for ref in (own_ref, sib_ref)]
    tags = jnp.where(core == 0, tags[1], tags[0]) if ends else jnp.concatenate(tags, axis=0)
    found = []
    for table in sources:
        source = jnp.int32(table[0])
        for block in range(1, len(table)):
            source = jnp.where(where_ref[0] == block, table[block], source)
        found.append(source)
    row = lax.broadcasted_iota(jnp.int32, (height, 1), 0)
    if ends:
        ids = found[0] * height + row
    else:
        own = jnp.where(core == 0, found[0], found[1])
        sib = jnp.where(core == 0, found[1], found[0])
        ids = jnp.concatenate([own * height + row, sib * height + row], axis=0)
    state = add_rows(tags, ids, logs_ref, sig_ref, get_state(state_ref), acc, energy)
    put_state(state, out_ref)


def ring_scores(phase, ends, sources, where, noise, particles, own, sib, rest):
    per_device, freqs = particles.shape
    rows = own.shape[0] * (1 if ends else 2)
    sums = [
        jax.ShapeDtypeStruct((per_device, rows), jnp.float32),
        jax.ShapeDtypeStruct((rows, LANES), jnp.float32),
    ]
    params = {}
    if phase == 0:
        params.update(out_specs=[in_vmem(), in_vmem()], out_shape=sums)
        rest_specs = []
    else:
        state = jax.ShapeDtypeStruct(rest[-1].shape, jnp.float32)
        scratch = [pltpu.VMEM(array.shape, array.dtype) for array in sums]
        params.update(out_specs=in_vmem(), out_shape=state, scratch_shapes=scratch)
        rest_specs = [in_vmem(), in_vmem(), in_smem(), in_vmem(), in_vmem()]
    return pl.pallas_call(
        functools.partial(ring_kernel, phase, ends, sources),
        in_specs=[in_smem()] + [in_vmem()] * 4 + rest_specs,
        compiler_params=pltpu.CompilerParams(vmem_limit_bytes=VMEM_LIMIT),
        cost_estimate=pl.CostEstimate(
            flops=2 * 128 * per_device * freqs,
            bytes_accessed=per_device * freqs,
            transcendentals=0,
        ),
        **params,
    )(
        where,
        noise,
        pltpu.with_memory_space_constraint(particles, pltpu.VMEM),
        own,
        sib,
        *rest,
    )


def sums_kernel(own_ref, state_ref, part_ref, loglik_ref, mine_ref, theirs_ref):
    blocks, per_owner = mine_ref.shape[:2]
    width = part_ref.shape[1] // blocks
    _, _, _, weights = get_state(state_ref)
    loglik_ref[...] = state_ref[0:1, :] + jnp.log(state_ref[1:2, :])
    weights = weights / jnp.sum(weights, axis=0, keepdims=True)
    turned = jnp.concatenate([weights[per_owner:], weights[:per_owner]], axis=0)
    weights = jnp.where(own_ref[0] == 0, weights, turned)
    rounded = weights.astype(jnp.bfloat16)
    total = jnp.broadcast_to(
        jnp.sum(weights, axis=1, keepdims=True), (weights.shape[0], LANES)
    )

    @pl.loop(0, blocks)
    def _(block):
        columns = pl.ds(pl.multiple_of(block * width, width), width)
        sums = jnp.dot(rounded, part_ref[:, columns], preferred_element_type=jnp.float32)
        mine_ref[block, :, :width] = sums[:per_owner]
        theirs_ref[block, :, :width] = sums[per_owner:]
        mine_ref[block, :, width:] = total[:per_owner]
        theirs_ref[block, :, width:] = total[per_owner:]


def class_sums(own, state, particles, blocks, classes, owners):
    per_device, freqs = particles.shape
    width = freqs // blocks
    per_owner = classes // owners
    piece = jax.ShapeDtypeStruct((blocks, per_owner, width + LANES), jnp.float32)
    return pl.pallas_call(
        sums_kernel,
        in_specs=[in_smem(), in_vmem(), in_vmem()],
        out_specs=[in_vmem()] * 3,
        out_shape=[jax.ShapeDtypeStruct((1, per_device), jnp.float32), piece, piece],
        compiler_params=pltpu.CompilerParams(vmem_limit_bytes=VMEM_LIMIT),
        cost_estimate=pl.CostEstimate(
            flops=2 * 128 * per_device * freqs,
            bytes_accessed=2 * per_device * freqs,
            transcendentals=0,
        ),
    )(own, state, pltpu.with_memory_space_constraint(particles, pltpu.VMEM))


def scatter_sum(pieces, blocks, block_id):
    if blocks & (blocks - 1):
        pieces = lax.all_to_all(pieces, "blk", split_axis=0, concat_axis=0, tiled=True)
        return jnp.sum(pieces, axis=0)
    steps = blocks.bit_length() - 1
    tail = pieces.shape[1:]
    for step in range(steps):
        stride = 1 << step
        bit = lax.rem(lax.div(block_id, stride), 2)
        pairs = pieces.reshape((-1, 2) + tail)
        keep = lax.dynamic_index_in_dim(pairs, bit, 1, keepdims=False)
        send = lax.dynamic_index_in_dim(pairs, 1 - bit, 1, keepdims=False)
        swaps = [(i, i ^ stride) for i in range(blocks)]
        pieces = keep + lax.ppermute(send, "blk", swaps)
    return pieces[0]


def body(particles, significant, templates, template_class, class_counts, inv_noise):
    per_device, freqs = particles.shape
    classes = class_counts.shape[0]
    blocks = lax.axis_size("blk")
    owners = lax.axis_size("cls")
    order = ring_order(blocks)
    place = [order.index(block) for block in range(blocks)]
    block_id = lax.axis_index("blk")
    core = lax.axis_index("cls")
    ring = [(2 * order[i], 2 * order[(i + 1) % blocks]) for i in range(blocks)]
    ring += [(2 * order[(i + 1) % blocks] + 1, 2 * order[i] + 1) for i in range(blocks)]
    swap = [(i, owners - 1 - i) for i in range(owners)]

    noise = inv_noise[None, :]
    logs = jnp.log(class_counts.astype(jnp.float32))
    held = make_messages(template_class, templates)
    where = jnp.stack([block_id, core])
    state, near = score_own(
        where, logs, template_class, significant, noise, templates, particles
    )
    last = blocks // 2
    gates = [state]
    for distance in range(1, last + 1):
        ends = distance == last
        sources = [
            tuple(order[(place[block] - sign * distance) % blocks] for block in range(blocks))
            for sign in (1, -1)
        ]
        arrived = []
        sums = ()
        for phase in range(2):
            message = held[phase]
            if ends:
                cut = freqs // 4
                message = lax.dynamic_slice_in_dim(
                    message, core * cut, message.shape[1] - cut, 1
                )
            own = lax.ppermute(message, ("blk", "cls"), ring)
            own, _ = lax.optimization_barrier((own, gates[max(len(gates) - 2, 0)]))
            sib = lax.ppermute(own, "cls", swap)
            rest = () if phase == 0 else (*sums, logs, significant, state)
            sums = ring_scores(phase, ends, sources, where, noise, near, own, sib, rest)
            gates.append(sums)
            if phase == 1:
                state = sums
            arrived.append(own)
        held = arrived

    loglik, mine, theirs = class_sums(core[None], state, near, blocks, classes, owners)
    reduced = mine + lax.ppermute(theirs, "cls", swap)
    total = scatter_sum(reduced, blocks, block_id)
    width = freqs // blocks
    per_owner = classes // owners
    counts = lax.dynamic_slice_in_dim(class_counts, core * per_owner, per_owner, 0)
    class_avg = total[:, :width] / (total[:, width] + counts.astype(jnp.float32))[:, None]
    return loglik[0], class_avg


def solution(mesh):
    placed = (
        P(("grp", "blk", "cls"), None),
        P(None, ("grp", "blk", "cls")),
        P(("grp", "blk"), None),
        P(("grp", "blk")),
        P("grp"),
        P(),
    )
    return jax.shard_map(
        body,
        mesh=mesh,
        in_specs=placed,
        out_specs=(P(("grp", "blk", "cls")), P(("grp", "cls"), "blk")),
        check_vma=False,
    )
```

time: 111 us -> 92.2 us (0.83)
  between operations: 9.79 us -> 0.83 us
  starting transfers between devices: 25.4 us -> 20.5 us
  waiting for transfers between devices: 18 us -> 13.4 us
  Pallas kernels: 47.1 us -> 49.1 us
  local copies, waits for them, and re-layouts: 8.36 us -> 6.46 us
    ppermute x31 -> x19, waiting for transfers between devices: 17 us -> 12.1 us  [the longest x3 8.96 us: scatter_sum(): pieces = keep + lax.ppermute(send, 'blk', swaps)]
    ppermute x31 -> x19, starting transfers between devices: 24.9 us -> 20.5 us  [the longest x8 15.1 us: body(): own = lax.ppermute(message, ('blk', 'cls'), ring)]
    dynamic_slice x5 -> x2, local copies, waits for them, and re-layouts: 2.88 us -> 0.06 us  [body(): lax.dynamic_slice_in_dim(message, core * cut, message.shape[1] - cut, 1)]
    pallas_call x5 -> x9, Pallas kernels: 34.6 us -> 36.2 us  [the longest x8 34.2 us: ring_scores(): pl.pallas_call(functools.partial(ring_kernel, phase, ends, sources), in_s...]
    unnamed x18 -> x12, local copies, waits for them, and re-layouts: 5.36 us -> 6.24 us
  transfers between devices with their start and end apart: 32 -> 20, of which waited for: 6 -> 6; matrix products, arithmetic and copies ran while one was open for 3% -> 1% of each run, Pallas kernels for 32% -> 43%
where the time goes in v3:
time: 92.2 us; the launch traced here: 91.9 us
  Pallas kernels  49.1 us (53%)
  starting transfers between devices  20.5 us (22%)
  waiting for transfers between devices  13.4 us (15%)
  local copies, waits for them, and re-layouts  6.46 us (7%)
  other arithmetic  1.58 us (2%)
    pallas_call x8, Pallas kernels, ring_scores(): pl.pallas_call(functools.partial(ring_kernel, phase, ends, sources), in_s...  34.2 us
    ppermute x8, starting transfers between devices, body(): own = lax.ppermute(message, ('blk', 'cls'), ring)  15.1 us
    pallas_call x1, Pallas kernels, score_own(): pl.pallas_call(own_kernel, in_specs=[in_smem()] * 3 + [in_vmem()] * 3 + [...  9.47 us
    ppermute x3, waiting for transfers between devices, scatter_sum(): pieces = keep + lax.ppermute(send, 'blk', swaps)  8.96 us
    unnamed x12, local copies, waits for them, and re-layouts  6.24 us
    ppermute x3, starting transfers between devices, scatter_sum(): pieces = keep + lax.ppermute(send, 'blk', swaps)  4.21 us
    pallas_call x1, Pallas kernels, class_sums(): pl.pallas_call(sums_kernel, in_specs=[in_smem(), in_vmem(), in_vmem()], o...  3.43 us
    ppermute x8, waiting for transfers between devices, body(): own = lax.ppermute(message, ('blk', 'cls'), ring)  3.08 us
  transfers between devices with their start and end apart: 20, of which 6 were waited for; matrix products, arithmetic and copies ran while one was open for 1% of the time, Pallas kernels for 43%

profile of v3, /device:TPU:0, one launch (start us, length us, event | category | flops | bytes accessed | tf_op | source)
XLA Modules:
  0.0 91.9 jit_solution(5109939288542168452)
XLA Ops:
  0.6 2.0 %shard_map.78 = (bf16[64,4096]{1,0:T(8,128)(2,1)S(1)}, bf16[64,4224]{1,0:T(8,128)(2,1)S(1)}) custom-call(s32[64]{0:T(128)} %tags_ref.3, bf16[64,8192]{1,0:T(8,128)(2,1)} %rows_ref.1), custom_call_target="tpu_custom_call" | custom-call | tf_op jit(solution)/shard_map/pallas_call | solution.py:40
  2.7 3.1 %collective-permute-start = (bf16[64,4224]{1,0:T(8,128)(2,1)S(1)}, bf16[64,4224]{1,0:T(8,128)(2,1)S(1)}, u32[]{:S(2)}, u32[]{:S(2)}) collective-permute-start(bf16[64,4224]{1,0:T(8,128)(2,1)S(1)} %get-tuple-element.26), channel_id=1, source_target_pairs={{0,4},{4,8},{8,12},{12,14},{14,10},{10,6},{6,2},{2,0},{5,1},{9,5},... | collective-permute-start | bytes 1622024 | tf_op jit(solution)/shard_map/ppermute | solution.py:380
  5.7 1.6 %collective-permute-start.3 = (bf16[64,4096]{1,0:T(8,128)(2,1)S(1)}, bf16[64,4096]{1,0:T(8,128)(2,1)S(1)}, u32[]{:S(2)}, u32[]{:S(2)}) collective-permute-start(bf16[64,4096]{1,0:T(8,128)(2,1)S(1)} %get-tuple-element.29), channel_id=1, source_target_pairs={{0,4},{4,8},{8,12},{12,14},{14,10},{10,6},{6,2},{2,0},{5,1},{9,5},... | collective-permute-start | bytes 1572872 | tf_op jit(solution)/shard_map/ppermute | solution.py:380
  8.1 9.5 %shard_map.77 = (f32[16,1024]{1,0:T(8,128)S(1)}, bf16[1024,8192]{1,0:T(8,128)(2,1)S(1)}) custom-call(s32[2]{0:T(128)S(1)} %pad_add_fusion.where_ref, f32[8]{0:T(128)S(1)} %convert_log_fusion.logs_ref.rest_2_, s32[64]{0:T(128)} %tags_ref.3, s32[16,1024]{1,0:T(8,128)} %rest_3_.7, f32[1,8192]{1,0:T(1,128)} %bitcast.16, bf16[64,8192]{1,0:T(8,128)(2,1)} %rows_ref.1, ...), custom_call_target="tpu_custom_call" | custom-call | flops 4294967296 | bytes 16777216 | tf_op jit(solution)/shard_map/pallas_call | solution.py:171
  18.6 2.1 %collective-permute-start.7 = (bf16[64,4096]{1,0:T(8,128)(2,1)S(1)}, bf16[64,4096]{1,0:T(8,128)(2,1)S(1)}, u32[]{:S(2)}, u32[]{:S(2)}) collective-permute-start(bf16[64,4096]{1,0:T(8,128)(2,1)S(1)} %collective-permute-done.3.own_ref), channel_id=1, source_target_pairs={{0,4},{4,8},{8,12},{12,14},{14,10},{10,6},{6,2},{2,0},{5,1},{9,5},... | collective-permute-start | bytes 1572872 | tf_op jit(solution)/shard_map/ppermute | solution.py:380
  22.3 3.5 %shard_map.79 = (f32[1024,128]{1,0:T(8,128)S(1)}, f32[128,128]{1,0:T(8,128)S(1)}) custom-call(s32[2]{0:T(128)S(1)} %pad_add_fusion.where_ref, f32[1,8192]{1,0:T(1,128)S(1)} %bitcast.17, bf16[1024,8192]{1,0:T(8,128)(2,1)S(1)} %get-tuple-element.25.part_ref, bf16[64,4096]{1,0:T(8,128)(2,1)S(1)} %collective-permute-done.3.own_ref, ...), custom_call_target="tpu_custom_call" | custom-call | flops 2147483648 | bytes 8388608 | tf_op jit(solution)/shard_map/pallas_call | solution.py:264
  25.9 2.0 %collective-permute-done.7.own_ref = bf16[64,4096]{1,0:T(8,128)(2,1)S(1)} collective-permute-done((bf16[64,4096]{1,0:T(8,128)(2,1)S(1)}, bf16[64,4096]{1,0:T(8,128)(2,1)S(1)}, u32[]{:S(2)}, u32[]{:S(2)}) %collective-permute-start.7) | collective-permute-done | bytes 524320 | tf_op jit(solution)/shard_map/ppermute | solution.py:380
  27.8 2.1 %collective-permute-start.11 = (bf16[64,4096]{1,0:T(8,128)(2,1)S(1)}, bf16[64,4096]{1,0:T(8,128)(2,1)S(1)}, u32[]{:S(2)}, u32[]{:S(2)}) collective-permute-start(bf16[64,4096]{1,0:T(8,128)(2,1)S(1)} %collective-permute-done.7.own_ref), channel_id=1, source_target_pairs={{0,4},{4,8},{8,12},{12,14},{14,10},{10,6},{6,2},{2,0},{5,1},{9,5},... | collective-permute-start | bytes 1572872 | tf_op jit(solution)/shard_map/ppermute | solution.py:380
  29.9 5.3 %shard_map.80.rest_4_ = f32[16,1024]{1,0:T(8,128)S(1)} custom-call(s32[2]{0:T(128)S(1)} %pad_add_fusion.where_ref, f32[1,8192]{1,0:T(1,128)S(1)} %bitcast.18, bf16[1024,8192]{1,0:T(8,128)(2,1)S(1)} %get-tuple-element.25.part_ref, bf16[64,4224]{1,0:T(8,128)(2,1)S(1)} %collective-permute-done.own_ref, bf16[64,4224]{1,0:T(8,128)(2,1)S(1)} %collective-permute-done.2.sib_ref, ...), custom_call_target="tpu_custom_call" | custom-call | flops 2147483648 | bytes 8388608 | tf_op jit(solution)/shard_map/pallas_call | solution.py:264
  36.9 5.8 %copy-done.1 = bf16[1024,8192]{1,0:T(8,128)(2,1)S(1)} copy-done((bf16[1024,8192]{1,0:T(8,128)(2,1)S(1)}, bf16[1024,8192]{1,0:T(8,128)(2,1)}, u32[]{:S(2)}) %copy-start.1) | copy-done | bytes 16777240
  42.7 3.5 %shard_map.81 = (f32[1024,128]{1,0:T(8,128)S(1)}, f32[128,128]{1,0:T(8,128)S(1)}) custom-call(s32[2]{0:T(128)S(1)} %pad_add_fusion.where_ref, f32[1,8192]{1,0:T(1,128)S(1)} %bitcast.19, bf16[1024,8192]{1,0:T(8,128)(2,1)S(1)} %copy-done.1, bf16[64,4096]{1,0:T(8,128)(2,1)S(1)} %collective-permute-done.7.own_ref, ...), custom_call_target="tpu_custom_call" | custom-call | flops 2147483648 | bytes 8388608 | tf_op jit(solution)/shard_map/pallas_call | solution.py:264
  46.4 1.6 %collective-permute-start.14 = (bf16[64,2048]{1,0:T(8,128)(2,1)S(1)}, bf16[64,2048]{1,0:T(8,128)(2,1)S(1)}, u32[]{:S(2)}, u32[]{:S(2)}) collective-permute-start(bf16[64,2048]{1,0:T(8,128)(2,1)S(1)} %constant_dynamic-slice_fusion.1), channel_id=1, source_target_pairs={{0,4},{4,8},{8,12},{12,14},{14,10},{10,6},{6,2},{2,0},{5,1},{9,5},... | collective-permute-start | bytes 786440 | tf_op jit(solution)/shard_map/ppermute | solution.py:380
  48.4 5.3 %shard_map.82.rest_4_ = f32[16,1024]{1,0:T(8,128)S(1)} custom-call(s32[2]{0:T(128)S(1)} %pad_add_fusion.where_ref, f32[1,8192]{1,0:T(1,128)S(1)} %bitcast.20, bf16[1024,8192]{1,0:T(8,128)(2,1)S(1)} %copy-done.2, bf16[64,4224]{1,0:T(8,128)(2,1)S(1)} %collective-permute-done.1.own_ref, bf16[64,4224]{1,0:T(8,128)(2,1)S(1)} %collective-permute-done.6.sib_ref, ...), custom_call_target="tpu_custom_call" | custom-call | flops 2147483648 | bytes 8388608 | tf_op jit(solution)/shard_map/pallas_call | solution.py:264
  53.8 1.8 %collective-permute-start.9 = (bf16[64,2176]{1,0:T(8,128)(2,1)S(1)}, bf16[64,2176]{1,0:T(8,128)(2,1)S(1)}, u32[]{:S(2)}, u32[]{:S(2)}) collective-permute-start(bf16[64,2176]{1,0:T(8,128)(2,1)S(1)} %constant_dynamic-slice_fusion.2), channel_id=1, source_target_pairs={{0,4},{4,8},{8,12},{12,14},{14,10},{10,6},{6,2},{2,0},{5,1},{9,5},... | collective-permute-start | bytes 835592 | tf_op jit(solution)/shard_map/ppermute | solution.py:380
  55.6 3.5 %shard_map.83 = (f32[1024,128]{1,0:T(8,128)S(1)}, f32[128,128]{1,0:T(8,128)S(1)}) custom-call(s32[2]{0:T(128)S(1)} %pad_add_fusion.where_ref, f32[1,8192]{1,0:T(1,128)S(1)} %bitcast.21, bf16[1024,8192]{1,0:T(8,128)(2,1)S(1)} %copy-done.2, bf16[64,4096]{1,0:T(8,128)(2,1)S(1)} %collective-permute-done.11.own_ref, ...), custom_call_target="tpu_custom_call" | custom-call | flops 2147483648 | bytes 8388608 | tf_op jit(solution)/shard_map/pallas_call | solution.py:264
  59.3 5.3 %shard_map.84.rest_4_ = f32[16,1024]{1,0:T(8,128)S(1)} custom-call(s32[2]{0:T(128)S(1)} %pad_add_fusion.where_ref, f32[1,8192]{1,0:T(1,128)S(1)} %bitcast.22, bf16[1024,8192]{1,0:T(8,128)(2,1)S(1)} %copy-done.2, bf16[64,4224]{1,0:T(8,128)(2,1)S(1)} %collective-permute-done.5.own_ref, bf16[64,4224]{1,0:T(8,128)(2,1)S(1)} %collective-permute-done.10.sib_ref, ...), custom_call_target="tpu_custom_call" | custom-call | flops 2147483648 | bytes 8388608 | tf_op jit(solution)/shard_map/pallas_call | solution.py:264
  65.1 3.4 %shard_map.85 = (f32[1024,64]{1,0:T(8,128)S(1)}, f32[64,128]{1,0:T(8,128)S(1)}) custom-call(s32[2]{0:T(128)S(1)} %pad_add_fusion.where_ref, f32[1,8192]{1,0:T(1,128)S(1)} %bitcast.23, bf16[1024,8192]{1,0:T(8,128)(2,1)S(1)} %copy-done.2, bf16[64,2048]{1,0:T(8,128)(2,1)S(1)} %collective-permute-done.14.own_ref, ...), custom_call_target="tpu_custom_call" | custom-call | flops 2147483648 | bytes 8388608 | tf_op jit(solution)/shard_map/pallas_call | solution.py:264
  68.5 4.4 %shard_map.86.state_ref = f32[16,1024]{1,0:T(8,128)S(1)} custom-call(s32[2]{0:T(128)S(1)} %pad_add_fusion.where_ref, f32[1,8192]{1,0:T(1,128)S(1)} %bitcast.24, bf16[1024,8192]{1,0:T(8,128)(2,1)S(1)} %copy-done.2, bf16[64,2176]{1,0:T(8,128)(2,1)S(1)} %collective-permute-done.9.own_ref, bf16[64,2176]{1,0:T(8,128)(2,1)S(1)} %collective-permute-done.13.sib_ref, ...), custom_call_target="tpu_custom_call" | custom-call | flops 2147483648 | bytes 8388608 | tf_op jit(solution)/shard_map/pallas_call | solution.py:264
  72.9 3.4 %shard_map.87 = (f32[1,1024]{1,0:T(1,128)}, f32[8,4,1152]{2,1,0:T(4,128)S(1)}, f32[8,4,1152]{2,1,0:T(4,128)S(1)}) custom-call(s32[1]{0:T(128)} %bitcast.own_ref, f32[16,1024]{1,0:T(8,128)S(1)} %shard_map.86.state_ref, bf16[1024,8192]{1,0:T(8,128)(2,1)S(1)} %copy-done.2), custom_call_target="tpu_custom_call" | custom-call | flops 2147483648 | bytes 16777216 | tf_op jit(solution)/shard_map/pallas_call | solution.py:312
  78.7 3.5 %collective-permute-done.17 = f32[4,4,1152]{2,1,0:T(4,128)S(1)} collective-permute-done((f32[4,4,1152]{2,1,0:T(4,128)S(1)}, f32[4,4,1152]{2,1,0:T(4,128)S(1)}, u32[]{:S(2)}, u32[]{:S(2)}) %collective-permute-start.17) | collective-permute-done | bytes 73760 | tf_op jit(solution)/shard_map/ppermute | solution.py:339
  82.2 1.6 %collective-permute-start.18 = (f32[2,4,1152]{2,1,0:T(4,128)S(1)}, f32[2,4,1152]{2,1,0:T(4,128)S(1)}, u32[]{:S(2)}, u32[]{:S(2)}) collective-permute-start(f32[2,4,1152]{2,1,0:T(4,128)S(1)} %dynamic-slice_bitcast_fusion.1), channel_id=1, source_target_pairs={{0,4},{2,6},{4,0},{6,2},{8,12},{10,14},{12,8},{14,10},{1,5},{3,7},... | collective-permute-start | bytes 110600 | tf_op jit(solution)/shard_map/ppermute | solution.py:339
  83.8 2.4 %collective-permute-done.18 = f32[2,4,1152]{2,1,0:T(4,128)S(1)} collective-permute-done((f32[2,4,1152]{2,1,0:T(4,128)S(1)}, f32[2,4,1152]{2,1,0:T(4,128)S(1)}, u32[]{:S(2)}, u32[]{:S(2)}) %collective-permute-start.18) | collective-permute-done | bytes 36896 | tf_op jit(solution)/shard_map/ppermute | solution.py:339
  86.3 1.7 %collective-permute-start.19 = (f32[1,4,1152]{2,1,0:T(4,128)S(1)}, f32[1,4,1152]{2,1,0:T(4,128)S(1)}, u32[]{:S(2)}, u32[]{:S(2)}) collective-permute-start(f32[1,4,1152]{2,1,0:T(4,128)S(1)} %constant_dynamic-slice_fusion), channel_id=1, source_target_pairs={{0,8},{2,10},{4,12},{6,14},{8,0},{10,2},{12,4},{14,6},{1,9},{3,11}... | collective-permute-start | bytes 55304 | tf_op jit(solution)/shard_map/ppermute | solution.py:339
  88.0 3.0 %collective-permute-done.19 = f32[1,4,1152]{2,1,0:T(4,128)S(1)} collective-permute-done((f32[1,4,1152]{2,1,0:T(4,128)S(1)}, f32[1,4,1152]{2,1,0:T(4,128)S(1)}, u32[]{:S(2)}, u32[]{:S(2)}) %collective-permute-start.19) | collective-permute-done | bytes 18464 | tf_op jit(solution)/shard_map/ppermute | solution.py:339
  (53 shorter events, 9.7 us)
Async XLA Ops:
  0.6 21.7 %copy-start.3 = (f32[8192]{0:T(1024)S(1)}, f32[8192]{0:T(1024)}, u32[]{:S(2)}) copy-start(f32[8192]{0:T(1024)} %param.11) | copy-start | bytes 98308
  2.7 18.1 %collective-permute-start = (bf16[64,4224]{1,0:T(8,128)(2,1)S(1)}, bf16[64,4224]{1,0:T(8,128)(2,1)S(1)}, u32[]{:S(2)}, u32[]{:S(2)}) collective-permute-start(bf16[64,4224]{1,0:T(8,128)(2,1)S(1)} %get-tuple-element.26), channel_id=1, source_target_pairs={{0,4},{4,8},{8,12},{12,14},{14,10},{10,6},{6,2},{2,0},{5,1},{9,5},... | collective-permute-start | bytes 1622024 | tf_op jit(solution)/shard_map/ppermute | solution.py:380
  5.7 12.9 %collective-permute-start.3 = (bf16[64,4096]{1,0:T(8,128)(2,1)S(1)}, bf16[64,4096]{1,0:T(8,128)(2,1)S(1)}, u32[]{:S(2)}, u32[]{:S(2)}) collective-permute-start(bf16[64,4096]{1,0:T(8,128)(2,1)S(1)} %get-tuple-element.29), channel_id=1, source_target_pairs={{0,4},{4,8},{8,12},{12,14},{14,10},{10,6},{6,2},{2,0},{5,1},{9,5},... | collective-permute-start | bytes 1572872 | tf_op jit(solution)/shard_map/ppermute | solution.py:380
  8.1 21.9 %copy-start.4 = (s32[16,1024]{1,0:T(8,128)S(1)}, s32[16,1024]{1,0:T(8,128)}, u32[]{:S(2)}) copy-start(s32[16,1024]{1,0:T(8,128)} %rest_3_.7) | copy-start | bytes 196612
  17.5 17.6 %copy-start = (bf16[1024,8192]{1,0:T(8,128)(2,1)}, bf16[1024,8192]{1,0:T(8,128)(2,1)S(1)}, u32[]{:S(2)}) copy-start(bf16[1024,8192]{1,0:T(8,128)(2,1)S(1)} %get-tuple-element.25.part_ref) | copy-start | bytes 50331652
  18.6 3.7 %collective-permute-start.4 = (bf16[64,4096]{1,0:T(8,128)(2,1)S(1)}, bf16[64,4096]{1,0:T(8,128)(2,1)S(1)}, u32[]{:S(2)}, u32[]{:S(2)}) collective-permute-start(bf16[64,4096]{1,0:T(8,128)(2,1)S(1)} %collective-permute-done.3.own_ref), channel_id=1, source_target_pairs={{0,1},{1,0},{2,3},{3,2},{4,5},{5,4},{6,7},{7,6},{8,9},{9,8},{10,11... | collective-permute-start | bytes 1572872 | tf_op jit(solution)/shard_map/ppermute | solution.py:382
  18.6 9.2 %collective-permute-start.7 = (bf16[64,4096]{1,0:T(8,128)(2,1)S(1)}, bf16[64,4096]{1,0:T(8,128)(2,1)S(1)}, u32[]{:S(2)}, u32[]{:S(2)}) collective-permute-start(bf16[64,4096]{1,0:T(8,128)(2,1)S(1)} %collective-permute-done.3.own_ref), channel_id=1, source_target_pairs={{0,4},{4,8},{8,12},{12,14},{14,10},{10,6},{6,2},{2,0},{5,1},{9,5},... | collective-permute-start | bytes 1572872 | tf_op jit(solution)/shard_map/ppermute | solution.py:380
  20.7 9.2 %collective-permute-start.2 = (bf16[64,4224]{1,0:T(8,128)(2,1)S(1)}, bf16[64,4224]{1,0:T(8,128)(2,1)S(1)}, u32[]{:S(2)}, u32[]{:S(2)}) collective-permute-start(bf16[64,4224]{1,0:T(8,128)(2,1)S(1)} %collective-permute-done.own_ref), channel_id=1, source_target_pairs={{0,1},{1,0},{2,3},{3,2},{4,5},{5,4},{6,7},{7,6},{8,9},{9,8},{10,11... | collective-permute-start | bytes 1622024 | tf_op jit(solution)/shard_map/ppermute | solution.py:382
  20.9 14.3 %collective-permute-start.1 = (bf16[64,4224]{1,0:T(8,128)(2,1)S(1)}, bf16[64,4224]{1,0:T(8,128)(2,1)S(1)}, u32[]{:S(2)}, u32[]{:S(2)}) collective-permute-start(bf16[64,4224]{1,0:T(8,128)(2,1)S(1)} %collective-permute-done.own_ref), channel_id=1, source_target_pairs={{0,4},{4,8},{8,12},{12,14},{14,10},{10,6},{6,2},{2,0},{5,1},{9,5},... | collective-permute-start | bytes 1622024 | tf_op jit(solution)/shard_map/ppermute | solution.py:380
  27.8 9.1 %collective-permute-start.8 = (bf16[64,4096]{1,0:T(8,128)(2,1)S(1)}, bf16[64,4096]{1,0:T(8,128)(2,1)S(1)}, u32[]{:S(2)}, u32[]{:S(2)}) collective-permute-start(bf16[64,4096]{1,0:T(8,128)(2,1)S(1)} %collective-permute-done.7.own_ref), channel_id=1, source_target_pairs={{0,1},{1,0},{2,3},{3,2},{4,5},{5,4},{6,7},{7,6},{8,9},{9,8},{10,11... | collective-permute-start | bytes 1572872 | tf_op jit(solution)/shard_map/ppermute | solution.py:382
  27.8 18.4 %collective-permute-start.11 = (bf16[64,4096]{1,0:T(8,128)(2,1)S(1)}, bf16[64,4096]{1,0:T(8,128)(2,1)S(1)}, u32[]{:S(2)}, u32[]{:S(2)}) collective-permute-start(bf16[64,4096]{1,0:T(8,128)(2,1)S(1)} %collective-permute-done.7.own_ref), channel_id=1, source_target_pairs={{0,4},{4,8},{8,12},{12,14},{14,10},{10,6},{6,2},{2,0},{5,1},{9,5},... | collective-permute-start | bytes 1572872 | tf_op jit(solution)/shard_map/ppermute | solution.py:380
  35.2 12.8 %collective-permute-start.6 = (bf16[64,4224]{1,0:T(8,128)(2,1)S(1)}, bf16[64,4224]{1,0:T(8,128)(2,1)S(1)}, u32[]{:S(2)}, u32[]{:S(2)}) collective-permute-start(bf16[64,4224]{1,0:T(8,128)(2,1)S(1)} %collective-permute-done.1.own_ref), channel_id=1, source_target_pairs={{0,1},{1,0},{2,3},{3,2},{4,5},{5,4},{6,7},{7,6},{8,9},{9,8},{10,11... | collective-permute-start | bytes 1622024 | tf_op jit(solution)/shard_map/ppermute | solution.py:382
  35.4 18.3 %collective-permute-start.5 = (bf16[64,4224]{1,0:T(8,128)(2,1)S(1)}, bf16[64,4224]{1,0:T(8,128)(2,1)S(1)}, u32[]{:S(2)}, u32[]{:S(2)}) collective-permute-start(bf16[64,4224]{1,0:T(8,128)(2,1)S(1)} %collective-permute-done.1.own_ref), channel_id=1, source_target_pairs={{0,4},{4,8},{8,12},{12,14},{14,10},{10,6},{6,2},{2,0},{5,1},{9,5},... | collective-permute-start | bytes 1622024 | tf_op jit(solution)/shard_map/ppermute | solution.py:380
  46.2 9.4 %collective-permute-start.12 = (bf16[64,4096]{1,0:T(8,128)(2,1)S(1)}, bf16[64,4096]{1,0:T(8,128)(2,1)S(1)}, u32[]{:S(2)}, u32[]{:S(2)}) collective-permute-start(bf16[64,4096]{1,0:T(8,128)(2,1)S(1)} %collective-permute-done.11.own_ref), channel_id=1, source_target_pairs={{0,1},{1,0},{2,3},{3,2},{4,5},{5,4},{6,7},{7,6},{8,9},{9,8},{10,11... | collective-permute-start | bytes 1572872 | tf_op jit(solution)/shard_map/ppermute | solution.py:382
  46.4 12.8 %collective-permute-start.14 = (bf16[64,2048]{1,0:T(8,128)(2,1)S(1)}, bf16[64,2048]{1,0:T(8,128)(2,1)S(1)}, u32[]{:S(2)}, u32[]{:S(2)}) collective-permute-start(bf16[64,2048]{1,0:T(8,128)(2,1)S(1)} %constant_dynamic-slice_fusion.1), channel_id=1, source_target_pairs={{0,4},{4,8},{8,12},{12,14},{14,10},{10,6},{6,2},{2,0},{5,1},{9,5},... | collective-permute-start | bytes 786440 | tf_op jit(solution)/shard_map/ppermute | solution.py:380
  53.7 5.5 %collective-permute-start.10 = (bf16[64,4224]{1,0:T(8,128)(2,1)S(1)}, bf16[64,4224]{1,0:T(8,128)(2,1)S(1)}, u32[]{:S(2)}, u32[]{:S(2)}) collective-permute-start(bf16[64,4224]{1,0:T(8,128)(2,1)S(1)} %collective-permute-done.5.own_ref), channel_id=1, source_target_pairs={{0,1},{1,0},{2,3},{3,2},{4,5},{5,4},{6,7},{7,6},{8,9},{9,8},{10,11... | collective-permute-start | bytes 1622024 | tf_op jit(solution)/shard_map/ppermute | solution.py:382
  53.8 10.7 %collective-permute-start.9 = (bf16[64,2176]{1,0:T(8,128)(2,1)S(1)}, bf16[64,2176]{1,0:T(8,128)(2,1)S(1)}, u32[]{:S(2)}, u32[]{:S(2)}) collective-permute-start(bf16[64,2176]{1,0:T(8,128)(2,1)S(1)} %constant_dynamic-slice_fusion.2), channel_id=1, source_target_pairs={{0,4},{4,8},{8,12},{12,14},{14,10},{10,6},{6,2},{2,0},{5,1},{9,5},... | collective-permute-start | bytes 835592 | tf_op jit(solution)/shard_map/ppermute | solution.py:380
  59.2 5.9 %collective-permute-start.15 = (bf16[64,2048]{1,0:T(8,128)(2,1)S(1)}, bf16[64,2048]{1,0:T(8,128)(2,1)S(1)}, u32[]{:S(2)}, u32[]{:S(2)}) collective-permute-start(bf16[64,2048]{1,0:T(8,128)(2,1)S(1)} %collective-permute-done.14.own_ref), channel_id=1, source_target_pairs={{0,1},{1,0},{2,3},{3,2},{4,5},{5,4},{6,7},{7,6},{8,9},{9,8},{10,11... | collective-permute-start | bytes 786440 | tf_op jit(solution)/shard_map/ppermute | solution.py:382
  64.5 4.0 %collective-permute-start.13 = (bf16[64,2176]{1,0:T(8,128)(2,1)S(1)}, bf16[64,2176]{1,0:T(8,128)(2,1)S(1)}, u32[]{:S(2)}, u32[]{:S(2)}) collective-permute-start(bf16[64,2176]{1,0:T(8,128)(2,1)S(1)} %collective-permute-done.9.own_ref), channel_id=1, source_target_pairs={{0,1},{1,0},{2,3},{3,2},{4,5},{5,4},{6,7},{7,6},{8,9},{9,8},{10,11... | collective-permute-start | bytes 835592 | tf_op jit(solution)/shard_map/ppermute | solution.py:382
  68.5 22.7 %copy-start.5 = (s32[8]{0:T(128)S(1)}, s32[8]{0:T(128)}, u32[]{:S(2)}) copy-start(s32[8]{0:T(128)} %param.10) | copy-start | bytes 100
  76.3 1.4 %collective-permute-start.16 = (f32[8,4,1152]{2,1,0:T(4,128)S(1)}, f32[8,4,1152]{2,1,0:T(4,128)S(1)}, u32[]{:S(2)}, u32[]{:S(2)}) collective-permute-start(f32[8,4,1152]{2,1,0:T(4,128)S(1)} %get-tuple-element.47), channel_id=1, source_target_pairs={{0,1},{1,0},{2,3},{3,2},{4,5},{5,4},{6,7},{7,6},{8,9},{9,8},{10,11... | collective-permute-start | bytes 442376 | tf_op jit(solution)/shard_map/ppermute | solution.py:392
  77.8 4.4 %collective-permute-start.17 = (f32[4,4,1152]{2,1,0:T(4,128)S(1)}, f32[4,4,1152]{2,1,0:T(4,128)S(1)}, u32[]{:S(2)}, u32[]{:S(2)}) collective-permute-start(f32[4,4,1152]{2,1,0:T(4,128)S(1)} %dynamic-slice_bitcast_fusion), channel_id=1, source_target_pairs={{0,2},{2,0},{4,6},{6,4},{8,10},{10,8},{12,14},{14,12},{1,3},{3,1},... | collective-permute-start | bytes 221192 | tf_op jit(solution)/shard_map/ppermute | solution.py:339
  82.2 4.0 %collective-permute-start.18 = (f32[2,4,1152]{2,1,0:T(4,128)S(1)}, f32[2,4,1152]{2,1,0:T(4,128)S(1)}, u32[]{:S(2)}, u32[]{:S(2)}) collective-permute-start(f32[2,4,1152]{2,1,0:T(4,128)S(1)} %dynamic-slice_bitcast_fusion.1), channel_id=1, source_target_pairs={{0,4},{2,6},{4,0},{6,2},{8,12},{10,14},{12,8},{14,10},{1,5},{3,7},... | collective-permute-start | bytes 110600 | tf_op jit(solution)/shard_map/ppermute | solution.py:339
  86.3 4.7 %collective-permute-start.19 = (f32[1,4,1152]{2,1,0:T(4,128)S(1)}, f32[1,4,1152]{2,1,0:T(4,128)S(1)}, u32[]{:S(2)}, u32[]{:S(2)}) collective-permute-start(f32[1,4,1152]{2,1,0:T(4,128)S(1)} %constant_dynamic-slice_fusion), channel_id=1, source_target_pairs={{0,8},{2,10},{4,12},{6,14},{8,0},{10,2},{12,4},{14,6},{1,9},{3,11}... | collective-permute-start | bytes 55304 | tf_op jit(solution)/shard_map/ppermute | solution.py:339
  (2 other events, 11.5 us)

commit v4 on v3

--- a/solution.py
+++ b/solution.py
@@ -10,9 +10,11 @@
 LOWEST = -1e30
 STEPS = 8
 WIDTH = 1024
+SLOTS = 3
+STRIP = 256
 LANES = 128
 STATE_ROWS = 8
-VMEM_LIMIT = 16 * 1024 * 1024
+VMEM_LIMIT = 12 * 1024 * 1024
 
 
 def ring_order(blocks):
@@ -78,28 +80,43 @@
         folded = folded + square[:, lane : lane + LANES]
     energy[...] += folded
     acc[...] += lax.dot_general(
+        product.astype(jnp.bfloat16),
         part,
-        product.astype(jnp.bfloat16),
-        (((1,), (1,)), ((), ())),
+        (((1,), (0,)), ((), ())),
         preferred_element_type=jnp.float32,
     )
 
 
-def add_rows(tags, ids, logs_ref, sig_ref, state, acc, energy):
+def pick_words(sig_ref, words_ref):
+    word = lax.broadcasted_iota(jnp.int32, words_ref.shape, 0)
+    words = jnp.zeros(words_ref.shape, jnp.int32)
+    for pick in range(sig_ref.shape[0]):
+        chosen = sig_ref[pick : pick + 1, :]
+        bit = jnp.left_shift(1, jnp.bitwise_and(chosen, 31))
+        words = words | jnp.where(jnp.right_shift(chosen, 5) == word, bit, 0)
+    words_ref[...] = words
+
+
+def picked_rows(words_ref, source, height):
+    bit = jnp.left_shift(1, lax.broadcasted_iota(jnp.int32, (32, 1), 0))
+    rows = []
+    for word in range(height // 32):
+        rows.append((words_ref[pl.ds(source * (height // 32) + word, 1), :] & bit) != 0)
+    return jnp.concatenate(rows, axis=0)
+
+
+def add_rows(tags, hit, logs_ref, state, acc, energy):
     classes = logs_ref.shape[0]
     prior = jnp.zeros_like(tags[:, :1])
     for tag in range(classes):
         prior = jnp.where(tags[:, :1] == tag, logs_ref[tag], prior)
     bias = prior - 0.5 * jnp.sum(energy[...], axis=1, keepdims=True)
-    scores = jnp.transpose(acc[...]) + bias
+    scores = acc[...] + bias
     old_max, old_sum, old_top, weights = state
     new_max = jnp.maximum(old_max, jnp.max(scores, axis=0, keepdims=True))
     new_sum = old_sum * jnp.exp(old_max - new_max) + jnp.sum(
         jnp.exp(scores - new_max), axis=0, keepdims=True
     )
-    hit = sig_ref[0:1, :] == ids
-    for pick in range(1, sig_ref.shape[0]):
-        hit = hit | (sig_ref[pick : pick + 1, :] == ids)
     new_top = jnp.maximum(
         old_top, jnp.max(jnp.where(hit, scores, LOWEST), axis=0, keepdims=True)
     )
@@ -130,7 +147,7 @@
 
 def own_kernel(
     where_ref, logs_ref, tags_ref, sig_ref, noise_ref, tmpl_ref, far_ref,
-    out_ref, near_ref, acc, energy, arrived,
+    out_ref, turned_ref, words_ref, acc, energy, slots, arrived,
 ):
     freqs = noise_ref.shape[1]
     height = tmpl_ref.shape[0]
@@ -138,12 +155,12 @@
 
     def copy(step):
         columns = pl.ds(pl.multiple_of(step * width, width), width)
-        return pltpu.make_async_copy(
-            far_ref.at[:, columns], near_ref.at[:, columns], arrived.at[step]
-        )
-
-    for step in range(STEPS):
+        slot = lax.rem(step, SLOTS)
+        return pltpu.make_async_copy(far_ref.at[:, columns], slots.at[slot], arrived.at[slot])
+
+    for step in range(SLOTS):
         copy(step).start()
+    pick_words(sig_ref, words_ref)
     acc[...] = jnp.zeros_like(acc)
     energy[...] = jnp.zeros_like(energy)
 
@@ -151,35 +168,49 @@
     def _(step):
         copy(step).wait()
         columns = pl.ds(pl.multiple_of(step * width, width), width)
+        slot = lax.rem(step, SLOTS)
+
+        @pl.loop(0, width // STRIP)
+        def _(strip):
+            some = pl.ds(pl.multiple_of(strip * STRIP, STRIP), STRIP)
+            there = pl.ds(pl.multiple_of(step * width + strip * STRIP, STRIP), STRIP)
+            turned_ref[there, :] = jnp.transpose(slots[slot, :, some])
+
+        @pl.when(step + SLOTS < STEPS)
+        def _():
+            copy(step + SLOTS).start()
+
         add_scores(
-            tmpl_ref[:, columns], noise_ref[:, columns], near_ref[:, columns], acc, energy
+            tmpl_ref[:, columns], noise_ref[:, columns], turned_ref[columns, :], acc, energy
         )
 
     tags = tag_rows(tags_ref, height)
-    ids = where_ref[0] * height + lax.broadcasted_iota(jnp.int32, (height, 1), 0)
-    lowest = jnp.full((1, acc.shape[0]), LOWEST, jnp.float32)
-    none = jnp.zeros((1, acc.shape[0]), jnp.float32)
-    weights = jnp.zeros((logs_ref.shape[0], acc.shape[0]), jnp.float32)
+    hit = picked_rows(words_ref, where_ref[0], height)
+    lowest = jnp.full((1, acc.shape[1]), LOWEST, jnp.float32)
+    none = jnp.zeros((1, acc.shape[1]), jnp.float32)
+    weights = jnp.zeros((logs_ref.shape[0], acc.shape[1]), jnp.float32)
     state = (lowest, none, lowest, weights)
-    put_state(add_rows(tags, ids, logs_ref, sig_ref, state, acc, energy), out_ref)
-
-
-def score_own(where, logs, template_class, significant, noise, templates, particles):
+    put_state(add_rows(tags, hit, logs_ref, state, acc, energy), out_ref)
+
+
+def score_own(where, logs, template_class, significant, noise, templates, particles, total):
     per_device, freqs = particles.shape
     height = templates.shape[0]
     rows = STATE_ROWS + logs.shape[0]
     return pl.pallas_call(
         own_kernel,
         in_specs=[in_smem()] * 3 + [in_vmem()] * 3 + [pl.BlockSpec(memory_space=pl.ANY)],
-        out_specs=[in_vmem(), in_vmem()],
+        out_specs=[in_vmem()] * 3,
         out_shape=[
             jax.ShapeDtypeStruct((rows, per_device), jnp.float32),
-            pltpu.VMEM(particles.shape, particles.dtype),
+            pltpu.VMEM((freqs, per_device), particles.dtype),
+            jax.ShapeDtypeStruct((total // 32, per_device), jnp.int32),
         ],
         scratch_shapes=[
-            pltpu.VMEM((per_device, height), jnp.float32),
+            pltpu.VMEM((height, per_device), jnp.float32),
             pltpu.VMEM((height, LANES), jnp.float32),
-            pltpu.SemaphoreType.DMA((STEPS,)),
+            pltpu.VMEM((SLOTS, per_device, freqs // STEPS), particles.dtype),
+            pltpu.SemaphoreType.DMA((SLOTS,)),
         ],
         compiler_params=pltpu.CompilerParams(vmem_limit_bytes=VMEM_LIMIT),
         cost_estimate=pl.CostEstimate(
@@ -197,13 +228,51 @@
     )
 
 
+def near_copies(far_ref, near, arrived):
+    blocks, _, width = near.shape
+    return [
+        pltpu.make_async_copy(
+            far_ref.at[:, block * width : (block + 1) * width], near.at[block], arrived.at[block]
+        )
+        for block in range(blocks)
+    ]
+
+
+def class_sums(state, core, near, copies, loglik_ref, mine_ref, theirs_ref):
+    top, total, _, weights = state
+    loglik_ref[...] = top + jnp.log(total)
+    per_owner = mine_ref.shape[1]
+    width = near.shape[2]
+    weights = weights / jnp.sum(weights, axis=0, keepdims=True)
+    turned = jnp.concatenate([weights[per_owner:], weights[:per_owner]], axis=0)
+    weights = jnp.where(core == 0, weights, turned)
+    rounded = weights.astype(jnp.bfloat16)
+    totals = jnp.broadcast_to(
+        jnp.sum(weights, axis=1, keepdims=True), (weights.shape[0], LANES)
+    )
+    for block, copy in enumerate(copies):
+        copy.wait()
+        sums = jnp.dot(rounded, near[block], preferred_element_type=jnp.float32)
+        mine_ref[block, :, :width] = sums[:per_owner]
+        theirs_ref[block, :, :width] = sums[per_owner:]
+        mine_ref[block, :, width:] = totals[:per_owner]
+        theirs_ref[block, :, width:] = totals[per_owner:]
+
+
 def ring_kernel(phase, ends, sources, where_ref, noise_ref, part_ref, own_ref, sib_ref, *rest):
     if phase == 0:
         acc, energy = rest
         acc[...] = jnp.zeros_like(acc)
         energy[...] = jnp.zeros_like(energy)
     else:
-        acc_in, energy_in, logs_ref, sig_ref, state_ref, out_ref, acc, energy = rest
+        acc_in, energy_in, logs_ref, words_ref, state_ref, *rest = rest
+        if ends:
+            far_ref, loglik_ref, mine_ref, theirs_ref, acc, energy, near, arrived = rest
+            copies = near_copies(far_ref, near, arrived)
+            for copy in copies:
+                copy.start()
+        else:
+            out_ref, acc, energy = rest
         acc[...] = acc_in[...]
         energy[...] = energy_in[...]
     freqs = noise_ref.shape[1]
@@ -221,7 +290,7 @@
             near = pl.ds(pl.multiple_of(step * WIDTH, WIDTH), WIDTH)
             columns = pl.ds(pl.multiple_of(start + step * WIDTH, WIDTH), WIDTH)
             rows = jnp.concatenate([ref[:, near] for ref in refs], axis=0)
-            add_scores(rows, noise_ref[:, columns], part_ref[:, columns], acc, energy)
+            add_scores(rows, noise_ref[:, columns], part_ref[columns, :], acc, energy)
 
     if phase == 0:
         return
@@ -234,93 +303,70 @@
         for block in range(1, len(table)):
             source = jnp.where(where_ref[0] == block, table[block], source)
         found.append(source)
-    row = lax.broadcasted_iota(jnp.int32, (height, 1), 0)
     if ends:
-        ids = found[0] * height + row
+        hit = picked_rows(words_ref, found[0], height)
     else:
         own = jnp.where(core == 0, found[0], found[1])
         sib = jnp.where(core == 0, found[1], found[0])
-        ids = jnp.concatenate([own * height + row, sib * height + row], axis=0)
-    state = add_rows(tags, ids, logs_ref, sig_ref, get_state(state_ref), acc, energy)
-    put_state(state, out_ref)
-
-
-def ring_scores(phase, ends, sources, where, noise, particles, own, sib, rest):
-    per_device, freqs = particles.shape
+        hit = jnp.concatenate(
+            [picked_rows(words_ref, source, height) for source in (own, sib)], axis=0
+        )
+    state = add_rows(tags, hit, logs_ref, get_state(state_ref), acc, energy)
+    if ends:
+        class_sums(state, core, near, copies, loglik_ref, mine_ref, theirs_ref)
+    else:
+        put_state(state, out_ref)
+
+
+def ring_scores(phase, sources, where, noise, turned, own, sib, rest, blocks=0, owners=0):
+    ends = blocks > 0
+    freqs, per_device = turned.shape
     rows = own.shape[0] * (1 if ends else 2)
     sums = [
-        jax.ShapeDtypeStruct((per_device, rows), jnp.float32),
+        jax.ShapeDtypeStruct((rows, per_device), jnp.float32),
         jax.ShapeDtypeStruct((rows, LANES), jnp.float32),
     ]
-    params = {}
+    scratch = [pltpu.VMEM(array.shape, array.dtype) for array in sums]
+    limit = VMEM_LIMIT
     if phase == 0:
-        params.update(out_specs=[in_vmem(), in_vmem()], out_shape=sums)
-        rest_specs = []
+        shapes, scratch, rest_specs = sums, [], []
     else:
-        state = jax.ShapeDtypeStruct(rest[-1].shape, jnp.float32)
-        scratch = [pltpu.VMEM(array.shape, array.dtype) for array in sums]
-        params.update(out_specs=in_vmem(), out_shape=state, scratch_shapes=scratch)
+        logs, state = rest[2], rest[4]
         rest_specs = [in_vmem(), in_vmem(), in_smem(), in_vmem(), in_vmem()]
+        if ends:
+            width = freqs // blocks
+            per_owner = logs.shape[0] // owners
+            piece = jax.ShapeDtypeStruct((blocks, per_owner, width + LANES), jnp.float32)
+            shapes = [jax.ShapeDtypeStruct((1, per_device), jnp.float32), piece, piece]
+            scratch += [
+                pltpu.VMEM((blocks, per_device, width), turned.dtype),
+                pltpu.SemaphoreType.DMA((blocks,)),
+            ]
+            rest_specs.append(pl.BlockSpec(memory_space=pl.ANY))
+            rest = (*rest[:-1], pltpu.with_memory_space_constraint(rest[-1], pltpu.HBM))
+            limit += 2 * per_device * freqs
+        else:
+            shapes = [jax.ShapeDtypeStruct(state.shape, jnp.float32)]
     return pl.pallas_call(
         functools.partial(ring_kernel, phase, ends, sources),
         in_specs=[in_smem()] + [in_vmem()] * 4 + rest_specs,
-        compiler_params=pltpu.CompilerParams(vmem_limit_bytes=VMEM_LIMIT),
+        out_specs=[in_vmem()] * len(shapes),
+        out_shape=shapes,
+        scratch_shapes=scratch,
+        compiler_params=pltpu.CompilerParams(vmem_limit_bytes=limit),
         cost_estimate=pl.CostEstimate(
             flops=2 * 128 * per_device * freqs,
             bytes_accessed=per_device * freqs,
             transcendentals=0,
         ),
-        **params,
     )(
         where,
         noise,
-        pltpu.with_memory_space_constraint(particles, pltpu.VMEM),
+        pltpu.with_memory_space_constraint(turned, pltpu.VMEM),
         own,
         sib,
         *rest,
     )
-
-
-def sums_kernel(own_ref, state_ref, part_ref, loglik_ref, mine_ref, theirs_ref):
-    blocks, per_owner = mine_ref.shape[:2]
-    width = part_ref.shape[1] // blocks
-    _, _, _, weights = get_state(state_ref)
-    loglik_ref[...] = state_ref[0:1, :] + jnp.log(state_ref[1:2, :])
-    weights = weights / jnp.sum(weights, axis=0, keepdims=True)
-    turned = jnp.concatenate([weights[per_owner:], weights[:per_owner]], axis=0)
-    weights = jnp.where(own_ref[0] == 0, weights, turned)
-    rounded = weights.astype(jnp.bfloat16)
-    total = jnp.broadcast_to(
-        jnp.sum(weights, axis=1, keepdims=True), (weights.shape[0], LANES)
-    )
-
-    @pl.loop(0, blocks)
-    def _(block):
-        columns = pl.ds(pl.multiple_of(block * width, width), width)
-        sums = jnp.dot(rounded, part_ref[:, columns], preferred_element_type=jnp.float32)
-        mine_ref[block, :, :width] = sums[:per_owner]
-        theirs_ref[block, :, :width] = sums[per_owner:]
-        mine_ref[block, :, width:] = total[:per_owner]
-        theirs_ref[block, :, width:] = total[per_owner:]
-
-
-def class_sums(own, state, particles, blocks, classes, owners):
-    per_device, freqs = particles.shape
-    width = freqs // blocks
-    per_owner = classes // owners
-    piece = jax.ShapeDtypeStruct((blocks, per_owner, width + LANES), jnp.float32)
-    return pl.pallas_call(
-        sums_kernel,
-        in_specs=[in_smem(), in_vmem(), in_vmem()],
-        out_specs=[in_vmem()] * 3,
-        out_shape=[jax.ShapeDtypeStruct((1, per_device), jnp.float32), piece, piece],
-        compiler_params=pltpu.CompilerParams(vmem_limit_bytes=VMEM_LIMIT),
-        cost_estimate=pl.CostEstimate(
-            flops=2 * 128 * per_device * freqs,
-            bytes_accessed=2 * per_device * freqs,
-            transcendentals=0,
-        ),
-    )(own, state, pltpu.with_memory_space_constraint(particles, pltpu.VMEM))
 
 
 def scatter_sum(pieces, blocks, block_id):
@@ -357,8 +403,9 @@
     logs = jnp.log(class_counts.astype(jnp.float32))
     held = make_messages(template_class, templates)
     where = jnp.stack([block_id, core])
-    state, near = score_own(
-        where, logs, template_class, significant, noise, templates, particles
+    state, turned, words = score_own(
+        where, logs, template_class, significant, noise, templates, particles,
+        blocks * templates.shape[0],
     )
     last = blocks // 2
     gates = [state]
@@ -380,15 +427,21 @@
             own = lax.ppermute(message, ("blk", "cls"), ring)
             own, _ = lax.optimization_barrier((own, gates[max(len(gates) - 2, 0)]))
             sib = lax.ppermute(own, "cls", swap)
-            rest = () if phase == 0 else (*sums, logs, significant, state)
-            sums = ring_scores(phase, ends, sources, where, noise, near, own, sib, rest)
+            rest = () if phase == 0 else (*sums, logs, words, state)
+            if ends:
+                rest += (particles,) if phase else ()
+                sums = ring_scores(
+                    phase, sources, where, noise, turned, own, sib, rest, blocks, owners
+                )
+            else:
+                sums = ring_scores(phase, sources, where, noise, turned, own, sib, rest)
             gates.append(sums)
-            if phase == 1:
-                state = sums
             arrived.append(own)
         held = arrived
-
-    loglik, mine, theirs = class_sums(core[None], state, near, blocks, classes, owners)
+        if not ends:
+            (state,) = sums
+
+    loglik, mine, theirs = sums
     reduced = mine + lax.ppermute(theirs, "cls", swap)
     total = scatter_sum(reduced, blocks, block_id)
     width = freqs // blocks

time: 92.2 us -> 87.2 us (0.946)
  Pallas kernels: 49.1 us -> 42.8 us
  starting transfers between devices: 20.5 us -> 18.1 us
  waiting for transfers between devices: 13.4 us -> 15.4 us
  local copies, waits for them, and re-layouts: 6.46 us -> 8.19 us
    pallas_call x8, Pallas kernels: 34.2 us -> 27 us  [ring_scores(): pl.pallas_call(functools.partial(ring_kernel, phase, ends, sources), in_s...]
    pallas_call x1, Pallas kernels: 9.47 us -> 13.8 us  [score_own(): pl.pallas_call(own_kernel, in_specs=[in_smem()] * 3 + [in_vmem()] * 3 + [...]
    pallas_call x1 -> x0, Pallas kernels: 3.43 us -> none  [class_sums(): pl.pallas_call(sums_kernel, in_specs=[in_smem(), in_vmem(), in_vmem()], o...]
    unnamed x12 -> x14, local copies, waits for them, and re-layouts: 6.24 us -> 7.97 us
    ppermute x3, waiting for transfers between devices: 8.96 us -> 10.1 us  [scatter_sum(): pieces = keep + lax.ppermute(send, 'blk', swaps)]
    ppermute x3, starting transfers between devices: 4.21 us -> 3.06 us  [scatter_sum(): pieces = keep + lax.ppermute(send, 'blk', swaps)]
    ppermute x8, starting transfers between devices: 15.1 us -> 14.1 us  [body(): own = lax.ppermute(message, ('blk', 'cls'), ring)]
  transfers between devices with their start and end apart: 20 -> 20, of which waited for: 6 -> 6; matrix products, arithmetic and copies ran while one was open for 1% -> 1% of each run, Pallas kernels for 43% -> 39%
where the time goes in v4:
time: 87.2 us; the launch traced here: 86.9 us
  Pallas kernels  42.8 us (49%)
  starting transfers between devices  18.1 us (21%)
  waiting for transfers between devices  15.4 us (18%)
  local copies, waits for them, and re-layouts  8.19 us (9%)
  other arithmetic  1.58 us (2%)
    pallas_call x8, Pallas kernels, ring_scores(): pl.pallas_call(functools.partial(ring_kernel, phase, ends, sources), in_s...  27 us
    ppermute x8, starting transfers between devices, body(): own = lax.ppermute(message, ('blk', 'cls'), ring)  14.1 us
    pallas_call x1, Pallas kernels, score_own(): pl.pallas_call(own_kernel, in_specs=[in_smem()] * 3 + [in_vmem()] * 3 + [...  13.8 us
    ppermute x3, waiting for transfers between devices, scatter_sum(): pieces = keep + lax.ppermute(send, 'blk', swaps)  10.1 us
    unnamed x14, local copies, waits for them, and re-layouts  7.97 us
    ppermute x8, waiting for transfers between devices, body(): own = lax.ppermute(message, ('blk', 'cls'), ring)  3.88 us
    ppermute x3, starting transfers between devices, scatter_sum(): pieces = keep + lax.ppermute(send, 'blk', swaps)  3.06 us
    pallas_call x1, Pallas kernels, make_messages(): pl.pallas_call(message_kernel, in_specs=[in_smem(), pl.BlockSpec(memory_s...  2.01 us
  transfers between devices with their start and end apart: 20, of which 6 were waited for; matrix products, arithmetic and copies ran while one was open for 1% of the time, Pallas kernels for 39%

profile of v4, /device:TPU:0, one launch (start us, length us, event | category | flops | bytes accessed | tf_op | source)
XLA Modules:
  0.0 86.9 jit_solution(7597070414018376811)
XLA Ops:
  0.6 2.0 %shard_map.78 = (bf16[64,4096]{1,0:T(8,128)(2,1)S(1)}, bf16[64,4224]{1,0:T(8,128)(2,1)S(1)}) custom-call(s32[64]{0:T(128)} %tags_ref.3, bf16[64,8192]{1,0:T(8,128)(2,1)} %rows_ref.1), custom_call_target="tpu_custom_call" | custom-call | tf_op jit(solution)/shard_map/pallas_call | solution.py:42
  2.7 3.1 %collective-permute-start = (bf16[64,4224]{1,0:T(8,128)(2,1)S(1)}, bf16[64,4224]{1,0:T(8,128)(2,1)S(1)}, u32[]{:S(2)}, u32[]{:S(2)}) collective-permute-start(bf16[64,4224]{1,0:T(8,128)(2,1)S(1)} %get-tuple-element.27), channel_id=1, source_target_pairs={{0,4},{4,8},{8,12},{12,14},{14,10},{10,6},{6,2},{2,0},{5,1},{9,5},... | collective-permute-start | bytes 1622024 | tf_op jit(solution)/shard_map/ppermute | solution.py:427
  5.7 1.6 %collective-permute-start.3 = (bf16[64,4096]{1,0:T(8,128)(2,1)S(1)}, bf16[64,4096]{1,0:T(8,128)(2,1)S(1)}, u32[]{:S(2)}, u32[]{:S(2)}) collective-permute-start(bf16[64,4096]{1,0:T(8,128)(2,1)S(1)} %get-tuple-element.30), channel_id=1, source_target_pairs={{0,4},{4,8},{8,12},{12,14},{14,10},{10,6},{6,2},{2,0},{5,1},{9,5},... | collective-permute-start | bytes 1572872 | tf_op jit(solution)/shard_map/ppermute | solution.py:427
  8.1 13.8 %shard_map.77 = (f32[16,1024]{1,0:T(8,128)S(1)}, bf16[8192,1024]{1,0:T(8,128)(2,1)S(1)}, s32[16,1024]{1,0:T(8,128)S(1)}) custom-call(s32[2]{0:T(128)S(1)} %pad_add_fusion.where_ref, f32[8]{0:T(128)S(1)} %convert_log_fusion.logs_ref.rest_2_, s32[64]{0:T(128)} %tags_ref.3, s32[16,1024]{1,0:T(8,128)} %sig_ref.1, f32[1,8192]{1,0:T(1,128)} %bitcast.16, ...), custom_call_target="tpu_custom_call" | custom-call | flops 4294967296 | bytes 16777216 | tf_op jit(solution)/shard_map/pallas_call | solution.py:200
  22.0 1.6 %collective-permute-start.7 = (bf16[64,4096]{1,0:T(8,128)(2,1)S(1)}, bf16[64,4096]{1,0:T(8,128)(2,1)S(1)}, u32[]{:S(2)}, u32[]{:S(2)}) collective-permute-start(bf16[64,4096]{1,0:T(8,128)(2,1)S(1)} %collective-permute-done.3.own_ref), channel_id=1, source_target_pairs={{0,4},{4,8},{8,12},{12,14},{14,10},{10,6},{6,2},{2,0},{5,1},{9,5},... | collective-permute-start | bytes 1572872 | tf_op jit(solution)/shard_map/ppermute | solution.py:427
  25.1 2.5 %shard_map.79 = (f32[128,1024]{1,0:T(8,128)S(1)}, f32[128,128]{1,0:T(8,128)S(1)}) custom-call(s32[2]{0:T(128)S(1)} %pad_add_fusion.where_ref, f32[1,8192]{1,0:T(1,128)S(1)} %bitcast.17, bf16[8192,1024]{1,0:T(8,128)(2,1)S(1)} %get-tuple-element.26.part_ref, bf16[64,4096]{1,0:T(8,128)(2,1)S(1)} %collective-permute-done.3.own_ref, ...), custom_call_target="tpu_custom_call" | custom-call | flops 2147483648 | bytes 8388608 | tf_op jit(solution)/shard_map/pallas_call | solution.py:350
  27.6 3.6 %collective-permute-done.7.own_ref = bf16[64,4096]{1,0:T(8,128)(2,1)S(1)} collective-permute-done((bf16[64,4096]{1,0:T(8,128)(2,1)S(1)}, bf16[64,4096]{1,0:T(8,128)(2,1)S(1)}, u32[]{:S(2)}, u32[]{:S(2)}) %collective-permute-start.7) | collective-permute-done | bytes 524320 | tf_op jit(solution)/shard_map/ppermute | solution.py:427
  31.2 1.6 %collective-permute-start.11 = (bf16[64,4096]{1,0:T(8,128)(2,1)S(1)}, bf16[64,4096]{1,0:T(8,128)(2,1)S(1)}, u32[]{:S(2)}, u32[]{:S(2)}) collective-permute-start(bf16[64,4096]{1,0:T(8,128)(2,1)S(1)} %collective-permute-done.7.own_ref), channel_id=1, source_target_pairs={{0,4},{4,8},{8,12},{12,14},{14,10},{10,6},{6,2},{2,0},{5,1},{9,5},... | collective-permute-start | bytes 1572872 | tf_op jit(solution)/shard_map/ppermute | solution.py:427
  32.8 3.3 %shard_map.80.rest_4_ = f32[16,1024]{1,0:T(8,128)S(1)} custom-call(s32[2]{0:T(128)S(1)} %pad_add_fusion.where_ref, f32[1,8192]{1,0:T(1,128)S(1)} %bitcast.18, bf16[8192,1024]{1,0:T(8,128)(2,1)S(1)} %get-tuple-element.26.part_ref, bf16[64,4224]{1,0:T(8,128)(2,1)S(1)} %collective-permute-done.own_ref, bf16[64,4224]{1,0:T(8,128)(2,1)S(1)} %collective-permute-done.2.sib_ref, ...), custom_call_target="tpu_custom_call" | custom-call | flops 2147483648 | bytes 8388608 | tf_op jit(solution)/shard_map/pallas_call | solution.py:350
  37.0 1.6 %collective-permute-start.5 = (bf16[64,4224]{1,0:T(8,128)(2,1)S(1)}, bf16[64,4224]{1,0:T(8,128)(2,1)S(1)}, u32[]{:S(2)}, u32[]{:S(2)}) collective-permute-start(bf16[64,4224]{1,0:T(8,128)(2,1)S(1)} %collective-permute-done.1.own_ref), channel_id=1, source_target_pairs={{0,4},{4,8},{8,12},{12,14},{14,10},{10,6},{6,2},{2,0},{5,1},{9,5},... | collective-permute-start | bytes 1622024 | tf_op jit(solution)/shard_map/ppermute | solution.py:427
  38.6 5.8 %copy-done.1 = bf16[8192,1024]{1,0:T(8,128)(2,1)S(1)} copy-done((bf16[8192,1024]{1,0:T(8,128)(2,1)S(1)}, bf16[8192,1024]{1,0:T(8,128)(2,1)}, u32[]{:S(2)}) %copy-start.1) | copy-done | bytes 16777240
  44.4 2.5 %shard_map.81 = (f32[128,1024]{1,0:T(8,128)S(1)}, f32[128,128]{1,0:T(8,128)S(1)}) custom-call(s32[2]{0:T(128)S(1)} %pad_add_fusion.where_ref, f32[1,8192]{1,0:T(1,128)S(1)} %bitcast.19, bf16[8192,1024]{1,0:T(8,128)(2,1)S(1)} %copy-done.1, bf16[64,4096]{1,0:T(8,128)(2,1)S(1)} %collective-permute-done.7.own_ref, ...), custom_call_target="tpu_custom_call" | custom-call | flops 2147483648 | bytes 8388608 | tf_op jit(solution)/shard_map/pallas_call | solution.py:350
  47.0 1.6 %collective-permute-start.14 = (bf16[64,2048]{1,0:T(8,128)(2,1)S(1)}, bf16[64,2048]{1,0:T(8,128)(2,1)S(1)}, u32[]{:S(2)}, u32[]{:S(2)}) collective-permute-start(bf16[64,2048]{1,0:T(8,128)(2,1)S(1)} %constant_dynamic-slice_fusion.1), channel_id=1, source_target_pairs={{0,4},{4,8},{8,12},{12,14},{14,10},{10,6},{6,2},{2,0},{5,1},{9,5},... | collective-permute-start | bytes 786440 | tf_op jit(solution)/shard_map/ppermute | solution.py:427
  48.6 1.6 %copy-done.2 = bf16[8192,1024]{1,0:T(8,128)(2,1)S(1)} copy-done((bf16[8192,1024]{1,0:T(8,128)(2,1)S(1)}, bf16[8192,1024]{1,0:T(8,128)(2,1)}, u32[]{:S(2)}) %copy-start.2) | copy-done | bytes 16777240
  50.1 3.3 %shard_map.82.rest_4_ = f32[16,1024]{1,0:T(8,128)S(1)} custom-call(s32[2]{0:T(128)S(1)} %pad_add_fusion.where_ref, f32[1,8192]{1,0:T(1,128)S(1)} %bitcast.20, bf16[8192,1024]{1,0:T(8,128)(2,1)S(1)} %copy-done.2, bf16[64,4224]{1,0:T(8,128)(2,1)S(1)} %collective-permute-done.1.own_ref, bf16[64,4224]{1,0:T(8,128)(2,1)S(1)} %collective-permute-done.6.sib_ref, ...), custom_call_target="tpu_custom_call" | custom-call | flops 2147483648 | bytes 8388608 | tf_op jit(solution)/shard_map/pallas_call | solution.py:350
  53.5 1.6 %collective-permute-start.9 = (bf16[64,2176]{1,0:T(8,128)(2,1)S(1)}, bf16[64,2176]{1,0:T(8,128)(2,1)S(1)}, u32[]{:S(2)}, u32[]{:S(2)}) collective-permute-start(bf16[64,2176]{1,0:T(8,128)(2,1)S(1)} %constant_dynamic-slice_fusion.2), channel_id=1, source_target_pairs={{0,4},{4,8},{8,12},{12,14},{14,10},{10,6},{6,2},{2,0},{5,1},{9,5},... | collective-permute-start | bytes 835592 | tf_op jit(solution)/shard_map/ppermute | solution.py:427
  55.1 2.5 %shard_map.83 = (f32[128,1024]{1,0:T(8,128)S(1)}, f32[128,128]{1,0:T(8,128)S(1)}) custom-call(s32[2]{0:T(128)S(1)} %pad_add_fusion.where_ref, f32[1,8192]{1,0:T(1,128)S(1)} %bitcast.21, bf16[8192,1024]{1,0:T(8,128)(2,1)S(1)} %copy-done.2, bf16[64,4096]{1,0:T(8,128)(2,1)S(1)} %collective-permute-done.11.own_ref, ...), custom_call_target="tpu_custom_call" | custom-call | flops 2147483648 | bytes 8388608 | tf_op jit(solution)/shard_map/pallas_call | solution.py:350
  57.7 3.3 %shard_map.84.rest_4_ = f32[16,1024]{1,0:T(8,128)S(1)} custom-call(s32[2]{0:T(128)S(1)} %pad_add_fusion.where_ref, f32[1,8192]{1,0:T(1,128)S(1)} %bitcast.22, bf16[8192,1024]{1,0:T(8,128)(2,1)S(1)} %copy-done.2, bf16[64,4224]{1,0:T(8,128)(2,1)S(1)} %collective-permute-done.5.own_ref, bf16[64,4224]{1,0:T(8,128)(2,1)S(1)} %collective-permute-done.10.sib_ref, ...), custom_call_target="tpu_custom_call" | custom-call | flops 2147483648 | bytes 8388608 | tf_op jit(solution)/shard_map/pallas_call | solution.py:350
  61.5 2.6 %shard_map.85 = (f32[64,1024]{1,0:T(8,128)S(1)}, f32[64,128]{1,0:T(8,128)S(1)}) custom-call(s32[2]{0:T(128)S(1)} %pad_add_fusion.where_ref, f32[1,8192]{1,0:T(1,128)S(1)} %bitcast.23, bf16[8192,1024]{1,0:T(8,128)(2,1)S(1)} %copy-done.2, bf16[64,2048]{1,0:T(8,128)(2,1)S(1)} %collective-permute-done.14.own_ref, ...), custom_call_target="tpu_custom_call" | custom-call | flops 2147483648 | bytes 8388608 | tf_op jit(solution)/shard_map/pallas_call | solution.py:350
  64.1 7.1 %shard_map.86 = (f32[1,1024]{1,0:T(1,128)}, f32[8,4,1152]{2,1,0:T(4,128)S(1)}, f32[8,4,1152]{2,1,0:T(4,128)S(1)}) custom-call(s32[2]{0:T(128)S(1)} %pad_add_fusion.where_ref, f32[1,8192]{1,0:T(1,128)S(1)} %bitcast.24, bf16[8192,1024]{1,0:T(8,128)(2,1)S(1)} %copy-done.2, bf16[64,2176]{1,0:T(8,128)(2,1)S(1)} %collective-permute-done.9.own_ref, ...), custom_call_target="tpu_custom_call" | custom-call | flops 2147483648 | bytes 8388608 | tf_op jit(solution)/shard_map/pallas_call | solution.py:350
  73.3 3.8 %collective-permute-done.17 = f32[4,4,1152]{2,1,0:T(4,128)S(1)} collective-permute-done((f32[4,4,1152]{2,1,0:T(4,128)S(1)}, f32[4,4,1152]{2,1,0:T(4,128)S(1)}, u32[]{:S(2)}, u32[]{:S(2)}) %collective-permute-start.17) | collective-permute-done | bytes 73760 | tf_op jit(solution)/shard_map/ppermute | solution.py:385
  78.0 3.3 %collective-permute-done.18 = f32[2,4,1152]{2,1,0:T(4,128)S(1)} collective-permute-done((f32[2,4,1152]{2,1,0:T(4,128)S(1)}, f32[2,4,1152]{2,1,0:T(4,128)S(1)}, u32[]{:S(2)}, u32[]{:S(2)}) %collective-permute-start.18) | collective-permute-done | bytes 36896 | tf_op jit(solution)/shard_map/ppermute | solution.py:385
  81.3 1.7 %collective-permute-start.19 = (f32[1,4,1152]{2,1,0:T(4,128)S(1)}, f32[1,4,1152]{2,1,0:T(4,128)S(1)}, u32[]{:S(2)}, u32[]{:S(2)}) collective-permute-start(f32[1,4,1152]{2,1,0:T(4,128)S(1)} %constant_dynamic-slice_fusion), channel_id=1, source_target_pairs={{0,8},{2,10},{4,12},{6,14},{8,0},{10,2},{12,4},{14,6},{1,9},{3,11}... | collective-permute-start | bytes 55304 | tf_op jit(solution)/shard_map/ppermute | solution.py:385
  83.0 3.0 %collective-permute-done.19 = f32[1,4,1152]{2,1,0:T(4,128)S(1)} collective-permute-done((f32[1,4,1152]{2,1,0:T(4,128)S(1)}, f32[1,4,1152]{2,1,0:T(4,128)S(1)}, u32[]{:S(2)}, u32[]{:S(2)}) %collective-permute-start.19) | collective-permute-done | bytes 18464 | tf_op jit(solution)/shard_map/ppermute | solution.py:385
  (54 shorter events, 7.9 us)
Async XLA Ops:
  0.6 24.5 %copy-start.3 = (f32[8192]{0:T(1024)S(1)}, f32[8192]{0:T(1024)}, u32[]{:S(2)}) copy-start(f32[8192]{0:T(1024)} %param.11) | copy-start | bytes 98308
  2.7 21.0 %collective-permute-start = (bf16[64,4224]{1,0:T(8,128)(2,1)S(1)}, bf16[64,4224]{1,0:T(8,128)(2,1)S(1)}, u32[]{:S(2)}, u32[]{:S(2)}) collective-permute-start(bf16[64,4224]{1,0:T(8,128)(2,1)S(1)} %get-tuple-element.27), channel_id=1, source_target_pairs={{0,4},{4,8},{8,12},{12,14},{14,10},{10,6},{6,2},{2,0},{5,1},{9,5},... | collective-permute-start | bytes 1622024 | tf_op jit(solution)/shard_map/ppermute | solution.py:427
  5.7 16.2 %collective-permute-start.3 = (bf16[64,4096]{1,0:T(8,128)(2,1)S(1)}, bf16[64,4096]{1,0:T(8,128)(2,1)S(1)}, u32[]{:S(2)}, u32[]{:S(2)}) collective-permute-start(bf16[64,4096]{1,0:T(8,128)(2,1)S(1)} %get-tuple-element.30), channel_id=1, source_target_pairs={{0,4},{4,8},{8,12},{12,14},{14,10},{10,6},{6,2},{2,0},{5,1},{9,5},... | collective-permute-start | bytes 1572872 | tf_op jit(solution)/shard_map/ppermute | solution.py:427
  21.9 14.2 %copy-start = (bf16[8192,1024]{1,0:T(8,128)(2,1)}, bf16[8192,1024]{1,0:T(8,128)(2,1)S(1)}, u32[]{:S(2)}) copy-start(bf16[8192,1024]{1,0:T(8,128)(2,1)S(1)} %get-tuple-element.26.part_ref) | copy-start | bytes 50331652
  21.9 3.2 %collective-permute-start.4 = (bf16[64,4096]{1,0:T(8,128)(2,1)S(1)}, bf16[64,4096]{1,0:T(8,128)(2,1)S(1)}, u32[]{:S(2)}, u32[]{:S(2)}) collective-permute-start(bf16[64,4096]{1,0:T(8,128)(2,1)S(1)} %collective-permute-done.3.own_ref), channel_id=1, source_target_pairs={{0,1},{1,0},{2,3},{3,2},{4,5},{5,4},{6,7},{7,6},{8,9},{9,8},{10,11... | collective-permute-start | bytes 1572872 | tf_op jit(solution)/shard_map/ppermute | solution.py:429
  22.0 9.2 %collective-permute-start.7 = (bf16[64,4096]{1,0:T(8,128)(2,1)S(1)}, bf16[64,4096]{1,0:T(8,128)(2,1)S(1)}, u32[]{:S(2)}, u32[]{:S(2)}) collective-permute-start(bf16[64,4096]{1,0:T(8,128)(2,1)S(1)} %collective-permute-done.3.own_ref), channel_id=1, source_target_pairs={{0,4},{4,8},{8,12},{12,14},{14,10},{10,6},{6,2},{2,0},{5,1},{9,5},... | collective-permute-start | bytes 1572872 | tf_op jit(solution)/shard_map/ppermute | solution.py:427
  23.6 9.2 %collective-permute-start.2 = (bf16[64,4224]{1,0:T(8,128)(2,1)S(1)}, bf16[64,4224]{1,0:T(8,128)(2,1)S(1)}, u32[]{:S(2)}, u32[]{:S(2)}) collective-permute-start(bf16[64,4224]{1,0:T(8,128)(2,1)S(1)} %collective-permute-done.own_ref), channel_id=1, source_target_pairs={{0,1},{1,0},{2,3},{3,2},{4,5},{5,4},{6,7},{7,6},{8,9},{9,8},{10,11... | collective-permute-start | bytes 1622024 | tf_op jit(solution)/shard_map/ppermute | solution.py:429
  23.6 13.4 %collective-permute-start.1 = (bf16[64,4224]{1,0:T(8,128)(2,1)S(1)}, bf16[64,4224]{1,0:T(8,128)(2,1)S(1)}, u32[]{:S(2)}, u32[]{:S(2)}) collective-permute-start(bf16[64,4224]{1,0:T(8,128)(2,1)S(1)} %collective-permute-done.own_ref), channel_id=1, source_target_pairs={{0,4},{4,8},{8,12},{12,14},{14,10},{10,6},{6,2},{2,0},{5,1},{9,5},... | collective-permute-start | bytes 1622024 | tf_op jit(solution)/shard_map/ppermute | solution.py:427
  31.2 7.4 %collective-permute-start.8 = (bf16[64,4096]{1,0:T(8,128)(2,1)S(1)}, bf16[64,4096]{1,0:T(8,128)(2,1)S(1)}, u32[]{:S(2)}, u32[]{:S(2)}) collective-permute-start(bf16[64,4096]{1,0:T(8,128)(2,1)S(1)} %collective-permute-done.7.own_ref), channel_id=1, source_target_pairs={{0,1},{1,0},{2,3},{3,2},{4,5},{5,4},{6,7},{7,6},{8,9},{9,8},{10,11... | collective-permute-start | bytes 1572872 | tf_op jit(solution)/shard_map/ppermute | solution.py:429
  31.2 15.7 %collective-permute-start.11 = (bf16[64,4096]{1,0:T(8,128)(2,1)S(1)}, bf16[64,4096]{1,0:T(8,128)(2,1)S(1)}, u32[]{:S(2)}, u32[]{:S(2)}) collective-permute-start(bf16[64,4096]{1,0:T(8,128)(2,1)S(1)} %collective-permute-done.7.own_ref), channel_id=1, source_target_pairs={{0,4},{4,8},{8,12},{12,14},{14,10},{10,6},{6,2},{2,0},{5,1},{9,5},... | collective-permute-start | bytes 1572872 | tf_op jit(solution)/shard_map/ppermute | solution.py:427
  37.0 11.6 %collective-permute-start.6 = (bf16[64,4224]{1,0:T(8,128)(2,1)S(1)}, bf16[64,4224]{1,0:T(8,128)(2,1)S(1)}, u32[]{:S(2)}, u32[]{:S(2)}) collective-permute-start(bf16[64,4224]{1,0:T(8,128)(2,1)S(1)} %collective-permute-done.1.own_ref), channel_id=1, source_target_pairs={{0,1},{1,0},{2,3},{3,2},{4,5},{5,4},{6,7},{7,6},{8,9},{9,8},{10,11... | collective-permute-start | bytes 1622024 | tf_op jit(solution)/shard_map/ppermute | solution.py:429
  37.0 16.4 %collective-permute-start.5 = (bf16[64,4224]{1,0:T(8,128)(2,1)S(1)}, bf16[64,4224]{1,0:T(8,128)(2,1)S(1)}, u32[]{:S(2)}, u32[]{:S(2)}) collective-permute-start(bf16[64,4224]{1,0:T(8,128)(2,1)S(1)} %collective-permute-done.1.own_ref), channel_id=1, source_target_pairs={{0,4},{4,8},{8,12},{12,14},{14,10},{10,6},{6,2},{2,0},{5,1},{9,5},... | collective-permute-start | bytes 1622024 | tf_op jit(solution)/shard_map/ppermute | solution.py:427
  38.6 5.8 %copy-start.1 = (bf16[8192,1024]{1,0:T(8,128)(2,1)S(1)}, bf16[8192,1024]{1,0:T(8,128)(2,1)}, u32[]{:S(2)}) copy-start(bf16[8192,1024]{1,0:T(8,128)(2,1)} %copy-done) | copy-start | bytes 50331652
  46.9 8.2 %collective-permute-start.12 = (bf16[64,4096]{1,0:T(8,128)(2,1)S(1)}, bf16[64,4096]{1,0:T(8,128)(2,1)S(1)}, u32[]{:S(2)}, u32[]{:S(2)}) collective-permute-start(bf16[64,4096]{1,0:T(8,128)(2,1)S(1)} %collective-permute-done.11.own_ref), channel_id=1, source_target_pairs={{0,1},{1,0},{2,3},{3,2},{4,5},{5,4},{6,7},{7,6},{8,9},{9,8},{10,11... | collective-permute-start | bytes 1572872 | tf_op jit(solution)/shard_map/ppermute | solution.py:429
  47.0 10.6 %collective-permute-start.14 = (bf16[64,2048]{1,0:T(8,128)(2,1)S(1)}, bf16[64,2048]{1,0:T(8,128)(2,1)S(1)}, u32[]{:S(2)}, u32[]{:S(2)}) collective-permute-start(bf16[64,2048]{1,0:T(8,128)(2,1)S(1)} %constant_dynamic-slice_fusion.1), channel_id=1, source_target_pairs={{0,4},{4,8},{8,12},{12,14},{14,10},{10,6},{6,2},{2,0},{5,1},{9,5},... | collective-permute-start | bytes 786440 | tf_op jit(solution)/shard_map/ppermute | solution.py:427
  53.4 4.3 %collective-permute-start.10 = (bf16[64,4224]{1,0:T(8,128)(2,1)S(1)}, bf16[64,4224]{1,0:T(8,128)(2,1)S(1)}, u32[]{:S(2)}, u32[]{:S(2)}) collective-permute-start(bf16[64,4224]{1,0:T(8,128)(2,1)S(1)} %collective-permute-done.5.own_ref), channel_id=1, source_target_pairs={{0,1},{1,0},{2,3},{3,2},{4,5},{5,4},{6,7},{7,6},{8,9},{9,8},{10,11... | collective-permute-start | bytes 1622024 | tf_op jit(solution)/shard_map/ppermute | solution.py:429
  53.5 7.4 %collective-permute-start.9 = (bf16[64,2176]{1,0:T(8,128)(2,1)S(1)}, bf16[64,2176]{1,0:T(8,128)(2,1)S(1)}, u32[]{:S(2)}, u32[]{:S(2)}) collective-permute-start(bf16[64,2176]{1,0:T(8,128)(2,1)S(1)} %constant_dynamic-slice_fusion.2), channel_id=1, source_target_pairs={{0,4},{4,8},{8,12},{12,14},{14,10},{10,6},{6,2},{2,0},{5,1},{9,5},... | collective-permute-start | bytes 835592 | tf_op jit(solution)/shard_map/ppermute | solution.py:427
  57.6 3.9 %collective-permute-start.15 = (bf16[64,2048]{1,0:T(8,128)(2,1)S(1)}, bf16[64,2048]{1,0:T(8,128)(2,1)S(1)}, u32[]{:S(2)}, u32[]{:S(2)}) collective-permute-start(bf16[64,2048]{1,0:T(8,128)(2,1)S(1)} %collective-permute-done.14.own_ref), channel_id=1, source_target_pairs={{0,1},{1,0},{2,3},{3,2},{4,5},{5,4},{6,7},{7,6},{8,9},{9,8},{10,11... | collective-permute-start | bytes 786440 | tf_op jit(solution)/shard_map/ppermute | solution.py:429
  60.9 3.2 %collective-permute-start.13 = (bf16[64,2176]{1,0:T(8,128)(2,1)S(1)}, bf16[64,2176]{1,0:T(8,128)(2,1)S(1)}, u32[]{:S(2)}, u32[]{:S(2)}) collective-permute-start(bf16[64,2176]{1,0:T(8,128)(2,1)S(1)} %collective-permute-done.9.own_ref), channel_id=1, source_target_pairs={{0,1},{1,0},{2,3},{3,2},{4,5},{5,4},{6,7},{7,6},{8,9},{9,8},{10,11... | collective-permute-start | bytes 835592 | tf_op jit(solution)/shard_map/ppermute | solution.py:429
  64.1 22.0 %copy-start.6 = (s32[8]{0:T(128)S(1)}, s32[8]{0:T(128)}, u32[]{:S(2)}) copy-start(s32[8]{0:T(128)} %param.10) | copy-start | bytes 100
  71.2 1.4 %collective-permute-start.16 = (f32[8,4,1152]{2,1,0:T(4,128)S(1)}, f32[8,4,1152]{2,1,0:T(4,128)S(1)}, u32[]{:S(2)}, u32[]{:S(2)}) collective-permute-start(f32[8,4,1152]{2,1,0:T(4,128)S(1)} %get-tuple-element.49), channel_id=1, source_target_pairs={{0,1},{1,0},{2,3},{3,2},{4,5},{5,4},{6,7},{7,6},{8,9},{9,8},{10,11... | collective-permute-start | bytes 442376 | tf_op jit(solution)/shard_map/ppermute | solution.py:445
  72.7 4.4 %collective-permute-start.17 = (f32[4,4,1152]{2,1,0:T(4,128)S(1)}, f32[4,4,1152]{2,1,0:T(4,128)S(1)}, u32[]{:S(2)}, u32[]{:S(2)}) collective-permute-start(f32[4,4,1152]{2,1,0:T(4,128)S(1)} %dynamic-slice_bitcast_fusion), channel_id=1, source_target_pairs={{0,2},{2,0},{4,6},{6,4},{8,10},{10,8},{12,14},{14,12},{1,3},{3,1},... | collective-permute-start | bytes 221192 | tf_op jit(solution)/shard_map/ppermute | solution.py:385
  77.2 4.0 %collective-permute-start.18 = (f32[2,4,1152]{2,1,0:T(4,128)S(1)}, f32[2,4,1152]{2,1,0:T(4,128)S(1)}, u32[]{:S(2)}, u32[]{:S(2)}) collective-permute-start(f32[2,4,1152]{2,1,0:T(4,128)S(1)} %dynamic-slice_bitcast_fusion.1), channel_id=1, source_target_pairs={{0,4},{2,6},{4,0},{6,2},{8,12},{10,14},{12,8},{14,10},{1,5},{3,7},... | collective-permute-start | bytes 110600 | tf_op jit(solution)/shard_map/ppermute | solution.py:385
  81.3 4.7 %collective-permute-start.19 = (f32[1,4,1152]{2,1,0:T(4,128)S(1)}, f32[1,4,1152]{2,1,0:T(4,128)S(1)}, u32[]{:S(2)}, u32[]{:S(2)}) collective-permute-start(f32[1,4,1152]{2,1,0:T(4,128)S(1)} %constant_dynamic-slice_fusion), channel_id=1, source_target_pairs={{0,8},{2,10},{4,12},{6,14},{8,0},{10,2},{12,4},{14,6},{1,9},{3,11}... | collective-permute-start | bytes 55304 | tf_op jit(solution)/shard_map/ppermute | solution.py:385
  (3 other events, 12.2 us)

commit v5 on v4

--- a/solution.py
+++ b/solution.py
@@ -8,13 +8,14 @@
 from jax.sharding import PartitionSpec as P
 
 LOWEST = -1e30
-STEPS = 8
+STEPS = 16
 WIDTH = 1024
-SLOTS = 3
+SLOTS = 4
 STRIP = 256
 LANES = 128
 STATE_ROWS = 8
-VMEM_LIMIT = 12 * 1024 * 1024
+VMEM_LIMIT = 10 * 1024 * 1024
+SMALL_LIMIT = 6 * 1024 * 1024
 
 
 def ring_order(blocks):
@@ -23,44 +24,45 @@
     return list(range(blocks))
 
 
-def message_kernel(tags_ref, rows_ref, first_ref, second_ref, sent):
+def message_kernel(tags_ref, rows_ref, first_ref, second_ref, tags, sent):
     height, span = first_ref.shape
     copies = [
-        pltpu.make_async_copy(rows_ref.at[:, :span], first_ref, sent.at[0]),
-        pltpu.make_async_copy(rows_ref.at[:, span:], second_ref.at[:, :span], sent.at[1]),
+        pltpu.make_async_copy(tags_ref, tags, sent.at[0]),
+        pltpu.make_async_copy(rows_ref.at[:, :span], first_ref, sent.at[1]),
+        pltpu.make_async_copy(rows_ref.at[:, span:], second_ref.at[:, :span], sent.at[2]),
     ]
     for copy in copies:
         copy.start()
-    second_ref[:, span:] = tag_rows(tags_ref, height).astype(jnp.bfloat16)
-    for copy in copies:
+    copies[0].wait()
+    second_ref[:, span:] = tag_rows(tags, height).astype(jnp.bfloat16)
+    for copy in copies[1:]:
         copy.wait()
 
 
-def make_messages(template_class, templates):
+def make_messages(tags, templates):
     height, freqs = templates.shape
     span = freqs // 2
     return pl.pallas_call(
         message_kernel,
-        in_specs=[in_smem(), pl.BlockSpec(memory_space=pl.ANY)],
+        in_specs=[pl.BlockSpec(memory_space=pl.ANY)] * 2,
         out_specs=[in_vmem(), in_vmem()],
         out_shape=[
             pltpu.VMEM((height, span), jnp.bfloat16),
             pltpu.VMEM((height, span + LANES), jnp.bfloat16),
         ],
-        scratch_shapes=[pltpu.SemaphoreType.DMA((2,))],
-        compiler_params=pltpu.CompilerParams(vmem_limit_bytes=VMEM_LIMIT),
+        scratch_shapes=[pltpu.VMEM(tags.shape, tags.dtype), pltpu.SemaphoreType.DMA((3,))],
+        compiler_params=pltpu.CompilerParams(vmem_limit_bytes=SMALL_LIMIT),
     )(
-        pltpu.with_memory_space_constraint(template_class, pltpu.HBM),
+        pltpu.with_memory_space_constraint(tags, pltpu.HBM),
         pltpu.with_memory_space_constraint(templates, pltpu.HBM),
     )
 
 
 def tag_rows(tags_ref, height):
-    row = lax.broadcasted_iota(jnp.int32, (height, LANES), 0)
-    tags = jnp.zeros((height, LANES), jnp.float32)
-    for r in range(height):
-        tags = jnp.where(row == r, tags_ref[r].astype(jnp.float32), tags)
-    return tags
+    row = lax.broadcasted_iota(jnp.int32, (height, height), 0)
+    lane = lax.broadcasted_iota(jnp.int32, (height, height), 1)
+    spread = jnp.where(row == lane, tags_ref[...].astype(jnp.float32), 0.0)
+    return jnp.broadcast_to(jnp.sum(spread, axis=1, keepdims=True), (height, LANES))
 
 
 def in_smem():
@@ -71,7 +73,7 @@
     return pl.BlockSpec(memory_space=pltpu.VMEM)
 
 
-def add_scores(rows, noise, part, acc, energy):
+def weigh(rows, noise, energy):
     widened = rows.astype(jnp.float32)
     product = widened * noise
     square = product * widened
@@ -79,12 +81,7 @@
     for lane in range(LANES, square.shape[1], LANES):
         folded = folded + square[:, lane : lane + LANES]
     energy[...] += folded
-    acc[...] += lax.dot_general(
-        product.astype(jnp.bfloat16),
-        part,
-        (((1,), (0,)), ((), ())),
-        preferred_element_type=jnp.float32,
-    )
+    return product.astype(jnp.bfloat16)
 
 
 def pick_words(sig_ref, words_ref):
@@ -145,45 +142,58 @@
     return state_ref[0:1, :], state_ref[1:2, :], state_ref[2:3, :], state_ref[STATE_ROWS:, :]
 
 
-def own_kernel(
-    where_ref, logs_ref, tags_ref, sig_ref, noise_ref, tmpl_ref, far_ref,
-    out_ref, turned_ref, words_ref, acc, energy, slots, arrived,
-):
-    freqs = noise_ref.shape[1]
+def own_kernel(phase, where_ref, noise_ref, tmpl_ref, far_ref, *rest):
+    if phase == 0:
+        sig_ref, turned_ref, words_ref, acc, energy, slots, arrived = rest
+    else:
+        acc_in, energy_in, logs_ref, tags_ref, words_ref, *rest = rest
+        turned_ref, out_ref, acc, energy, slots, arrived = rest
+    span = turned_ref.shape[0]
     height = tmpl_ref.shape[0]
-    width = freqs // STEPS
+    width = slots.shape[2]
+    steps = span // width
+    low = phase * span
 
     def copy(step):
-        columns = pl.ds(pl.multiple_of(step * width, width), width)
+        columns = pl.ds(pl.multiple_of(low + step * width, width), width)
         slot = lax.rem(step, SLOTS)
         return pltpu.make_async_copy(far_ref.at[:, columns], slots.at[slot], arrived.at[slot])
 
     for step in range(SLOTS):
         copy(step).start()
-    pick_words(sig_ref, words_ref)
-    acc[...] = jnp.zeros_like(acc)
-    energy[...] = jnp.zeros_like(energy)
-
-    @pl.loop(0, STEPS)
+    if phase == 0:
+        pick_words(sig_ref, words_ref)
+        acc[...] = jnp.zeros_like(acc)
+        energy[...] = jnp.zeros_like(energy)
+    else:
+        acc[...] = acc_in[...]
+        energy[...] = energy_in[...]
+    across = lax.broadcasted_iota(jnp.int32, (STRIP, STRIP), 0)
+    along = lax.broadcasted_iota(jnp.int32, (STRIP, STRIP), 1)
+    identity = jnp.where(across == along, 1.0, 0.0).astype(jnp.bfloat16)
+
+    @pl.loop(0, steps)
     def _(step):
         copy(step).wait()
-        columns = pl.ds(pl.multiple_of(step * width, width), width)
         slot = lax.rem(step, SLOTS)
-
-        @pl.loop(0, width // STRIP)
-        def _(strip):
-            some = pl.ds(pl.multiple_of(strip * STRIP, STRIP), STRIP)
-            there = pl.ds(pl.multiple_of(step * width + strip * STRIP, STRIP), STRIP)
-            turned_ref[there, :] = jnp.transpose(slots[slot, :, some])
-
-        @pl.when(step + SLOTS < STEPS)
+        for strip in range(0, width, STRIP):
+            there = pl.ds(pl.multiple_of(step * width + strip, STRIP), STRIP)
+            weighted = weigh(tmpl_ref[:, there], noise_ref[:, there], energy)
+            both = lax.dot_general(
+                jnp.concatenate([weighted, identity], axis=0),
+                slots[slot, :, strip : strip + STRIP],
+                (((1,), (1,)), ((), ())),
+                preferred_element_type=jnp.float32,
+            )
+            acc[...] += both[:height]
+            turned_ref[there, :] = both[height:].astype(jnp.bfloat16)
+
+        @pl.when(step + SLOTS < steps)
         def _():
             copy(step + SLOTS).start()
 
-        add_scores(
-            tmpl_ref[:, columns], noise_ref[:, columns], turned_ref[columns, :], acc, energy
-        )
-
+    if phase == 0:
+        return
     tags = tag_rows(tags_ref, height)
     hit = picked_rows(words_ref, where_ref[0], height)
     lowest = jnp.full((1, acc.shape[1]), LOWEST, jnp.float32)
@@ -193,38 +203,50 @@
     put_state(add_rows(tags, hit, logs_ref, state, acc, energy), out_ref)
 
 
-def score_own(where, logs, template_class, significant, noise, templates, particles, total):
+def own_scores(phase, where, noise, templates, particles, rest, total=0):
     per_device, freqs = particles.shape
     height = templates.shape[0]
-    rows = STATE_ROWS + logs.shape[0]
+    width = freqs // STEPS
+    sums = [
+        jax.ShapeDtypeStruct((height, per_device), jnp.float32),
+        jax.ShapeDtypeStruct((height, LANES), jnp.float32),
+    ]
+    shapes = [pltpu.VMEM((freqs // 2, per_device), particles.dtype)]
+    scratch = [
+        pltpu.VMEM((SLOTS, per_device, width), particles.dtype),
+        pltpu.SemaphoreType.DMA((SLOTS,)),
+    ]
+    if phase == 0:
+        shapes += [jax.ShapeDtypeStruct((total // 32, per_device), jnp.int32)] + sums
+        rest_specs = [in_vmem()]
+    else:
+        rows = STATE_ROWS + rest[2].shape[0]
+        shapes.append(jax.ShapeDtypeStruct((rows, per_device), jnp.float32))
+        scratch = [pltpu.VMEM(array.shape, array.dtype) for array in sums] + scratch
+        rest_specs = [in_vmem(), in_vmem(), in_smem(), in_vmem(), in_vmem()]
     return pl.pallas_call(
-        own_kernel,
-        in_specs=[in_smem()] * 3 + [in_vmem()] * 3 + [pl.BlockSpec(memory_space=pl.ANY)],
-        out_specs=[in_vmem()] * 3,
-        out_shape=[
-            jax.ShapeDtypeStruct((rows, per_device), jnp.float32),
-            pltpu.VMEM((freqs, per_device), particles.dtype),
-            jax.ShapeDtypeStruct((total // 32, per_device), jnp.int32),
+        functools.partial(own_kernel, phase),
+        grid=(1,),
+        in_specs=[
+            in_smem(),
+            pl.BlockSpec((1, freqs // 2), lambda j: (0, phase)),
+            pl.BlockSpec((height, freqs // 2), lambda j: (0, phase)),
+            pl.BlockSpec(memory_space=pl.ANY),
+            *rest_specs,
         ],
-        scratch_shapes=[
-            pltpu.VMEM((height, per_device), jnp.float32),
-            pltpu.VMEM((height, LANES), jnp.float32),
-            pltpu.VMEM((SLOTS, per_device, freqs // STEPS), particles.dtype),
-            pltpu.SemaphoreType.DMA((SLOTS,)),
-        ],
+        out_specs=[in_vmem()] * len(shapes),
+        out_shape=shapes,
+        scratch_shapes=scratch,
         compiler_params=pltpu.CompilerParams(vmem_limit_bytes=VMEM_LIMIT),
         cost_estimate=pl.CostEstimate(
-            flops=4 * 128 * per_device * freqs,
-            bytes_accessed=2 * per_device * freqs,
+            flops=2 * 128 * per_device * freqs,
+            bytes_accessed=per_device * freqs,
             transcendentals=0,
         ),
     )(
         where,
-        logs,
-        *(
-            pltpu.with_memory_space_constraint(x, pltpu.HBM)
-            for x in (template_class, significant, noise, templates, particles)
-        ),
+        *(pltpu.with_memory_space_constraint(x, pltpu.HBM) for x in (noise, templates, particles)),
+        *rest,
     )
 
 
@@ -275,22 +297,25 @@
             out_ref, acc, energy = rest
         acc[...] = acc_in[...]
         energy[...] = energy_in[...]
-    freqs = noise_ref.shape[1]
-    span = freqs // 4 if ends else freqs // 2
+    half = part_ref.shape[0]
+    span = half // 2 if ends else half
     core = where_ref[1]
-    low = phase * (freqs // 2)
     if ends:
-        pieces = [((own_ref,), low + core * span), ((sib_ref,), low + (1 - core) * span)]
-    else:
-        pieces = [((own_ref, sib_ref), low)]
+        pieces = [((own_ref,), core * span), ((sib_ref,), (1 - core) * span)]
+    else:
+        pieces = [((own_ref, sib_ref), 0)]
     for refs, start in pieces:
 
         @pl.loop(0, span // WIDTH)
         def _(step):
             near = pl.ds(pl.multiple_of(step * WIDTH, WIDTH), WIDTH)
-            columns = pl.ds(pl.multiple_of(start + step * WIDTH, WIDTH), WIDTH)
+            there = pl.ds(pl.multiple_of(start + step * WIDTH, WIDTH), WIDTH)
+            columns = pl.ds(pl.multiple_of(phase * half + start + step * WIDTH, WIDTH), WIDTH)
             rows = jnp.concatenate([ref[:, near] for ref in refs], axis=0)
-            add_scores(rows, noise_ref[:, columns], part_ref[columns, :], acc, energy)
+            weighted = weigh(rows, noise_ref[:, columns], energy)
+            acc[...] += jnp.dot(
+                weighted, part_ref[there, :], preferred_element_type=jnp.float32
+            )
 
     if phase == 0:
         return
@@ -320,14 +345,15 @@
 
 def ring_scores(phase, sources, where, noise, turned, own, sib, rest, blocks=0, owners=0):
     ends = blocks > 0
-    freqs, per_device = turned.shape
+    half, per_device = turned.shape
+    freqs = 2 * half
     rows = own.shape[0] * (1 if ends else 2)
     sums = [
         jax.ShapeDtypeStruct((rows, per_device), jnp.float32),
         jax.ShapeDtypeStruct((rows, LANES), jnp.float32),
     ]
     scratch = [pltpu.VMEM(array.shape, array.dtype) for array in sums]
-    limit = VMEM_LIMIT
+    limit = SMALL_LIMIT
     if phase == 0:
         shapes, scratch, rest_specs = sums, [], []
     else:
@@ -401,14 +427,21 @@
 
     noise = inv_noise[None, :]
     logs = jnp.log(class_counts.astype(jnp.float32))
-    held = make_messages(template_class, templates)
+    tags = template_class[None, :]
+    held = make_messages(tags, templates)
     where = jnp.stack([block_id, core])
-    state, turned, words = score_own(
-        where, logs, template_class, significant, noise, templates, particles,
-        blocks * templates.shape[0],
-    )
+    cut = freqs // 4
+    where, cut_at = lax.optimization_barrier((where, core.astype(jnp.uint32) * cut))
+    picks = pltpu.with_memory_space_constraint(significant, pltpu.HBM)
+    first, words, *sums = own_scores(
+        0, where, noise, templates, particles, (picks,), blocks * templates.shape[0]
+    )
+    second, state = own_scores(
+        1, where, noise, templates, particles, (*sums, logs, tags, words)
+    )
+    turned = (first, second)
     last = blocks // 2
-    gates = [state]
+    gates = [sums, state]
     for distance in range(1, last + 1):
         ends = distance == last
         sources = [
@@ -420,21 +453,22 @@
         for phase in range(2):
             message = held[phase]
             if ends:
-                cut = freqs // 4
-                message = lax.dynamic_slice_in_dim(
-                    message, core * cut, message.shape[1] - cut, 1
+                message = lax.dynamic_slice(
+                    message,
+                    (jnp.uint32(0), cut_at),
+                    (message.shape[0], message.shape[1] - cut),
                 )
             own = lax.ppermute(message, ("blk", "cls"), ring)
-            own, _ = lax.optimization_barrier((own, gates[max(len(gates) - 2, 0)]))
+            own, _ = lax.optimization_barrier((own, gates[len(gates) - 2]))
             sib = lax.ppermute(own, "cls", swap)
             rest = () if phase == 0 else (*sums, logs, words, state)
             if ends:
                 rest += (particles,) if phase else ()
                 sums = ring_scores(
-                    phase, sources, where, noise, turned, own, sib, rest, blocks, owners
+                    phase, sources, where, noise, turned[phase], own, sib, rest, blocks, owners
                 )
             else:
-                sums = ring_scores(phase, sources, where, noise, turned, own, sib, rest)
+                sums = ring_scores(phase, sources, where, noise, turned[phase], own, sib, rest)
             gates.append(sums)
             arrived.append(own)
         held = arrived

time: 87.2 us -> 76.8 us (0.88)
  local copies, waits for them, and re-layouts: 8.19 us -> 0.45 us
  waiting for transfers between devices: 15.4 us -> 14.5 us
    unnamed x14 -> x6, local copies, waits for them, and re-layouts: 7.97 us -> 0.01 us
    pallas_call x2 -> x3, Pallas kernels: 15.8 us -> 15 us  [the longest x2 13.8 us: own_scores(): pl.pallas_call(functools.partial(own_kernel, phase), grid=(1,), in_specs=...]
  transfers between devices with their start and end apart: 20 -> 20, of which waited for: 6 -> 7; matrix products, arithmetic and copies ran while one was open for 1% -> 0% of each run, Pallas kernels for 39% -> 44%
where the time goes in v5:
time: 76.8 us; the launch traced here: 76.6 us
  Pallas kernels  42.1 us (55%)
  starting transfers between devices  17.9 us (23%)
  waiting for transfers between devices  14.5 us (19%)
  other arithmetic  0.93 us (1%)
  between operations  0.84 us (1%)
    pallas_call x8, Pallas kernels, ring_scores(): pl.pallas_call(functools.partial(ring_kernel, phase, ends, sources), in_s...  27 us
    pallas_call x2, Pallas kernels, own_scores(): pl.pallas_call(functools.partial(own_kernel, phase), grid=(1,), in_specs=...  13.8 us
    ppermute x8, starting transfers between devices, body(): own = lax.ppermute(message, ('blk', 'cls'), ring)  13.4 us
    ppermute x3, waiting for transfers between devices, scatter_sum(): pieces = keep + lax.ppermute(send, 'blk', swaps)  9.61 us
    ppermute x3, starting transfers between devices, scatter_sum(): pieces = keep + lax.ppermute(send, 'blk', swaps)  3.55 us
    ppermute x8, waiting for transfers between devices, body(): own = lax.ppermute(message, ('blk', 'cls'), ring)  3.49 us
  transfers between devices with their start and end apart: 20, of which 7 were waited for; matrix products, arithmetic and copies ran while one was open for 0% of the time, Pallas kernels for 44%

profile of v5, /device:TPU:0, one launch (start us, length us, event | category | flops | bytes accessed | tf_op | source)
XLA Modules:
  0.0 76.6 jit_solution(17319192699002335081)
XLA Ops:
  0.6 1.2 %shard_map.79 = (bf16[64,4096]{1,0:T(8,128)(2,1)S(1)}, bf16[64,4224]{1,0:T(8,128)(2,1)S(1)}) custom-call(s32[1,64]{1,0:T(1,128)} %bitcast.27, bf16[64,8192]{1,0:T(8,128)(2,1)} %rows_ref.1), custom_call_target="tpu_custom_call" | custom-call | tf_op jit(solution)/shard_map/pallas_call | solution.py:45
  1.9 3.1 %collective-permute-start.3 = (bf16[64,4096]{1,0:T(8,128)(2,1)S(1)}, bf16[64,4096]{1,0:T(8,128)(2,1)S(1)}, u32[]{:S(2)}, u32[]{:S(2)}) collective-permute-start(bf16[64,4096]{1,0:T(8,128)(2,1)S(1)} %get-tuple-element.40), channel_id=1, source_target_pairs={{0,4},{4,8},{8,12},{12,14},{14,10},{10,6},{6,2},{2,0},{5,1},{9,5},... | collective-permute-start | bytes 1572872 | tf_op jit(solution)/shard_map/ppermute | solution.py:461
  5.0 1.6 %collective-permute-start = (bf16[64,4224]{1,0:T(8,128)(2,1)S(1)}, bf16[64,4224]{1,0:T(8,128)(2,1)S(1)}, u32[]{:S(2)}, u32[]{:S(2)}) collective-permute-start(bf16[64,4224]{1,0:T(8,128)(2,1)S(1)} %get-tuple-element.36), channel_id=1, source_target_pairs={{0,4},{4,8},{8,12},{12,14},{14,10},{10,6},{6,2},{2,0},{5,1},{9,5},... | collective-permute-start | bytes 1622024 | tf_op jit(solution)/shard_map/ppermute | solution.py:461
  6.6 6.6 %shard_map.77 = (bf16[4096,1024]{1,0:T(8,128)(2,1)S(1)}, s32[16,1024]{1,0:T(8,128)S(1)}, f32[64,1024]{1,0:T(8,128)S(1)}, f32[64,128]{1,0:T(8,128)S(1)}) custom-call(s32[2]{0:T(128)S(1)} %pad_add_fusion.where_ref, f32[1,8192]{1,0:T(1,128)} %bitcast.17, bf16[64,8192]{1,0:T(8,128)(2,1)} %rows_ref.1, bf16[1024,8192]{1,0:T(8,128)(2,1)} %rest_5_.1, s32[16,1024]{1,0:T(8,128)} %rest_0_.1), custom_call_target="tpu_custom_call" | custom-call | flops 2147483648 | bytes 8388608 | tf_op jit(solution)/shard_map/pallas_call | solution.py:227
  13.4 1.6 %collective-permute-start.7 = (bf16[64,4096]{1,0:T(8,128)(2,1)S(1)}, bf16[64,4096]{1,0:T(8,128)(2,1)S(1)}, u32[]{:S(2)}, u32[]{:S(2)}) collective-permute-start(bf16[64,4096]{1,0:T(8,128)(2,1)S(1)} %collective-permute-done.3.own_ref), channel_id=1, source_target_pairs={{0,4},{4,8},{8,12},{12,14},{14,10},{10,6},{6,2},{2,0},{5,1},{9,5},... | collective-permute-start | bytes 1572872 | tf_op jit(solution)/shard_map/ppermute | solution.py:461
  15.0 7.1 %shard_map.78 = (bf16[4096,1024]{1,0:T(8,128)(2,1)S(1)}, f32[16,1024]{1,0:T(8,128)S(1)}) custom-call(s32[2]{0:T(128)S(1)} %pad_add_fusion.where_ref, f32[1,8192]{1,0:T(1,128)} %bitcast.18, bf16[64,8192]{1,0:T(8,128)(2,1)} %rows_ref.1, bf16[1024,8192]{1,0:T(8,128)(2,1)} %rest_5_.1, f32[64,1024]{1,0:T(8,128)S(1)} %get-tuple-element.32.rest_0_, ...), custom_call_target="tpu_custom_call" | custom-call | flops 2147483648 | bytes 8388608 | tf_op jit(solution)/shard_map/pallas_call | solution.py:227
  22.2 1.6 %collective-permute-start.1 = (bf16[64,4224]{1,0:T(8,128)(2,1)S(1)}, bf16[64,4224]{1,0:T(8,128)(2,1)S(1)}, u32[]{:S(2)}, u32[]{:S(2)}) collective-permute-start(bf16[64,4224]{1,0:T(8,128)(2,1)S(1)} %collective-permute-done.own_ref), channel_id=1, source_target_pairs={{0,4},{4,8},{8,12},{12,14},{14,10},{10,6},{6,2},{2,0},{5,1},{9,5},... | collective-permute-start | bytes 1622024 | tf_op jit(solution)/shard_map/ppermute | solution.py:461
  23.8 2.5 %shard_map.80 = (f32[128,1024]{1,0:T(8,128)S(1)}, f32[128,128]{1,0:T(8,128)S(1)}) custom-call(s32[2]{0:T(128)S(1)} %pad_add_fusion.where_ref, f32[1,8192]{1,0:T(1,128)S(1)} %bitcast.19, bf16[4096,1024]{1,0:T(8,128)(2,1)S(1)} %get-tuple-element.39.part_ref, bf16[64,4096]{1,0:T(8,128)(2,1)S(1)} %collective-permute-done.3.own_ref, ...), custom_call_target="tpu_custom_call" | custom-call | flops 2147483648 | bytes 8388608 | tf_op jit(solution)/shard_map/pallas_call | solution.py:376
  27.3 3.3 %shard_map.81.rest_4_ = f32[16,1024]{1,0:T(8,128)S(1)} custom-call(s32[2]{0:T(128)S(1)} %pad_add_fusion.where_ref, f32[1,8192]{1,0:T(1,128)S(1)} %bitcast.20, bf16[4096,1024]{1,0:T(8,128)(2,1)S(1)} %get-tuple-element.35.part_ref, bf16[64,4224]{1,0:T(8,128)(2,1)S(1)} %collective-permute-done.own_ref, bf16[64,4224]{1,0:T(8,128)(2,1)S(1)} %collective-permute-done.2.sib_ref, ...), custom_call_target="tpu_custom_call" | custom-call | flops 2147483648 | bytes 8388608 | tf_op jit(solution)/shard_map/pallas_call | solution.py:376
  31.7 1.5 %collective-permute-start.5 = (bf16[64,4224]{1,0:T(8,128)(2,1)S(1)}, bf16[64,4224]{1,0:T(8,128)(2,1)S(1)}, u32[]{:S(2)}, u32[]{:S(2)}) collective-permute-start(bf16[64,4224]{1,0:T(8,128)(2,1)S(1)} %collective-permute-done.1.own_ref), channel_id=1, source_target_pairs={{0,4},{4,8},{8,12},{12,14},{14,10},{10,6},{6,2},{2,0},{5,1},{9,5},... | collective-permute-start | bytes 1622024 | tf_op jit(solution)/shard_map/ppermute | solution.py:461
  33.2 2.5 %shard_map.82 = (f32[128,1024]{1,0:T(8,128)S(1)}, f32[128,128]{1,0:T(8,128)S(1)}) custom-call(s32[2]{0:T(128)S(1)} %pad_add_fusion.where_ref, f32[1,8192]{1,0:T(1,128)S(1)} %bitcast.21, bf16[4096,1024]{1,0:T(8,128)(2,1)S(1)} %get-tuple-element.39.part_ref, bf16[64,4096]{1,0:T(8,128)(2,1)S(1)} %collective-permute-done.7.own_ref, ...), custom_call_target="tpu_custom_call" | custom-call | flops 2147483648 | bytes 8388608 | tf_op jit(solution)/shard_map/pallas_call | solution.py:376
  35.7 1.6 %collective-permute-done.11.own_ref = bf16[64,4096]{1,0:T(8,128)(2,1)S(1)} collective-permute-done((bf16[64,4096]{1,0:T(8,128)(2,1)S(1)}, bf16[64,4096]{1,0:T(8,128)(2,1)S(1)}, u32[]{:S(2)}, u32[]{:S(2)}) %collective-permute-start.11) | collective-permute-done | bytes 524320 | tf_op jit(solution)/shard_map/ppermute | solution.py:461
  37.4 1.6 %collective-permute-start.14 = (bf16[64,2048]{1,0:T(8,128)(2,1)S(1)}, bf16[64,2048]{1,0:T(8,128)(2,1)S(1)}, u32[]{:S(2)}, u32[]{:S(2)}) collective-permute-start(bf16[64,2048]{1,0:T(8,128)(2,1)S(1)} %constant_dynamic-slice_fusion.1), channel_id=1, source_target_pairs={{0,4},{4,8},{8,12},{12,14},{14,10},{10,6},{6,2},{2,0},{5,1},{9,5},... | collective-permute-start | bytes 786440 | tf_op jit(solution)/shard_map/ppermute | solution.py:461
  39.0 3.3 %shard_map.83.rest_4_ = f32[16,1024]{1,0:T(8,128)S(1)} custom-call(s32[2]{0:T(128)S(1)} %pad_add_fusion.where_ref, f32[1,8192]{1,0:T(1,128)S(1)} %bitcast.22, bf16[4096,1024]{1,0:T(8,128)(2,1)S(1)} %get-tuple-element.35.part_ref, bf16[64,4224]{1,0:T(8,128)(2,1)S(1)} %collective-permute-done.1.own_ref, bf16[64,4224]{1,0:T(8,128)(2,1)S(1)} %collective-permute-done.6.sib_ref, ...), custom_call_target="tpu_custom_call" | custom-call | flops 2147483648 | bytes 8388608 | tf_op jit(solution)/shard_map/pallas_call | solution.py:376
  43.2 1.6 %collective-permute-start.9 = (bf16[64,2176]{1,0:T(8,128)(2,1)S(1)}, bf16[64,2176]{1,0:T(8,128)(2,1)S(1)}, u32[]{:S(2)}, u32[]{:S(2)}) collective-permute-start(bf16[64,2176]{1,0:T(8,128)(2,1)S(1)} %constant_dynamic-slice_fusion.2), channel_id=1, source_target_pairs={{0,4},{4,8},{8,12},{12,14},{14,10},{10,6},{6,2},{2,0},{5,1},{9,5},... | collective-permute-start | bytes 835592 | tf_op jit(solution)/shard_map/ppermute | solution.py:461
  44.8 2.5 %shard_map.84 = (f32[128,1024]{1,0:T(8,128)S(1)}, f32[128,128]{1,0:T(8,128)S(1)}) custom-call(s32[2]{0:T(128)S(1)} %pad_add_fusion.where_ref, f32[1,8192]{1,0:T(1,128)S(1)} %bitcast.23, bf16[4096,1024]{1,0:T(8,128)(2,1)S(1)} %get-tuple-element.39.part_ref, bf16[64,4096]{1,0:T(8,128)(2,1)S(1)} %collective-permute-done.11.own_ref, ...), custom_call_target="tpu_custom_call" | custom-call | flops 2147483648 | bytes 8388608 | tf_op jit(solution)/shard_map/pallas_call | solution.py:376
  47.4 3.3 %shard_map.85.rest_4_ = f32[16,1024]{1,0:T(8,128)S(1)} custom-call(s32[2]{0:T(128)S(1)} %pad_add_fusion.where_ref, f32[1,8192]{1,0:T(1,128)S(1)} %bitcast.24, bf16[4096,1024]{1,0:T(8,128)(2,1)S(1)} %get-tuple-element.35.part_ref, bf16[64,4224]{1,0:T(8,128)(2,1)S(1)} %collective-permute-done.5.own_ref, bf16[64,4224]{1,0:T(8,128)(2,1)S(1)} %collective-permute-done.10.sib_ref, ...), custom_call_target="tpu_custom_call" | custom-call | flops 2147483648 | bytes 8388608 | tf_op jit(solution)/shard_map/pallas_call | solution.py:376
  51.2 2.6 %shard_map.86 = (f32[64,1024]{1,0:T(8,128)S(1)}, f32[64,128]{1,0:T(8,128)S(1)}) custom-call(s32[2]{0:T(128)S(1)} %pad_add_fusion.where_ref, f32[1,8192]{1,0:T(1,128)S(1)} %bitcast.25, bf16[4096,1024]{1,0:T(8,128)(2,1)S(1)} %get-tuple-element.39.part_ref, bf16[64,2048]{1,0:T(8,128)(2,1)S(1)} %collective-permute-done.14.own_ref, ...), custom_call_target="tpu_custom_call" | custom-call | flops 2147483648 | bytes 8388608 | tf_op jit(solution)/shard_map/pallas_call | solution.py:376
  53.8 7.1 %shard_map.87 = (f32[1,1024]{1,0:T(1,128)}, f32[8,4,1152]{2,1,0:T(4,128)S(1)}, f32[8,4,1152]{2,1,0:T(4,128)S(1)}) custom-call(s32[2]{0:T(128)S(1)} %pad_add_fusion.where_ref, f32[1,8192]{1,0:T(1,128)S(1)} %bitcast.26, bf16[4096,1024]{1,0:T(8,128)(2,1)S(1)} %get-tuple-element.35.part_ref, bf16[64,2176]{1,0:T(8,128)(2,1)S(1)} %collective-permute-done.9.own_ref, ...), custom_call_target="tpu_custom_call" | custom-call | flops 2147483648 | bytes 8388608 | tf_op jit(solution)/shard_map/pallas_call | solution.py:376
  61.1 1.3 %collective-permute-done.16 = f32[8,4,1152]{2,1,0:T(4,128)S(1)} collective-permute-done((f32[8,4,1152]{2,1,0:T(4,128)S(1)}, f32[8,4,1152]{2,1,0:T(4,128)S(1)}, u32[]{:S(2)}, u32[]{:S(2)}) %collective-permute-start.16) | collective-permute-done | bytes 147488 | tf_op jit(solution)/shard_map/ppermute | solution.py:479
  63.3 3.6 %collective-permute-done.17 = f32[4,4,1152]{2,1,0:T(4,128)S(1)} collective-permute-done((f32[4,4,1152]{2,1,0:T(4,128)S(1)}, f32[4,4,1152]{2,1,0:T(4,128)S(1)}, u32[]{:S(2)}, u32[]{:S(2)}) %collective-permute-start.17) | collective-permute-done | bytes 73760 | tf_op jit(solution)/shard_map/ppermute | solution.py:411
  67.8 3.1 %collective-permute-done.18 = f32[2,4,1152]{2,1,0:T(4,128)S(1)} collective-permute-done((f32[2,4,1152]{2,1,0:T(4,128)S(1)}, f32[2,4,1152]{2,1,0:T(4,128)S(1)}, u32[]{:S(2)}, u32[]{:S(2)}) %collective-permute-start.18) | collective-permute-done | bytes 36896 | tf_op jit(solution)/shard_map/ppermute | solution.py:411
  71.0 1.8 %collective-permute-start.19 = (f32[1,4,1152]{2,1,0:T(4,128)S(1)}, f32[1,4,1152]{2,1,0:T(4,128)S(1)}, u32[]{:S(2)}, u32[]{:S(2)}) collective-permute-start(f32[1,4,1152]{2,1,0:T(4,128)S(1)} %constant_dynamic-slice_fusion), channel_id=1, source_target_pairs={{0,8},{2,10},{4,12},{6,14},{8,0},{10,2},{12,4},{14,6},{1,9},{3,11}... | collective-permute-start | bytes 55304 | tf_op jit(solution)/shard_map/ppermute | solution.py:411
  72.9 2.9 %collective-permute-done.19 = f32[1,4,1152]{2,1,0:T(4,128)S(1)} collective-permute-done((f32[1,4,1152]{2,1,0:T(4,128)S(1)}, f32[1,4,1152]{2,1,0:T(4,128)S(1)}, u32[]{:S(2)}, u32[]{:S(2)}) %collective-permute-start.19) | collective-permute-done | bytes 18464 | tf_op jit(solution)/shard_map/ppermute | solution.py:411
  (47 shorter events, 6.8 us)
Async XLA Ops:
  1.9 11.4 %collective-permute-start.3 = (bf16[64,4096]{1,0:T(8,128)(2,1)S(1)}, bf16[64,4096]{1,0:T(8,128)(2,1)S(1)}, u32[]{:S(2)}, u32[]{:S(2)}) collective-permute-start(bf16[64,4096]{1,0:T(8,128)(2,1)S(1)} %get-tuple-element.40), channel_id=1, source_target_pairs={{0,4},{4,8},{8,12},{12,14},{14,10},{10,6},{6,2},{2,0},{5,1},{9,5},... | collective-permute-start | bytes 1572872 | tf_op jit(solution)/shard_map/ppermute | solution.py:461
  5.0 17.2 %collective-permute-start = (bf16[64,4224]{1,0:T(8,128)(2,1)S(1)}, bf16[64,4224]{1,0:T(8,128)(2,1)S(1)}, u32[]{:S(2)}, u32[]{:S(2)}) collective-permute-start(bf16[64,4224]{1,0:T(8,128)(2,1)S(1)} %get-tuple-element.36), channel_id=1, source_target_pairs={{0,4},{4,8},{8,12},{12,14},{14,10},{10,6},{6,2},{2,0},{5,1},{9,5},... | collective-permute-start | bytes 1622024 | tf_op jit(solution)/shard_map/ppermute | solution.py:461
  6.6 6.8 %copy-start.2 = (s32[8]{0:T(128)S(1)}, s32[8]{0:T(128)}, u32[]{:S(2)}) copy-start(s32[8]{0:T(128)} %param.10) | copy-start | bytes 100
  6.6 8.4 %copy-start.1 = (s32[64]{0:T(128)S(1)}, s32[64]{0:T(128)}, u32[]{:S(2)}) copy-start(s32[64]{0:T(128)} %param.9) | copy-start | bytes 772
  13.3 10.5 %collective-permute-start.4 = (bf16[64,4096]{1,0:T(8,128)(2,1)S(1)}, bf16[64,4096]{1,0:T(8,128)(2,1)S(1)}, u32[]{:S(2)}, u32[]{:S(2)}) collective-permute-start(bf16[64,4096]{1,0:T(8,128)(2,1)S(1)} %collective-permute-done.3.own_ref), channel_id=1, source_target_pairs={{0,1},{1,0},{2,3},{3,2},{4,5},{5,4},{6,7},{7,6},{8,9},{9,8},{10,11... | collective-permute-start | bytes 1572872 | tf_op jit(solution)/shard_map/ppermute | solution.py:463
  13.4 12.9 %collective-permute-start.7 = (bf16[64,4096]{1,0:T(8,128)(2,1)S(1)}, bf16[64,4096]{1,0:T(8,128)(2,1)S(1)}, u32[]{:S(2)}, u32[]{:S(2)}) collective-permute-start(bf16[64,4096]{1,0:T(8,128)(2,1)S(1)} %collective-permute-done.3.own_ref), channel_id=1, source_target_pairs={{0,4},{4,8},{8,12},{12,14},{14,10},{10,6},{6,2},{2,0},{5,1},{9,5},... | collective-permute-start | bytes 1572872 | tf_op jit(solution)/shard_map/ppermute | solution.py:461
  15.0 8.8 %copy-start = (f32[8192]{0:T(1024)S(1)}, f32[8192]{0:T(1024)}, u32[]{:S(2)}) copy-start(f32[8192]{0:T(1024)} %param.11) | copy-start | bytes 98308
  22.2 5.1 %collective-permute-start.2 = (bf16[64,4224]{1,0:T(8,128)(2,1)S(1)}, bf16[64,4224]{1,0:T(8,128)(2,1)S(1)}, u32[]{:S(2)}, u32[]{:S(2)}) collective-permute-start(bf16[64,4224]{1,0:T(8,128)(2,1)S(1)} %collective-permute-done.own_ref), channel_id=1, source_target_pairs={{0,1},{1,0},{2,3},{3,2},{4,5},{5,4},{6,7},{7,6},{8,9},{9,8},{10,11... | collective-permute-start | bytes 1622024 | tf_op jit(solution)/shard_map/ppermute | solution.py:463
  22.2 9.4 %collective-permute-start.1 = (bf16[64,4224]{1,0:T(8,128)(2,1)S(1)}, bf16[64,4224]{1,0:T(8,128)(2,1)S(1)}, u32[]{:S(2)}, u32[]{:S(2)}) collective-permute-start(bf16[64,4224]{1,0:T(8,128)(2,1)S(1)} %collective-permute-done.own_ref), channel_id=1, source_target_pairs={{0,4},{4,8},{8,12},{12,14},{14,10},{10,6},{6,2},{2,0},{5,1},{9,5},... | collective-permute-start | bytes 1622024 | tf_op jit(solution)/shard_map/ppermute | solution.py:461
  26.3 6.8 %collective-permute-start.8 = (bf16[64,4096]{1,0:T(8,128)(2,1)S(1)}, bf16[64,4096]{1,0:T(8,128)(2,1)S(1)}, u32[]{:S(2)}, u32[]{:S(2)}) collective-permute-start(bf16[64,4096]{1,0:T(8,128)(2,1)S(1)} %collective-permute-done.7.own_ref), channel_id=1, source_target_pairs={{0,1},{1,0},{2,3},{3,2},{4,5},{5,4},{6,7},{7,6},{8,9},{9,8},{10,11... | collective-permute-start | bytes 1572872 | tf_op jit(solution)/shard_map/ppermute | solution.py:463
  26.4 10.8 %collective-permute-start.11 = (bf16[64,4096]{1,0:T(8,128)(2,1)S(1)}, bf16[64,4096]{1,0:T(8,128)(2,1)S(1)}, u32[]{:S(2)}, u32[]{:S(2)}) collective-permute-start(bf16[64,4096]{1,0:T(8,128)(2,1)S(1)} %collective-permute-done.7.own_ref), channel_id=1, source_target_pairs={{0,4},{4,8},{8,12},{12,14},{14,10},{10,6},{6,2},{2,0},{5,1},{9,5},... | collective-permute-start | bytes 1572872 | tf_op jit(solution)/shard_map/ppermute | solution.py:461
  31.6 7.3 %collective-permute-start.6 = (bf16[64,4224]{1,0:T(8,128)(2,1)S(1)}, bf16[64,4224]{1,0:T(8,128)(2,1)S(1)}, u32[]{:S(2)}, u32[]{:S(2)}) collective-permute-start(bf16[64,4224]{1,0:T(8,128)(2,1)S(1)} %collective-permute-done.1.own_ref), channel_id=1, source_target_pairs={{0,1},{1,0},{2,3},{3,2},{4,5},{5,4},{6,7},{7,6},{8,9},{9,8},{10,11... | collective-permute-start | bytes 1622024 | tf_op jit(solution)/shard_map/ppermute | solution.py:463
  31.7 11.4 %collective-permute-start.5 = (bf16[64,4224]{1,0:T(8,128)(2,1)S(1)}, bf16[64,4224]{1,0:T(8,128)(2,1)S(1)}, u32[]{:S(2)}, u32[]{:S(2)}) collective-permute-start(bf16[64,4224]{1,0:T(8,128)(2,1)S(1)} %collective-permute-done.1.own_ref), channel_id=1, source_target_pairs={{0,4},{4,8},{8,12},{12,14},{14,10},{10,6},{6,2},{2,0},{5,1},{9,5},... | collective-permute-start | bytes 1622024 | tf_op jit(solution)/shard_map/ppermute | solution.py:461
  37.3 7.5 %collective-permute-start.12 = (bf16[64,4096]{1,0:T(8,128)(2,1)S(1)}, bf16[64,4096]{1,0:T(8,128)(2,1)S(1)}, u32[]{:S(2)}, u32[]{:S(2)}) collective-permute-start(bf16[64,4096]{1,0:T(8,128)(2,1)S(1)} %collective-permute-done.11.own_ref), channel_id=1, source_target_pairs={{0,1},{1,0},{2,3},{3,2},{4,5},{5,4},{6,7},{7,6},{8,9},{9,8},{10,11... | collective-permute-start | bytes 1572872 | tf_op jit(solution)/shard_map/ppermute | solution.py:463
  37.4 9.9 %collective-permute-start.14 = (bf16[64,2048]{1,0:T(8,128)(2,1)S(1)}, bf16[64,2048]{1,0:T(8,128)(2,1)S(1)}, u32[]{:S(2)}, u32[]{:S(2)}) collective-permute-start(bf16[64,2048]{1,0:T(8,128)(2,1)S(1)} %constant_dynamic-slice_fusion.1), channel_id=1, source_target_pairs={{0,4},{4,8},{8,12},{12,14},{14,10},{10,6},{6,2},{2,0},{5,1},{9,5},... | collective-permute-start | bytes 786440 | tf_op jit(solution)/shard_map/ppermute | solution.py:461
  43.1 4.3 %collective-permute-start.10 = (bf16[64,4224]{1,0:T(8,128)(2,1)S(1)}, bf16[64,4224]{1,0:T(8,128)(2,1)S(1)}, u32[]{:S(2)}, u32[]{:S(2)}) collective-permute-start(bf16[64,4224]{1,0:T(8,128)(2,1)S(1)} %collective-permute-done.5.own_ref), channel_id=1, source_target_pairs={{0,1},{1,0},{2,3},{3,2},{4,5},{5,4},{6,7},{7,6},{8,9},{9,8},{10,11... | collective-permute-start | bytes 1622024 | tf_op jit(solution)/shard_map/ppermute | solution.py:463
  43.2 7.5 %collective-permute-start.9 = (bf16[64,2176]{1,0:T(8,128)(2,1)S(1)}, bf16[64,2176]{1,0:T(8,128)(2,1)S(1)}, u32[]{:S(2)}, u32[]{:S(2)}) collective-permute-start(bf16[64,2176]{1,0:T(8,128)(2,1)S(1)} %constant_dynamic-slice_fusion.2), channel_id=1, source_target_pairs={{0,4},{4,8},{8,12},{12,14},{14,10},{10,6},{6,2},{2,0},{5,1},{9,5},... | collective-permute-start | bytes 835592 | tf_op jit(solution)/shard_map/ppermute | solution.py:461
  47.3 3.9 %collective-permute-start.15 = (bf16[64,2048]{1,0:T(8,128)(2,1)S(1)}, bf16[64,2048]{1,0:T(8,128)(2,1)S(1)}, u32[]{:S(2)}, u32[]{:S(2)}) collective-permute-start(bf16[64,2048]{1,0:T(8,128)(2,1)S(1)} %collective-permute-done.14.own_ref), channel_id=1, source_target_pairs={{0,1},{1,0},{2,3},{3,2},{4,5},{5,4},{6,7},{7,6},{8,9},{9,8},{10,11... | collective-permute-start | bytes 786440 | tf_op jit(solution)/shard_map/ppermute | solution.py:463
  50.7 3.2 %collective-permute-start.13 = (bf16[64,2176]{1,0:T(8,128)(2,1)S(1)}, bf16[64,2176]{1,0:T(8,128)(2,1)S(1)}, u32[]{:S(2)}, u32[]{:S(2)}) collective-permute-start(bf16[64,2176]{1,0:T(8,128)(2,1)S(1)} %collective-permute-done.9.own_ref), channel_id=1, source_target_pairs={{0,1},{1,0},{2,3},{3,2},{4,5},{5,4},{6,7},{7,6},{8,9},{9,8},{10,11... | collective-permute-start | bytes 835592 | tf_op jit(solution)/shard_map/ppermute | solution.py:463
  61.0 1.4 %collective-permute-start.16 = (f32[8,4,1152]{2,1,0:T(4,128)S(1)}, f32[8,4,1152]{2,1,0:T(4,128)S(1)}, u32[]{:S(2)}, u32[]{:S(2)}) collective-permute-start(f32[8,4,1152]{2,1,0:T(4,128)S(1)} %get-tuple-element.59), channel_id=1, source_target_pairs={{0,1},{1,0},{2,3},{3,2},{4,5},{5,4},{6,7},{7,6},{8,9},{9,8},{10,11... | collective-permute-start | bytes 442376 | tf_op jit(solution)/shard_map/ppermute | solution.py:479
  62.5 4.4 %collective-permute-start.17 = (f32[4,4,1152]{2,1,0:T(4,128)S(1)}, f32[4,4,1152]{2,1,0:T(4,128)S(1)}, u32[]{:S(2)}, u32[]{:S(2)}) collective-permute-start(f32[4,4,1152]{2,1,0:T(4,128)S(1)} %dynamic-slice_bitcast_fusion), channel_id=1, source_target_pairs={{0,2},{2,0},{4,6},{6,4},{8,10},{10,8},{12,14},{14,12},{1,3},{3,1},... | collective-permute-start | bytes 221192 | tf_op jit(solution)/shard_map/ppermute | solution.py:411
  66.9 4.0 %collective-permute-start.18 = (f32[2,4,1152]{2,1,0:T(4,128)S(1)}, f32[2,4,1152]{2,1,0:T(4,128)S(1)}, u32[]{:S(2)}, u32[]{:S(2)}) collective-permute-start(f32[2,4,1152]{2,1,0:T(4,128)S(1)} %dynamic-slice_bitcast_fusion.1), channel_id=1, source_target_pairs={{0,4},{2,6},{4,0},{6,2},{8,12},{10,14},{12,8},{14,10},{1,5},{3,7},... | collective-permute-start | bytes 110600 | tf_op jit(solution)/shard_map/ppermute | solution.py:411
  71.0 4.7 %collective-permute-start.19 = (f32[1,4,1152]{2,1,0:T(4,128)S(1)}, f32[1,4,1152]{2,1,0:T(4,128)S(1)}, u32[]{:S(2)}, u32[]{:S(2)}) collective-permute-start(f32[1,4,1152]{2,1,0:T(4,128)S(1)} %constant_dynamic-slice_fusion), channel_id=1, source_target_pairs={{0,8},{2,10},{4,12},{6,14},{8,0},{10,2},{12,4},{14,6},{1,9},{3,11}... | collective-permute-start | bytes 55304 | tf_op jit(solution)/shard_map/ppermute | solution.py:411

commit v6 on v5

--- a/solution.py
+++ b/solution.py
@@ -24,33 +24,27 @@
     return list(range(blocks))
 
 
-def message_kernel(tags_ref, rows_ref, first_ref, second_ref, tags, sent):
-    height, span = first_ref.shape
+def message_kernel(tags_ref, rows_ref, out_ref, tags, sent):
+    height, span = out_ref.shape[0], out_ref.shape[1] - LANES
     copies = [
         pltpu.make_async_copy(tags_ref, tags, sent.at[0]),
-        pltpu.make_async_copy(rows_ref.at[:, :span], first_ref, sent.at[1]),
-        pltpu.make_async_copy(rows_ref.at[:, span:], second_ref.at[:, :span], sent.at[2]),
+        pltpu.make_async_copy(rows_ref.at[:, span:], out_ref.at[:, :span], sent.at[1]),
     ]
     for copy in copies:
         copy.start()
     copies[0].wait()
-    second_ref[:, span:] = tag_rows(tags, height).astype(jnp.bfloat16)
-    for copy in copies[1:]:
-        copy.wait()
-
-
-def make_messages(tags, templates):
+    out_ref[:, span:] = tag_rows(tags, height).astype(jnp.bfloat16)
+    copies[1].wait()
+
+
+def tagged_message(tags, templates):
     height, freqs = templates.shape
-    span = freqs // 2
     return pl.pallas_call(
         message_kernel,
         in_specs=[pl.BlockSpec(memory_space=pl.ANY)] * 2,
-        out_specs=[in_vmem(), in_vmem()],
-        out_shape=[
-            pltpu.VMEM((height, span), jnp.bfloat16),
-            pltpu.VMEM((height, span + LANES), jnp.bfloat16),
-        ],
-        scratch_shapes=[pltpu.VMEM(tags.shape, tags.dtype), pltpu.SemaphoreType.DMA((3,))],
+        out_specs=in_vmem(),
+        out_shape=pltpu.VMEM((height, freqs // 2 + LANES), jnp.bfloat16),
+        scratch_shapes=[pltpu.VMEM(tags.shape, tags.dtype), pltpu.SemaphoreType.DMA((2,))],
         compiler_params=pltpu.CompilerParams(vmem_limit_bytes=SMALL_LIMIT),
     )(
         pltpu.with_memory_space_constraint(tags, pltpu.HBM),
@@ -168,10 +162,6 @@
     else:
         acc[...] = acc_in[...]
         energy[...] = energy_in[...]
-    across = lax.broadcasted_iota(jnp.int32, (STRIP, STRIP), 0)
-    along = lax.broadcasted_iota(jnp.int32, (STRIP, STRIP), 1)
-    identity = jnp.where(across == along, 1.0, 0.0).astype(jnp.bfloat16)
-
     @pl.loop(0, steps)
     def _(step):
         copy(step).wait()
@@ -179,14 +169,9 @@
         for strip in range(0, width, STRIP):
             there = pl.ds(pl.multiple_of(step * width + strip, STRIP), STRIP)
             weighted = weigh(tmpl_ref[:, there], noise_ref[:, there], energy)
-            both = lax.dot_general(
-                jnp.concatenate([weighted, identity], axis=0),
-                slots[slot, :, strip : strip + STRIP],
-                (((1,), (1,)), ((), ())),
-                preferred_element_type=jnp.float32,
-            )
-            acc[...] += both[:height]
-            turned_ref[there, :] = both[height:].astype(jnp.bfloat16)
+            turned = jnp.transpose(slots[slot, :, strip : strip + STRIP])
+            turned_ref[there, :] = turned
+            acc[...] += jnp.dot(weighted, turned, preferred_element_type=jnp.float32)
 
         @pl.when(step + SLOTS < steps)
         def _():
@@ -281,7 +266,8 @@
         theirs_ref[block, :, width:] = totals[per_owner:]
 
 
-def ring_kernel(phase, ends, sources, where_ref, noise_ref, part_ref, own_ref, sib_ref, *rest):
+def ring_kernel(phase, ends, sources, where_ref, noise_ref, part_ref, *rest):
+    row_refs, rest = rest[: 2 * len(sources)], rest[2 * len(sources) :]
     if phase == 0:
         acc, energy = rest
         acc[...] = jnp.zeros_like(acc)
@@ -301,17 +287,15 @@
     span = half // 2 if ends else half
     core = where_ref[1]
     if ends:
-        pieces = [((own_ref,), core * span), ((sib_ref,), (1 - core) * span)]
-    else:
-        pieces = [((own_ref, sib_ref), 0)]
+        pieces = [(row_refs[:1], core * span), (row_refs[1:], (1 - core) * span)]
+    else:
+        pieces = [(row_refs, 0)]
     for refs, start in pieces:
-
-        @pl.loop(0, span // WIDTH)
-        def _(step):
-            near = pl.ds(pl.multiple_of(step * WIDTH, WIDTH), WIDTH)
+        for step in range(span // WIDTH):
+            here = pl.ds(step * WIDTH, WIDTH)
             there = pl.ds(pl.multiple_of(start + step * WIDTH, WIDTH), WIDTH)
             columns = pl.ds(pl.multiple_of(phase * half + start + step * WIDTH, WIDTH), WIDTH)
-            rows = jnp.concatenate([ref[:, near] for ref in refs], axis=0)
+            rows = jnp.concatenate([ref[:, here] for ref in refs], axis=0)
             weighted = weigh(rows, noise_ref[:, columns], energy)
             acc[...] += jnp.dot(
                 weighted, part_ref[there, :], preferred_element_type=jnp.float32
@@ -319,23 +303,24 @@
 
     if phase == 0:
         return
-    height = own_ref.shape[0]
-    tags = [ref[:, span:].astype(jnp.float32) for ref in (own_ref, sib_ref)]
+    height = row_refs[0].shape[0]
+    tags = [ref[:, span:].astype(jnp.float32) for ref in row_refs]
     tags = jnp.where(core == 0, tags[1], tags[0]) if ends else jnp.concatenate(tags, axis=0)
     found = []
-    for table in sources:
-        source = jnp.int32(table[0])
-        for block in range(1, len(table)):
-            source = jnp.where(where_ref[0] == block, table[block], source)
-        found.append(source)
+    for tables in sources:
+        for table in tables:
+            source = jnp.int32(table[0])
+            for block in range(1, len(table)):
+                source = jnp.where(where_ref[0] == block, table[block], source)
+            found.append(source)
     if ends:
-        hit = picked_rows(words_ref, found[0], height)
-    else:
-        own = jnp.where(core == 0, found[0], found[1])
-        sib = jnp.where(core == 0, found[1], found[0])
-        hit = jnp.concatenate(
-            [picked_rows(words_ref, source, height) for source in (own, sib)], axis=0
-        )
+        found = found[:1]
+    else:
+        for at in range(0, len(found), 2):
+            front, back = found[at : at + 2]
+            found[at] = jnp.where(core == 0, front, back)
+            found[at + 1] = jnp.where(core == 0, back, front)
+    hit = jnp.concatenate([picked_rows(words_ref, source, height) for source in found], axis=0)
     state = add_rows(tags, hit, logs_ref, get_state(state_ref), acc, energy)
     if ends:
         class_sums(state, core, near, copies, loglik_ref, mine_ref, theirs_ref)
@@ -343,11 +328,11 @@
         put_state(state, out_ref)
 
 
-def ring_scores(phase, sources, where, noise, turned, own, sib, rest, blocks=0, owners=0):
+def ring_scores(phase, sources, where, noise, turned, arrays, rest, blocks=0, owners=0):
     ends = blocks > 0
     half, per_device = turned.shape
     freqs = 2 * half
-    rows = own.shape[0] * (1 if ends else 2)
+    rows = arrays[0].shape[0] * (1 if ends else len(arrays))
     sums = [
         jax.ShapeDtypeStruct((rows, per_device), jnp.float32),
         jax.ShapeDtypeStruct((rows, LANES), jnp.float32),
@@ -375,7 +360,7 @@
             shapes = [jax.ShapeDtypeStruct(state.shape, jnp.float32)]
     return pl.pallas_call(
         functools.partial(ring_kernel, phase, ends, sources),
-        in_specs=[in_smem()] + [in_vmem()] * 4 + rest_specs,
+        in_specs=[in_smem()] + [in_vmem()] * (2 + len(arrays)) + rest_specs,
         out_specs=[in_vmem()] * len(shapes),
         out_shape=shapes,
         scratch_shapes=scratch,
@@ -389,8 +374,7 @@
         where,
         noise,
         pltpu.with_memory_space_constraint(turned, pltpu.VMEM),
-        own,
-        sib,
+        *arrays,
         *rest,
     )
 
@@ -428,7 +412,9 @@
     noise = inv_noise[None, :]
     logs = jnp.log(class_counts.astype(jnp.float32))
     tags = template_class[None, :]
-    held = make_messages(tags, templates)
+    head = templates[:, : freqs // 2]
+    head, later = lax.optimization_barrier((head, templates))
+    held = [head, tagged_message(tags, later)]
     where = jnp.stack([block_id, core])
     cut = freqs // 4
     where, cut_at = lax.optimization_barrier((where, core.astype(jnp.uint32) * cut))
@@ -442,14 +428,16 @@
     turned = (first, second)
     last = blocks // 2
     gates = [sums, state]
+    pairs, tables = ([], []), []
     for distance in range(1, last + 1):
         ends = distance == last
-        sources = [
-            tuple(order[(place[block] - sign * distance) % blocks] for block in range(blocks))
-            for sign in (1, -1)
-        ]
+        tables.append(
+            [
+                tuple(order[(place[block] - sign * distance) % blocks] for block in range(blocks))
+                for sign in (1, -1)
+            ]
+        )
         arrived = []
-        sums = ()
         for phase in range(2):
             message = held[phase]
             if ends:
@@ -460,18 +448,19 @@
                 )
             own = lax.ppermute(message, ("blk", "cls"), ring)
             own, _ = lax.optimization_barrier((own, gates[len(gates) - 2]))
-            sib = lax.ppermute(own, "cls", swap)
+            arrived.append(own)
+            pairs[phase].extend((own, lax.ppermute(own, "cls", swap)))
             rest = () if phase == 0 else (*sums, logs, words, state)
             if ends:
                 rest += (particles,) if phase else ()
                 sums = ring_scores(
-                    phase, sources, where, noise, turned[phase], own, sib, rest, blocks, owners
+                    phase, tables, where, noise, turned[phase], pairs[phase], rest, blocks, owners
                 )
             else:
-                sums = ring_scores(phase, sources, where, noise, turned[phase], own, sib, rest)
+                sums = ring_scores(phase, tables, where, noise, turned[phase], pairs[phase], rest)
             gates.append(sums)
-            arrived.append(own)
         held = arrived
+        pairs, tables = ([], []), []
         if not ends:
             (state,) = sums
 

time: 76.8 us -> 77.7 us (1.012)
  Pallas kernels: 42.1 us -> 38.6 us
  waiting for transfers between devices: 14.5 us -> 17.5 us
  local copies, waits for them, and re-layouts: 0.45 us -> 1.53 us
    ppermute x8, waiting for transfers between devices: 3.49 us -> 6.88 us  [body(): own = lax.ppermute(message, ('blk', 'cls'), ring)]
    pallas_call x8, Pallas kernels: 27 us -> 24.4 us  [ring_scores(): pl.pallas_call(functools.partial(ring_kernel, phase, ends, sources), in_s...]
    slice x0 -> x1, local copies, waits for them, and re-layouts: none -> 1.08 us  [body(): head = templates[:, :freqs // 2]]
  transfers between devices with their start and end apart: 20 -> 20, of which waited for: 7 -> 8; matrix products, arithmetic and copies ran while one was open for 0% -> 0% of each run, Pallas kernels for 44% -> 38%
where the time goes in v6:
time: 77.7 us; the launch traced here: 77.5 us
  Pallas kernels  38.6 us (50%)
  starting transfers between devices  18 us (23%)
  waiting for transfers between devices  17.5 us (23%)
  local copies, waits for them, and re-layouts  1.53 us (2%)
  other arithmetic  0.93 us (1%)
  between operations  0.85 us (1%)
    pallas_call x8, Pallas kernels, ring_scores(): pl.pallas_call(functools.partial(ring_kernel, phase, ends, sources), in_s...  24.4 us
    ppermute x8, starting transfers between devices, body(): own = lax.ppermute(message, ('blk', 'cls'), ring)  13.4 us
    pallas_call x2, Pallas kernels, own_scores(): pl.pallas_call(functools.partial(own_kernel, phase), grid=(1,), in_specs=...  13.2 us
    ppermute x3, waiting for transfers between devices, scatter_sum(): pieces = keep + lax.ppermute(send, 'blk', swaps)  9.61 us
    ppermute x8, waiting for transfers between devices, body(): own = lax.ppermute(message, ('blk', 'cls'), ring)  6.88 us
    ppermute x3, starting transfers between devices, scatter_sum(): pieces = keep + lax.ppermute(send, 'blk', swaps)  3.74 us
  transfers between devices with their start and end apart: 20, of which 8 were waited for; matrix products, arithmetic and copies ran while one was open for 0% of the time, Pallas kernels for 38%

profile of v6, /device:TPU:0, one launch (start us, length us, event | category | flops | bytes accessed | tf_op | source)
XLA Modules:
  0.0 77.5 jit_solution(15485282332355070980)
XLA Ops:
  1.7 3.1 %collective-permute-start.3 = (bf16[64,4096]{1,0:T(8,128)(2,1)S(1)}, bf16[64,4096]{1,0:T(8,128)(2,1)S(1)}, u32[]{:S(2)}, u32[]{:S(2)}) collective-permute-start(bf16[64,4096]{1,0:T(8,128)(2,1)S(1)} %slice.9), channel_id=1, source_target_pairs={{0,4},{4,8},{8,12},{12,14},{14,10},{10,6},{6,2},{2,0},{5,1},{9,5},... | collective-permute-start | bytes 1572872 | tf_op jit(solution)/shard_map/ppermute | solution.py:449
  5.9 1.6 %collective-permute-start = (bf16[64,4224]{1,0:T(8,128)(2,1)S(1)}, bf16[64,4224]{1,0:T(8,128)(2,1)S(1)}, u32[]{:S(2)}, u32[]{:S(2)}) collective-permute-start(bf16[64,4224]{1,0:T(8,128)(2,1)S(1)} %shard_map.79), channel_id=1, source_target_pairs={{0,4},{4,8},{8,12},{12,14},{14,10},{10,6},{6,2},{2,0},{5,1},{9,5},... | collective-permute-start | bytes 1622024 | tf_op jit(solution)/shard_map/ppermute | solution.py:449
  7.6 6.4 %shard_map.77 = (bf16[4096,1024]{1,0:T(8,128)(2,1)S(1)}, s32[16,1024]{1,0:T(8,128)S(1)}, f32[64,1024]{1,0:T(8,128)S(1)}, f32[64,128]{1,0:T(8,128)S(1)}) custom-call(s32[2]{0:T(128)S(1)} %pad_add_fusion.where_ref, f32[1,8192]{1,0:T(1,128)} %bitcast.17, bf16[64,8192]{1,0:T(8,128)(2,1)} %rows_ref, bf16[1024,8192]{1,0:T(8,128)(2,1)} %rest_7_.1, s32[16,1024]{1,0:T(8,128)} %rest_0_.1), custom_call_target="tpu_custom_call" | custom-call | flops 2147483648 | bytes 8388608 | tf_op jit(solution)/shard_map/pallas_call | solution.py:212
  14.1 1.6 %collective-permute-start.7 = (bf16[64,4096]{1,0:T(8,128)(2,1)S(1)}, bf16[64,4096]{1,0:T(8,128)(2,1)S(1)}, u32[]{:S(2)}, u32[]{:S(2)}) collective-permute-start(bf16[64,4096]{1,0:T(8,128)(2,1)S(1)} %collective-permute-done.3.rest_0_), channel_id=1, source_target_pairs={{0,4},{4,8},{8,12},{12,14},{14,10},{10,6},{6,2},{2,0},{5,1},{9,5},... | collective-permute-start | bytes 1572872 | tf_op jit(solution)/shard_map/ppermute | solution.py:449
  15.7 6.8 %shard_map.78 = (bf16[4096,1024]{1,0:T(8,128)(2,1)S(1)}, f32[16,1024]{1,0:T(8,128)S(1)}) custom-call(s32[2]{0:T(128)S(1)} %pad_add_fusion.where_ref, f32[1,8192]{1,0:T(1,128)} %bitcast.18, bf16[64,8192]{1,0:T(8,128)(2,1)} %rows_ref, bf16[1024,8192]{1,0:T(8,128)(2,1)} %rest_7_.1, f32[64,1024]{1,0:T(8,128)S(1)} %get-tuple-element.32.rest_0_, ...), custom_call_target="tpu_custom_call" | custom-call | flops 2147483648 | bytes 8388608 | tf_op jit(solution)/shard_map/pallas_call | solution.py:212
  22.6 1.6 %collective-permute-start.1 = (bf16[64,4224]{1,0:T(8,128)(2,1)S(1)}, bf16[64,4224]{1,0:T(8,128)(2,1)S(1)}, u32[]{:S(2)}, u32[]{:S(2)}) collective-permute-start(bf16[64,4224]{1,0:T(8,128)(2,1)S(1)} %collective-permute-done.rest_0_), channel_id=1, source_target_pairs={{0,4},{4,8},{8,12},{12,14},{14,10},{10,6},{6,2},{2,0},{5,1},{9,5},... | collective-permute-start | bytes 1622024 | tf_op jit(solution)/shard_map/ppermute | solution.py:449
  24.2 2.0 %shard_map.80 = (f32[128,1024]{1,0:T(8,128)S(1)}, f32[128,128]{1,0:T(8,128)S(1)}) custom-call(s32[2]{0:T(128)S(1)} %pad_add_fusion.where_ref, f32[1,8192]{1,0:T(1,128)S(1)} %bitcast.19, bf16[4096,1024]{1,0:T(8,128)(2,1)S(1)} %get-tuple-element.39.part_ref, bf16[64,4096]{1,0:T(8,128)(2,1)S(1)} %collective-permute-done.3.rest_0_, ...), custom_call_target="tpu_custom_call" | custom-call | flops 2147483648 | bytes 8388608 | tf_op jit(solution)/shard_map/pallas_call | solution.py:361
  26.9 2.4 %shard_map.81.rest_6_ = f32[16,1024]{1,0:T(8,128)S(1)} custom-call(s32[2]{0:T(128)S(1)} %pad_add_fusion.where_ref, f32[1,8192]{1,0:T(1,128)S(1)} %bitcast.20, bf16[4096,1024]{1,0:T(8,128)(2,1)S(1)} %get-tuple-element.35.part_ref, bf16[64,4224]{1,0:T(8,128)(2,1)S(1)} %collective-permute-done.rest_0_, bf16[64,4224]{1,0:T(8,128)(2,1)S(1)} %collective-permute-done.2.rest_1_, ...), custom_call_target="tpu_custom_call" | custom-call | flops 2147483648 | bytes 8388608 | tf_op jit(solution)/shard_map/pallas_call | solution.py:361
  29.3 2.7 %collective-permute-done.1.rest_0_ = bf16[64,4224]{1,0:T(8,128)(2,1)S(1)} collective-permute-done((bf16[64,4224]{1,0:T(8,128)(2,1)S(1)}, bf16[64,4224]{1,0:T(8,128)(2,1)S(1)}, u32[]{:S(2)}, u32[]{:S(2)}) %collective-permute-start.1) | collective-permute-done | bytes 540704 | tf_op jit(solution)/shard_map/ppermute | solution.py:449
  33.5 2.0 %shard_map.82 = (f32[128,1024]{1,0:T(8,128)S(1)}, f32[128,128]{1,0:T(8,128)S(1)}) custom-call(s32[2]{0:T(128)S(1)} %pad_add_fusion.where_ref, f32[1,8192]{1,0:T(1,128)S(1)} %bitcast.21, bf16[4096,1024]{1,0:T(8,128)(2,1)S(1)} %get-tuple-element.39.part_ref, bf16[64,4096]{1,0:T(8,128)(2,1)S(1)} %collective-permute-done.7.rest_0_, ...), custom_call_target="tpu_custom_call" | custom-call | flops 2147483648 | bytes 8388608 | tf_op jit(solution)/shard_map/pallas_call | solution.py:361
  35.5 2.1 %collective-permute-done.11.rest_0_ = bf16[64,4096]{1,0:T(8,128)(2,1)S(1)} collective-permute-done((bf16[64,4096]{1,0:T(8,128)(2,1)S(1)}, bf16[64,4096]{1,0:T(8,128)(2,1)S(1)}, u32[]{:S(2)}, u32[]{:S(2)}) %collective-permute-start.11) | collective-permute-done | bytes 524320 | tf_op jit(solution)/shard_map/ppermute | solution.py:449
  37.8 1.6 %collective-permute-start.14 = (bf16[64,2048]{1,0:T(8,128)(2,1)S(1)}, bf16[64,2048]{1,0:T(8,128)(2,1)S(1)}, u32[]{:S(2)}, u32[]{:S(2)}) collective-permute-start(bf16[64,2048]{1,0:T(8,128)(2,1)S(1)} %constant_dynamic-slice_fusion.1), channel_id=1, source_target_pairs={{0,4},{4,8},{8,12},{12,14},{14,10},{10,6},{6,2},{2,0},{5,1},{9,5},... | collective-permute-start | bytes 786440 | tf_op jit(solution)/shard_map/ppermute | solution.py:449
  39.3 2.4 %shard_map.83.rest_6_ = f32[16,1024]{1,0:T(8,128)S(1)} custom-call(s32[2]{0:T(128)S(1)} %pad_add_fusion.where_ref, f32[1,8192]{1,0:T(1,128)S(1)} %bitcast.22, bf16[4096,1024]{1,0:T(8,128)(2,1)S(1)} %get-tuple-element.35.part_ref, bf16[64,4224]{1,0:T(8,128)(2,1)S(1)} %collective-permute-done.1.rest_0_, bf16[64,4224]{1,0:T(8,128)(2,1)S(1)} %collective-permute-done.6.rest_1_, ...), custom_call_target="tpu_custom_call" | custom-call | flops 2147483648 | bytes 8388608 | tf_op jit(solution)/shard_map/pallas_call | solution.py:361
  41.8 1.6 %collective-permute-done.5.rest_0_ = bf16[64,4224]{1,0:T(8,128)(2,1)S(1)} collective-permute-done((bf16[64,4224]{1,0:T(8,128)(2,1)S(1)}, bf16[64,4224]{1,0:T(8,128)(2,1)S(1)}, u32[]{:S(2)}, u32[]{:S(2)}) %collective-permute-start.5) | collective-permute-done | bytes 540704 | tf_op jit(solution)/shard_map/ppermute | solution.py:449
  43.6 1.8 %collective-permute-start.9 = (bf16[64,2176]{1,0:T(8,128)(2,1)S(1)}, bf16[64,2176]{1,0:T(8,128)(2,1)S(1)}, u32[]{:S(2)}, u32[]{:S(2)}) collective-permute-start(bf16[64,2176]{1,0:T(8,128)(2,1)S(1)} %constant_dynamic-slice_fusion.2), channel_id=1, source_target_pairs={{0,4},{4,8},{8,12},{12,14},{14,10},{10,6},{6,2},{2,0},{5,1},{9,5},... | collective-permute-start | bytes 835592 | tf_op jit(solution)/shard_map/ppermute | solution.py:449
  45.3 2.0 %shard_map.84 = (f32[128,1024]{1,0:T(8,128)S(1)}, f32[128,128]{1,0:T(8,128)S(1)}) custom-call(s32[2]{0:T(128)S(1)} %pad_add_fusion.where_ref, f32[1,8192]{1,0:T(1,128)S(1)} %bitcast.23, bf16[4096,1024]{1,0:T(8,128)(2,1)S(1)} %get-tuple-element.39.part_ref, bf16[64,4096]{1,0:T(8,128)(2,1)S(1)} %collective-permute-done.11.rest_0_, ...), custom_call_target="tpu_custom_call" | custom-call | flops 2147483648 | bytes 8388608 | tf_op jit(solution)/shard_map/pallas_call | solution.py:361
  47.4 2.4 %shard_map.85.rest_6_ = f32[16,1024]{1,0:T(8,128)S(1)} custom-call(s32[2]{0:T(128)S(1)} %pad_add_fusion.where_ref, f32[1,8192]{1,0:T(1,128)S(1)} %bitcast.24, bf16[4096,1024]{1,0:T(8,128)(2,1)S(1)} %get-tuple-element.35.part_ref, bf16[64,4224]{1,0:T(8,128)(2,1)S(1)} %collective-permute-done.5.rest_0_, bf16[64,4224]{1,0:T(8,128)(2,1)S(1)} %collective-permute-done.10.rest_1_, ...), custom_call_target="tpu_custom_call" | custom-call | flops 2147483648 | bytes 8388608 | tf_op jit(solution)/shard_map/pallas_call | solution.py:361
  50.4 2.2 %shard_map.86 = (f32[64,1024]{1,0:T(8,128)S(1)}, f32[64,128]{1,0:T(8,128)S(1)}) custom-call(s32[2]{0:T(128)S(1)} %pad_add_fusion.where_ref, f32[1,8192]{1,0:T(1,128)S(1)} %bitcast.25, bf16[4096,1024]{1,0:T(8,128)(2,1)S(1)} %get-tuple-element.39.part_ref, bf16[64,2048]{1,0:T(8,128)(2,1)S(1)} %collective-permute-done.14.rest_0_, ...), custom_call_target="tpu_custom_call" | custom-call | flops 2147483648 | bytes 8388608 | tf_op jit(solution)/shard_map/pallas_call | solution.py:361
  52.6 9.0 %shard_map.87 = (f32[1,1024]{1,0:T(1,128)}, f32[8,4,1152]{2,1,0:T(4,128)S(1)}, f32[8,4,1152]{2,1,0:T(4,128)S(1)}) custom-call(s32[2]{0:T(128)S(1)} %pad_add_fusion.where_ref, f32[1,8192]{1,0:T(1,128)S(1)} %bitcast.26, bf16[4096,1024]{1,0:T(8,128)(2,1)S(1)} %get-tuple-element.35.part_ref, bf16[64,2176]{1,0:T(8,128)(2,1)S(1)} %collective-permute-done.9.rest_0_, ...), custom_call_target="tpu_custom_call" | custom-call | flops 2147483648 | bytes 8388608 | tf_op jit(solution)/shard_map/pallas_call | solution.py:361
  63.7 4.1 %collective-permute-done.17 = f32[4,4,1152]{2,1,0:T(4,128)S(1)} collective-permute-done((f32[4,4,1152]{2,1,0:T(4,128)S(1)}, f32[4,4,1152]{2,1,0:T(4,128)S(1)}, u32[]{:S(2)}, u32[]{:S(2)}) %collective-permute-start.17) | collective-permute-done | bytes 73760 | tf_op jit(solution)/shard_map/ppermute | solution.py:395
  67.8 1.6 %collective-permute-start.18 = (f32[2,4,1152]{2,1,0:T(4,128)S(1)}, f32[2,4,1152]{2,1,0:T(4,128)S(1)}, u32[]{:S(2)}, u32[]{:S(2)}) collective-permute-start(f32[2,4,1152]{2,1,0:T(4,128)S(1)} %dynamic-slice_bitcast_fusion.1), channel_id=1, source_target_pairs={{0,4},{2,6},{4,0},{6,2},{8,12},{10,14},{12,8},{14,10},{1,5},{3,7},... | collective-permute-start | bytes 110600 | tf_op jit(solution)/shard_map/ppermute | solution.py:395
  69.4 2.4 %collective-permute-done.18 = f32[2,4,1152]{2,1,0:T(4,128)S(1)} collective-permute-done((f32[2,4,1152]{2,1,0:T(4,128)S(1)}, f32[2,4,1152]{2,1,0:T(4,128)S(1)}, u32[]{:S(2)}, u32[]{:S(2)}) %collective-permute-start.18) | collective-permute-done | bytes 36896 | tf_op jit(solution)/shard_map/ppermute | solution.py:395
  71.8 1.6 %collective-permute-start.19 = (f32[1,4,1152]{2,1,0:T(4,128)S(1)}, f32[1,4,1152]{2,1,0:T(4,128)S(1)}, u32[]{:S(2)}, u32[]{:S(2)}) collective-permute-start(f32[1,4,1152]{2,1,0:T(4,128)S(1)} %constant_dynamic-slice_fusion), channel_id=1, source_target_pairs={{0,8},{2,10},{4,12},{6,14},{8,0},{10,2},{12,4},{14,6},{1,9},{3,11}... | collective-permute-start | bytes 55304 | tf_op jit(solution)/shard_map/ppermute | solution.py:395
  73.5 3.1 %collective-permute-done.19 = f32[1,4,1152]{2,1,0:T(4,128)S(1)} collective-permute-done((f32[1,4,1152]{2,1,0:T(4,128)S(1)}, f32[1,4,1152]{2,1,0:T(4,128)S(1)}, u32[]{:S(2)}, u32[]{:S(2)}) %collective-permute-start.19) | collective-permute-done | bytes 18464 | tf_op jit(solution)/shard_map/ppermute | solution.py:395
  (48 shorter events, 8.6 us)
Async XLA Ops:
  1.7 12.3 %collective-permute-start.3 = (bf16[64,4096]{1,0:T(8,128)(2,1)S(1)}, bf16[64,4096]{1,0:T(8,128)(2,1)S(1)}, u32[]{:S(2)}, u32[]{:S(2)}) collective-permute-start(bf16[64,4096]{1,0:T(8,128)(2,1)S(1)} %slice.9), channel_id=1, source_target_pairs={{0,4},{4,8},{8,12},{12,14},{14,10},{10,6},{6,2},{2,0},{5,1},{9,5},... | collective-permute-start | bytes 1572872 | tf_op jit(solution)/shard_map/ppermute | solution.py:449
  5.9 16.6 %collective-permute-start = (bf16[64,4224]{1,0:T(8,128)(2,1)S(1)}, bf16[64,4224]{1,0:T(8,128)(2,1)S(1)}, u32[]{:S(2)}, u32[]{:S(2)}) collective-permute-start(bf16[64,4224]{1,0:T(8,128)(2,1)S(1)} %shard_map.79), channel_id=1, source_target_pairs={{0,4},{4,8},{8,12},{12,14},{14,10},{10,6},{6,2},{2,0},{5,1},{9,5},... | collective-permute-start | bytes 1622024 | tf_op jit(solution)/shard_map/ppermute | solution.py:449
  7.6 6.5 %copy-start.2 = (s32[8]{0:T(128)S(1)}, s32[8]{0:T(128)}, u32[]{:S(2)}) copy-start(s32[8]{0:T(128)} %param.10) | copy-start | bytes 100
  7.6 8.1 %copy-start.1 = (s32[64]{0:T(128)S(1)}, s32[64]{0:T(128)}, u32[]{:S(2)}) copy-start(s32[64]{0:T(128)} %param.9) | copy-start | bytes 772
  14.0 10.2 %collective-permute-start.4 = (bf16[64,4096]{1,0:T(8,128)(2,1)S(1)}, bf16[64,4096]{1,0:T(8,128)(2,1)S(1)}, u32[]{:S(2)}, u32[]{:S(2)}) collective-permute-start(bf16[64,4096]{1,0:T(8,128)(2,1)S(1)} %collective-permute-done.3.rest_0_), channel_id=1, source_target_pairs={{0,1},{1,0},{2,3},{3,2},{4,5},{5,4},{6,7},{7,6},{8,9},{9,8},{10,11... | collective-permute-start | bytes 1572872 | tf_op jit(solution)/shard_map/ppermute | solution.py:452
  14.1 12.1 %collective-permute-start.7 = (bf16[64,4096]{1,0:T(8,128)(2,1)S(1)}, bf16[64,4096]{1,0:T(8,128)(2,1)S(1)}, u32[]{:S(2)}, u32[]{:S(2)}) collective-permute-start(bf16[64,4096]{1,0:T(8,128)(2,1)S(1)} %collective-permute-done.3.rest_0_), channel_id=1, source_target_pairs={{0,4},{4,8},{8,12},{12,14},{14,10},{10,6},{6,2},{2,0},{5,1},{9,5},... | collective-permute-start | bytes 1572872 | tf_op jit(solution)/shard_map/ppermute | solution.py:449
  15.7 8.5 %copy-start = (f32[8192]{0:T(1024)S(1)}, f32[8192]{0:T(1024)}, u32[]{:S(2)}) copy-start(f32[8192]{0:T(1024)} %param.11) | copy-start | bytes 98308
  22.5 4.4 %collective-permute-start.2 = (bf16[64,4224]{1,0:T(8,128)(2,1)S(1)}, bf16[64,4224]{1,0:T(8,128)(2,1)S(1)}, u32[]{:S(2)}, u32[]{:S(2)}) collective-permute-start(bf16[64,4224]{1,0:T(8,128)(2,1)S(1)} %collective-permute-done.rest_0_), channel_id=1, source_target_pairs={{0,1},{1,0},{2,3},{3,2},{4,5},{5,4},{6,7},{7,6},{8,9},{9,8},{10,11... | collective-permute-start | bytes 1622024 | tf_op jit(solution)/shard_map/ppermute | solution.py:452
  22.6 9.4 %collective-permute-start.1 = (bf16[64,4224]{1,0:T(8,128)(2,1)S(1)}, bf16[64,4224]{1,0:T(8,128)(2,1)S(1)}, u32[]{:S(2)}, u32[]{:S(2)}) collective-permute-start(bf16[64,4224]{1,0:T(8,128)(2,1)S(1)} %collective-permute-done.rest_0_), channel_id=1, source_target_pairs={{0,4},{4,8},{8,12},{12,14},{14,10},{10,6},{6,2},{2,0},{5,1},{9,5},... | collective-permute-start | bytes 1622024 | tf_op jit(solution)/shard_map/ppermute | solution.py:449
  26.2 7.4 %collective-permute-start.8 = (bf16[64,4096]{1,0:T(8,128)(2,1)S(1)}, bf16[64,4096]{1,0:T(8,128)(2,1)S(1)}, u32[]{:S(2)}, u32[]{:S(2)}) collective-permute-start(bf16[64,4096]{1,0:T(8,128)(2,1)S(1)} %collective-permute-done.7.rest_0_), channel_id=1, source_target_pairs={{0,1},{1,0},{2,3},{3,2},{4,5},{5,4},{6,7},{7,6},{8,9},{9,8},{10,11... | collective-permute-start | bytes 1572872 | tf_op jit(solution)/shard_map/ppermute | solution.py:452
  26.2 11.4 %collective-permute-start.11 = (bf16[64,4096]{1,0:T(8,128)(2,1)S(1)}, bf16[64,4096]{1,0:T(8,128)(2,1)S(1)}, u32[]{:S(2)}, u32[]{:S(2)}) collective-permute-start(bf16[64,4096]{1,0:T(8,128)(2,1)S(1)} %collective-permute-done.7.rest_0_), channel_id=1, source_target_pairs={{0,4},{4,8},{8,12},{12,14},{14,10},{10,6},{6,2},{2,0},{5,1},{9,5},... | collective-permute-start | bytes 1572872 | tf_op jit(solution)/shard_map/ppermute | solution.py:449
  32.0 7.3 %collective-permute-start.6 = (bf16[64,4224]{1,0:T(8,128)(2,1)S(1)}, bf16[64,4224]{1,0:T(8,128)(2,1)S(1)}, u32[]{:S(2)}, u32[]{:S(2)}) collective-permute-start(bf16[64,4224]{1,0:T(8,128)(2,1)S(1)} %collective-permute-done.1.rest_0_), channel_id=1, source_target_pairs={{0,1},{1,0},{2,3},{3,2},{4,5},{5,4},{6,7},{7,6},{8,9},{9,8},{10,11... | collective-permute-start | bytes 1622024 | tf_op jit(solution)/shard_map/ppermute | solution.py:452
  32.0 11.4 %collective-permute-start.5 = (bf16[64,4224]{1,0:T(8,128)(2,1)S(1)}, bf16[64,4224]{1,0:T(8,128)(2,1)S(1)}, u32[]{:S(2)}, u32[]{:S(2)}) collective-permute-start(bf16[64,4224]{1,0:T(8,128)(2,1)S(1)} %collective-permute-done.1.rest_0_), channel_id=1, source_target_pairs={{0,4},{4,8},{8,12},{12,14},{14,10},{10,6},{6,2},{2,0},{5,1},{9,5},... | collective-permute-start | bytes 1622024 | tf_op jit(solution)/shard_map/ppermute | solution.py:449
  37.6 7.7 %collective-permute-start.12 = (bf16[64,4096]{1,0:T(8,128)(2,1)S(1)}, bf16[64,4096]{1,0:T(8,128)(2,1)S(1)}, u32[]{:S(2)}, u32[]{:S(2)}) collective-permute-start(bf16[64,4096]{1,0:T(8,128)(2,1)S(1)} %collective-permute-done.11.rest_0_), channel_id=1, source_target_pairs={{0,1},{1,0},{2,3},{3,2},{4,5},{5,4},{6,7},{7,6},{8,9},{9,8},{10,11... | collective-permute-start | bytes 1572872 | tf_op jit(solution)/shard_map/ppermute | solution.py:452
  37.8 9.6 %collective-permute-start.14 = (bf16[64,2048]{1,0:T(8,128)(2,1)S(1)}, bf16[64,2048]{1,0:T(8,128)(2,1)S(1)}, u32[]{:S(2)}, u32[]{:S(2)}) collective-permute-start(bf16[64,2048]{1,0:T(8,128)(2,1)S(1)} %constant_dynamic-slice_fusion.1), channel_id=1, source_target_pairs={{0,4},{4,8},{8,12},{12,14},{14,10},{10,6},{6,2},{2,0},{5,1},{9,5},... | collective-permute-start | bytes 786440 | tf_op jit(solution)/shard_map/ppermute | solution.py:449
  43.4 4.0 %collective-permute-start.10 = (bf16[64,4224]{1,0:T(8,128)(2,1)S(1)}, bf16[64,4224]{1,0:T(8,128)(2,1)S(1)}, u32[]{:S(2)}, u32[]{:S(2)}) collective-permute-start(bf16[64,4224]{1,0:T(8,128)(2,1)S(1)} %collective-permute-done.5.rest_0_), channel_id=1, source_target_pairs={{0,1},{1,0},{2,3},{3,2},{4,5},{5,4},{6,7},{7,6},{8,9},{9,8},{10,11... | collective-permute-start | bytes 1622024 | tf_op jit(solution)/shard_map/ppermute | solution.py:452
  43.6 6.8 %collective-permute-start.9 = (bf16[64,2176]{1,0:T(8,128)(2,1)S(1)}, bf16[64,2176]{1,0:T(8,128)(2,1)S(1)}, u32[]{:S(2)}, u32[]{:S(2)}) collective-permute-start(bf16[64,2176]{1,0:T(8,128)(2,1)S(1)} %constant_dynamic-slice_fusion.2), channel_id=1, source_target_pairs={{0,4},{4,8},{8,12},{12,14},{14,10},{10,6},{6,2},{2,0},{5,1},{9,5},... | collective-permute-start | bytes 835592 | tf_op jit(solution)/shard_map/ppermute | solution.py:449
  47.3 3.1 %collective-permute-start.15 = (bf16[64,2048]{1,0:T(8,128)(2,1)S(1)}, bf16[64,2048]{1,0:T(8,128)(2,1)S(1)}, u32[]{:S(2)}, u32[]{:S(2)}) collective-permute-start(bf16[64,2048]{1,0:T(8,128)(2,1)S(1)} %collective-permute-done.14.rest_0_), channel_id=1, source_target_pairs={{0,1},{1,0},{2,3},{3,2},{4,5},{5,4},{6,7},{7,6},{8,9},{9,8},{10,11... | collective-permute-start | bytes 786440 | tf_op jit(solution)/shard_map/ppermute | solution.py:452
  50.3 2.2 %collective-permute-start.13 = (bf16[64,2176]{1,0:T(8,128)(2,1)S(1)}, bf16[64,2176]{1,0:T(8,128)(2,1)S(1)}, u32[]{:S(2)}, u32[]{:S(2)}) collective-permute-start(bf16[64,2176]{1,0:T(8,128)(2,1)S(1)} %collective-permute-done.9.rest_0_), channel_id=1, source_target_pairs={{0,1},{1,0},{2,3},{3,2},{4,5},{5,4},{6,7},{7,6},{8,9},{9,8},{10,11... | collective-permute-start | bytes 835592 | tf_op jit(solution)/shard_map/ppermute | solution.py:452
  61.6 1.5 %collective-permute-start.16 = (f32[8,4,1152]{2,1,0:T(4,128)S(1)}, f32[8,4,1152]{2,1,0:T(4,128)S(1)}, u32[]{:S(2)}, u32[]{:S(2)}) collective-permute-start(f32[8,4,1152]{2,1,0:T(4,128)S(1)} %get-tuple-element.59), channel_id=1, source_target_pairs={{0,1},{1,0},{2,3},{3,2},{4,5},{5,4},{6,7},{7,6},{8,9},{9,8},{10,11... | collective-permute-start | bytes 442376 | tf_op jit(solution)/shard_map/ppermute | solution.py:468
  63.1 4.6 %collective-permute-start.17 = (f32[4,4,1152]{2,1,0:T(4,128)S(1)}, f32[4,4,1152]{2,1,0:T(4,128)S(1)}, u32[]{:S(2)}, u32[]{:S(2)}) collective-permute-start(f32[4,4,1152]{2,1,0:T(4,128)S(1)} %dynamic-slice_bitcast_fusion), channel_id=1, source_target_pairs={{0,2},{2,0},{4,6},{6,4},{8,10},{10,8},{12,14},{14,12},{1,3},{3,1},... | collective-permute-start | bytes 221192 | tf_op jit(solution)/shard_map/ppermute | solution.py:395
  67.8 4.0 %collective-permute-start.18 = (f32[2,4,1152]{2,1,0:T(4,128)S(1)}, f32[2,4,1152]{2,1,0:T(4,128)S(1)}, u32[]{:S(2)}, u32[]{:S(2)}) collective-permute-start(f32[2,4,1152]{2,1,0:T(4,128)S(1)} %dynamic-slice_bitcast_fusion.1), channel_id=1, source_target_pairs={{0,4},{2,6},{4,0},{6,2},{8,12},{10,14},{12,8},{14,10},{1,5},{3,7},... | collective-permute-start | bytes 110600 | tf_op jit(solution)/shard_map/ppermute | solution.py:395
  71.8 4.7 %collective-permute-start.19 = (f32[1,4,1152]{2,1,0:T(4,128)S(1)}, f32[1,4,1152]{2,1,0:T(4,128)S(1)}, u32[]{:S(2)}, u32[]{:S(2)}) collective-permute-start(f32[1,4,1152]{2,1,0:T(4,128)S(1)} %constant_dynamic-slice_fusion), channel_id=1, source_target_pairs={{0,8},{2,10},{4,12},{6,14},{8,0},{10,2},{12,4},{14,6},{1,9},{3,11}... | collective-permute-start | bytes 55304 | tf_op jit(solution)/shard_map/ppermute | solution.py:395

commit v7 on v6

--- a/solution.py
+++ b/solution.py
@@ -10,11 +10,10 @@
 LOWEST = -1e30
 STEPS = 16
 WIDTH = 1024
-SLOTS = 4
 STRIP = 256
 LANES = 128
 STATE_ROWS = 8
-VMEM_LIMIT = 10 * 1024 * 1024
+VMEM_LIMIT = 14 * 1024 * 1024
 SMALL_LIMIT = 6 * 1024 * 1024
 
 
@@ -24,27 +23,33 @@
     return list(range(blocks))
 
 
-def message_kernel(tags_ref, rows_ref, out_ref, tags, sent):
-    height, span = out_ref.shape[0], out_ref.shape[1] - LANES
+def message_kernel(tags_ref, rows_ref, first_ref, second_ref, tags, sent):
+    height, span = first_ref.shape
     copies = [
         pltpu.make_async_copy(tags_ref, tags, sent.at[0]),
-        pltpu.make_async_copy(rows_ref.at[:, span:], out_ref.at[:, :span], sent.at[1]),
+        pltpu.make_async_copy(rows_ref.at[:, :span], first_ref, sent.at[1]),
+        pltpu.make_async_copy(rows_ref.at[:, span:], second_ref.at[:, :span], sent.at[2]),
     ]
     for copy in copies:
         copy.start()
     copies[0].wait()
-    out_ref[:, span:] = tag_rows(tags, height).astype(jnp.bfloat16)
-    copies[1].wait()
-
-
-def tagged_message(tags, templates):
+    second_ref[:, span:] = tag_rows(tags, height).astype(jnp.bfloat16)
+    for copy in copies[1:]:
+        copy.wait()
+
+
+def make_messages(tags, templates):
     height, freqs = templates.shape
+    span = freqs // 2
     return pl.pallas_call(
         message_kernel,
         in_specs=[pl.BlockSpec(memory_space=pl.ANY)] * 2,
-        out_specs=in_vmem(),
-        out_shape=pltpu.VMEM((height, freqs // 2 + LANES), jnp.bfloat16),
-        scratch_shapes=[pltpu.VMEM(tags.shape, tags.dtype), pltpu.SemaphoreType.DMA((2,))],
+        out_specs=[in_vmem(), in_vmem()],
+        out_shape=[
+            pltpu.VMEM((height, span), jnp.bfloat16),
+            pltpu.VMEM((height, span + LANES), jnp.bfloat16),
+        ],
+        scratch_shapes=[pltpu.VMEM(tags.shape, tags.dtype), pltpu.SemaphoreType.DMA((3,))],
         compiler_params=pltpu.CompilerParams(vmem_limit_bytes=SMALL_LIMIT),
     )(
         pltpu.with_memory_space_constraint(tags, pltpu.HBM),
@@ -138,22 +143,21 @@
 
 def own_kernel(phase, where_ref, noise_ref, tmpl_ref, far_ref, *rest):
     if phase == 0:
-        sig_ref, turned_ref, words_ref, acc, energy, slots, arrived = rest
+        sig_ref, turned_ref, words_ref, acc, energy, near, arrived = rest
     else:
         acc_in, energy_in, logs_ref, tags_ref, words_ref, *rest = rest
-        turned_ref, out_ref, acc, energy, slots, arrived = rest
+        turned_ref, out_ref, acc, energy, near, arrived = rest
     span = turned_ref.shape[0]
     height = tmpl_ref.shape[0]
-    width = slots.shape[2]
+    width = near.shape[2]
     steps = span // width
     low = phase * span
 
     def copy(step):
         columns = pl.ds(pl.multiple_of(low + step * width, width), width)
-        slot = lax.rem(step, SLOTS)
-        return pltpu.make_async_copy(far_ref.at[:, columns], slots.at[slot], arrived.at[slot])
-
-    for step in range(SLOTS):
+        return pltpu.make_async_copy(far_ref.at[:, columns], near.at[step], arrived.at[step])
+
+    for step in range(steps):
         copy(step).start()
     if phase == 0:
         pick_words(sig_ref, words_ref)
@@ -165,17 +169,12 @@
     @pl.loop(0, steps)
     def _(step):
         copy(step).wait()
-        slot = lax.rem(step, SLOTS)
         for strip in range(0, width, STRIP):
             there = pl.ds(pl.multiple_of(step * width + strip, STRIP), STRIP)
             weighted = weigh(tmpl_ref[:, there], noise_ref[:, there], energy)
-            turned = jnp.transpose(slots[slot, :, strip : strip + STRIP])
+            turned = jnp.transpose(near[step, :, strip : strip + STRIP])
             turned_ref[there, :] = turned
             acc[...] += jnp.dot(weighted, turned, preferred_element_type=jnp.float32)
-
-        @pl.when(step + SLOTS < steps)
-        def _():
-            copy(step + SLOTS).start()
 
     if phase == 0:
         return
@@ -198,8 +197,8 @@
     ]
     shapes = [pltpu.VMEM((freqs // 2, per_device), particles.dtype)]
     scratch = [
-        pltpu.VMEM((SLOTS, per_device, width), particles.dtype),
-        pltpu.SemaphoreType.DMA((SLOTS,)),
+        pltpu.VMEM((STEPS // 2, per_device, width), particles.dtype),
+        pltpu.SemaphoreType.DMA((STEPS // 2,)),
     ]
     if phase == 0:
         shapes += [jax.ShapeDtypeStruct((total // 32, per_device), jnp.int32)] + sums
@@ -291,8 +290,9 @@
     else:
         pieces = [(row_refs, 0)]
     for refs, start in pieces:
-        for step in range(span // WIDTH):
-            here = pl.ds(step * WIDTH, WIDTH)
+
+        def add(step):
+            here = pl.ds(pl.multiple_of(step * WIDTH, WIDTH), WIDTH)
             there = pl.ds(pl.multiple_of(start + step * WIDTH, WIDTH), WIDTH)
             columns = pl.ds(pl.multiple_of(phase * half + start + step * WIDTH, WIDTH), WIDTH)
             rows = jnp.concatenate([ref[:, here] for ref in refs], axis=0)
@@ -300,6 +300,12 @@
             acc[...] += jnp.dot(
                 weighted, part_ref[there, :], preferred_element_type=jnp.float32
             )
+
+        if ends and phase == 1:
+            pl.loop(0, span // WIDTH)(add)
+        else:
+            for step in range(span // WIDTH):
+                add(step)
 
     if phase == 0:
         return
@@ -412,9 +418,7 @@
     noise = inv_noise[None, :]
     logs = jnp.log(class_counts.astype(jnp.float32))
     tags = template_class[None, :]
-    head = templates[:, : freqs // 2]
-    head, later = lax.optimization_barrier((head, templates))
-    held = [head, tagged_message(tags, later)]
+    held = make_messages(tags, templates)
     where = jnp.stack([block_id, core])
     cut = freqs // 4
     where, cut_at = lax.optimization_barrier((where, core.astype(jnp.uint32) * cut))

time: 77.7 us -> 74.9 us (0.964)
  waiting for transfers between devices: 17.5 us -> 15.9 us
  Pallas kernels: 38.6 us -> 37.1 us
  starting transfers between devices: 18 us -> 19.5 us
  local copies, waits for them, and re-layouts: 1.53 us -> 0.45 us
    pallas_call x8, Pallas kernels: 24.4 us -> 22.6 us  [ring_scores(): pl.pallas_call(functools.partial(ring_kernel, phase, ends, sources), in_s...]
    slice x1 -> x0, local copies, waits for them, and re-layouts: 1.08 us -> none  [body(): head = templates[:, :freqs // 2]]
    ppermute x3, waiting for transfers between devices: 9.61 us -> 8.53 us  [scatter_sum(): pieces = keep + lax.ppermute(send, 'blk', swaps)]
    ppermute x3, starting transfers between devices: 3.74 us -> 4.82 us  [scatter_sum(): pieces = keep + lax.ppermute(send, 'blk', swaps)]
where the time goes in v7:
time: 74.9 us; the launch traced here: 74.7 us
  Pallas kernels  37.1 us (50%)
  starting transfers between devices  19.5 us (26%)
  waiting for transfers between devices  15.9 us (21%)
  other arithmetic  0.93 us (1%)
  between operations  0.85 us (1%)
    pallas_call x8, Pallas kernels, ring_scores(): pl.pallas_call(functools.partial(ring_kernel, phase, ends, sources), in_s...  22.6 us
    ppermute x8, starting transfers between devices, body(): own = lax.ppermute(message, ('blk', 'cls'), ring)  13.8 us
    pallas_call x2, Pallas kernels, own_scores(): pl.pallas_call(functools.partial(own_kernel, phase), grid=(1,), in_specs=...  13.2 us
    ppermute x3, waiting for transfers between devices, scatter_sum(): pieces = keep + lax.ppermute(send, 'blk', swaps)  8.53 us
    ppermute x8, waiting for transfers between devices, body(): own = lax.ppermute(message, ('blk', 'cls'), ring)  6.38 us
    ppermute x3, starting transfers between devices, scatter_sum(): pieces = keep + lax.ppermute(send, 'blk', swaps)  4.82 us
  transfers between devices with their start and end apart: 20, of which 8 were waited for; matrix products, arithmetic and copies ran while one was open for 0% of the time, Pallas kernels for 38%

profile of v7, /device:TPU:0, one launch (start us, length us, event | category | flops | bytes accessed | tf_op | source)
XLA Modules:
  0.0 74.7 jit_solution(12933467769282211850)
XLA Ops:
  1.9 3.1 %collective-permute-start.3 = (bf16[64,4096]{1,0:T(8,128)(2,1)S(1)}, bf16[64,4096]{1,0:T(8,128)(2,1)S(1)}, u32[]{:S(2)}, u32[]{:S(2)}) collective-permute-start(bf16[64,4096]{1,0:T(8,128)(2,1)S(1)} %get-tuple-element.40), channel_id=1, source_target_pairs={{0,4},{4,8},{8,12},{12,14},{14,10},{10,6},{6,2},{2,0},{5,1},{9,5},... | collective-permute-start | bytes 1572872 | tf_op jit(solution)/shard_map/ppermute | solution.py:453
  5.0 1.6 %collective-permute-start = (bf16[64,4224]{1,0:T(8,128)(2,1)S(1)}, bf16[64,4224]{1,0:T(8,128)(2,1)S(1)}, u32[]{:S(2)}, u32[]{:S(2)}) collective-permute-start(bf16[64,4224]{1,0:T(8,128)(2,1)S(1)} %get-tuple-element.36), channel_id=1, source_target_pairs={{0,4},{4,8},{8,12},{12,14},{14,10},{10,6},{6,2},{2,0},{5,1},{9,5},... | collective-permute-start | bytes 1622024 | tf_op jit(solution)/shard_map/ppermute | solution.py:453
  6.6 6.4 %shard_map.77 = (bf16[4096,1024]{1,0:T(8,128)(2,1)S(1)}, s32[16,1024]{1,0:T(8,128)S(1)}, f32[64,1024]{1,0:T(8,128)S(1)}, f32[64,128]{1,0:T(8,128)S(1)}) custom-call(s32[2]{0:T(128)S(1)} %pad_add_fusion.where_ref, f32[1,8192]{1,0:T(1,128)} %bitcast.17, bf16[64,8192]{1,0:T(8,128)(2,1)} %rows_ref.1, bf16[1024,8192]{1,0:T(8,128)(2,1)} %rest_7_.1, s32[16,1024]{1,0:T(8,128)} %rest_0_.1), custom_call_target="tpu_custom_call" | custom-call | flops 2147483648 | bytes 8388608 | tf_op jit(solution)/shard_map/pallas_call | solution.py:211
  13.1 1.6 %collective-permute-start.7 = (bf16[64,4096]{1,0:T(8,128)(2,1)S(1)}, bf16[64,4096]{1,0:T(8,128)(2,1)S(1)}, u32[]{:S(2)}, u32[]{:S(2)}) collective-permute-start(bf16[64,4096]{1,0:T(8,128)(2,1)S(1)} %collective-permute-done.3.rest_0_), channel_id=1, source_target_pairs={{0,4},{4,8},{8,12},{12,14},{14,10},{10,6},{6,2},{2,0},{5,1},{9,5},... | collective-permute-start | bytes 1572872 | tf_op jit(solution)/shard_map/ppermute | solution.py:453
  14.8 6.8 %shard_map.78 = (bf16[4096,1024]{1,0:T(8,128)(2,1)S(1)}, f32[16,1024]{1,0:T(8,128)S(1)}) custom-call(s32[2]{0:T(128)S(1)} %pad_add_fusion.where_ref, f32[1,8192]{1,0:T(1,128)} %bitcast.18, bf16[64,8192]{1,0:T(8,128)(2,1)} %rows_ref.1, bf16[1024,8192]{1,0:T(8,128)(2,1)} %rest_7_.1, f32[64,1024]{1,0:T(8,128)S(1)} %get-tuple-element.32.rest_0_, ...), custom_call_target="tpu_custom_call" | custom-call | flops 2147483648 | bytes 8388608 | tf_op jit(solution)/shard_map/pallas_call | solution.py:211
  21.7 1.6 %collective-permute-start.1 = (bf16[64,4224]{1,0:T(8,128)(2,1)S(1)}, bf16[64,4224]{1,0:T(8,128)(2,1)S(1)}, u32[]{:S(2)}, u32[]{:S(2)}) collective-permute-start(bf16[64,4224]{1,0:T(8,128)(2,1)S(1)} %collective-permute-done.rest_0_), channel_id=1, source_target_pairs={{0,4},{4,8},{8,12},{12,14},{14,10},{10,6},{6,2},{2,0},{5,1},{9,5},... | collective-permute-start | bytes 1622024 | tf_op jit(solution)/shard_map/ppermute | solution.py:453
  23.3 2.0 %shard_map.80 = (f32[128,1024]{1,0:T(8,128)S(1)}, f32[128,128]{1,0:T(8,128)S(1)}) custom-call(s32[2]{0:T(128)S(1)} %pad_add_fusion.where_ref, f32[1,8192]{1,0:T(1,128)S(1)} %bitcast.19, bf16[4096,1024]{1,0:T(8,128)(2,1)S(1)} %get-tuple-element.39.part_ref, bf16[64,4096]{1,0:T(8,128)(2,1)S(1)} %collective-permute-done.3.rest_0_, ...), custom_call_target="tpu_custom_call" | custom-call | flops 2147483648 | bytes 8388608 | tf_op jit(solution)/shard_map/pallas_call | solution.py:367
  26.5 2.4 %shard_map.81.rest_6_ = f32[16,1024]{1,0:T(8,128)S(1)} custom-call(s32[2]{0:T(128)S(1)} %pad_add_fusion.where_ref, f32[1,8192]{1,0:T(1,128)S(1)} %bitcast.20, bf16[4096,1024]{1,0:T(8,128)(2,1)S(1)} %get-tuple-element.35.part_ref, bf16[64,4224]{1,0:T(8,128)(2,1)S(1)} %collective-permute-done.rest_0_, bf16[64,4224]{1,0:T(8,128)(2,1)S(1)} %collective-permute-done.2.rest_1_, ...), custom_call_target="tpu_custom_call" | custom-call | flops 2147483648 | bytes 8388608 | tf_op jit(solution)/shard_map/pallas_call | solution.py:367
  28.9 2.2 %collective-permute-done.1.rest_0_ = bf16[64,4224]{1,0:T(8,128)(2,1)S(1)} collective-permute-done((bf16[64,4224]{1,0:T(8,128)(2,1)S(1)}, bf16[64,4224]{1,0:T(8,128)(2,1)S(1)}, u32[]{:S(2)}, u32[]{:S(2)}) %collective-permute-start.1) | collective-permute-done | bytes 540704 | tf_op jit(solution)/shard_map/ppermute | solution.py:453
  32.6 2.0 %shard_map.82 = (f32[128,1024]{1,0:T(8,128)S(1)}, f32[128,128]{1,0:T(8,128)S(1)}) custom-call(s32[2]{0:T(128)S(1)} %pad_add_fusion.where_ref, f32[1,8192]{1,0:T(1,128)S(1)} %bitcast.21, bf16[4096,1024]{1,0:T(8,128)(2,1)S(1)} %get-tuple-element.39.part_ref, bf16[64,4096]{1,0:T(8,128)(2,1)S(1)} %collective-permute-done.7.rest_0_, ...), custom_call_target="tpu_custom_call" | custom-call | flops 2147483648 | bytes 8388608 | tf_op jit(solution)/shard_map/pallas_call | solution.py:367
  34.7 2.1 %collective-permute-done.11.rest_0_ = bf16[64,4096]{1,0:T(8,128)(2,1)S(1)} collective-permute-done((bf16[64,4096]{1,0:T(8,128)(2,1)S(1)}, bf16[64,4096]{1,0:T(8,128)(2,1)S(1)}, u32[]{:S(2)}, u32[]{:S(2)}) %collective-permute-start.11) | collective-permute-done | bytes 524320 | tf_op jit(solution)/shard_map/ppermute | solution.py:453
  36.9 1.6 %collective-permute-start.14 = (bf16[64,2048]{1,0:T(8,128)(2,1)S(1)}, bf16[64,2048]{1,0:T(8,128)(2,1)S(1)}, u32[]{:S(2)}, u32[]{:S(2)}) collective-permute-start(bf16[64,2048]{1,0:T(8,128)(2,1)S(1)} %constant_dynamic-slice_fusion.1), channel_id=1, source_target_pairs={{0,4},{4,8},{8,12},{12,14},{14,10},{10,6},{6,2},{2,0},{5,1},{9,5},... | collective-permute-start | bytes 786440 | tf_op jit(solution)/shard_map/ppermute | solution.py:453
  38.4 2.4 %shard_map.83.rest_6_ = f32[16,1024]{1,0:T(8,128)S(1)} custom-call(s32[2]{0:T(128)S(1)} %pad_add_fusion.where_ref, f32[1,8192]{1,0:T(1,128)S(1)} %bitcast.22, bf16[4096,1024]{1,0:T(8,128)(2,1)S(1)} %get-tuple-element.35.part_ref, bf16[64,4224]{1,0:T(8,128)(2,1)S(1)} %collective-permute-done.1.rest_0_, bf16[64,4224]{1,0:T(8,128)(2,1)S(1)} %collective-permute-done.6.rest_1_, ...), custom_call_target="tpu_custom_call" | custom-call | flops 2147483648 | bytes 8388608 | tf_op jit(solution)/shard_map/pallas_call | solution.py:367
  40.9 1.6 %collective-permute-done.5.rest_0_ = bf16[64,4224]{1,0:T(8,128)(2,1)S(1)} collective-permute-done((bf16[64,4224]{1,0:T(8,128)(2,1)S(1)}, bf16[64,4224]{1,0:T(8,128)(2,1)S(1)}, u32[]{:S(2)}, u32[]{:S(2)}) %collective-permute-start.5) | collective-permute-done | bytes 540704 | tf_op jit(solution)/shard_map/ppermute | solution.py:453
  42.7 1.7 %collective-permute-start.9 = (bf16[64,2176]{1,0:T(8,128)(2,1)S(1)}, bf16[64,2176]{1,0:T(8,128)(2,1)S(1)}, u32[]{:S(2)}, u32[]{:S(2)}) collective-permute-start(bf16[64,2176]{1,0:T(8,128)(2,1)S(1)} %constant_dynamic-slice_fusion.2), channel_id=1, source_target_pairs={{0,4},{4,8},{8,12},{12,14},{14,10},{10,6},{6,2},{2,0},{5,1},{9,5},... | collective-permute-start | bytes 835592 | tf_op jit(solution)/shard_map/ppermute | solution.py:453
  44.4 2.0 %shard_map.84 = (f32[128,1024]{1,0:T(8,128)S(1)}, f32[128,128]{1,0:T(8,128)S(1)}) custom-call(s32[2]{0:T(128)S(1)} %pad_add_fusion.where_ref, f32[1,8192]{1,0:T(1,128)S(1)} %bitcast.23, bf16[4096,1024]{1,0:T(8,128)(2,1)S(1)} %get-tuple-element.39.part_ref, bf16[64,4096]{1,0:T(8,128)(2,1)S(1)} %collective-permute-done.11.rest_0_, ...), custom_call_target="tpu_custom_call" | custom-call | flops 2147483648 | bytes 8388608 | tf_op jit(solution)/shard_map/pallas_call | solution.py:367
  46.5 2.4 %shard_map.85.rest_6_ = f32[16,1024]{1,0:T(8,128)S(1)} custom-call(s32[2]{0:T(128)S(1)} %pad_add_fusion.where_ref, f32[1,8192]{1,0:T(1,128)S(1)} %bitcast.24, bf16[4096,1024]{1,0:T(8,128)(2,1)S(1)} %get-tuple-element.35.part_ref, bf16[64,4224]{1,0:T(8,128)(2,1)S(1)} %collective-permute-done.5.rest_0_, bf16[64,4224]{1,0:T(8,128)(2,1)S(1)} %collective-permute-done.10.rest_1_, ...), custom_call_target="tpu_custom_call" | custom-call | flops 2147483648 | bytes 8388608 | tf_op jit(solution)/shard_map/pallas_call | solution.py:367
  49.5 2.2 %shard_map.86 = (f32[64,1024]{1,0:T(8,128)S(1)}, f32[64,128]{1,0:T(8,128)S(1)}) custom-call(s32[2]{0:T(128)S(1)} %pad_add_fusion.where_ref, f32[1,8192]{1,0:T(1,128)S(1)} %bitcast.25, bf16[4096,1024]{1,0:T(8,128)(2,1)S(1)} %get-tuple-element.39.part_ref, bf16[64,2048]{1,0:T(8,128)(2,1)S(1)} %collective-permute-done.14.rest_0_, ...), custom_call_target="tpu_custom_call" | custom-call | flops 2147483648 | bytes 8388608 | tf_op jit(solution)/shard_map/pallas_call | solution.py:367
  51.7 7.1 %shard_map.87 = (f32[1,1024]{1,0:T(1,128)}, f32[8,4,1152]{2,1,0:T(4,128)S(1)}, f32[8,4,1152]{2,1,0:T(4,128)S(1)}) custom-call(s32[2]{0:T(128)S(1)} %pad_add_fusion.where_ref, f32[1,8192]{1,0:T(1,128)S(1)} %bitcast.26, bf16[4096,1024]{1,0:T(8,128)(2,1)S(1)} %get-tuple-element.35.part_ref, bf16[64,2176]{1,0:T(8,128)(2,1)S(1)} %collective-permute-done.9.rest_0_, ...), custom_call_target="tpu_custom_call" | custom-call | flops 2147483648 | bytes 8388608 | tf_op jit(solution)/shard_map/pallas_call | solution.py:367
  61.6 3.5 %collective-permute-done.17 = f32[4,4,1152]{2,1,0:T(4,128)S(1)} collective-permute-done((f32[4,4,1152]{2,1,0:T(4,128)S(1)}, f32[4,4,1152]{2,1,0:T(4,128)S(1)}, u32[]{:S(2)}, u32[]{:S(2)}) %collective-permute-start.17) | collective-permute-done | bytes 73760 | tf_op jit(solution)/shard_map/ppermute | solution.py:401
  65.1 1.6 %collective-permute-start.18 = (f32[2,4,1152]{2,1,0:T(4,128)S(1)}, f32[2,4,1152]{2,1,0:T(4,128)S(1)}, u32[]{:S(2)}, u32[]{:S(2)}) collective-permute-start(f32[2,4,1152]{2,1,0:T(4,128)S(1)} %dynamic-slice_bitcast_fusion.1), channel_id=1, source_target_pairs={{0,4},{2,6},{4,0},{6,2},{8,12},{10,14},{12,8},{14,10},{1,5},{3,7},... | collective-permute-start | bytes 110600 | tf_op jit(solution)/shard_map/ppermute | solution.py:401
  66.6 2.4 %collective-permute-done.18 = f32[2,4,1152]{2,1,0:T(4,128)S(1)} collective-permute-done((f32[2,4,1152]{2,1,0:T(4,128)S(1)}, f32[2,4,1152]{2,1,0:T(4,128)S(1)}, u32[]{:S(2)}, u32[]{:S(2)}) %collective-permute-start.18) | collective-permute-done | bytes 36896 | tf_op jit(solution)/shard_map/ppermute | solution.py:401
  69.1 2.1 %collective-permute-start.19 = (f32[1,4,1152]{2,1,0:T(4,128)S(1)}, f32[1,4,1152]{2,1,0:T(4,128)S(1)}, u32[]{:S(2)}, u32[]{:S(2)}) collective-permute-start(f32[1,4,1152]{2,1,0:T(4,128)S(1)} %constant_dynamic-slice_fusion), channel_id=1, source_target_pairs={{0,8},{2,10},{4,12},{6,14},{8,0},{10,2},{12,4},{14,6},{1,9},{3,11}... | collective-permute-start | bytes 55304 | tf_op jit(solution)/shard_map/ppermute | solution.py:401
  71.2 2.6 %collective-permute-done.19 = f32[1,4,1152]{2,1,0:T(4,128)S(1)} collective-permute-done((f32[1,4,1152]{2,1,0:T(4,128)S(1)}, f32[1,4,1152]{2,1,0:T(4,128)S(1)}, u32[]{:S(2)}, u32[]{:S(2)}) %collective-permute-start.19) | collective-permute-done | bytes 18464 | tf_op jit(solution)/shard_map/ppermute | solution.py:401
  (47 shorter events, 8.8 us)
Async XLA Ops:
  1.9 11.1 %collective-permute-start.3 = (bf16[64,4096]{1,0:T(8,128)(2,1)S(1)}, bf16[64,4096]{1,0:T(8,128)(2,1)S(1)}, u32[]{:S(2)}, u32[]{:S(2)}) collective-permute-start(bf16[64,4096]{1,0:T(8,128)(2,1)S(1)} %get-tuple-element.40), channel_id=1, source_target_pairs={{0,4},{4,8},{8,12},{12,14},{14,10},{10,6},{6,2},{2,0},{5,1},{9,5},... | collective-permute-start | bytes 1572872 | tf_op jit(solution)/shard_map/ppermute | solution.py:453
  5.0 16.7 %collective-permute-start = (bf16[64,4224]{1,0:T(8,128)(2,1)S(1)}, bf16[64,4224]{1,0:T(8,128)(2,1)S(1)}, u32[]{:S(2)}, u32[]{:S(2)}) collective-permute-start(bf16[64,4224]{1,0:T(8,128)(2,1)S(1)} %get-tuple-element.36), channel_id=1, source_target_pairs={{0,4},{4,8},{8,12},{12,14},{14,10},{10,6},{6,2},{2,0},{5,1},{9,5},... | collective-permute-start | bytes 1622024 | tf_op jit(solution)/shard_map/ppermute | solution.py:453
  6.6 6.5 %copy-start.2 = (s32[8]{0:T(128)S(1)}, s32[8]{0:T(128)}, u32[]{:S(2)}) copy-start(s32[8]{0:T(128)} %param.10) | copy-start | bytes 100
  6.6 8.2 %copy-start.1 = (s32[64]{0:T(128)S(1)}, s32[64]{0:T(128)}, u32[]{:S(2)}) copy-start(s32[64]{0:T(128)} %param.9) | copy-start | bytes 772
  13.0 10.2 %collective-permute-start.4 = (bf16[64,4096]{1,0:T(8,128)(2,1)S(1)}, bf16[64,4096]{1,0:T(8,128)(2,1)S(1)}, u32[]{:S(2)}, u32[]{:S(2)}) collective-permute-start(bf16[64,4096]{1,0:T(8,128)(2,1)S(1)} %collective-permute-done.3.rest_0_), channel_id=1, source_target_pairs={{0,1},{1,0},{2,3},{3,2},{4,5},{5,4},{6,7},{7,6},{8,9},{9,8},{10,11... | collective-permute-start | bytes 1572872 | tf_op jit(solution)/shard_map/ppermute | solution.py:456
  13.1 12.1 %collective-permute-start.7 = (bf16[64,4096]{1,0:T(8,128)(2,1)S(1)}, bf16[64,4096]{1,0:T(8,128)(2,1)S(1)}, u32[]{:S(2)}, u32[]{:S(2)}) collective-permute-start(bf16[64,4096]{1,0:T(8,128)(2,1)S(1)} %collective-permute-done.3.rest_0_), channel_id=1, source_target_pairs={{0,4},{4,8},{8,12},{12,14},{14,10},{10,6},{6,2},{2,0},{5,1},{9,5},... | collective-permute-start | bytes 1572872 | tf_op jit(solution)/shard_map/ppermute | solution.py:453
  14.8 8.5 %copy-start = (f32[8192]{0:T(1024)S(1)}, f32[8192]{0:T(1024)}, u32[]{:S(2)}) copy-start(f32[8192]{0:T(1024)} %param.11) | copy-start | bytes 98308
  21.6 4.9 %collective-permute-start.2 = (bf16[64,4224]{1,0:T(8,128)(2,1)S(1)}, bf16[64,4224]{1,0:T(8,128)(2,1)S(1)}, u32[]{:S(2)}, u32[]{:S(2)}) collective-permute-start(bf16[64,4224]{1,0:T(8,128)(2,1)S(1)} %collective-permute-done.rest_0_), channel_id=1, source_target_pairs={{0,1},{1,0},{2,3},{3,2},{4,5},{5,4},{6,7},{7,6},{8,9},{9,8},{10,11... | collective-permute-start | bytes 1622024 | tf_op jit(solution)/shard_map/ppermute | solution.py:456
  21.7 9.4 %collective-permute-start.1 = (bf16[64,4224]{1,0:T(8,128)(2,1)S(1)}, bf16[64,4224]{1,0:T(8,128)(2,1)S(1)}, u32[]{:S(2)}, u32[]{:S(2)}) collective-permute-start(bf16[64,4224]{1,0:T(8,128)(2,1)S(1)} %collective-permute-done.rest_0_), channel_id=1, source_target_pairs={{0,4},{4,8},{8,12},{12,14},{14,10},{10,6},{6,2},{2,0},{5,1},{9,5},... | collective-permute-start | bytes 1622024 | tf_op jit(solution)/shard_map/ppermute | solution.py:453
  25.3 7.3 %collective-permute-start.8 = (bf16[64,4096]{1,0:T(8,128)(2,1)S(1)}, bf16[64,4096]{1,0:T(8,128)(2,1)S(1)}, u32[]{:S(2)}, u32[]{:S(2)}) collective-permute-start(bf16[64,4096]{1,0:T(8,128)(2,1)S(1)} %collective-permute-done.7.rest_0_), channel_id=1, source_target_pairs={{0,1},{1,0},{2,3},{3,2},{4,5},{5,4},{6,7},{7,6},{8,9},{9,8},{10,11... | collective-permute-start | bytes 1572872 | tf_op jit(solution)/shard_map/ppermute | solution.py:456
  25.4 11.4 %collective-permute-start.11 = (bf16[64,4096]{1,0:T(8,128)(2,1)S(1)}, bf16[64,4096]{1,0:T(8,128)(2,1)S(1)}, u32[]{:S(2)}, u32[]{:S(2)}) collective-permute-start(bf16[64,4096]{1,0:T(8,128)(2,1)S(1)} %collective-permute-done.7.rest_0_), channel_id=1, source_target_pairs={{0,4},{4,8},{8,12},{12,14},{14,10},{10,6},{6,2},{2,0},{5,1},{9,5},... | collective-permute-start | bytes 1572872 | tf_op jit(solution)/shard_map/ppermute | solution.py:453
  31.1 7.3 %collective-permute-start.6 = (bf16[64,4224]{1,0:T(8,128)(2,1)S(1)}, bf16[64,4224]{1,0:T(8,128)(2,1)S(1)}, u32[]{:S(2)}, u32[]{:S(2)}) collective-permute-start(bf16[64,4224]{1,0:T(8,128)(2,1)S(1)} %collective-permute-done.1.rest_0_), channel_id=1, source_target_pairs={{0,1},{1,0},{2,3},{3,2},{4,5},{5,4},{6,7},{7,6},{8,9},{9,8},{10,11... | collective-permute-start | bytes 1622024 | tf_op jit(solution)/shard_map/ppermute | solution.py:456
  31.1 11.4 %collective-permute-start.5 = (bf16[64,4224]{1,0:T(8,128)(2,1)S(1)}, bf16[64,4224]{1,0:T(8,128)(2,1)S(1)}, u32[]{:S(2)}, u32[]{:S(2)}) collective-permute-start(bf16[64,4224]{1,0:T(8,128)(2,1)S(1)} %collective-permute-done.1.rest_0_), channel_id=1, source_target_pairs={{0,4},{4,8},{8,12},{12,14},{14,10},{10,6},{6,2},{2,0},{5,1},{9,5},... | collective-permute-start | bytes 1622024 | tf_op jit(solution)/shard_map/ppermute | solution.py:453
  36.7 7.7 %collective-permute-start.12 = (bf16[64,4096]{1,0:T(8,128)(2,1)S(1)}, bf16[64,4096]{1,0:T(8,128)(2,1)S(1)}, u32[]{:S(2)}, u32[]{:S(2)}) collective-permute-start(bf16[64,4096]{1,0:T(8,128)(2,1)S(1)} %collective-permute-done.11.rest_0_), channel_id=1, source_target_pairs={{0,1},{1,0},{2,3},{3,2},{4,5},{5,4},{6,7},{7,6},{8,9},{9,8},{10,11... | collective-permute-start | bytes 1572872 | tf_op jit(solution)/shard_map/ppermute | solution.py:456
  36.9 9.6 %collective-permute-start.14 = (bf16[64,2048]{1,0:T(8,128)(2,1)S(1)}, bf16[64,2048]{1,0:T(8,128)(2,1)S(1)}, u32[]{:S(2)}, u32[]{:S(2)}) collective-permute-start(bf16[64,2048]{1,0:T(8,128)(2,1)S(1)} %constant_dynamic-slice_fusion.1), channel_id=1, source_target_pairs={{0,4},{4,8},{8,12},{12,14},{14,10},{10,6},{6,2},{2,0},{5,1},{9,5},... | collective-permute-start | bytes 786440 | tf_op jit(solution)/shard_map/ppermute | solution.py:453
  42.5 4.0 %collective-permute-start.10 = (bf16[64,4224]{1,0:T(8,128)(2,1)S(1)}, bf16[64,4224]{1,0:T(8,128)(2,1)S(1)}, u32[]{:S(2)}, u32[]{:S(2)}) collective-permute-start(bf16[64,4224]{1,0:T(8,128)(2,1)S(1)} %collective-permute-done.5.rest_0_), channel_id=1, source_target_pairs={{0,1},{1,0},{2,3},{3,2},{4,5},{5,4},{6,7},{7,6},{8,9},{9,8},{10,11... | collective-permute-start | bytes 1622024 | tf_op jit(solution)/shard_map/ppermute | solution.py:456
  42.7 6.8 %collective-permute-start.9 = (bf16[64,2176]{1,0:T(8,128)(2,1)S(1)}, bf16[64,2176]{1,0:T(8,128)(2,1)S(1)}, u32[]{:S(2)}, u32[]{:S(2)}) collective-permute-start(bf16[64,2176]{1,0:T(8,128)(2,1)S(1)} %constant_dynamic-slice_fusion.2), channel_id=1, source_target_pairs={{0,4},{4,8},{8,12},{12,14},{14,10},{10,6},{6,2},{2,0},{5,1},{9,5},... | collective-permute-start | bytes 835592 | tf_op jit(solution)/shard_map/ppermute | solution.py:453
  46.4 3.1 %collective-permute-start.15 = (bf16[64,2048]{1,0:T(8,128)(2,1)S(1)}, bf16[64,2048]{1,0:T(8,128)(2,1)S(1)}, u32[]{:S(2)}, u32[]{:S(2)}) collective-permute-start(bf16[64,2048]{1,0:T(8,128)(2,1)S(1)} %collective-permute-done.14.rest_0_), channel_id=1, source_target_pairs={{0,1},{1,0},{2,3},{3,2},{4,5},{5,4},{6,7},{7,6},{8,9},{9,8},{10,11... | collective-permute-start | bytes 786440 | tf_op jit(solution)/shard_map/ppermute | solution.py:456
  49.4 2.2 %collective-permute-start.13 = (bf16[64,2176]{1,0:T(8,128)(2,1)S(1)}, bf16[64,2176]{1,0:T(8,128)(2,1)S(1)}, u32[]{:S(2)}, u32[]{:S(2)}) collective-permute-start(bf16[64,2176]{1,0:T(8,128)(2,1)S(1)} %collective-permute-done.9.rest_0_), channel_id=1, source_target_pairs={{0,1},{1,0},{2,3},{3,2},{4,5},{5,4},{6,7},{7,6},{8,9},{9,8},{10,11... | collective-permute-start | bytes 835592 | tf_op jit(solution)/shard_map/ppermute | solution.py:456
  58.8 1.5 %collective-permute-start.16 = (f32[8,4,1152]{2,1,0:T(4,128)S(1)}, f32[8,4,1152]{2,1,0:T(4,128)S(1)}, u32[]{:S(2)}, u32[]{:S(2)}) collective-permute-start(f32[8,4,1152]{2,1,0:T(4,128)S(1)} %get-tuple-element.59), channel_id=1, source_target_pairs={{0,1},{1,0},{2,3},{3,2},{4,5},{5,4},{6,7},{7,6},{8,9},{9,8},{10,11... | collective-permute-start | bytes 442376 | tf_op jit(solution)/shard_map/ppermute | solution.py:472
  60.4 4.6 %collective-permute-start.17 = (f32[4,4,1152]{2,1,0:T(4,128)S(1)}, f32[4,4,1152]{2,1,0:T(4,128)S(1)}, u32[]{:S(2)}, u32[]{:S(2)}) collective-permute-start(f32[4,4,1152]{2,1,0:T(4,128)S(1)} %dynamic-slice_bitcast_fusion), channel_id=1, source_target_pairs={{0,2},{2,0},{4,6},{6,4},{8,10},{10,8},{12,14},{14,12},{1,3},{3,1},... | collective-permute-start | bytes 221192 | tf_op jit(solution)/shard_map/ppermute | solution.py:401
  65.1 4.0 %collective-permute-start.18 = (f32[2,4,1152]{2,1,0:T(4,128)S(1)}, f32[2,4,1152]{2,1,0:T(4,128)S(1)}, u32[]{:S(2)}, u32[]{:S(2)}) collective-permute-start(f32[2,4,1152]{2,1,0:T(4,128)S(1)} %dynamic-slice_bitcast_fusion.1), channel_id=1, source_target_pairs={{0,4},{2,6},{4,0},{6,2},{8,12},{10,14},{12,8},{14,10},{1,5},{3,7},... | collective-permute-start | bytes 110600 | tf_op jit(solution)/shard_map/ppermute | solution.py:401
  69.1 4.7 %collective-permute-start.19 = (f32[1,4,1152]{2,1,0:T(4,128)S(1)}, f32[1,4,1152]{2,1,0:T(4,128)S(1)}, u32[]{:S(2)}, u32[]{:S(2)}) collective-permute-start(f32[1,4,1152]{2,1,0:T(4,128)S(1)} %constant_dynamic-slice_fusion), channel_id=1, source_target_pairs={{0,8},{2,10},{4,12},{6,14},{8,0},{10,2},{12,4},{14,6},{1,9},{3,11}... | collective-permute-start | bytes 55304 | tf_op jit(solution)/shard_map/ppermute | solution.py:401

commit v8 on v7

--- a/solution.py
+++ b/solution.py
@@ -13,7 +13,7 @@
 STRIP = 256
 LANES = 128
 STATE_ROWS = 8
-VMEM_LIMIT = 14 * 1024 * 1024
+VMEM_LIMIT = 16 * 1024 * 1024
 SMALL_LIMIT = 6 * 1024 * 1024
 
 
@@ -141,17 +141,22 @@
     return state_ref[0:1, :], state_ref[1:2, :], state_ref[2:3, :], state_ref[STATE_ROWS:, :]
 
 
-def own_kernel(phase, where_ref, noise_ref, tmpl_ref, far_ref, *rest):
-    if phase == 0:
-        sig_ref, turned_ref, words_ref, acc, energy, near, arrived = rest
-    else:
-        acc_in, energy_in, logs_ref, tags_ref, words_ref, *rest = rest
-        turned_ref, out_ref, acc, energy, near, arrived = rest
-    span = turned_ref.shape[0]
-    height = tmpl_ref.shape[0]
-    width = near.shape[2]
-    steps = span // width
-    low = phase * span
+def own_kernel(first, last, low, where_ref, noise_ref, tmpl_ref, far_ref, *rest):
+    if first:
+        sig_ref, words_ref, acc, energy, *turned_refs, near, arrived = rest
+        pick_words(sig_ref, words_ref)
+        acc[...] = jnp.zeros_like(acc)
+        energy[...] = jnp.zeros_like(energy)
+    else:
+        acc_in, energy_in, *rest = rest
+        if last:
+            logs_ref, tags_ref, words_ref, out_ref, *turned_refs, acc, energy, near, arrived = rest
+        else:
+            acc, energy, *turned_refs, near, arrived = rest
+        acc[...] = acc_in[...]
+        energy[...] = energy_in[...]
+    span, height, width = turned_refs[0].shape[0], tmpl_ref.shape[0], near.shape[2]
+    steps = near.shape[0]
 
     def copy(step):
         columns = pl.ds(pl.multiple_of(low + step * width, width), width)
@@ -159,24 +164,21 @@
 
     for step in range(steps):
         copy(step).start()
-    if phase == 0:
-        pick_words(sig_ref, words_ref)
-        acc[...] = jnp.zeros_like(acc)
-        energy[...] = jnp.zeros_like(energy)
-    else:
-        acc[...] = acc_in[...]
-        energy[...] = energy_in[...]
-    @pl.loop(0, steps)
-    def _(step):
-        copy(step).wait()
-        for strip in range(0, width, STRIP):
-            there = pl.ds(pl.multiple_of(step * width + strip, STRIP), STRIP)
-            weighted = weigh(tmpl_ref[:, there], noise_ref[:, there], energy)
-            turned = jnp.transpose(near[step, :, strip : strip + STRIP])
-            turned_ref[there, :] = turned
-            acc[...] += jnp.dot(weighted, turned, preferred_element_type=jnp.float32)
-
-    if phase == 0:
+    for quarter, turned_ref in enumerate(turned_refs):
+
+        @pl.loop(0, span // width)
+        def _(inner):
+            step = quarter * (span // width) + inner
+            copy(step).wait()
+            for strip in range(0, width, STRIP):
+                there = pl.ds(pl.multiple_of(inner * width + strip, STRIP), STRIP)
+                columns = pl.ds(pl.multiple_of(low + step * width + strip, STRIP), STRIP)
+                weighted = weigh(tmpl_ref[:, columns], noise_ref[:, columns], energy)
+                turned = jnp.transpose(near[step, :, strip : strip + STRIP])
+                turned_ref[there, :] = turned
+                acc[...] += jnp.dot(weighted, turned, preferred_element_type=jnp.float32)
+
+    if not last:
         return
     tags = tag_rows(tags_ref, height)
     hit = picked_rows(words_ref, where_ref[0], height)
@@ -187,39 +189,39 @@
     put_state(add_rows(tags, hit, logs_ref, state, acc, energy), out_ref)
 
 
-def own_scores(phase, where, noise, templates, particles, rest, total=0):
+def own_scores(quarters, where, noise, templates, particles, rest, total=0):
     per_device, freqs = particles.shape
     height = templates.shape[0]
     width = freqs // STEPS
+    span = freqs // 4
+    steps = len(quarters) * span // width
+    first, last = quarters[0] == 0, quarters[-1] == 3
     sums = [
         jax.ShapeDtypeStruct((height, per_device), jnp.float32),
         jax.ShapeDtypeStruct((height, LANES), jnp.float32),
     ]
-    shapes = [pltpu.VMEM((freqs // 2, per_device), particles.dtype)]
+    turned = [pltpu.VMEM((span, per_device), particles.dtype)] * len(quarters)
     scratch = [
-        pltpu.VMEM((STEPS // 2, per_device, width), particles.dtype),
-        pltpu.SemaphoreType.DMA((STEPS // 2,)),
+        pltpu.VMEM((steps, per_device, width), particles.dtype),
+        pltpu.SemaphoreType.DMA((steps,)),
     ]
-    if phase == 0:
-        shapes += [jax.ShapeDtypeStruct((total // 32, per_device), jnp.int32)] + sums
+    if first:
+        shapes = [jax.ShapeDtypeStruct((total // 32, per_device), jnp.int32)] + sums
         rest_specs = [in_vmem()]
-    else:
+    elif last:
         rows = STATE_ROWS + rest[2].shape[0]
-        shapes.append(jax.ShapeDtypeStruct((rows, per_device), jnp.float32))
+        shapes = [jax.ShapeDtypeStruct((rows, per_device), jnp.float32)]
+        rest_specs = [in_vmem(), in_vmem(), in_smem(), in_vmem(), in_vmem()]
+    else:
+        shapes = sums
+        rest_specs = [in_vmem(), in_vmem()]
+    if last:
         scratch = [pltpu.VMEM(array.shape, array.dtype) for array in sums] + scratch
-        rest_specs = [in_vmem(), in_vmem(), in_smem(), in_vmem(), in_vmem()]
     return pl.pallas_call(
-        functools.partial(own_kernel, phase),
-        grid=(1,),
-        in_specs=[
-            in_smem(),
-            pl.BlockSpec((1, freqs // 2), lambda j: (0, phase)),
-            pl.BlockSpec((height, freqs // 2), lambda j: (0, phase)),
-            pl.BlockSpec(memory_space=pl.ANY),
-            *rest_specs,
-        ],
-        out_specs=[in_vmem()] * len(shapes),
-        out_shape=shapes,
+        functools.partial(own_kernel, first, last, quarters[0] * span),
+        in_specs=[in_smem(), in_vmem(), in_vmem(), pl.BlockSpec(memory_space=pl.ANY)] + rest_specs,
+        out_specs=[in_vmem()] * (len(shapes) + len(turned)),
+        out_shape=shapes + turned,
         scratch_shapes=scratch,
         compiler_params=pltpu.CompilerParams(vmem_limit_bytes=VMEM_LIMIT),
         cost_estimate=pl.CostEstimate(
@@ -234,20 +236,16 @@
     )
 
 
-def near_copies(far_ref, near, arrived):
-    blocks, _, width = near.shape
-    return [
-        pltpu.make_async_copy(
-            far_ref.at[:, block * width : (block + 1) * width], near.at[block], arrived.at[block]
-        )
-        for block in range(blocks)
-    ]
-
-
-def class_sums(state, core, near, copies, loglik_ref, mine_ref, theirs_ref):
+def near_copy(block, far_ref, near, arrived):
+    width = near.shape[2]
+    columns = pl.ds(pl.multiple_of(block * width, width), width)
+    return pltpu.make_async_copy(far_ref.at[:, columns], near.at[block], arrived.at[block])
+
+
+def class_sums(state, core, far_ref, near, arrived, loglik_ref, mine_ref, theirs_ref):
     top, total, _, weights = state
     loglik_ref[...] = top + jnp.log(total)
-    per_owner = mine_ref.shape[1]
+    blocks, per_owner = mine_ref.shape[:2]
     width = near.shape[2]
     weights = weights / jnp.sum(weights, axis=0, keepdims=True)
     turned = jnp.concatenate([weights[per_owner:], weights[:per_owner]], axis=0)
@@ -256,8 +254,10 @@
     totals = jnp.broadcast_to(
         jnp.sum(weights, axis=1, keepdims=True), (weights.shape[0], LANES)
     )
-    for block, copy in enumerate(copies):
-        copy.wait()
+
+    @pl.loop(0, blocks)
+    def _(block):
+        near_copy(block, far_ref, near, arrived).wait()
         sums = jnp.dot(rounded, near[block], preferred_element_type=jnp.float32)
         mine_ref[block, :, :width] = sums[:per_owner]
         theirs_ref[block, :, :width] = sums[per_owner:]
@@ -265,7 +265,7 @@
         theirs_ref[block, :, width:] = totals[per_owner:]
 
 
-def ring_kernel(phase, ends, sources, where_ref, noise_ref, part_ref, *rest):
+def ring_kernel(phase, ends, sources, where_ref, noise_ref, low_ref, high_ref, *rest):
     row_refs, rest = rest[: 2 * len(sources)], rest[2 * len(sources) :]
     if phase == 0:
         acc, energy = rest
@@ -275,41 +275,37 @@
         acc_in, energy_in, logs_ref, words_ref, state_ref, *rest = rest
         if ends:
             far_ref, loglik_ref, mine_ref, theirs_ref, acc, energy, near, arrived = rest
-            copies = near_copies(far_ref, near, arrived)
-            for copy in copies:
-                copy.start()
+            for block in range(near.shape[0]):
+                near_copy(block, far_ref, near, arrived).start()
         else:
             out_ref, acc, energy = rest
         acc[...] = acc_in[...]
         energy[...] = energy_in[...]
-    half = part_ref.shape[0]
-    span = half // 2 if ends else half
+    quarter = low_ref.shape[0]
     core = where_ref[1]
-    if ends:
-        pieces = [(row_refs[:1], core * span), (row_refs[1:], (1 - core) * span)]
-    else:
-        pieces = [(row_refs, 0)]
-    for refs, start in pieces:
-
-        def add(step):
-            here = pl.ds(pl.multiple_of(step * WIDTH, WIDTH), WIDTH)
-            there = pl.ds(pl.multiple_of(start + step * WIDTH, WIDTH), WIDTH)
-            columns = pl.ds(pl.multiple_of(phase * half + start + step * WIDTH, WIDTH), WIDTH)
-            rows = jnp.concatenate([ref[:, here] for ref in refs], axis=0)
-            weighted = weigh(rows, noise_ref[:, columns], energy)
-            acc[...] += jnp.dot(
-                weighted, part_ref[there, :], preferred_element_type=jnp.float32
-            )
-
-        if ends and phase == 1:
-            pl.loop(0, span // WIDTH)(add)
-        else:
-            for step in range(span // WIDTH):
-                add(step)
+
+    def add(refs, part_ref, at, step, start):
+        here = pl.ds(pl.multiple_of(start + step * WIDTH, WIDTH), WIDTH)
+        there = pl.ds(pl.multiple_of(step * WIDTH, WIDTH), WIDTH)
+        columns = pl.ds((2 * phase + at) * quarter + step * WIDTH, WIDTH)
+        rows = jnp.concatenate([ref[:, here] for ref in refs], axis=0)
+        weighted = weigh(rows, noise_ref[:, columns], energy)
+        acc[...] += jnp.dot(weighted, part_ref[there, :], preferred_element_type=jnp.float32)
+
+    for at, part_ref in enumerate((low_ref, high_ref)):
+        for step in range(quarter // WIDTH):
+            if ends:
+                for own, ref in ((True, row_refs[0]), (False, row_refs[1])):
+                    pl.when((core == at) == own)(
+                        functools.partial(add, [ref], part_ref, at, step, 0)
+                    )
+            else:
+                add(row_refs, part_ref, at, step, at * quarter)
 
     if phase == 0:
         return
     height = row_refs[0].shape[0]
+    span = quarter if ends else 2 * quarter
     tags = [ref[:, span:].astype(jnp.float32) for ref in row_refs]
     tags = jnp.where(core == 0, tags[1], tags[0]) if ends else jnp.concatenate(tags, axis=0)
     found = []
@@ -329,15 +325,15 @@
     hit = jnp.concatenate([picked_rows(words_ref, source, height) for source in found], axis=0)
     state = add_rows(tags, hit, logs_ref, get_state(state_ref), acc, energy)
     if ends:
-        class_sums(state, core, near, copies, loglik_ref, mine_ref, theirs_ref)
+        class_sums(state, core, far_ref, near, arrived, loglik_ref, mine_ref, theirs_ref)
     else:
         put_state(state, out_ref)
 
 
 def ring_scores(phase, sources, where, noise, turned, arrays, rest, blocks=0, owners=0):
     ends = blocks > 0
-    half, per_device = turned.shape
-    freqs = 2 * half
+    quarter, per_device = turned[0].shape
+    freqs = 4 * quarter
     rows = arrays[0].shape[0] * (1 if ends else len(arrays))
     sums = [
         jax.ShapeDtypeStruct((rows, per_device), jnp.float32),
@@ -356,7 +352,7 @@
             piece = jax.ShapeDtypeStruct((blocks, per_owner, width + LANES), jnp.float32)
             shapes = [jax.ShapeDtypeStruct((1, per_device), jnp.float32), piece, piece]
             scratch += [
-                pltpu.VMEM((blocks, per_device, width), turned.dtype),
+                pltpu.VMEM((blocks, per_device, width), turned[0].dtype),
                 pltpu.SemaphoreType.DMA((blocks,)),
             ]
             rest_specs.append(pl.BlockSpec(memory_space=pl.ANY))
@@ -366,7 +362,7 @@
             shapes = [jax.ShapeDtypeStruct(state.shape, jnp.float32)]
     return pl.pallas_call(
         functools.partial(ring_kernel, phase, ends, sources),
-        in_specs=[in_smem()] + [in_vmem()] * (2 + len(arrays)) + rest_specs,
+        in_specs=[in_smem()] + [in_vmem()] * (3 + len(arrays)) + rest_specs,
         out_specs=[in_vmem()] * len(shapes),
         out_shape=shapes,
         scratch_shapes=scratch,
@@ -379,7 +375,7 @@
     )(
         where,
         noise,
-        pltpu.with_memory_space_constraint(turned, pltpu.VMEM),
+        *(pltpu.with_memory_space_constraint(part, pltpu.VMEM) for part in turned),
         *arrays,
         *rest,
     )
@@ -423,15 +419,18 @@
     cut = freqs // 4
     where, cut_at = lax.optimization_barrier((where, core.astype(jnp.uint32) * cut))
     picks = pltpu.with_memory_space_constraint(significant, pltpu.HBM)
-    first, words, *sums = own_scores(
-        0, where, noise, templates, particles, (picks,), blocks * templates.shape[0]
-    )
-    second, state = own_scores(
-        1, where, noise, templates, particles, (*sums, logs, tags, words)
-    )
-    turned = (first, second)
+    own = functools.partial(
+        own_scores, where=where, noise=noise, templates=templates, particles=particles
+    )
+    words, *sums, low, high = own([0, 1], rest=(picks,), total=blocks * templates.shape[0])
+    turned = [(low, high)]
+    gates = [sums]
+    *sums, low = own([2], rest=tuple(sums))
+    gates.append(sums)
+    state, high = own([3], rest=(*sums, logs, tags, words))
+    turned.append((low, high))
+    gates.append(state)
     last = blocks // 2
-    gates = [sums, state]
     pairs, tables = ([], []), []
     for distance in range(1, last + 1):
         ends = distance == last
@@ -451,7 +450,8 @@
                     (message.shape[0], message.shape[1] - cut),
                 )
             own = lax.ppermute(message, ("blk", "cls"), ring)
-            own, _ = lax.optimization_barrier((own, gates[len(gates) - 2]))
+            gate = phase if distance == 1 else len(gates) - (3 if distance == 2 else 2)
+            own, _ = lax.optimization_barrier((own, gates[gate]))
             arrived.append(own)
             pairs[phase].extend((own, lax.ppermute(own, "cls", swap)))
             rest = () if phase == 0 else (*sums, logs, words, state)

time: 74.9 us -> 74.4 us (level)
  waiting for transfers between devices: 15.9 us -> 12 us
  Pallas kernels: 37.1 us -> 40.2 us
    ppermute x8, waiting for transfers between devices: 6.38 us -> 2.28 us  [body(): own = lax.ppermute(message, ('blk', 'cls'), ring)]
    pallas_call x2 -> x3, Pallas kernels: 13.2 us -> 16 us  [own_scores(): pl.pallas_call(functools.partial(own_kernel, first, last, quarters[0] * s...]
    ppermute x8, starting transfers between devices: 0.36 us -> 1.17 us  [body(): pairs[phase].extend((own, lax.ppermute(own, 'cls', swap)))]
  transfers between devices with their start and end apart: 20 -> 20, of which waited for: 8 -> 6; matrix products, arithmetic and copies ran while one was open for 0% -> 0% of each run, Pallas kernels for 38% -> 43%
where the time goes in v8:
time: 74.4 us; the launch traced here: 74.2 us
  Pallas kernels  40.2 us (54%)
  starting transfers between devices  19.8 us (27%)
  waiting for transfers between devices  12 us (16%)
  other arithmetic  0.92 us (1%)
  between operations  0.86 us (1%)
    pallas_call x8, Pallas kernels, ring_scores(): pl.pallas_call(functools.partial(ring_kernel, phase, ends, sources), in_s...  22.9 us
    pallas_call x3, Pallas kernels, own_scores(): pl.pallas_call(functools.partial(own_kernel, first, last, quarters[0] * s...  16 us
    ppermute x8, starting transfers between devices, body(): own = lax.ppermute(message, ('blk', 'cls'), ring)  13.4 us
    ppermute x3, waiting for transfers between devices, scatter_sum(): pieces = keep + lax.ppermute(send, 'blk', swaps)  8.68 us
    ppermute x3, starting transfers between devices, scatter_sum(): pieces = keep + lax.ppermute(send, 'blk', swaps)  4.67 us
    ppermute x8, waiting for transfers between devices, body(): own = lax.ppermute(message, ('blk', 'cls'), ring)  2.28 us
  transfers between devices with their start and end apart: 20, of which 6 were waited for; matrix products, arithmetic and copies ran while one was open for 0% of the time, Pallas kernels for 43%

profile of v8, /device:TPU:0, one launch (start us, length us, event | category | flops | bytes accessed | tf_op | source)
XLA Modules:
  0.0 74.2 jit_solution(15203480555762144069)
XLA Ops:
  0.6 1.2 %shard_map.80 = (bf16[64,4096]{1,0:T(8,128)(2,1)S(1)}, bf16[64,4224]{1,0:T(8,128)(2,1)S(1)}) custom-call(s32[1,64]{1,0:T(1,128)} %bitcast.28, bf16[64,8192]{1,0:T(8,128)(2,1)} %rows_ref.1), custom_call_target="tpu_custom_call" | custom-call | tf_op jit(solution)/shard_map/pallas_call | solution.py:44
  1.9 3.1 %collective-permute-start.2 = (bf16[64,4096]{1,0:T(8,128)(2,1)S(1)}, bf16[64,4096]{1,0:T(8,128)(2,1)S(1)}, u32[]{:S(2)}, u32[]{:S(2)}) collective-permute-start(bf16[64,4096]{1,0:T(8,128)(2,1)S(1)} %get-tuple-element.47), channel_id=1, source_target_pairs={{0,4},{4,8},{8,12},{12,14},{14,10},{10,6},{6,2},{2,0},{5,1},{9,5},... | collective-permute-start | bytes 1572872 | tf_op jit(solution)/shard_map/ppermute | solution.py:452
  5.0 1.6 %collective-permute-start = (bf16[64,4224]{1,0:T(8,128)(2,1)S(1)}, bf16[64,4224]{1,0:T(8,128)(2,1)S(1)}, u32[]{:S(2)}, u32[]{:S(2)}) collective-permute-start(bf16[64,4224]{1,0:T(8,128)(2,1)S(1)} %get-tuple-element.43), channel_id=1, source_target_pairs={{0,4},{4,8},{8,12},{12,14},{14,10},{10,6},{6,2},{2,0},{5,1},{9,5},... | collective-permute-start | bytes 1622024 | tf_op jit(solution)/shard_map/ppermute | solution.py:452
  6.6 6.6 %shard_map.77 = (s32[16,1024]{1,0:T(8,128)S(1)}, f32[64,1024]{1,0:T(8,128)S(1)}, f32[64,128]{1,0:T(8,128)S(1)}, bf16[2048,1024]{1,0:T(8,128)(2,1)S(1)}, bf16[2048,1024]{1,0:T(8,128)(2,1)S(1)}) custom-call(s32[2]{0:T(128)S(1)} %pad_add_fusion.where_ref, f32[1,8192]{1,0:T(1,128)} %bitcast.17, bf16[64,8192]{1,0:T(8,128)(2,1)} %rows_ref.1, ...), custom_call_target="tpu_custom_call" | custom-call | flops 2147483648 | bytes 8388608 | tf_op jit(solution)/shard_map/pallas_call | solution.py:220
  13.2 1.6 %collective-permute-start.6 = (bf16[64,4096]{1,0:T(8,128)(2,1)S(1)}, bf16[64,4096]{1,0:T(8,128)(2,1)S(1)}, u32[]{:S(2)}, u32[]{:S(2)}) collective-permute-start(bf16[64,4096]{1,0:T(8,128)(2,1)S(1)} %collective-permute-done.2.rest_0_), channel_id=1, source_target_pairs={{0,4},{4,8},{8,12},{12,14},{14,10},{10,6},{6,2},{2,0},{5,1},{9,5},... | collective-permute-start | bytes 1572872 | tf_op jit(solution)/shard_map/ppermute | solution.py:452
  14.8 4.5 %shard_map.78 = (f32[64,1024]{1,0:T(8,128)S(1)}, f32[64,128]{1,0:T(8,128)S(1)}, bf16[2048,1024]{1,0:T(8,128)(2,1)S(1)}) custom-call(s32[2]{0:T(128)S(1)} %pad_add_fusion.where_ref, f32[1,8192]{1,0:T(1,128)} %bitcast.18, bf16[64,8192]{1,0:T(8,128)(2,1)} %rows_ref.1, bf16[1024,8192]{1,0:T(8,128)(2,1)} %rest_7_.1, f32[64,1024]{1,0:T(8,128)S(1)} %get-tuple-element.36.rest_0_, ...), custom_call_target="tpu_custom_call" | custom-call | flops 2147483648 | bytes 8388608 | tf_op jit(solution)/shard_map/pallas_call | solution.py:220
  20.0 1.5 %collective-permute-start.1 = (bf16[64,4224]{1,0:T(8,128)(2,1)S(1)}, bf16[64,4224]{1,0:T(8,128)(2,1)S(1)}, u32[]{:S(2)}, u32[]{:S(2)}) collective-permute-start(bf16[64,4224]{1,0:T(8,128)(2,1)S(1)} %collective-permute-done.rest_0_), channel_id=1, source_target_pairs={{0,4},{4,8},{8,12},{12,14},{14,10},{10,6},{6,2},{2,0},{5,1},{9,5},... | collective-permute-start | bytes 1622024 | tf_op jit(solution)/shard_map/ppermute | solution.py:452
  21.5 5.0 %shard_map.79 = (f32[16,1024]{1,0:T(8,128)S(1)}, bf16[2048,1024]{1,0:T(8,128)(2,1)S(1)}) custom-call(s32[2]{0:T(128)S(1)} %pad_add_fusion.where_ref, f32[1,8192]{1,0:T(1,128)} %bitcast.19, bf16[64,8192]{1,0:T(8,128)(2,1)} %rows_ref.1, bf16[1024,8192]{1,0:T(8,128)(2,1)} %rest_7_.1, f32[64,1024]{1,0:T(8,128)S(1)} %get-tuple-element.39.rest_0_, ...), custom_call_target="tpu_custom_call" | custom-call | flops 2147483648 | bytes 8388608 | tf_op jit(solution)/shard_map/pallas_call | solution.py:220
  27.6 2.0 %shard_map.81 = (f32[128,1024]{1,0:T(8,128)S(1)}, f32[128,128]{1,0:T(8,128)S(1)}) custom-call(s32[2]{0:T(128)S(1)} %pad_add_fusion.where_ref, f32[1,8192]{1,0:T(1,128)S(1)} %bitcast.20, bf16[2048,1024]{1,0:T(8,128)(2,1)S(1)} %get-tuple-element.45.low_ref, bf16[2048,1024]{1,0:T(8,128)(2,1)S(1)} %get-tuple-element.46.high_ref, ...), custom_call_target="tpu_custom_call" | custom-call | flops 2147483648 | bytes 8388608 | tf_op jit(solution)/shard_map/pallas_call | solution.py:363
  29.6 1.7 %collective-permute-start.4 = (bf16[64,4224]{1,0:T(8,128)(2,1)S(1)}, bf16[64,4224]{1,0:T(8,128)(2,1)S(1)}, u32[]{:S(2)}, u32[]{:S(2)}) collective-permute-start(bf16[64,4224]{1,0:T(8,128)(2,1)S(1)} %collective-permute-done.1.rest_0_), channel_id=1, source_target_pairs={{0,4},{4,8},{8,12},{12,14},{14,10},{10,6},{6,2},{2,0},{5,1},{9,5},... | collective-permute-start | bytes 1622024 | tf_op jit(solution)/shard_map/ppermute | solution.py:452
  31.4 2.4 %shard_map.83.rest_6_ = f32[16,1024]{1,0:T(8,128)S(1)} custom-call(s32[2]{0:T(128)S(1)} %pad_add_fusion.where_ref, f32[1,8192]{1,0:T(1,128)S(1)} %bitcast.21, bf16[2048,1024]{1,0:T(8,128)(2,1)S(1)} %get-tuple-element.38.low_ref, bf16[2048,1024]{1,0:T(8,128)(2,1)S(1)} %get-tuple-element.42.high_ref, bf16[64,4224]{1,0:T(8,128)(2,1)S(1)} %collective-permute-done.rest_0_, ...), custom_call_target="tpu_custom_call" | custom-call | flops 2147483648 | bytes 8388608 | tf_op jit(solution)/shard_map/pallas_call | solution.py:363
  33.8 2.0 %shard_map.82 = (f32[128,1024]{1,0:T(8,128)S(1)}, f32[128,128]{1,0:T(8,128)S(1)}) custom-call(s32[2]{0:T(128)S(1)} %pad_add_fusion.where_ref, f32[1,8192]{1,0:T(1,128)S(1)} %bitcast.22, bf16[2048,1024]{1,0:T(8,128)(2,1)S(1)} %get-tuple-element.45.low_ref, bf16[2048,1024]{1,0:T(8,128)(2,1)S(1)} %get-tuple-element.46.high_ref, ...), custom_call_target="tpu_custom_call" | custom-call | flops 2147483648 | bytes 8388608 | tf_op jit(solution)/shard_map/pallas_call | solution.py:363
  36.2 1.5 %collective-permute-start.14 = (bf16[64,2048]{1,0:T(8,128)(2,1)S(1)}, bf16[64,2048]{1,0:T(8,128)(2,1)S(1)}, u32[]{:S(2)}, u32[]{:S(2)}) collective-permute-start(bf16[64,2048]{1,0:T(8,128)(2,1)S(1)} %constant_dynamic-slice_fusion.1), channel_id=1, source_target_pairs={{0,4},{4,8},{8,12},{12,14},{14,10},{10,6},{6,2},{2,0},{5,1},{9,5},... | collective-permute-start | bytes 786440 | tf_op jit(solution)/shard_map/ppermute | solution.py:452
  37.6 2.4 %shard_map.84.rest_6_ = f32[16,1024]{1,0:T(8,128)S(1)} custom-call(s32[2]{0:T(128)S(1)} %pad_add_fusion.where_ref, f32[1,8192]{1,0:T(1,128)S(1)} %bitcast.23, bf16[2048,1024]{1,0:T(8,128)(2,1)S(1)} %get-tuple-element.38.low_ref, bf16[2048,1024]{1,0:T(8,128)(2,1)S(1)} %get-tuple-element.42.high_ref, bf16[64,4224]{1,0:T(8,128)(2,1)S(1)} %collective-permute-done.1.rest_0_, ...), custom_call_target="tpu_custom_call" | custom-call | flops 2147483648 | bytes 8388608 | tf_op jit(solution)/shard_map/pallas_call | solution.py:363
  40.1 1.5 %collective-permute-done.4.rest_0_ = bf16[64,4224]{1,0:T(8,128)(2,1)S(1)} collective-permute-done((bf16[64,4224]{1,0:T(8,128)(2,1)S(1)}, bf16[64,4224]{1,0:T(8,128)(2,1)S(1)}, u32[]{:S(2)}, u32[]{:S(2)}) %collective-permute-start.4) | collective-permute-done | bytes 540704 | tf_op jit(solution)/shard_map/ppermute | solution.py:452
  41.7 1.4 %collective-permute-start.9 = (bf16[64,2176]{1,0:T(8,128)(2,1)S(1)}, bf16[64,2176]{1,0:T(8,128)(2,1)S(1)}, u32[]{:S(2)}, u32[]{:S(2)}) collective-permute-start(bf16[64,2176]{1,0:T(8,128)(2,1)S(1)} %constant_dynamic-slice_fusion.2), channel_id=1, source_target_pairs={{0,4},{4,8},{8,12},{12,14},{14,10},{10,6},{6,2},{2,0},{5,1},{9,5},... | collective-permute-start | bytes 835592 | tf_op jit(solution)/shard_map/ppermute | solution.py:452
  43.1 2.0 %shard_map.85 = (f32[128,1024]{1,0:T(8,128)S(1)}, f32[128,128]{1,0:T(8,128)S(1)}) custom-call(s32[2]{0:T(128)S(1)} %pad_add_fusion.where_ref, f32[1,8192]{1,0:T(1,128)S(1)} %bitcast.24, bf16[2048,1024]{1,0:T(8,128)(2,1)S(1)} %get-tuple-element.45.low_ref, bf16[2048,1024]{1,0:T(8,128)(2,1)S(1)} %get-tuple-element.46.high_ref, ...), custom_call_target="tpu_custom_call" | custom-call | flops 2147483648 | bytes 8388608 | tf_op jit(solution)/shard_map/pallas_call | solution.py:363
  45.4 2.4 %shard_map.86.rest_6_ = f32[16,1024]{1,0:T(8,128)S(1)} custom-call(s32[2]{0:T(128)S(1)} %pad_add_fusion.where_ref, f32[1,8192]{1,0:T(1,128)S(1)} %bitcast.25, bf16[2048,1024]{1,0:T(8,128)(2,1)S(1)} %get-tuple-element.38.low_ref, bf16[2048,1024]{1,0:T(8,128)(2,1)S(1)} %get-tuple-element.42.high_ref, bf16[64,4224]{1,0:T(8,128)(2,1)S(1)} %collective-permute-done.4.rest_0_, ...), custom_call_target="tpu_custom_call" | custom-call | flops 2147483648 | bytes 8388608 | tf_op jit(solution)/shard_map/pallas_call | solution.py:363
  48.5 2.6 %shard_map.87 = (f32[64,1024]{1,0:T(8,128)S(1)}, f32[64,128]{1,0:T(8,128)S(1)}) custom-call(s32[2]{0:T(128)S(1)} %pad_add_fusion.where_ref, f32[1,8192]{1,0:T(1,128)S(1)} %bitcast.26, bf16[2048,1024]{1,0:T(8,128)(2,1)S(1)} %get-tuple-element.45.low_ref, bf16[2048,1024]{1,0:T(8,128)(2,1)S(1)} %get-tuple-element.46.high_ref, ...), custom_call_target="tpu_custom_call" | custom-call | flops 2147483648 | bytes 8388608 | tf_op jit(solution)/shard_map/pallas_call | solution.py:363
  51.1 7.1 %shard_map.88 = (f32[1,1024]{1,0:T(1,128)}, f32[8,4,1152]{2,1,0:T(4,128)S(1)}, f32[8,4,1152]{2,1,0:T(4,128)S(1)}) custom-call(s32[2]{0:T(128)S(1)} %pad_add_fusion.where_ref, f32[1,8192]{1,0:T(1,128)S(1)} %bitcast.27, bf16[2048,1024]{1,0:T(8,128)(2,1)S(1)} %get-tuple-element.38.low_ref, bf16[2048,1024]{1,0:T(8,128)(2,1)S(1)} %get-tuple-element.42.high_ref, ...), custom_call_target="tpu_custom_call" | custom-call | flops 2147483648 | bytes 8388608 | tf_op jit(solution)/shard_map/pallas_call | solution.py:363
  61.1 3.4 %collective-permute-done.17 = f32[4,4,1152]{2,1,0:T(4,128)S(1)} collective-permute-done((f32[4,4,1152]{2,1,0:T(4,128)S(1)}, f32[4,4,1152]{2,1,0:T(4,128)S(1)}, u32[]{:S(2)}, u32[]{:S(2)}) %collective-permute-start.17) | collective-permute-done | bytes 73760 | tf_op jit(solution)/shard_map/ppermute | solution.py:397
  65.8 2.8 %collective-permute-done.18 = f32[2,4,1152]{2,1,0:T(4,128)S(1)} collective-permute-done((f32[2,4,1152]{2,1,0:T(4,128)S(1)}, f32[2,4,1152]{2,1,0:T(4,128)S(1)}, u32[]{:S(2)}, u32[]{:S(2)}) %collective-permute-start.18) | collective-permute-done | bytes 36896 | tf_op jit(solution)/shard_map/ppermute | solution.py:397
  68.6 2.2 %collective-permute-start.19 = (f32[1,4,1152]{2,1,0:T(4,128)S(1)}, f32[1,4,1152]{2,1,0:T(4,128)S(1)}, u32[]{:S(2)}, u32[]{:S(2)}) collective-permute-start(f32[1,4,1152]{2,1,0:T(4,128)S(1)} %constant_dynamic-slice_fusion), channel_id=1, source_target_pairs={{0,8},{2,10},{4,12},{6,14},{8,0},{10,2},{12,4},{14,6},{1,9},{3,11}... | collective-permute-start | bytes 55304 | tf_op jit(solution)/shard_map/ppermute | solution.py:397
  70.8 2.5 %collective-permute-done.19 = f32[1,4,1152]{2,1,0:T(4,128)S(1)} collective-permute-done((f32[1,4,1152]{2,1,0:T(4,128)S(1)}, f32[1,4,1152]{2,1,0:T(4,128)S(1)}, u32[]{:S(2)}, u32[]{:S(2)}) %collective-permute-start.19) | collective-permute-done | bytes 18464 | tf_op jit(solution)/shard_map/ppermute | solution.py:397
  (48 shorter events, 8.3 us)
Async XLA Ops:
  1.9 11.3 %collective-permute-start.2 = (bf16[64,4096]{1,0:T(8,128)(2,1)S(1)}, bf16[64,4096]{1,0:T(8,128)(2,1)S(1)}, u32[]{:S(2)}, u32[]{:S(2)}) collective-permute-start(bf16[64,4096]{1,0:T(8,128)(2,1)S(1)} %get-tuple-element.47), channel_id=1, source_target_pairs={{0,4},{4,8},{8,12},{12,14},{14,10},{10,6},{6,2},{2,0},{5,1},{9,5},... | collective-permute-start | bytes 1572872 | tf_op jit(solution)/shard_map/ppermute | solution.py:452
  5.0 14.5 %collective-permute-start = (bf16[64,4224]{1,0:T(8,128)(2,1)S(1)}, bf16[64,4224]{1,0:T(8,128)(2,1)S(1)}, u32[]{:S(2)}, u32[]{:S(2)}) collective-permute-start(bf16[64,4224]{1,0:T(8,128)(2,1)S(1)} %get-tuple-element.43), channel_id=1, source_target_pairs={{0,4},{4,8},{8,12},{12,14},{14,10},{10,6},{6,2},{2,0},{5,1},{9,5},... | collective-permute-start | bytes 1622024 | tf_op jit(solution)/shard_map/ppermute | solution.py:452
  13.2 8.3 %copy-start.2 = (s32[8]{0:T(128)S(1)}, s32[8]{0:T(128)}, u32[]{:S(2)}) copy-start(s32[8]{0:T(128)} %param.10) | copy-start | bytes 100
  13.2 8.3 %copy-start.1 = (s32[64]{0:T(128)S(1)}, s32[64]{0:T(128)}, u32[]{:S(2)}) copy-start(s32[64]{0:T(128)} %param.9) | copy-start | bytes 772
  13.2 13.3 %collective-permute-start.6 = (bf16[64,4096]{1,0:T(8,128)(2,1)S(1)}, bf16[64,4096]{1,0:T(8,128)(2,1)S(1)}, u32[]{:S(2)}, u32[]{:S(2)}) collective-permute-start(bf16[64,4096]{1,0:T(8,128)(2,1)S(1)} %collective-permute-done.2.rest_0_), channel_id=1, source_target_pairs={{0,4},{4,8},{8,12},{12,14},{14,10},{10,6},{6,2},{2,0},{5,1},{9,5},... | collective-permute-start | bytes 1572872 | tf_op jit(solution)/shard_map/ppermute | solution.py:452
  19.4 8.2 %collective-permute-start.3 = (bf16[64,4096]{1,0:T(8,128)(2,1)S(1)}, bf16[64,4096]{1,0:T(8,128)(2,1)S(1)}, u32[]{:S(2)}, u32[]{:S(2)}) collective-permute-start(bf16[64,4096]{1,0:T(8,128)(2,1)S(1)} %collective-permute-done.2.rest_0_), channel_id=1, source_target_pairs={{0,1},{1,0},{2,3},{3,2},{4,5},{5,4},{6,7},{7,6},{8,9},{9,8},{10,11... | collective-permute-start | bytes 1572872 | tf_op jit(solution)/shard_map/ppermute | solution.py:456
  19.5 11.9 %collective-permute-start.8 = (bf16[64,4224]{1,0:T(8,128)(2,1)S(1)}, bf16[64,4224]{1,0:T(8,128)(2,1)S(1)}, u32[]{:S(2)}, u32[]{:S(2)}) collective-permute-start(bf16[64,4224]{1,0:T(8,128)(2,1)S(1)} %collective-permute-done.rest_0_), channel_id=1, source_target_pairs={{0,1},{1,0},{2,3},{3,2},{4,5},{5,4},{6,7},{7,6},{8,9},{9,8},{10,11... | collective-permute-start | bytes 1622024 | tf_op jit(solution)/shard_map/ppermute | solution.py:456
  20.0 9.6 %collective-permute-start.1 = (bf16[64,4224]{1,0:T(8,128)(2,1)S(1)}, bf16[64,4224]{1,0:T(8,128)(2,1)S(1)}, u32[]{:S(2)}, u32[]{:S(2)}) collective-permute-start(bf16[64,4224]{1,0:T(8,128)(2,1)S(1)} %collective-permute-done.rest_0_), channel_id=1, source_target_pairs={{0,4},{4,8},{8,12},{12,14},{14,10},{10,6},{6,2},{2,0},{5,1},{9,5},... | collective-permute-start | bytes 1622024 | tf_op jit(solution)/shard_map/ppermute | solution.py:452
  21.5 6.1 %copy-start = (f32[8192]{0:T(1024)S(1)}, f32[8192]{0:T(1024)}, u32[]{:S(2)}) copy-start(f32[8192]{0:T(1024)} %param.11) | copy-start | bytes 98308
  26.5 7.3 %collective-permute-start.7 = (bf16[64,4096]{1,0:T(8,128)(2,1)S(1)}, bf16[64,4096]{1,0:T(8,128)(2,1)S(1)}, u32[]{:S(2)}, u32[]{:S(2)}) collective-permute-start(bf16[64,4096]{1,0:T(8,128)(2,1)S(1)} %collective-permute-done.6.rest_0_), channel_id=1, source_target_pairs={{0,1},{1,0},{2,3},{3,2},{4,5},{5,4},{6,7},{7,6},{8,9},{9,8},{10,11... | collective-permute-start | bytes 1572872 | tf_op jit(solution)/shard_map/ppermute | solution.py:456
  26.6 9.2 %collective-permute-start.11 = (bf16[64,4096]{1,0:T(8,128)(2,1)S(1)}, bf16[64,4096]{1,0:T(8,128)(2,1)S(1)}, u32[]{:S(2)}, u32[]{:S(2)}) collective-permute-start(bf16[64,4096]{1,0:T(8,128)(2,1)S(1)} %collective-permute-done.6.rest_0_), channel_id=1, source_target_pairs={{0,4},{4,8},{8,12},{12,14},{14,10},{10,6},{6,2},{2,0},{5,1},{9,5},... | collective-permute-start | bytes 1572872 | tf_op jit(solution)/shard_map/ppermute | solution.py:452
  29.6 8.1 %collective-permute-start.5 = (bf16[64,4224]{1,0:T(8,128)(2,1)S(1)}, bf16[64,4224]{1,0:T(8,128)(2,1)S(1)}, u32[]{:S(2)}, u32[]{:S(2)}) collective-permute-start(bf16[64,4224]{1,0:T(8,128)(2,1)S(1)} %collective-permute-done.1.rest_0_), channel_id=1, source_target_pairs={{0,1},{1,0},{2,3},{3,2},{4,5},{5,4},{6,7},{7,6},{8,9},{9,8},{10,11... | collective-permute-start | bytes 1622024 | tf_op jit(solution)/shard_map/ppermute | solution.py:456
  29.6 11.9 %collective-permute-start.4 = (bf16[64,4224]{1,0:T(8,128)(2,1)S(1)}, bf16[64,4224]{1,0:T(8,128)(2,1)S(1)}, u32[]{:S(2)}, u32[]{:S(2)}) collective-permute-start(bf16[64,4224]{1,0:T(8,128)(2,1)S(1)} %collective-permute-done.1.rest_0_), channel_id=1, source_target_pairs={{0,4},{4,8},{8,12},{12,14},{14,10},{10,6},{6,2},{2,0},{5,1},{9,5},... | collective-permute-start | bytes 1622024 | tf_op jit(solution)/shard_map/ppermute | solution.py:452
  35.8 7.3 %collective-permute-start.12 = (bf16[64,4096]{1,0:T(8,128)(2,1)S(1)}, bf16[64,4096]{1,0:T(8,128)(2,1)S(1)}, u32[]{:S(2)}, u32[]{:S(2)}) collective-permute-start(bf16[64,4096]{1,0:T(8,128)(2,1)S(1)} %collective-permute-done.11.rest_0_), channel_id=1, source_target_pairs={{0,1},{1,0},{2,3},{3,2},{4,5},{5,4},{6,7},{7,6},{8,9},{9,8},{10,11... | collective-permute-start | bytes 1572872 | tf_op jit(solution)/shard_map/ppermute | solution.py:456
  36.2 9.0 %collective-permute-start.14 = (bf16[64,2048]{1,0:T(8,128)(2,1)S(1)}, bf16[64,2048]{1,0:T(8,128)(2,1)S(1)}, u32[]{:S(2)}, u32[]{:S(2)}) collective-permute-start(bf16[64,2048]{1,0:T(8,128)(2,1)S(1)} %constant_dynamic-slice_fusion.1), channel_id=1, source_target_pairs={{0,4},{4,8},{8,12},{12,14},{14,10},{10,6},{6,2},{2,0},{5,1},{9,5},... | collective-permute-start | bytes 786440 | tf_op jit(solution)/shard_map/ppermute | solution.py:452
  41.6 3.8 %collective-permute-start.10 = (bf16[64,4224]{1,0:T(8,128)(2,1)S(1)}, bf16[64,4224]{1,0:T(8,128)(2,1)S(1)}, u32[]{:S(2)}, u32[]{:S(2)}) collective-permute-start(bf16[64,4224]{1,0:T(8,128)(2,1)S(1)} %collective-permute-done.4.rest_0_), channel_id=1, source_target_pairs={{0,1},{1,0},{2,3},{3,2},{4,5},{5,4},{6,7},{7,6},{8,9},{9,8},{10,11... | collective-permute-start | bytes 1622024 | tf_op jit(solution)/shard_map/ppermute | solution.py:456
  41.7 6.8 %collective-permute-start.9 = (bf16[64,2176]{1,0:T(8,128)(2,1)S(1)}, bf16[64,2176]{1,0:T(8,128)(2,1)S(1)}, u32[]{:S(2)}, u32[]{:S(2)}) collective-permute-start(bf16[64,2176]{1,0:T(8,128)(2,1)S(1)} %constant_dynamic-slice_fusion.2), channel_id=1, source_target_pairs={{0,4},{4,8},{8,12},{12,14},{14,10},{10,6},{6,2},{2,0},{5,1},{9,5},... | collective-permute-start | bytes 835592 | tf_op jit(solution)/shard_map/ppermute | solution.py:452
  45.1 3.4 %collective-permute-start.15 = (bf16[64,2048]{1,0:T(8,128)(2,1)S(1)}, bf16[64,2048]{1,0:T(8,128)(2,1)S(1)}, u32[]{:S(2)}, u32[]{:S(2)}) collective-permute-start(bf16[64,2048]{1,0:T(8,128)(2,1)S(1)} %collective-permute-done.14.rest_0_), channel_id=1, source_target_pairs={{0,1},{1,0},{2,3},{3,2},{4,5},{5,4},{6,7},{7,6},{8,9},{9,8},{10,11... | collective-permute-start | bytes 786440 | tf_op jit(solution)/shard_map/ppermute | solution.py:456
  48.5 2.6 %collective-permute-start.13 = (bf16[64,2176]{1,0:T(8,128)(2,1)S(1)}, bf16[64,2176]{1,0:T(8,128)(2,1)S(1)}, u32[]{:S(2)}, u32[]{:S(2)}) collective-permute-start(bf16[64,2176]{1,0:T(8,128)(2,1)S(1)} %collective-permute-done.9.rest_0_), channel_id=1, source_target_pairs={{0,1},{1,0},{2,3},{3,2},{4,5},{5,4},{6,7},{7,6},{8,9},{9,8},{10,11... | collective-permute-start | bytes 835592 | tf_op jit(solution)/shard_map/ppermute | solution.py:456
  58.2 1.6 %collective-permute-start.16 = (f32[8,4,1152]{2,1,0:T(4,128)S(1)}, f32[8,4,1152]{2,1,0:T(4,128)S(1)}, u32[]{:S(2)}, u32[]{:S(2)}) collective-permute-start(f32[8,4,1152]{2,1,0:T(4,128)S(1)} %get-tuple-element.67), channel_id=1, source_target_pairs={{0,1},{1,0},{2,3},{3,2},{4,5},{5,4},{6,7},{7,6},{8,9},{9,8},{10,11... | collective-permute-start | bytes 442376 | tf_op jit(solution)/shard_map/ppermute | solution.py:472
  59.9 4.6 %collective-permute-start.17 = (f32[4,4,1152]{2,1,0:T(4,128)S(1)}, f32[4,4,1152]{2,1,0:T(4,128)S(1)}, u32[]{:S(2)}, u32[]{:S(2)}) collective-permute-start(f32[4,4,1152]{2,1,0:T(4,128)S(1)} %dynamic-slice_bitcast_fusion), channel_id=1, source_target_pairs={{0,2},{2,0},{4,6},{6,4},{8,10},{10,8},{12,14},{14,12},{1,3},{3,1},... | collective-permute-start | bytes 221192 | tf_op jit(solution)/shard_map/ppermute | solution.py:397
  64.5 4.0 %collective-permute-start.18 = (f32[2,4,1152]{2,1,0:T(4,128)S(1)}, f32[2,4,1152]{2,1,0:T(4,128)S(1)}, u32[]{:S(2)}, u32[]{:S(2)}) collective-permute-start(f32[2,4,1152]{2,1,0:T(4,128)S(1)} %dynamic-slice_bitcast_fusion.1), channel_id=1, source_target_pairs={{0,4},{2,6},{4,0},{6,2},{8,12},{10,14},{12,8},{14,10},{1,5},{3,7},... | collective-permute-start | bytes 110600 | tf_op jit(solution)/shard_map/ppermute | solution.py:397
  68.6 4.7 %collective-permute-start.19 = (f32[1,4,1152]{2,1,0:T(4,128)S(1)}, f32[1,4,1152]{2,1,0:T(4,128)S(1)}, u32[]{:S(2)}, u32[]{:S(2)}) collective-permute-start(f32[1,4,1152]{2,1,0:T(4,128)S(1)} %constant_dynamic-slice_fusion), channel_id=1, source_target_pairs={{0,8},{2,10},{4,12},{6,14},{8,0},{10,2},{12,4},{14,6},{1,9},{3,11}... | collective-permute-start | bytes 55304 | tf_op jit(solution)/shard_map/ppermute | solution.py:397

commit v9 on v8

v9 whole, which is shorter than its diff:
```python
import functools

import jax
import jax.numpy as jnp
from jax import lax
from jax.experimental import pallas as pl
from jax.experimental.pallas import tpu as pltpu
from jax.sharding import PartitionSpec as P

LOWEST = -1e30
STEPS = 16
WIDTH = 1024
STRIP = 256
LANES = 128
STATE_ROWS = 8
VMEM_LIMIT = 16 * 1024 * 1024
SMALL_LIMIT = 6 * 1024 * 1024


def ring_order(blocks):
    if blocks <= 8:
        return list(range(0, blocks, 2)) + list(range(blocks - 1, 0, -2))
    return list(range(blocks))


def message_kernel(
    tags_ref, noise_ref, sig_ref, rows_ref,
    first_ref, second_ref, near_noise_ref, near_sig_ref, tags, sent,
):
    height, span = first_ref.shape
    copies = [
        pltpu.make_async_copy(rows_ref.at[:, :span], first_ref, sent.at[0]),
        pltpu.make_async_copy(rows_ref.at[:, span:], second_ref.at[:, :span], sent.at[1]),
        pltpu.make_async_copy(tags_ref, tags, sent.at[2]),
        pltpu.make_async_copy(noise_ref, near_noise_ref, sent.at[3]),
        pltpu.make_async_copy(sig_ref, near_sig_ref, sent.at[4]),
    ]
    for copy in copies:
        copy.start()
    copies[2].wait()
    second_ref[:, span:] = tag_rows(tags, height).astype(jnp.bfloat16)
    for copy in copies[:2] + copies[3:]:
        copy.wait()


def make_messages(tags, noise, significant, templates):
    height, freqs = templates.shape
    span = freqs // 2
    return pl.pallas_call(
        message_kernel,
        in_specs=[pl.BlockSpec(memory_space=pl.ANY)] * 4,
        out_specs=[in_vmem()] * 4,
        out_shape=[
            pltpu.VMEM((height, span), jnp.bfloat16),
            pltpu.VMEM((height, span + LANES), jnp.bfloat16),
            pltpu.VMEM(noise.shape, noise.dtype),
            pltpu.VMEM(significant.shape, significant.dtype),
        ],
        scratch_shapes=[pltpu.VMEM(tags.shape, tags.dtype), pltpu.SemaphoreType.DMA((5,))],
        compiler_params=pltpu.CompilerParams(vmem_limit_bytes=SMALL_LIMIT),
    )(
        *(
            pltpu.with_memory_space_constraint(x, pltpu.HBM)
            for x in (tags, noise, significant, templates)
        )
    )


def tag_rows(tags_ref, height):
    row = lax.broadcasted_iota(jnp.int32, (height, height), 0)
    lane = lax.broadcasted_iota(jnp.int32, (height, height), 1)
    spread = jnp.where(row == lane, tags_ref[...].astype(jnp.float32), 0.0)
    return jnp.broadcast_to(jnp.sum(spread, axis=1, keepdims=True), (height, LANES))


def in_smem():
    return pl.BlockSpec(memory_space=pltpu.SMEM)


def in_vmem():
    return pl.BlockSpec(memory_space=pltpu.VMEM)


def weigh(rows, noise, energy):
    widened = rows.astype(jnp.float32)
    product = widened * noise
    square = product * widened
    folded = square[:, :LANES]
    for lane in range(LANES, square.shape[1], LANES):
        folded = folded + square[:, lane : lane + LANES]
    energy[...] += folded
    return product.astype(jnp.bfloat16)


def pick_words(sig_ref, words_ref):
    word = lax.broadcasted_iota(jnp.int32, words_ref.shape, 0)
    words = jnp.zeros(words_ref.shape, jnp.int32)
    for pick in range(sig_ref.shape[0]):
        chosen = sig_ref[pick : pick + 1, :]
        bit = jnp.left_shift(1, jnp.bitwise_and(chosen, 31))
        words = words | jnp.where(jnp.right_shift(chosen, 5) == word, bit, 0)
    words_ref[...] = words


def picked_rows(words_ref, source, height):
    bit = jnp.left_shift(1, lax.broadcasted_iota(jnp.int32, (32, 1), 0))
    rows = []
    for word in range(height // 32):
        rows.append((words_ref[pl.ds(source * (height // 32) + word, 1), :] & bit) != 0)
    return jnp.concatenate(rows, axis=0)


def add_rows(tags, hit, logs_ref, state, acc, energy):
    classes = logs_ref.shape[0]
    prior = jnp.zeros_like(tags[:, :1])
    for tag in range(classes):
        prior = jnp.where(tags[:, :1] == tag, logs_ref[tag], prior)
    bias = prior - 0.5 * jnp.sum(energy[...], axis=1, keepdims=True)
    scores = acc[...] + bias
    old_max, old_sum, old_top, weights = state
    new_max = jnp.maximum(old_max, jnp.max(scores, axis=0, keepdims=True))
    new_sum = old_sum * jnp.exp(old_max - new_max) + jnp.sum(
        jnp.exp(scores - new_max), axis=0, keepdims=True
    )
    new_top = jnp.maximum(
        old_top, jnp.max(jnp.where(hit, scores, LOWEST), axis=0, keepdims=True)
    )
    value = jnp.where(hit, jnp.exp(scores - new_top), 0.0)
    lane = lax.broadcasted_iota(jnp.int32, tags.shape, 1).astype(jnp.float32)
    onehot = jnp.transpose(jnp.where(tags == lane, 1.0, 0.0))[:classes, :].astype(jnp.bfloat16)
    weights = weights * jnp.exp(old_top - new_top)
    left = value
    for _ in range(3):
        piece = left.astype(jnp.bfloat16)
        left = left - piece.astype(jnp.float32)
        weights = weights + jnp.dot(onehot, piece, preferred_element_type=jnp.float32)
    return new_max, new_sum, new_top, weights


def put_state(state, out_ref):
    new_max, new_sum, new_top, weights = state
    out_ref[0:1, :] = new_max
    out_ref[1:2, :] = new_sum
    out_ref[2:3, :] = new_top
    out_ref[3:STATE_ROWS, :] = jnp.zeros_like(out_ref[3:STATE_ROWS, :])
    out_ref[STATE_ROWS:, :] = weights


def get_state(state_ref):
    return state_ref[0:1, :], state_ref[1:2, :], state_ref[2:3, :], state_ref[STATE_ROWS:, :]


def own_kernel(quarters, where_ref, noise_ref, tmpl_ref, far_ref, *rest):
    first, last = quarters[0] == 0, quarters[-1] == 3
    if first:
        sig_ref, words_ref, acc, energy, *turned_refs, next_ref, near, arrived, late = rest
    elif last:
        acc_in, energy_in, logs_ref, tags_ref, words_ref, near, out_ref, *rest = rest
        *turned_refs, acc, energy = rest
    else:
        acc_in, energy_in, near, acc, energy, *turned_refs, next_ref, late = rest
    span, height = turned_refs[0].shape[0], tmpl_ref.shape[0]
    steps, _, width = near.shape
    low = quarters[0] * span

    def copy(step):
        columns = pl.ds(pl.multiple_of(low + step * width, width), width)
        return pltpu.make_async_copy(far_ref.at[:, columns], near.at[step], arrived.at[step])

    def following(step):
        columns = pl.ds(low + (steps + step) * width, width)
        return pltpu.make_async_copy(far_ref.at[:, columns], next_ref.at[step], late.at[step])

    if first:
        for step in range(steps):
            copy(step).start()
    if not last:
        for step in range(next_ref.shape[0]):
            following(step).start()
    if first:
        pick_words(sig_ref, words_ref)
        acc[...] = jnp.zeros_like(acc)
        energy[...] = jnp.zeros_like(energy)
    else:
        acc[...] = acc_in[...]
        energy[...] = energy_in[...]
    for quarter, turned_ref in zip(quarters, turned_refs):

        @pl.loop(0, span // width)
        def _(inner):
            step = (quarter - quarters[0]) * (span // width) + inner
            if first:
                copy(step).wait()
            for strip in range(0, width, STRIP):
                there = pl.ds(pl.multiple_of(inner * width + strip, STRIP), STRIP)
                part = quarter % 2 * span + inner * width + strip
                here = pl.ds(pl.multiple_of(part, STRIP), STRIP)
                columns = pl.ds(pl.multiple_of(low + step * width + strip, STRIP), STRIP)
                weighted = weigh(tmpl_ref[:, here], noise_ref[:, columns], energy)
                turned = jnp.transpose(near[step, :, strip : strip + STRIP])
                turned_ref[there, :] = turned
                acc[...] += jnp.dot(weighted, turned, preferred_element_type=jnp.float32)

    if not last:
        for step in range(next_ref.shape[0]):
            following(step).wait()
        return
    tags = tag_rows(tags_ref, height)
    hit = picked_rows(words_ref, where_ref[0], height)
    lowest = jnp.full((1, acc.shape[1]), LOWEST, jnp.float32)
    none = jnp.zeros((1, acc.shape[1]), jnp.float32)
    weights = jnp.zeros((logs_ref.shape[0], acc.shape[1]), jnp.float32)
    state = (lowest, none, lowest, weights)
    put_state(add_rows(tags, hit, logs_ref, state, acc, energy), out_ref)


def own_scores(quarters, where, noise, particles, templates, rest, total=0):
    per_device, freqs = particles.shape
    height = templates.shape[0]
    width = freqs // STEPS
    span = freqs // 4
    steps = span // width
    first, last = quarters[0] == 0, quarters[-1] == 3
    sums = [
        jax.ShapeDtypeStruct((height, per_device), jnp.float32),
        jax.ShapeDtypeStruct((height, LANES), jnp.float32),
    ]
    turned = [pltpu.VMEM((span, per_device), particles.dtype)] * len(quarters)
    raw = pltpu.VMEM((steps, per_device, width), particles.dtype)
    if first:
        shapes = [jax.ShapeDtypeStruct((total // 32, per_device), jnp.int32)] + sums
        shapes += turned + [raw]
        rest_specs = [in_vmem()]
        scratch = [
            pltpu.VMEM((2 * steps, per_device, width), particles.dtype),
            pltpu.SemaphoreType.DMA((2 * steps,)),
            pltpu.SemaphoreType.DMA((steps,)),
        ]
    elif last:
        rows = STATE_ROWS + rest[2].shape[0]
        shapes = [jax.ShapeDtypeStruct((rows, per_device), jnp.float32)] + turned
        rest_specs = [in_vmem(), in_vmem(), in_smem(), in_vmem(), in_vmem(), in_vmem()]
        scratch = [pltpu.VMEM(array.shape, array.dtype) for array in sums]
    else:
        shapes = sums + turned + [raw]
        rest_specs = [in_vmem()] * 3
        scratch = [pltpu.SemaphoreType.DMA((steps,))]
    if not first:
        rest = (*rest[:-1], pltpu.with_memory_space_constraint(rest[-1], pltpu.VMEM))
    return pl.pallas_call(
        functools.partial(own_kernel, quarters),
        in_specs=[in_smem(), in_vmem(), in_vmem(), pl.BlockSpec(memory_space=pl.ANY)] + rest_specs,
        out_specs=[in_vmem()] * len(shapes),
        out_shape=shapes,
        scratch_shapes=scratch,
        compiler_params=pltpu.CompilerParams(vmem_limit_bytes=VMEM_LIMIT if first else SMALL_LIMIT),
        cost_estimate=pl.CostEstimate(
            flops=2 * 128 * per_device * freqs,
            bytes_accessed=per_device * freqs,
            transcendentals=0,
        ),
    )(where, noise, templates, pltpu.with_memory_space_constraint(particles, pltpu.HBM), *rest)


def near_copies(part, far_ref, near, arrived):
    blocks, _, width = near.shape
    return [
        pltpu.make_async_copy(
            far_ref.at[:, pl.ds((part * blocks + block) * width, width)],
            near.at[block],
            arrived.at[block],
        )
        for block in range(blocks)
    ]


def class_sums(state, core, nears, copies, loglik_ref, mine_ref, theirs_ref):
    top, total, _, weights = state
    loglik_ref[...] = top + jnp.log(total)
    per_owner = mine_ref.shape[1]
    blocks, _, width = nears[0].shape
    weights = weights / jnp.sum(weights, axis=0, keepdims=True)
    turned = jnp.concatenate([weights[per_owner:], weights[:per_owner]], axis=0)
    weights = jnp.where(core == 0, weights, turned)
    rounded = weights.astype(jnp.bfloat16)
    totals = jnp.broadcast_to(
        jnp.sum(weights, axis=1, keepdims=True), (weights.shape[0], LANES)
    )
    for part, near in enumerate(nears):
        if part == len(nears) - 1:
            for copy in copies:
                copy.wait()

        @pl.loop(0, blocks)
        def _(inner):
            block = part * blocks + inner
            sums = jnp.dot(rounded, near[inner], preferred_element_type=jnp.float32)
            mine_ref[block, :, :width] = sums[:per_owner]
            theirs_ref[block, :, :width] = sums[per_owner:]
            mine_ref[block, :, width:] = totals[:per_owner]
            theirs_ref[block, :, width:] = totals[per_owner:]


def ring_kernel(phase, ends, part, sources, where_ref, noise_ref, low_ref, high_ref, *rest):
    row_refs, rest = rest[: 2 * len(sources)], rest[2 * len(sources) :]
    far_ref = near = copies = None
    if part is not None:
        far_ref, *rest = rest
    if phase == 0:
        acc, energy, *rest = rest
    else:
        acc_in, energy_in, logs_ref, words_ref, state_ref, *rest = rest
        if ends:
            *nears, loglik_ref, mine_ref, theirs_ref, acc, energy = rest[:8]
            rest = rest[8:]
        else:
            out_ref, *rest = rest
            if part is not None:
                near, acc, energy, arrived = rest
            else:
                acc, energy = rest
    if part is not None:
        if phase == 0 or ends:
            near, arrived = rest
        copies = near_copies(part, far_ref, near, arrived)
        for copy in copies:
            copy.start()
    if phase == 0:
        acc[...] = jnp.zeros_like(acc)
        energy[...] = jnp.zeros_like(energy)
    else:
        acc[...] = acc_in[...]
        energy[...] = energy_in[...]
    quarter = low_ref.shape[0]
    core = where_ref[1]

    def add(refs, part_ref, at, step, start):
        here = pl.ds(pl.multiple_of(start + step * WIDTH, WIDTH), WIDTH)
        there = pl.ds(pl.multiple_of(step * WIDTH, WIDTH), WIDTH)
        columns = pl.ds((2 * phase + at) * quarter + step * WIDTH, WIDTH)
        rows = jnp.concatenate([ref[:, here] for ref in refs], axis=0)
        weighted = weigh(rows, noise_ref[:, columns], energy)
        acc[...] += jnp.dot(weighted, part_ref[there, :], preferred_element_type=jnp.float32)

    for at, part_ref in enumerate((low_ref, high_ref)):
        for step in range(quarter // WIDTH):
            if ends:
                for own, ref in ((True, row_refs[0]), (False, row_refs[1])):
                    pl.when((core == at) == own)(
                        functools.partial(add, [ref], part_ref, at, step, 0)
                    )
            else:
                add(row_refs, part_ref, at, step, at * quarter)

    if part is not None and not (ends and phase == 1):
        for copy in copies:
            copy.wait()
    if phase == 0:
        return
    height = row_refs[0].shape[0]
    span = quarter if ends else 2 * quarter
    tags = [ref[:, span:].astype(jnp.float32) for ref in row_refs]
    tags = jnp.where(core == 0, tags[1], tags[0]) if ends else jnp.concatenate(tags, axis=0)
    found = []
    for tables in sources:
        for table in tables:
            source = jnp.int32(table[0])
            for block in range(1, len(table)):
                source = jnp.where(where_ref[0] == block, table[block], source)
            found.append(source)
    if ends:
        found = found[:1]
    else:
        for at in range(0, len(found), 2):
            front, back = found[at : at + 2]
            found[at] = jnp.where(core == 0, front, back)
            found[at + 1] = jnp.where(core == 0, back, front)
    hit = jnp.concatenate([picked_rows(words_ref, source, height) for source in found], axis=0)
    state = add_rows(tags, hit, logs_ref, get_state(state_ref), acc, energy)
    if ends:
        class_sums(state, core, [*nears, near], copies, loglik_ref, mine_ref, theirs_ref)
    else:
        put_state(state, out_ref)


def ring_scores(phase, sources, where, noise, turned, arrays, rest, ends, particles, part, shape):
    quarter, per_device = turned[0].shape
    freqs = 4 * quarter
    rows = arrays[0].shape[0] * (1 if ends else len(arrays))
    sums = [
        jax.ShapeDtypeStruct((rows, per_device), jnp.float32),
        jax.ShapeDtypeStruct((rows, LANES), jnp.float32),
    ]
    scratch = [pltpu.VMEM(array.shape, array.dtype) for array in sums]
    blocks = shape[0] // 4
    raw = (blocks, per_device, freqs // shape[0])
    specs, inputs = [], []
    if part is not None:
        specs = [pl.BlockSpec(memory_space=pl.ANY)]
        inputs = [pltpu.with_memory_space_constraint(particles, pltpu.HBM)]
    if phase == 0:
        shapes, scratch = sums, []
    else:
        specs += [in_vmem(), in_vmem(), in_smem(), in_vmem(), in_vmem()]
        if ends:
            piece = jax.ShapeDtypeStruct(shape, jnp.float32)
            shapes = [jax.ShapeDtypeStruct((1, per_device), jnp.float32), piece, piece]
            specs += [in_vmem()] * 3
            nears = [pltpu.with_memory_space_constraint(x, pltpu.VMEM) for x in rest[5:]]
            rest = (*rest[:5], *nears)
        else:
            shapes = [jax.ShapeDtypeStruct(rest[4].shape, jnp.float32)]
    if part is not None:
        if ends and phase == 1:
            scratch.append(pltpu.VMEM(raw, particles.dtype))
        else:
            shapes.append(pltpu.VMEM(raw, particles.dtype))
        scratch.append(pltpu.SemaphoreType.DMA((blocks,)))
    return pl.pallas_call(
        functools.partial(ring_kernel, phase, ends, part, sources),
        in_specs=[in_smem()] + [in_vmem()] * (3 + len(arrays)) + specs,
        out_specs=[in_vmem()] * len(shapes),
        out_shape=shapes,
        scratch_shapes=scratch,
        compiler_params=pltpu.CompilerParams(vmem_limit_bytes=VMEM_LIMIT if ends else SMALL_LIMIT),
        cost_estimate=pl.CostEstimate(
            flops=2 * 128 * per_device * freqs,
            bytes_accessed=per_device * freqs,
            transcendentals=0,
        ),
    )(
        where,
        noise,
        *(pltpu.with_memory_space_constraint(part, pltpu.VMEM) for part in turned),
        *arrays,
        *inputs,
        *rest,
    )


def scatter_sum(pieces, blocks, block_id):
    tail = pieces.shape[1:]
    stride, left = 1, blocks
    while left > 1:
        radix = 4 if stride > 1 and left % 4 == 0 else 2
        digit = lax.rem(lax.div(block_id, jnp.uint32(stride)), jnp.uint32(radix))
        groups = pieces.reshape((-1, radix) + tail)
        total = lax.dynamic_index_in_dim(groups, digit, 1, keepdims=False)
        for change in range(1, radix):
            there = lax.bitwise_xor(digit, jnp.uint32(change))
            send = lax.dynamic_index_in_dim(groups, there, 1, keepdims=False)
            swaps = [(i, i ^ (change * stride)) for i in range(blocks)]
            total = total + lax.ppermute(send, "blk", swaps)
        pieces = total
        stride, left = stride * radix, left // radix
    return pieces[0]


def body(particles, significant, templates, template_class, class_counts, inv_noise):
    per_device, freqs = particles.shape
    classes = class_counts.shape[0]
    blocks = lax.axis_size("blk")
    owners = lax.axis_size("cls")
    order = ring_order(blocks)
    place = [order.index(block) for block in range(blocks)]
    block_id = lax.axis_index("blk")
    core = lax.axis_index("cls")
    ring = [(2 * order[i], 2 * order[(i + 1) % blocks]) for i in range(blocks)]
    ring += [(2 * order[(i + 1) % blocks] + 1, 2 * order[i] + 1) for i in range(blocks)]
    swap = [(i, owners - 1 - i) for i in range(owners)]

    noise = inv_noise[None, :]
    logs = jnp.log(class_counts.astype(jnp.float32))
    tags = template_class[None, :]
    *held, near_noise, picks = make_messages(tags, noise, significant, templates)
    where = jnp.stack([block_id, core])
    cut = freqs // 4
    where, cut_at = lax.optimization_barrier((where, core.astype(jnp.uint32) * cut))
    own = functools.partial(own_scores, where=where, noise=near_noise, particles=particles)
    total = blocks * templates.shape[0]
    words, *sums, low, high, raw = own([0, 1], templates=held[0], rest=(picks,), total=total)
    turned = [(low, high)]
    gates = [sums]
    *sums, low, raw = own([2], templates=held[1], rest=(*sums, raw))
    gates.append(sums)
    state, high = own([3], templates=held[1], rest=(*sums, logs, tags, words, raw))
    turned.append((low, high))
    gates.append(state)
    width = freqs // blocks
    per_owner = classes // owners
    shape = (blocks, per_owner, width + LANES)
    nears = []
    last = blocks // 2
    for distance in range(1, last + 1):
        ends = distance == last
        tables = [
            [
                tuple(order[(place[block] - sign * distance) % blocks] for block in range(blocks))
                for sign in (1, -1)
            ]
        ]
        arrived = []
        for phase in range(2):
            message = held[phase]
            if ends:
                message = lax.dynamic_slice(
                    message,
                    (jnp.uint32(0), cut_at),
                    (message.shape[0], message.shape[1] - cut),
                )
            own = lax.ppermute(message, ("blk", "cls"), ring)
            lag = 3 if distance == 2 else 2
            gate = phase if distance == 1 else len(gates) - lag
            own, _ = lax.optimization_barrier((own, gates[gate]))
            pair = (own, lax.ppermute(own, "cls", swap))
            arrived.append(own)
            rest = (*sums, logs, words, state) if phase else ()
            if ends and phase:
                rest += tuple(nears)
            part = 2 * (distance - last) + phase + 2
            part = part if part >= 0 else None
            sums = ring_scores(
                phase, tables, where, near_noise, turned[phase], pair, rest,
                ends, particles, part, shape,
            )
            gates.append(sums)
            if part is not None and part < 3:
                *sums, near = sums
                nears.append(near)
        held = arrived
        if not ends:
            (state,) = sums

    loglik, mine, theirs = sums
    reduced = mine + lax.ppermute(theirs, "cls", swap)
    total = scatter_sum(reduced, blocks, block_id.astype(jnp.uint32))
    counts = lax.dynamic_slice_in_dim(class_counts, core * per_owner, per_owner, 0)
    class_avg = total[:, :width] / (total[:, width] + counts.astype(jnp.float32))[:, None]
    return loglik[0], class_avg


def solution(mesh):
    placed = (
        P(("grp", "blk", "cls"), None),
        P(None, ("grp", "blk", "cls")),
        P(("grp", "blk"), None),
        P(("grp", "blk")),
        P("grp"),
        P(),
    )
    return jax.shard_map(
        body,
        mesh=mesh,
        in_specs=placed,
        out_specs=(P(("grp", "blk", "cls")), P(("grp", "cls"), "blk")),
        check_vma=False,
    )
```

time: 74.4 us -> 76.7 us (1.031)
  starting transfers between devices: 19.8 us -> 23.1 us
  Pallas kernels: 40.2 us -> 38.6 us
    ppermute x8, starting transfers between devices: 13.4 us -> 16.3 us  [body(): own = lax.ppermute(message, ('blk', 'cls'), ring)]
    pallas_call x11, Pallas kernels: 38.9 us -> 37.3 us  [the longest x8 25.7 us: ring_scores(): pl.pallas_call(functools.partial(ring_kernel, phase, ends, part, sources)...]
    ppermute x8, waiting for transfers between devices: 2.28 us -> 3.68 us  [body(): own = lax.ppermute(message, ('blk', 'cls'), ring)]
    ppermute x11 -> x12, waiting for transfers between devices: 8.7 us -> 7.78 us  [the longest x4 7.76 us: scatter_sum(): total = total + lax.ppermute(send, 'blk', swaps)]
    ppermute x11 -> x12, starting transfers between devices: 5.84 us -> 6.59 us  [the longest x4 5.63 us: scatter_sum(): total = total + lax.ppermute(send, 'blk', swaps)]
  transfers between devices with their start and end apart: 20 -> 21, of which waited for: 6 -> 8; matrix products, arithmetic and copies ran while one was open for 0% -> 0% of each run, Pallas kernels for 43% -> 40%
where the time goes in v9:
time: 76.7 us; the launch traced here: 76.5 us
  Pallas kernels  38.6 us (50%)
  starting transfers between devices  23.1 us (30%)
  waiting for transfers between devices  12.7 us (17%)
  other arithmetic  0.92 us (1%)
  between operations  0.81 us (1%)
    pallas_call x8, Pallas kernels, ring_scores(): pl.pallas_call(functools.partial(ring_kernel, phase, ends, part, sources)...  25.7 us
    ppermute x8, starting transfers between devices, body(): own = lax.ppermute(message, ('blk', 'cls'), ring)  16.3 us
    pallas_call x3, Pallas kernels, own_scores(): pl.pallas_call(functools.partial(own_kernel, quarters), in_specs=[in_smem...  11.7 us
    ppermute x4, waiting for transfers between devices, scatter_sum(): total = total + lax.ppermute(send, 'blk', swaps)  7.76 us
    ppermute x4, starting transfers between devices, scatter_sum(): total = total + lax.ppermute(send, 'blk', swaps)  5.63 us
    ppermute x8, waiting for transfers between devices, body(): own = lax.ppermute(message, ('blk', 'cls'), ring)  3.68 us
  transfers between devices with their start and end apart: 21, of which 8 were waited for; matrix products, arithmetic and copies ran while one was open for 0% of the time, Pallas kernels for 40%

profile of v9, /device:TPU:0, one launch (start us, length us, event | category | flops | bytes accessed | tf_op | source)
XLA Modules:
  0.0 76.5 jit_solution(3877241564525319212)
XLA Ops:
  1.9 3.1 %collective-permute-start.2 = (bf16[64,4096]{1,0:T(8,128)(2,1)S(1)}, bf16[64,4096]{1,0:T(8,128)(2,1)S(1)}, u32[]{:S(2)}, u32[]{:S(2)}) collective-permute-start(bf16[64,4096]{1,0:T(8,128)(2,1)S(1)} %get-tuple-element.46.tmpl_ref), channel_id=1, source_target_pairs={{0,4},{4,8},{8,12},{12,14},{14,10},{10,6},{6,2},{2,0},{5,1},{9,5},... | collective-permute-start | bytes 1572872 | tf_op jit(solution)/shard_map/ppermute | solution.py:511
  5.0 1.6 %collective-permute-start = (bf16[64,4224]{1,0:T(8,128)(2,1)S(1)}, bf16[64,4224]{1,0:T(8,128)(2,1)S(1)}, u32[]{:S(2)}, u32[]{:S(2)}) collective-permute-start(bf16[64,4224]{1,0:T(8,128)(2,1)S(1)} %get-tuple-element.45.tmpl_ref), channel_id=1, source_target_pairs={{0,4},{4,8},{8,12},{12,14},{14,10},{10,6},{6,2},{2,0},{5,1},{9,5},... | collective-permute-start | bytes 1622024 | tf_op jit(solution)/shard_map/ppermute | solution.py:511
  6.6 5.9 %shard_map.78 = (s32[16,1024]{1,0:T(8,128)S(1)}, f32[64,1024]{1,0:T(8,128)S(1)}, f32[64,128]{1,0:T(8,128)S(1)}, bf16[2048,1024]{1,0:T(8,128)(2,1)S(1)}, bf16[204...) custom-call(s32[2]{0:T(128)S(1)} %pad_add_fusion.where_ref, f32[1,8192]{1,0:T(1,128)S(1)} %get-tuple-element.44.noise_ref, ...), custom_call_target="tpu_custom_call" | custom-call | flops 2147483648 | bytes 8388608 | tf_op jit(solution)/shard_map/pallas_call | solution.py:250
  12.5 1.6 %collective-permute-start.6 = (bf16[64,4096]{1,0:T(8,128)(2,1)S(1)}, bf16[64,4096]{1,0:T(8,128)(2,1)S(1)}, u32[]{:S(2)}, u32[]{:S(2)}) collective-permute-start(bf16[64,4096]{1,0:T(8,128)(2,1)S(1)} %collective-permute-done.2.rest_0_), channel_id=1, source_target_pairs={{0,4},{4,8},{8,12},{12,14},{14,10},{10,6},{6,2},{2,0},{5,1},{9,5},... | collective-permute-start | bytes 1572872 | tf_op jit(solution)/shard_map/ppermute | solution.py:511
  14.2 2.8 %shard_map.79 = (f32[64,1024]{1,0:T(8,128)S(1)}, f32[64,128]{1,0:T(8,128)S(1)}, bf16[2048,1024]{1,0:T(8,128)(2,1)S(1)}, bf16[4,1024,512]{2,1,0:T(8,128)(2,1)S(1)}) custom-call(s32[2]{0:T(128)S(1)} %pad_add_fusion.where_ref, f32[1,8192]{1,0:T(1,128)S(1)} %get-tuple-element.44.noise_ref, bf16[64,4224]{1,0:T(8,128)(2,1)S(1)} %get-tuple-element.45.tmpl_ref, ...), custom_call_target="tpu_custom_call" | custom-call | flops 2147483648 | bytes 8388608 | tf_op jit(solution)/shard_map/pallas_call | solution.py:250
  17.9 2.1 %collective-permute-start.1 = (bf16[64,4224]{1,0:T(8,128)(2,1)S(1)}, bf16[64,4224]{1,0:T(8,128)(2,1)S(1)}, u32[]{:S(2)}, u32[]{:S(2)}) collective-permute-start(bf16[64,4224]{1,0:T(8,128)(2,1)S(1)} %collective-permute-done.rest_0_), channel_id=1, source_target_pairs={{0,4},{4,8},{8,12},{12,14},{14,10},{10,6},{6,2},{2,0},{5,1},{9,5},... | collective-permute-start | bytes 1622024 | tf_op jit(solution)/shard_map/ppermute | solution.py:511
  20.0 3.0 %shard_map.80 = (f32[16,1024]{1,0:T(8,128)S(1)}, bf16[2048,1024]{1,0:T(8,128)(2,1)S(1)}) custom-call(s32[2]{0:T(128)S(1)} %pad_add_fusion.where_ref, f32[1,8192]{1,0:T(1,128)S(1)} %get-tuple-element.44.noise_ref, bf16[64,4224]{1,0:T(8,128)(2,1)S(1)} %get-tuple-element.45.tmpl_ref, bf16[1024,8192]{1,0:T(8,128)(2,1)} %rest_2_.7, ...), custom_call_target="tpu_custom_call" | custom-call | flops 2147483648 | bytes 8388608 | tf_op jit(solution)/shard_map/pallas_call | solution.py:250
  23.5 2.1 %collective-permute-start.11 = (bf16[64,4096]{1,0:T(8,128)(2,1)S(1)}, bf16[64,4096]{1,0:T(8,128)(2,1)S(1)}, u32[]{:S(2)}, u32[]{:S(2)}) collective-permute-start(bf16[64,4096]{1,0:T(8,128)(2,1)S(1)} %collective-permute-done.6.rest_0_), channel_id=1, source_target_pairs={{0,4},{4,8},{8,12},{12,14},{14,10},{10,6},{6,2},{2,0},{5,1},{9,5},... | collective-permute-start | bytes 1572872 | tf_op jit(solution)/shard_map/ppermute | solution.py:511
  25.6 2.0 %shard_map.81 = (f32[128,1024]{1,0:T(8,128)S(1)}, f32[128,128]{1,0:T(8,128)S(1)}) custom-call(s32[2]{0:T(128)S(1)} %pad_add_fusion.where_ref, f32[1,8192]{1,0:T(1,128)S(1)} %get-tuple-element.44.noise_ref, bf16[2048,1024]{1,0:T(8,128)(2,1)S(1)} %get-tuple-element.58.low_ref, bf16[2048,1024]{1,0:T(8,128)(2,1)S(1)} %get-tuple-element.59.high_ref, ...), custom_call_target="tpu_custom_call" | custom-call | flops 2147483648 | bytes 8388608 | tf_op jit(solution)/shard_map/pallas_call | solution.py:419
  27.6 1.7 %collective-permute-done.1.rest_0_ = bf16[64,4224]{1,0:T(8,128)(2,1)S(1)} collective-permute-done((bf16[64,4224]{1,0:T(8,128)(2,1)S(1)}, bf16[64,4224]{1,0:T(8,128)(2,1)S(1)}, u32[]{:S(2)}, u32[]{:S(2)}) %collective-permute-start.1) | collective-permute-done | bytes 540704 | tf_op jit(solution)/shard_map/ppermute | solution.py:511
  29.3 2.1 %collective-permute-start.4 = (bf16[64,4224]{1,0:T(8,128)(2,1)S(1)}, bf16[64,4224]{1,0:T(8,128)(2,1)S(1)}, u32[]{:S(2)}, u32[]{:S(2)}) collective-permute-start(bf16[64,4224]{1,0:T(8,128)(2,1)S(1)} %collective-permute-done.1.rest_0_), channel_id=1, source_target_pairs={{0,4},{4,8},{8,12},{12,14},{14,10},{10,6},{6,2},{2,0},{5,1},{9,5},... | collective-permute-start | bytes 1622024 | tf_op jit(solution)/shard_map/ppermute | solution.py:511
  31.4 2.4 %shard_map.83.rest_6_ = f32[16,1024]{1,0:T(8,128)S(1)} custom-call(s32[2]{0:T(128)S(1)} %pad_add_fusion.where_ref, f32[1,8192]{1,0:T(1,128)S(1)} %get-tuple-element.44.noise_ref, bf16[2048,1024]{1,0:T(8,128)(2,1)S(1)} %get-tuple-element.51.low_ref, bf16[2048,1024]{1,0:T(8,128)(2,1)S(1)} %get-tuple-element.56.high_ref, ...), custom_call_target="tpu_custom_call" | custom-call | flops 2147483648 | bytes 8388608 | tf_op jit(solution)/shard_map/pallas_call | solution.py:419
  33.8 2.0 %shard_map.82 = (f32[128,1024]{1,0:T(8,128)S(1)}, f32[128,128]{1,0:T(8,128)S(1)}) custom-call(s32[2]{0:T(128)S(1)} %pad_add_fusion.where_ref, f32[1,8192]{1,0:T(1,128)S(1)} %get-tuple-element.44.noise_ref, bf16[2048,1024]{1,0:T(8,128)(2,1)S(1)} %get-tuple-element.58.low_ref, bf16[2048,1024]{1,0:T(8,128)(2,1)S(1)} %get-tuple-element.59.high_ref, ...), custom_call_target="tpu_custom_call" | custom-call | flops 2147483648 | bytes 8388608 | tf_op jit(solution)/shard_map/pallas_call | solution.py:419
  37.7 2.4 %shard_map.84.rest_7_ = f32[16,1024]{1,0:T(8,128)S(1)} custom-call(s32[2]{0:T(128)S(1)} %pad_add_fusion.where_ref, f32[1,8192]{1,0:T(1,128)S(1)} %get-tuple-element.44.noise_ref, bf16[2048,1024]{1,0:T(8,128)(2,1)S(1)} %get-tuple-element.51.low_ref, bf16[2048,1024]{1,0:T(8,128)(2,1)S(1)} %get-tuple-element.56.high_ref, ...), custom_call_target="tpu_custom_call" | custom-call | flops 2147483648 | bytes 8388608 | tf_op jit(solution)/shard_map/pallas_call | solution.py:419
  40.8 2.3 %collective-permute-start.9 = (bf16[64,2176]{1,0:T(8,128)(2,1)S(1)}, bf16[64,2176]{1,0:T(8,128)(2,1)S(1)}, u32[]{:S(2)}, u32[]{:S(2)}) collective-permute-start(bf16[64,2176]{1,0:T(8,128)(2,1)S(1)} %constant_dynamic-slice_fusion.4), channel_id=1, source_target_pairs={{0,4},{4,8},{8,12},{12,14},{14,10},{10,6},{6,2},{2,0},{5,1},{9,5},... | collective-permute-start | bytes 835592 | tf_op jit(solution)/shard_map/ppermute | solution.py:511
  43.1 3.9 %shard_map.85 = (f32[128,1024]{1,0:T(8,128)S(1)}, f32[128,128]{1,0:T(8,128)S(1)}, bf16[2,1024,1024]{2,1,0:T(8,128)(2,1)S(1)}) custom-call(s32[2]{0:T(128)S(1)} %pad_add_fusion.where_ref, f32[1,8192]{1,0:T(1,128)S(1)} %get-tuple-element.44.noise_ref, bf16[2048,1024]{1,0:T(8,128)(2,1)S(1)} %get-tuple-element.58.low_ref, ...), custom_call_target="tpu_custom_call" | custom-call | flops 2147483648 | bytes 8388608 | tf_op jit(solution)/shard_map/pallas_call | solution.py:419
  47.3 3.5 %shard_map.86 = (f32[16,1024]{1,0:T(8,128)S(1)}, bf16[2,1024,1024]{2,1,0:T(8,128)(2,1)S(1)}) custom-call(s32[2]{0:T(128)S(1)} %pad_add_fusion.where_ref, f32[1,8192]{1,0:T(1,128)S(1)} %get-tuple-element.44.noise_ref, bf16[2048,1024]{1,0:T(8,128)(2,1)S(1)} %get-tuple-element.51.low_ref, bf16[2048,1024]{1,0:T(8,128)(2,1)S(1)} %get-tuple-element.56.high_ref, ...), custom_call_target="tpu_custom_call" | custom-call | flops 2147483648 | bytes 8388608 | tf_op jit(solution)/shard_map/pallas_call | solution.py:419
  51.3 2.8 %shard_map.87 = (f32[64,1024]{1,0:T(8,128)S(1)}, f32[64,128]{1,0:T(8,128)S(1)}, bf16[2,1024,1024]{2,1,0:T(8,128)(2,1)S(1)}) custom-call(s32[2]{0:T(128)S(1)} %pad_add_fusion.where_ref, f32[1,8192]{1,0:T(1,128)S(1)} %get-tuple-element.44.noise_ref, bf16[2048,1024]{1,0:T(8,128)(2,1)S(1)} %get-tuple-element.58.low_ref, ...), custom_call_target="tpu_custom_call" | custom-call | flops 2147483648 | bytes 8388608 | tf_op jit(solution)/shard_map/pallas_call | solution.py:419
  54.1 6.5 %shard_map.88 = (f32[1,1024]{1,0:T(1,128)}, f32[8,4,1152]{2,1,0:T(4,128)S(1)}, f32[8,4,1152]{2,1,0:T(4,128)S(1)}) custom-call(s32[2]{0:T(128)S(1)} %pad_add_fusion.where_ref, f32[1,8192]{1,0:T(1,128)S(1)} %get-tuple-element.44.noise_ref, bf16[2048,1024]{1,0:T(8,128)(2,1)S(1)} %get-tuple-element.51.low_ref, ...), custom_call_target="tpu_custom_call" | custom-call | flops 2147483648 | bytes 8388608 | tf_op jit(solution)/shard_map/pallas_call | solution.py:419
  63.6 3.0 %collective-permute-done.17 = f32[4,4,1152]{2,1,0:T(4,128)S(1)} collective-permute-done((f32[4,4,1152]{2,1,0:T(4,128)S(1)}, f32[4,4,1152]{2,1,0:T(4,128)S(1)}, u32[]{:S(2)}, u32[]{:S(2)}) %collective-permute-start.17) | collective-permute-done | bytes 73760 | tf_op jit(solution)/shard_map/ppermute | solution.py:453
  66.7 1.6 %collective-permute-start.18 = (f32[1,4,1152]{2,1,0:T(4,128)S(1)}, f32[1,4,1152]{2,1,0:T(4,128)S(1)}, u32[]{:S(2)}, u32[]{:S(2)}) collective-permute-start(f32[1,4,1152]{2,1,0:T(4,128)S(1)} %get-tuple-element.84), channel_id=1, source_target_pairs={{0,4},{2,6},{4,0},{6,2},{8,12},{10,14},{12,8},{14,10},{1,5},{3,7},... | collective-permute-start | bytes 55304 | tf_op jit(solution)/shard_map/ppermute | solution.py:453
  68.3 2.5 %collective-permute-start.20 = (f32[1,4,1152]{2,1,0:T(4,128)S(1)}, f32[1,4,1152]{2,1,0:T(4,128)S(1)}, u32[]{:S(2)}, u32[]{:S(2)}) collective-permute-start(f32[1,4,1152]{2,1,0:T(4,128)S(1)} %get-tuple-element.85), channel_id=1, source_target_pairs={{0,12},{2,14},{4,8},{6,10},{8,4},{10,6},{12,0},{14,2},{1,13},{3,15... | collective-permute-start | bytes 55304 | tf_op jit(solution)/shard_map/ppermute | solution.py:453
  70.8 3.0 %collective-permute-done.20 = f32[1,4,1152]{2,1,0:T(4,128)S(1)} collective-permute-done((f32[1,4,1152]{2,1,0:T(4,128)S(1)}, f32[1,4,1152]{2,1,0:T(4,128)S(1)}, u32[]{:S(2)}, u32[]{:S(2)}) %collective-permute-start.20) | collective-permute-done | bytes 18464 | tf_op jit(solution)/shard_map/ppermute | solution.py:453
  73.9 1.8 %collective-permute-done.19 = f32[1,4,1152]{2,1,0:T(4,128)S(1)} collective-permute-done((f32[1,4,1152]{2,1,0:T(4,128)S(1)}, f32[1,4,1152]{2,1,0:T(4,128)S(1)}, u32[]{:S(2)}, u32[]{:S(2)}) %collective-permute-start.19) | collective-permute-done | bytes 18464 | tf_op jit(solution)/shard_map/ppermute | solution.py:453
  (46 shorter events, 10.0 us)
Async XLA Ops:
  1.9 10.6 %collective-permute-start.2 = (bf16[64,4096]{1,0:T(8,128)(2,1)S(1)}, bf16[64,4096]{1,0:T(8,128)(2,1)S(1)}, u32[]{:S(2)}, u32[]{:S(2)}) collective-permute-start(bf16[64,4096]{1,0:T(8,128)(2,1)S(1)} %get-tuple-element.46.tmpl_ref), channel_id=1, source_target_pairs={{0,4},{4,8},{8,12},{12,14},{14,10},{10,6},{6,2},{2,0},{5,1},{9,5},... | collective-permute-start | bytes 1572872 | tf_op jit(solution)/shard_map/ppermute | solution.py:511
  5.0 12.9 %collective-permute-start = (bf16[64,4224]{1,0:T(8,128)(2,1)S(1)}, bf16[64,4224]{1,0:T(8,128)(2,1)S(1)}, u32[]{:S(2)}, u32[]{:S(2)}) collective-permute-start(bf16[64,4224]{1,0:T(8,128)(2,1)S(1)} %get-tuple-element.45.tmpl_ref), channel_id=1, source_target_pairs={{0,4},{4,8},{8,12},{12,14},{14,10},{10,6},{6,2},{2,0},{5,1},{9,5},... | collective-permute-start | bytes 1622024 | tf_op jit(solution)/shard_map/ppermute | solution.py:511
  12.5 10.9 %collective-permute-start.6 = (bf16[64,4096]{1,0:T(8,128)(2,1)S(1)}, bf16[64,4096]{1,0:T(8,128)(2,1)S(1)}, u32[]{:S(2)}, u32[]{:S(2)}) collective-permute-start(bf16[64,4096]{1,0:T(8,128)(2,1)S(1)} %collective-permute-done.2.rest_0_), channel_id=1, source_target_pairs={{0,4},{4,8},{8,12},{12,14},{14,10},{10,6},{6,2},{2,0},{5,1},{9,5},... | collective-permute-start | bytes 1572872 | tf_op jit(solution)/shard_map/ppermute | solution.py:511
  14.2 5.8 %copy-start.1 = (s32[8]{0:T(128)S(1)}, s32[8]{0:T(128)}, u32[]{:S(2)}) copy-start(s32[8]{0:T(128)} %param.10) | copy-start | bytes 100
  14.2 5.8 %copy-start = (s32[64]{0:T(128)S(1)}, s32[64]{0:T(128)}, u32[]{:S(2)}) copy-start(s32[64]{0:T(128)} %param.9) | copy-start | bytes 772
  16.9 8.6 %collective-permute-start.3 = (bf16[64,4096]{1,0:T(8,128)(2,1)S(1)}, bf16[64,4096]{1,0:T(8,128)(2,1)S(1)}, u32[]{:S(2)}, u32[]{:S(2)}) collective-permute-start(bf16[64,4096]{1,0:T(8,128)(2,1)S(1)} %collective-permute-done.2.rest_0_), channel_id=1, source_target_pairs={{0,1},{1,0},{2,3},{3,2},{4,5},{5,4},{6,7},{7,6},{8,9},{9,8},{10,11... | collective-permute-start | bytes 1572872 | tf_op jit(solution)/shard_map/ppermute | solution.py:515
  17.9 13.5 %collective-permute-start.8 = (bf16[64,4224]{1,0:T(8,128)(2,1)S(1)}, bf16[64,4224]{1,0:T(8,128)(2,1)S(1)}, u32[]{:S(2)}, u32[]{:S(2)}) collective-permute-start(bf16[64,4224]{1,0:T(8,128)(2,1)S(1)} %collective-permute-done.rest_0_), channel_id=1, source_target_pairs={{0,1},{1,0},{2,3},{3,2},{4,5},{5,4},{6,7},{7,6},{8,9},{9,8},{10,11... | collective-permute-start | bytes 1622024 | tf_op jit(solution)/shard_map/ppermute | solution.py:515
  17.9 11.4 %collective-permute-start.1 = (bf16[64,4224]{1,0:T(8,128)(2,1)S(1)}, bf16[64,4224]{1,0:T(8,128)(2,1)S(1)}, u32[]{:S(2)}, u32[]{:S(2)}) collective-permute-start(bf16[64,4224]{1,0:T(8,128)(2,1)S(1)} %collective-permute-done.rest_0_), channel_id=1, source_target_pairs={{0,4},{4,8},{8,12},{12,14},{14,10},{10,6},{6,2},{2,0},{5,1},{9,5},... | collective-permute-start | bytes 1622024 | tf_op jit(solution)/shard_map/ppermute | solution.py:511
  23.5 10.3 %collective-permute-start.7 = (bf16[64,4096]{1,0:T(8,128)(2,1)S(1)}, bf16[64,4096]{1,0:T(8,128)(2,1)S(1)}, u32[]{:S(2)}, u32[]{:S(2)}) collective-permute-start(bf16[64,4096]{1,0:T(8,128)(2,1)S(1)} %collective-permute-done.6.rest_0_), channel_id=1, source_target_pairs={{0,1},{1,0},{2,3},{3,2},{4,5},{5,4},{6,7},{7,6},{8,9},{9,8},{10,11... | collective-permute-start | bytes 1572872 | tf_op jit(solution)/shard_map/ppermute | solution.py:515
  23.5 12.3 %collective-permute-start.11 = (bf16[64,4096]{1,0:T(8,128)(2,1)S(1)}, bf16[64,4096]{1,0:T(8,128)(2,1)S(1)}, u32[]{:S(2)}, u32[]{:S(2)}) collective-permute-start(bf16[64,4096]{1,0:T(8,128)(2,1)S(1)} %collective-permute-done.6.rest_0_), channel_id=1, source_target_pairs={{0,4},{4,8},{8,12},{12,14},{14,10},{10,6},{6,2},{2,0},{5,1},{9,5},... | collective-permute-start | bytes 1572872 | tf_op jit(solution)/shard_map/ppermute | solution.py:511
  29.3 8.4 %collective-permute-start.5 = (bf16[64,4224]{1,0:T(8,128)(2,1)S(1)}, bf16[64,4224]{1,0:T(8,128)(2,1)S(1)}, u32[]{:S(2)}, u32[]{:S(2)}) collective-permute-start(bf16[64,4224]{1,0:T(8,128)(2,1)S(1)} %collective-permute-done.1.rest_0_), channel_id=1, source_target_pairs={{0,1},{1,0},{2,3},{3,2},{4,5},{5,4},{6,7},{7,6},{8,9},{9,8},{10,11... | collective-permute-start | bytes 1622024 | tf_op jit(solution)/shard_map/ppermute | solution.py:515
  29.3 11.4 %collective-permute-start.4 = (bf16[64,4224]{1,0:T(8,128)(2,1)S(1)}, bf16[64,4224]{1,0:T(8,128)(2,1)S(1)}, u32[]{:S(2)}, u32[]{:S(2)}) collective-permute-start(bf16[64,4224]{1,0:T(8,128)(2,1)S(1)} %collective-permute-done.1.rest_0_), channel_id=1, source_target_pairs={{0,4},{4,8},{8,12},{12,14},{14,10},{10,6},{6,2},{2,0},{5,1},{9,5},... | collective-permute-start | bytes 1622024 | tf_op jit(solution)/shard_map/ppermute | solution.py:511
  35.8 7.4 %collective-permute-start.12 = (bf16[64,4096]{1,0:T(8,128)(2,1)S(1)}, bf16[64,4096]{1,0:T(8,128)(2,1)S(1)}, u32[]{:S(2)}, u32[]{:S(2)}) collective-permute-start(bf16[64,4096]{1,0:T(8,128)(2,1)S(1)} %collective-permute-done.11.rest_0_), channel_id=1, source_target_pairs={{0,1},{1,0},{2,3},{3,2},{4,5},{5,4},{6,7},{7,6},{8,9},{9,8},{10,11... | collective-permute-start | bytes 1572872 | tf_op jit(solution)/shard_map/ppermute | solution.py:515
  36.2 10.9 %collective-permute-start.14 = (bf16[64,2048]{1,0:T(8,128)(2,1)S(1)}, bf16[64,2048]{1,0:T(8,128)(2,1)S(1)}, u32[]{:S(2)}, u32[]{:S(2)}) collective-permute-start(bf16[64,2048]{1,0:T(8,128)(2,1)S(1)} %constant_dynamic-slice_fusion.3), channel_id=1, source_target_pairs={{0,4},{4,8},{8,12},{12,14},{14,10},{10,6},{6,2},{2,0},{5,1},{9,5},... | collective-permute-start | bytes 786440 | tf_op jit(solution)/shard_map/ppermute | solution.py:511
  40.7 6.7 %collective-permute-start.10 = (bf16[64,4224]{1,0:T(8,128)(2,1)S(1)}, bf16[64,4224]{1,0:T(8,128)(2,1)S(1)}, u32[]{:S(2)}, u32[]{:S(2)}) collective-permute-start(bf16[64,4224]{1,0:T(8,128)(2,1)S(1)} %collective-permute-done.4.rest_0_), channel_id=1, source_target_pairs={{0,1},{1,0},{2,3},{3,2},{4,5},{5,4},{6,7},{7,6},{8,9},{9,8},{10,11... | collective-permute-start | bytes 1622024 | tf_op jit(solution)/shard_map/ppermute | solution.py:515
  40.8 10.1 %collective-permute-start.9 = (bf16[64,2176]{1,0:T(8,128)(2,1)S(1)}, bf16[64,2176]{1,0:T(8,128)(2,1)S(1)}, u32[]{:S(2)}, u32[]{:S(2)}) collective-permute-start(bf16[64,2176]{1,0:T(8,128)(2,1)S(1)} %constant_dynamic-slice_fusion.4), channel_id=1, source_target_pairs={{0,4},{4,8},{8,12},{12,14},{14,10},{10,6},{6,2},{2,0},{5,1},{9,5},... | collective-permute-start | bytes 835592 | tf_op jit(solution)/shard_map/ppermute | solution.py:511
  47.1 4.2 %collective-permute-start.15 = (bf16[64,2048]{1,0:T(8,128)(2,1)S(1)}, bf16[64,2048]{1,0:T(8,128)(2,1)S(1)}, u32[]{:S(2)}, u32[]{:S(2)}) collective-permute-start(bf16[64,2048]{1,0:T(8,128)(2,1)S(1)} %collective-permute-done.14.rest_0_), channel_id=1, source_target_pairs={{0,1},{1,0},{2,3},{3,2},{4,5},{5,4},{6,7},{7,6},{8,9},{9,8},{10,11... | collective-permute-start | bytes 786440 | tf_op jit(solution)/shard_map/ppermute | solution.py:515
  50.9 3.2 %collective-permute-start.13 = (bf16[64,2176]{1,0:T(8,128)(2,1)S(1)}, bf16[64,2176]{1,0:T(8,128)(2,1)S(1)}, u32[]{:S(2)}, u32[]{:S(2)}) collective-permute-start(bf16[64,2176]{1,0:T(8,128)(2,1)S(1)} %collective-permute-done.9.rest_0_), channel_id=1, source_target_pairs={{0,1},{1,0},{2,3},{3,2},{4,5},{5,4},{6,7},{7,6},{8,9},{9,8},{10,11... | collective-permute-start | bytes 835592 | tf_op jit(solution)/shard_map/ppermute | solution.py:515
  60.7 1.4 %collective-permute-start.16 = (f32[8,4,1152]{2,1,0:T(4,128)S(1)}, f32[8,4,1152]{2,1,0:T(4,128)S(1)}, u32[]{:S(2)}, u32[]{:S(2)}) collective-permute-start(f32[8,4,1152]{2,1,0:T(4,128)S(1)} %get-tuple-element.83), channel_id=1, source_target_pairs={{0,1},{1,0},{2,3},{3,2},{4,5},{5,4},{6,7},{7,6},{8,9},{9,8},{10,11... | collective-permute-start | bytes 442376 | tf_op jit(solution)/shard_map/ppermute | solution.py:535
  62.2 4.4 %collective-permute-start.17 = (f32[4,4,1152]{2,1,0:T(4,128)S(1)}, f32[4,4,1152]{2,1,0:T(4,128)S(1)}, u32[]{:S(2)}, u32[]{:S(2)}) collective-permute-start(f32[4,4,1152]{2,1,0:T(4,128)S(1)} %dynamic-slice_bitcast_fusion), channel_id=1, source_target_pairs={{0,2},{2,0},{4,6},{6,4},{8,10},{10,8},{12,14},{14,12},{1,3},{3,1},... | collective-permute-start | bytes 221192 | tf_op jit(solution)/shard_map/ppermute | solution.py:453
  66.7 4.2 %collective-permute-start.18 = (f32[1,4,1152]{2,1,0:T(4,128)S(1)}, f32[1,4,1152]{2,1,0:T(4,128)S(1)}, u32[]{:S(2)}, u32[]{:S(2)}) collective-permute-start(f32[1,4,1152]{2,1,0:T(4,128)S(1)} %get-tuple-element.84), channel_id=1, source_target_pairs={{0,4},{2,6},{4,0},{6,2},{8,12},{10,14},{12,8},{14,10},{1,5},{3,7},... | collective-permute-start | bytes 55304 | tf_op jit(solution)/shard_map/ppermute | solution.py:453
  68.3 5.6 %collective-permute-start.20 = (f32[1,4,1152]{2,1,0:T(4,128)S(1)}, f32[1,4,1152]{2,1,0:T(4,128)S(1)}, u32[]{:S(2)}, u32[]{:S(2)}) collective-permute-start(f32[1,4,1152]{2,1,0:T(4,128)S(1)} %get-tuple-element.85), channel_id=1, source_target_pairs={{0,12},{2,14},{4,8},{6,10},{8,4},{10,6},{12,0},{14,2},{1,13},{3,15... | collective-permute-start | bytes 55304 | tf_op jit(solution)/shard_map/ppermute | solution.py:453
  70.8 4.9 %collective-permute-start.19 = (f32[1,4,1152]{2,1,0:T(4,128)S(1)}, f32[1,4,1152]{2,1,0:T(4,128)S(1)}, u32[]{:S(2)}, u32[]{:S(2)}) collective-permute-start(f32[1,4,1152]{2,1,0:T(4,128)S(1)} %get-tuple-element.86), channel_id=1, source_target_pairs={{0,8},{2,10},{4,12},{6,14},{8,0},{10,2},{12,4},{14,6},{1,9},{3,11}... | collective-permute-start | bytes 55304 | tf_op jit(solution)/shard_map/ppermute | solution.py:453

commit v10 on v9

--- a/solution.py
+++ b/solution.py
@@ -262,23 +262,21 @@
     )(where, noise, templates, pltpu.with_memory_space_constraint(particles, pltpu.HBM), *rest)
 
 
-def near_copies(part, far_ref, near, arrived):
-    blocks, _, width = near.shape
-    return [
-        pltpu.make_async_copy(
-            far_ref.at[:, pl.ds((part * blocks + block) * width, width)],
-            near.at[block],
-            arrived.at[block],
-        )
-        for block in range(blocks)
-    ]
-
-
-def class_sums(state, core, nears, copies, loglik_ref, mine_ref, theirs_ref):
+def near_copy(block, far_ref, near, arrived):
+    width = near.shape[1]
+    return pltpu.make_async_copy(far_ref.at[:, pl.ds(block * width, width)], near, arrived)
+
+
+def swapped_bits(block, core):
+    low, next_low = lax.rem(block, 2), lax.rem(lax.div(block, 2), 2)
+    return block + jnp.where(core == 1, next_low - low, 0) + 2 * jnp.where(core == 1, low - next_low, 0)
+
+
+def class_sums(state, core, nears, last_copy, loglik_ref, mine_ref, theirs_ref):
     top, total, _, weights = state
     loglik_ref[...] = top + jnp.log(total)
     per_owner = mine_ref.shape[1]
-    blocks, _, width = nears[0].shape
+    width = nears[0].shape[1]
     weights = weights / jnp.sum(weights, axis=0, keepdims=True)
     turned = jnp.concatenate([weights[per_owner:], weights[:per_owner]], axis=0)
     weights = jnp.where(core == 0, weights, turned)
@@ -286,45 +284,30 @@
     totals = jnp.broadcast_to(
         jnp.sum(weights, axis=1, keepdims=True), (weights.shape[0], LANES)
     )
-    for part, near in enumerate(nears):
-        if part == len(nears) - 1:
-            for copy in copies:
-                copy.wait()
-
-        @pl.loop(0, blocks)
-        def _(inner):
-            block = part * blocks + inner
-            sums = jnp.dot(rounded, near[inner], preferred_element_type=jnp.float32)
-            mine_ref[block, :, :width] = sums[:per_owner]
-            theirs_ref[block, :, :width] = sums[per_owner:]
-            mine_ref[block, :, width:] = totals[:per_owner]
-            theirs_ref[block, :, width:] = totals[per_owner:]
-
-
-def ring_kernel(phase, ends, part, sources, where_ref, noise_ref, low_ref, high_ref, *rest):
+    for block, near in enumerate(nears):
+        if block == len(nears) - 1:
+            last_copy.wait()
+        sums = jnp.dot(rounded, near[...], preferred_element_type=jnp.float32)
+        for ref, rows, owner in ((mine_ref, slice(0, per_owner), core),
+                                 (theirs_ref, slice(per_owner, None), 1 - core)):
+            at = swapped_bits(jnp.int32(block), owner)
+            ref[at, :, :width] = sums[rows]
+            ref[at, :, width:] = totals[rows]
+
+
+def ring_kernel(phase, ends, block, sources, where_ref, noise_ref, low_ref, high_ref, *rest):
     row_refs, rest = rest[: 2 * len(sources)], rest[2 * len(sources) :]
-    far_ref = near = copies = None
-    if part is not None:
-        far_ref, *rest = rest
+    far_ref, *rest = rest
     if phase == 0:
-        acc, energy, *rest = rest
+        acc, energy, near, arrived = rest
     else:
         acc_in, energy_in, logs_ref, words_ref, state_ref, *rest = rest
         if ends:
-            *nears, loglik_ref, mine_ref, theirs_ref, acc, energy = rest[:8]
-            rest = rest[8:]
+            *nears, loglik_ref, mine_ref, theirs_ref, acc, energy, near, arrived = rest
         else:
-            out_ref, *rest = rest
-            if part is not None:
-                near, acc, energy, arrived = rest
-            else:
-                acc, energy = rest
-    if part is not None:
-        if phase == 0 or ends:
-            near, arrived = rest
-        copies = near_copies(part, far_ref, near, arrived)
-        for copy in copies:
-            copy.start()
+            out_ref, near, acc, energy, arrived = rest
+    copy = near_copy(block, far_ref, near, arrived)
+    copy.start()
     if phase == 0:
         acc[...] = jnp.zeros_like(acc)
         energy[...] = jnp.zeros_like(energy)
@@ -334,27 +317,20 @@
     quarter = low_ref.shape[0]
     core = where_ref[1]
 
-    def add(refs, part_ref, at, step, start):
-        here = pl.ds(pl.multiple_of(start + step * WIDTH, WIDTH), WIDTH)
-        there = pl.ds(pl.multiple_of(step * WIDTH, WIDTH), WIDTH)
-        columns = pl.ds((2 * phase + at) * quarter + step * WIDTH, WIDTH)
-        rows = jnp.concatenate([ref[:, here] for ref in refs], axis=0)
-        weighted = weigh(rows, noise_ref[:, columns], energy)
-        acc[...] += jnp.dot(weighted, part_ref[there, :], preferred_element_type=jnp.float32)
-
     for at, part_ref in enumerate((low_ref, high_ref)):
         for step in range(quarter // WIDTH):
+            there = pl.ds(step * WIDTH, WIDTH)
+            columns = pl.ds((2 * phase + at) * quarter + step * WIDTH, WIDTH)
             if ends:
-                for own, ref in ((True, row_refs[0]), (False, row_refs[1])):
-                    pl.when((core == at) == own)(
-                        functools.partial(add, [ref], part_ref, at, step, 0)
-                    )
+                rows = jnp.where(core == at, row_refs[0][:, there], row_refs[1][:, there])
             else:
-                add(row_refs, part_ref, at, step, at * quarter)
-
-    if part is not None and not (ends and phase == 1):
-        for copy in copies:
-            copy.wait()
+                here = pl.ds(at * quarter + step * WIDTH, WIDTH)
+                rows = jnp.concatenate([ref[:, here] for ref in row_refs], axis=0)
+            weighted = weigh(rows, noise_ref[:, columns], energy)
+            acc[...] += jnp.dot(weighted, part_ref[there, :], preferred_element_type=jnp.float32)
+
+    if not (ends and phase == 1):
+        copy.wait()
     if phase == 0:
         return
     height = row_refs[0].shape[0]
@@ -378,12 +354,12 @@
     hit = jnp.concatenate([picked_rows(words_ref, source, height) for source in found], axis=0)
     state = add_rows(tags, hit, logs_ref, get_state(state_ref), acc, energy)
     if ends:
-        class_sums(state, core, [*nears, near], copies, loglik_ref, mine_ref, theirs_ref)
+        class_sums(state, core, [*nears, near], copy, loglik_ref, mine_ref, theirs_ref)
     else:
         put_state(state, out_ref)
 
 
-def ring_scores(phase, sources, where, noise, turned, arrays, rest, ends, particles, part, shape):
+def ring_scores(phase, sources, where, noise, turned, arrays, rest, ends, particles, block, shape):
     quarter, per_device = turned[0].shape
     freqs = 4 * quarter
     rows = arrays[0].shape[0] * (1 if ends else len(arrays))
@@ -392,37 +368,29 @@
         jax.ShapeDtypeStruct((rows, LANES), jnp.float32),
     ]
     scratch = [pltpu.VMEM(array.shape, array.dtype) for array in sums]
-    blocks = shape[0] // 4
-    raw = (blocks, per_device, freqs // shape[0])
-    specs, inputs = [], []
-    if part is not None:
-        specs = [pl.BlockSpec(memory_space=pl.ANY)]
-        inputs = [pltpu.with_memory_space_constraint(particles, pltpu.HBM)]
+    raw = pltpu.VMEM((per_device, freqs // shape[0]), particles.dtype)
+    specs = [pl.BlockSpec(memory_space=pl.ANY)]
     if phase == 0:
-        shapes, scratch = sums, []
+        shapes, scratch = sums + [raw], []
     else:
         specs += [in_vmem(), in_vmem(), in_smem(), in_vmem(), in_vmem()]
         if ends:
             piece = jax.ShapeDtypeStruct(shape, jnp.float32)
             shapes = [jax.ShapeDtypeStruct((1, per_device), jnp.float32), piece, piece]
-            specs += [in_vmem()] * 3
             nears = [pltpu.with_memory_space_constraint(x, pltpu.VMEM) for x in rest[5:]]
+            specs += [in_vmem()] * len(nears)
             rest = (*rest[:5], *nears)
+            scratch.append(raw)
         else:
-            shapes = [jax.ShapeDtypeStruct(rest[4].shape, jnp.float32)]
-    if part is not None:
-        if ends and phase == 1:
-            scratch.append(pltpu.VMEM(raw, particles.dtype))
-        else:
-            shapes.append(pltpu.VMEM(raw, particles.dtype))
-        scratch.append(pltpu.SemaphoreType.DMA((blocks,)))
+            shapes = [jax.ShapeDtypeStruct(rest[4].shape, jnp.float32), raw]
+    scratch.append(pltpu.SemaphoreType.DMA)
     return pl.pallas_call(
-        functools.partial(ring_kernel, phase, ends, part, sources),
+        functools.partial(ring_kernel, phase, ends, block, sources),
         in_specs=[in_smem()] + [in_vmem()] * (3 + len(arrays)) + specs,
         out_specs=[in_vmem()] * len(shapes),
         out_shape=shapes,
         scratch_shapes=scratch,
-        compiler_params=pltpu.CompilerParams(vmem_limit_bytes=VMEM_LIMIT if ends else SMALL_LIMIT),
+        compiler_params=pltpu.CompilerParams(vmem_limit_bytes=SMALL_LIMIT),
         cost_estimate=pl.CostEstimate(
             flops=2 * 128 * per_device * freqs,
             bytes_accessed=per_device * freqs,
@@ -433,26 +401,25 @@
         noise,
         *(pltpu.with_memory_space_constraint(part, pltpu.VMEM) for part in turned),
         *arrays,
-        *inputs,
+        pltpu.with_memory_space_constraint(particles, pltpu.HBM),
         *rest,
     )
 
 
-def scatter_sum(pieces, blocks, block_id):
+def scatter_sum(pieces, blocks, block_id, core):
     tail = pieces.shape[1:]
-    stride, left = 1, blocks
-    while left > 1:
-        radix = 4 if stride > 1 and left % 4 == 0 else 2
-        digit = lax.rem(lax.div(block_id, jnp.uint32(stride)), jnp.uint32(radix))
-        groups = pieces.reshape((-1, radix) + tail)
-        total = lax.dynamic_index_in_dim(groups, digit, 1, keepdims=False)
-        for change in range(1, radix):
-            there = lax.bitwise_xor(digit, jnp.uint32(change))
-            send = lax.dynamic_index_in_dim(groups, there, 1, keepdims=False)
-            swaps = [(i, i ^ (change * stride)) for i in range(blocks)]
-            total = total + lax.ppermute(send, "blk", swaps)
-        pieces = total
-        stride, left = stride * radix, left // radix
+    place = swapped_bits(block_id, core)
+    for step in range(blocks.bit_length() - 1):
+        bit = lax.rem(lax.div(place, 1 << step), 2)
+        pairs = pieces.reshape((-1, 2) + tail)
+        keep = lax.dynamic_index_in_dim(pairs, bit, 1, keepdims=False)
+        send = lax.dynamic_index_in_dim(pairs, 1 - bit, 1, keepdims=False)
+        swaps = []
+        for block in range(blocks):
+            for owner in range(2):
+                change = (2, 1)[step] if owner == 1 and step < 2 else 1 << step
+                swaps.append((2 * block + owner, 2 * (block ^ change) + owner))
+        pieces = keep + lax.ppermute(send, ("blk", "cls"), swaps)
     return pieces[0]
 
 
@@ -517,23 +484,19 @@
             rest = (*sums, logs, words, state) if phase else ()
             if ends and phase:
                 rest += tuple(nears)
-            part = 2 * (distance - last) + phase + 2
-            part = part if part >= 0 else None
-            sums = ring_scores(
+            *sums, near = ring_scores(
                 phase, tables, where, near_noise, turned[phase], pair, rest,
-                ends, particles, part, shape,
+                ends, particles, len(nears), shape,
             )
             gates.append(sums)
-            if part is not None and part < 3:
-                *sums, near = sums
-                nears.append(near)
+            nears.append(near)
         held = arrived
         if not ends:
             (state,) = sums
 
-    loglik, mine, theirs = sums
+    loglik, mine, theirs = (*sums, near)
     reduced = mine + lax.ppermute(theirs, "cls", swap)
-    total = scatter_sum(reduced, blocks, block_id.astype(jnp.uint32))
+    total = scatter_sum(reduced, blocks, block_id, core)
     counts = lax.dynamic_slice_in_dim(class_counts, core * per_owner, per_owner, 0)
     class_avg = total[:, :width] / (total[:, width] + counts.astype(jnp.float32))[:, None]
     return loglik[0], class_avg

time: 76.7 us -> 75.8 us (0.988)
  starting transfers between devices: 23.1 us -> 21.1 us
  Pallas kernels: 38.6 us -> 40 us
    ppermute x8, waiting for transfers between devices: 3.68 us -> 1.83 us  [body(): own = lax.ppermute(message, ('blk', 'cls'), ring)]
    ppermute x4 -> x3, starting transfers between devices: 5.63 us -> 4.21 us  [scatter_sum(): pieces = keep + lax.ppermute(send, ('blk', 'cls'), swaps)]
    pallas_call x8, Pallas kernels: 25.7 us -> 27 us  [ring_scores(): pl.pallas_call(functools.partial(ring_kernel, phase, ends, block, sources...]
    ppermute x4 -> x3, waiting for transfers between devices: 7.76 us -> 8.95 us  [scatter_sum(): pieces = keep + lax.ppermute(send, ('blk', 'cls'), swaps)]
  transfers between devices with their start and end apart: 21 -> 20, of which waited for: 8 -> 7; matrix products, arithmetic and copies ran while one was open for 0% -> 0% of each run, Pallas kernels for 40% -> 44%
where the time goes in v10:
time: 75.8 us; the launch traced here: 75.5 us
  Pallas kernels  40 us (53%)
  starting transfers between devices  21.1 us (28%)
  waiting for transfers between devices  12.1 us (16%)
  other arithmetic  0.92 us (1%)
  between operations  0.89 us (1%)
    pallas_call x8, Pallas kernels, ring_scores(): pl.pallas_call(functools.partial(ring_kernel, phase, ends, block, sources...  27 us
    ppermute x8, starting transfers between devices, body(): own = lax.ppermute(message, ('blk', 'cls'), ring)  15.8 us
    pallas_call x3, Pallas kernels, own_scores(): pl.pallas_call(functools.partial(own_kernel, quarters), in_specs=[in_smem...  11.7 us
    ppermute x3, waiting for transfers between devices, scatter_sum(): pieces = keep + lax.ppermute(send, ('blk', 'cls'), swaps)  8.95 us
    ppermute x3, starting transfers between devices, scatter_sum(): pieces = keep + lax.ppermute(send, ('blk', 'cls'), swaps)  4.21 us
    ppermute x8, waiting for transfers between devices, body(): own = lax.ppermute(message, ('blk', 'cls'), ring)  1.83 us
  transfers between devices with their start and end apart: 20, of which 7 were waited for; matrix products, arithmetic and copies ran while one was open for 0% of the time, Pallas kernels for 44%

profile of v10, /device:TPU:0, one launch (start us, length us, event | category | flops | bytes accessed | tf_op | source)
XLA Modules:
  0.0 75.5 jit_solution(12395183750667463520)
XLA Ops:
  1.9 3.1 %collective-permute-start.2 = (bf16[64,4096]{1,0:T(8,128)(2,1)S(1)}, bf16[64,4096]{1,0:T(8,128)(2,1)S(1)}, u32[]{:S(2)}, u32[]{:S(2)}) collective-permute-start(bf16[64,4096]{1,0:T(8,128)(2,1)S(1)} %get-tuple-element.52.tmpl_ref), channel_id=1, source_target_pairs={{0,4},{4,8},{8,12},{12,14},{14,10},{10,6},{6,2},{2,0},{5,1},{9,5},... | collective-permute-start | bytes 1572872 | tf_op jit(solution)/shard_map/ppermute | solution.py:478
  5.0 1.6 %collective-permute-start = (bf16[64,4224]{1,0:T(8,128)(2,1)S(1)}, bf16[64,4224]{1,0:T(8,128)(2,1)S(1)}, u32[]{:S(2)}, u32[]{:S(2)}) collective-permute-start(bf16[64,4224]{1,0:T(8,128)(2,1)S(1)} %get-tuple-element.51.tmpl_ref), channel_id=1, source_target_pairs={{0,4},{4,8},{8,12},{12,14},{14,10},{10,6},{6,2},{2,0},{5,1},{9,5},... | collective-permute-start | bytes 1622024 | tf_op jit(solution)/shard_map/ppermute | solution.py:478
  6.6 5.9 %shard_map.78 = (s32[16,1024]{1,0:T(8,128)S(1)}, f32[64,1024]{1,0:T(8,128)S(1)}, f32[64,128]{1,0:T(8,128)S(1)}, bf16[2048,1024]{1,0:T(8,128)(2,1)S(1)}, bf16[204...) custom-call(s32[2]{0:T(128)S(1)} %pad_add_fusion.where_ref, f32[1,8192]{1,0:T(1,128)S(1)} %get-tuple-element.50.noise_ref, ...), custom_call_target="tpu_custom_call" | custom-call | flops 2147483648 | bytes 8388608 | tf_op jit(solution)/shard_map/pallas_call | solution.py:250
  12.5 1.6 %collective-permute-start.6 = (bf16[64,4096]{1,0:T(8,128)(2,1)S(1)}, bf16[64,4096]{1,0:T(8,128)(2,1)S(1)}, u32[]{:S(2)}, u32[]{:S(2)}) collective-permute-start(bf16[64,4096]{1,0:T(8,128)(2,1)S(1)} %collective-permute-done.2.rest_0_), channel_id=1, source_target_pairs={{0,4},{4,8},{8,12},{12,14},{14,10},{10,6},{6,2},{2,0},{5,1},{9,5},... | collective-permute-start | bytes 1572872 | tf_op jit(solution)/shard_map/ppermute | solution.py:478
  14.2 2.8 %shard_map.79 = (f32[64,1024]{1,0:T(8,128)S(1)}, f32[64,128]{1,0:T(8,128)S(1)}, bf16[2048,1024]{1,0:T(8,128)(2,1)S(1)}, bf16[4,1024,512]{2,1,0:T(8,128)(2,1)S(1)}) custom-call(s32[2]{0:T(128)S(1)} %pad_add_fusion.where_ref, f32[1,8192]{1,0:T(1,128)S(1)} %get-tuple-element.50.noise_ref, bf16[64,4224]{1,0:T(8,128)(2,1)S(1)} %get-tuple-element.51.tmpl_ref, ...), custom_call_target="tpu_custom_call" | custom-call | flops 2147483648 | bytes 8388608 | tf_op jit(solution)/shard_map/pallas_call | solution.py:250
  17.9 2.1 %collective-permute-start.1 = (bf16[64,4224]{1,0:T(8,128)(2,1)S(1)}, bf16[64,4224]{1,0:T(8,128)(2,1)S(1)}, u32[]{:S(2)}, u32[]{:S(2)}) collective-permute-start(bf16[64,4224]{1,0:T(8,128)(2,1)S(1)} %collective-permute-done.rest_0_), channel_id=1, source_target_pairs={{0,4},{4,8},{8,12},{12,14},{14,10},{10,6},{6,2},{2,0},{5,1},{9,5},... | collective-permute-start | bytes 1622024 | tf_op jit(solution)/shard_map/ppermute | solution.py:478
  20.0 3.0 %shard_map.80 = (f32[16,1024]{1,0:T(8,128)S(1)}, bf16[2048,1024]{1,0:T(8,128)(2,1)S(1)}) custom-call(s32[2]{0:T(128)S(1)} %pad_add_fusion.where_ref, f32[1,8192]{1,0:T(1,128)S(1)} %get-tuple-element.50.noise_ref, bf16[64,4224]{1,0:T(8,128)(2,1)S(1)} %get-tuple-element.51.tmpl_ref, bf16[1024,8192]{1,0:T(8,128)(2,1)} %rest_2_.15, ...), custom_call_target="tpu_custom_call" | custom-call | flops 2147483648 | bytes 8388608 | tf_op jit(solution)/shard_map/pallas_call | solution.py:250
  23.5 2.1 %collective-permute-start.11 = (bf16[64,4096]{1,0:T(8,128)(2,1)S(1)}, bf16[64,4096]{1,0:T(8,128)(2,1)S(1)}, u32[]{:S(2)}, u32[]{:S(2)}) collective-permute-start(bf16[64,4096]{1,0:T(8,128)(2,1)S(1)} %collective-permute-done.6.rest_0_), channel_id=1, source_target_pairs={{0,4},{4,8},{8,12},{12,14},{14,10},{10,6},{6,2},{2,0},{5,1},{9,5},... | collective-permute-start | bytes 1572872 | tf_op jit(solution)/shard_map/ppermute | solution.py:478
  25.6 3.2 %shard_map.81 = (f32[128,1024]{1,0:T(8,128)S(1)}, f32[128,128]{1,0:T(8,128)S(1)}, bf16[1024,1024]{1,0:T(8,128)(2,1)S(1)}) custom-call(s32[2]{0:T(128)S(1)} %pad_add_fusion.where_ref, f32[1,8192]{1,0:T(1,128)S(1)} %get-tuple-element.50.noise_ref, bf16[2048,1024]{1,0:T(8,128)(2,1)S(1)} %get-tuple-element.64.low_ref, ...), custom_call_target="tpu_custom_call" | custom-call | flops 2147483648 | bytes 8388608 | tf_op jit(solution)/shard_map/pallas_call | solution.py:387
  29.3 2.1 %collective-permute-start.4 = (bf16[64,4224]{1,0:T(8,128)(2,1)S(1)}, bf16[64,4224]{1,0:T(8,128)(2,1)S(1)}, u32[]{:S(2)}, u32[]{:S(2)}) collective-permute-start(bf16[64,4224]{1,0:T(8,128)(2,1)S(1)} %collective-permute-done.1.rest_0_), channel_id=1, source_target_pairs={{0,4},{4,8},{8,12},{12,14},{14,10},{10,6},{6,2},{2,0},{5,1},{9,5},... | collective-permute-start | bytes 1622024 | tf_op jit(solution)/shard_map/ppermute | solution.py:478
  31.4 2.9 %shard_map.83 = (f32[16,1024]{1,0:T(8,128)S(1)}, bf16[1024,1024]{1,0:T(8,128)(2,1)S(1)}) custom-call(s32[2]{0:T(128)S(1)} %pad_add_fusion.where_ref, f32[1,8192]{1,0:T(1,128)S(1)} %get-tuple-element.50.noise_ref, bf16[2048,1024]{1,0:T(8,128)(2,1)S(1)} %get-tuple-element.57.low_ref, bf16[2048,1024]{1,0:T(8,128)(2,1)S(1)} %get-tuple-element.62.high_ref, ...), custom_call_target="tpu_custom_call" | custom-call | flops 2147483648 | bytes 8388608 | tf_op jit(solution)/shard_map/pallas_call | solution.py:387
  34.3 3.3 %shard_map.82 = (f32[128,1024]{1,0:T(8,128)S(1)}, f32[128,128]{1,0:T(8,128)S(1)}, bf16[1024,1024]{1,0:T(8,128)(2,1)S(1)}) custom-call(s32[2]{0:T(128)S(1)} %pad_add_fusion.where_ref, f32[1,8192]{1,0:T(1,128)S(1)} %get-tuple-element.50.noise_ref, bf16[2048,1024]{1,0:T(8,128)(2,1)S(1)} %get-tuple-element.64.low_ref, ...), custom_call_target="tpu_custom_call" | custom-call | flops 2147483648 | bytes 8388608 | tf_op jit(solution)/shard_map/pallas_call | solution.py:387
  38.0 1.5 %collective-permute-start.14 = (bf16[64,2048]{1,0:T(8,128)(2,1)S(1)}, bf16[64,2048]{1,0:T(8,128)(2,1)S(1)}, u32[]{:S(2)}, u32[]{:S(2)}) collective-permute-start(bf16[64,2048]{1,0:T(8,128)(2,1)S(1)} %constant_dynamic-slice_fusion.1), channel_id=1, source_target_pairs={{0,4},{4,8},{8,12},{12,14},{14,10},{10,6},{6,2},{2,0},{5,1},{9,5},... | collective-permute-start | bytes 786440 | tf_op jit(solution)/shard_map/ppermute | solution.py:478
  39.5 2.9 %shard_map.84 = (f32[16,1024]{1,0:T(8,128)S(1)}, bf16[1024,1024]{1,0:T(8,128)(2,1)S(1)}) custom-call(s32[2]{0:T(128)S(1)} %pad_add_fusion.where_ref, f32[1,8192]{1,0:T(1,128)S(1)} %get-tuple-element.50.noise_ref, bf16[2048,1024]{1,0:T(8,128)(2,1)S(1)} %get-tuple-element.57.low_ref, bf16[2048,1024]{1,0:T(8,128)(2,1)S(1)} %get-tuple-element.62.high_ref, ...), custom_call_target="tpu_custom_call" | custom-call | flops 2147483648 | bytes 8388608 | tf_op jit(solution)/shard_map/pallas_call | solution.py:387
  42.6 1.8 %collective-permute-start.9 = (bf16[64,2176]{1,0:T(8,128)(2,1)S(1)}, bf16[64,2176]{1,0:T(8,128)(2,1)S(1)}, u32[]{:S(2)}, u32[]{:S(2)}) collective-permute-start(bf16[64,2176]{1,0:T(8,128)(2,1)S(1)} %constant_dynamic-slice_fusion.2), channel_id=1, source_target_pairs={{0,4},{4,8},{8,12},{12,14},{14,10},{10,6},{6,2},{2,0},{5,1},{9,5},... | collective-permute-start | bytes 835592 | tf_op jit(solution)/shard_map/ppermute | solution.py:478
  44.4 3.3 %shard_map.85 = (f32[128,1024]{1,0:T(8,128)S(1)}, f32[128,128]{1,0:T(8,128)S(1)}, bf16[1024,1024]{1,0:T(8,128)(2,1)S(1)}) custom-call(s32[2]{0:T(128)S(1)} %pad_add_fusion.where_ref, f32[1,8192]{1,0:T(1,128)S(1)} %get-tuple-element.50.noise_ref, bf16[2048,1024]{1,0:T(8,128)(2,1)S(1)} %get-tuple-element.64.low_ref, ...), custom_call_target="tpu_custom_call" | custom-call | flops 2147483648 | bytes 8388608 | tf_op jit(solution)/shard_map/pallas_call | solution.py:387
  47.8 2.9 %shard_map.86 = (f32[16,1024]{1,0:T(8,128)S(1)}, bf16[1024,1024]{1,0:T(8,128)(2,1)S(1)}) custom-call(s32[2]{0:T(128)S(1)} %pad_add_fusion.where_ref, f32[1,8192]{1,0:T(1,128)S(1)} %get-tuple-element.50.noise_ref, bf16[2048,1024]{1,0:T(8,128)(2,1)S(1)} %get-tuple-element.57.low_ref, bf16[2048,1024]{1,0:T(8,128)(2,1)S(1)} %get-tuple-element.62.high_ref, ...), custom_call_target="tpu_custom_call" | custom-call | flops 2147483648 | bytes 8388608 | tf_op jit(solution)/shard_map/pallas_call | solution.py:387
  51.3 3.4 %shard_map.87 = (f32[64,1024]{1,0:T(8,128)S(1)}, f32[64,128]{1,0:T(8,128)S(1)}, bf16[1024,1024]{1,0:T(8,128)(2,1)S(1)}) custom-call(s32[2]{0:T(128)S(1)} %pad_add_fusion.where_ref, f32[1,8192]{1,0:T(1,128)S(1)} %get-tuple-element.50.noise_ref, bf16[2048,1024]{1,0:T(8,128)(2,1)S(1)} %get-tuple-element.64.low_ref, ...), custom_call_target="tpu_custom_call" | custom-call | flops 2147483648 | bytes 8388608 | tf_op jit(solution)/shard_map/pallas_call | solution.py:387
  54.7 5.1 %shard_map.88 = (f32[1,1024]{1,0:T(1,128)}, f32[8,4,1152]{2,1,0:T(4,128)S(1)}, f32[8,4,1152]{2,1,0:T(4,128)S(1)}) custom-call(s32[2]{0:T(128)S(1)} %pad_add_fusion.where_ref, f32[1,8192]{1,0:T(1,128)S(1)} %get-tuple-element.50.noise_ref, bf16[2048,1024]{1,0:T(8,128)(2,1)S(1)} %get-tuple-element.57.low_ref, ...), custom_call_target="tpu_custom_call" | custom-call | flops 2147483648 | bytes 8388608 | tf_op jit(solution)/shard_map/pallas_call | solution.py:387
  62.2 3.5 %collective-permute-done.17 = f32[4,4,1152]{2,1,0:T(4,128)S(1)} collective-permute-done((f32[4,4,1152]{2,1,0:T(4,128)S(1)}, f32[4,4,1152]{2,1,0:T(4,128)S(1)}, u32[]{:S(2)}, u32[]{:S(2)}) %collective-permute-start.17) | collective-permute-done | bytes 73760 | tf_op jit(solution)/shard_map/ppermute | solution.py:422
  65.8 1.6 %collective-permute-start.18 = (f32[2,4,1152]{2,1,0:T(4,128)S(1)}, f32[2,4,1152]{2,1,0:T(4,128)S(1)}, u32[]{:S(2)}, u32[]{:S(2)}) collective-permute-start(f32[2,4,1152]{2,1,0:T(4,128)S(1)} %dynamic-slice_bitcast_fusion.1), channel_id=1, source_target_pairs={{0,4},{1,3},{2,6},{3,1},{4,0},{5,7},{6,2},{7,5},{8,12},{9,11},{10,... | collective-permute-start | bytes 110600 | tf_op jit(solution)/shard_map/ppermute | solution.py:422
  67.4 2.4 %collective-permute-done.18 = f32[2,4,1152]{2,1,0:T(4,128)S(1)} collective-permute-done((f32[2,4,1152]{2,1,0:T(4,128)S(1)}, f32[2,4,1152]{2,1,0:T(4,128)S(1)}, u32[]{:S(2)}, u32[]{:S(2)}) %collective-permute-start.18) | collective-permute-done | bytes 36896 | tf_op jit(solution)/shard_map/ppermute | solution.py:422
  69.8 1.7 %collective-permute-start.19 = (f32[1,4,1152]{2,1,0:T(4,128)S(1)}, f32[1,4,1152]{2,1,0:T(4,128)S(1)}, u32[]{:S(2)}, u32[]{:S(2)}) collective-permute-start(f32[1,4,1152]{2,1,0:T(4,128)S(1)} %constant_dynamic-slice_fusion), channel_id=1, source_target_pairs={{0,8},{1,9},{2,10},{3,11},{4,12},{5,13},{6,14},{7,15},{8,0},{9,1},... | collective-permute-start | bytes 55304 | tf_op jit(solution)/shard_map/ppermute | solution.py:422
  71.6 3.0 %collective-permute-done.19 = f32[1,4,1152]{2,1,0:T(4,128)S(1)} collective-permute-done((f32[1,4,1152]{2,1,0:T(4,128)S(1)}, f32[1,4,1152]{2,1,0:T(4,128)S(1)}, u32[]{:S(2)}, u32[]{:S(2)}) %collective-permute-start.19) | collective-permute-done | bytes 18464 | tf_op jit(solution)/shard_map/ppermute | solution.py:422
  (46 shorter events, 7.8 us)
Async XLA Ops:
  1.9 10.6 %collective-permute-start.2 = (bf16[64,4096]{1,0:T(8,128)(2,1)S(1)}, bf16[64,4096]{1,0:T(8,128)(2,1)S(1)}, u32[]{:S(2)}, u32[]{:S(2)}) collective-permute-start(bf16[64,4096]{1,0:T(8,128)(2,1)S(1)} %get-tuple-element.52.tmpl_ref), channel_id=1, source_target_pairs={{0,4},{4,8},{8,12},{12,14},{14,10},{10,6},{6,2},{2,0},{5,1},{9,5},... | collective-permute-start | bytes 1572872 | tf_op jit(solution)/shard_map/ppermute | solution.py:478
  5.0 12.9 %collective-permute-start = (bf16[64,4224]{1,0:T(8,128)(2,1)S(1)}, bf16[64,4224]{1,0:T(8,128)(2,1)S(1)}, u32[]{:S(2)}, u32[]{:S(2)}) collective-permute-start(bf16[64,4224]{1,0:T(8,128)(2,1)S(1)} %get-tuple-element.51.tmpl_ref), channel_id=1, source_target_pairs={{0,4},{4,8},{8,12},{12,14},{14,10},{10,6},{6,2},{2,0},{5,1},{9,5},... | collective-permute-start | bytes 1622024 | tf_op jit(solution)/shard_map/ppermute | solution.py:478
  12.5 10.9 %collective-permute-start.6 = (bf16[64,4096]{1,0:T(8,128)(2,1)S(1)}, bf16[64,4096]{1,0:T(8,128)(2,1)S(1)}, u32[]{:S(2)}, u32[]{:S(2)}) collective-permute-start(bf16[64,4096]{1,0:T(8,128)(2,1)S(1)} %collective-permute-done.2.rest_0_), channel_id=1, source_target_pairs={{0,4},{4,8},{8,12},{12,14},{14,10},{10,6},{6,2},{2,0},{5,1},{9,5},... | collective-permute-start | bytes 1572872 | tf_op jit(solution)/shard_map/ppermute | solution.py:478
  14.2 5.8 %copy-start.1 = (s32[8]{0:T(128)S(1)}, s32[8]{0:T(128)}, u32[]{:S(2)}) copy-start(s32[8]{0:T(128)} %param.10) | copy-start | bytes 100
  14.2 5.8 %copy-start = (s32[64]{0:T(128)S(1)}, s32[64]{0:T(128)}, u32[]{:S(2)}) copy-start(s32[64]{0:T(128)} %param.9) | copy-start | bytes 772
  16.9 8.6 %collective-permute-start.3 = (bf16[64,4096]{1,0:T(8,128)(2,1)S(1)}, bf16[64,4096]{1,0:T(8,128)(2,1)S(1)}, u32[]{:S(2)}, u32[]{:S(2)}) collective-permute-start(bf16[64,4096]{1,0:T(8,128)(2,1)S(1)} %collective-permute-done.2.rest_0_), channel_id=1, source_target_pairs={{0,1},{1,0},{2,3},{3,2},{4,5},{5,4},{6,7},{7,6},{8,9},{9,8},{10,11... | collective-permute-start | bytes 1572872 | tf_op jit(solution)/shard_map/ppermute | solution.py:482
  17.9 13.5 %collective-permute-start.8 = (bf16[64,4224]{1,0:T(8,128)(2,1)S(1)}, bf16[64,4224]{1,0:T(8,128)(2,1)S(1)}, u32[]{:S(2)}, u32[]{:S(2)}) collective-permute-start(bf16[64,4224]{1,0:T(8,128)(2,1)S(1)} %collective-permute-done.rest_0_), channel_id=1, source_target_pairs={{0,1},{1,0},{2,3},{3,2},{4,5},{5,4},{6,7},{7,6},{8,9},{9,8},{10,11... | collective-permute-start | bytes 1622024 | tf_op jit(solution)/shard_map/ppermute | solution.py:482
  17.9 11.4 %collective-permute-start.1 = (bf16[64,4224]{1,0:T(8,128)(2,1)S(1)}, bf16[64,4224]{1,0:T(8,128)(2,1)S(1)}, u32[]{:S(2)}, u32[]{:S(2)}) collective-permute-start(bf16[64,4224]{1,0:T(8,128)(2,1)S(1)} %collective-permute-done.rest_0_), channel_id=1, source_target_pairs={{0,4},{4,8},{8,12},{12,14},{14,10},{10,6},{6,2},{2,0},{5,1},{9,5},... | collective-permute-start | bytes 1622024 | tf_op jit(solution)/shard_map/ppermute | solution.py:478
  23.5 10.8 %collective-permute-start.7 = (bf16[64,4096]{1,0:T(8,128)(2,1)S(1)}, bf16[64,4096]{1,0:T(8,128)(2,1)S(1)}, u32[]{:S(2)}, u32[]{:S(2)}) collective-permute-start(bf16[64,4096]{1,0:T(8,128)(2,1)S(1)} %collective-permute-done.6.rest_0_), channel_id=1, source_target_pairs={{0,1},{1,0},{2,3},{3,2},{4,5},{5,4},{6,7},{7,6},{8,9},{9,8},{10,11... | collective-permute-start | bytes 1572872 | tf_op jit(solution)/shard_map/ppermute | solution.py:482
  23.5 14.1 %collective-permute-start.11 = (bf16[64,4096]{1,0:T(8,128)(2,1)S(1)}, bf16[64,4096]{1,0:T(8,128)(2,1)S(1)}, u32[]{:S(2)}, u32[]{:S(2)}) collective-permute-start(bf16[64,4096]{1,0:T(8,128)(2,1)S(1)} %collective-permute-done.6.rest_0_), channel_id=1, source_target_pairs={{0,4},{4,8},{8,12},{12,14},{14,10},{10,6},{6,2},{2,0},{5,1},{9,5},... | collective-permute-start | bytes 1572872 | tf_op jit(solution)/shard_map/ppermute | solution.py:478
  29.3 10.2 %collective-permute-start.5 = (bf16[64,4224]{1,0:T(8,128)(2,1)S(1)}, bf16[64,4224]{1,0:T(8,128)(2,1)S(1)}, u32[]{:S(2)}, u32[]{:S(2)}) collective-permute-start(bf16[64,4224]{1,0:T(8,128)(2,1)S(1)} %collective-permute-done.1.rest_0_), channel_id=1, source_target_pairs={{0,1},{1,0},{2,3},{3,2},{4,5},{5,4},{6,7},{7,6},{8,9},{9,8},{10,11... | collective-permute-start | bytes 1622024 | tf_op jit(solution)/shard_map/ppermute | solution.py:482
  29.3 13.1 %collective-permute-start.4 = (bf16[64,4224]{1,0:T(8,128)(2,1)S(1)}, bf16[64,4224]{1,0:T(8,128)(2,1)S(1)}, u32[]{:S(2)}, u32[]{:S(2)}) collective-permute-start(bf16[64,4224]{1,0:T(8,128)(2,1)S(1)} %collective-permute-done.1.rest_0_), channel_id=1, source_target_pairs={{0,4},{4,8},{8,12},{12,14},{14,10},{10,6},{6,2},{2,0},{5,1},{9,5},... | collective-permute-start | bytes 1622024 | tf_op jit(solution)/shard_map/ppermute | solution.py:478
  37.6 6.8 %collective-permute-start.12 = (bf16[64,4096]{1,0:T(8,128)(2,1)S(1)}, bf16[64,4096]{1,0:T(8,128)(2,1)S(1)}, u32[]{:S(2)}, u32[]{:S(2)}) collective-permute-start(bf16[64,4096]{1,0:T(8,128)(2,1)S(1)} %collective-permute-done.11.rest_0_), channel_id=1, source_target_pairs={{0,1},{1,0},{2,3},{3,2},{4,5},{5,4},{6,7},{7,6},{8,9},{9,8},{10,11... | collective-permute-start | bytes 1572872 | tf_op jit(solution)/shard_map/ppermute | solution.py:482
  38.0 9.8 %collective-permute-start.14 = (bf16[64,2048]{1,0:T(8,128)(2,1)S(1)}, bf16[64,2048]{1,0:T(8,128)(2,1)S(1)}, u32[]{:S(2)}, u32[]{:S(2)}) collective-permute-start(bf16[64,2048]{1,0:T(8,128)(2,1)S(1)} %constant_dynamic-slice_fusion.1), channel_id=1, source_target_pairs={{0,4},{4,8},{8,12},{12,14},{14,10},{10,6},{6,2},{2,0},{5,1},{9,5},... | collective-permute-start | bytes 786440 | tf_op jit(solution)/shard_map/ppermute | solution.py:478
  42.4 5.4 %collective-permute-start.10 = (bf16[64,4224]{1,0:T(8,128)(2,1)S(1)}, bf16[64,4224]{1,0:T(8,128)(2,1)S(1)}, u32[]{:S(2)}, u32[]{:S(2)}) collective-permute-start(bf16[64,4224]{1,0:T(8,128)(2,1)S(1)} %collective-permute-done.4.rest_0_), channel_id=1, source_target_pairs={{0,1},{1,0},{2,3},{3,2},{4,5},{5,4},{6,7},{7,6},{8,9},{9,8},{10,11... | collective-permute-start | bytes 1622024 | tf_op jit(solution)/shard_map/ppermute | solution.py:482
  42.6 8.1 %collective-permute-start.9 = (bf16[64,2176]{1,0:T(8,128)(2,1)S(1)}, bf16[64,2176]{1,0:T(8,128)(2,1)S(1)}, u32[]{:S(2)}, u32[]{:S(2)}) collective-permute-start(bf16[64,2176]{1,0:T(8,128)(2,1)S(1)} %constant_dynamic-slice_fusion.2), channel_id=1, source_target_pairs={{0,4},{4,8},{8,12},{12,14},{14,10},{10,6},{6,2},{2,0},{5,1},{9,5},... | collective-permute-start | bytes 835592 | tf_op jit(solution)/shard_map/ppermute | solution.py:478
  47.7 3.6 %collective-permute-start.15 = (bf16[64,2048]{1,0:T(8,128)(2,1)S(1)}, bf16[64,2048]{1,0:T(8,128)(2,1)S(1)}, u32[]{:S(2)}, u32[]{:S(2)}) collective-permute-start(bf16[64,2048]{1,0:T(8,128)(2,1)S(1)} %collective-permute-done.14.rest_0_), channel_id=1, source_target_pairs={{0,1},{1,0},{2,3},{3,2},{4,5},{5,4},{6,7},{7,6},{8,9},{9,8},{10,11... | collective-permute-start | bytes 786440 | tf_op jit(solution)/shard_map/ppermute | solution.py:482
  50.7 3.9 %collective-permute-start.13 = (bf16[64,2176]{1,0:T(8,128)(2,1)S(1)}, bf16[64,2176]{1,0:T(8,128)(2,1)S(1)}, u32[]{:S(2)}, u32[]{:S(2)}) collective-permute-start(bf16[64,2176]{1,0:T(8,128)(2,1)S(1)} %collective-permute-done.9.rest_0_), channel_id=1, source_target_pairs={{0,1},{1,0},{2,3},{3,2},{4,5},{5,4},{6,7},{7,6},{8,9},{9,8},{10,11... | collective-permute-start | bytes 835592 | tf_op jit(solution)/shard_map/ppermute | solution.py:482
  59.8 1.4 %collective-permute-start.16 = (f32[8,4,1152]{2,1,0:T(4,128)S(1)}, f32[8,4,1152]{2,1,0:T(4,128)S(1)}, u32[]{:S(2)}, u32[]{:S(2)}) collective-permute-start(f32[8,4,1152]{2,1,0:T(4,128)S(1)} %get-tuple-element.95), channel_id=1, source_target_pairs={{0,1},{1,0},{2,3},{3,2},{4,5},{5,4},{6,7},{7,6},{8,9},{9,8},{10,11... | collective-permute-start | bytes 442376 | tf_op jit(solution)/shard_map/ppermute | solution.py:498
  61.3 4.4 %collective-permute-start.17 = (f32[4,4,1152]{2,1,0:T(4,128)S(1)}, f32[4,4,1152]{2,1,0:T(4,128)S(1)}, u32[]{:S(2)}, u32[]{:S(2)}) collective-permute-start(f32[4,4,1152]{2,1,0:T(4,128)S(1)} %dynamic-slice_bitcast_fusion), channel_id=1, source_target_pairs={{0,2},{1,5},{2,0},{3,7},{4,6},{5,1},{6,4},{7,3},{8,10},{9,13},{10,... | collective-permute-start | bytes 221192 | tf_op jit(solution)/shard_map/ppermute | solution.py:422
  65.8 4.0 %collective-permute-start.18 = (f32[2,4,1152]{2,1,0:T(4,128)S(1)}, f32[2,4,1152]{2,1,0:T(4,128)S(1)}, u32[]{:S(2)}, u32[]{:S(2)}) collective-permute-start(f32[2,4,1152]{2,1,0:T(4,128)S(1)} %dynamic-slice_bitcast_fusion.1), channel_id=1, source_target_pairs={{0,4},{1,3},{2,6},{3,1},{4,0},{5,7},{6,2},{7,5},{8,12},{9,11},{10,... | collective-permute-start | bytes 110600 | tf_op jit(solution)/shard_map/ppermute | solution.py:422
  69.8 4.7 %collective-permute-start.19 = (f32[1,4,1152]{2,1,0:T(4,128)S(1)}, f32[1,4,1152]{2,1,0:T(4,128)S(1)}, u32[]{:S(2)}, u32[]{:S(2)}) collective-permute-start(f32[1,4,1152]{2,1,0:T(4,128)S(1)} %constant_dynamic-slice_fusion), channel_id=1, source_target_pairs={{0,8},{1,9},{2,10},{3,11},{4,12},{5,13},{6,14},{7,15},{8,0},{9,1},... | collective-permute-start | bytes 55304 | tf_op jit(solution)/shard_map/ppermute | solution.py:422

commit v11 on v10

--- a/solution.py
+++ b/solution.py
@@ -23,23 +23,34 @@
     return list(range(blocks))
 
 
+def spread_copies(source, target, sent):
+    count = sent.shape[0]
+    rows = target.shape[0] // count
+    return [
+        pltpu.make_async_copy(
+            source.at[pl.ds(at * rows, rows)], target.at[pl.ds(at * rows, rows)], sent.at[at]
+        )
+        for at in range(count)
+    ]
+
+
 def message_kernel(
     tags_ref, noise_ref, sig_ref, rows_ref,
-    first_ref, second_ref, near_noise_ref, near_sig_ref, tags, sent,
+    first_ref, second_ref, near_noise_ref, near_sig_ref, tags, sent, spread,
 ):
     height, span = first_ref.shape
     copies = [
-        pltpu.make_async_copy(rows_ref.at[:, :span], first_ref, sent.at[0]),
-        pltpu.make_async_copy(rows_ref.at[:, span:], second_ref.at[:, :span], sent.at[1]),
-        pltpu.make_async_copy(tags_ref, tags, sent.at[2]),
-        pltpu.make_async_copy(noise_ref, near_noise_ref, sent.at[3]),
-        pltpu.make_async_copy(sig_ref, near_sig_ref, sent.at[4]),
+        pltpu.make_async_copy(tags_ref, tags, sent.at[0]),
+        pltpu.make_async_copy(noise_ref, near_noise_ref, sent.at[1]),
+        pltpu.make_async_copy(sig_ref, near_sig_ref, sent.at[2]),
+        *spread_copies(rows_ref.at[:, :span], first_ref, spread.at[0]),
+        *spread_copies(rows_ref.at[:, span:], second_ref.at[:, :span], spread.at[1]),
     ]
     for copy in copies:
         copy.start()
-    copies[2].wait()
+    copies[0].wait()
     second_ref[:, span:] = tag_rows(tags, height).astype(jnp.bfloat16)
-    for copy in copies[:2] + copies[3:]:
+    for copy in copies[1:]:
         copy.wait()
 
 
@@ -56,7 +67,11 @@
             pltpu.VMEM(noise.shape, noise.dtype),
             pltpu.VMEM(significant.shape, significant.dtype),
         ],
-        scratch_shapes=[pltpu.VMEM(tags.shape, tags.dtype), pltpu.SemaphoreType.DMA((5,))],
+        scratch_shapes=[
+            pltpu.VMEM(tags.shape, tags.dtype),
+            pltpu.SemaphoreType.DMA((3,)),
+            pltpu.SemaphoreType.DMA((2, 4)),
+        ],
         compiler_params=pltpu.CompilerParams(vmem_limit_bytes=SMALL_LIMIT),
     )(
         *(
@@ -163,20 +178,22 @@
     steps, _, width = near.shape
     low = quarters[0] * span
 
-    def copy(step):
+    def copies(step):
         columns = pl.ds(pl.multiple_of(low + step * width, width), width)
-        return pltpu.make_async_copy(far_ref.at[:, columns], near.at[step], arrived.at[step])
+        return spread_copies(far_ref.at[:, columns], near.at[step], arrived.at[step])
 
     def following(step):
         columns = pl.ds(low + (steps + step) * width, width)
-        return pltpu.make_async_copy(far_ref.at[:, columns], next_ref.at[step], late.at[step])
+        return spread_copies(far_ref.at[:, columns], next_ref.at[step], late.at[step])
 
     if first:
         for step in range(steps):
-            copy(step).start()
+            for copy in copies(step):
+                copy.start()
     if not last:
         for step in range(next_ref.shape[0]):
-            following(step).start()
+            for copy in following(step):
+                copy.start()
     if first:
         pick_words(sig_ref, words_ref)
         acc[...] = jnp.zeros_like(acc)
@@ -190,7 +207,8 @@
         def _(inner):
             step = (quarter - quarters[0]) * (span // width) + inner
             if first:
-                copy(step).wait()
+                for copy in copies(step):
+                    copy.wait()
             for strip in range(0, width, STRIP):
                 there = pl.ds(pl.multiple_of(inner * width + strip, STRIP), STRIP)
                 part = quarter % 2 * span + inner * width + strip
@@ -203,7 +221,8 @@
 
     if not last:
         for step in range(next_ref.shape[0]):
-            following(step).wait()
+            for copy in following(step):
+                copy.wait()
         return
     tags = tag_rows(tags_ref, height)
     hit = picked_rows(words_ref, where_ref[0], height)
@@ -233,8 +252,8 @@
         rest_specs = [in_vmem()]
         scratch = [
             pltpu.VMEM((2 * steps, per_device, width), particles.dtype),
-            pltpu.SemaphoreType.DMA((2 * steps,)),
-            pltpu.SemaphoreType.DMA((steps,)),
+            pltpu.SemaphoreType.DMA((2 * steps, 4)),
+            pltpu.SemaphoreType.DMA((steps, 4)),
         ]
     elif last:
         rows = STATE_ROWS + rest[2].shape[0]
@@ -244,7 +263,7 @@
     else:
         shapes = sums + turned + [raw]
         rest_specs = [in_vmem()] * 3
-        scratch = [pltpu.SemaphoreType.DMA((steps,))]
+        scratch = [pltpu.SemaphoreType.DMA((steps, 4))]
     if not first:
         rest = (*rest[:-1], pltpu.with_memory_space_constraint(rest[-1], pltpu.VMEM))
     return pl.pallas_call(
@@ -262,40 +281,48 @@
     )(where, noise, templates, pltpu.with_memory_space_constraint(particles, pltpu.HBM), *rest)
 
 
-def near_copy(block, far_ref, near, arrived):
-    width = near.shape[1]
-    return pltpu.make_async_copy(far_ref.at[:, pl.ds(block * width, width)], near, arrived)
-
-
-def swapped_bits(block, core):
-    low, next_low = lax.rem(block, 2), lax.rem(lax.div(block, 2), 2)
-    return block + jnp.where(core == 1, next_low - low, 0) + 2 * jnp.where(core == 1, low - next_low, 0)
-
-
-def class_sums(state, core, nears, last_copy, loglik_ref, mine_ref, theirs_ref):
-    top, total, _, weights = state
-    loglik_ref[...] = top + jnp.log(total)
-    per_owner = mine_ref.shape[1]
-    width = nears[0].shape[1]
+def class_weights(state, core, per_owner):
+    _, _, _, weights = state
     weights = weights / jnp.sum(weights, axis=0, keepdims=True)
     turned = jnp.concatenate([weights[per_owner:], weights[:per_owner]], axis=0)
     weights = jnp.where(core == 0, weights, turned)
-    rounded = weights.astype(jnp.bfloat16)
-    totals = jnp.broadcast_to(
-        jnp.sum(weights, axis=1, keepdims=True), (weights.shape[0], LANES)
-    )
+    totals = jnp.sum(weights, axis=1, keepdims=True)
+    return weights.astype(jnp.bfloat16), jnp.broadcast_to(totals, (weights.shape[0], LANES))
+
+
+def class_sums(rounded, totals, nears, mine_ref, theirs_ref):
+    per_owner = mine_ref.shape[1]
     for block, near in enumerate(nears):
-        if block == len(nears) - 1:
-            last_copy.wait()
+        width = near.shape[1]
         sums = jnp.dot(rounded, near[...], preferred_element_type=jnp.float32)
-        for ref, rows, owner in ((mine_ref, slice(0, per_owner), core),
-                                 (theirs_ref, slice(per_owner, None), 1 - core)):
-            at = swapped_bits(jnp.int32(block), owner)
-            ref[at, :, :width] = sums[rows]
-            ref[at, :, width:] = totals[rows]
-
-
-def ring_kernel(phase, ends, block, sources, where_ref, noise_ref, low_ref, high_ref, *rest):
+        mine_ref[block, :, :width] = sums[:per_owner]
+        theirs_ref[block, :, :width] = sums[per_owner:]
+        mine_ref[block, :, width:] = totals[:per_owner]
+        theirs_ref[block, :, width:] = totals[per_owner:]
+
+
+def rest_kernel(rounded_ref, totals_ref, *rest):
+    *nears, mine_ref, theirs_ref = rest
+    class_sums(rounded_ref[...], totals_ref[...], nears, mine_ref, theirs_ref)
+
+
+def rest_sums(rounded, totals, nears, piece):
+    per_device, width = nears[0].shape
+    return pl.pallas_call(
+        rest_kernel,
+        in_specs=[in_vmem()] * (2 + len(nears)),
+        out_specs=[in_vmem()] * 2,
+        out_shape=[piece, piece],
+        compiler_params=pltpu.CompilerParams(vmem_limit_bytes=SMALL_LIMIT),
+        cost_estimate=pl.CostEstimate(
+            flops=2 * 128 * per_device * width * len(nears),
+            bytes_accessed=per_device * width * len(nears),
+            transcendentals=0,
+        ),
+    )(rounded, totals, *(pltpu.with_memory_space_constraint(x, pltpu.VMEM) for x in nears))
+
+
+def ring_kernel(phase, ends, slot, sources, where_ref, noise_ref, low_ref, high_ref, *rest):
     row_refs, rest = rest[: 2 * len(sources)], rest[2 * len(sources) :]
     far_ref, *rest = rest
     if phase == 0:
@@ -303,11 +330,18 @@
     else:
         acc_in, energy_in, logs_ref, words_ref, state_ref, *rest = rest
         if ends:
-            *nears, loglik_ref, mine_ref, theirs_ref, acc, energy, near, arrived = rest
+            *nears, loglik_ref, mine_ref, theirs_ref, rounded_ref, totals_ref = rest[:-4]
+            near, acc, energy, arrived = rest[-4:]
         else:
             out_ref, near, acc, energy, arrived = rest
-    copy = near_copy(block, far_ref, near, arrived)
-    copy.start()
+    width = near.shape[1]
+    slots = len(sources[0][0])
+    bit = lax.rem(where_ref[0], 2)
+    block = 2 * (slot % (slots // 2)) + (1 - bit if slot < slots // 2 else bit)
+    columns = pl.ds(pl.multiple_of(block * width, width), width)
+    copies = spread_copies(far_ref.at[:, columns], near, arrived)
+    for copy in copies:
+        copy.start()
     if phase == 0:
         acc[...] = jnp.zeros_like(acc)
         energy[...] = jnp.zeros_like(energy)
@@ -329,9 +363,9 @@
             weighted = weigh(rows, noise_ref[:, columns], energy)
             acc[...] += jnp.dot(weighted, part_ref[there, :], preferred_element_type=jnp.float32)
 
-    if not (ends and phase == 1):
-        copy.wait()
     if phase == 0:
+        for copy in copies:
+            copy.wait()
         return
     height = row_refs[0].shape[0]
     span = quarter if ends else 2 * quarter
@@ -354,12 +388,18 @@
     hit = jnp.concatenate([picked_rows(words_ref, source, height) for source in found], axis=0)
     state = add_rows(tags, hit, logs_ref, get_state(state_ref), acc, energy)
     if ends:
-        class_sums(state, core, [*nears, near], copy, loglik_ref, mine_ref, theirs_ref)
+        loglik_ref[...] = state[0] + jnp.log(state[1])
+        rounded, totals = class_weights(state, core, mine_ref.shape[1])
+        rounded_ref[...] = rounded
+        totals_ref[...] = totals
+        class_sums(rounded, totals, nears, mine_ref, theirs_ref)
     else:
         put_state(state, out_ref)
-
-
-def ring_scores(phase, sources, where, noise, turned, arrays, rest, ends, particles, block, shape):
+    for copy in copies:
+        copy.wait()
+
+
+def ring_scores(phase, sources, where, noise, turned, arrays, rest, ends, particles, slot, piece):
     quarter, per_device = turned[0].shape
     freqs = 4 * quarter
     rows = arrays[0].shape[0] * (1 if ends else len(arrays))
@@ -368,24 +408,30 @@
         jax.ShapeDtypeStruct((rows, LANES), jnp.float32),
     ]
     scratch = [pltpu.VMEM(array.shape, array.dtype) for array in sums]
-    raw = pltpu.VMEM((per_device, freqs // shape[0]), particles.dtype)
+    raw = pltpu.VMEM((per_device, freqs // len(sources[0][0])), particles.dtype)
     specs = [pl.BlockSpec(memory_space=pl.ANY)]
     if phase == 0:
         shapes, scratch = sums + [raw], []
     else:
         specs += [in_vmem(), in_vmem(), in_smem(), in_vmem(), in_vmem()]
         if ends:
-            piece = jax.ShapeDtypeStruct(shape, jnp.float32)
-            shapes = [jax.ShapeDtypeStruct((1, per_device), jnp.float32), piece, piece]
+            classes = rest[2].shape[0]
+            shapes = [
+                jax.ShapeDtypeStruct((1, per_device), jnp.float32),
+                piece,
+                piece,
+                jax.ShapeDtypeStruct((classes, per_device), jnp.bfloat16),
+                jax.ShapeDtypeStruct((classes, LANES), jnp.float32),
+                raw,
+            ]
             nears = [pltpu.with_memory_space_constraint(x, pltpu.VMEM) for x in rest[5:]]
             specs += [in_vmem()] * len(nears)
             rest = (*rest[:5], *nears)
-            scratch.append(raw)
         else:
             shapes = [jax.ShapeDtypeStruct(rest[4].shape, jnp.float32), raw]
-    scratch.append(pltpu.SemaphoreType.DMA)
+    scratch.append(pltpu.SemaphoreType.DMA((8,)))
     return pl.pallas_call(
-        functools.partial(ring_kernel, phase, ends, block, sources),
+        functools.partial(ring_kernel, phase, ends, slot, sources),
         in_specs=[in_smem()] + [in_vmem()] * (3 + len(arrays)) + specs,
         out_specs=[in_vmem()] * len(shapes),
         out_shape=shapes,
@@ -406,20 +452,18 @@
     )
 
 
-def scatter_sum(pieces, blocks, block_id, core):
+def scatter_sum(pieces, blocks, bits):
     tail = pieces.shape[1:]
-    place = swapped_bits(block_id, core)
-    for step in range(blocks.bit_length() - 1):
-        bit = lax.rem(lax.div(place, 1 << step), 2)
+    zero = jnp.uint32(0)
+    for step, (bit, other) in enumerate(bits):
         pairs = pieces.reshape((-1, 2) + tail)
-        keep = lax.dynamic_index_in_dim(pairs, bit, 1, keepdims=False)
-        send = lax.dynamic_index_in_dim(pairs, 1 - bit, 1, keepdims=False)
-        swaps = []
-        for block in range(blocks):
-            for owner in range(2):
-                change = (2, 1)[step] if owner == 1 and step < 2 else 1 << step
-                swaps.append((2 * block + owner, 2 * (block ^ change) + owner))
-        pieces = keep + lax.ppermute(send, ("blk", "cls"), swaps)
+        size = (pairs.shape[0], 1) + tail
+        keep, send = (
+            lax.dynamic_slice(pairs, (zero, which, zero, zero), size).reshape((-1,) + tail)
+            for which in (bit, other)
+        )
+        swaps = [(block, block ^ (2 << step)) for block in range(blocks)]
+        pieces = keep + lax.ppermute(send, "blk", swaps)
     return pieces[0]
 
 
@@ -442,7 +486,14 @@
     *held, near_noise, picks = make_messages(tags, noise, significant, templates)
     where = jnp.stack([block_id, core])
     cut = freqs // 4
-    where, cut_at = lax.optimization_barrier((where, core.astype(jnp.uint32) * cut))
+    per_owner = classes // owners
+    counts = lax.dynamic_slice_in_dim(class_counts, core * per_owner, per_owner, 0)
+    bits = [
+        lax.rem(lax.div(block_id, 2 << step), 2) for step in range(blocks.bit_length() - 2)
+    ]
+    bits = [(bit.astype(jnp.uint32), (1 - bit).astype(jnp.uint32)) for bit in bits]
+    cut_at = core.astype(jnp.uint32) * cut
+    where, cut_at, bits, counts = lax.optimization_barrier((where, cut_at, bits, counts))
     own = functools.partial(own_scores, where=where, noise=near_noise, particles=particles)
     total = blocks * templates.shape[0]
     words, *sums, low, high, raw = own([0, 1], templates=held[0], rest=(picks,), total=total)
@@ -454,8 +505,7 @@
     turned.append((low, high))
     gates.append(state)
     width = freqs // blocks
-    per_owner = classes // owners
-    shape = (blocks, per_owner, width + LANES)
+    piece = jax.ShapeDtypeStruct((blocks // 2, per_owner, width + LANES), jnp.float32)
     nears = []
     last = blocks // 2
     for distance in range(1, last + 1):
@@ -483,10 +533,10 @@
             arrived.append(own)
             rest = (*sums, logs, words, state) if phase else ()
             if ends and phase:
-                rest += tuple(nears)
+                rest += tuple(nears[: blocks // 2])
             *sums, near = ring_scores(
                 phase, tables, where, near_noise, turned[phase], pair, rest,
-                ends, particles, len(nears), shape,
+                ends, particles, len(nears), piece,
             )
             gates.append(sums)
             nears.append(near)
@@ -494,10 +544,13 @@
         if not ends:
             (state,) = sums
 
-    loglik, mine, theirs = (*sums, near)
-    reduced = mine + lax.ppermute(theirs, "cls", swap)
-    total = scatter_sum(reduced, blocks, block_id, core)
-    counts = lax.dynamic_slice_in_dim(class_counts, core * per_owner, per_owner, 0)
+    loglik, mine, theirs, rounded, totals = sums
+    given = lax.ppermute(theirs, "cls", swap)
+    across = lax.ppermute(mine + given, "blk", [(i, i ^ 1) for i in range(blocks)])
+    rounded, _ = lax.optimization_barrier((rounded, given))
+    mine, theirs = rest_sums(rounded, totals, nears[blocks // 2 :], piece)
+    kept = lax.optimization_barrier(mine + across)
+    total = scatter_sum(kept + lax.ppermute(theirs, "cls", swap), blocks, bits)
     class_avg = total[:, :width] / (total[:, width] + counts.astype(jnp.float32))[:, None]
     return loglik[0], class_avg
 

time: 75.8 us -> 78.8 us (1.040)
  Pallas kernels: 40 us -> 44.7 us
  waiting for transfers between devices: 12.1 us -> 9.64 us
    pallas_call x8 -> x9, Pallas kernels: 27 us -> 31.2 us  [the longest x8 30 us: ring_scores(): pl.pallas_call(functools.partial(ring_kernel, phase, ends, slot, sources)...]
    ppermute x4 -> x5, waiting for transfers between devices: 10.3 us -> 8.93 us  [the longest x2 5.44 us: scatter_sum(): pieces = keep + lax.ppermute(send, 'blk', swaps)]
    ppermute x8, waiting for transfers between devices: 1.83 us -> 0.69 us  [body(): own = lax.ppermute(message, ('blk', 'cls'), ring)]
    ppermute x4 -> x5, starting transfers between devices: 4.31 us -> 4.37 us  [the longest x2 3.31 us: scatter_sum(): pieces = keep + lax.ppermute(send, 'blk', swaps)]
  transfers between devices with their start and end apart: 20 -> 21, of which waited for: 7 -> 6; matrix products, arithmetic and copies ran while one was open for 0% -> 1% of each run, Pallas kernels for 44% -> 48%
where the time goes in v11:
time: 78.8 us; the launch traced here: 78.4 us
  Pallas kernels  44.7 us (57%)
  starting transfers between devices  21.1 us (27%)
  waiting for transfers between devices  9.64 us (12%)
  local copies, waits for them, and re-layouts  1.16 us (1%)
  between operations  0.89 us (1%)
  other arithmetic  0.86 us (1%)
    pallas_call x8, Pallas kernels, ring_scores(): pl.pallas_call(functools.partial(ring_kernel, phase, ends, slot, sources)...  30 us
    ppermute x8, starting transfers between devices, body(): own = lax.ppermute(message, ('blk', 'cls'), ring)  15.2 us
    pallas_call x3, Pallas kernels, own_scores(): pl.pallas_call(functools.partial(own_kernel, quarters), in_specs=[in_smem...  12.1 us
    ppermute x2, waiting for transfers between devices, scatter_sum(): pieces = keep + lax.ppermute(send, 'blk', swaps)  5.44 us
    ppermute x2, starting transfers between devices, scatter_sum(): pieces = keep + lax.ppermute(send, 'blk', swaps)  3.31 us
    ppermute x1, waiting for transfers between devices, body(): lax.ppermute(mine + given, 'blk', [(i, i ^ 1) for i in range(blocks)])  2.25 us
  transfers between devices with their start and end apart: 21, of which 6 were waited for; matrix products, arithmetic and copies ran while one was open for 1% of the time, Pallas kernels for 48%

profile of v11, /device:TPU:0, one launch (start us, length us, event | category | flops | bytes accessed | tf_op | source)
XLA Modules:
  0.0 78.4 jit_solution(10390480323767428097)
XLA Ops:
  2.1 3.1 %collective-permute-start.2 = (bf16[64,4096]{1,0:T(8,128)(2,1)S(1)}, bf16[64,4096]{1,0:T(8,128)(2,1)S(1)}, u32[]{:S(2)}, u32[]{:S(2)}) collective-permute-start(bf16[64,4096]{1,0:T(8,128)(2,1)S(1)} %get-tuple-element.63.tmpl_ref), channel_id=1, source_target_pairs={{0,4},{4,8},{8,12},{12,14},{14,10},{10,6},{6,2},{2,0},{5,1},{9,5},... | collective-permute-start | bytes 1572872 | tf_op jit(solution)/shard_map/ppermute | solution.py:528
  5.1 1.6 %collective-permute-start = (bf16[64,4224]{1,0:T(8,128)(2,1)S(1)}, bf16[64,4224]{1,0:T(8,128)(2,1)S(1)}, u32[]{:S(2)}, u32[]{:S(2)}) collective-permute-start(bf16[64,4224]{1,0:T(8,128)(2,1)S(1)} %get-tuple-element.62.tmpl_ref), channel_id=1, source_target_pairs={{0,4},{4,8},{8,12},{12,14},{14,10},{10,6},{6,2},{2,0},{5,1},{9,5},... | collective-permute-start | bytes 1622024 | tf_op jit(solution)/shard_map/ppermute | solution.py:528
  7.5 6.2 %shard_map.78 = (s32[16,1024]{1,0:T(8,128)S(1)}, f32[64,1024]{1,0:T(8,128)S(1)}, f32[64,128]{1,0:T(8,128)S(1)}, bf16[2048,1024]{1,0:T(8,128)(2,1)S(1)}, bf16[204...) custom-call(s32[2]{0:T(128)S(1)} %pad_add_fusion.where_ref, f32[1,8192]{1,0:T(1,128)S(1)} %get-tuple-element.61.noise_ref, ...), custom_call_target="tpu_custom_call" | custom-call | flops 2147483648 | bytes 8388608 | tf_op jit(solution)/shard_map/pallas_call | solution.py:269
  13.8 1.6 %collective-permute-start.6 = (bf16[64,4096]{1,0:T(8,128)(2,1)S(1)}, bf16[64,4096]{1,0:T(8,128)(2,1)S(1)}, u32[]{:S(2)}, u32[]{:S(2)}) collective-permute-start(bf16[64,4096]{1,0:T(8,128)(2,1)S(1)} %collective-permute-done.2.rest_0_), channel_id=1, source_target_pairs={{0,4},{4,8},{8,12},{12,14},{14,10},{10,6},{6,2},{2,0},{5,1},{9,5},... | collective-permute-start | bytes 1572872 | tf_op jit(solution)/shard_map/ppermute | solution.py:528
  15.4 2.8 %shard_map.79 = (f32[64,1024]{1,0:T(8,128)S(1)}, f32[64,128]{1,0:T(8,128)S(1)}, bf16[2048,1024]{1,0:T(8,128)(2,1)S(1)}, bf16[4,1024,512]{2,1,0:T(8,128)(2,1)S(1)}) custom-call(s32[2]{0:T(128)S(1)} %pad_add_fusion.where_ref, f32[1,8192]{1,0:T(1,128)S(1)} %get-tuple-element.61.noise_ref, bf16[64,4224]{1,0:T(8,128)(2,1)S(1)} %get-tuple-element.62.tmpl_ref, ...), custom_call_target="tpu_custom_call" | custom-call | flops 2147483648 | bytes 8388608 | tf_op jit(solution)/shard_map/pallas_call | solution.py:269
  18.9 1.5 %collective-permute-start.1 = (bf16[64,4224]{1,0:T(8,128)(2,1)S(1)}, bf16[64,4224]{1,0:T(8,128)(2,1)S(1)}, u32[]{:S(2)}, u32[]{:S(2)}) collective-permute-start(bf16[64,4224]{1,0:T(8,128)(2,1)S(1)} %collective-permute-done.rest_0_), channel_id=1, source_target_pairs={{0,4},{4,8},{8,12},{12,14},{14,10},{10,6},{6,2},{2,0},{5,1},{9,5},... | collective-permute-start | bytes 1622024 | tf_op jit(solution)/shard_map/ppermute | solution.py:528
  20.4 3.0 %shard_map.80 = (f32[16,1024]{1,0:T(8,128)S(1)}, bf16[2048,1024]{1,0:T(8,128)(2,1)S(1)}) custom-call(s32[2]{0:T(128)S(1)} %pad_add_fusion.where_ref, f32[1,8192]{1,0:T(1,128)S(1)} %get-tuple-element.61.noise_ref, bf16[64,4224]{1,0:T(8,128)(2,1)S(1)} %get-tuple-element.62.tmpl_ref, bf16[1024,8192]{1,0:T(8,128)(2,1)} %rest_2_.15, ...), custom_call_target="tpu_custom_call" | custom-call | flops 2147483648 | bytes 8388608 | tf_op jit(solution)/shard_map/pallas_call | solution.py:269
  23.7 2.1 %collective-permute-start.11 = (bf16[64,4096]{1,0:T(8,128)(2,1)S(1)}, bf16[64,4096]{1,0:T(8,128)(2,1)S(1)}, u32[]{:S(2)}, u32[]{:S(2)}) collective-permute-start(bf16[64,4096]{1,0:T(8,128)(2,1)S(1)} %collective-permute-done.6.rest_0_), channel_id=1, source_target_pairs={{0,4},{4,8},{8,12},{12,14},{14,10},{10,6},{6,2},{2,0},{5,1},{9,5},... | collective-permute-start | bytes 1572872 | tf_op jit(solution)/shard_map/ppermute | solution.py:528
  25.7 3.3 %shard_map.81 = (f32[128,1024]{1,0:T(8,128)S(1)}, f32[128,128]{1,0:T(8,128)S(1)}, bf16[1024,1024]{1,0:T(8,128)(2,1)S(1)}) custom-call(s32[2]{0:T(128)S(1)} %pad_add_fusion.where_ref, f32[1,8192]{1,0:T(1,128)S(1)} %get-tuple-element.61.noise_ref, bf16[2048,1024]{1,0:T(8,128)(2,1)S(1)} %get-tuple-element.75.low_ref, ...), custom_call_target="tpu_custom_call" | custom-call | flops 2147483648 | bytes 8388608 | tf_op jit(solution)/shard_map/pallas_call | solution.py:433
  29.5 2.1 %collective-permute-start.4 = (bf16[64,4224]{1,0:T(8,128)(2,1)S(1)}, bf16[64,4224]{1,0:T(8,128)(2,1)S(1)}, u32[]{:S(2)}, u32[]{:S(2)}) collective-permute-start(bf16[64,4224]{1,0:T(8,128)(2,1)S(1)} %collective-permute-done.1.rest_0_), channel_id=1, source_target_pairs={{0,4},{4,8},{8,12},{12,14},{14,10},{10,6},{6,2},{2,0},{5,1},{9,5},... | collective-permute-start | bytes 1622024 | tf_op jit(solution)/shard_map/ppermute | solution.py:528
  31.5 3.6 %shard_map.83 = (f32[16,1024]{1,0:T(8,128)S(1)}, bf16[1024,1024]{1,0:T(8,128)(2,1)S(1)}) custom-call(s32[2]{0:T(128)S(1)} %pad_add_fusion.where_ref, f32[1,8192]{1,0:T(1,128)S(1)} %get-tuple-element.61.noise_ref, bf16[2048,1024]{1,0:T(8,128)(2,1)S(1)} %get-tuple-element.68.low_ref, bf16[2048,1024]{1,0:T(8,128)(2,1)S(1)} %get-tuple-element.73.high_ref, ...), custom_call_target="tpu_custom_call" | custom-call | flops 2147483648 | bytes 8388608 | tf_op jit(solution)/shard_map/pallas_call | solution.py:433
  35.1 3.3 %shard_map.82 = (f32[128,1024]{1,0:T(8,128)S(1)}, f32[128,128]{1,0:T(8,128)S(1)}, bf16[1024,1024]{1,0:T(8,128)(2,1)S(1)}) custom-call(s32[2]{0:T(128)S(1)} %pad_add_fusion.where_ref, f32[1,8192]{1,0:T(1,128)S(1)} %get-tuple-element.61.noise_ref, bf16[2048,1024]{1,0:T(8,128)(2,1)S(1)} %get-tuple-element.75.low_ref, ...), custom_call_target="tpu_custom_call" | custom-call | flops 2147483648 | bytes 8388608 | tf_op jit(solution)/shard_map/pallas_call | solution.py:433
  38.8 1.5 %collective-permute-start.14 = (bf16[64,2048]{1,0:T(8,128)(2,1)S(1)}, bf16[64,2048]{1,0:T(8,128)(2,1)S(1)}, u32[]{:S(2)}, u32[]{:S(2)}) collective-permute-start(bf16[64,2048]{1,0:T(8,128)(2,1)S(1)} %constant_dynamic-slice_fusion.1), channel_id=1, source_target_pairs={{0,4},{4,8},{8,12},{12,14},{14,10},{10,6},{6,2},{2,0},{5,1},{9,5},... | collective-permute-start | bytes 786440 | tf_op jit(solution)/shard_map/ppermute | solution.py:528
  40.3 3.6 %shard_map.84 = (f32[16,1024]{1,0:T(8,128)S(1)}, bf16[1024,1024]{1,0:T(8,128)(2,1)S(1)}) custom-call(s32[2]{0:T(128)S(1)} %pad_add_fusion.where_ref, f32[1,8192]{1,0:T(1,128)S(1)} %get-tuple-element.61.noise_ref, bf16[2048,1024]{1,0:T(8,128)(2,1)S(1)} %get-tuple-element.68.low_ref, bf16[2048,1024]{1,0:T(8,128)(2,1)S(1)} %get-tuple-element.73.high_ref, ...), custom_call_target="tpu_custom_call" | custom-call | flops 2147483648 | bytes 8388608 | tf_op jit(solution)/shard_map/pallas_call | solution.py:433
  44.1 1.8 %collective-permute-start.9 = (bf16[64,2176]{1,0:T(8,128)(2,1)S(1)}, bf16[64,2176]{1,0:T(8,128)(2,1)S(1)}, u32[]{:S(2)}, u32[]{:S(2)}) collective-permute-start(bf16[64,2176]{1,0:T(8,128)(2,1)S(1)} %constant_dynamic-slice_fusion.2), channel_id=1, source_target_pairs={{0,4},{4,8},{8,12},{12,14},{14,10},{10,6},{6,2},{2,0},{5,1},{9,5},... | collective-permute-start | bytes 835592 | tf_op jit(solution)/shard_map/ppermute | solution.py:528
  46.0 3.3 %shard_map.85 = (f32[128,1024]{1,0:T(8,128)S(1)}, f32[128,128]{1,0:T(8,128)S(1)}, bf16[1024,1024]{1,0:T(8,128)(2,1)S(1)}) custom-call(s32[2]{0:T(128)S(1)} %pad_add_fusion.where_ref, f32[1,8192]{1,0:T(1,128)S(1)} %get-tuple-element.61.noise_ref, bf16[2048,1024]{1,0:T(8,128)(2,1)S(1)} %get-tuple-element.75.low_ref, ...), custom_call_target="tpu_custom_call" | custom-call | flops 2147483648 | bytes 8388608 | tf_op jit(solution)/shard_map/pallas_call | solution.py:433
  49.4 3.6 %shard_map.86 = (f32[16,1024]{1,0:T(8,128)S(1)}, bf16[1024,1024]{1,0:T(8,128)(2,1)S(1)}) custom-call(s32[2]{0:T(128)S(1)} %pad_add_fusion.where_ref, f32[1,8192]{1,0:T(1,128)S(1)} %get-tuple-element.61.noise_ref, bf16[2048,1024]{1,0:T(8,128)(2,1)S(1)} %get-tuple-element.68.low_ref, bf16[2048,1024]{1,0:T(8,128)(2,1)S(1)} %get-tuple-element.73.high_ref, ...), custom_call_target="tpu_custom_call" | custom-call | flops 2147483648 | bytes 8388608 | tf_op jit(solution)/shard_map/pallas_call | solution.py:433
  53.5 3.6 %shard_map.87 = (f32[64,1024]{1,0:T(8,128)S(1)}, f32[64,128]{1,0:T(8,128)S(1)}, bf16[1024,1024]{1,0:T(8,128)(2,1)S(1)}) custom-call(s32[2]{0:T(128)S(1)} %pad_add_fusion.where_ref, f32[1,8192]{1,0:T(1,128)S(1)} %get-tuple-element.61.noise_ref, bf16[2048,1024]{1,0:T(8,128)(2,1)S(1)} %get-tuple-element.75.low_ref, ...), custom_call_target="tpu_custom_call" | custom-call | flops 2147483648 | bytes 8388608 | tf_op jit(solution)/shard_map/pallas_call | solution.py:433
  57.1 5.8 %shard_map.88 = (f32[1,1024]{1,0:T(1,128)}, f32[4,4,1152]{2,1,0:T(4,128)S(1)}, f32[4,4,1152]{2,1,0:T(4,128)S(1)}, bf16[8,1024]{1,0:T(8,128)(2,1)S(1)}, f32[8,128...) custom-call(s32[2]{0:T(128)S(1)} %pad_add_fusion.where_ref, f32[1,8192]{1,0:T(1,128)S(1)} %get-tuple-element.61.noise_ref, ...), custom_call_target="tpu_custom_call" | custom-call | flops 2147483648 | bytes 8388608 | tf_op jit(solution)/shard_map/pallas_call | solution.py:433
  66.4 2.2 %collective-permute-done.17 = f32[4,4,1152]{2,1,0:T(4,128)S(1)} collective-permute-done((f32[4,4,1152]{2,1,0:T(4,128)S(1)}, f32[4,4,1152]{2,1,0:T(4,128)S(1)}, u32[]{:S(2)}, u32[]{:S(2)}) %collective-permute-start.17) | collective-permute-done | bytes 73760 | tf_op jit(solution)/shard_map/ppermute | solution.py:549
  68.8 1.6 %collective-permute-start.19 = (f32[2,4,1152]{2,1,0:T(4,128)S(1)}, f32[2,4,1152]{2,1,0:T(4,128)S(1)}, u32[]{:S(2)}, u32[]{:S(2)}) collective-permute-start(f32[2,4,1152]{2,1,0:T(4,128)S(1)} %dynamic-slice_bitcast_fusion), channel_id=1, source_target_pairs={{0,4},{2,6},{4,0},{6,2},{8,12},{10,14},{12,8},{14,10},{1,5},{3,7},... | collective-permute-start | bytes 110600 | tf_op jit(solution)/shard_map/ppermute | solution.py:466
  70.3 2.4 %collective-permute-done.19 = f32[2,4,1152]{2,1,0:T(4,128)S(1)} collective-permute-done((f32[2,4,1152]{2,1,0:T(4,128)S(1)}, f32[2,4,1152]{2,1,0:T(4,128)S(1)}, u32[]{:S(2)}, u32[]{:S(2)}) %collective-permute-start.19) | collective-permute-done | bytes 36896 | tf_op jit(solution)/shard_map/ppermute | solution.py:466
  72.8 1.7 %collective-permute-start.20 = (f32[1,4,1152]{2,1,0:T(4,128)S(1)}, f32[1,4,1152]{2,1,0:T(4,128)S(1)}, u32[]{:S(2)}, u32[]{:S(2)}) collective-permute-start(f32[1,4,1152]{2,1,0:T(4,128)S(1)} %constant_dynamic-slice_fusion), channel_id=1, source_target_pairs={{0,8},{2,10},{4,12},{6,14},{8,0},{10,2},{12,4},{14,6},{1,9},{3,11}... | collective-permute-start | bytes 55304 | tf_op jit(solution)/shard_map/ppermute | solution.py:466
  74.5 3.0 %collective-permute-done.20 = f32[1,4,1152]{2,1,0:T(4,128)S(1)} collective-permute-done((f32[1,4,1152]{2,1,0:T(4,128)S(1)}, f32[1,4,1152]{2,1,0:T(4,128)S(1)}, u32[]{:S(2)}, u32[]{:S(2)}) %collective-permute-start.20) | collective-permute-done | bytes 18464 | tf_op jit(solution)/shard_map/ppermute | solution.py:466
  (50 shorter events, 9.2 us)
Async XLA Ops:
  2.1 11.7 %collective-permute-start.2 = (bf16[64,4096]{1,0:T(8,128)(2,1)S(1)}, bf16[64,4096]{1,0:T(8,128)(2,1)S(1)}, u32[]{:S(2)}, u32[]{:S(2)}) collective-permute-start(bf16[64,4096]{1,0:T(8,128)(2,1)S(1)} %get-tuple-element.63.tmpl_ref), channel_id=1, source_target_pairs={{0,4},{4,8},{8,12},{12,14},{14,10},{10,6},{6,2},{2,0},{5,1},{9,5},... | collective-permute-start | bytes 1572872 | tf_op jit(solution)/shard_map/ppermute | solution.py:528
  5.1 13.2 %collective-permute-start = (bf16[64,4224]{1,0:T(8,128)(2,1)S(1)}, bf16[64,4224]{1,0:T(8,128)(2,1)S(1)}, u32[]{:S(2)}, u32[]{:S(2)}) collective-permute-start(bf16[64,4224]{1,0:T(8,128)(2,1)S(1)} %get-tuple-element.62.tmpl_ref), channel_id=1, source_target_pairs={{0,4},{4,8},{8,12},{12,14},{14,10},{10,6},{6,2},{2,0},{5,1},{9,5},... | collective-permute-start | bytes 1622024 | tf_op jit(solution)/shard_map/ppermute | solution.py:528
  13.8 9.9 %collective-permute-start.6 = (bf16[64,4096]{1,0:T(8,128)(2,1)S(1)}, bf16[64,4096]{1,0:T(8,128)(2,1)S(1)}, u32[]{:S(2)}, u32[]{:S(2)}) collective-permute-start(bf16[64,4096]{1,0:T(8,128)(2,1)S(1)} %collective-permute-done.2.rest_0_), channel_id=1, source_target_pairs={{0,4},{4,8},{8,12},{12,14},{14,10},{10,6},{6,2},{2,0},{5,1},{9,5},... | collective-permute-start | bytes 1572872 | tf_op jit(solution)/shard_map/ppermute | solution.py:528
  15.4 5.0 %copy-start.1 = (s32[8]{0:T(128)S(1)}, s32[8]{0:T(128)}, u32[]{:S(2)}) copy-start(s32[8]{0:T(128)} %param.10) | copy-start | bytes 100
  15.4 5.0 %copy-start = (s32[64]{0:T(128)S(1)}, s32[64]{0:T(128)}, u32[]{:S(2)}) copy-start(s32[64]{0:T(128)} %param.9) | copy-start | bytes 772
  18.3 7.5 %collective-permute-start.3 = (bf16[64,4096]{1,0:T(8,128)(2,1)S(1)}, bf16[64,4096]{1,0:T(8,128)(2,1)S(1)}, u32[]{:S(2)}, u32[]{:S(2)}) collective-permute-start(bf16[64,4096]{1,0:T(8,128)(2,1)S(1)} %collective-permute-done.2.rest_0_), channel_id=1, source_target_pairs={{0,1},{1,0},{2,3},{3,2},{4,5},{5,4},{6,7},{7,6},{8,9},{9,8},{10,11... | collective-permute-start | bytes 1572872 | tf_op jit(solution)/shard_map/ppermute | solution.py:532
  18.4 13.2 %collective-permute-start.8 = (bf16[64,4224]{1,0:T(8,128)(2,1)S(1)}, bf16[64,4224]{1,0:T(8,128)(2,1)S(1)}, u32[]{:S(2)}, u32[]{:S(2)}) collective-permute-start(bf16[64,4224]{1,0:T(8,128)(2,1)S(1)} %collective-permute-done.rest_0_), channel_id=1, source_target_pairs={{0,1},{1,0},{2,3},{3,2},{4,5},{5,4},{6,7},{7,6},{8,9},{9,8},{10,11... | collective-permute-start | bytes 1622024 | tf_op jit(solution)/shard_map/ppermute | solution.py:532
  18.9 10.6 %collective-permute-start.1 = (bf16[64,4224]{1,0:T(8,128)(2,1)S(1)}, bf16[64,4224]{1,0:T(8,128)(2,1)S(1)}, u32[]{:S(2)}, u32[]{:S(2)}) collective-permute-start(bf16[64,4224]{1,0:T(8,128)(2,1)S(1)} %collective-permute-done.rest_0_), channel_id=1, source_target_pairs={{0,4},{4,8},{8,12},{12,14},{14,10},{10,6},{6,2},{2,0},{5,1},{9,5},... | collective-permute-start | bytes 1622024 | tf_op jit(solution)/shard_map/ppermute | solution.py:528
  23.7 11.5 %collective-permute-start.7 = (bf16[64,4096]{1,0:T(8,128)(2,1)S(1)}, bf16[64,4096]{1,0:T(8,128)(2,1)S(1)}, u32[]{:S(2)}, u32[]{:S(2)}) collective-permute-start(bf16[64,4096]{1,0:T(8,128)(2,1)S(1)} %collective-permute-done.6.rest_0_), channel_id=1, source_target_pairs={{0,1},{1,0},{2,3},{3,2},{4,5},{5,4},{6,7},{7,6},{8,9},{9,8},{10,11... | collective-permute-start | bytes 1572872 | tf_op jit(solution)/shard_map/ppermute | solution.py:532
  23.7 14.8 %collective-permute-start.11 = (bf16[64,4096]{1,0:T(8,128)(2,1)S(1)}, bf16[64,4096]{1,0:T(8,128)(2,1)S(1)}, u32[]{:S(2)}, u32[]{:S(2)}) collective-permute-start(bf16[64,4096]{1,0:T(8,128)(2,1)S(1)} %collective-permute-done.6.rest_0_), channel_id=1, source_target_pairs={{0,4},{4,8},{8,12},{12,14},{14,10},{10,6},{6,2},{2,0},{5,1},{9,5},... | collective-permute-start | bytes 1572872 | tf_op jit(solution)/shard_map/ppermute | solution.py:528
  29.5 10.9 %collective-permute-start.5 = (bf16[64,4224]{1,0:T(8,128)(2,1)S(1)}, bf16[64,4224]{1,0:T(8,128)(2,1)S(1)}, u32[]{:S(2)}, u32[]{:S(2)}) collective-permute-start(bf16[64,4224]{1,0:T(8,128)(2,1)S(1)} %collective-permute-done.1.rest_0_), channel_id=1, source_target_pairs={{0,1},{1,0},{2,3},{3,2},{4,5},{5,4},{6,7},{7,6},{8,9},{9,8},{10,11... | collective-permute-start | bytes 1622024 | tf_op jit(solution)/shard_map/ppermute | solution.py:532
  29.5 14.4 %collective-permute-start.4 = (bf16[64,4224]{1,0:T(8,128)(2,1)S(1)}, bf16[64,4224]{1,0:T(8,128)(2,1)S(1)}, u32[]{:S(2)}, u32[]{:S(2)}) collective-permute-start(bf16[64,4224]{1,0:T(8,128)(2,1)S(1)} %collective-permute-done.1.rest_0_), channel_id=1, source_target_pairs={{0,4},{4,8},{8,12},{12,14},{14,10},{10,6},{6,2},{2,0},{5,1},{9,5},... | collective-permute-start | bytes 1622024 | tf_op jit(solution)/shard_map/ppermute | solution.py:528
  38.5 7.5 %collective-permute-start.12 = (bf16[64,4096]{1,0:T(8,128)(2,1)S(1)}, bf16[64,4096]{1,0:T(8,128)(2,1)S(1)}, u32[]{:S(2)}, u32[]{:S(2)}) collective-permute-start(bf16[64,4096]{1,0:T(8,128)(2,1)S(1)} %collective-permute-done.11.rest_0_), channel_id=1, source_target_pairs={{0,1},{1,0},{2,3},{3,2},{4,5},{5,4},{6,7},{7,6},{8,9},{9,8},{10,11... | collective-permute-start | bytes 1572872 | tf_op jit(solution)/shard_map/ppermute | solution.py:532
  38.8 10.4 %collective-permute-start.14 = (bf16[64,2048]{1,0:T(8,128)(2,1)S(1)}, bf16[64,2048]{1,0:T(8,128)(2,1)S(1)}, u32[]{:S(2)}, u32[]{:S(2)}) collective-permute-start(bf16[64,2048]{1,0:T(8,128)(2,1)S(1)} %constant_dynamic-slice_fusion.1), channel_id=1, source_target_pairs={{0,4},{4,8},{8,12},{12,14},{14,10},{10,6},{6,2},{2,0},{5,1},{9,5},... | collective-permute-start | bytes 786440 | tf_op jit(solution)/shard_map/ppermute | solution.py:528
  43.9 5.4 %collective-permute-start.10 = (bf16[64,4224]{1,0:T(8,128)(2,1)S(1)}, bf16[64,4224]{1,0:T(8,128)(2,1)S(1)}, u32[]{:S(2)}, u32[]{:S(2)}) collective-permute-start(bf16[64,4224]{1,0:T(8,128)(2,1)S(1)} %collective-permute-done.4.rest_0_), channel_id=1, source_target_pairs={{0,1},{1,0},{2,3},{3,2},{4,5},{5,4},{6,7},{7,6},{8,9},{9,8},{10,11... | collective-permute-start | bytes 1622024 | tf_op jit(solution)/shard_map/ppermute | solution.py:532
  44.1 8.8 %collective-permute-start.9 = (bf16[64,2176]{1,0:T(8,128)(2,1)S(1)}, bf16[64,2176]{1,0:T(8,128)(2,1)S(1)}, u32[]{:S(2)}, u32[]{:S(2)}) collective-permute-start(bf16[64,2176]{1,0:T(8,128)(2,1)S(1)} %constant_dynamic-slice_fusion.2), channel_id=1, source_target_pairs={{0,4},{4,8},{8,12},{12,14},{14,10},{10,6},{6,2},{2,0},{5,1},{9,5},... | collective-permute-start | bytes 835592 | tf_op jit(solution)/shard_map/ppermute | solution.py:528
  49.3 4.2 %collective-permute-start.15 = (bf16[64,2048]{1,0:T(8,128)(2,1)S(1)}, bf16[64,2048]{1,0:T(8,128)(2,1)S(1)}, u32[]{:S(2)}, u32[]{:S(2)}) collective-permute-start(bf16[64,2048]{1,0:T(8,128)(2,1)S(1)} %collective-permute-done.14.rest_0_), channel_id=1, source_target_pairs={{0,1},{1,0},{2,3},{3,2},{4,5},{5,4},{6,7},{7,6},{8,9},{9,8},{10,11... | collective-permute-start | bytes 786440 | tf_op jit(solution)/shard_map/ppermute | solution.py:532
  53.0 4.2 %collective-permute-start.13 = (bf16[64,2176]{1,0:T(8,128)(2,1)S(1)}, bf16[64,2176]{1,0:T(8,128)(2,1)S(1)}, u32[]{:S(2)}, u32[]{:S(2)}) collective-permute-start(bf16[64,2176]{1,0:T(8,128)(2,1)S(1)} %collective-permute-done.9.rest_0_), channel_id=1, source_target_pairs={{0,1},{1,0},{2,3},{3,2},{4,5},{5,4},{6,7},{7,6},{8,9},{9,8},{10,11... | collective-permute-start | bytes 835592 | tf_op jit(solution)/shard_map/ppermute | solution.py:532
  62.9 1.3 %collective-permute-start.16 = (f32[4,4,1152]{2,1,0:T(4,128)S(1)}, f32[4,4,1152]{2,1,0:T(4,128)S(1)}, u32[]{:S(2)}, u32[]{:S(2)}) collective-permute-start(f32[4,4,1152]{2,1,0:T(4,128)S(1)} %get-tuple-element.103), channel_id=1, source_target_pairs={{0,1},{1,0},{2,3},{3,2},{4,5},{5,4},{6,7},{7,6},{8,9},{9,8},{10,11... | collective-permute-start | bytes 221192 | tf_op jit(solution)/shard_map/ppermute | solution.py:548
  64.3 4.4 %collective-permute-start.17 = (f32[4,4,1152]{2,1,0:T(4,128)S(1)}, f32[4,4,1152]{2,1,0:T(4,128)S(1)}, u32[]{:S(2)}, u32[]{:S(2)}) collective-permute-start(f32[4,4,1152]{2,1,0:T(4,128)S(1)} %add.22), channel_id=1, source_target_pairs={{0,2},{2,0},{4,6},{6,4},{8,10},{10,8},{12,14},{14,12},{1,3},{3,1},... | collective-permute-start | bytes 221192 | tf_op jit(solution)/shard_map/ppermute | solution.py:549
  66.3 2.4 %collective-permute-start.18 = (f32[4,4,1152]{2,1,0:T(4,128)S(1)}, f32[4,4,1152]{2,1,0:T(4,128)S(1)}, u32[]{:S(2)}, u32[]{:S(2)}) collective-permute-start(f32[4,4,1152]{2,1,0:T(4,128)S(1)} %get-tuple-element.112), channel_id=1, source_target_pairs={{0,1},{1,0},{2,3},{3,2},{4,5},{5,4},{6,7},{7,6},{8,9},{9,8},{10,11... | collective-permute-start | bytes 221192 | tf_op jit(solution)/shard_map/ppermute | solution.py:553
  68.8 4.0 %collective-permute-start.19 = (f32[2,4,1152]{2,1,0:T(4,128)S(1)}, f32[2,4,1152]{2,1,0:T(4,128)S(1)}, u32[]{:S(2)}, u32[]{:S(2)}) collective-permute-start(f32[2,4,1152]{2,1,0:T(4,128)S(1)} %dynamic-slice_bitcast_fusion), channel_id=1, source_target_pairs={{0,4},{2,6},{4,0},{6,2},{8,12},{10,14},{12,8},{14,10},{1,5},{3,7},... | collective-permute-start | bytes 110600 | tf_op jit(solution)/shard_map/ppermute | solution.py:466
  72.8 4.7 %collective-permute-start.20 = (f32[1,4,1152]{2,1,0:T(4,128)S(1)}, f32[1,4,1152]{2,1,0:T(4,128)S(1)}, u32[]{:S(2)}, u32[]{:S(2)}) collective-permute-start(f32[1,4,1152]{2,1,0:T(4,128)S(1)} %constant_dynamic-slice_fusion), channel_id=1, source_target_pairs={{0,8},{2,10},{4,12},{6,14},{8,0},{10,2},{12,4},{14,6},{1,9},{3,11}... | collective-permute-start | bytes 55304 | tf_op jit(solution)/shard_map/ppermute | solution.py:466

commit v12 on v11

--- a/solution.py
+++ b/solution.py
@@ -13,8 +13,7 @@
 STRIP = 256
 LANES = 128
 STATE_ROWS = 8
-VMEM_LIMIT = 16 * 1024 * 1024
-SMALL_LIMIT = 6 * 1024 * 1024
+VMEM_LIMIT = 6 * 1024 * 1024
 
 
 def ring_order(blocks):
@@ -72,7 +71,7 @@
             pltpu.SemaphoreType.DMA((3,)),
             pltpu.SemaphoreType.DMA((2, 4)),
         ],
-        compiler_params=pltpu.CompilerParams(vmem_limit_bytes=SMALL_LIMIT),
+        compiler_params=pltpu.CompilerParams(vmem_limit_bytes=VMEM_LIMIT),
     )(
         *(
             pltpu.with_memory_space_constraint(x, pltpu.HBM)
@@ -168,7 +167,7 @@
 def own_kernel(quarters, where_ref, noise_ref, tmpl_ref, far_ref, *rest):
     first, last = quarters[0] == 0, quarters[-1] == 3
     if first:
-        sig_ref, words_ref, acc, energy, *turned_refs, next_ref, near, arrived, late = rest
+        sig_ref, words_ref, acc, energy, *turned_refs, near, next_ref, arrived, late = rest
     elif last:
         acc_in, energy_in, logs_ref, tags_ref, words_ref, near, out_ref, *rest = rest
         *turned_refs, acc, energy = rest
@@ -248,10 +247,9 @@
     raw = pltpu.VMEM((steps, per_device, width), particles.dtype)
     if first:
         shapes = [jax.ShapeDtypeStruct((total // 32, per_device), jnp.int32)] + sums
-        shapes += turned + [raw]
+        shapes += turned + [pltpu.VMEM((2 * steps, per_device, width), particles.dtype), raw]
         rest_specs = [in_vmem()]
         scratch = [
-            pltpu.VMEM((2 * steps, per_device, width), particles.dtype),
             pltpu.SemaphoreType.DMA((2 * steps, 4)),
             pltpu.SemaphoreType.DMA((steps, 4)),
         ]
@@ -272,7 +270,7 @@
         out_specs=[in_vmem()] * len(shapes),
         out_shape=shapes,
         scratch_shapes=scratch,
-        compiler_params=pltpu.CompilerParams(vmem_limit_bytes=VMEM_LIMIT if first else SMALL_LIMIT),
+        compiler_params=pltpu.CompilerParams(vmem_limit_bytes=VMEM_LIMIT),
         cost_estimate=pl.CostEstimate(
             flops=2 * 128 * per_device * freqs,
             bytes_accessed=per_device * freqs,
@@ -281,67 +279,78 @@
     )(where, noise, templates, pltpu.with_memory_space_constraint(particles, pltpu.HBM), *rest)
 
 
-def class_weights(state, core, per_owner):
+def class_weights(state, where_ref, counts_ref, per_owner):
     _, _, _, weights = state
+    classes = weights.shape[0]
+    row = lax.broadcasted_iota(jnp.int32, (classes, LANES), 0)
+    counts = jnp.zeros((classes, LANES), jnp.float32)
+    for tag in range(classes):
+        mine = (where_ref[0] == 0) & (where_ref[1] == tag // per_owner)
+        count = jnp.where(mine, counts_ref[tag], 0).astype(jnp.float32)
+        counts = jnp.where(row == tag, count, counts)
     weights = weights / jnp.sum(weights, axis=0, keepdims=True)
-    turned = jnp.concatenate([weights[per_owner:], weights[:per_owner]], axis=0)
-    weights = jnp.where(core == 0, weights, turned)
-    totals = jnp.sum(weights, axis=1, keepdims=True)
-    return weights.astype(jnp.bfloat16), jnp.broadcast_to(totals, (weights.shape[0], LANES))
-
-
-def class_sums(rounded, totals, nears, mine_ref, theirs_ref):
+    totals = jnp.sum(weights, axis=1, keepdims=True) + counts
+
+    def own_first(rows):
+        turned = jnp.concatenate([rows[per_owner:], rows[:per_owner]], axis=0)
+        return jnp.where(where_ref[1] == 0, rows, turned)
+
+    return own_first(weights).astype(jnp.bfloat16), own_first(totals)
+
+
+def class_sums(rounded, totals, bit, nears, mine_ref, theirs_ref):
     per_owner = mine_ref.shape[1]
-    for block, near in enumerate(nears):
-        width = near.shape[1]
-        sums = jnp.dot(rounded, near[...], preferred_element_type=jnp.float32)
-        mine_ref[block, :, :width] = sums[:per_owner]
-        theirs_ref[block, :, :width] = sums[per_owner:]
-        mine_ref[block, :, width:] = totals[:per_owner]
-        theirs_ref[block, :, width:] = totals[per_owner:]
-
-
-def rest_kernel(rounded_ref, totals_ref, *rest):
+    chunk = nears[0].shape[2]
+    share = mine_ref.shape[2] // chunk
+    piece = 0
+    for near in nears:
+        for pair in range(near.shape[0] // (2 * share)):
+            for part in range(share):
+                at = (2 * pair + bit) * share + part
+                sums = jnp.dot(rounded, near[at], preferred_element_type=jnp.float32)
+                columns = pl.ds(part * chunk, chunk)
+                mine_ref[piece, :, columns] = sums[:per_owner]
+                theirs_ref[piece, :, columns] = sums[per_owner:]
+            mine_ref[piece, :, share * chunk :] = totals[:per_owner]
+            theirs_ref[piece, :, share * chunk :] = totals[per_owner:]
+            piece += 1
+
+
+def rest_kernel(where_ref, rounded_ref, totals_ref, *rest):
     *nears, mine_ref, theirs_ref = rest
-    class_sums(rounded_ref[...], totals_ref[...], nears, mine_ref, theirs_ref)
-
-
-def rest_sums(rounded, totals, nears, piece):
-    per_device, width = nears[0].shape
+    bit = lax.rem(where_ref[0], 2)
+    class_sums(rounded_ref[...], totals_ref[...], bit, nears, mine_ref, theirs_ref)
+
+
+def rest_sums(where, rounded, totals, nears, piece):
+    classes, per_device = rounded.shape
+    blocks = 2 * piece.shape[0]
+    freqs = blocks * (piece.shape[2] - LANES)
     return pl.pallas_call(
         rest_kernel,
-        in_specs=[in_vmem()] * (2 + len(nears)),
+        in_specs=[in_smem()] + [in_vmem()] * (2 + len(nears)),
         out_specs=[in_vmem()] * 2,
         out_shape=[piece, piece],
-        compiler_params=pltpu.CompilerParams(vmem_limit_bytes=SMALL_LIMIT),
+        compiler_params=pltpu.CompilerParams(vmem_limit_bytes=VMEM_LIMIT),
         cost_estimate=pl.CostEstimate(
-            flops=2 * 128 * per_device * width * len(nears),
-            bytes_accessed=per_device * width * len(nears),
+            flops=128 * per_device * freqs,
+            bytes_accessed=per_device * freqs // 2,
             transcendentals=0,
         ),
-    )(rounded, totals, *(pltpu.with_memory_space_constraint(x, pltpu.VMEM) for x in nears))
-
-
-def ring_kernel(phase, ends, slot, sources, where_ref, noise_ref, low_ref, high_ref, *rest):
+    )(where, rounded, totals, *(pltpu.with_memory_space_constraint(x, pltpu.VMEM) for x in nears))
+
+
+def ring_kernel(phase, ends, sources, where_ref, noise_ref, low_ref, high_ref, *rest):
     row_refs, rest = rest[: 2 * len(sources)], rest[2 * len(sources) :]
-    far_ref, *rest = rest
     if phase == 0:
-        acc, energy, near, arrived = rest
+        acc, energy = rest
     else:
         acc_in, energy_in, logs_ref, words_ref, state_ref, *rest = rest
         if ends:
-            *nears, loglik_ref, mine_ref, theirs_ref, rounded_ref, totals_ref = rest[:-4]
-            near, acc, energy, arrived = rest[-4:]
+            counts_ref, *nears, loglik_ref, mine_ref, theirs_ref = rest[:-4]
+            rounded_ref, totals_ref, acc, energy = rest[-4:]
         else:
-            out_ref, near, acc, energy, arrived = rest
-    width = near.shape[1]
-    slots = len(sources[0][0])
-    bit = lax.rem(where_ref[0], 2)
-    block = 2 * (slot % (slots // 2)) + (1 - bit if slot < slots // 2 else bit)
-    columns = pl.ds(pl.multiple_of(block * width, width), width)
-    copies = spread_copies(far_ref.at[:, columns], near, arrived)
-    for copy in copies:
-        copy.start()
+            out_ref, acc, energy = rest
     if phase == 0:
         acc[...] = jnp.zeros_like(acc)
         energy[...] = jnp.zeros_like(energy)
@@ -364,8 +373,6 @@
             acc[...] += jnp.dot(weighted, part_ref[there, :], preferred_element_type=jnp.float32)
 
     if phase == 0:
-        for copy in copies:
-            copy.wait()
         return
     height = row_refs[0].shape[0]
     span = quarter if ends else 2 * quarter
@@ -389,17 +396,16 @@
     state = add_rows(tags, hit, logs_ref, get_state(state_ref), acc, energy)
     if ends:
         loglik_ref[...] = state[0] + jnp.log(state[1])
-        rounded, totals = class_weights(state, core, mine_ref.shape[1])
+        rounded, totals = class_weights(state, where_ref, counts_ref, mine_ref.shape[1])
         rounded_ref[...] = rounded
         totals_ref[...] = totals
-        class_sums(rounded, totals, nears, mine_ref, theirs_ref)
+        bit = 1 - lax.rem(where_ref[0], 2)
+        class_sums(rounded, totals, bit, nears, mine_ref, theirs_ref)
     else:
         put_state(state, out_ref)
-    for copy in copies:
-        copy.wait()
-
-
-def ring_scores(phase, sources, where, noise, turned, arrays, rest, ends, particles, slot, piece):
+
+
+def ring_scores(phase, sources, where, noise, turned, arrays, rest, ends, piece):
     quarter, per_device = turned[0].shape
     freqs = 4 * quarter
     rows = arrays[0].shape[0] * (1 if ends else len(arrays))
@@ -408,12 +414,11 @@
         jax.ShapeDtypeStruct((rows, LANES), jnp.float32),
     ]
     scratch = [pltpu.VMEM(array.shape, array.dtype) for array in sums]
-    raw = pltpu.VMEM((per_device, freqs // len(sources[0][0])), particles.dtype)
-    specs = [pl.BlockSpec(memory_space=pl.ANY)]
+    specs = []
     if phase == 0:
-        shapes, scratch = sums + [raw], []
-    else:
-        specs += [in_vmem(), in_vmem(), in_smem(), in_vmem(), in_vmem()]
+        shapes, scratch = sums, []
+    else:
+        specs = [in_vmem(), in_vmem(), in_smem(), in_vmem(), in_vmem()]
         if ends:
             classes = rest[2].shape[0]
             shapes = [
@@ -422,21 +427,19 @@
                 piece,
                 jax.ShapeDtypeStruct((classes, per_device), jnp.bfloat16),
                 jax.ShapeDtypeStruct((classes, LANES), jnp.float32),
-                raw,
             ]
-            nears = [pltpu.with_memory_space_constraint(x, pltpu.VMEM) for x in rest[5:]]
-            specs += [in_vmem()] * len(nears)
-            rest = (*rest[:5], *nears)
+            nears = [pltpu.with_memory_space_constraint(x, pltpu.VMEM) for x in rest[6:]]
+            specs += [in_smem()] + [in_vmem()] * len(nears)
+            rest = (*rest[:6], *nears)
         else:
-            shapes = [jax.ShapeDtypeStruct(rest[4].shape, jnp.float32), raw]
-    scratch.append(pltpu.SemaphoreType.DMA((8,)))
+            shapes = [jax.ShapeDtypeStruct(rest[4].shape, jnp.float32)]
     return pl.pallas_call(
-        functools.partial(ring_kernel, phase, ends, slot, sources),
+        functools.partial(ring_kernel, phase, ends, sources),
         in_specs=[in_smem()] + [in_vmem()] * (3 + len(arrays)) + specs,
         out_specs=[in_vmem()] * len(shapes),
         out_shape=shapes,
         scratch_shapes=scratch,
-        compiler_params=pltpu.CompilerParams(vmem_limit_bytes=SMALL_LIMIT),
+        compiler_params=pltpu.CompilerParams(vmem_limit_bytes=VMEM_LIMIT),
         cost_estimate=pl.CostEstimate(
             flops=2 * 128 * per_device * freqs,
             bytes_accessed=per_device * freqs,
@@ -447,7 +450,6 @@
         noise,
         *(pltpu.with_memory_space_constraint(part, pltpu.VMEM) for part in turned),
         *arrays,
-        pltpu.with_memory_space_constraint(particles, pltpu.HBM),
         *rest,
     )
 
@@ -487,26 +489,25 @@
     where = jnp.stack([block_id, core])
     cut = freqs // 4
     per_owner = classes // owners
-    counts = lax.dynamic_slice_in_dim(class_counts, core * per_owner, per_owner, 0)
     bits = [
         lax.rem(lax.div(block_id, 2 << step), 2) for step in range(blocks.bit_length() - 2)
     ]
     bits = [(bit.astype(jnp.uint32), (1 - bit).astype(jnp.uint32)) for bit in bits]
     cut_at = core.astype(jnp.uint32) * cut
-    where, cut_at, bits, counts = lax.optimization_barrier((where, cut_at, bits, counts))
+    where, cut_at, bits = lax.optimization_barrier((where, cut_at, bits))
     own = functools.partial(own_scores, where=where, noise=near_noise, particles=particles)
     total = blocks * templates.shape[0]
-    words, *sums, low, high, raw = own([0, 1], templates=held[0], rest=(picks,), total=total)
-    turned = [(low, high)]
+    words, *sums, low, high, near, raw = own([0, 1], templates=held[0], rest=(picks,), total=total)
+    turned, nears = [(low, high)], [near, raw]
     gates = [sums]
     *sums, low, raw = own([2], templates=held[1], rest=(*sums, raw))
+    nears.append(raw)
     gates.append(sums)
     state, high = own([3], templates=held[1], rest=(*sums, logs, tags, words, raw))
     turned.append((low, high))
     gates.append(state)
     width = freqs // blocks
     piece = jax.ShapeDtypeStruct((blocks // 2, per_owner, width + LANES), jnp.float32)
-    nears = []
     last = blocks // 2
     for distance in range(1, last + 1):
         ends = distance == last
@@ -533,13 +534,11 @@
             arrived.append(own)
             rest = (*sums, logs, words, state) if phase else ()
             if ends and phase:
-                rest += tuple(nears[: blocks // 2])
-            *sums, near = ring_scores(
-                phase, tables, where, near_noise, turned[phase], pair, rest,
-                ends, particles, len(nears), piece,
+                rest += (class_counts, *nears)
+            sums = ring_scores(
+                phase, tables, where, near_noise, turned[phase], pair, rest, ends, piece
             )
             gates.append(sums)
-            nears.append(near)
         held = arrived
         if not ends:
             (state,) = sums
@@ -548,10 +547,10 @@
     given = lax.ppermute(theirs, "cls", swap)
     across = lax.ppermute(mine + given, "blk", [(i, i ^ 1) for i in range(blocks)])
     rounded, _ = lax.optimization_barrier((rounded, given))
-    mine, theirs = rest_sums(rounded, totals, nears[blocks // 2 :], piece)
+    mine, theirs = rest_sums(where, rounded, totals, nears, piece)
     kept = lax.optimization_barrier(mine + across)
     total = scatter_sum(kept + lax.ppermute(theirs, "cls", swap), blocks, bits)
-    class_avg = total[:, :width] / (total[:, width] + counts.astype(jnp.float32))[:, None]
+    class_avg = total[:, :width] / total[:, width][:, None]
     return loglik[0], class_avg
 
 

time: 78.8 us -> 70 us (0.89)
  Pallas kernels: 44.7 us -> 34.3 us
  starting transfers between devices: 21.1 us -> 23.5 us
    pallas_call x9, Pallas kernels: 31.2 us -> 20.8 us  [the longest x8 19 us: ring_scores(): pl.pallas_call(functools.partial(ring_kernel, phase, ends, sources), in_s...]
    ppermute x8, waiting for transfers between devices: 0.69 us -> 3.29 us  [body(): own = lax.ppermute(message, ('blk', 'cls'), ring)]
    ppermute x1, waiting for transfers between devices: 2.25 us -> 0.96 us  [body(): lax.ppermute(mine + given, 'blk', [(i, i ^ 1) for i in range(blocks)])]
    ppermute x2, starting transfers between devices: 3.31 us -> 4.36 us  [scatter_sum(): pieces = keep + lax.ppermute(send, 'blk', swaps)]
    ppermute x2, waiting for transfers between devices: 5.44 us -> 4.39 us  [scatter_sum(): pieces = keep + lax.ppermute(send, 'blk', swaps)]
    ppermute x8, starting transfers between devices: 15.2 us -> 16.2 us  [body(): own = lax.ppermute(message, ('blk', 'cls'), ring)]
  transfers between devices with their start and end apart: 21 -> 21, of which waited for: 6 -> 9; matrix products, arithmetic and copies ran while one was open for 1% -> 1% of each run, Pallas kernels for 48% -> 42%
where the time goes in v12:
time: 70 us; the launch traced here: 69.8 us
  Pallas kernels  34.3 us (49%)
  starting transfers between devices  23.5 us (34%)
  waiting for transfers between devices  9.96 us (14%)
  other arithmetic  0.85 us (1%)
  between operations  0.79 us (1%)
    pallas_call x8, Pallas kernels, ring_scores(): pl.pallas_call(functools.partial(ring_kernel, phase, ends, sources), in_s...  19 us
    ppermute x8, starting transfers between devices, body(): own = lax.ppermute(message, ('blk', 'cls'), ring)  16.2 us
    pallas_call x3, Pallas kernels, own_scores(): pl.pallas_call(functools.partial(own_kernel, quarters), in_specs=[in_smem...  12.1 us
    ppermute x2, waiting for transfers between devices, scatter_sum(): pieces = keep + lax.ppermute(send, 'blk', swaps)  4.39 us
    ppermute x2, starting transfers between devices, scatter_sum(): pieces = keep + lax.ppermute(send, 'blk', swaps)  4.36 us
    ppermute x8, waiting for transfers between devices, body(): own = lax.ppermute(message, ('blk', 'cls'), ring)  3.29 us
    pallas_call x1, Pallas kernels, rest_sums(): pl.pallas_call(rest_kernel, in_specs=[in_smem()] + [in_vmem()] * (2 + len...  1.74 us
    ppermute x1, starting transfers between devices, body(): lax.ppermute(mine + given, 'blk', [(i, i ^ 1) for i in range(blocks)])  1.64 us
  transfers between devices with their start and end apart: 21, of which 9 were waited for; matrix products, arithmetic and copies ran while one was open for 1% of the time, Pallas kernels for 42%

profile of v12, /device:TPU:0, one launch (start us, length us, event | category | flops | bytes accessed | tf_op | source)
XLA Modules:
  0.0 69.8 jit_solution(2363199001646083732)
XLA Ops:
  2.1 3.1 %collective-permute-start.2 = (bf16[64,4096]{1,0:T(8,128)(2,1)S(1)}, bf16[64,4096]{1,0:T(8,128)(2,1)S(1)}, u32[]{:S(2)}, u32[]{:S(2)}) collective-permute-start(bf16[64,4096]{1,0:T(8,128)(2,1)S(1)} %get-tuple-element.52.tmpl_ref), channel_id=1, source_target_pairs={{0,4},{4,8},{8,12},{12,14},{14,10},{10,6},{6,2},{2,0},{5,1},{9,5},... | collective-permute-start | bytes 1572872 | tf_op jit(solution)/shard_map/ppermute | solution.py:529
  6.8 6.2 %shard_map.78 = (s32[16,1024]{1,0:T(8,128)S(1)}, f32[64,1024]{1,0:T(8,128)S(1)}, f32[64,128]{1,0:T(8,128)S(1)}, bf16[2048,1024]{1,0:T(8,128)(2,1)S(1)}, bf16[204...) custom-call(s32[2]{0:T(128)S(1)} %pad_add_fusion.where_ref, ...), custom_call_target="tpu_custom_call" | custom-call | flops 2147483648 | bytes 8388608 | tf_op jit(solution)/shard_map/pallas_call | solution.py:267
  13.0 1.6 %collective-permute-start.6 = (bf16[64,4096]{1,0:T(8,128)(2,1)S(1)}, bf16[64,4096]{1,0:T(8,128)(2,1)S(1)}, u32[]{:S(2)}, u32[]{:S(2)}) collective-permute-start(bf16[64,4096]{1,0:T(8,128)(2,1)S(1)} %collective-permute-done.2.rest_0_), channel_id=1, source_target_pairs={{0,4},{4,8},{8,12},{12,14},{14,10},{10,6},{6,2},{2,0},{5,1},{9,5},... | collective-permute-start | bytes 1572872 | tf_op jit(solution)/shard_map/ppermute | solution.py:529
  14.7 2.8 %shard_map.79 = (f32[64,1024]{1,0:T(8,128)S(1)}, f32[64,128]{1,0:T(8,128)S(1)}, bf16[2048,1024]{1,0:T(8,128)(2,1)S(1)}, bf16[4,1024,512]{2,1,0:T(8,128)(2,1)S(1)}) custom-call(s32[2]{0:T(128)S(1)} %pad_add_fusion.where_ref, f32[1,8192]{1,0:T(1,128)S(1)} %get-tuple-element.50.noise_ref, bf16[64,4224]{1,0:T(8,128)(2,1)S(1)} %get-tuple-element.51.tmpl_ref, ...), custom_call_target="tpu_custom_call" | custom-call | flops 2147483648 | bytes 8388608 | tf_op jit(solution)/shard_map/pallas_call | solution.py:267
  18.1 2.0 %collective-permute-start.1 = (bf16[64,4224]{1,0:T(8,128)(2,1)S(1)}, bf16[64,4224]{1,0:T(8,128)(2,1)S(1)}, u32[]{:S(2)}, u32[]{:S(2)}) collective-permute-start(bf16[64,4224]{1,0:T(8,128)(2,1)S(1)} %collective-permute-done.rest_0_), channel_id=1, source_target_pairs={{0,4},{4,8},{8,12},{12,14},{14,10},{10,6},{6,2},{2,0},{5,1},{9,5},... | collective-permute-start | bytes 1622024 | tf_op jit(solution)/shard_map/ppermute | solution.py:529
  20.1 3.0 %shard_map.80 = (f32[16,1024]{1,0:T(8,128)S(1)}, bf16[2048,1024]{1,0:T(8,128)(2,1)S(1)}) custom-call(s32[2]{0:T(128)S(1)} %pad_add_fusion.where_ref, f32[1,8192]{1,0:T(1,128)S(1)} %get-tuple-element.50.noise_ref, bf16[64,4224]{1,0:T(8,128)(2,1)S(1)} %get-tuple-element.51.tmpl_ref, bf16[1024,8192]{1,0:T(8,128)(2,1)} %far_ref.5, ...), custom_call_target="tpu_custom_call" | custom-call | flops 2147483648 | bytes 8388608 | tf_op jit(solution)/shard_map/pallas_call | solution.py:267
  23.7 2.1 %collective-permute-start.11 = (bf16[64,4096]{1,0:T(8,128)(2,1)S(1)}, bf16[64,4096]{1,0:T(8,128)(2,1)S(1)}, u32[]{:S(2)}, u32[]{:S(2)}) collective-permute-start(bf16[64,4096]{1,0:T(8,128)(2,1)S(1)} %collective-permute-done.6.rest_0_), channel_id=1, source_target_pairs={{0,4},{4,8},{8,12},{12,14},{14,10},{10,6},{6,2},{2,0},{5,1},{9,5},... | collective-permute-start | bytes 1572872 | tf_op jit(solution)/shard_map/ppermute | solution.py:529
  25.7 2.0 %shard_map.81 = (f32[128,1024]{1,0:T(8,128)S(1)}, f32[128,128]{1,0:T(8,128)S(1)}) custom-call(s32[2]{0:T(128)S(1)} %pad_add_fusion.where_ref, f32[1,8192]{1,0:T(1,128)S(1)} %get-tuple-element.50.noise_ref, bf16[2048,1024]{1,0:T(8,128)(2,1)S(1)} %get-tuple-element.64.low_ref, bf16[2048,1024]{1,0:T(8,128)(2,1)S(1)} %get-tuple-element.65.high_ref, ...), custom_call_target="tpu_custom_call" | custom-call | flops 2147483648 | bytes 8388608 | tf_op jit(solution)/shard_map/pallas_call | solution.py:436
  27.8 1.7 %collective-permute-done.1.rest_0_ = bf16[64,4224]{1,0:T(8,128)(2,1)S(1)} collective-permute-done((bf16[64,4224]{1,0:T(8,128)(2,1)S(1)}, bf16[64,4224]{1,0:T(8,128)(2,1)S(1)}, u32[]{:S(2)}, u32[]{:S(2)}) %collective-permute-start.1) | collective-permute-done | bytes 540704 | tf_op jit(solution)/shard_map/ppermute | solution.py:529
  29.5 2.1 %collective-permute-start.4 = (bf16[64,4224]{1,0:T(8,128)(2,1)S(1)}, bf16[64,4224]{1,0:T(8,128)(2,1)S(1)}, u32[]{:S(2)}, u32[]{:S(2)}) collective-permute-start(bf16[64,4224]{1,0:T(8,128)(2,1)S(1)} %collective-permute-done.1.rest_0_), channel_id=1, source_target_pairs={{0,4},{4,8},{8,12},{12,14},{14,10},{10,6},{6,2},{2,0},{5,1},{9,5},... | collective-permute-start | bytes 1622024 | tf_op jit(solution)/shard_map/ppermute | solution.py:529
  31.5 2.4 %shard_map.83.rest_6_ = f32[16,1024]{1,0:T(8,128)S(1)} custom-call(s32[2]{0:T(128)S(1)} %pad_add_fusion.where_ref, f32[1,8192]{1,0:T(1,128)S(1)} %get-tuple-element.50.noise_ref, bf16[2048,1024]{1,0:T(8,128)(2,1)S(1)} %get-tuple-element.57.low_ref, bf16[2048,1024]{1,0:T(8,128)(2,1)S(1)} %get-tuple-element.62.high_ref, ...), custom_call_target="tpu_custom_call" | custom-call | flops 2147483648 | bytes 8388608 | tf_op jit(solution)/shard_map/pallas_call | solution.py:436
  34.0 2.0 %shard_map.82 = (f32[128,1024]{1,0:T(8,128)S(1)}, f32[128,128]{1,0:T(8,128)S(1)}) custom-call(s32[2]{0:T(128)S(1)} %pad_add_fusion.where_ref, f32[1,8192]{1,0:T(1,128)S(1)} %get-tuple-element.50.noise_ref, bf16[2048,1024]{1,0:T(8,128)(2,1)S(1)} %get-tuple-element.64.low_ref, bf16[2048,1024]{1,0:T(8,128)(2,1)S(1)} %get-tuple-element.65.high_ref, ...), custom_call_target="tpu_custom_call" | custom-call | flops 2147483648 | bytes 8388608 | tf_op jit(solution)/shard_map/pallas_call | solution.py:436
  37.8 2.4 %shard_map.84.rest_6_ = f32[16,1024]{1,0:T(8,128)S(1)} custom-call(s32[2]{0:T(128)S(1)} %pad_add_fusion.where_ref, f32[1,8192]{1,0:T(1,128)S(1)} %get-tuple-element.50.noise_ref, bf16[2048,1024]{1,0:T(8,128)(2,1)S(1)} %get-tuple-element.57.low_ref, bf16[2048,1024]{1,0:T(8,128)(2,1)S(1)} %get-tuple-element.62.high_ref, ...), custom_call_target="tpu_custom_call" | custom-call | flops 2147483648 | bytes 8388608 | tf_op jit(solution)/shard_map/pallas_call | solution.py:436
  41.0 2.3 %collective-permute-start.9 = (bf16[64,2176]{1,0:T(8,128)(2,1)S(1)}, bf16[64,2176]{1,0:T(8,128)(2,1)S(1)}, u32[]{:S(2)}, u32[]{:S(2)}) collective-permute-start(bf16[64,2176]{1,0:T(8,128)(2,1)S(1)} %constant_dynamic-slice_fusion.2), channel_id=1, source_target_pairs={{0,4},{4,8},{8,12},{12,14},{14,10},{10,6},{6,2},{2,0},{5,1},{9,5},... | collective-permute-start | bytes 835592 | tf_op jit(solution)/shard_map/ppermute | solution.py:529
  43.3 2.0 %shard_map.85 = (f32[128,1024]{1,0:T(8,128)S(1)}, f32[128,128]{1,0:T(8,128)S(1)}) custom-call(s32[2]{0:T(128)S(1)} %pad_add_fusion.where_ref, f32[1,8192]{1,0:T(1,128)S(1)} %get-tuple-element.50.noise_ref, bf16[2048,1024]{1,0:T(8,128)(2,1)S(1)} %get-tuple-element.64.low_ref, bf16[2048,1024]{1,0:T(8,128)(2,1)S(1)} %get-tuple-element.65.high_ref, ...), custom_call_target="tpu_custom_call" | custom-call | flops 2147483648 | bytes 8388608 | tf_op jit(solution)/shard_map/pallas_call | solution.py:436
  45.6 2.4 %shard_map.86.rest_6_ = f32[16,1024]{1,0:T(8,128)S(1)} custom-call(s32[2]{0:T(128)S(1)} %pad_add_fusion.where_ref, f32[1,8192]{1,0:T(1,128)S(1)} %get-tuple-element.50.noise_ref, bf16[2048,1024]{1,0:T(8,128)(2,1)S(1)} %get-tuple-element.57.low_ref, bf16[2048,1024]{1,0:T(8,128)(2,1)S(1)} %get-tuple-element.62.high_ref, ...), custom_call_target="tpu_custom_call" | custom-call | flops 2147483648 | bytes 8388608 | tf_op jit(solution)/shard_map/pallas_call | solution.py:436
  48.4 2.2 %shard_map.87 = (f32[64,1024]{1,0:T(8,128)S(1)}, f32[64,128]{1,0:T(8,128)S(1)}) custom-call(s32[2]{0:T(128)S(1)} %pad_add_fusion.where_ref, f32[1,8192]{1,0:T(1,128)S(1)} %get-tuple-element.50.noise_ref, bf16[2048,1024]{1,0:T(8,128)(2,1)S(1)} %get-tuple-element.64.low_ref, bf16[2048,1024]{1,0:T(8,128)(2,1)S(1)} %get-tuple-element.65.high_ref, ...), custom_call_target="tpu_custom_call" | custom-call | flops 2147483648 | bytes 8388608 | tf_op jit(solution)/shard_map/pallas_call | solution.py:436
  50.6 3.6 %shard_map.88 = (f32[1,1024]{1,0:T(1,128)}, f32[4,4,1152]{2,1,0:T(4,128)S(1)}, f32[4,4,1152]{2,1,0:T(4,128)S(1)}, bf16[8,1024]{1,0:T(8,128)(2,1)S(1)}, f32[8,128]{1,0:T(8,128)S(1)}) custom-call(s32[2]{0:T(128)S(1)} %pad_add_fusion.where_ref, f32[1,8192]{1,0:T(1,128)S(1)} %get-tuple-element.50.noise_ref, bf16[2048,1024]{1,0:T(8,128)(2,1)S(1)} %get-tuple-element.57.low_ref, ...), custom_call_target="tpu_custom_call" | custom-call | flops 2147483648 | bytes 8388608 | tf_op jit(solution)/shard_map/pallas_call | solution.py:436
  55.5 1.6 %collective-permute-start.17 = (f32[4,4,1152]{2,1,0:T(4,128)S(1)}, f32[4,4,1152]{2,1,0:T(4,128)S(1)}, u32[]{:S(2)}, u32[]{:S(2)}) collective-permute-start(f32[4,4,1152]{2,1,0:T(4,128)S(1)} %add.15), channel_id=1, source_target_pairs={{0,2},{2,0},{4,6},{6,4},{8,10},{10,8},{12,14},{14,12},{1,3},{3,1},... | collective-permute-start | bytes 221192 | tf_op jit(solution)/shard_map/ppermute | solution.py:548
  57.2 1.7 %shard_map.89 = (f32[4,4,1152]{2,1,0:T(4,128)S(1)}, f32[4,4,1152]{2,1,0:T(4,128)S(1)}) custom-call(s32[2]{0:T(128)S(1)} %pad_add_fusion.where_ref, bf16[8,1024]{1,0:T(8,128)(2,1)S(1)} %get-tuple-element.87.rounded_ref, f32[8,128]{1,0:T(8,128)S(1)} %get-tuple-element.88.totals_ref, bf16[8,1024,512]{2,1,0:T(8,128)(2,1)S(1)} %get-tuple-element.83.rest_8_.rest_0_, ...), custom_call_target="tpu_custom_call" | custom-call | flops 1073741824 | bytes 4194304 | tf_op jit(solution)/shard_map/pallas_call | solution.py:329
  60.2 1.7 %collective-permute-start.19 = (f32[2,4,1152]{2,1,0:T(4,128)S(1)}, f32[2,4,1152]{2,1,0:T(4,128)S(1)}, u32[]{:S(2)}, u32[]{:S(2)}) collective-permute-start(f32[2,4,1152]{2,1,0:T(4,128)S(1)} %dynamic-slice_bitcast_fusion), channel_id=1, source_target_pairs={{0,4},{2,6},{4,0},{6,2},{8,12},{10,14},{12,8},{14,10},{1,5},{3,7},... | collective-permute-start | bytes 110600 | tf_op jit(solution)/shard_map/ppermute | solution.py:468
  61.9 2.4 %collective-permute-done.19 = f32[2,4,1152]{2,1,0:T(4,128)S(1)} collective-permute-done((f32[2,4,1152]{2,1,0:T(4,128)S(1)}, f32[2,4,1152]{2,1,0:T(4,128)S(1)}, u32[]{:S(2)}, u32[]{:S(2)}) %collective-permute-start.19) | collective-permute-done | bytes 36896 | tf_op jit(solution)/shard_map/ppermute | solution.py:468
  64.3 2.7 %collective-permute-start.20 = (f32[1,4,1152]{2,1,0:T(4,128)S(1)}, f32[1,4,1152]{2,1,0:T(4,128)S(1)}, u32[]{:S(2)}, u32[]{:S(2)}) collective-permute-start(f32[1,4,1152]{2,1,0:T(4,128)S(1)} %constant_dynamic-slice_fusion), channel_id=1, source_target_pairs={{0,8},{2,10},{4,12},{6,14},{8,0},{10,2},{12,4},{14,6},{1,9},{3,11}... | collective-permute-start | bytes 55304 | tf_op jit(solution)/shard_map/ppermute | solution.py:468
  67.0 2.0 %collective-permute-done.20 = f32[1,4,1152]{2,1,0:T(4,128)S(1)} collective-permute-done((f32[1,4,1152]{2,1,0:T(4,128)S(1)}, f32[1,4,1152]{2,1,0:T(4,128)S(1)}, u32[]{:S(2)}, u32[]{:S(2)}) %collective-permute-start.20) | collective-permute-done | bytes 18464 | tf_op jit(solution)/shard_map/ppermute | solution.py:468
  (48 shorter events, 10.9 us)
Async XLA Ops:
  2.1 11.0 %collective-permute-start.2 = (bf16[64,4096]{1,0:T(8,128)(2,1)S(1)}, bf16[64,4096]{1,0:T(8,128)(2,1)S(1)}, u32[]{:S(2)}, u32[]{:S(2)}) collective-permute-start(bf16[64,4096]{1,0:T(8,128)(2,1)S(1)} %get-tuple-element.52.tmpl_ref), channel_id=1, source_target_pairs={{0,4},{4,8},{8,12},{12,14},{14,10},{10,6},{6,2},{2,0},{5,1},{9,5},... | collective-permute-start | bytes 1572872 | tf_op jit(solution)/shard_map/ppermute | solution.py:529
  5.1 12.9 %collective-permute-start = (bf16[64,4224]{1,0:T(8,128)(2,1)S(1)}, bf16[64,4224]{1,0:T(8,128)(2,1)S(1)}, u32[]{:S(2)}, u32[]{:S(2)}) collective-permute-start(bf16[64,4224]{1,0:T(8,128)(2,1)S(1)} %get-tuple-element.51.tmpl_ref), channel_id=1, source_target_pairs={{0,4},{4,8},{8,12},{12,14},{14,10},{10,6},{6,2},{2,0},{5,1},{9,5},... | collective-permute-start | bytes 1622024 | tf_op jit(solution)/shard_map/ppermute | solution.py:529
  13.0 10.6 %collective-permute-start.6 = (bf16[64,4096]{1,0:T(8,128)(2,1)S(1)}, bf16[64,4096]{1,0:T(8,128)(2,1)S(1)}, u32[]{:S(2)}, u32[]{:S(2)}) collective-permute-start(bf16[64,4096]{1,0:T(8,128)(2,1)S(1)} %collective-permute-done.2.rest_0_), channel_id=1, source_target_pairs={{0,4},{4,8},{8,12},{12,14},{14,10},{10,6},{6,2},{2,0},{5,1},{9,5},... | collective-permute-start | bytes 1572872 | tf_op jit(solution)/shard_map/ppermute | solution.py:529
  14.7 5.5 %copy-start.1 = (s32[8]{0:T(128)S(1)}, s32[8]{0:T(128)}, u32[]{:S(2)}) copy-start(s32[8]{0:T(128)} %rest_7_.1) | copy-start | bytes 100
  14.7 5.5 %copy-start = (s32[64]{0:T(128)S(1)}, s32[64]{0:T(128)}, u32[]{:S(2)}) copy-start(s32[64]{0:T(128)} %param.9) | copy-start | bytes 772
  17.5 8.2 %collective-permute-start.3 = (bf16[64,4096]{1,0:T(8,128)(2,1)S(1)}, bf16[64,4096]{1,0:T(8,128)(2,1)S(1)}, u32[]{:S(2)}, u32[]{:S(2)}) collective-permute-start(bf16[64,4096]{1,0:T(8,128)(2,1)S(1)} %collective-permute-done.2.rest_0_), channel_id=1, source_target_pairs={{0,1},{1,0},{2,3},{3,2},{4,5},{5,4},{6,7},{7,6},{8,9},{9,8},{10,11... | collective-permute-start | bytes 1572872 | tf_op jit(solution)/shard_map/ppermute | solution.py:533
  18.0 13.5 %collective-permute-start.8 = (bf16[64,4224]{1,0:T(8,128)(2,1)S(1)}, bf16[64,4224]{1,0:T(8,128)(2,1)S(1)}, u32[]{:S(2)}, u32[]{:S(2)}) collective-permute-start(bf16[64,4224]{1,0:T(8,128)(2,1)S(1)} %collective-permute-done.rest_0_), channel_id=1, source_target_pairs={{0,1},{1,0},{2,3},{3,2},{4,5},{5,4},{6,7},{7,6},{8,9},{9,8},{10,11... | collective-permute-start | bytes 1622024 | tf_op jit(solution)/shard_map/ppermute | solution.py:533
  18.1 11.3 %collective-permute-start.1 = (bf16[64,4224]{1,0:T(8,128)(2,1)S(1)}, bf16[64,4224]{1,0:T(8,128)(2,1)S(1)}, u32[]{:S(2)}, u32[]{:S(2)}) collective-permute-start(bf16[64,4224]{1,0:T(8,128)(2,1)S(1)} %collective-permute-done.rest_0_), channel_id=1, source_target_pairs={{0,4},{4,8},{8,12},{12,14},{14,10},{10,6},{6,2},{2,0},{5,1},{9,5},... | collective-permute-start | bytes 1622024 | tf_op jit(solution)/shard_map/ppermute | solution.py:529
  23.7 10.3 %collective-permute-start.7 = (bf16[64,4096]{1,0:T(8,128)(2,1)S(1)}, bf16[64,4096]{1,0:T(8,128)(2,1)S(1)}, u32[]{:S(2)}, u32[]{:S(2)}) collective-permute-start(bf16[64,4096]{1,0:T(8,128)(2,1)S(1)} %collective-permute-done.6.rest_0_), channel_id=1, source_target_pairs={{0,1},{1,0},{2,3},{3,2},{4,5},{5,4},{6,7},{7,6},{8,9},{9,8},{10,11... | collective-permute-start | bytes 1572872 | tf_op jit(solution)/shard_map/ppermute | solution.py:533
  23.7 12.3 %collective-permute-start.11 = (bf16[64,4096]{1,0:T(8,128)(2,1)S(1)}, bf16[64,4096]{1,0:T(8,128)(2,1)S(1)}, u32[]{:S(2)}, u32[]{:S(2)}) collective-permute-start(bf16[64,4096]{1,0:T(8,128)(2,1)S(1)} %collective-permute-done.6.rest_0_), channel_id=1, source_target_pairs={{0,4},{4,8},{8,12},{12,14},{14,10},{10,6},{6,2},{2,0},{5,1},{9,5},... | collective-permute-start | bytes 1572872 | tf_op jit(solution)/shard_map/ppermute | solution.py:529
  29.5 8.4 %collective-permute-start.5 = (bf16[64,4224]{1,0:T(8,128)(2,1)S(1)}, bf16[64,4224]{1,0:T(8,128)(2,1)S(1)}, u32[]{:S(2)}, u32[]{:S(2)}) collective-permute-start(bf16[64,4224]{1,0:T(8,128)(2,1)S(1)} %collective-permute-done.1.rest_0_), channel_id=1, source_target_pairs={{0,1},{1,0},{2,3},{3,2},{4,5},{5,4},{6,7},{7,6},{8,9},{9,8},{10,11... | collective-permute-start | bytes 1622024 | tf_op jit(solution)/shard_map/ppermute | solution.py:533
  29.5 11.4 %collective-permute-start.4 = (bf16[64,4224]{1,0:T(8,128)(2,1)S(1)}, bf16[64,4224]{1,0:T(8,128)(2,1)S(1)}, u32[]{:S(2)}, u32[]{:S(2)}) collective-permute-start(bf16[64,4224]{1,0:T(8,128)(2,1)S(1)} %collective-permute-done.1.rest_0_), channel_id=1, source_target_pairs={{0,4},{4,8},{8,12},{12,14},{14,10},{10,6},{6,2},{2,0},{5,1},{9,5},... | collective-permute-start | bytes 1622024 | tf_op jit(solution)/shard_map/ppermute | solution.py:529
  36.0 7.4 %collective-permute-start.12 = (bf16[64,4096]{1,0:T(8,128)(2,1)S(1)}, bf16[64,4096]{1,0:T(8,128)(2,1)S(1)}, u32[]{:S(2)}, u32[]{:S(2)}) collective-permute-start(bf16[64,4096]{1,0:T(8,128)(2,1)S(1)} %collective-permute-done.11.rest_0_), channel_id=1, source_target_pairs={{0,1},{1,0},{2,3},{3,2},{4,5},{5,4},{6,7},{7,6},{8,9},{9,8},{10,11... | collective-permute-start | bytes 1572872 | tf_op jit(solution)/shard_map/ppermute | solution.py:533
  36.3 9.0 %collective-permute-start.14 = (bf16[64,2048]{1,0:T(8,128)(2,1)S(1)}, bf16[64,2048]{1,0:T(8,128)(2,1)S(1)}, u32[]{:S(2)}, u32[]{:S(2)}) collective-permute-start(bf16[64,2048]{1,0:T(8,128)(2,1)S(1)} %constant_dynamic-slice_fusion.1), channel_id=1, source_target_pairs={{0,4},{4,8},{8,12},{12,14},{14,10},{10,6},{6,2},{2,0},{5,1},{9,5},... | collective-permute-start | bytes 786440 | tf_op jit(solution)/shard_map/ppermute | solution.py:529
  40.9 4.7 %collective-permute-start.10 = (bf16[64,4224]{1,0:T(8,128)(2,1)S(1)}, bf16[64,4224]{1,0:T(8,128)(2,1)S(1)}, u32[]{:S(2)}, u32[]{:S(2)}) collective-permute-start(bf16[64,4224]{1,0:T(8,128)(2,1)S(1)} %collective-permute-done.4.rest_0_), channel_id=1, source_target_pairs={{0,1},{1,0},{2,3},{3,2},{4,5},{5,4},{6,7},{7,6},{8,9},{9,8},{10,11... | collective-permute-start | bytes 1622024 | tf_op jit(solution)/shard_map/ppermute | solution.py:533
  41.0 7.0 %collective-permute-start.9 = (bf16[64,2176]{1,0:T(8,128)(2,1)S(1)}, bf16[64,2176]{1,0:T(8,128)(2,1)S(1)}, u32[]{:S(2)}, u32[]{:S(2)}) collective-permute-start(bf16[64,2176]{1,0:T(8,128)(2,1)S(1)} %constant_dynamic-slice_fusion.2), channel_id=1, source_target_pairs={{0,4},{4,8},{8,12},{12,14},{14,10},{10,6},{6,2},{2,0},{5,1},{9,5},... | collective-permute-start | bytes 835592 | tf_op jit(solution)/shard_map/ppermute | solution.py:529
  45.3 3.1 %collective-permute-start.15 = (bf16[64,2048]{1,0:T(8,128)(2,1)S(1)}, bf16[64,2048]{1,0:T(8,128)(2,1)S(1)}, u32[]{:S(2)}, u32[]{:S(2)}) collective-permute-start(bf16[64,2048]{1,0:T(8,128)(2,1)S(1)} %collective-permute-done.14.rest_0_), channel_id=1, source_target_pairs={{0,1},{1,0},{2,3},{3,2},{4,5},{5,4},{6,7},{7,6},{8,9},{9,8},{10,11... | collective-permute-start | bytes 786440 | tf_op jit(solution)/shard_map/ppermute | solution.py:533
  48.0 2.6 %collective-permute-start.13 = (bf16[64,2176]{1,0:T(8,128)(2,1)S(1)}, bf16[64,2176]{1,0:T(8,128)(2,1)S(1)}, u32[]{:S(2)}, u32[]{:S(2)}) collective-permute-start(bf16[64,2176]{1,0:T(8,128)(2,1)S(1)} %collective-permute-done.9.rest_0_), channel_id=1, source_target_pairs={{0,1},{1,0},{2,3},{3,2},{4,5},{5,4},{6,7},{7,6},{8,9},{9,8},{10,11... | collective-permute-start | bytes 835592 | tf_op jit(solution)/shard_map/ppermute | solution.py:533
  54.2 1.3 %collective-permute-start.16 = (f32[4,4,1152]{2,1,0:T(4,128)S(1)}, f32[4,4,1152]{2,1,0:T(4,128)S(1)}, u32[]{:S(2)}, u32[]{:S(2)}) collective-permute-start(f32[4,4,1152]{2,1,0:T(4,128)S(1)} %get-tuple-element.86), channel_id=1, source_target_pairs={{0,1},{1,0},{2,3},{3,2},{4,5},{5,4},{6,7},{7,6},{8,9},{9,8},{10,11... | collective-permute-start | bytes 221192 | tf_op jit(solution)/shard_map/ppermute | solution.py:547
  55.5 4.4 %collective-permute-start.17 = (f32[4,4,1152]{2,1,0:T(4,128)S(1)}, f32[4,4,1152]{2,1,0:T(4,128)S(1)}, u32[]{:S(2)}, u32[]{:S(2)}) collective-permute-start(f32[4,4,1152]{2,1,0:T(4,128)S(1)} %add.15), channel_id=1, source_target_pairs={{0,2},{2,0},{4,6},{6,4},{8,10},{10,8},{12,14},{14,12},{1,3},{3,1},... | collective-permute-start | bytes 221192 | tf_op jit(solution)/shard_map/ppermute | solution.py:548
  58.9 1.3 %collective-permute-start.18 = (f32[4,4,1152]{2,1,0:T(4,128)S(1)}, f32[4,4,1152]{2,1,0:T(4,128)S(1)}, u32[]{:S(2)}, u32[]{:S(2)}) collective-permute-start(f32[4,4,1152]{2,1,0:T(4,128)S(1)} %get-tuple-element.91), channel_id=1, source_target_pairs={{0,1},{1,0},{2,3},{3,2},{4,5},{5,4},{6,7},{7,6},{8,9},{9,8},{10,11... | collective-permute-start | bytes 221192 | tf_op jit(solution)/shard_map/ppermute | solution.py:552
  60.2 4.0 %collective-permute-start.19 = (f32[2,4,1152]{2,1,0:T(4,128)S(1)}, f32[2,4,1152]{2,1,0:T(4,128)S(1)}, u32[]{:S(2)}, u32[]{:S(2)}) collective-permute-start(f32[2,4,1152]{2,1,0:T(4,128)S(1)} %dynamic-slice_bitcast_fusion), channel_id=1, source_target_pairs={{0,4},{2,6},{4,0},{6,2},{8,12},{10,14},{12,8},{14,10},{1,5},{3,7},... | collective-permute-start | bytes 110600 | tf_op jit(solution)/shard_map/ppermute | solution.py:468
  64.3 4.7 %collective-permute-start.20 = (f32[1,4,1152]{2,1,0:T(4,128)S(1)}, f32[1,4,1152]{2,1,0:T(4,128)S(1)}, u32[]{:S(2)}, u32[]{:S(2)}) collective-permute-start(f32[1,4,1152]{2,1,0:T(4,128)S(1)} %constant_dynamic-slice_fusion), channel_id=1, source_target_pairs={{0,8},{2,10},{4,12},{6,14},{8,0},{10,2},{12,4},{14,6},{1,9},{3,11}... | collective-permute-start | bytes 55304 | tf_op jit(solution)/shard_map/ppermute | solution.py:468

commit v13 on v12

--- a/solution.py
+++ b/solution.py
@@ -279,47 +279,38 @@
     )(where, noise, templates, pltpu.with_memory_space_constraint(particles, pltpu.HBM), *rest)
 
 
-def class_weights(state, where_ref, counts_ref, per_owner):
+def class_weights(state, where_ref, counts_ref):
     _, _, _, weights = state
     classes = weights.shape[0]
     row = lax.broadcasted_iota(jnp.int32, (classes, LANES), 0)
     counts = jnp.zeros((classes, LANES), jnp.float32)
     for tag in range(classes):
-        mine = (where_ref[0] == 0) & (where_ref[1] == tag // per_owner)
-        count = jnp.where(mine, counts_ref[tag], 0).astype(jnp.float32)
-        counts = jnp.where(row == tag, count, counts)
+        count = jnp.where((where_ref[0] == 0) & (where_ref[1] == 1), counts_ref[tag], 0)
+        counts = jnp.where(row == tag, count.astype(jnp.float32), counts)
     weights = weights / jnp.sum(weights, axis=0, keepdims=True)
     totals = jnp.sum(weights, axis=1, keepdims=True) + counts
-
-    def own_first(rows):
-        turned = jnp.concatenate([rows[per_owner:], rows[:per_owner]], axis=0)
-        return jnp.where(where_ref[1] == 0, rows, turned)
-
-    return own_first(weights).astype(jnp.bfloat16), own_first(totals)
-
-
-def class_sums(rounded, totals, bit, nears, mine_ref, theirs_ref):
-    per_owner = mine_ref.shape[1]
+    return weights.astype(jnp.bfloat16), totals
+
+
+def class_sums(rounded, totals, bit, nears, sums_ref):
     chunk = nears[0].shape[2]
-    share = mine_ref.shape[2] // chunk
+    share = sums_ref.shape[2] // chunk
     piece = 0
     for near in nears:
         for pair in range(near.shape[0] // (2 * share)):
             for part in range(share):
                 at = (2 * pair + bit) * share + part
-                sums = jnp.dot(rounded, near[at], preferred_element_type=jnp.float32)
-                columns = pl.ds(part * chunk, chunk)
-                mine_ref[piece, :, columns] = sums[:per_owner]
-                theirs_ref[piece, :, columns] = sums[per_owner:]
-            mine_ref[piece, :, share * chunk :] = totals[:per_owner]
-            theirs_ref[piece, :, share * chunk :] = totals[per_owner:]
+                sums_ref[piece, :, pl.ds(part * chunk, chunk)] = jnp.dot(
+                    rounded, near[at], preferred_element_type=jnp.float32
+                )
+            sums_ref[piece, :, share * chunk :] = totals
             piece += 1
 
 
 def rest_kernel(where_ref, rounded_ref, totals_ref, *rest):
-    *nears, mine_ref, theirs_ref = rest
+    *nears, sums_ref = rest
     bit = lax.rem(where_ref[0], 2)
-    class_sums(rounded_ref[...], totals_ref[...], bit, nears, mine_ref, theirs_ref)
+    class_sums(rounded_ref[...], totals_ref[...], bit, nears, sums_ref)
 
 
 def rest_sums(where, rounded, totals, nears, piece):
@@ -329,8 +320,8 @@
     return pl.pallas_call(
         rest_kernel,
         in_specs=[in_smem()] + [in_vmem()] * (2 + len(nears)),
-        out_specs=[in_vmem()] * 2,
-        out_shape=[piece, piece],
+        out_specs=in_vmem(),
+        out_shape=piece,
         compiler_params=pltpu.CompilerParams(vmem_limit_bytes=VMEM_LIMIT),
         cost_estimate=pl.CostEstimate(
             flops=128 * per_device * freqs,
@@ -347,7 +338,7 @@
     else:
         acc_in, energy_in, logs_ref, words_ref, state_ref, *rest = rest
         if ends:
-            counts_ref, *nears, loglik_ref, mine_ref, theirs_ref = rest[:-4]
+            counts_ref, *nears, loglik_ref, sums_ref = rest[:-4]
             rounded_ref, totals_ref, acc, energy = rest[-4:]
         else:
             out_ref, acc, energy = rest
@@ -396,11 +387,11 @@
     state = add_rows(tags, hit, logs_ref, get_state(state_ref), acc, energy)
     if ends:
         loglik_ref[...] = state[0] + jnp.log(state[1])
-        rounded, totals = class_weights(state, where_ref, counts_ref, mine_ref.shape[1])
+        rounded, totals = class_weights(state, where_ref, counts_ref)
         rounded_ref[...] = rounded
         totals_ref[...] = totals
         bit = 1 - lax.rem(where_ref[0], 2)
-        class_sums(rounded, totals, bit, nears, mine_ref, theirs_ref)
+        class_sums(rounded, totals, bit, nears, sums_ref)
     else:
         put_state(state, out_ref)
 
@@ -423,7 +414,6 @@
             classes = rest[2].shape[0]
             shapes = [
                 jax.ShapeDtypeStruct((1, per_device), jnp.float32),
-                piece,
                 piece,
                 jax.ShapeDtypeStruct((classes, per_device), jnp.bfloat16),
                 jax.ShapeDtypeStruct((classes, LANES), jnp.float32),
@@ -464,9 +454,12 @@
             lax.dynamic_slice(pairs, (zero, which, zero, zero), size).reshape((-1,) + tail)
             for which in (bit, other)
         )
-        swaps = [(block, block ^ (2 << step)) for block in range(blocks)]
-        pieces = keep + lax.ppermute(send, "blk", swaps)
+        pieces = keep + lax.ppermute(send, ("blk", "cls"), across_chips(blocks, 2 << step))
     return pieces[0]
+
+
+def across_chips(blocks, change):
+    return [(2 * block + 1, 2 * (block ^ change) + 1) for block in range(blocks)]
 
 
 def body(particles, significant, templates, template_class, class_counts, inv_noise):
@@ -507,7 +500,7 @@
     turned.append((low, high))
     gates.append(state)
     width = freqs // blocks
-    piece = jax.ShapeDtypeStruct((blocks // 2, per_owner, width + LANES), jnp.float32)
+    piece = jax.ShapeDtypeStruct((blocks // 2, classes, width + LANES), jnp.float32)
     last = blocks // 2
     for distance in range(1, last + 1):
         ends = distance == last
@@ -543,13 +536,15 @@
         if not ends:
             (state,) = sums
 
-    loglik, mine, theirs, rounded, totals = sums
-    given = lax.ppermute(theirs, "cls", swap)
-    across = lax.ppermute(mine + given, "blk", [(i, i ^ 1) for i in range(blocks)])
+    loglik, sums, rounded, totals = sums
+    given = lax.ppermute(sums, "cls", [(0, 1)])
+    across = lax.ppermute(sums + given, ("blk", "cls"), across_chips(blocks, 1))
     rounded, _ = lax.optimization_barrier((rounded, given))
-    mine, theirs = rest_sums(where, rounded, totals, nears, piece)
-    kept = lax.optimization_barrier(mine + across)
-    total = scatter_sum(kept + lax.ppermute(theirs, "cls", swap), blocks, bits)
+    rest = rest_sums(where, rounded, totals, nears, piece)
+    kept = lax.optimization_barrier(rest + across)
+    total = scatter_sum(kept + lax.ppermute(rest, "cls", [(0, 1)]), blocks, bits)
+    handed = lax.ppermute(total[:per_owner], "cls", [(1, 0)])
+    total = jnp.where(core == 0, handed, total[per_owner:])
     class_avg = total[:, :width] / total[:, width][:, None]
     return loglik[0], class_avg
 

time: 70 us -> 79.9 us (1.14)
  waiting for transfers between devices: 9.96 us -> 15.6 us
  starting transfers between devices: 23.5 us -> 27.6 us
    ppermute x5 -> x6, waiting for transfers between devices: 6.65 us -> 12.3 us  [the longest x1 10.3 us: body(): handed = lax.ppermute(total[:per_owner], 'cls', [(1, 0)])]
    ppermute x5 -> x6, starting transfers between devices: 6.26 us -> 10.4 us  [the longest x1 4.99 us: body(): lax.ppermute(rest, 'cls', [(0, 1)])]
  transfers between devices with their start and end apart: 21 -> 22, of which waited for: 9 -> 7; matrix products, arithmetic and copies ran while one was open for 1% -> 0% of each run, Pallas kernels for 42% -> 37%
where the time goes in v13:
time: 79.9 us; the launch traced here: 79.6 us
  Pallas kernels  34.3 us (43%)
  starting transfers between devices  27.6 us (35%)
  waiting for transfers between devices  15.6 us (20%)
  between operations  0.89 us (1%)
  other arithmetic  0.86 us (1%)
    pallas_call x8, Pallas kernels, ring_scores(): pl.pallas_call(functools.partial(ring_kernel, phase, ends, sources), in_s...  19 us
    ppermute x8, starting transfers between devices, body(): own = lax.ppermute(message, ('blk', 'cls'), ring)  16.2 us
    pallas_call x3, Pallas kernels, own_scores(): pl.pallas_call(functools.partial(own_kernel, quarters), in_specs=[in_smem...  12.1 us
    ppermute x1, waiting for transfers between devices, body(): handed = lax.ppermute(total[:per_owner], 'cls', [(1, 0)])  10.3 us
    ppermute x1, starting transfers between devices, body(): lax.ppermute(rest, 'cls', [(0, 1)])  4.99 us
    ppermute x8, waiting for transfers between devices, body(): own = lax.ppermute(message, ('blk', 'cls'), ring)  3.29 us
    ppermute x1, starting transfers between devices, body(): given = lax.ppermute(sums, 'cls', [(0, 1)])  2.08 us
    pallas_call x1, Pallas kernels, rest_sums(): pl.pallas_call(rest_kernel, in_specs=[in_smem()] + [in_vmem()] * (2 + len...  1.74 us
  transfers between devices with their start and end apart: 22, of which 7 were waited for; matrix products, arithmetic and copies ran while one was open for 0% of the time, Pallas kernels for 37%

profile of v13, /device:TPU:0, one launch (start us, length us, event | category | flops | bytes accessed | tf_op | source)
XLA Modules:
  0.0 79.6 jit_solution(11399453613366103290)
XLA Ops:
  2.1 3.1 %collective-permute-start.2 = (bf16[64,4096]{1,0:T(8,128)(2,1)S(1)}, bf16[64,4096]{1,0:T(8,128)(2,1)S(1)}, u32[]{:S(2)}, u32[]{:S(2)}) collective-permute-start(bf16[64,4096]{1,0:T(8,128)(2,1)S(1)} %get-tuple-element.49.tmpl_ref), channel_id=1, source_target_pairs={{0,4},{4,8},{8,12},{12,14},{14,10},{10,6},{6,2},{2,0},{5,1},{9,5},... | collective-permute-start | bytes 1572872 | tf_op jit(solution)/shard_map/ppermute | solution.py:522
  5.1 1.6 %collective-permute-start = (bf16[64,4224]{1,0:T(8,128)(2,1)S(1)}, bf16[64,4224]{1,0:T(8,128)(2,1)S(1)}, u32[]{:S(2)}, u32[]{:S(2)}) collective-permute-start(bf16[64,4224]{1,0:T(8,128)(2,1)S(1)} %get-tuple-element.48.tmpl_ref), channel_id=1, source_target_pairs={{0,4},{4,8},{8,12},{12,14},{14,10},{10,6},{6,2},{2,0},{5,1},{9,5},... | collective-permute-start | bytes 1622024 | tf_op jit(solution)/shard_map/ppermute | solution.py:522
  6.8 6.2 %shard_map.78 = (s32[16,1024]{1,0:T(8,128)S(1)}, f32[64,1024]{1,0:T(8,128)S(1)}, f32[64,128]{1,0:T(8,128)S(1)}, bf16[2048,1024]{1,0:T(8,128)(2,1)S(1)}, bf16[204...) custom-call(s32[2]{0:T(128)S(1)} %pad_add_fusion.where_ref, ...), custom_call_target="tpu_custom_call" | custom-call | flops 2147483648 | bytes 8388608 | tf_op jit(solution)/shard_map/pallas_call | solution.py:267
  13.0 1.6 %collective-permute-start.6 = (bf16[64,4096]{1,0:T(8,128)(2,1)S(1)}, bf16[64,4096]{1,0:T(8,128)(2,1)S(1)}, u32[]{:S(2)}, u32[]{:S(2)}) collective-permute-start(bf16[64,4096]{1,0:T(8,128)(2,1)S(1)} %collective-permute-done.2.rest_0_), channel_id=1, source_target_pairs={{0,4},{4,8},{8,12},{12,14},{14,10},{10,6},{6,2},{2,0},{5,1},{9,5},... | collective-permute-start | bytes 1572872 | tf_op jit(solution)/shard_map/ppermute | solution.py:522
  14.7 2.8 %shard_map.79 = (f32[64,1024]{1,0:T(8,128)S(1)}, f32[64,128]{1,0:T(8,128)S(1)}, bf16[2048,1024]{1,0:T(8,128)(2,1)S(1)}, bf16[4,1024,512]{2,1,0:T(8,128)(2,1)S(1)}) custom-call(s32[2]{0:T(128)S(1)} %pad_add_fusion.where_ref, f32[1,8192]{1,0:T(1,128)S(1)} %get-tuple-element.47.noise_ref, bf16[64,4224]{1,0:T(8,128)(2,1)S(1)} %get-tuple-element.48.tmpl_ref, ...), custom_call_target="tpu_custom_call" | custom-call | flops 2147483648 | bytes 8388608 | tf_op jit(solution)/shard_map/pallas_call | solution.py:267
  18.1 2.0 %collective-permute-start.1 = (bf16[64,4224]{1,0:T(8,128)(2,1)S(1)}, bf16[64,4224]{1,0:T(8,128)(2,1)S(1)}, u32[]{:S(2)}, u32[]{:S(2)}) collective-permute-start(bf16[64,4224]{1,0:T(8,128)(2,1)S(1)} %collective-permute-done.rest_0_), channel_id=1, source_target_pairs={{0,4},{4,8},{8,12},{12,14},{14,10},{10,6},{6,2},{2,0},{5,1},{9,5},... | collective-permute-start | bytes 1622024 | tf_op jit(solution)/shard_map/ppermute | solution.py:522
  20.1 3.0 %shard_map.80 = (f32[16,1024]{1,0:T(8,128)S(1)}, bf16[2048,1024]{1,0:T(8,128)(2,1)S(1)}) custom-call(s32[2]{0:T(128)S(1)} %pad_add_fusion.where_ref, f32[1,8192]{1,0:T(1,128)S(1)} %get-tuple-element.47.noise_ref, bf16[64,4224]{1,0:T(8,128)(2,1)S(1)} %get-tuple-element.48.tmpl_ref, bf16[1024,8192]{1,0:T(8,128)(2,1)} %far_ref.5, ...), custom_call_target="tpu_custom_call" | custom-call | flops 2147483648 | bytes 8388608 | tf_op jit(solution)/shard_map/pallas_call | solution.py:267
  23.7 2.1 %collective-permute-start.11 = (bf16[64,4096]{1,0:T(8,128)(2,1)S(1)}, bf16[64,4096]{1,0:T(8,128)(2,1)S(1)}, u32[]{:S(2)}, u32[]{:S(2)}) collective-permute-start(bf16[64,4096]{1,0:T(8,128)(2,1)S(1)} %collective-permute-done.6.rest_0_), channel_id=1, source_target_pairs={{0,4},{4,8},{8,12},{12,14},{14,10},{10,6},{6,2},{2,0},{5,1},{9,5},... | collective-permute-start | bytes 1572872 | tf_op jit(solution)/shard_map/ppermute | solution.py:522
  25.7 2.0 %shard_map.81 = (f32[128,1024]{1,0:T(8,128)S(1)}, f32[128,128]{1,0:T(8,128)S(1)}) custom-call(s32[2]{0:T(128)S(1)} %pad_add_fusion.where_ref, f32[1,8192]{1,0:T(1,128)S(1)} %get-tuple-element.47.noise_ref, bf16[2048,1024]{1,0:T(8,128)(2,1)S(1)} %get-tuple-element.61.low_ref, bf16[2048,1024]{1,0:T(8,128)(2,1)S(1)} %get-tuple-element.62.high_ref, ...), custom_call_target="tpu_custom_call" | custom-call | flops 2147483648 | bytes 8388608 | tf_op jit(solution)/shard_map/pallas_call | solution.py:426
  27.8 1.7 %collective-permute-done.1.rest_0_ = bf16[64,4224]{1,0:T(8,128)(2,1)S(1)} collective-permute-done((bf16[64,4224]{1,0:T(8,128)(2,1)S(1)}, bf16[64,4224]{1,0:T(8,128)(2,1)S(1)}, u32[]{:S(2)}, u32[]{:S(2)}) %collective-permute-start.1) | collective-permute-done | bytes 540704 | tf_op jit(solution)/shard_map/ppermute | solution.py:522
  29.5 2.1 %collective-permute-start.4 = (bf16[64,4224]{1,0:T(8,128)(2,1)S(1)}, bf16[64,4224]{1,0:T(8,128)(2,1)S(1)}, u32[]{:S(2)}, u32[]{:S(2)}) collective-permute-start(bf16[64,4224]{1,0:T(8,128)(2,1)S(1)} %collective-permute-done.1.rest_0_), channel_id=1, source_target_pairs={{0,4},{4,8},{8,12},{12,14},{14,10},{10,6},{6,2},{2,0},{5,1},{9,5},... | collective-permute-start | bytes 1622024 | tf_op jit(solution)/shard_map/ppermute | solution.py:522
  31.5 2.4 %shard_map.83.rest_6_ = f32[16,1024]{1,0:T(8,128)S(1)} custom-call(s32[2]{0:T(128)S(1)} %pad_add_fusion.where_ref, f32[1,8192]{1,0:T(1,128)S(1)} %get-tuple-element.47.noise_ref, bf16[2048,1024]{1,0:T(8,128)(2,1)S(1)} %get-tuple-element.54.low_ref, bf16[2048,1024]{1,0:T(8,128)(2,1)S(1)} %get-tuple-element.59.high_ref, ...), custom_call_target="tpu_custom_call" | custom-call | flops 2147483648 | bytes 8388608 | tf_op jit(solution)/shard_map/pallas_call | solution.py:426
  34.0 2.0 %shard_map.82 = (f32[128,1024]{1,0:T(8,128)S(1)}, f32[128,128]{1,0:T(8,128)S(1)}) custom-call(s32[2]{0:T(128)S(1)} %pad_add_fusion.where_ref, f32[1,8192]{1,0:T(1,128)S(1)} %get-tuple-element.47.noise_ref, bf16[2048,1024]{1,0:T(8,128)(2,1)S(1)} %get-tuple-element.61.low_ref, bf16[2048,1024]{1,0:T(8,128)(2,1)S(1)} %get-tuple-element.62.high_ref, ...), custom_call_target="tpu_custom_call" | custom-call | flops 2147483648 | bytes 8388608 | tf_op jit(solution)/shard_map/pallas_call | solution.py:426
  36.3 1.5 %collective-permute-start.14 = (bf16[64,2048]{1,0:T(8,128)(2,1)S(1)}, bf16[64,2048]{1,0:T(8,128)(2,1)S(1)}, u32[]{:S(2)}, u32[]{:S(2)}) collective-permute-start(bf16[64,2048]{1,0:T(8,128)(2,1)S(1)} %constant_dynamic-slice_fusion.1), channel_id=1, source_target_pairs={{0,4},{4,8},{8,12},{12,14},{14,10},{10,6},{6,2},{2,0},{5,1},{9,5},... | collective-permute-start | bytes 786440 | tf_op jit(solution)/shard_map/ppermute | solution.py:522
  37.8 2.4 %shard_map.84.rest_6_ = f32[16,1024]{1,0:T(8,128)S(1)} custom-call(s32[2]{0:T(128)S(1)} %pad_add_fusion.where_ref, f32[1,8192]{1,0:T(1,128)S(1)} %get-tuple-element.47.noise_ref, bf16[2048,1024]{1,0:T(8,128)(2,1)S(1)} %get-tuple-element.54.low_ref, bf16[2048,1024]{1,0:T(8,128)(2,1)S(1)} %get-tuple-element.59.high_ref, ...), custom_call_target="tpu_custom_call" | custom-call | flops 2147483648 | bytes 8388608 | tf_op jit(solution)/shard_map/pallas_call | solution.py:426
  41.0 2.3 %collective-permute-start.9 = (bf16[64,2176]{1,0:T(8,128)(2,1)S(1)}, bf16[64,2176]{1,0:T(8,128)(2,1)S(1)}, u32[]{:S(2)}, u32[]{:S(2)}) collective-permute-start(bf16[64,2176]{1,0:T(8,128)(2,1)S(1)} %constant_dynamic-slice_fusion.2), channel_id=1, source_target_pairs={{0,4},{4,8},{8,12},{12,14},{14,10},{10,6},{6,2},{2,0},{5,1},{9,5},... | collective-permute-start | bytes 835592 | tf_op jit(solution)/shard_map/ppermute | solution.py:522
  43.3 2.0 %shard_map.85 = (f32[128,1024]{1,0:T(8,128)S(1)}, f32[128,128]{1,0:T(8,128)S(1)}) custom-call(s32[2]{0:T(128)S(1)} %pad_add_fusion.where_ref, f32[1,8192]{1,0:T(1,128)S(1)} %get-tuple-element.47.noise_ref, bf16[2048,1024]{1,0:T(8,128)(2,1)S(1)} %get-tuple-element.61.low_ref, bf16[2048,1024]{1,0:T(8,128)(2,1)S(1)} %get-tuple-element.62.high_ref, ...), custom_call_target="tpu_custom_call" | custom-call | flops 2147483648 | bytes 8388608 | tf_op jit(solution)/shard_map/pallas_call | solution.py:426
  45.6 2.4 %shard_map.86.rest_6_ = f32[16,1024]{1,0:T(8,128)S(1)} custom-call(s32[2]{0:T(128)S(1)} %pad_add_fusion.where_ref, f32[1,8192]{1,0:T(1,128)S(1)} %get-tuple-element.47.noise_ref, bf16[2048,1024]{1,0:T(8,128)(2,1)S(1)} %get-tuple-element.54.low_ref, bf16[2048,1024]{1,0:T(8,128)(2,1)S(1)} %get-tuple-element.59.high_ref, ...), custom_call_target="tpu_custom_call" | custom-call | flops 2147483648 | bytes 8388608 | tf_op jit(solution)/shard_map/pallas_call | solution.py:426
  48.4 2.2 %shard_map.87 = (f32[64,1024]{1,0:T(8,128)S(1)}, f32[64,128]{1,0:T(8,128)S(1)}) custom-call(s32[2]{0:T(128)S(1)} %pad_add_fusion.where_ref, f32[1,8192]{1,0:T(1,128)S(1)} %get-tuple-element.47.noise_ref, bf16[2048,1024]{1,0:T(8,128)(2,1)S(1)} %get-tuple-element.61.low_ref, bf16[2048,1024]{1,0:T(8,128)(2,1)S(1)} %get-tuple-element.62.high_ref, ...), custom_call_target="tpu_custom_call" | custom-call | flops 2147483648 | bytes 8388608 | tf_op jit(solution)/shard_map/pallas_call | solution.py:426
  50.6 3.6 %shard_map.88 = (f32[1,1024]{1,0:T(1,128)}, f32[4,8,1152]{2,1,0:T(8,128)S(1)}, bf16[8,1024]{1,0:T(8,128)(2,1)S(1)}, f32[8,128]{1,0:T(8,128)S(1)}) custom-call(s32[2]{0:T(128)S(1)} %pad_add_fusion.where_ref, f32[1,8192]{1,0:T(1,128)S(1)} %get-tuple-element.47.noise_ref, bf16[2048,1024]{1,0:T(8,128)(2,1)S(1)} %get-tuple-element.54.low_ref, ...), custom_call_target="tpu_custom_call" | custom-call | flops 2147483648 | bytes 8388608 | tf_op jit(solution)/shard_map/pallas_call | solution.py:426
  54.2 2.1 %collective-permute-start.16 = (f32[4,8,1152]{2,1,0:T(8,128)S(1)}, f32[4,8,1152]{2,1,0:T(8,128)S(1)}, u32[]{:S(2)}, u32[]{:S(2)}) collective-permute-start(f32[4,8,1152]{2,1,0:T(8,128)S(1)} %get-tuple-element.83), channel_id=1, source_target_pairs={{0,1},{2,3},{4,5},{6,7},{8,9},{10,11},{12,13},{14,15},{16,17},{18,... | collective-permute-start | bytes 442376 | tf_op jit(solution)/shard_map/ppermute | solution.py:540
  58.0 1.7 %shard_map.89 = f32[4,8,1152]{2,1,0:T(8,128)S(1)} custom-call(s32[2]{0:T(128)S(1)} %pad_add_fusion.where_ref, bf16[8,1024]{1,0:T(8,128)(2,1)S(1)} %get-tuple-element.84.rounded_ref, f32[8,128]{1,0:T(8,128)S(1)} %get-tuple-element.85.totals_ref, bf16[8,1024,512]{2,1,0:T(8,128)(2,1)S(1)} %get-tuple-element.80.rest_8_.rest_0_, ...), custom_call_target="tpu_custom_call" | custom-call | flops 1073741824 | bytes 4194304 | tf_op jit(solution)/shard_map/pallas_call | solution.py:320
  59.7 5.0 %collective-permute-start.18 = (f32[4,8,1152]{2,1,0:T(8,128)S(1)}, f32[4,8,1152]{2,1,0:T(8,128)S(1)}, u32[]{:S(2)}, u32[]{:S(2)}) collective-permute-start(f32[4,8,1152]{2,1,0:T(8,128)S(1)} %shard_map.89), channel_id=1, source_target_pairs={{0,1},{2,3},{4,5},{6,7},{8,9},{10,11},{12,13},{14,15},{16,17},{18,... | collective-permute-start | bytes 442376 | tf_op jit(solution)/shard_map/ppermute | solution.py:545
  68.5 10.3 %collective-permute-done.21 = f32[4,1152]{1,0:T(4,128)S(1)} collective-permute-done((f32[4,1152]{1,0:T(4,128)S(1)}, f32[4,1152]{1,0:T(4,128)S(1)}, u32[]{:S(2)}, u32[]{:S(2)}) %collective-permute-start.21) | collective-permute-done | bytes 18464 | tf_op jit(solution)/shard_map/ppermute | solution.py:546
  (52 shorter events, 10.6 us)
Async XLA Ops:
  2.1 11.0 %collective-permute-start.2 = (bf16[64,4096]{1,0:T(8,128)(2,1)S(1)}, bf16[64,4096]{1,0:T(8,128)(2,1)S(1)}, u32[]{:S(2)}, u32[]{:S(2)}) collective-permute-start(bf16[64,4096]{1,0:T(8,128)(2,1)S(1)} %get-tuple-element.49.tmpl_ref), channel_id=1, source_target_pairs={{0,4},{4,8},{8,12},{12,14},{14,10},{10,6},{6,2},{2,0},{5,1},{9,5},... | collective-permute-start | bytes 1572872 | tf_op jit(solution)/shard_map/ppermute | solution.py:522
  5.1 12.9 %collective-permute-start = (bf16[64,4224]{1,0:T(8,128)(2,1)S(1)}, bf16[64,4224]{1,0:T(8,128)(2,1)S(1)}, u32[]{:S(2)}, u32[]{:S(2)}) collective-permute-start(bf16[64,4224]{1,0:T(8,128)(2,1)S(1)} %get-tuple-element.48.tmpl_ref), channel_id=1, source_target_pairs={{0,4},{4,8},{8,12},{12,14},{14,10},{10,6},{6,2},{2,0},{5,1},{9,5},... | collective-permute-start | bytes 1622024 | tf_op jit(solution)/shard_map/ppermute | solution.py:522
  13.0 10.6 %collective-permute-start.6 = (bf16[64,4096]{1,0:T(8,128)(2,1)S(1)}, bf16[64,4096]{1,0:T(8,128)(2,1)S(1)}, u32[]{:S(2)}, u32[]{:S(2)}) collective-permute-start(bf16[64,4096]{1,0:T(8,128)(2,1)S(1)} %collective-permute-done.2.rest_0_), channel_id=1, source_target_pairs={{0,4},{4,8},{8,12},{12,14},{14,10},{10,6},{6,2},{2,0},{5,1},{9,5},... | collective-permute-start | bytes 1572872 | tf_op jit(solution)/shard_map/ppermute | solution.py:522
  14.7 5.5 %copy-start.1 = (s32[8]{0:T(128)S(1)}, s32[8]{0:T(128)}, u32[]{:S(2)}) copy-start(s32[8]{0:T(128)} %rest_7_.1) | copy-start | bytes 100
  14.7 5.5 %copy-start = (s32[64]{0:T(128)S(1)}, s32[64]{0:T(128)}, u32[]{:S(2)}) copy-start(s32[64]{0:T(128)} %param.9) | copy-start | bytes 772
  17.5 8.2 %collective-permute-start.3 = (bf16[64,4096]{1,0:T(8,128)(2,1)S(1)}, bf16[64,4096]{1,0:T(8,128)(2,1)S(1)}, u32[]{:S(2)}, u32[]{:S(2)}) collective-permute-start(bf16[64,4096]{1,0:T(8,128)(2,1)S(1)} %collective-permute-done.2.rest_0_), channel_id=1, source_target_pairs={{0,1},{1,0},{2,3},{3,2},{4,5},{5,4},{6,7},{7,6},{8,9},{9,8},{10,11... | collective-permute-start | bytes 1572872 | tf_op jit(solution)/shard_map/ppermute | solution.py:526
  18.0 13.5 %collective-permute-start.8 = (bf16[64,4224]{1,0:T(8,128)(2,1)S(1)}, bf16[64,4224]{1,0:T(8,128)(2,1)S(1)}, u32[]{:S(2)}, u32[]{:S(2)}) collective-permute-start(bf16[64,4224]{1,0:T(8,128)(2,1)S(1)} %collective-permute-done.rest_0_), channel_id=1, source_target_pairs={{0,1},{1,0},{2,3},{3,2},{4,5},{5,4},{6,7},{7,6},{8,9},{9,8},{10,11... | collective-permute-start | bytes 1622024 | tf_op jit(solution)/shard_map/ppermute | solution.py:526
  18.1 11.3 %collective-permute-start.1 = (bf16[64,4224]{1,0:T(8,128)(2,1)S(1)}, bf16[64,4224]{1,0:T(8,128)(2,1)S(1)}, u32[]{:S(2)}, u32[]{:S(2)}) collective-permute-start(bf16[64,4224]{1,0:T(8,128)(2,1)S(1)} %collective-permute-done.rest_0_), channel_id=1, source_target_pairs={{0,4},{4,8},{8,12},{12,14},{14,10},{10,6},{6,2},{2,0},{5,1},{9,5},... | collective-permute-start | bytes 1622024 | tf_op jit(solution)/shard_map/ppermute | solution.py:522
  23.7 10.3 %collective-permute-start.7 = (bf16[64,4096]{1,0:T(8,128)(2,1)S(1)}, bf16[64,4096]{1,0:T(8,128)(2,1)S(1)}, u32[]{:S(2)}, u32[]{:S(2)}) collective-permute-start(bf16[64,4096]{1,0:T(8,128)(2,1)S(1)} %collective-permute-done.6.rest_0_), channel_id=1, source_target_pairs={{0,1},{1,0},{2,3},{3,2},{4,5},{5,4},{6,7},{7,6},{8,9},{9,8},{10,11... | collective-permute-start | bytes 1572872 | tf_op jit(solution)/shard_map/ppermute | solution.py:526
  23.7 12.3 %collective-permute-start.11 = (bf16[64,4096]{1,0:T(8,128)(2,1)S(1)}, bf16[64,4096]{1,0:T(8,128)(2,1)S(1)}, u32[]{:S(2)}, u32[]{:S(2)}) collective-permute-start(bf16[64,4096]{1,0:T(8,128)(2,1)S(1)} %collective-permute-done.6.rest_0_), channel_id=1, source_target_pairs={{0,4},{4,8},{8,12},{12,14},{14,10},{10,6},{6,2},{2,0},{5,1},{9,5},... | collective-permute-start | bytes 1572872 | tf_op jit(solution)/shard_map/ppermute | solution.py:522
  29.5 8.4 %collective-permute-start.5 = (bf16[64,4224]{1,0:T(8,128)(2,1)S(1)}, bf16[64,4224]{1,0:T(8,128)(2,1)S(1)}, u32[]{:S(2)}, u32[]{:S(2)}) collective-permute-start(bf16[64,4224]{1,0:T(8,128)(2,1)S(1)} %collective-permute-done.1.rest_0_), channel_id=1, source_target_pairs={{0,1},{1,0},{2,3},{3,2},{4,5},{5,4},{6,7},{7,6},{8,9},{9,8},{10,11... | collective-permute-start | bytes 1622024 | tf_op jit(solution)/shard_map/ppermute | solution.py:526
  29.5 11.4 %collective-permute-start.4 = (bf16[64,4224]{1,0:T(8,128)(2,1)S(1)}, bf16[64,4224]{1,0:T(8,128)(2,1)S(1)}, u32[]{:S(2)}, u32[]{:S(2)}) collective-permute-start(bf16[64,4224]{1,0:T(8,128)(2,1)S(1)} %collective-permute-done.1.rest_0_), channel_id=1, source_target_pairs={{0,4},{4,8},{8,12},{12,14},{14,10},{10,6},{6,2},{2,0},{5,1},{9,5},... | collective-permute-start | bytes 1622024 | tf_op jit(solution)/shard_map/ppermute | solution.py:522
  36.0 7.4 %collective-permute-start.12 = (bf16[64,4096]{1,0:T(8,128)(2,1)S(1)}, bf16[64,4096]{1,0:T(8,128)(2,1)S(1)}, u32[]{:S(2)}, u32[]{:S(2)}) collective-permute-start(bf16[64,4096]{1,0:T(8,128)(2,1)S(1)} %collective-permute-done.11.rest_0_), channel_id=1, source_target_pairs={{0,1},{1,0},{2,3},{3,2},{4,5},{5,4},{6,7},{7,6},{8,9},{9,8},{10,11... | collective-permute-start | bytes 1572872 | tf_op jit(solution)/shard_map/ppermute | solution.py:526
  36.3 9.0 %collective-permute-start.14 = (bf16[64,2048]{1,0:T(8,128)(2,1)S(1)}, bf16[64,2048]{1,0:T(8,128)(2,1)S(1)}, u32[]{:S(2)}, u32[]{:S(2)}) collective-permute-start(bf16[64,2048]{1,0:T(8,128)(2,1)S(1)} %constant_dynamic-slice_fusion.1), channel_id=1, source_target_pairs={{0,4},{4,8},{8,12},{12,14},{14,10},{10,6},{6,2},{2,0},{5,1},{9,5},... | collective-permute-start | bytes 786440 | tf_op jit(solution)/shard_map/ppermute | solution.py:522
  40.9 4.7 %collective-permute-start.10 = (bf16[64,4224]{1,0:T(8,128)(2,1)S(1)}, bf16[64,4224]{1,0:T(8,128)(2,1)S(1)}, u32[]{:S(2)}, u32[]{:S(2)}) collective-permute-start(bf16[64,4224]{1,0:T(8,128)(2,1)S(1)} %collective-permute-done.4.rest_0_), channel_id=1, source_target_pairs={{0,1},{1,0},{2,3},{3,2},{4,5},{5,4},{6,7},{7,6},{8,9},{9,8},{10,11... | collective-permute-start | bytes 1622024 | tf_op jit(solution)/shard_map/ppermute | solution.py:526
  41.0 7.0 %collective-permute-start.9 = (bf16[64,2176]{1,0:T(8,128)(2,1)S(1)}, bf16[64,2176]{1,0:T(8,128)(2,1)S(1)}, u32[]{:S(2)}, u32[]{:S(2)}) collective-permute-start(bf16[64,2176]{1,0:T(8,128)(2,1)S(1)} %constant_dynamic-slice_fusion.2), channel_id=1, source_target_pairs={{0,4},{4,8},{8,12},{12,14},{14,10},{10,6},{6,2},{2,0},{5,1},{9,5},... | collective-permute-start | bytes 835592 | tf_op jit(solution)/shard_map/ppermute | solution.py:522
  45.3 3.1 %collective-permute-start.15 = (bf16[64,2048]{1,0:T(8,128)(2,1)S(1)}, bf16[64,2048]{1,0:T(8,128)(2,1)S(1)}, u32[]{:S(2)}, u32[]{:S(2)}) collective-permute-start(bf16[64,2048]{1,0:T(8,128)(2,1)S(1)} %collective-permute-done.14.rest_0_), channel_id=1, source_target_pairs={{0,1},{1,0},{2,3},{3,2},{4,5},{5,4},{6,7},{7,6},{8,9},{9,8},{10,11... | collective-permute-start | bytes 786440 | tf_op jit(solution)/shard_map/ppermute | solution.py:526
  48.0 2.6 %collective-permute-start.13 = (bf16[64,2176]{1,0:T(8,128)(2,1)S(1)}, bf16[64,2176]{1,0:T(8,128)(2,1)S(1)}, u32[]{:S(2)}, u32[]{:S(2)}) collective-permute-start(bf16[64,2176]{1,0:T(8,128)(2,1)S(1)} %collective-permute-done.9.rest_0_), channel_id=1, source_target_pairs={{0,1},{1,0},{2,3},{3,2},{4,5},{5,4},{6,7},{7,6},{8,9},{9,8},{10,11... | collective-permute-start | bytes 835592 | tf_op jit(solution)/shard_map/ppermute | solution.py:526
  54.2 3.1 %collective-permute-start.16 = (f32[4,8,1152]{2,1,0:T(8,128)S(1)}, f32[4,8,1152]{2,1,0:T(8,128)S(1)}, u32[]{:S(2)}, u32[]{:S(2)}) collective-permute-start(f32[4,8,1152]{2,1,0:T(8,128)S(1)} %get-tuple-element.83), channel_id=1, source_target_pairs={{0,1},{2,3},{4,5},{6,7},{8,9},{10,11},{12,13},{14,15},{16,17},{18,... | collective-permute-start | bytes 442376 | tf_op jit(solution)/shard_map/ppermute | solution.py:540
  57.3 7.4 %collective-permute-start.17 = (f32[4,8,1152]{2,1,0:T(8,128)S(1)}, f32[4,8,1152]{2,1,0:T(8,128)S(1)}, u32[]{:S(2)}, u32[]{:S(2)}) collective-permute-start(f32[4,8,1152]{2,1,0:T(8,128)S(1)} %add.15), channel_id=1, source_target_pairs={{1,3},{3,1},{5,7},{7,5},{9,11},{11,9},{13,15},{15,13},{17,19},{19,... | collective-permute-start | bytes 442376 | tf_op jit(solution)/shard_map/ppermute | solution.py:541
  59.7 6.0 %collective-permute-start.18 = (f32[4,8,1152]{2,1,0:T(8,128)S(1)}, f32[4,8,1152]{2,1,0:T(8,128)S(1)}, u32[]{:S(2)}, u32[]{:S(2)}) collective-permute-start(f32[4,8,1152]{2,1,0:T(8,128)S(1)} %shard_map.89), channel_id=1, source_target_pairs={{0,1},{2,3},{4,5},{6,7},{8,9},{10,11},{12,13},{14,15},{16,17},{18,... | collective-permute-start | bytes 442376 | tf_op jit(solution)/shard_map/ppermute | solution.py:545
  65.7 0.7 collective-permute-start.19
  66.5 0.7 collective-permute-start.20
  67.2 11.6 %collective-permute-start.21 = (f32[4,1152]{1,0:T(4,128)S(1)}, f32[4,1152]{1,0:T(4,128)S(1)}, u32[]{:S(2)}, u32[]{:S(2)}) collective-permute-start(f32[4,1152]{1,0:T(4,128)S(1)} %slice_bitcast_fusion.1), channel_id=1, source_target_pairs={{1,0},{3,2},{5,4},{7,6},{9,8},{11,10},{13,12},{15,14},{17,16},{19,... | collective-permute-start | bytes 55304 | tf_op jit(solution)/shard_map/ppermute | solution.py:546

commit v14 on v13

--- a/solution.py
+++ b/solution.py
@@ -459,7 +459,8 @@
 
 
 def across_chips(blocks, change):
-    return [(2 * block + 1, 2 * (block ^ change) + 1) for block in range(blocks)]
+    pairs = [(2 * block, 2 * block) for block in range(blocks)]
+    return pairs + [(2 * block + 1, 2 * (block ^ change) + 1) for block in range(blocks)]
 
 
 def body(particles, significant, templates, template_class, class_counts, inv_noise):
@@ -537,13 +538,13 @@
             (state,) = sums
 
     loglik, sums, rounded, totals = sums
-    given = lax.ppermute(sums, "cls", [(0, 1)])
+    given = lax.ppermute(sums, "cls", swap)
     across = lax.ppermute(sums + given, ("blk", "cls"), across_chips(blocks, 1))
     rounded, _ = lax.optimization_barrier((rounded, given))
     rest = rest_sums(where, rounded, totals, nears, piece)
     kept = lax.optimization_barrier(rest + across)
-    total = scatter_sum(kept + lax.ppermute(rest, "cls", [(0, 1)]), blocks, bits)
-    handed = lax.ppermute(total[:per_owner], "cls", [(1, 0)])
+    total = scatter_sum(kept + lax.ppermute(rest, "cls", swap), blocks, bits)
+    handed = lax.ppermute(total[:per_owner], "cls", swap)
     total = jnp.where(core == 0, handed, total[per_owner:])
     class_avg = total[:, :width] / total[:, width][:, None]
     return loglik[0], class_avg

time: 79.9 us -> 75 us (0.939)
  waiting for transfers between devices: 15.6 us -> 6.34 us
  starting transfers between devices: 27.6 us -> 32.1 us
    ppermute x3, waiting for transfers between devices: 12.2 us -> 3.02 us  [the longest x1 1.2 us: body(): given = lax.ppermute(sums, 'cls', swap)]
    ppermute x3, starting transfers between devices: 8.37 us -> 12.8 us  [the longest x1 9.74 us: body(): handed = lax.ppermute(total[:per_owner], 'cls', swap)]
  transfers between devices with their start and end apart: 22 -> 22, of which waited for: 7 -> 7; matrix products, arithmetic and copies ran while one was open for 0% -> 1% of each run, Pallas kernels for 37% -> 39%
where the time goes in v14:
time: 75 us; the launch traced here: 74.8 us
  Pallas kernels  34.3 us (46%)
  starting transfers between devices  32.1 us (43%)
  waiting for transfers between devices  6.34 us (8%)
  other arithmetic  0.85 us (1%)
  between operations  0.85 us (1%)
    pallas_call x8, Pallas kernels, ring_scores(): pl.pallas_call(functools.partial(ring_kernel, phase, ends, sources), in_s...  19 us
    ppermute x8, starting transfers between devices, body(): own = lax.ppermute(message, ('blk', 'cls'), ring)  16.2 us
    pallas_call x3, Pallas kernels, own_scores(): pl.pallas_call(functools.partial(own_kernel, quarters), in_specs=[in_smem...  12.1 us
    ppermute x1, starting transfers between devices, body(): handed = lax.ppermute(total[:per_owner], 'cls', swap)  9.74 us
    ppermute x8, waiting for transfers between devices, body(): own = lax.ppermute(message, ('blk', 'cls'), ring)  3.29 us
    ppermute x1, starting transfers between devices, body(): total = scatter_sum(kept + lax.ppermute(rest, 'cls', swap), blocks, bits)  2.9 us
    pallas_call x1, Pallas kernels, rest_sums(): pl.pallas_call(rest_kernel, in_specs=[in_smem()] + [in_vmem()] * (2 + len...  1.74 us
  transfers between devices with their start and end apart: 22, of which 7 were waited for; matrix products, arithmetic and copies ran while one was open for 1% of the time, Pallas kernels for 39%

profile of v14, /device:TPU:0, one launch (start us, length us, event | category | flops | bytes accessed | tf_op | source)
XLA Modules:
  0.0 74.8 jit_solution(2523301139538092004)
XLA Ops:
  0.6 1.4 %shard_map.77 = (bf16[64,4096]{1,0:T(8,128)(2,1)S(1)}, bf16[64,4224]{1,0:T(8,128)(2,1)S(1)}, f32[1,8192]{1,0:T(1,128)S(1)}, s32[16,1024]{1,0:T(8,128)S(1)}) custom-call(s32[1,64]{1,0:T(1,128)} %bitcast.16, f32[1,8192]{1,0:T(1,128)} %bitcast.20, s32[16,1024]{1,0:T(8,128)} %sig_ref.1, bf16[64,8192]{1,0:T(8,128)(2,1)} %rows_ref.1), custom_call_target="tpu_custom_call" | custom-call | tf_op jit(solution)/shard_map/pallas_call | solution.py:59
  2.1 3.1 %collective-permute-start.2 = (bf16[64,4096]{1,0:T(8,128)(2,1)S(1)}, bf16[64,4096]{1,0:T(8,128)(2,1)S(1)}, u32[]{:S(2)}, u32[]{:S(2)}) collective-permute-start(bf16[64,4096]{1,0:T(8,128)(2,1)S(1)} %get-tuple-element.49.tmpl_ref), channel_id=1, source_target_pairs={{0,4},{4,8},{8,12},{12,14},{14,10},{10,6},{6,2},{2,0},{5,1},{9,5},... | collective-permute-start | bytes 1572872 | tf_op jit(solution)/shard_map/ppermute | solution.py:523
  5.1 1.6 %collective-permute-start = (bf16[64,4224]{1,0:T(8,128)(2,1)S(1)}, bf16[64,4224]{1,0:T(8,128)(2,1)S(1)}, u32[]{:S(2)}, u32[]{:S(2)}) collective-permute-start(bf16[64,4224]{1,0:T(8,128)(2,1)S(1)} %get-tuple-element.48.tmpl_ref), channel_id=1, source_target_pairs={{0,4},{4,8},{8,12},{12,14},{14,10},{10,6},{6,2},{2,0},{5,1},{9,5},... | collective-permute-start | bytes 1622024 | tf_op jit(solution)/shard_map/ppermute | solution.py:523
  6.8 6.2 %shard_map.78 = (s32[16,1024]{1,0:T(8,128)S(1)}, f32[64,1024]{1,0:T(8,128)S(1)}, f32[64,128]{1,0:T(8,128)S(1)}, bf16[2048,1024]{1,0:T(8,128)(2,1)S(1)}, bf16[204...) custom-call(s32[2]{0:T(128)S(1)} %pad_add_fusion.where_ref, ...), custom_call_target="tpu_custom_call" | custom-call | flops 2147483648 | bytes 8388608 | tf_op jit(solution)/shard_map/pallas_call | solution.py:267
  13.0 1.6 %collective-permute-start.6 = (bf16[64,4096]{1,0:T(8,128)(2,1)S(1)}, bf16[64,4096]{1,0:T(8,128)(2,1)S(1)}, u32[]{:S(2)}, u32[]{:S(2)}) collective-permute-start(bf16[64,4096]{1,0:T(8,128)(2,1)S(1)} %collective-permute-done.2.rest_0_), channel_id=1, source_target_pairs={{0,4},{4,8},{8,12},{12,14},{14,10},{10,6},{6,2},{2,0},{5,1},{9,5},... | collective-permute-start | bytes 1572872 | tf_op jit(solution)/shard_map/ppermute | solution.py:523
  14.7 2.8 %shard_map.79 = (f32[64,1024]{1,0:T(8,128)S(1)}, f32[64,128]{1,0:T(8,128)S(1)}, bf16[2048,1024]{1,0:T(8,128)(2,1)S(1)}, bf16[4,1024,512]{2,1,0:T(8,128)(2,1)S(1)}) custom-call(s32[2]{0:T(128)S(1)} %pad_add_fusion.where_ref, f32[1,8192]{1,0:T(1,128)S(1)} %get-tuple-element.47.noise_ref, bf16[64,4224]{1,0:T(8,128)(2,1)S(1)} %get-tuple-element.48.tmpl_ref, ...), custom_call_target="tpu_custom_call" | custom-call | flops 2147483648 | bytes 8388608 | tf_op jit(solution)/shard_map/pallas_call | solution.py:267
  18.1 2.0 %collective-permute-start.1 = (bf16[64,4224]{1,0:T(8,128)(2,1)S(1)}, bf16[64,4224]{1,0:T(8,128)(2,1)S(1)}, u32[]{:S(2)}, u32[]{:S(2)}) collective-permute-start(bf16[64,4224]{1,0:T(8,128)(2,1)S(1)} %collective-permute-done.rest_0_), channel_id=1, source_target_pairs={{0,4},{4,8},{8,12},{12,14},{14,10},{10,6},{6,2},{2,0},{5,1},{9,5},... | collective-permute-start | bytes 1622024 | tf_op jit(solution)/shard_map/ppermute | solution.py:523
  20.1 3.0 %shard_map.80 = (f32[16,1024]{1,0:T(8,128)S(1)}, bf16[2048,1024]{1,0:T(8,128)(2,1)S(1)}) custom-call(s32[2]{0:T(128)S(1)} %pad_add_fusion.where_ref, f32[1,8192]{1,0:T(1,128)S(1)} %get-tuple-element.47.noise_ref, bf16[64,4224]{1,0:T(8,128)(2,1)S(1)} %get-tuple-element.48.tmpl_ref, bf16[1024,8192]{1,0:T(8,128)(2,1)} %far_ref.5, ...), custom_call_target="tpu_custom_call" | custom-call | flops 2147483648 | bytes 8388608 | tf_op jit(solution)/shard_map/pallas_call | solution.py:267
  23.7 2.1 %collective-permute-start.11 = (bf16[64,4096]{1,0:T(8,128)(2,1)S(1)}, bf16[64,4096]{1,0:T(8,128)(2,1)S(1)}, u32[]{:S(2)}, u32[]{:S(2)}) collective-permute-start(bf16[64,4096]{1,0:T(8,128)(2,1)S(1)} %collective-permute-done.6.rest_0_), channel_id=1, source_target_pairs={{0,4},{4,8},{8,12},{12,14},{14,10},{10,6},{6,2},{2,0},{5,1},{9,5},... | collective-permute-start | bytes 1572872 | tf_op jit(solution)/shard_map/ppermute | solution.py:523
  25.7 2.0 %shard_map.81 = (f32[128,1024]{1,0:T(8,128)S(1)}, f32[128,128]{1,0:T(8,128)S(1)}) custom-call(s32[2]{0:T(128)S(1)} %pad_add_fusion.where_ref, f32[1,8192]{1,0:T(1,128)S(1)} %get-tuple-element.47.noise_ref, bf16[2048,1024]{1,0:T(8,128)(2,1)S(1)} %get-tuple-element.61.low_ref, bf16[2048,1024]{1,0:T(8,128)(2,1)S(1)} %get-tuple-element.62.high_ref, ...), custom_call_target="tpu_custom_call" | custom-call | flops 2147483648 | bytes 8388608 | tf_op jit(solution)/shard_map/pallas_call | solution.py:426
  27.8 1.7 %collective-permute-done.1.rest_0_ = bf16[64,4224]{1,0:T(8,128)(2,1)S(1)} collective-permute-done((bf16[64,4224]{1,0:T(8,128)(2,1)S(1)}, bf16[64,4224]{1,0:T(8,128)(2,1)S(1)}, u32[]{:S(2)}, u32[]{:S(2)}) %collective-permute-start.1) | collective-permute-done | bytes 540704 | tf_op jit(solution)/shard_map/ppermute | solution.py:523
  29.5 2.1 %collective-permute-start.4 = (bf16[64,4224]{1,0:T(8,128)(2,1)S(1)}, bf16[64,4224]{1,0:T(8,128)(2,1)S(1)}, u32[]{:S(2)}, u32[]{:S(2)}) collective-permute-start(bf16[64,4224]{1,0:T(8,128)(2,1)S(1)} %collective-permute-done.1.rest_0_), channel_id=1, source_target_pairs={{0,4},{4,8},{8,12},{12,14},{14,10},{10,6},{6,2},{2,0},{5,1},{9,5},... | collective-permute-start | bytes 1622024 | tf_op jit(solution)/shard_map/ppermute | solution.py:523
  31.5 2.4 %shard_map.83.rest_6_ = f32[16,1024]{1,0:T(8,128)S(1)} custom-call(s32[2]{0:T(128)S(1)} %pad_add_fusion.where_ref, f32[1,8192]{1,0:T(1,128)S(1)} %get-tuple-element.47.noise_ref, bf16[2048,1024]{1,0:T(8,128)(2,1)S(1)} %get-tuple-element.54.low_ref, bf16[2048,1024]{1,0:T(8,128)(2,1)S(1)} %get-tuple-element.59.high_ref, ...), custom_call_target="tpu_custom_call" | custom-call | flops 2147483648 | bytes 8388608 | tf_op jit(solution)/shard_map/pallas_call | solution.py:426
  34.0 2.0 %shard_map.82 = (f32[128,1024]{1,0:T(8,128)S(1)}, f32[128,128]{1,0:T(8,128)S(1)}) custom-call(s32[2]{0:T(128)S(1)} %pad_add_fusion.where_ref, f32[1,8192]{1,0:T(1,128)S(1)} %get-tuple-element.47.noise_ref, bf16[2048,1024]{1,0:T(8,128)(2,1)S(1)} %get-tuple-element.61.low_ref, bf16[2048,1024]{1,0:T(8,128)(2,1)S(1)} %get-tuple-element.62.high_ref, ...), custom_call_target="tpu_custom_call" | custom-call | flops 2147483648 | bytes 8388608 | tf_op jit(solution)/shard_map/pallas_call | solution.py:426
  36.3 1.5 %collective-permute-start.14 = (bf16[64,2048]{1,0:T(8,128)(2,1)S(1)}, bf16[64,2048]{1,0:T(8,128)(2,1)S(1)}, u32[]{:S(2)}, u32[]{:S(2)}) collective-permute-start(bf16[64,2048]{1,0:T(8,128)(2,1)S(1)} %constant_dynamic-slice_fusion.1), channel_id=1, source_target_pairs={{0,4},{4,8},{8,12},{12,14},{14,10},{10,6},{6,2},{2,0},{5,1},{9,5},... | collective-permute-start | bytes 786440 | tf_op jit(solution)/shard_map/ppermute | solution.py:523
  37.8 2.4 %shard_map.84.rest_6_ = f32[16,1024]{1,0:T(8,128)S(1)} custom-call(s32[2]{0:T(128)S(1)} %pad_add_fusion.where_ref, f32[1,8192]{1,0:T(1,128)S(1)} %get-tuple-element.47.noise_ref, bf16[2048,1024]{1,0:T(8,128)(2,1)S(1)} %get-tuple-element.54.low_ref, bf16[2048,1024]{1,0:T(8,128)(2,1)S(1)} %get-tuple-element.59.high_ref, ...), custom_call_target="tpu_custom_call" | custom-call | flops 2147483648 | bytes 8388608 | tf_op jit(solution)/shard_map/pallas_call | solution.py:426
  41.0 2.3 %collective-permute-start.9 = (bf16[64,2176]{1,0:T(8,128)(2,1)S(1)}, bf16[64,2176]{1,0:T(8,128)(2,1)S(1)}, u32[]{:S(2)}, u32[]{:S(2)}) collective-permute-start(bf16[64,2176]{1,0:T(8,128)(2,1)S(1)} %constant_dynamic-slice_fusion.2), channel_id=1, source_target_pairs={{0,4},{4,8},{8,12},{12,14},{14,10},{10,6},{6,2},{2,0},{5,1},{9,5},... | collective-permute-start | bytes 835592 | tf_op jit(solution)/shard_map/ppermute | solution.py:523
  43.3 2.0 %shard_map.85 = (f32[128,1024]{1,0:T(8,128)S(1)}, f32[128,128]{1,0:T(8,128)S(1)}) custom-call(s32[2]{0:T(128)S(1)} %pad_add_fusion.where_ref, f32[1,8192]{1,0:T(1,128)S(1)} %get-tuple-element.47.noise_ref, bf16[2048,1024]{1,0:T(8,128)(2,1)S(1)} %get-tuple-element.61.low_ref, bf16[2048,1024]{1,0:T(8,128)(2,1)S(1)} %get-tuple-element.62.high_ref, ...), custom_call_target="tpu_custom_call" | custom-call | flops 2147483648 | bytes 8388608 | tf_op jit(solution)/shard_map/pallas_call | solution.py:426
  45.6 2.4 %shard_map.86.rest_6_ = f32[16,1024]{1,0:T(8,128)S(1)} custom-call(s32[2]{0:T(128)S(1)} %pad_add_fusion.where_ref, f32[1,8192]{1,0:T(1,128)S(1)} %get-tuple-element.47.noise_ref, bf16[2048,1024]{1,0:T(8,128)(2,1)S(1)} %get-tuple-element.54.low_ref, bf16[2048,1024]{1,0:T(8,128)(2,1)S(1)} %get-tuple-element.59.high_ref, ...), custom_call_target="tpu_custom_call" | custom-call | flops 2147483648 | bytes 8388608 | tf_op jit(solution)/shard_map/pallas_call | solution.py:426
  48.4 2.2 %shard_map.87 = (f32[64,1024]{1,0:T(8,128)S(1)}, f32[64,128]{1,0:T(8,128)S(1)}) custom-call(s32[2]{0:T(128)S(1)} %pad_add_fusion.where_ref, f32[1,8192]{1,0:T(1,128)S(1)} %get-tuple-element.47.noise_ref, bf16[2048,1024]{1,0:T(8,128)(2,1)S(1)} %get-tuple-element.61.low_ref, bf16[2048,1024]{1,0:T(8,128)(2,1)S(1)} %get-tuple-element.62.high_ref, ...), custom_call_target="tpu_custom_call" | custom-call | flops 2147483648 | bytes 8388608 | tf_op jit(solution)/shard_map/pallas_call | solution.py:426
  50.6 3.6 %shard_map.88 = (f32[1,1024]{1,0:T(1,128)}, f32[4,8,1152]{2,1,0:T(8,128)S(1)}, bf16[8,1024]{1,0:T(8,128)(2,1)S(1)}, f32[8,128]{1,0:T(8,128)S(1)}) custom-call(s32[2]{0:T(128)S(1)} %pad_add_fusion.where_ref, f32[1,8192]{1,0:T(1,128)S(1)} %get-tuple-element.47.noise_ref, bf16[2048,1024]{1,0:T(8,128)(2,1)S(1)} %get-tuple-element.54.low_ref, ...), custom_call_target="tpu_custom_call" | custom-call | flops 2147483648 | bytes 8388608 | tf_op jit(solution)/shard_map/pallas_call | solution.py:426
  56.3 1.7 %shard_map.89 = f32[4,8,1152]{2,1,0:T(8,128)S(1)} custom-call(s32[2]{0:T(128)S(1)} %pad_add_fusion.where_ref, bf16[8,1024]{1,0:T(8,128)(2,1)S(1)} %get-tuple-element.84.rounded_ref, f32[8,128]{1,0:T(8,128)S(1)} %get-tuple-element.85.totals_ref, bf16[8,1024,512]{2,1,0:T(8,128)(2,1)S(1)} %get-tuple-element.80.rest_8_.rest_0_, ...), custom_call_target="tpu_custom_call" | custom-call | flops 1073741824 | bytes 4194304 | tf_op jit(solution)/shard_map/pallas_call | solution.py:320
  58.0 2.9 %collective-permute-start.18 = (f32[4,8,1152]{2,1,0:T(8,128)S(1)}, f32[4,8,1152]{2,1,0:T(8,128)S(1)}, u32[]{:S(2)}, u32[]{:S(2)}) collective-permute-start(f32[4,8,1152]{2,1,0:T(8,128)S(1)} %shard_map.89), channel_id=1, source_target_pairs={{0,1},{1,0},{2,3},{3,2},{4,5},{5,4},{6,7},{7,6},{8,9},{9,8},{10,11... | collective-permute-start | bytes 442376 | tf_op jit(solution)/shard_map/ppermute | solution.py:546
  63.4 9.7 %collective-permute-start.21 = (f32[4,1152]{1,0:T(4,128)S(1)}, f32[4,1152]{1,0:T(4,128)S(1)}, u32[]{:S(2)}, u32[]{:S(2)}) collective-permute-start(f32[4,1152]{1,0:T(4,128)S(1)} %slice_bitcast_fusion.1), channel_id=1, source_target_pairs={{0,1},{1,0},{2,3},{3,2},{4,5},{5,4},{6,7},{7,6},{8,9},{9,8},{10,11... | collective-permute-start | bytes 55304 | tf_op jit(solution)/shard_map/ppermute | solution.py:547
  (52 shorter events, 9.1 us)
Async XLA Ops:
  2.1 11.0 %collective-permute-start.2 = (bf16[64,4096]{1,0:T(8,128)(2,1)S(1)}, bf16[64,4096]{1,0:T(8,128)(2,1)S(1)}, u32[]{:S(2)}, u32[]{:S(2)}) collective-permute-start(bf16[64,4096]{1,0:T(8,128)(2,1)S(1)} %get-tuple-element.49.tmpl_ref), channel_id=1, source_target_pairs={{0,4},{4,8},{8,12},{12,14},{14,10},{10,6},{6,2},{2,0},{5,1},{9,5},... | collective-permute-start | bytes 1572872 | tf_op jit(solution)/shard_map/ppermute | solution.py:523
  5.1 12.9 %collective-permute-start = (bf16[64,4224]{1,0:T(8,128)(2,1)S(1)}, bf16[64,4224]{1,0:T(8,128)(2,1)S(1)}, u32[]{:S(2)}, u32[]{:S(2)}) collective-permute-start(bf16[64,4224]{1,0:T(8,128)(2,1)S(1)} %get-tuple-element.48.tmpl_ref), channel_id=1, source_target_pairs={{0,4},{4,8},{8,12},{12,14},{14,10},{10,6},{6,2},{2,0},{5,1},{9,5},... | collective-permute-start | bytes 1622024 | tf_op jit(solution)/shard_map/ppermute | solution.py:523
  13.0 10.6 %collective-permute-start.6 = (bf16[64,4096]{1,0:T(8,128)(2,1)S(1)}, bf16[64,4096]{1,0:T(8,128)(2,1)S(1)}, u32[]{:S(2)}, u32[]{:S(2)}) collective-permute-start(bf16[64,4096]{1,0:T(8,128)(2,1)S(1)} %collective-permute-done.2.rest_0_), channel_id=1, source_target_pairs={{0,4},{4,8},{8,12},{12,14},{14,10},{10,6},{6,2},{2,0},{5,1},{9,5},... | collective-permute-start | bytes 1572872 | tf_op jit(solution)/shard_map/ppermute | solution.py:523
  14.7 5.5 %copy-start.1 = (s32[8]{0:T(128)S(1)}, s32[8]{0:T(128)}, u32[]{:S(2)}) copy-start(s32[8]{0:T(128)} %rest_7_.1) | copy-start | bytes 100
  14.7 5.5 %copy-start = (s32[64]{0:T(128)S(1)}, s32[64]{0:T(128)}, u32[]{:S(2)}) copy-start(s32[64]{0:T(128)} %param.9) | copy-start | bytes 772
  17.5 8.2 %collective-permute-start.3 = (bf16[64,4096]{1,0:T(8,128)(2,1)S(1)}, bf16[64,4096]{1,0:T(8,128)(2,1)S(1)}, u32[]{:S(2)}, u32[]{:S(2)}) collective-permute-start(bf16[64,4096]{1,0:T(8,128)(2,1)S(1)} %collective-permute-done.2.rest_0_), channel_id=1, source_target_pairs={{0,1},{1,0},{2,3},{3,2},{4,5},{5,4},{6,7},{7,6},{8,9},{9,8},{10,11... | collective-permute-start | bytes 1572872 | tf_op jit(solution)/shard_map/ppermute | solution.py:527
  18.0 13.5 %collective-permute-start.8 = (bf16[64,4224]{1,0:T(8,128)(2,1)S(1)}, bf16[64,4224]{1,0:T(8,128)(2,1)S(1)}, u32[]{:S(2)}, u32[]{:S(2)}) collective-permute-start(bf16[64,4224]{1,0:T(8,128)(2,1)S(1)} %collective-permute-done.rest_0_), channel_id=1, source_target_pairs={{0,1},{1,0},{2,3},{3,2},{4,5},{5,4},{6,7},{7,6},{8,9},{9,8},{10,11... | collective-permute-start | bytes 1622024 | tf_op jit(solution)/shard_map/ppermute | solution.py:527
  18.1 11.3 %collective-permute-start.1 = (bf16[64,4224]{1,0:T(8,128)(2,1)S(1)}, bf16[64,4224]{1,0:T(8,128)(2,1)S(1)}, u32[]{:S(2)}, u32[]{:S(2)}) collective-permute-start(bf16[64,4224]{1,0:T(8,128)(2,1)S(1)} %collective-permute-done.rest_0_), channel_id=1, source_target_pairs={{0,4},{4,8},{8,12},{12,14},{14,10},{10,6},{6,2},{2,0},{5,1},{9,5},... | collective-permute-start | bytes 1622024 | tf_op jit(solution)/shard_map/ppermute | solution.py:523
  23.7 10.3 %collective-permute-start.7 = (bf16[64,4096]{1,0:T(8,128)(2,1)S(1)}, bf16[64,4096]{1,0:T(8,128)(2,1)S(1)}, u32[]{:S(2)}, u32[]{:S(2)}) collective-permute-start(bf16[64,4096]{1,0:T(8,128)(2,1)S(1)} %collective-permute-done.6.rest_0_), channel_id=1, source_target_pairs={{0,1},{1,0},{2,3},{3,2},{4,5},{5,4},{6,7},{7,6},{8,9},{9,8},{10,11... | collective-permute-start | bytes 1572872 | tf_op jit(solution)/shard_map/ppermute | solution.py:527
  23.7 12.3 %collective-permute-start.11 = (bf16[64,4096]{1,0:T(8,128)(2,1)S(1)}, bf16[64,4096]{1,0:T(8,128)(2,1)S(1)}, u32[]{:S(2)}, u32[]{:S(2)}) collective-permute-start(bf16[64,4096]{1,0:T(8,128)(2,1)S(1)} %collective-permute-done.6.rest_0_), channel_id=1, source_target_pairs={{0,4},{4,8},{8,12},{12,14},{14,10},{10,6},{6,2},{2,0},{5,1},{9,5},... | collective-permute-start | bytes 1572872 | tf_op jit(solution)/shard_map/ppermute | solution.py:523
  29.5 8.4 %collective-permute-start.5 = (bf16[64,4224]{1,0:T(8,128)(2,1)S(1)}, bf16[64,4224]{1,0:T(8,128)(2,1)S(1)}, u32[]{:S(2)}, u32[]{:S(2)}) collective-permute-start(bf16[64,4224]{1,0:T(8,128)(2,1)S(1)} %collective-permute-done.1.rest_0_), channel_id=1, source_target_pairs={{0,1},{1,0},{2,3},{3,2},{4,5},{5,4},{6,7},{7,6},{8,9},{9,8},{10,11... | collective-permute-start | bytes 1622024 | tf_op jit(solution)/shard_map/ppermute | solution.py:527
  29.5 11.4 %collective-permute-start.4 = (bf16[64,4224]{1,0:T(8,128)(2,1)S(1)}, bf16[64,4224]{1,0:T(8,128)(2,1)S(1)}, u32[]{:S(2)}, u32[]{:S(2)}) collective-permute-start(bf16[64,4224]{1,0:T(8,128)(2,1)S(1)} %collective-permute-done.1.rest_0_), channel_id=1, source_target_pairs={{0,4},{4,8},{8,12},{12,14},{14,10},{10,6},{6,2},{2,0},{5,1},{9,5},... | collective-permute-start | bytes 1622024 | tf_op jit(solution)/shard_map/ppermute | solution.py:523
  36.0 7.4 %collective-permute-start.12 = (bf16[64,4096]{1,0:T(8,128)(2,1)S(1)}, bf16[64,4096]{1,0:T(8,128)(2,1)S(1)}, u32[]{:S(2)}, u32[]{:S(2)}) collective-permute-start(bf16[64,4096]{1,0:T(8,128)(2,1)S(1)} %collective-permute-done.11.rest_0_), channel_id=1, source_target_pairs={{0,1},{1,0},{2,3},{3,2},{4,5},{5,4},{6,7},{7,6},{8,9},{9,8},{10,11... | collective-permute-start | bytes 1572872 | tf_op jit(solution)/shard_map/ppermute | solution.py:527
  36.3 9.0 %collective-permute-start.14 = (bf16[64,2048]{1,0:T(8,128)(2,1)S(1)}, bf16[64,2048]{1,0:T(8,128)(2,1)S(1)}, u32[]{:S(2)}, u32[]{:S(2)}) collective-permute-start(bf16[64,2048]{1,0:T(8,128)(2,1)S(1)} %constant_dynamic-slice_fusion.1), channel_id=1, source_target_pairs={{0,4},{4,8},{8,12},{12,14},{14,10},{10,6},{6,2},{2,0},{5,1},{9,5},... | collective-permute-start | bytes 786440 | tf_op jit(solution)/shard_map/ppermute | solution.py:523
  40.9 4.7 %collective-permute-start.10 = (bf16[64,4224]{1,0:T(8,128)(2,1)S(1)}, bf16[64,4224]{1,0:T(8,128)(2,1)S(1)}, u32[]{:S(2)}, u32[]{:S(2)}) collective-permute-start(bf16[64,4224]{1,0:T(8,128)(2,1)S(1)} %collective-permute-done.4.rest_0_), channel_id=1, source_target_pairs={{0,1},{1,0},{2,3},{3,2},{4,5},{5,4},{6,7},{7,6},{8,9},{9,8},{10,11... | collective-permute-start | bytes 1622024 | tf_op jit(solution)/shard_map/ppermute | solution.py:527
  41.0 7.0 %collective-permute-start.9 = (bf16[64,2176]{1,0:T(8,128)(2,1)S(1)}, bf16[64,2176]{1,0:T(8,128)(2,1)S(1)}, u32[]{:S(2)}, u32[]{:S(2)}) collective-permute-start(bf16[64,2176]{1,0:T(8,128)(2,1)S(1)} %constant_dynamic-slice_fusion.2), channel_id=1, source_target_pairs={{0,4},{4,8},{8,12},{12,14},{14,10},{10,6},{6,2},{2,0},{5,1},{9,5},... | collective-permute-start | bytes 835592 | tf_op jit(solution)/shard_map/ppermute | solution.py:523
  45.3 3.1 %collective-permute-start.15 = (bf16[64,2048]{1,0:T(8,128)(2,1)S(1)}, bf16[64,2048]{1,0:T(8,128)(2,1)S(1)}, u32[]{:S(2)}, u32[]{:S(2)}) collective-permute-start(bf16[64,2048]{1,0:T(8,128)(2,1)S(1)} %collective-permute-done.14.rest_0_), channel_id=1, source_target_pairs={{0,1},{1,0},{2,3},{3,2},{4,5},{5,4},{6,7},{7,6},{8,9},{9,8},{10,11... | collective-permute-start | bytes 786440 | tf_op jit(solution)/shard_map/ppermute | solution.py:527
  48.0 2.6 %collective-permute-start.13 = (bf16[64,2176]{1,0:T(8,128)(2,1)S(1)}, bf16[64,2176]{1,0:T(8,128)(2,1)S(1)}, u32[]{:S(2)}, u32[]{:S(2)}) collective-permute-start(bf16[64,2176]{1,0:T(8,128)(2,1)S(1)} %collective-permute-done.9.rest_0_), channel_id=1, source_target_pairs={{0,1},{1,0},{2,3},{3,2},{4,5},{5,4},{6,7},{7,6},{8,9},{9,8},{10,11... | collective-permute-start | bytes 835592 | tf_op jit(solution)/shard_map/ppermute | solution.py:527
  54.2 1.4 %collective-permute-start.16 = (f32[4,8,1152]{2,1,0:T(8,128)S(1)}, f32[4,8,1152]{2,1,0:T(8,128)S(1)}, u32[]{:S(2)}, u32[]{:S(2)}) collective-permute-start(f32[4,8,1152]{2,1,0:T(8,128)S(1)} %get-tuple-element.83), channel_id=1, source_target_pairs={{0,1},{1,0},{2,3},{3,2},{4,5},{5,4},{6,7},{7,6},{8,9},{9,8},{10,11... | collective-permute-start | bytes 442376 | tf_op jit(solution)/shard_map/ppermute | solution.py:541
  55.6 5.3 %collective-permute-start.17 = (f32[4,8,1152]{2,1,0:T(8,128)S(1)}, f32[4,8,1152]{2,1,0:T(8,128)S(1)}, u32[]{:S(2)}, u32[]{:S(2)}) collective-permute-start(f32[4,8,1152]{2,1,0:T(8,128)S(1)} %add.15), channel_id=1, source_target_pairs={{0,0},{2,2},{4,4},{6,6},{8,8},{10,10},{12,12},{14,14},{1,3},{3,1},... | collective-permute-start | bytes 442376 | tf_op jit(solution)/shard_map/ppermute | solution.py:542
  58.0 3.9 %collective-permute-start.18 = (f32[4,8,1152]{2,1,0:T(8,128)S(1)}, f32[4,8,1152]{2,1,0:T(8,128)S(1)}, u32[]{:S(2)}, u32[]{:S(2)}) collective-permute-start(f32[4,8,1152]{2,1,0:T(8,128)S(1)} %shard_map.89), channel_id=1, source_target_pairs={{0,1},{1,0},{2,3},{3,2},{4,5},{5,4},{6,7},{7,6},{8,9},{9,8},{10,11... | collective-permute-start | bytes 442376 | tf_op jit(solution)/shard_map/ppermute | solution.py:546
  62.0 0.7 collective-permute-start.19
  62.7 0.7 collective-permute-start.20
  63.4 10.6 %collective-permute-start.21 = (f32[4,1152]{1,0:T(4,128)S(1)}, f32[4,1152]{1,0:T(4,128)S(1)}, u32[]{:S(2)}, u32[]{:S(2)}) collective-permute-start(f32[4,1152]{1,0:T(4,128)S(1)} %slice_bitcast_fusion.1), channel_id=1, source_target_pairs={{0,1},{1,0},{2,3},{3,2},{4,5},{5,4},{6,7},{7,6},{8,9},{9,8},{10,11... | collective-permute-start | bytes 55304 | tf_op jit(solution)/shard_map/ppermute | solution.py:547

commit v15 on v12

--- a/solution.py
+++ b/solution.py
@@ -8,7 +8,8 @@
 from jax.sharding import PartitionSpec as P
 
 LOWEST = -1e30
-STEPS = 16
+CHUNK = 1024
+PIECES = 2
 WIDTH = 1024
 STRIP = 256
 LANES = 128
@@ -174,23 +175,29 @@
     else:
         acc_in, energy_in, near, acc, energy, *turned_refs, next_ref, late = rest
     span, height = turned_refs[0].shape[0], tmpl_ref.shape[0]
-    steps, _, width = near.shape
+    chunks, _, chunk = near.shape
+    steps = chunks * PIECES
+    width = chunk // PIECES
     low = quarters[0] * span
+
+    def part(ref, step):
+        columns = pl.ds(pl.multiple_of(lax.rem(step, PIECES) * width, width), width)
+        return ref.at[lax.div(step, PIECES), :, columns]
 
     def copies(step):
         columns = pl.ds(pl.multiple_of(low + step * width, width), width)
-        return spread_copies(far_ref.at[:, columns], near.at[step], arrived.at[step])
+        return spread_copies(far_ref.at[:, columns], part(near, step), arrived.at[step])
 
     def following(step):
         columns = pl.ds(low + (steps + step) * width, width)
-        return spread_copies(far_ref.at[:, columns], next_ref.at[step], late.at[step])
+        return spread_copies(far_ref.at[:, columns], part(next_ref, step), late.at[step])
 
     if first:
         for step in range(steps):
             for copy in copies(step):
                 copy.start()
     if not last:
-        for step in range(next_ref.shape[0]):
+        for step in range(next_ref.shape[0] * PIECES):
             for copy in following(step):
                 copy.start()
     if first:
@@ -210,16 +217,16 @@
                     copy.wait()
             for strip in range(0, width, STRIP):
                 there = pl.ds(pl.multiple_of(inner * width + strip, STRIP), STRIP)
-                part = quarter % 2 * span + inner * width + strip
-                here = pl.ds(pl.multiple_of(part, STRIP), STRIP)
+                start = quarter % 2 * span + inner * width + strip
+                here = pl.ds(pl.multiple_of(start, STRIP), STRIP)
                 columns = pl.ds(pl.multiple_of(low + step * width + strip, STRIP), STRIP)
                 weighted = weigh(tmpl_ref[:, here], noise_ref[:, columns], energy)
-                turned = jnp.transpose(near[step, :, strip : strip + STRIP])
+                turned = jnp.transpose(part(near, step)[:, strip : strip + STRIP])
                 turned_ref[there, :] = turned
                 acc[...] += jnp.dot(weighted, turned, preferred_element_type=jnp.float32)
 
     if not last:
-        for step in range(next_ref.shape[0]):
+        for step in range(next_ref.shape[0] * PIECES):
             for copy in following(step):
                 copy.wait()
         return
@@ -235,19 +242,19 @@
 def own_scores(quarters, where, noise, particles, templates, rest, total=0):
     per_device, freqs = particles.shape
     height = templates.shape[0]
-    width = freqs // STEPS
     span = freqs // 4
-    steps = span // width
+    chunks = span // CHUNK
+    steps = chunks * PIECES
     first, last = quarters[0] == 0, quarters[-1] == 3
     sums = [
         jax.ShapeDtypeStruct((height, per_device), jnp.float32),
         jax.ShapeDtypeStruct((height, LANES), jnp.float32),
     ]
     turned = [pltpu.VMEM((span, per_device), particles.dtype)] * len(quarters)
-    raw = pltpu.VMEM((steps, per_device, width), particles.dtype)
+    raw = pltpu.VMEM((chunks, per_device, CHUNK), particles.dtype)
     if first:
         shapes = [jax.ShapeDtypeStruct((total // 32, per_device), jnp.int32)] + sums
-        shapes += turned + [pltpu.VMEM((2 * steps, per_device, width), particles.dtype), raw]
+        shapes += turned + [pltpu.VMEM((2 * chunks, per_device, CHUNK), particles.dtype), raw]
         rest_specs = [in_vmem()]
         scratch = [
             pltpu.SemaphoreType.DMA((2 * steps, 4)),
@@ -301,18 +308,18 @@
 def class_sums(rounded, totals, bit, nears, mine_ref, theirs_ref):
     per_owner = mine_ref.shape[1]
     chunk = nears[0].shape[2]
-    share = mine_ref.shape[2] // chunk
+    width = mine_ref.shape[2] - LANES
     piece = 0
     for near in nears:
-        for pair in range(near.shape[0] // (2 * share)):
-            for part in range(share):
-                at = (2 * pair + bit) * share + part
-                sums = jnp.dot(rounded, near[at], preferred_element_type=jnp.float32)
-                columns = pl.ds(part * chunk, chunk)
-                mine_ref[piece, :, columns] = sums[:per_owner]
-                theirs_ref[piece, :, columns] = sums[per_owner:]
-            mine_ref[piece, :, share * chunk :] = totals[:per_owner]
-            theirs_ref[piece, :, share * chunk :] = totals[per_owner:]
+        for pair in range(near.shape[0] * chunk // (2 * width)):
+            start = (2 * pair + bit) * width
+            at, low = lax.div(start, chunk), lax.rem(start, chunk)
+            columns = pl.ds(pl.multiple_of(low, width), width) if width < chunk else slice(None)
+            sums = jnp.dot(rounded, near[at, :, columns], preferred_element_type=jnp.float32)
+            mine_ref[piece, :, :width] = sums[:per_owner]
+            theirs_ref[piece, :, :width] = sums[per_owner:]
+            mine_ref[piece, :, width:] = totals[:per_owner]
+            theirs_ref[piece, :, width:] = totals[per_owner:]
             piece += 1
 
 

time: 70 us -> 70 us (level)
  transfers between devices with their start and end apart: 21 -> 21, of which waited for: 9 -> 9; matrix products, arithmetic and copies ran while one was open for 1% -> 1% of each run, Pallas kernels for 42% -> 43%
where the time goes in v15:
time: 70 us; the launch traced here: 69.8 us
  Pallas kernels  34.8 us (50%)
  starting transfers between devices  23.5 us (34%)
  waiting for transfers between devices  9.48 us (14%)
  other arithmetic  0.85 us (1%)
  between operations  0.79 us (1%)
    pallas_call x8, Pallas kernels, ring_scores(): pl.pallas_call(functools.partial(ring_kernel, phase, ends, sources), in_s...  19 us
    ppermute x8, starting transfers between devices, body(): own = lax.ppermute(message, ('blk', 'cls'), ring)  15.9 us
    pallas_call x3, Pallas kernels, own_scores(): pl.pallas_call(functools.partial(own_kernel, quarters), in_specs=[in_smem...  12.6 us
    ppermute x2, waiting for transfers between devices, scatter_sum(): pieces = keep + lax.ppermute(send, 'blk', swaps)  4.4 us
    ppermute x2, starting transfers between devices, scatter_sum(): pieces = keep + lax.ppermute(send, 'blk', swaps)  4.35 us
    ppermute x8, waiting for transfers between devices, body(): own = lax.ppermute(message, ('blk', 'cls'), ring)  2.8 us
    pallas_call x1, Pallas kernels, rest_sums(): pl.pallas_call(rest_kernel, in_specs=[in_smem()] + [in_vmem()] * (2 + len...  1.75 us
    ppermute x1, starting transfers between devices, body(): lax.ppermute(mine + given, 'blk', [(i, i ^ 1) for i in range(blocks)])  1.64 us
  transfers between devices with their start and end apart: 21, of which 9 were waited for; matrix products, arithmetic and copies ran while one was open for 1% of the time, Pallas kernels for 43%

profile of v15, /device:TPU:0, one launch (start us, length us, event | category | flops | bytes accessed | tf_op | source)
XLA Modules:
  0.0 69.8 jit_solution(7035302039158997693)
XLA Ops:
  2.1 3.1 %collective-permute-start.2 = (bf16[64,4096]{1,0:T(8,128)(2,1)S(1)}, bf16[64,4096]{1,0:T(8,128)(2,1)S(1)}, u32[]{:S(2)}, u32[]{:S(2)}) collective-permute-start(bf16[64,4096]{1,0:T(8,128)(2,1)S(1)} %get-tuple-element.52.tmpl_ref), channel_id=1, source_target_pairs={{0,4},{4,8},{8,12},{12,14},{14,10},{10,6},{6,2},{2,0},{5,1},{9,5},... | collective-permute-start | bytes 1572872 | tf_op jit(solution)/shard_map/ppermute | solution.py:536
  6.8 6.5 %shard_map.78 = (s32[16,1024]{1,0:T(8,128)S(1)}, f32[64,1024]{1,0:T(8,128)S(1)}, f32[64,128]{1,0:T(8,128)S(1)}, bf16[2048,1024]{1,0:T(8,128)(2,1)S(1)}, bf16[204...) custom-call(s32[2]{0:T(128)S(1)} %pad_add_fusion.where_ref, ...), custom_call_target="tpu_custom_call" | custom-call | flops 2147483648 | bytes 8388608 | tf_op jit(solution)/shard_map/pallas_call | solution.py:274
  13.3 1.6 %collective-permute-start.6 = (bf16[64,4096]{1,0:T(8,128)(2,1)S(1)}, bf16[64,4096]{1,0:T(8,128)(2,1)S(1)}, u32[]{:S(2)}, u32[]{:S(2)}) collective-permute-start(bf16[64,4096]{1,0:T(8,128)(2,1)S(1)} %collective-permute-done.2.rest_0_), channel_id=1, source_target_pairs={{0,4},{4,8},{8,12},{12,14},{14,10},{10,6},{6,2},{2,0},{5,1},{9,5},... | collective-permute-start | bytes 1572872 | tf_op jit(solution)/shard_map/ppermute | solution.py:536
  15.0 2.9 %shard_map.79 = (f32[64,1024]{1,0:T(8,128)S(1)}, f32[64,128]{1,0:T(8,128)S(1)}, bf16[2048,1024]{1,0:T(8,128)(2,1)S(1)}, bf16[2,1024,1024]{2,1,0:T(8,128)(2,1)S(1)}) custom-call(s32[2]{0:T(128)S(1)} %pad_add_fusion.where_ref, f32[1,8192]{1,0:T(1,128)S(1)} %get-tuple-element.50.noise_ref, bf16[64,4224]{1,0:T(8,128)(2,1)S(1)} %get-tuple-element.51.tmpl_ref, ...), custom_call_target="tpu_custom_call" | custom-call | flops 2147483648 | bytes 8388608 | tf_op jit(solution)/shard_map/pallas_call | solution.py:274
  18.5 1.7 %collective-permute-start.1 = (bf16[64,4224]{1,0:T(8,128)(2,1)S(1)}, bf16[64,4224]{1,0:T(8,128)(2,1)S(1)}, u32[]{:S(2)}, u32[]{:S(2)}) collective-permute-start(bf16[64,4224]{1,0:T(8,128)(2,1)S(1)} %collective-permute-done.rest_0_), channel_id=1, source_target_pairs={{0,4},{4,8},{8,12},{12,14},{14,10},{10,6},{6,2},{2,0},{5,1},{9,5},... | collective-permute-start | bytes 1622024 | tf_op jit(solution)/shard_map/ppermute | solution.py:536
  20.1 3.1 %shard_map.80 = (f32[16,1024]{1,0:T(8,128)S(1)}, bf16[2048,1024]{1,0:T(8,128)(2,1)S(1)}) custom-call(s32[2]{0:T(128)S(1)} %pad_add_fusion.where_ref, f32[1,8192]{1,0:T(1,128)S(1)} %get-tuple-element.50.noise_ref, bf16[64,4224]{1,0:T(8,128)(2,1)S(1)} %get-tuple-element.51.tmpl_ref, bf16[1024,8192]{1,0:T(8,128)(2,1)} %far_ref.5, ...), custom_call_target="tpu_custom_call" | custom-call | flops 2147483648 | bytes 8388608 | tf_op jit(solution)/shard_map/pallas_call | solution.py:274
  23.7 2.1 %collective-permute-start.11 = (bf16[64,4096]{1,0:T(8,128)(2,1)S(1)}, bf16[64,4096]{1,0:T(8,128)(2,1)S(1)}, u32[]{:S(2)}, u32[]{:S(2)}) collective-permute-start(bf16[64,4096]{1,0:T(8,128)(2,1)S(1)} %collective-permute-done.6.rest_0_), channel_id=1, source_target_pairs={{0,4},{4,8},{8,12},{12,14},{14,10},{10,6},{6,2},{2,0},{5,1},{9,5},... | collective-permute-start | bytes 1572872 | tf_op jit(solution)/shard_map/ppermute | solution.py:536
  25.7 2.0 %shard_map.81 = (f32[128,1024]{1,0:T(8,128)S(1)}, f32[128,128]{1,0:T(8,128)S(1)}) custom-call(s32[2]{0:T(128)S(1)} %pad_add_fusion.where_ref, f32[1,8192]{1,0:T(1,128)S(1)} %get-tuple-element.50.noise_ref, bf16[2048,1024]{1,0:T(8,128)(2,1)S(1)} %get-tuple-element.64.low_ref, bf16[2048,1024]{1,0:T(8,128)(2,1)S(1)} %get-tuple-element.65.high_ref, ...), custom_call_target="tpu_custom_call" | custom-call | flops 2147483648 | bytes 8388608 | tf_op jit(solution)/shard_map/pallas_call | solution.py:443
  27.8 1.7 %collective-permute-done.1.rest_0_ = bf16[64,4224]{1,0:T(8,128)(2,1)S(1)} collective-permute-done((bf16[64,4224]{1,0:T(8,128)(2,1)S(1)}, bf16[64,4224]{1,0:T(8,128)(2,1)S(1)}, u32[]{:S(2)}, u32[]{:S(2)}) %collective-permute-start.1) | collective-permute-done | bytes 540704 | tf_op jit(solution)/shard_map/ppermute | solution.py:536
  29.5 2.1 %collective-permute-start.4 = (bf16[64,4224]{1,0:T(8,128)(2,1)S(1)}, bf16[64,4224]{1,0:T(8,128)(2,1)S(1)}, u32[]{:S(2)}, u32[]{:S(2)}) collective-permute-start(bf16[64,4224]{1,0:T(8,128)(2,1)S(1)} %collective-permute-done.1.rest_0_), channel_id=1, source_target_pairs={{0,4},{4,8},{8,12},{12,14},{14,10},{10,6},{6,2},{2,0},{5,1},{9,5},... | collective-permute-start | bytes 1622024 | tf_op jit(solution)/shard_map/ppermute | solution.py:536
  31.5 2.4 %shard_map.83.rest_6_ = f32[16,1024]{1,0:T(8,128)S(1)} custom-call(s32[2]{0:T(128)S(1)} %pad_add_fusion.where_ref, f32[1,8192]{1,0:T(1,128)S(1)} %get-tuple-element.50.noise_ref, bf16[2048,1024]{1,0:T(8,128)(2,1)S(1)} %get-tuple-element.57.low_ref, bf16[2048,1024]{1,0:T(8,128)(2,1)S(1)} %get-tuple-element.62.high_ref, ...), custom_call_target="tpu_custom_call" | custom-call | flops 2147483648 | bytes 8388608 | tf_op jit(solution)/shard_map/pallas_call | solution.py:443
  34.0 2.0 %shard_map.82 = (f32[128,1024]{1,0:T(8,128)S(1)}, f32[128,128]{1,0:T(8,128)S(1)}) custom-call(s32[2]{0:T(128)S(1)} %pad_add_fusion.where_ref, f32[1,8192]{1,0:T(1,128)S(1)} %get-tuple-element.50.noise_ref, bf16[2048,1024]{1,0:T(8,128)(2,1)S(1)} %get-tuple-element.64.low_ref, bf16[2048,1024]{1,0:T(8,128)(2,1)S(1)} %get-tuple-element.65.high_ref, ...), custom_call_target="tpu_custom_call" | custom-call | flops 2147483648 | bytes 8388608 | tf_op jit(solution)/shard_map/pallas_call | solution.py:443
  37.8 2.4 %shard_map.84.rest_6_ = f32[16,1024]{1,0:T(8,128)S(1)} custom-call(s32[2]{0:T(128)S(1)} %pad_add_fusion.where_ref, f32[1,8192]{1,0:T(1,128)S(1)} %get-tuple-element.50.noise_ref, bf16[2048,1024]{1,0:T(8,128)(2,1)S(1)} %get-tuple-element.57.low_ref, bf16[2048,1024]{1,0:T(8,128)(2,1)S(1)} %get-tuple-element.62.high_ref, ...), custom_call_target="tpu_custom_call" | custom-call | flops 2147483648 | bytes 8388608 | tf_op jit(solution)/shard_map/pallas_call | solution.py:443
  41.0 2.3 %collective-permute-start.9 = (bf16[64,2176]{1,0:T(8,128)(2,1)S(1)}, bf16[64,2176]{1,0:T(8,128)(2,1)S(1)}, u32[]{:S(2)}, u32[]{:S(2)}) collective-permute-start(bf16[64,2176]{1,0:T(8,128)(2,1)S(1)} %constant_dynamic-slice_fusion.2), channel_id=1, source_target_pairs={{0,4},{4,8},{8,12},{12,14},{14,10},{10,6},{6,2},{2,0},{5,1},{9,5},... | collective-permute-start | bytes 835592 | tf_op jit(solution)/shard_map/ppermute | solution.py:536
  43.3 2.0 %shard_map.85 = (f32[128,1024]{1,0:T(8,128)S(1)}, f32[128,128]{1,0:T(8,128)S(1)}) custom-call(s32[2]{0:T(128)S(1)} %pad_add_fusion.where_ref, f32[1,8192]{1,0:T(1,128)S(1)} %get-tuple-element.50.noise_ref, bf16[2048,1024]{1,0:T(8,128)(2,1)S(1)} %get-tuple-element.64.low_ref, bf16[2048,1024]{1,0:T(8,128)(2,1)S(1)} %get-tuple-element.65.high_ref, ...), custom_call_target="tpu_custom_call" | custom-call | flops 2147483648 | bytes 8388608 | tf_op jit(solution)/shard_map/pallas_call | solution.py:443
  45.6 2.4 %shard_map.86.rest_6_ = f32[16,1024]{1,0:T(8,128)S(1)} custom-call(s32[2]{0:T(128)S(1)} %pad_add_fusion.where_ref, f32[1,8192]{1,0:T(1,128)S(1)} %get-tuple-element.50.noise_ref, bf16[2048,1024]{1,0:T(8,128)(2,1)S(1)} %get-tuple-element.57.low_ref, bf16[2048,1024]{1,0:T(8,128)(2,1)S(1)} %get-tuple-element.62.high_ref, ...), custom_call_target="tpu_custom_call" | custom-call | flops 2147483648 | bytes 8388608 | tf_op jit(solution)/shard_map/pallas_call | solution.py:443
  48.4 2.2 %shard_map.87 = (f32[64,1024]{1,0:T(8,128)S(1)}, f32[64,128]{1,0:T(8,128)S(1)}) custom-call(s32[2]{0:T(128)S(1)} %pad_add_fusion.where_ref, f32[1,8192]{1,0:T(1,128)S(1)} %get-tuple-element.50.noise_ref, bf16[2048,1024]{1,0:T(8,128)(2,1)S(1)} %get-tuple-element.64.low_ref, bf16[2048,1024]{1,0:T(8,128)(2,1)S(1)} %get-tuple-element.65.high_ref, ...), custom_call_target="tpu_custom_call" | custom-call | flops 2147483648 | bytes 8388608 | tf_op jit(solution)/shard_map/pallas_call | solution.py:443
  50.6 3.6 %shard_map.88 = (f32[1,1024]{1,0:T(1,128)}, f32[4,4,1152]{2,1,0:T(4,128)S(1)}, f32[4,4,1152]{2,1,0:T(4,128)S(1)}, bf16[8,1024]{1,0:T(8,128)(2,1)S(1)}, f32[8,128]{1,0:T(8,128)S(1)}) custom-call(s32[2]{0:T(128)S(1)} %pad_add_fusion.where_ref, f32[1,8192]{1,0:T(1,128)S(1)} %get-tuple-element.50.noise_ref, bf16[2048,1024]{1,0:T(8,128)(2,1)S(1)} %get-tuple-element.57.low_ref, ...), custom_call_target="tpu_custom_call" | custom-call | flops 2147483648 | bytes 8388608 | tf_op jit(solution)/shard_map/pallas_call | solution.py:443
  55.5 1.6 %collective-permute-start.17 = (f32[4,4,1152]{2,1,0:T(4,128)S(1)}, f32[4,4,1152]{2,1,0:T(4,128)S(1)}, u32[]{:S(2)}, u32[]{:S(2)}) collective-permute-start(f32[4,4,1152]{2,1,0:T(4,128)S(1)} %add.15), channel_id=1, source_target_pairs={{0,2},{2,0},{4,6},{6,4},{8,10},{10,8},{12,14},{14,12},{1,3},{3,1},... | collective-permute-start | bytes 221192 | tf_op jit(solution)/shard_map/ppermute | solution.py:555
  57.1 1.7 %shard_map.89 = (f32[4,4,1152]{2,1,0:T(4,128)S(1)}, f32[4,4,1152]{2,1,0:T(4,128)S(1)}) custom-call(s32[2]{0:T(128)S(1)} %pad_add_fusion.where_ref, bf16[8,1024]{1,0:T(8,128)(2,1)S(1)} %get-tuple-element.87.rounded_ref, f32[8,128]{1,0:T(8,128)S(1)} %get-tuple-element.88.totals_ref, bf16[4,1024,1024]{2,1,0:T(8,128)(2,1)S(1)} %get-tuple-element.83.rest_8_.rest_0_, ...), custom_call_target="tpu_custom_call" | custom-call | flops 1073741824 | bytes 4194304 | tf_op jit(solution)/shard_map/pallas_call | solution.py:336
  60.2 1.7 %collective-permute-start.19 = (f32[2,4,1152]{2,1,0:T(4,128)S(1)}, f32[2,4,1152]{2,1,0:T(4,128)S(1)}, u32[]{:S(2)}, u32[]{:S(2)}) collective-permute-start(f32[2,4,1152]{2,1,0:T(4,128)S(1)} %dynamic-slice_bitcast_fusion), channel_id=1, source_target_pairs={{0,4},{2,6},{4,0},{6,2},{8,12},{10,14},{12,8},{14,10},{1,5},{3,7},... | collective-permute-start | bytes 110600 | tf_op jit(solution)/shard_map/ppermute | solution.py:475
  61.9 2.4 %collective-permute-done.19 = f32[2,4,1152]{2,1,0:T(4,128)S(1)} collective-permute-done((f32[2,4,1152]{2,1,0:T(4,128)S(1)}, f32[2,4,1152]{2,1,0:T(4,128)S(1)}, u32[]{:S(2)}, u32[]{:S(2)}) %collective-permute-start.19) | collective-permute-done | bytes 36896 | tf_op jit(solution)/shard_map/ppermute | solution.py:475
  64.3 2.7 %collective-permute-start.20 = (f32[1,4,1152]{2,1,0:T(4,128)S(1)}, f32[1,4,1152]{2,1,0:T(4,128)S(1)}, u32[]{:S(2)}, u32[]{:S(2)}) collective-permute-start(f32[1,4,1152]{2,1,0:T(4,128)S(1)} %constant_dynamic-slice_fusion), channel_id=1, source_target_pairs={{0,8},{2,10},{4,12},{6,14},{8,0},{10,2},{12,4},{14,6},{1,9},{3,11}... | collective-permute-start | bytes 55304 | tf_op jit(solution)/shard_map/ppermute | solution.py:475
  67.0 2.0 %collective-permute-done.20 = f32[1,4,1152]{2,1,0:T(4,128)S(1)} collective-permute-done((f32[1,4,1152]{2,1,0:T(4,128)S(1)}, f32[1,4,1152]{2,1,0:T(4,128)S(1)}, u32[]{:S(2)}, u32[]{:S(2)}) %collective-permute-start.20) | collective-permute-done | bytes 18464 | tf_op jit(solution)/shard_map/ppermute | solution.py:475
  (48 shorter events, 10.8 us)
Async XLA Ops:
  2.1 11.3 %collective-permute-start.2 = (bf16[64,4096]{1,0:T(8,128)(2,1)S(1)}, bf16[64,4096]{1,0:T(8,128)(2,1)S(1)}, u32[]{:S(2)}, u32[]{:S(2)}) collective-permute-start(bf16[64,4096]{1,0:T(8,128)(2,1)S(1)} %get-tuple-element.52.tmpl_ref), channel_id=1, source_target_pairs={{0,4},{4,8},{8,12},{12,14},{14,10},{10,6},{6,2},{2,0},{5,1},{9,5},... | collective-permute-start | bytes 1572872 | tf_op jit(solution)/shard_map/ppermute | solution.py:536
  5.1 12.9 %collective-permute-start = (bf16[64,4224]{1,0:T(8,128)(2,1)S(1)}, bf16[64,4224]{1,0:T(8,128)(2,1)S(1)}, u32[]{:S(2)}, u32[]{:S(2)}) collective-permute-start(bf16[64,4224]{1,0:T(8,128)(2,1)S(1)} %get-tuple-element.51.tmpl_ref), channel_id=1, source_target_pairs={{0,4},{4,8},{8,12},{12,14},{14,10},{10,6},{6,2},{2,0},{5,1},{9,5},... | collective-permute-start | bytes 1622024 | tf_op jit(solution)/shard_map/ppermute | solution.py:536
  13.3 10.3 %collective-permute-start.6 = (bf16[64,4096]{1,0:T(8,128)(2,1)S(1)}, bf16[64,4096]{1,0:T(8,128)(2,1)S(1)}, u32[]{:S(2)}, u32[]{:S(2)}) collective-permute-start(bf16[64,4096]{1,0:T(8,128)(2,1)S(1)} %collective-permute-done.2.rest_0_), channel_id=1, source_target_pairs={{0,4},{4,8},{8,12},{12,14},{14,10},{10,6},{6,2},{2,0},{5,1},{9,5},... | collective-permute-start | bytes 1572872 | tf_op jit(solution)/shard_map/ppermute | solution.py:536
  15.0 5.2 %copy-start.1 = (s32[8]{0:T(128)S(1)}, s32[8]{0:T(128)}, u32[]{:S(2)}) copy-start(s32[8]{0:T(128)} %rest_7_.1) | copy-start | bytes 100
  15.0 5.2 %copy-start = (s32[64]{0:T(128)S(1)}, s32[64]{0:T(128)}, u32[]{:S(2)}) copy-start(s32[64]{0:T(128)} %param.9) | copy-start | bytes 772
  17.9 7.9 %collective-permute-start.3 = (bf16[64,4096]{1,0:T(8,128)(2,1)S(1)}, bf16[64,4096]{1,0:T(8,128)(2,1)S(1)}, u32[]{:S(2)}, u32[]{:S(2)}) collective-permute-start(bf16[64,4096]{1,0:T(8,128)(2,1)S(1)} %collective-permute-done.2.rest_0_), channel_id=1, source_target_pairs={{0,1},{1,0},{2,3},{3,2},{4,5},{5,4},{6,7},{7,6},{8,9},{9,8},{10,11... | collective-permute-start | bytes 1572872 | tf_op jit(solution)/shard_map/ppermute | solution.py:540
  18.0 13.5 %collective-permute-start.8 = (bf16[64,4224]{1,0:T(8,128)(2,1)S(1)}, bf16[64,4224]{1,0:T(8,128)(2,1)S(1)}, u32[]{:S(2)}, u32[]{:S(2)}) collective-permute-start(bf16[64,4224]{1,0:T(8,128)(2,1)S(1)} %collective-permute-done.rest_0_), channel_id=1, source_target_pairs={{0,1},{1,0},{2,3},{3,2},{4,5},{5,4},{6,7},{7,6},{8,9},{9,8},{10,11... | collective-permute-start | bytes 1622024 | tf_op jit(solution)/shard_map/ppermute | solution.py:540
  18.5 11.0 %collective-permute-start.1 = (bf16[64,4224]{1,0:T(8,128)(2,1)S(1)}, bf16[64,4224]{1,0:T(8,128)(2,1)S(1)}, u32[]{:S(2)}, u32[]{:S(2)}) collective-permute-start(bf16[64,4224]{1,0:T(8,128)(2,1)S(1)} %collective-permute-done.rest_0_), channel_id=1, source_target_pairs={{0,4},{4,8},{8,12},{12,14},{14,10},{10,6},{6,2},{2,0},{5,1},{9,5},... | collective-permute-start | bytes 1622024 | tf_op jit(solution)/shard_map/ppermute | solution.py:536
  23.7 10.3 %collective-permute-start.7 = (bf16[64,4096]{1,0:T(8,128)(2,1)S(1)}, bf16[64,4096]{1,0:T(8,128)(2,1)S(1)}, u32[]{:S(2)}, u32[]{:S(2)}) collective-permute-start(bf16[64,4096]{1,0:T(8,128)(2,1)S(1)} %collective-permute-done.6.rest_0_), channel_id=1, source_target_pairs={{0,1},{1,0},{2,3},{3,2},{4,5},{5,4},{6,7},{7,6},{8,9},{9,8},{10,11... | collective-permute-start | bytes 1572872 | tf_op jit(solution)/shard_map/ppermute | solution.py:540
  23.7 12.3 %collective-permute-start.11 = (bf16[64,4096]{1,0:T(8,128)(2,1)S(1)}, bf16[64,4096]{1,0:T(8,128)(2,1)S(1)}, u32[]{:S(2)}, u32[]{:S(2)}) collective-permute-start(bf16[64,4096]{1,0:T(8,128)(2,1)S(1)} %collective-permute-done.6.rest_0_), channel_id=1, source_target_pairs={{0,4},{4,8},{8,12},{12,14},{14,10},{10,6},{6,2},{2,0},{5,1},{9,5},... | collective-permute-start | bytes 1572872 | tf_op jit(solution)/shard_map/ppermute | solution.py:536
  29.5 8.4 %collective-permute-start.5 = (bf16[64,4224]{1,0:T(8,128)(2,1)S(1)}, bf16[64,4224]{1,0:T(8,128)(2,1)S(1)}, u32[]{:S(2)}, u32[]{:S(2)}) collective-permute-start(bf16[64,4224]{1,0:T(8,128)(2,1)S(1)} %collective-permute-done.1.rest_0_), channel_id=1, source_target_pairs={{0,1},{1,0},{2,3},{3,2},{4,5},{5,4},{6,7},{7,6},{8,9},{9,8},{10,11... | collective-permute-start | bytes 1622024 | tf_op jit(solution)/shard_map/ppermute | solution.py:540
  29.5 11.4 %collective-permute-start.4 = (bf16[64,4224]{1,0:T(8,128)(2,1)S(1)}, bf16[64,4224]{1,0:T(8,128)(2,1)S(1)}, u32[]{:S(2)}, u32[]{:S(2)}) collective-permute-start(bf16[64,4224]{1,0:T(8,128)(2,1)S(1)} %collective-permute-done.1.rest_0_), channel_id=1, source_target_pairs={{0,4},{4,8},{8,12},{12,14},{14,10},{10,6},{6,2},{2,0},{5,1},{9,5},... | collective-permute-start | bytes 1622024 | tf_op jit(solution)/shard_map/ppermute | solution.py:536
  36.0 7.4 %collective-permute-start.12 = (bf16[64,4096]{1,0:T(8,128)(2,1)S(1)}, bf16[64,4096]{1,0:T(8,128)(2,1)S(1)}, u32[]{:S(2)}, u32[]{:S(2)}) collective-permute-start(bf16[64,4096]{1,0:T(8,128)(2,1)S(1)} %collective-permute-done.11.rest_0_), channel_id=1, source_target_pairs={{0,1},{1,0},{2,3},{3,2},{4,5},{5,4},{6,7},{7,6},{8,9},{9,8},{10,11... | collective-permute-start | bytes 1572872 | tf_op jit(solution)/shard_map/ppermute | solution.py:540
  36.3 9.0 %collective-permute-start.14 = (bf16[64,2048]{1,0:T(8,128)(2,1)S(1)}, bf16[64,2048]{1,0:T(8,128)(2,1)S(1)}, u32[]{:S(2)}, u32[]{:S(2)}) collective-permute-start(bf16[64,2048]{1,0:T(8,128)(2,1)S(1)} %constant_dynamic-slice_fusion.1), channel_id=1, source_target_pairs={{0,4},{4,8},{8,12},{12,14},{14,10},{10,6},{6,2},{2,0},{5,1},{9,5},... | collective-permute-start | bytes 786440 | tf_op jit(solution)/shard_map/ppermute | solution.py:536
  40.9 4.7 %collective-permute-start.10 = (bf16[64,4224]{1,0:T(8,128)(2,1)S(1)}, bf16[64,4224]{1,0:T(8,128)(2,1)S(1)}, u32[]{:S(2)}, u32[]{:S(2)}) collective-permute-start(bf16[64,4224]{1,0:T(8,128)(2,1)S(1)} %collective-permute-done.4.rest_0_), channel_id=1, source_target_pairs={{0,1},{1,0},{2,3},{3,2},{4,5},{5,4},{6,7},{7,6},{8,9},{9,8},{10,11... | collective-permute-start | bytes 1622024 | tf_op jit(solution)/shard_map/ppermute | solution.py:540
  41.0 7.0 %collective-permute-start.9 = (bf16[64,2176]{1,0:T(8,128)(2,1)S(1)}, bf16[64,2176]{1,0:T(8,128)(2,1)S(1)}, u32[]{:S(2)}, u32[]{:S(2)}) collective-permute-start(bf16[64,2176]{1,0:T(8,128)(2,1)S(1)} %constant_dynamic-slice_fusion.2), channel_id=1, source_target_pairs={{0,4},{4,8},{8,12},{12,14},{14,10},{10,6},{6,2},{2,0},{5,1},{9,5},... | collective-permute-start | bytes 835592 | tf_op jit(solution)/shard_map/ppermute | solution.py:536
  45.3 3.1 %collective-permute-start.15 = (bf16[64,2048]{1,0:T(8,128)(2,1)S(1)}, bf16[64,2048]{1,0:T(8,128)(2,1)S(1)}, u32[]{:S(2)}, u32[]{:S(2)}) collective-permute-start(bf16[64,2048]{1,0:T(8,128)(2,1)S(1)} %collective-permute-done.14.rest_0_), channel_id=1, source_target_pairs={{0,1},{1,0},{2,3},{3,2},{4,5},{5,4},{6,7},{7,6},{8,9},{9,8},{10,11... | collective-permute-start | bytes 786440 | tf_op jit(solution)/shard_map/ppermute | solution.py:540
  48.0 2.6 %collective-permute-start.13 = (bf16[64,2176]{1,0:T(8,128)(2,1)S(1)}, bf16[64,2176]{1,0:T(8,128)(2,1)S(1)}, u32[]{:S(2)}, u32[]{:S(2)}) collective-permute-start(bf16[64,2176]{1,0:T(8,128)(2,1)S(1)} %collective-permute-done.9.rest_0_), channel_id=1, source_target_pairs={{0,1},{1,0},{2,3},{3,2},{4,5},{5,4},{6,7},{7,6},{8,9},{9,8},{10,11... | collective-permute-start | bytes 835592 | tf_op jit(solution)/shard_map/ppermute | solution.py:540
  54.2 1.3 %collective-permute-start.16 = (f32[4,4,1152]{2,1,0:T(4,128)S(1)}, f32[4,4,1152]{2,1,0:T(4,128)S(1)}, u32[]{:S(2)}, u32[]{:S(2)}) collective-permute-start(f32[4,4,1152]{2,1,0:T(4,128)S(1)} %get-tuple-element.86), channel_id=1, source_target_pairs={{0,1},{1,0},{2,3},{3,2},{4,5},{5,4},{6,7},{7,6},{8,9},{9,8},{10,11... | collective-permute-start | bytes 221192 | tf_op jit(solution)/shard_map/ppermute | solution.py:554
  55.5 4.4 %collective-permute-start.17 = (f32[4,4,1152]{2,1,0:T(4,128)S(1)}, f32[4,4,1152]{2,1,0:T(4,128)S(1)}, u32[]{:S(2)}, u32[]{:S(2)}) collective-permute-start(f32[4,4,1152]{2,1,0:T(4,128)S(1)} %add.15), channel_id=1, source_target_pairs={{0,2},{2,0},{4,6},{6,4},{8,10},{10,8},{12,14},{14,12},{1,3},{3,1},... | collective-permute-start | bytes 221192 | tf_op jit(solution)/shard_map/ppermute | solution.py:555
  58.9 1.3 %collective-permute-start.18 = (f32[4,4,1152]{2,1,0:T(4,128)S(1)}, f32[4,4,1152]{2,1,0:T(4,128)S(1)}, u32[]{:S(2)}, u32[]{:S(2)}) collective-permute-start(f32[4,4,1152]{2,1,0:T(4,128)S(1)} %get-tuple-element.91), channel_id=1, source_target_pairs={{0,1},{1,0},{2,3},{3,2},{4,5},{5,4},{6,7},{7,6},{8,9},{9,8},{10,11... | collective-permute-start | bytes 221192 | tf_op jit(solution)/shard_map/ppermute | solution.py:559
  60.2 4.0 %collective-permute-start.19 = (f32[2,4,1152]{2,1,0:T(4,128)S(1)}, f32[2,4,1152]{2,1,0:T(4,128)S(1)}, u32[]{:S(2)}, u32[]{:S(2)}) collective-permute-start(f32[2,4,1152]{2,1,0:T(4,128)S(1)} %dynamic-slice_bitcast_fusion), channel_id=1, source_target_pairs={{0,4},{2,6},{4,0},{6,2},{8,12},{10,14},{12,8},{14,10},{1,5},{3,7},... | collective-permute-start | bytes 110600 | tf_op jit(solution)/shard_map/ppermute | solution.py:475
  64.3 4.7 %collective-permute-start.20 = (f32[1,4,1152]{2,1,0:T(4,128)S(1)}, f32[1,4,1152]{2,1,0:T(4,128)S(1)}, u32[]{:S(2)}, u32[]{:S(2)}) collective-permute-start(f32[1,4,1152]{2,1,0:T(4,128)S(1)} %constant_dynamic-slice_fusion), channel_id=1, source_target_pairs={{0,8},{2,10},{4,12},{6,14},{8,0},{10,2},{12,4},{14,6},{1,9},{3,11}... | collective-permute-start | bytes 55304 | tf_op jit(solution)/shard_map/ppermute | solution.py:475

commit v16 on v15

--- a/solution.py
+++ b/solution.py
@@ -309,18 +309,23 @@
     per_owner = mine_ref.shape[1]
     chunk = nears[0].shape[2]
     width = mine_ref.shape[2] - LANES
-    piece = 0
-    for near in nears:
-        for pair in range(near.shape[0] * chunk // (2 * width)):
-            start = (2 * pair + bit) * width
-            at, low = lax.div(start, chunk), lax.rem(start, chunk)
-            columns = pl.ds(pl.multiple_of(low, width), width) if width < chunk else slice(None)
-            sums = jnp.dot(rounded, near[at, :, columns], preferred_element_type=jnp.float32)
-            mine_ref[piece, :, :width] = sums[:per_owner]
-            theirs_ref[piece, :, :width] = sums[per_owner:]
-            mine_ref[piece, :, width:] = totals[:per_owner]
-            theirs_ref[piece, :, width:] = totals[per_owner:]
-            piece += 1
+
+    def sums_of(which):
+        piece = 0
+        for near in nears:
+            for pair in range(near.shape[0] * chunk // (2 * width)):
+                at, low = divmod((2 * pair + which) * width, chunk)
+                sums = jnp.dot(
+                    rounded, near[at, :, low : low + width], preferred_element_type=jnp.float32
+                )
+                mine_ref[piece, :, :width] = sums[:per_owner]
+                theirs_ref[piece, :, :width] = sums[per_owner:]
+                mine_ref[piece, :, width:] = totals[:per_owner]
+                theirs_ref[piece, :, width:] = totals[per_owner:]
+                piece += 1
+
+    for which in range(2):
+        pl.when(bit == which)(functools.partial(sums_of, which))
 
 
 def rest_kernel(where_ref, rounded_ref, totals_ref, *rest):

time: 70 us -> 70.7 us (1.010)
  Pallas kernels: 34.8 us -> 35.6 us
    pallas_call x8, Pallas kernels: 19 us -> 19.8 us  [ring_scores(): pl.pallas_call(functools.partial(ring_kernel, phase, ends, sources), in_s...]
  transfers between devices with their start and end apart: 21 -> 21, of which waited for: 9 -> 9; matrix products, arithmetic and copies ran while one was open for 1% -> 1% of each run, Pallas kernels for 43% -> 42%
where the time goes in v16:
time: 70.7 us; the launch traced here: 70.6 us
  Pallas kernels  35.6 us (50%)
  starting transfers between devices  23.5 us (33%)
  waiting for transfers between devices  9.47 us (13%)
  other arithmetic  0.85 us (1%)
  between operations  0.79 us (1%)
    pallas_call x8, Pallas kernels, ring_scores(): pl.pallas_call(functools.partial(ring_kernel, phase, ends, sources), in_s...  19.8 us
    ppermute x8, starting transfers between devices, body(): own = lax.ppermute(message, ('blk', 'cls'), ring)  15.9 us
    pallas_call x3, Pallas kernels, own_scores(): pl.pallas_call(functools.partial(own_kernel, quarters), in_specs=[in_smem...  12.6 us
    ppermute x2, waiting for transfers between devices, scatter_sum(): pieces = keep + lax.ppermute(send, 'blk', swaps)  4.39 us
    ppermute x2, starting transfers between devices, scatter_sum(): pieces = keep + lax.ppermute(send, 'blk', swaps)  4.36 us
    ppermute x8, waiting for transfers between devices, body(): own = lax.ppermute(message, ('blk', 'cls'), ring)  2.8 us
    pallas_call x1, Pallas kernels, rest_sums(): pl.pallas_call(rest_kernel, in_specs=[in_smem()] + [in_vmem()] * (2 + len...  1.74 us
    ppermute x1, starting transfers between devices, body(): lax.ppermute(mine + given, 'blk', [(i, i ^ 1) for i in range(blocks)])  1.63 us
  transfers between devices with their start and end apart: 21, of which 9 were waited for; matrix products, arithmetic and copies ran while one was open for 1% of the time, Pallas kernels for 42%

profile of v16, /device:TPU:0, one launch (start us, length us, event | category | flops | bytes accessed | tf_op | source)
XLA Modules:
  0.0 70.6 jit_solution(14342591282844673574)
XLA Ops:
  2.1 3.1 %collective-permute-start.2 = (bf16[64,4096]{1,0:T(8,128)(2,1)S(1)}, bf16[64,4096]{1,0:T(8,128)(2,1)S(1)}, u32[]{:S(2)}, u32[]{:S(2)}) collective-permute-start(bf16[64,4096]{1,0:T(8,128)(2,1)S(1)} %get-tuple-element.52.tmpl_ref), channel_id=1, source_target_pairs={{0,4},{4,8},{8,12},{12,14},{14,10},{10,6},{6,2},{2,0},{5,1},{9,5},... | collective-permute-start | bytes 1572872 | tf_op jit(solution)/shard_map/ppermute | solution.py:541
  6.8 6.5 %shard_map.78 = (s32[16,1024]{1,0:T(8,128)S(1)}, f32[64,1024]{1,0:T(8,128)S(1)}, f32[64,128]{1,0:T(8,128)S(1)}, bf16[2048,1024]{1,0:T(8,128)(2,1)S(1)}, bf16[204...) custom-call(s32[2]{0:T(128)S(1)} %pad_add_fusion.where_ref, ...), custom_call_target="tpu_custom_call" | custom-call | flops 2147483648 | bytes 8388608 | tf_op jit(solution)/shard_map/pallas_call | solution.py:274
  13.3 1.6 %collective-permute-start.6 = (bf16[64,4096]{1,0:T(8,128)(2,1)S(1)}, bf16[64,4096]{1,0:T(8,128)(2,1)S(1)}, u32[]{:S(2)}, u32[]{:S(2)}) collective-permute-start(bf16[64,4096]{1,0:T(8,128)(2,1)S(1)} %collective-permute-done.2.rest_0_), channel_id=1, source_target_pairs={{0,4},{4,8},{8,12},{12,14},{14,10},{10,6},{6,2},{2,0},{5,1},{9,5},... | collective-permute-start | bytes 1572872 | tf_op jit(solution)/shard_map/ppermute | solution.py:541
  15.0 2.9 %shard_map.79 = (f32[64,1024]{1,0:T(8,128)S(1)}, f32[64,128]{1,0:T(8,128)S(1)}, bf16[2048,1024]{1,0:T(8,128)(2,1)S(1)}, bf16[2,1024,1024]{2,1,0:T(8,128)(2,1)S(1)}) custom-call(s32[2]{0:T(128)S(1)} %pad_add_fusion.where_ref, f32[1,8192]{1,0:T(1,128)S(1)} %get-tuple-element.50.noise_ref, bf16[64,4224]{1,0:T(8,128)(2,1)S(1)} %get-tuple-element.51.tmpl_ref, ...), custom_call_target="tpu_custom_call" | custom-call | flops 2147483648 | bytes 8388608 | tf_op jit(solution)/shard_map/pallas_call | solution.py:274
  18.5 1.7 %collective-permute-start.1 = (bf16[64,4224]{1,0:T(8,128)(2,1)S(1)}, bf16[64,4224]{1,0:T(8,128)(2,1)S(1)}, u32[]{:S(2)}, u32[]{:S(2)}) collective-permute-start(bf16[64,4224]{1,0:T(8,128)(2,1)S(1)} %collective-permute-done.rest_0_), channel_id=1, source_target_pairs={{0,4},{4,8},{8,12},{12,14},{14,10},{10,6},{6,2},{2,0},{5,1},{9,5},... | collective-permute-start | bytes 1622024 | tf_op jit(solution)/shard_map/ppermute | solution.py:541
  20.1 3.1 %shard_map.80 = (f32[16,1024]{1,0:T(8,128)S(1)}, bf16[2048,1024]{1,0:T(8,128)(2,1)S(1)}) custom-call(s32[2]{0:T(128)S(1)} %pad_add_fusion.where_ref, f32[1,8192]{1,0:T(1,128)S(1)} %get-tuple-element.50.noise_ref, bf16[64,4224]{1,0:T(8,128)(2,1)S(1)} %get-tuple-element.51.tmpl_ref, bf16[1024,8192]{1,0:T(8,128)(2,1)} %far_ref.5, ...), custom_call_target="tpu_custom_call" | custom-call | flops 2147483648 | bytes 8388608 | tf_op jit(solution)/shard_map/pallas_call | solution.py:274
  23.7 2.1 %collective-permute-start.11 = (bf16[64,4096]{1,0:T(8,128)(2,1)S(1)}, bf16[64,4096]{1,0:T(8,128)(2,1)S(1)}, u32[]{:S(2)}, u32[]{:S(2)}) collective-permute-start(bf16[64,4096]{1,0:T(8,128)(2,1)S(1)} %collective-permute-done.6.rest_0_), channel_id=1, source_target_pairs={{0,4},{4,8},{8,12},{12,14},{14,10},{10,6},{6,2},{2,0},{5,1},{9,5},... | collective-permute-start | bytes 1572872 | tf_op jit(solution)/shard_map/ppermute | solution.py:541
  25.7 2.0 %shard_map.81 = (f32[128,1024]{1,0:T(8,128)S(1)}, f32[128,128]{1,0:T(8,128)S(1)}) custom-call(s32[2]{0:T(128)S(1)} %pad_add_fusion.where_ref, f32[1,8192]{1,0:T(1,128)S(1)} %get-tuple-element.50.noise_ref, bf16[2048,1024]{1,0:T(8,128)(2,1)S(1)} %get-tuple-element.64.low_ref, bf16[2048,1024]{1,0:T(8,128)(2,1)S(1)} %get-tuple-element.65.high_ref, ...), custom_call_target="tpu_custom_call" | custom-call | flops 2147483648 | bytes 8388608 | tf_op jit(solution)/shard_map/pallas_call | solution.py:448
  27.8 1.7 %collective-permute-done.1.rest_0_ = bf16[64,4224]{1,0:T(8,128)(2,1)S(1)} collective-permute-done((bf16[64,4224]{1,0:T(8,128)(2,1)S(1)}, bf16[64,4224]{1,0:T(8,128)(2,1)S(1)}, u32[]{:S(2)}, u32[]{:S(2)}) %collective-permute-start.1) | collective-permute-done | bytes 540704 | tf_op jit(solution)/shard_map/ppermute | solution.py:541
  29.5 2.1 %collective-permute-start.4 = (bf16[64,4224]{1,0:T(8,128)(2,1)S(1)}, bf16[64,4224]{1,0:T(8,128)(2,1)S(1)}, u32[]{:S(2)}, u32[]{:S(2)}) collective-permute-start(bf16[64,4224]{1,0:T(8,128)(2,1)S(1)} %collective-permute-done.1.rest_0_), channel_id=1, source_target_pairs={{0,4},{4,8},{8,12},{12,14},{14,10},{10,6},{6,2},{2,0},{5,1},{9,5},... | collective-permute-start | bytes 1622024 | tf_op jit(solution)/shard_map/ppermute | solution.py:541
  31.5 2.4 %shard_map.83.rest_6_ = f32[16,1024]{1,0:T(8,128)S(1)} custom-call(s32[2]{0:T(128)S(1)} %pad_add_fusion.where_ref, f32[1,8192]{1,0:T(1,128)S(1)} %get-tuple-element.50.noise_ref, bf16[2048,1024]{1,0:T(8,128)(2,1)S(1)} %get-tuple-element.57.low_ref, bf16[2048,1024]{1,0:T(8,128)(2,1)S(1)} %get-tuple-element.62.high_ref, ...), custom_call_target="tpu_custom_call" | custom-call | flops 2147483648 | bytes 8388608 | tf_op jit(solution)/shard_map/pallas_call | solution.py:448
  34.0 2.0 %shard_map.82 = (f32[128,1024]{1,0:T(8,128)S(1)}, f32[128,128]{1,0:T(8,128)S(1)}) custom-call(s32[2]{0:T(128)S(1)} %pad_add_fusion.where_ref, f32[1,8192]{1,0:T(1,128)S(1)} %get-tuple-element.50.noise_ref, bf16[2048,1024]{1,0:T(8,128)(2,1)S(1)} %get-tuple-element.64.low_ref, bf16[2048,1024]{1,0:T(8,128)(2,1)S(1)} %get-tuple-element.65.high_ref, ...), custom_call_target="tpu_custom_call" | custom-call | flops 2147483648 | bytes 8388608 | tf_op jit(solution)/shard_map/pallas_call | solution.py:448
  37.8 2.4 %shard_map.84.rest_6_ = f32[16,1024]{1,0:T(8,128)S(1)} custom-call(s32[2]{0:T(128)S(1)} %pad_add_fusion.where_ref, f32[1,8192]{1,0:T(1,128)S(1)} %get-tuple-element.50.noise_ref, bf16[2048,1024]{1,0:T(8,128)(2,1)S(1)} %get-tuple-element.57.low_ref, bf16[2048,1024]{1,0:T(8,128)(2,1)S(1)} %get-tuple-element.62.high_ref, ...), custom_call_target="tpu_custom_call" | custom-call | flops 2147483648 | bytes 8388608 | tf_op jit(solution)/shard_map/pallas_call | solution.py:448
  41.0 2.3 %collective-permute-start.9 = (bf16[64,2176]{1,0:T(8,128)(2,1)S(1)}, bf16[64,2176]{1,0:T(8,128)(2,1)S(1)}, u32[]{:S(2)}, u32[]{:S(2)}) collective-permute-start(bf16[64,2176]{1,0:T(8,128)(2,1)S(1)} %constant_dynamic-slice_fusion.2), channel_id=1, source_target_pairs={{0,4},{4,8},{8,12},{12,14},{14,10},{10,6},{6,2},{2,0},{5,1},{9,5},... | collective-permute-start | bytes 835592 | tf_op jit(solution)/shard_map/ppermute | solution.py:541
  43.3 2.0 %shard_map.85 = (f32[128,1024]{1,0:T(8,128)S(1)}, f32[128,128]{1,0:T(8,128)S(1)}) custom-call(s32[2]{0:T(128)S(1)} %pad_add_fusion.where_ref, f32[1,8192]{1,0:T(1,128)S(1)} %get-tuple-element.50.noise_ref, bf16[2048,1024]{1,0:T(8,128)(2,1)S(1)} %get-tuple-element.64.low_ref, bf16[2048,1024]{1,0:T(8,128)(2,1)S(1)} %get-tuple-element.65.high_ref, ...), custom_call_target="tpu_custom_call" | custom-call | flops 2147483648 | bytes 8388608 | tf_op jit(solution)/shard_map/pallas_call | solution.py:448
  45.6 2.4 %shard_map.86.rest_6_ = f32[16,1024]{1,0:T(8,128)S(1)} custom-call(s32[2]{0:T(128)S(1)} %pad_add_fusion.where_ref, f32[1,8192]{1,0:T(1,128)S(1)} %get-tuple-element.50.noise_ref, bf16[2048,1024]{1,0:T(8,128)(2,1)S(1)} %get-tuple-element.57.low_ref, bf16[2048,1024]{1,0:T(8,128)(2,1)S(1)} %get-tuple-element.62.high_ref, ...), custom_call_target="tpu_custom_call" | custom-call | flops 2147483648 | bytes 8388608 | tf_op jit(solution)/shard_map/pallas_call | solution.py:448
  48.4 2.2 %shard_map.87 = (f32[64,1024]{1,0:T(8,128)S(1)}, f32[64,128]{1,0:T(8,128)S(1)}) custom-call(s32[2]{0:T(128)S(1)} %pad_add_fusion.where_ref, f32[1,8192]{1,0:T(1,128)S(1)} %get-tuple-element.50.noise_ref, bf16[2048,1024]{1,0:T(8,128)(2,1)S(1)} %get-tuple-element.64.low_ref, bf16[2048,1024]{1,0:T(8,128)(2,1)S(1)} %get-tuple-element.65.high_ref, ...), custom_call_target="tpu_custom_call" | custom-call | flops 2147483648 | bytes 8388608 | tf_op jit(solution)/shard_map/pallas_call | solution.py:448
  50.6 4.4 %shard_map.88 = (f32[1,1024]{1,0:T(1,128)}, f32[4,4,1152]{2,1,0:T(4,128)S(1)}, f32[4,4,1152]{2,1,0:T(4,128)S(1)}, bf16[8,1024]{1,0:T(8,128)(2,1)S(1)}, f32[8,128]{1,0:T(8,128)S(1)}) custom-call(s32[2]{0:T(128)S(1)} %pad_add_fusion.where_ref, f32[1,8192]{1,0:T(1,128)S(1)} %get-tuple-element.50.noise_ref, bf16[2048,1024]{1,0:T(8,128)(2,1)S(1)} %get-tuple-element.57.low_ref, ...), custom_call_target="tpu_custom_call" | custom-call | flops 2147483648 | bytes 8388608 | tf_op jit(solution)/shard_map/pallas_call | solution.py:448
  56.3 1.6 %collective-permute-start.17 = (f32[4,4,1152]{2,1,0:T(4,128)S(1)}, f32[4,4,1152]{2,1,0:T(4,128)S(1)}, u32[]{:S(2)}, u32[]{:S(2)}) collective-permute-start(f32[4,4,1152]{2,1,0:T(4,128)S(1)} %add.15), channel_id=1, source_target_pairs={{0,2},{2,0},{4,6},{6,4},{8,10},{10,8},{12,14},{14,12},{1,3},{3,1},... | collective-permute-start | bytes 221192 | tf_op jit(solution)/shard_map/ppermute | solution.py:560
  57.9 1.7 %shard_map.89 = (f32[4,4,1152]{2,1,0:T(4,128)S(1)}, f32[4,4,1152]{2,1,0:T(4,128)S(1)}) custom-call(s32[2]{0:T(128)S(1)} %pad_add_fusion.where_ref, bf16[8,1024]{1,0:T(8,128)(2,1)S(1)} %get-tuple-element.87.rounded_ref, f32[8,128]{1,0:T(8,128)S(1)} %get-tuple-element.88.totals_ref, bf16[4,1024,1024]{2,1,0:T(8,128)(2,1)S(1)} %get-tuple-element.83.rest_8_.rest_0_, ...), custom_call_target="tpu_custom_call" | custom-call | flops 1073741824 | bytes 4194304 | tf_op jit(solution)/shard_map/pallas_call | solution.py:341
  61.0 1.7 %collective-permute-start.19 = (f32[2,4,1152]{2,1,0:T(4,128)S(1)}, f32[2,4,1152]{2,1,0:T(4,128)S(1)}, u32[]{:S(2)}, u32[]{:S(2)}) collective-permute-start(f32[2,4,1152]{2,1,0:T(4,128)S(1)} %dynamic-slice_bitcast_fusion), channel_id=1, source_target_pairs={{0,4},{2,6},{4,0},{6,2},{8,12},{10,14},{12,8},{14,10},{1,5},{3,7},... | collective-permute-start | bytes 110600 | tf_op jit(solution)/shard_map/ppermute | solution.py:480
  62.7 2.3 %collective-permute-done.19 = f32[2,4,1152]{2,1,0:T(4,128)S(1)} collective-permute-done((f32[2,4,1152]{2,1,0:T(4,128)S(1)}, f32[2,4,1152]{2,1,0:T(4,128)S(1)}, u32[]{:S(2)}, u32[]{:S(2)}) %collective-permute-start.19) | collective-permute-done | bytes 36896 | tf_op jit(solution)/shard_map/ppermute | solution.py:480
  65.0 2.7 %collective-permute-start.20 = (f32[1,4,1152]{2,1,0:T(4,128)S(1)}, f32[1,4,1152]{2,1,0:T(4,128)S(1)}, u32[]{:S(2)}, u32[]{:S(2)}) collective-permute-start(f32[1,4,1152]{2,1,0:T(4,128)S(1)} %constant_dynamic-slice_fusion), channel_id=1, source_target_pairs={{0,8},{2,10},{4,12},{6,14},{8,0},{10,2},{12,4},{14,6},{1,9},{3,11}... | collective-permute-start | bytes 55304 | tf_op jit(solution)/shard_map/ppermute | solution.py:480
  67.7 2.0 %collective-permute-done.20 = f32[1,4,1152]{2,1,0:T(4,128)S(1)} collective-permute-done((f32[1,4,1152]{2,1,0:T(4,128)S(1)}, f32[1,4,1152]{2,1,0:T(4,128)S(1)}, u32[]{:S(2)}, u32[]{:S(2)}) %collective-permute-start.20) | collective-permute-done | bytes 18464 | tf_op jit(solution)/shard_map/ppermute | solution.py:480
  (48 shorter events, 10.8 us)
Async XLA Ops:
  2.1 11.3 %collective-permute-start.2 = (bf16[64,4096]{1,0:T(8,128)(2,1)S(1)}, bf16[64,4096]{1,0:T(8,128)(2,1)S(1)}, u32[]{:S(2)}, u32[]{:S(2)}) collective-permute-start(bf16[64,4096]{1,0:T(8,128)(2,1)S(1)} %get-tuple-element.52.tmpl_ref), channel_id=1, source_target_pairs={{0,4},{4,8},{8,12},{12,14},{14,10},{10,6},{6,2},{2,0},{5,1},{9,5},... | collective-permute-start | bytes 1572872 | tf_op jit(solution)/shard_map/ppermute | solution.py:541
  5.1 12.9 %collective-permute-start = (bf16[64,4224]{1,0:T(8,128)(2,1)S(1)}, bf16[64,4224]{1,0:T(8,128)(2,1)S(1)}, u32[]{:S(2)}, u32[]{:S(2)}) collective-permute-start(bf16[64,4224]{1,0:T(8,128)(2,1)S(1)} %get-tuple-element.51.tmpl_ref), channel_id=1, source_target_pairs={{0,4},{4,8},{8,12},{12,14},{14,10},{10,6},{6,2},{2,0},{5,1},{9,5},... | collective-permute-start | bytes 1622024 | tf_op jit(solution)/shard_map/ppermute | solution.py:541
  13.3 10.3 %collective-permute-start.6 = (bf16[64,4096]{1,0:T(8,128)(2,1)S(1)}, bf16[64,4096]{1,0:T(8,128)(2,1)S(1)}, u32[]{:S(2)}, u32[]{:S(2)}) collective-permute-start(bf16[64,4096]{1,0:T(8,128)(2,1)S(1)} %collective-permute-done.2.rest_0_), channel_id=1, source_target_pairs={{0,4},{4,8},{8,12},{12,14},{14,10},{10,6},{6,2},{2,0},{5,1},{9,5},... | collective-permute-start | bytes 1572872 | tf_op jit(solution)/shard_map/ppermute | solution.py:541
  15.0 5.2 %copy-start.1 = (s32[8]{0:T(128)S(1)}, s32[8]{0:T(128)}, u32[]{:S(2)}) copy-start(s32[8]{0:T(128)} %rest_7_.1) | copy-start | bytes 100
  15.0 5.2 %copy-start = (s32[64]{0:T(128)S(1)}, s32[64]{0:T(128)}, u32[]{:S(2)}) copy-start(s32[64]{0:T(128)} %param.9) | copy-start | bytes 772
  17.9 7.9 %collective-permute-start.3 = (bf16[64,4096]{1,0:T(8,128)(2,1)S(1)}, bf16[64,4096]{1,0:T(8,128)(2,1)S(1)}, u32[]{:S(2)}, u32[]{:S(2)}) collective-permute-start(bf16[64,4096]{1,0:T(8,128)(2,1)S(1)} %collective-permute-done.2.rest_0_), channel_id=1, source_target_pairs={{0,1},{1,0},{2,3},{3,2},{4,5},{5,4},{6,7},{7,6},{8,9},{9,8},{10,11... | collective-permute-start | bytes 1572872 | tf_op jit(solution)/shard_map/ppermute | solution.py:545
  18.0 13.5 %collective-permute-start.8 = (bf16[64,4224]{1,0:T(8,128)(2,1)S(1)}, bf16[64,4224]{1,0:T(8,128)(2,1)S(1)}, u32[]{:S(2)}, u32[]{:S(2)}) collective-permute-start(bf16[64,4224]{1,0:T(8,128)(2,1)S(1)} %collective-permute-done.rest_0_), channel_id=1, source_target_pairs={{0,1},{1,0},{2,3},{3,2},{4,5},{5,4},{6,7},{7,6},{8,9},{9,8},{10,11... | collective-permute-start | bytes 1622024 | tf_op jit(solution)/shard_map/ppermute | solution.py:545
  18.5 11.0 %collective-permute-start.1 = (bf16[64,4224]{1,0:T(8,128)(2,1)S(1)}, bf16[64,4224]{1,0:T(8,128)(2,1)S(1)}, u32[]{:S(2)}, u32[]{:S(2)}) collective-permute-start(bf16[64,4224]{1,0:T(8,128)(2,1)S(1)} %collective-permute-done.rest_0_), channel_id=1, source_target_pairs={{0,4},{4,8},{8,12},{12,14},{14,10},{10,6},{6,2},{2,0},{5,1},{9,5},... | collective-permute-start | bytes 1622024 | tf_op jit(solution)/shard_map/ppermute | solution.py:541
  23.7 10.3 %collective-permute-start.7 = (bf16[64,4096]{1,0:T(8,128)(2,1)S(1)}, bf16[64,4096]{1,0:T(8,128)(2,1)S(1)}, u32[]{:S(2)}, u32[]{:S(2)}) collective-permute-start(bf16[64,4096]{1,0:T(8,128)(2,1)S(1)} %collective-permute-done.6.rest_0_), channel_id=1, source_target_pairs={{0,1},{1,0},{2,3},{3,2},{4,5},{5,4},{6,7},{7,6},{8,9},{9,8},{10,11... | collective-permute-start | bytes 1572872 | tf_op jit(solution)/shard_map/ppermute | solution.py:545
  23.7 12.3 %collective-permute-start.11 = (bf16[64,4096]{1,0:T(8,128)(2,1)S(1)}, bf16[64,4096]{1,0:T(8,128)(2,1)S(1)}, u32[]{:S(2)}, u32[]{:S(2)}) collective-permute-start(bf16[64,4096]{1,0:T(8,128)(2,1)S(1)} %collective-permute-done.6.rest_0_), channel_id=1, source_target_pairs={{0,4},{4,8},{8,12},{12,14},{14,10},{10,6},{6,2},{2,0},{5,1},{9,5},... | collective-permute-start | bytes 1572872 | tf_op jit(solution)/shard_map/ppermute | solution.py:541
  29.5 8.4 %collective-permute-start.5 = (bf16[64,4224]{1,0:T(8,128)(2,1)S(1)}, bf16[64,4224]{1,0:T(8,128)(2,1)S(1)}, u32[]{:S(2)}, u32[]{:S(2)}) collective-permute-start(bf16[64,4224]{1,0:T(8,128)(2,1)S(1)} %collective-permute-done.1.rest_0_), channel_id=1, source_target_pairs={{0,1},{1,0},{2,3},{3,2},{4,5},{5,4},{6,7},{7,6},{8,9},{9,8},{10,11... | collective-permute-start | bytes 1622024 | tf_op jit(solution)/shard_map/ppermute | solution.py:545
  29.5 11.4 %collective-permute-start.4 = (bf16[64,4224]{1,0:T(8,128)(2,1)S(1)}, bf16[64,4224]{1,0:T(8,128)(2,1)S(1)}, u32[]{:S(2)}, u32[]{:S(2)}) collective-permute-start(bf16[64,4224]{1,0:T(8,128)(2,1)S(1)} %collective-permute-done.1.rest_0_), channel_id=1, source_target_pairs={{0,4},{4,8},{8,12},{12,14},{14,10},{10,6},{6,2},{2,0},{5,1},{9,5},... | collective-permute-start | bytes 1622024 | tf_op jit(solution)/shard_map/ppermute | solution.py:541
  36.0 7.4 %collective-permute-start.12 = (bf16[64,4096]{1,0:T(8,128)(2,1)S(1)}, bf16[64,4096]{1,0:T(8,128)(2,1)S(1)}, u32[]{:S(2)}, u32[]{:S(2)}) collective-permute-start(bf16[64,4096]{1,0:T(8,128)(2,1)S(1)} %collective-permute-done.11.rest_0_), channel_id=1, source_target_pairs={{0,1},{1,0},{2,3},{3,2},{4,5},{5,4},{6,7},{7,6},{8,9},{9,8},{10,11... | collective-permute-start | bytes 1572872 | tf_op jit(solution)/shard_map/ppermute | solution.py:545
  36.3 9.0 %collective-permute-start.14 = (bf16[64,2048]{1,0:T(8,128)(2,1)S(1)}, bf16[64,2048]{1,0:T(8,128)(2,1)S(1)}, u32[]{:S(2)}, u32[]{:S(2)}) collective-permute-start(bf16[64,2048]{1,0:T(8,128)(2,1)S(1)} %constant_dynamic-slice_fusion.1), channel_id=1, source_target_pairs={{0,4},{4,8},{8,12},{12,14},{14,10},{10,6},{6,2},{2,0},{5,1},{9,5},... | collective-permute-start | bytes 786440 | tf_op jit(solution)/shard_map/ppermute | solution.py:541
  40.9 4.7 %collective-permute-start.10 = (bf16[64,4224]{1,0:T(8,128)(2,1)S(1)}, bf16[64,4224]{1,0:T(8,128)(2,1)S(1)}, u32[]{:S(2)}, u32[]{:S(2)}) collective-permute-start(bf16[64,4224]{1,0:T(8,128)(2,1)S(1)} %collective-permute-done.4.rest_0_), channel_id=1, source_target_pairs={{0,1},{1,0},{2,3},{3,2},{4,5},{5,4},{6,7},{7,6},{8,9},{9,8},{10,11... | collective-permute-start | bytes 1622024 | tf_op jit(solution)/shard_map/ppermute | solution.py:545
  41.0 7.0 %collective-permute-start.9 = (bf16[64,2176]{1,0:T(8,128)(2,1)S(1)}, bf16[64,2176]{1,0:T(8,128)(2,1)S(1)}, u32[]{:S(2)}, u32[]{:S(2)}) collective-permute-start(bf16[64,2176]{1,0:T(8,128)(2,1)S(1)} %constant_dynamic-slice_fusion.2), channel_id=1, source_target_pairs={{0,4},{4,8},{8,12},{12,14},{14,10},{10,6},{6,2},{2,0},{5,1},{9,5},... | collective-permute-start | bytes 835592 | tf_op jit(solution)/shard_map/ppermute | solution.py:541
  45.3 3.1 %collective-permute-start.15 = (bf16[64,2048]{1,0:T(8,128)(2,1)S(1)}, bf16[64,2048]{1,0:T(8,128)(2,1)S(1)}, u32[]{:S(2)}, u32[]{:S(2)}) collective-permute-start(bf16[64,2048]{1,0:T(8,128)(2,1)S(1)} %collective-permute-done.14.rest_0_), channel_id=1, source_target_pairs={{0,1},{1,0},{2,3},{3,2},{4,5},{5,4},{6,7},{7,6},{8,9},{9,8},{10,11... | collective-permute-start | bytes 786440 | tf_op jit(solution)/shard_map/ppermute | solution.py:545
  48.0 2.6 %collective-permute-start.13 = (bf16[64,2176]{1,0:T(8,128)(2,1)S(1)}, bf16[64,2176]{1,0:T(8,128)(2,1)S(1)}, u32[]{:S(2)}, u32[]{:S(2)}) collective-permute-start(bf16[64,2176]{1,0:T(8,128)(2,1)S(1)} %collective-permute-done.9.rest_0_), channel_id=1, source_target_pairs={{0,1},{1,0},{2,3},{3,2},{4,5},{5,4},{6,7},{7,6},{8,9},{9,8},{10,11... | collective-permute-start | bytes 835592 | tf_op jit(solution)/shard_map/ppermute | solution.py:545
  55.0 1.3 %collective-permute-start.16 = (f32[4,4,1152]{2,1,0:T(4,128)S(1)}, f32[4,4,1152]{2,1,0:T(4,128)S(1)}, u32[]{:S(2)}, u32[]{:S(2)}) collective-permute-start(f32[4,4,1152]{2,1,0:T(4,128)S(1)} %get-tuple-element.86), channel_id=1, source_target_pairs={{0,1},{1,0},{2,3},{3,2},{4,5},{5,4},{6,7},{7,6},{8,9},{9,8},{10,11... | collective-permute-start | bytes 221192 | tf_op jit(solution)/shard_map/ppermute | solution.py:559
  56.3 4.4 %collective-permute-start.17 = (f32[4,4,1152]{2,1,0:T(4,128)S(1)}, f32[4,4,1152]{2,1,0:T(4,128)S(1)}, u32[]{:S(2)}, u32[]{:S(2)}) collective-permute-start(f32[4,4,1152]{2,1,0:T(4,128)S(1)} %add.15), channel_id=1, source_target_pairs={{0,2},{2,0},{4,6},{6,4},{8,10},{10,8},{12,14},{14,12},{1,3},{3,1},... | collective-permute-start | bytes 221192 | tf_op jit(solution)/shard_map/ppermute | solution.py:560
  59.7 1.3 %collective-permute-start.18 = (f32[4,4,1152]{2,1,0:T(4,128)S(1)}, f32[4,4,1152]{2,1,0:T(4,128)S(1)}, u32[]{:S(2)}, u32[]{:S(2)}) collective-permute-start(f32[4,4,1152]{2,1,0:T(4,128)S(1)} %get-tuple-element.91), channel_id=1, source_target_pairs={{0,1},{1,0},{2,3},{3,2},{4,5},{5,4},{6,7},{7,6},{8,9},{9,8},{10,11... | collective-permute-start | bytes 221192 | tf_op jit(solution)/shard_map/ppermute | solution.py:564
  61.0 4.0 %collective-permute-start.19 = (f32[2,4,1152]{2,1,0:T(4,128)S(1)}, f32[2,4,1152]{2,1,0:T(4,128)S(1)}, u32[]{:S(2)}, u32[]{:S(2)}) collective-permute-start(f32[2,4,1152]{2,1,0:T(4,128)S(1)} %dynamic-slice_bitcast_fusion), channel_id=1, source_target_pairs={{0,4},{2,6},{4,0},{6,2},{8,12},{10,14},{12,8},{14,10},{1,5},{3,7},... | collective-permute-start | bytes 110600 | tf_op jit(solution)/shard_map/ppermute | solution.py:480
  65.0 4.7 %collective-permute-start.20 = (f32[1,4,1152]{2,1,0:T(4,128)S(1)}, f32[1,4,1152]{2,1,0:T(4,128)S(1)}, u32[]{:S(2)}, u32[]{:S(2)}) collective-permute-start(f32[1,4,1152]{2,1,0:T(4,128)S(1)} %constant_dynamic-slice_fusion), channel_id=1, source_target_pairs={{0,8},{2,10},{4,12},{6,14},{8,0},{10,2},{12,4},{14,6},{1,9},{3,11}... | collective-permute-start | bytes 55304 | tf_op jit(solution)/shard_map/ppermute | solution.py:480

commit v17 on v15

--- a/solution.py
+++ b/solution.py
@@ -165,7 +165,7 @@
     return state_ref[0:1, :], state_ref[1:2, :], state_ref[2:3, :], state_ref[STATE_ROWS:, :]
 
 
-def own_kernel(quarters, where_ref, noise_ref, tmpl_ref, far_ref, *rest):
+def own_kernel(quarters, blocks, where_ref, noise_ref, tmpl_ref, far_ref, *rest):
     first, last = quarters[0] == 0, quarters[-1] == 3
     if first:
         sig_ref, words_ref, acc, energy, *turned_refs, near, next_ref, arrived, late = rest
@@ -180,9 +180,15 @@
     width = chunk // PIECES
     low = quarters[0] * span
 
+    share = 4 * span // (blocks * width)
+    bit = lax.rem(where_ref[0], 2)
+
     def part(ref, step):
-        columns = pl.ds(pl.multiple_of(lax.rem(step, PIECES) * width, width), width)
-        return ref.at[lax.div(step, PIECES), :, columns]
+        block, rest = lax.div(step, share), lax.rem(step, share)
+        place = block - lax.rem(block, 2) + jnp.where(lax.rem(block, 2) == bit, 1, 0)
+        piece = place * share + rest
+        columns = pl.ds(pl.multiple_of(lax.rem(piece, PIECES) * width, width), width)
+        return ref.at[lax.div(piece, PIECES), :, columns]
 
     def copies(step):
         columns = pl.ds(pl.multiple_of(low + step * width, width), width)
@@ -239,7 +245,7 @@
     put_state(add_rows(tags, hit, logs_ref, state, acc, energy), out_ref)
 
 
-def own_scores(quarters, where, noise, particles, templates, rest, total=0):
+def own_scores(quarters, blocks, where, noise, particles, templates, rest, total=0):
     per_device, freqs = particles.shape
     height = templates.shape[0]
     span = freqs // 4
@@ -272,7 +278,7 @@
     if not first:
         rest = (*rest[:-1], pltpu.with_memory_space_constraint(rest[-1], pltpu.VMEM))
     return pl.pallas_call(
-        functools.partial(own_kernel, quarters),
+        functools.partial(own_kernel, quarters, blocks),
         in_specs=[in_smem(), in_vmem(), in_vmem(), pl.BlockSpec(memory_space=pl.ANY)] + rest_specs,
         out_specs=[in_vmem()] * len(shapes),
         out_shape=shapes,
@@ -305,17 +311,17 @@
     return own_first(weights).astype(jnp.bfloat16), own_first(totals)
 
 
-def class_sums(rounded, totals, bit, nears, mine_ref, theirs_ref):
+def class_sums(rounded, totals, which, nears, mine_ref, theirs_ref):
     per_owner = mine_ref.shape[1]
     chunk = nears[0].shape[2]
     width = mine_ref.shape[2] - LANES
     piece = 0
     for near in nears:
         for pair in range(near.shape[0] * chunk // (2 * width)):
-            start = (2 * pair + bit) * width
-            at, low = lax.div(start, chunk), lax.rem(start, chunk)
-            columns = pl.ds(pl.multiple_of(low, width), width) if width < chunk else slice(None)
-            sums = jnp.dot(rounded, near[at, :, columns], preferred_element_type=jnp.float32)
+            at, low = divmod((2 * pair + which) * width, chunk)
+            sums = jnp.dot(
+                rounded, near[at, :, low : low + width], preferred_element_type=jnp.float32
+            )
             mine_ref[piece, :, :width] = sums[:per_owner]
             theirs_ref[piece, :, :width] = sums[per_owner:]
             mine_ref[piece, :, width:] = totals[:per_owner]
@@ -323,19 +329,18 @@
             piece += 1
 
 
-def rest_kernel(where_ref, rounded_ref, totals_ref, *rest):
+def rest_kernel(rounded_ref, totals_ref, *rest):
     *nears, mine_ref, theirs_ref = rest
-    bit = lax.rem(where_ref[0], 2)
-    class_sums(rounded_ref[...], totals_ref[...], bit, nears, mine_ref, theirs_ref)
-
-
-def rest_sums(where, rounded, totals, nears, piece):
+    class_sums(rounded_ref[...], totals_ref[...], 1, nears, mine_ref, theirs_ref)
+
+
+def rest_sums(rounded, totals, nears, piece):
     classes, per_device = rounded.shape
     blocks = 2 * piece.shape[0]
     freqs = blocks * (piece.shape[2] - LANES)
     return pl.pallas_call(
         rest_kernel,
-        in_specs=[in_smem()] + [in_vmem()] * (2 + len(nears)),
+        in_specs=[in_vmem()] * (2 + len(nears)),
         out_specs=[in_vmem()] * 2,
         out_shape=[piece, piece],
         compiler_params=pltpu.CompilerParams(vmem_limit_bytes=VMEM_LIMIT),
@@ -344,7 +349,7 @@
             bytes_accessed=per_device * freqs // 2,
             transcendentals=0,
         ),
-    )(where, rounded, totals, *(pltpu.with_memory_space_constraint(x, pltpu.VMEM) for x in nears))
+    )(rounded, totals, *(pltpu.with_memory_space_constraint(x, pltpu.VMEM) for x in nears))
 
 
 def ring_kernel(phase, ends, sources, where_ref, noise_ref, low_ref, high_ref, *rest):
@@ -406,8 +411,7 @@
         rounded, totals = class_weights(state, where_ref, counts_ref, mine_ref.shape[1])
         rounded_ref[...] = rounded
         totals_ref[...] = totals
-        bit = 1 - lax.rem(where_ref[0], 2)
-        class_sums(rounded, totals, bit, nears, mine_ref, theirs_ref)
+        class_sums(rounded, totals, 0, nears, mine_ref, theirs_ref)
     else:
         put_state(state, out_ref)
 
@@ -502,7 +506,9 @@
     bits = [(bit.astype(jnp.uint32), (1 - bit).astype(jnp.uint32)) for bit in bits]
     cut_at = core.astype(jnp.uint32) * cut
     where, cut_at, bits = lax.optimization_barrier((where, cut_at, bits))
-    own = functools.partial(own_scores, where=where, noise=near_noise, particles=particles)
+    own = functools.partial(
+        own_scores, blocks=blocks, where=where, noise=near_noise, particles=particles
+    )
     total = blocks * templates.shape[0]
     words, *sums, low, high, near, raw = own([0, 1], templates=held[0], rest=(picks,), total=total)
     turned, nears = [(low, high)], [near, raw]
@@ -554,7 +560,7 @@
     given = lax.ppermute(theirs, "cls", swap)
     across = lax.ppermute(mine + given, "blk", [(i, i ^ 1) for i in range(blocks)])
     rounded, _ = lax.optimization_barrier((rounded, given))
-    mine, theirs = rest_sums(where, rounded, totals, nears, piece)
+    mine, theirs = rest_sums(rounded, totals, nears, piece)
     kept = lax.optimization_barrier(mine + across)
     total = scatter_sum(kept + lax.ppermute(theirs, "cls", swap), blocks, bits)
     class_avg = total[:, :width] / total[:, width][:, None]

time: 70 us -> 70.2 us (level)
  transfers between devices with their start and end apart: 21 -> 21, of which waited for: 9 -> 7; matrix products, arithmetic and copies ran while one was open for 1% -> 1% of each run, Pallas kernels for 43% -> 42%
where the time goes in v17:
time: 70.2 us; the launch traced here: 70.1 us
  Pallas kernels  34.7 us (49%)
  starting transfers between devices  23.9 us (34%)
  waiting for transfers between devices  9.38 us (13%)
  other arithmetic  0.85 us (1%)
  between operations  0.8 us (1%)
    pallas_call x8, Pallas kernels, ring_scores(): pl.pallas_call(functools.partial(ring_kernel, phase, ends, sources), in_s...  19.5 us
    ppermute x8, starting transfers between devices, body(): own = lax.ppermute(message, ('blk', 'cls'), ring)  15.9 us
    pallas_call x3, Pallas kernels, own_scores(): pl.pallas_call(functools.partial(own_kernel, quarters, blocks), in_specs=...  12.6 us
    ppermute x2, starting transfers between devices, scatter_sum(): pieces = keep + lax.ppermute(send, 'blk', swaps)  4.74 us
    ppermute x2, waiting for transfers between devices, scatter_sum(): pieces = keep + lax.ppermute(send, 'blk', swaps)  4.01 us
    ppermute x8, waiting for transfers between devices, body(): own = lax.ppermute(message, ('blk', 'cls'), ring)  2.75 us
    ppermute x1, starting transfers between devices, body(): lax.ppermute(mine + given, 'blk', [(i, i ^ 1) for i in range(blocks)])  1.65 us
    ppermute x1, waiting for transfers between devices, body(): lax.ppermute(mine + given, 'blk', [(i, i ^ 1) for i in range(blocks)])  1.5 us
  transfers between devices with their start and end apart: 21, of which 7 were waited for; matrix products, arithmetic and copies ran while one was open for 1% of the time, Pallas kernels for 42%

profile of v17, /device:TPU:0, one launch (start us, length us, event | category | flops | bytes accessed | tf_op | source)
XLA Modules:
  0.0 70.1 jit_solution(18386155442528705229)
XLA Ops:
  2.1 3.1 %collective-permute-start.2 = (bf16[64,4096]{1,0:T(8,128)(2,1)S(1)}, bf16[64,4096]{1,0:T(8,128)(2,1)S(1)}, u32[]{:S(2)}, u32[]{:S(2)}) collective-permute-start(bf16[64,4096]{1,0:T(8,128)(2,1)S(1)} %get-tuple-element.52.tmpl_ref), channel_id=1, source_target_pairs={{0,4},{4,8},{8,12},{12,14},{14,10},{10,6},{6,2},{2,0},{5,1},{9,5},... | collective-permute-start | bytes 1572872 | tf_op jit(solution)/shard_map/ppermute | solution.py:542
  5.1 1.6 %collective-permute-start = (bf16[64,4224]{1,0:T(8,128)(2,1)S(1)}, bf16[64,4224]{1,0:T(8,128)(2,1)S(1)}, u32[]{:S(2)}, u32[]{:S(2)}) collective-permute-start(bf16[64,4224]{1,0:T(8,128)(2,1)S(1)} %get-tuple-element.51.tmpl_ref), channel_id=1, source_target_pairs={{0,4},{4,8},{8,12},{12,14},{14,10},{10,6},{6,2},{2,0},{5,1},{9,5},... | collective-permute-start | bytes 1622024 | tf_op jit(solution)/shard_map/ppermute | solution.py:542
  6.8 6.5 %shard_map.78 = (s32[16,1024]{1,0:T(8,128)S(1)}, f32[64,1024]{1,0:T(8,128)S(1)}, f32[64,128]{1,0:T(8,128)S(1)}, bf16[2048,1024]{1,0:T(8,128)(2,1)S(1)}, bf16[204...) custom-call(s32[2]{0:T(128)S(1)} %pad_add_fusion.where_ref, ...), custom_call_target="tpu_custom_call" | custom-call | flops 2147483648 | bytes 8388608 | tf_op jit(solution)/shard_map/pallas_call | solution.py:280
  13.4 1.6 %collective-permute-start.6 = (bf16[64,4096]{1,0:T(8,128)(2,1)S(1)}, bf16[64,4096]{1,0:T(8,128)(2,1)S(1)}, u32[]{:S(2)}, u32[]{:S(2)}) collective-permute-start(bf16[64,4096]{1,0:T(8,128)(2,1)S(1)} %collective-permute-done.2.rest_0_), channel_id=1, source_target_pairs={{0,4},{4,8},{8,12},{12,14},{14,10},{10,6},{6,2},{2,0},{5,1},{9,5},... | collective-permute-start | bytes 1572872 | tf_op jit(solution)/shard_map/ppermute | solution.py:542
  15.0 2.9 %shard_map.79 = (f32[64,1024]{1,0:T(8,128)S(1)}, f32[64,128]{1,0:T(8,128)S(1)}, bf16[2048,1024]{1,0:T(8,128)(2,1)S(1)}, bf16[2,1024,1024]{2,1,0:T(8,128)(2,1)S(1)}) custom-call(s32[2]{0:T(128)S(1)} %pad_add_fusion.where_ref, f32[1,8192]{1,0:T(1,128)S(1)} %get-tuple-element.50.noise_ref, bf16[64,4224]{1,0:T(8,128)(2,1)S(1)} %get-tuple-element.51.tmpl_ref, ...), custom_call_target="tpu_custom_call" | custom-call | flops 2147483648 | bytes 8388608 | tf_op jit(solution)/shard_map/pallas_call | solution.py:280
  18.5 1.6 %collective-permute-start.1 = (bf16[64,4224]{1,0:T(8,128)(2,1)S(1)}, bf16[64,4224]{1,0:T(8,128)(2,1)S(1)}, u32[]{:S(2)}, u32[]{:S(2)}) collective-permute-start(bf16[64,4224]{1,0:T(8,128)(2,1)S(1)} %collective-permute-done.rest_0_), channel_id=1, source_target_pairs={{0,4},{4,8},{8,12},{12,14},{14,10},{10,6},{6,2},{2,0},{5,1},{9,5},... | collective-permute-start | bytes 1622024 | tf_op jit(solution)/shard_map/ppermute | solution.py:542
  20.1 3.1 %shard_map.80 = (f32[16,1024]{1,0:T(8,128)S(1)}, bf16[2048,1024]{1,0:T(8,128)(2,1)S(1)}) custom-call(s32[2]{0:T(128)S(1)} %pad_add_fusion.where_ref, f32[1,8192]{1,0:T(1,128)S(1)} %get-tuple-element.50.noise_ref, bf16[64,4224]{1,0:T(8,128)(2,1)S(1)} %get-tuple-element.51.tmpl_ref, bf16[1024,8192]{1,0:T(8,128)(2,1)} %far_ref.5, ...), custom_call_target="tpu_custom_call" | custom-call | flops 2147483648 | bytes 8388608 | tf_op jit(solution)/shard_map/pallas_call | solution.py:280
  23.7 2.1 %collective-permute-start.11 = (bf16[64,4096]{1,0:T(8,128)(2,1)S(1)}, bf16[64,4096]{1,0:T(8,128)(2,1)S(1)}, u32[]{:S(2)}, u32[]{:S(2)}) collective-permute-start(bf16[64,4096]{1,0:T(8,128)(2,1)S(1)} %collective-permute-done.6.rest_0_), channel_id=1, source_target_pairs={{0,4},{4,8},{8,12},{12,14},{14,10},{10,6},{6,2},{2,0},{5,1},{9,5},... | collective-permute-start | bytes 1572872 | tf_op jit(solution)/shard_map/ppermute | solution.py:542
  25.7 2.0 %shard_map.81 = (f32[128,1024]{1,0:T(8,128)S(1)}, f32[128,128]{1,0:T(8,128)S(1)}) custom-call(s32[2]{0:T(128)S(1)} %pad_add_fusion.where_ref, f32[1,8192]{1,0:T(1,128)S(1)} %get-tuple-element.50.noise_ref, bf16[2048,1024]{1,0:T(8,128)(2,1)S(1)} %get-tuple-element.64.low_ref, bf16[2048,1024]{1,0:T(8,128)(2,1)S(1)} %get-tuple-element.65.high_ref, ...), custom_call_target="tpu_custom_call" | custom-call | flops 2147483648 | bytes 8388608 | tf_op jit(solution)/shard_map/pallas_call | solution.py:447
  27.8 1.7 %collective-permute-done.1.rest_0_ = bf16[64,4224]{1,0:T(8,128)(2,1)S(1)} collective-permute-done((bf16[64,4224]{1,0:T(8,128)(2,1)S(1)}, bf16[64,4224]{1,0:T(8,128)(2,1)S(1)}, u32[]{:S(2)}, u32[]{:S(2)}) %collective-permute-start.1) | collective-permute-done | bytes 540704 | tf_op jit(solution)/shard_map/ppermute | solution.py:542
  29.5 2.1 %collective-permute-start.4 = (bf16[64,4224]{1,0:T(8,128)(2,1)S(1)}, bf16[64,4224]{1,0:T(8,128)(2,1)S(1)}, u32[]{:S(2)}, u32[]{:S(2)}) collective-permute-start(bf16[64,4224]{1,0:T(8,128)(2,1)S(1)} %collective-permute-done.1.rest_0_), channel_id=1, source_target_pairs={{0,4},{4,8},{8,12},{12,14},{14,10},{10,6},{6,2},{2,0},{5,1},{9,5},... | collective-permute-start | bytes 1622024 | tf_op jit(solution)/shard_map/ppermute | solution.py:542
  31.5 2.4 %shard_map.83.rest_6_ = f32[16,1024]{1,0:T(8,128)S(1)} custom-call(s32[2]{0:T(128)S(1)} %pad_add_fusion.where_ref, f32[1,8192]{1,0:T(1,128)S(1)} %get-tuple-element.50.noise_ref, bf16[2048,1024]{1,0:T(8,128)(2,1)S(1)} %get-tuple-element.57.low_ref, bf16[2048,1024]{1,0:T(8,128)(2,1)S(1)} %get-tuple-element.62.high_ref, ...), custom_call_target="tpu_custom_call" | custom-call | flops 2147483648 | bytes 8388608 | tf_op jit(solution)/shard_map/pallas_call | solution.py:447
  34.0 2.0 %shard_map.82 = (f32[128,1024]{1,0:T(8,128)S(1)}, f32[128,128]{1,0:T(8,128)S(1)}) custom-call(s32[2]{0:T(128)S(1)} %pad_add_fusion.where_ref, f32[1,8192]{1,0:T(1,128)S(1)} %get-tuple-element.50.noise_ref, bf16[2048,1024]{1,0:T(8,128)(2,1)S(1)} %get-tuple-element.64.low_ref, bf16[2048,1024]{1,0:T(8,128)(2,1)S(1)} %get-tuple-element.65.high_ref, ...), custom_call_target="tpu_custom_call" | custom-call | flops 2147483648 | bytes 8388608 | tf_op jit(solution)/shard_map/pallas_call | solution.py:447
  37.8 2.4 %shard_map.84.rest_6_ = f32[16,1024]{1,0:T(8,128)S(1)} custom-call(s32[2]{0:T(128)S(1)} %pad_add_fusion.where_ref, f32[1,8192]{1,0:T(1,128)S(1)} %get-tuple-element.50.noise_ref, bf16[2048,1024]{1,0:T(8,128)(2,1)S(1)} %get-tuple-element.57.low_ref, bf16[2048,1024]{1,0:T(8,128)(2,1)S(1)} %get-tuple-element.62.high_ref, ...), custom_call_target="tpu_custom_call" | custom-call | flops 2147483648 | bytes 8388608 | tf_op jit(solution)/shard_map/pallas_call | solution.py:447
  41.0 2.3 %collective-permute-start.9 = (bf16[64,2176]{1,0:T(8,128)(2,1)S(1)}, bf16[64,2176]{1,0:T(8,128)(2,1)S(1)}, u32[]{:S(2)}, u32[]{:S(2)}) collective-permute-start(bf16[64,2176]{1,0:T(8,128)(2,1)S(1)} %constant_dynamic-slice_fusion.2), channel_id=1, source_target_pairs={{0,4},{4,8},{8,12},{12,14},{14,10},{10,6},{6,2},{2,0},{5,1},{9,5},... | collective-permute-start | bytes 835592 | tf_op jit(solution)/shard_map/ppermute | solution.py:542
  43.3 2.0 %shard_map.85 = (f32[128,1024]{1,0:T(8,128)S(1)}, f32[128,128]{1,0:T(8,128)S(1)}) custom-call(s32[2]{0:T(128)S(1)} %pad_add_fusion.where_ref, f32[1,8192]{1,0:T(1,128)S(1)} %get-tuple-element.50.noise_ref, bf16[2048,1024]{1,0:T(8,128)(2,1)S(1)} %get-tuple-element.64.low_ref, bf16[2048,1024]{1,0:T(8,128)(2,1)S(1)} %get-tuple-element.65.high_ref, ...), custom_call_target="tpu_custom_call" | custom-call | flops 2147483648 | bytes 8388608 | tf_op jit(solution)/shard_map/pallas_call | solution.py:447
  45.6 2.4 %shard_map.86.rest_6_ = f32[16,1024]{1,0:T(8,128)S(1)} custom-call(s32[2]{0:T(128)S(1)} %pad_add_fusion.where_ref, f32[1,8192]{1,0:T(1,128)S(1)} %get-tuple-element.50.noise_ref, bf16[2048,1024]{1,0:T(8,128)(2,1)S(1)} %get-tuple-element.57.low_ref, bf16[2048,1024]{1,0:T(8,128)(2,1)S(1)} %get-tuple-element.62.high_ref, ...), custom_call_target="tpu_custom_call" | custom-call | flops 2147483648 | bytes 8388608 | tf_op jit(solution)/shard_map/pallas_call | solution.py:447
  48.4 2.1 %shard_map.87 = (f32[64,1024]{1,0:T(8,128)S(1)}, f32[64,128]{1,0:T(8,128)S(1)}) custom-call(s32[2]{0:T(128)S(1)} %pad_add_fusion.where_ref, f32[1,8192]{1,0:T(1,128)S(1)} %get-tuple-element.50.noise_ref, bf16[2048,1024]{1,0:T(8,128)(2,1)S(1)} %get-tuple-element.64.low_ref, bf16[2048,1024]{1,0:T(8,128)(2,1)S(1)} %get-tuple-element.65.high_ref, ...), custom_call_target="tpu_custom_call" | custom-call | flops 2147483648 | bytes 8388608 | tf_op jit(solution)/shard_map/pallas_call | solution.py:447
  50.5 4.1 %shard_map.88 = (f32[1,1024]{1,0:T(1,128)}, f32[4,4,1152]{2,1,0:T(4,128)S(1)}, f32[4,4,1152]{2,1,0:T(4,128)S(1)}, bf16[8,1024]{1,0:T(8,128)(2,1)S(1)}, f32[8,128]{1,0:T(8,128)S(1)}) custom-call(s32[2]{0:T(128)S(1)} %pad_add_fusion.where_ref, f32[1,8192]{1,0:T(1,128)S(1)} %get-tuple-element.50.noise_ref, bf16[2048,1024]{1,0:T(8,128)(2,1)S(1)} %get-tuple-element.57.low_ref, ...), custom_call_target="tpu_custom_call" | custom-call | flops 2147483648 | bytes 8388608 | tf_op jit(solution)/shard_map/pallas_call | solution.py:447
  55.9 1.6 %collective-permute-start.17 = (f32[4,4,1152]{2,1,0:T(4,128)S(1)}, f32[4,4,1152]{2,1,0:T(4,128)S(1)}, u32[]{:S(2)}, u32[]{:S(2)}) collective-permute-start(f32[4,4,1152]{2,1,0:T(4,128)S(1)} %add.15), channel_id=1, source_target_pairs={{0,2},{2,0},{4,6},{6,4},{8,10},{10,8},{12,14},{14,12},{1,3},{3,1},... | collective-permute-start | bytes 221192 | tf_op jit(solution)/shard_map/ppermute | solution.py:561
  60.5 1.9 %collective-permute-start.19 = (f32[2,4,1152]{2,1,0:T(4,128)S(1)}, f32[2,4,1152]{2,1,0:T(4,128)S(1)}, u32[]{:S(2)}, u32[]{:S(2)}) collective-permute-start(f32[2,4,1152]{2,1,0:T(4,128)S(1)} %dynamic-slice_bitcast_fusion), channel_id=1, source_target_pairs={{0,4},{2,6},{4,0},{6,2},{8,12},{10,14},{12,8},{14,10},{1,5},{3,7},... | collective-permute-start | bytes 110600 | tf_op jit(solution)/shard_map/ppermute | solution.py:479
  62.3 2.2 %collective-permute-done.19 = f32[2,4,1152]{2,1,0:T(4,128)S(1)} collective-permute-done((f32[2,4,1152]{2,1,0:T(4,128)S(1)}, f32[2,4,1152]{2,1,0:T(4,128)S(1)}, u32[]{:S(2)}, u32[]{:S(2)}) %collective-permute-start.19) | collective-permute-done | bytes 36896 | tf_op jit(solution)/shard_map/ppermute | solution.py:479
  64.5 2.9 %collective-permute-start.20 = (f32[1,4,1152]{2,1,0:T(4,128)S(1)}, f32[1,4,1152]{2,1,0:T(4,128)S(1)}, u32[]{:S(2)}, u32[]{:S(2)}) collective-permute-start(f32[1,4,1152]{2,1,0:T(4,128)S(1)} %constant_dynamic-slice_fusion), channel_id=1, source_target_pairs={{0,8},{2,10},{4,12},{6,14},{8,0},{10,2},{12,4},{14,6},{1,9},{3,11}... | collective-permute-start | bytes 55304 | tf_op jit(solution)/shard_map/ppermute | solution.py:479
  67.4 1.8 %collective-permute-done.20 = f32[1,4,1152]{2,1,0:T(4,128)S(1)} collective-permute-done((f32[1,4,1152]{2,1,0:T(4,128)S(1)}, f32[1,4,1152]{2,1,0:T(4,128)S(1)}, u32[]{:S(2)}, u32[]{:S(2)}) %collective-permute-start.20) | collective-permute-done | bytes 18464 | tf_op jit(solution)/shard_map/ppermute | solution.py:479
  (48 shorter events, 10.7 us)
Async XLA Ops:
  2.1 11.3 %collective-permute-start.2 = (bf16[64,4096]{1,0:T(8,128)(2,1)S(1)}, bf16[64,4096]{1,0:T(8,128)(2,1)S(1)}, u32[]{:S(2)}, u32[]{:S(2)}) collective-permute-start(bf16[64,4096]{1,0:T(8,128)(2,1)S(1)} %get-tuple-element.52.tmpl_ref), channel_id=1, source_target_pairs={{0,4},{4,8},{8,12},{12,14},{14,10},{10,6},{6,2},{2,0},{5,1},{9,5},... | collective-permute-start | bytes 1572872 | tf_op jit(solution)/shard_map/ppermute | solution.py:542
  5.1 12.9 %collective-permute-start = (bf16[64,4224]{1,0:T(8,128)(2,1)S(1)}, bf16[64,4224]{1,0:T(8,128)(2,1)S(1)}, u32[]{:S(2)}, u32[]{:S(2)}) collective-permute-start(bf16[64,4224]{1,0:T(8,128)(2,1)S(1)} %get-tuple-element.51.tmpl_ref), channel_id=1, source_target_pairs={{0,4},{4,8},{8,12},{12,14},{14,10},{10,6},{6,2},{2,0},{5,1},{9,5},... | collective-permute-start | bytes 1622024 | tf_op jit(solution)/shard_map/ppermute | solution.py:542
  13.4 10.3 %collective-permute-start.6 = (bf16[64,4096]{1,0:T(8,128)(2,1)S(1)}, bf16[64,4096]{1,0:T(8,128)(2,1)S(1)}, u32[]{:S(2)}, u32[]{:S(2)}) collective-permute-start(bf16[64,4096]{1,0:T(8,128)(2,1)S(1)} %collective-permute-done.2.rest_0_), channel_id=1, source_target_pairs={{0,4},{4,8},{8,12},{12,14},{14,10},{10,6},{6,2},{2,0},{5,1},{9,5},... | collective-permute-start | bytes 1572872 | tf_op jit(solution)/shard_map/ppermute | solution.py:542
  15.0 5.1 %copy-start.1 = (s32[8]{0:T(128)S(1)}, s32[8]{0:T(128)}, u32[]{:S(2)}) copy-start(s32[8]{0:T(128)} %rest_7_.1) | copy-start | bytes 100
  15.0 5.1 %copy-start = (s32[64]{0:T(128)S(1)}, s32[64]{0:T(128)}, u32[]{:S(2)}) copy-start(s32[64]{0:T(128)} %param.9) | copy-start | bytes 772
  17.9 7.8 %collective-permute-start.3 = (bf16[64,4096]{1,0:T(8,128)(2,1)S(1)}, bf16[64,4096]{1,0:T(8,128)(2,1)S(1)}, u32[]{:S(2)}, u32[]{:S(2)}) collective-permute-start(bf16[64,4096]{1,0:T(8,128)(2,1)S(1)} %collective-permute-done.2.rest_0_), channel_id=1, source_target_pairs={{0,1},{1,0},{2,3},{3,2},{4,5},{5,4},{6,7},{7,6},{8,9},{9,8},{10,11... | collective-permute-start | bytes 1572872 | tf_op jit(solution)/shard_map/ppermute | solution.py:546
  18.0 13.5 %collective-permute-start.8 = (bf16[64,4224]{1,0:T(8,128)(2,1)S(1)}, bf16[64,4224]{1,0:T(8,128)(2,1)S(1)}, u32[]{:S(2)}, u32[]{:S(2)}) collective-permute-start(bf16[64,4224]{1,0:T(8,128)(2,1)S(1)} %collective-permute-done.rest_0_), channel_id=1, source_target_pairs={{0,1},{1,0},{2,3},{3,2},{4,5},{5,4},{6,7},{7,6},{8,9},{9,8},{10,11... | collective-permute-start | bytes 1622024 | tf_op jit(solution)/shard_map/ppermute | solution.py:546
  18.5 11.0 %collective-permute-start.1 = (bf16[64,4224]{1,0:T(8,128)(2,1)S(1)}, bf16[64,4224]{1,0:T(8,128)(2,1)S(1)}, u32[]{:S(2)}, u32[]{:S(2)}) collective-permute-start(bf16[64,4224]{1,0:T(8,128)(2,1)S(1)} %collective-permute-done.rest_0_), channel_id=1, source_target_pairs={{0,4},{4,8},{8,12},{12,14},{14,10},{10,6},{6,2},{2,0},{5,1},{9,5},... | collective-permute-start | bytes 1622024 | tf_op jit(solution)/shard_map/ppermute | solution.py:542
  23.7 10.3 %collective-permute-start.7 = (bf16[64,4096]{1,0:T(8,128)(2,1)S(1)}, bf16[64,4096]{1,0:T(8,128)(2,1)S(1)}, u32[]{:S(2)}, u32[]{:S(2)}) collective-permute-start(bf16[64,4096]{1,0:T(8,128)(2,1)S(1)} %collective-permute-done.6.rest_0_), channel_id=1, source_target_pairs={{0,1},{1,0},{2,3},{3,2},{4,5},{5,4},{6,7},{7,6},{8,9},{9,8},{10,11... | collective-permute-start | bytes 1572872 | tf_op jit(solution)/shard_map/ppermute | solution.py:546
  23.7 12.3 %collective-permute-start.11 = (bf16[64,4096]{1,0:T(8,128)(2,1)S(1)}, bf16[64,4096]{1,0:T(8,128)(2,1)S(1)}, u32[]{:S(2)}, u32[]{:S(2)}) collective-permute-start(bf16[64,4096]{1,0:T(8,128)(2,1)S(1)} %collective-permute-done.6.rest_0_), channel_id=1, source_target_pairs={{0,4},{4,8},{8,12},{12,14},{14,10},{10,6},{6,2},{2,0},{5,1},{9,5},... | collective-permute-start | bytes 1572872 | tf_op jit(solution)/shard_map/ppermute | solution.py:542
  29.5 8.4 %collective-permute-start.5 = (bf16[64,4224]{1,0:T(8,128)(2,1)S(1)}, bf16[64,4224]{1,0:T(8,128)(2,1)S(1)}, u32[]{:S(2)}, u32[]{:S(2)}) collective-permute-start(bf16[64,4224]{1,0:T(8,128)(2,1)S(1)} %collective-permute-done.1.rest_0_), channel_id=1, source_target_pairs={{0,1},{1,0},{2,3},{3,2},{4,5},{5,4},{6,7},{7,6},{8,9},{9,8},{10,11... | collective-permute-start | bytes 1622024 | tf_op jit(solution)/shard_map/ppermute | solution.py:546
  29.5 11.4 %collective-permute-start.4 = (bf16[64,4224]{1,0:T(8,128)(2,1)S(1)}, bf16[64,4224]{1,0:T(8,128)(2,1)S(1)}, u32[]{:S(2)}, u32[]{:S(2)}) collective-permute-start(bf16[64,4224]{1,0:T(8,128)(2,1)S(1)} %collective-permute-done.1.rest_0_), channel_id=1, source_target_pairs={{0,4},{4,8},{8,12},{12,14},{14,10},{10,6},{6,2},{2,0},{5,1},{9,5},... | collective-permute-start | bytes 1622024 | tf_op jit(solution)/shard_map/ppermute | solution.py:542
  36.0 7.4 %collective-permute-start.12 = (bf16[64,4096]{1,0:T(8,128)(2,1)S(1)}, bf16[64,4096]{1,0:T(8,128)(2,1)S(1)}, u32[]{:S(2)}, u32[]{:S(2)}) collective-permute-start(bf16[64,4096]{1,0:T(8,128)(2,1)S(1)} %collective-permute-done.11.rest_0_), channel_id=1, source_target_pairs={{0,1},{1,0},{2,3},{3,2},{4,5},{5,4},{6,7},{7,6},{8,9},{9,8},{10,11... | collective-permute-start | bytes 1572872 | tf_op jit(solution)/shard_map/ppermute | solution.py:546
  36.3 9.0 %collective-permute-start.14 = (bf16[64,2048]{1,0:T(8,128)(2,1)S(1)}, bf16[64,2048]{1,0:T(8,128)(2,1)S(1)}, u32[]{:S(2)}, u32[]{:S(2)}) collective-permute-start(bf16[64,2048]{1,0:T(8,128)(2,1)S(1)} %constant_dynamic-slice_fusion.1), channel_id=1, source_target_pairs={{0,4},{4,8},{8,12},{12,14},{14,10},{10,6},{6,2},{2,0},{5,1},{9,5},... | collective-permute-start | bytes 786440 | tf_op jit(solution)/shard_map/ppermute | solution.py:542
  40.9 4.7 %collective-permute-start.10 = (bf16[64,4224]{1,0:T(8,128)(2,1)S(1)}, bf16[64,4224]{1,0:T(8,128)(2,1)S(1)}, u32[]{:S(2)}, u32[]{:S(2)}) collective-permute-start(bf16[64,4224]{1,0:T(8,128)(2,1)S(1)} %collective-permute-done.4.rest_0_), channel_id=1, source_target_pairs={{0,1},{1,0},{2,3},{3,2},{4,5},{5,4},{6,7},{7,6},{8,9},{9,8},{10,11... | collective-permute-start | bytes 1622024 | tf_op jit(solution)/shard_map/ppermute | solution.py:546
  41.0 7.0 %collective-permute-start.9 = (bf16[64,2176]{1,0:T(8,128)(2,1)S(1)}, bf16[64,2176]{1,0:T(8,128)(2,1)S(1)}, u32[]{:S(2)}, u32[]{:S(2)}) collective-permute-start(bf16[64,2176]{1,0:T(8,128)(2,1)S(1)} %constant_dynamic-slice_fusion.2), channel_id=1, source_target_pairs={{0,4},{4,8},{8,12},{12,14},{14,10},{10,6},{6,2},{2,0},{5,1},{9,5},... | collective-permute-start | bytes 835592 | tf_op jit(solution)/shard_map/ppermute | solution.py:542
  45.3 3.1 %collective-permute-start.15 = (bf16[64,2048]{1,0:T(8,128)(2,1)S(1)}, bf16[64,2048]{1,0:T(8,128)(2,1)S(1)}, u32[]{:S(2)}, u32[]{:S(2)}) collective-permute-start(bf16[64,2048]{1,0:T(8,128)(2,1)S(1)} %collective-permute-done.14.rest_0_), channel_id=1, source_target_pairs={{0,1},{1,0},{2,3},{3,2},{4,5},{5,4},{6,7},{7,6},{8,9},{9,8},{10,11... | collective-permute-start | bytes 786440 | tf_op jit(solution)/shard_map/ppermute | solution.py:546
  48.0 2.5 %collective-permute-start.13 = (bf16[64,2176]{1,0:T(8,128)(2,1)S(1)}, bf16[64,2176]{1,0:T(8,128)(2,1)S(1)}, u32[]{:S(2)}, u32[]{:S(2)}) collective-permute-start(bf16[64,2176]{1,0:T(8,128)(2,1)S(1)} %collective-permute-done.9.rest_0_), channel_id=1, source_target_pairs={{0,1},{1,0},{2,3},{3,2},{4,5},{5,4},{6,7},{7,6},{8,9},{9,8},{10,11... | collective-permute-start | bytes 835592 | tf_op jit(solution)/shard_map/ppermute | solution.py:546
  54.7 1.3 %collective-permute-start.16 = (f32[4,4,1152]{2,1,0:T(4,128)S(1)}, f32[4,4,1152]{2,1,0:T(4,128)S(1)}, u32[]{:S(2)}, u32[]{:S(2)}) collective-permute-start(f32[4,4,1152]{2,1,0:T(4,128)S(1)} %get-tuple-element.86), channel_id=1, source_target_pairs={{0,1},{1,0},{2,3},{3,2},{4,5},{5,4},{6,7},{7,6},{8,9},{9,8},{10,11... | collective-permute-start | bytes 221192 | tf_op jit(solution)/shard_map/ppermute | solution.py:560
  55.9 4.4 %collective-permute-start.17 = (f32[4,4,1152]{2,1,0:T(4,128)S(1)}, f32[4,4,1152]{2,1,0:T(4,128)S(1)}, u32[]{:S(2)}, u32[]{:S(2)}) collective-permute-start(f32[4,4,1152]{2,1,0:T(4,128)S(1)} %add.15), channel_id=1, source_target_pairs={{0,2},{2,0},{4,6},{6,4},{8,10},{10,8},{12,14},{14,12},{1,3},{3,1},... | collective-permute-start | bytes 221192 | tf_op jit(solution)/shard_map/ppermute | solution.py:561
  58.8 1.6 %collective-permute-start.18 = (f32[4,4,1152]{2,1,0:T(4,128)S(1)}, f32[4,4,1152]{2,1,0:T(4,128)S(1)}, u32[]{:S(2)}, u32[]{:S(2)}) collective-permute-start(f32[4,4,1152]{2,1,0:T(4,128)S(1)} %get-tuple-element.91), channel_id=1, source_target_pairs={{0,1},{1,0},{2,3},{3,2},{4,5},{5,4},{6,7},{7,6},{8,9},{9,8},{10,11... | collective-permute-start | bytes 221192 | tf_op jit(solution)/shard_map/ppermute | solution.py:565
  60.5 4.0 %collective-permute-start.19 = (f32[2,4,1152]{2,1,0:T(4,128)S(1)}, f32[2,4,1152]{2,1,0:T(4,128)S(1)}, u32[]{:S(2)}, u32[]{:S(2)}) collective-permute-start(f32[2,4,1152]{2,1,0:T(4,128)S(1)} %dynamic-slice_bitcast_fusion), channel_id=1, source_target_pairs={{0,4},{2,6},{4,0},{6,2},{8,12},{10,14},{12,8},{14,10},{1,5},{3,7},... | collective-permute-start | bytes 110600 | tf_op jit(solution)/shard_map/ppermute | solution.py:479
  64.5 4.7 %collective-permute-start.20 = (f32[1,4,1152]{2,1,0:T(4,128)S(1)}, f32[1,4,1152]{2,1,0:T(4,128)S(1)}, u32[]{:S(2)}, u32[]{:S(2)}) collective-permute-start(f32[1,4,1152]{2,1,0:T(4,128)S(1)} %constant_dynamic-slice_fusion), channel_id=1, source_target_pairs={{0,8},{2,10},{4,12},{6,14},{8,0},{10,2},{12,4},{14,6},{1,9},{3,11}... | collective-permute-start | bytes 55304 | tf_op jit(solution)/shard_map/ppermute | solution.py:479

commit v18 on v17

--- a/solution.py
+++ b/solution.py
@@ -411,7 +411,11 @@
         rounded, totals = class_weights(state, where_ref, counts_ref, mine_ref.shape[1])
         rounded_ref[...] = rounded
         totals_ref[...] = totals
-        class_sums(rounded, totals, 0, nears, mine_ref, theirs_ref)
+
+        @pl.when(core >= 0)
+        def _():
+            class_sums(rounded_ref[...], totals_ref[...], 0, nears, mine_ref, theirs_ref)
+
     else:
         put_state(state, out_ref)
 

time: 70.2 us -> 70.5 us (level)
  transfers between devices with their start and end apart: 21 -> 21, of which waited for: 7 -> 7; matrix products, arithmetic and copies ran while one was open for 1% -> 1% of each run, Pallas kernels for 42% -> 41%
where the time goes in v18:
time: 70.5 us; the launch traced here: 70.4 us
  Pallas kernels  35 us (50%)
  starting transfers between devices  23.9 us (34%)
  waiting for transfers between devices  9.38 us (13%)
  other arithmetic  0.85 us (1%)
  between operations  0.8 us (1%)
    pallas_call x8, Pallas kernels, ring_scores(): pl.pallas_call(functools.partial(ring_kernel, phase, ends, sources), in_s...  19.8 us
    ppermute x8, starting transfers between devices, body(): own = lax.ppermute(message, ('blk', 'cls'), ring)  15.9 us
    pallas_call x3, Pallas kernels, own_scores(): pl.pallas_call(functools.partial(own_kernel, quarters, blocks), in_specs=...  12.6 us
    ppermute x2, starting transfers between devices, scatter_sum(): pieces = keep + lax.ppermute(send, 'blk', swaps)  4.74 us
    ppermute x2, waiting for transfers between devices, scatter_sum(): pieces = keep + lax.ppermute(send, 'blk', swaps)  4.01 us
    ppermute x8, waiting for transfers between devices, body(): own = lax.ppermute(message, ('blk', 'cls'), ring)  2.75 us
    ppermute x1, starting transfers between devices, body(): lax.ppermute(mine + given, 'blk', [(i, i ^ 1) for i in range(blocks)])  1.65 us
    ppermute x1, waiting for transfers between devices, body(): lax.ppermute(mine + given, 'blk', [(i, i ^ 1) for i in range(blocks)])  1.5 us
  transfers between devices with their start and end apart: 21, of which 7 were waited for; matrix products, arithmetic and copies ran while one was open for 1% of the time, Pallas kernels for 41%

profile of v18, /device:TPU:0, one launch (start us, length us, event | category | flops | bytes accessed | tf_op | source)
XLA Modules:
  0.0 70.4 jit_solution(2730693260042181325)
XLA Ops:
  2.1 3.1 %collective-permute-start.2 = (bf16[64,4096]{1,0:T(8,128)(2,1)S(1)}, bf16[64,4096]{1,0:T(8,128)(2,1)S(1)}, u32[]{:S(2)}, u32[]{:S(2)}) collective-permute-start(bf16[64,4096]{1,0:T(8,128)(2,1)S(1)} %get-tuple-element.52.tmpl_ref), channel_id=1, source_target_pairs={{0,4},{4,8},{8,12},{12,14},{14,10},{10,6},{6,2},{2,0},{5,1},{9,5},... | collective-permute-start | bytes 1572872 | tf_op jit(solution)/shard_map/ppermute | solution.py:546
  5.1 1.6 %collective-permute-start = (bf16[64,4224]{1,0:T(8,128)(2,1)S(1)}, bf16[64,4224]{1,0:T(8,128)(2,1)S(1)}, u32[]{:S(2)}, u32[]{:S(2)}) collective-permute-start(bf16[64,4224]{1,0:T(8,128)(2,1)S(1)} %get-tuple-element.51.tmpl_ref), channel_id=1, source_target_pairs={{0,4},{4,8},{8,12},{12,14},{14,10},{10,6},{6,2},{2,0},{5,1},{9,5},... | collective-permute-start | bytes 1622024 | tf_op jit(solution)/shard_map/ppermute | solution.py:546
  6.8 6.5 %shard_map.78 = (s32[16,1024]{1,0:T(8,128)S(1)}, f32[64,1024]{1,0:T(8,128)S(1)}, f32[64,128]{1,0:T(8,128)S(1)}, bf16[2048,1024]{1,0:T(8,128)(2,1)S(1)}, bf16[204...) custom-call(s32[2]{0:T(128)S(1)} %pad_add_fusion.where_ref, ...), custom_call_target="tpu_custom_call" | custom-call | flops 2147483648 | bytes 8388608 | tf_op jit(solution)/shard_map/pallas_call | solution.py:280
  13.4 1.6 %collective-permute-start.6 = (bf16[64,4096]{1,0:T(8,128)(2,1)S(1)}, bf16[64,4096]{1,0:T(8,128)(2,1)S(1)}, u32[]{:S(2)}, u32[]{:S(2)}) collective-permute-start(bf16[64,4096]{1,0:T(8,128)(2,1)S(1)} %collective-permute-done.2.rest_0_), channel_id=1, source_target_pairs={{0,4},{4,8},{8,12},{12,14},{14,10},{10,6},{6,2},{2,0},{5,1},{9,5},... | collective-permute-start | bytes 1572872 | tf_op jit(solution)/shard_map/ppermute | solution.py:546
  15.0 2.9 %shard_map.79 = (f32[64,1024]{1,0:T(8,128)S(1)}, f32[64,128]{1,0:T(8,128)S(1)}, bf16[2048,1024]{1,0:T(8,128)(2,1)S(1)}, bf16[2,1024,1024]{2,1,0:T(8,128)(2,1)S(1)}) custom-call(s32[2]{0:T(128)S(1)} %pad_add_fusion.where_ref, f32[1,8192]{1,0:T(1,128)S(1)} %get-tuple-element.50.noise_ref, bf16[64,4224]{1,0:T(8,128)(2,1)S(1)} %get-tuple-element.51.tmpl_ref, ...), custom_call_target="tpu_custom_call" | custom-call | flops 2147483648 | bytes 8388608 | tf_op jit(solution)/shard_map/pallas_call | solution.py:280
  18.5 1.6 %collective-permute-start.1 = (bf16[64,4224]{1,0:T(8,128)(2,1)S(1)}, bf16[64,4224]{1,0:T(8,128)(2,1)S(1)}, u32[]{:S(2)}, u32[]{:S(2)}) collective-permute-start(bf16[64,4224]{1,0:T(8,128)(2,1)S(1)} %collective-permute-done.rest_0_), channel_id=1, source_target_pairs={{0,4},{4,8},{8,12},{12,14},{14,10},{10,6},{6,2},{2,0},{5,1},{9,5},... | collective-permute-start | bytes 1622024 | tf_op jit(solution)/shard_map/ppermute | solution.py:546
  20.1 3.1 %shard_map.80 = (f32[16,1024]{1,0:T(8,128)S(1)}, bf16[2048,1024]{1,0:T(8,128)(2,1)S(1)}) custom-call(s32[2]{0:T(128)S(1)} %pad_add_fusion.where_ref, f32[1,8192]{1,0:T(1,128)S(1)} %get-tuple-element.50.noise_ref, bf16[64,4224]{1,0:T(8,128)(2,1)S(1)} %get-tuple-element.51.tmpl_ref, bf16[1024,8192]{1,0:T(8,128)(2,1)} %far_ref.5, ...), custom_call_target="tpu_custom_call" | custom-call | flops 2147483648 | bytes 8388608 | tf_op jit(solution)/shard_map/pallas_call | solution.py:280
  23.7 2.1 %collective-permute-start.11 = (bf16[64,4096]{1,0:T(8,128)(2,1)S(1)}, bf16[64,4096]{1,0:T(8,128)(2,1)S(1)}, u32[]{:S(2)}, u32[]{:S(2)}) collective-permute-start(bf16[64,4096]{1,0:T(8,128)(2,1)S(1)} %collective-permute-done.6.rest_0_), channel_id=1, source_target_pairs={{0,4},{4,8},{8,12},{12,14},{14,10},{10,6},{6,2},{2,0},{5,1},{9,5},... | collective-permute-start | bytes 1572872 | tf_op jit(solution)/shard_map/ppermute | solution.py:546
  25.7 2.0 %shard_map.81 = (f32[128,1024]{1,0:T(8,128)S(1)}, f32[128,128]{1,0:T(8,128)S(1)}) custom-call(s32[2]{0:T(128)S(1)} %pad_add_fusion.where_ref, f32[1,8192]{1,0:T(1,128)S(1)} %get-tuple-element.50.noise_ref, bf16[2048,1024]{1,0:T(8,128)(2,1)S(1)} %get-tuple-element.64.low_ref, bf16[2048,1024]{1,0:T(8,128)(2,1)S(1)} %get-tuple-element.65.high_ref, ...), custom_call_target="tpu_custom_call" | custom-call | flops 2147483648 | bytes 8388608 | tf_op jit(solution)/shard_map/pallas_call | solution.py:451
  27.8 1.7 %collective-permute-done.1.rest_0_ = bf16[64,4224]{1,0:T(8,128)(2,1)S(1)} collective-permute-done((bf16[64,4224]{1,0:T(8,128)(2,1)S(1)}, bf16[64,4224]{1,0:T(8,128)(2,1)S(1)}, u32[]{:S(2)}, u32[]{:S(2)}) %collective-permute-start.1) | collective-permute-done | bytes 540704 | tf_op jit(solution)/shard_map/ppermute | solution.py:546
  29.5 2.1 %collective-permute-start.4 = (bf16[64,4224]{1,0:T(8,128)(2,1)S(1)}, bf16[64,4224]{1,0:T(8,128)(2,1)S(1)}, u32[]{:S(2)}, u32[]{:S(2)}) collective-permute-start(bf16[64,4224]{1,0:T(8,128)(2,1)S(1)} %collective-permute-done.1.rest_0_), channel_id=1, source_target_pairs={{0,4},{4,8},{8,12},{12,14},{14,10},{10,6},{6,2},{2,0},{5,1},{9,5},... | collective-permute-start | bytes 1622024 | tf_op jit(solution)/shard_map/ppermute | solution.py:546
  31.5 2.4 %shard_map.83.rest_6_ = f32[16,1024]{1,0:T(8,128)S(1)} custom-call(s32[2]{0:T(128)S(1)} %pad_add_fusion.where_ref, f32[1,8192]{1,0:T(1,128)S(1)} %get-tuple-element.50.noise_ref, bf16[2048,1024]{1,0:T(8,128)(2,1)S(1)} %get-tuple-element.57.low_ref, bf16[2048,1024]{1,0:T(8,128)(2,1)S(1)} %get-tuple-element.62.high_ref, ...), custom_call_target="tpu_custom_call" | custom-call | flops 2147483648 | bytes 8388608 | tf_op jit(solution)/shard_map/pallas_call | solution.py:451
  34.0 2.0 %shard_map.82 = (f32[128,1024]{1,0:T(8,128)S(1)}, f32[128,128]{1,0:T(8,128)S(1)}) custom-call(s32[2]{0:T(128)S(1)} %pad_add_fusion.where_ref, f32[1,8192]{1,0:T(1,128)S(1)} %get-tuple-element.50.noise_ref, bf16[2048,1024]{1,0:T(8,128)(2,1)S(1)} %get-tuple-element.64.low_ref, bf16[2048,1024]{1,0:T(8,128)(2,1)S(1)} %get-tuple-element.65.high_ref, ...), custom_call_target="tpu_custom_call" | custom-call | flops 2147483648 | bytes 8388608 | tf_op jit(solution)/shard_map/pallas_call | solution.py:451
  37.8 2.4 %shard_map.84.rest_6_ = f32[16,1024]{1,0:T(8,128)S(1)} custom-call(s32[2]{0:T(128)S(1)} %pad_add_fusion.where_ref, f32[1,8192]{1,0:T(1,128)S(1)} %get-tuple-element.50.noise_ref, bf16[2048,1024]{1,0:T(8,128)(2,1)S(1)} %get-tuple-element.57.low_ref, bf16[2048,1024]{1,0:T(8,128)(2,1)S(1)} %get-tuple-element.62.high_ref, ...), custom_call_target="tpu_custom_call" | custom-call | flops 2147483648 | bytes 8388608 | tf_op jit(solution)/shard_map/pallas_call | solution.py:451
  41.0 2.3 %collective-permute-start.9 = (bf16[64,2176]{1,0:T(8,128)(2,1)S(1)}, bf16[64,2176]{1,0:T(8,128)(2,1)S(1)}, u32[]{:S(2)}, u32[]{:S(2)}) collective-permute-start(bf16[64,2176]{1,0:T(8,128)(2,1)S(1)} %constant_dynamic-slice_fusion.2), channel_id=1, source_target_pairs={{0,4},{4,8},{8,12},{12,14},{14,10},{10,6},{6,2},{2,0},{5,1},{9,5},... | collective-permute-start | bytes 835592 | tf_op jit(solution)/shard_map/ppermute | solution.py:546
  43.3 2.0 %shard_map.85 = (f32[128,1024]{1,0:T(8,128)S(1)}, f32[128,128]{1,0:T(8,128)S(1)}) custom-call(s32[2]{0:T(128)S(1)} %pad_add_fusion.where_ref, f32[1,8192]{1,0:T(1,128)S(1)} %get-tuple-element.50.noise_ref, bf16[2048,1024]{1,0:T(8,128)(2,1)S(1)} %get-tuple-element.64.low_ref, bf16[2048,1024]{1,0:T(8,128)(2,1)S(1)} %get-tuple-element.65.high_ref, ...), custom_call_target="tpu_custom_call" | custom-call | flops 2147483648 | bytes 8388608 | tf_op jit(solution)/shard_map/pallas_call | solution.py:451
  45.6 2.4 %shard_map.86.rest_6_ = f32[16,1024]{1,0:T(8,128)S(1)} custom-call(s32[2]{0:T(128)S(1)} %pad_add_fusion.where_ref, f32[1,8192]{1,0:T(1,128)S(1)} %get-tuple-element.50.noise_ref, bf16[2048,1024]{1,0:T(8,128)(2,1)S(1)} %get-tuple-element.57.low_ref, bf16[2048,1024]{1,0:T(8,128)(2,1)S(1)} %get-tuple-element.62.high_ref, ...), custom_call_target="tpu_custom_call" | custom-call | flops 2147483648 | bytes 8388608 | tf_op jit(solution)/shard_map/pallas_call | solution.py:451
  48.4 2.1 %shard_map.87 = (f32[64,1024]{1,0:T(8,128)S(1)}, f32[64,128]{1,0:T(8,128)S(1)}) custom-call(s32[2]{0:T(128)S(1)} %pad_add_fusion.where_ref, f32[1,8192]{1,0:T(1,128)S(1)} %get-tuple-element.50.noise_ref, bf16[2048,1024]{1,0:T(8,128)(2,1)S(1)} %get-tuple-element.64.low_ref, bf16[2048,1024]{1,0:T(8,128)(2,1)S(1)} %get-tuple-element.65.high_ref, ...), custom_call_target="tpu_custom_call" | custom-call | flops 2147483648 | bytes 8388608 | tf_op jit(solution)/shard_map/pallas_call | solution.py:451
  50.5 4.4 %shard_map.88 = (f32[1,1024]{1,0:T(1,128)}, f32[4,4,1152]{2,1,0:T(4,128)S(1)}, f32[4,4,1152]{2,1,0:T(4,128)S(1)}, bf16[8,1024]{1,0:T(8,128)(2,1)S(1)}, f32[8,128]{1,0:T(8,128)S(1)}) custom-call(s32[2]{0:T(128)S(1)} %pad_add_fusion.where_ref, f32[1,8192]{1,0:T(1,128)S(1)} %get-tuple-element.50.noise_ref, bf16[2048,1024]{1,0:T(8,128)(2,1)S(1)} %get-tuple-element.57.low_ref, ...), custom_call_target="tpu_custom_call" | custom-call | flops 2147483648 | bytes 8388608 | tf_op jit(solution)/shard_map/pallas_call | solution.py:451
  56.3 1.6 %collective-permute-start.17 = (f32[4,4,1152]{2,1,0:T(4,128)S(1)}, f32[4,4,1152]{2,1,0:T(4,128)S(1)}, u32[]{:S(2)}, u32[]{:S(2)}) collective-permute-start(f32[4,4,1152]{2,1,0:T(4,128)S(1)} %add.15), channel_id=1, source_target_pairs={{0,2},{2,0},{4,6},{6,4},{8,10},{10,8},{12,14},{14,12},{1,3},{3,1},... | collective-permute-start | bytes 221192 | tf_op jit(solution)/shard_map/ppermute | solution.py:565
  60.8 1.9 %collective-permute-start.19 = (f32[2,4,1152]{2,1,0:T(4,128)S(1)}, f32[2,4,1152]{2,1,0:T(4,128)S(1)}, u32[]{:S(2)}, u32[]{:S(2)}) collective-permute-start(f32[2,4,1152]{2,1,0:T(4,128)S(1)} %dynamic-slice_bitcast_fusion), channel_id=1, source_target_pairs={{0,4},{2,6},{4,0},{6,2},{8,12},{10,14},{12,8},{14,10},{1,5},{3,7},... | collective-permute-start | bytes 110600 | tf_op jit(solution)/shard_map/ppermute | solution.py:483
  62.7 2.2 %collective-permute-done.19 = f32[2,4,1152]{2,1,0:T(4,128)S(1)} collective-permute-done((f32[2,4,1152]{2,1,0:T(4,128)S(1)}, f32[2,4,1152]{2,1,0:T(4,128)S(1)}, u32[]{:S(2)}, u32[]{:S(2)}) %collective-permute-start.19) | collective-permute-done | bytes 36896 | tf_op jit(solution)/shard_map/ppermute | solution.py:483
  64.8 2.9 %collective-permute-start.20 = (f32[1,4,1152]{2,1,0:T(4,128)S(1)}, f32[1,4,1152]{2,1,0:T(4,128)S(1)}, u32[]{:S(2)}, u32[]{:S(2)}) collective-permute-start(f32[1,4,1152]{2,1,0:T(4,128)S(1)} %constant_dynamic-slice_fusion), channel_id=1, source_target_pairs={{0,8},{2,10},{4,12},{6,14},{8,0},{10,2},{12,4},{14,6},{1,9},{3,11}... | collective-permute-start | bytes 55304 | tf_op jit(solution)/shard_map/ppermute | solution.py:483
  67.7 1.8 %collective-permute-done.20 = f32[1,4,1152]{2,1,0:T(4,128)S(1)} collective-permute-done((f32[1,4,1152]{2,1,0:T(4,128)S(1)}, f32[1,4,1152]{2,1,0:T(4,128)S(1)}, u32[]{:S(2)}, u32[]{:S(2)}) %collective-permute-start.20) | collective-permute-done | bytes 18464 | tf_op jit(solution)/shard_map/ppermute | solution.py:483
  (48 shorter events, 10.7 us)
Async XLA Ops:
  2.1 11.3 %collective-permute-start.2 = (bf16[64,4096]{1,0:T(8,128)(2,1)S(1)}, bf16[64,4096]{1,0:T(8,128)(2,1)S(1)}, u32[]{:S(2)}, u32[]{:S(2)}) collective-permute-start(bf16[64,4096]{1,0:T(8,128)(2,1)S(1)} %get-tuple-element.52.tmpl_ref), channel_id=1, source_target_pairs={{0,4},{4,8},{8,12},{12,14},{14,10},{10,6},{6,2},{2,0},{5,1},{9,5},... | collective-permute-start | bytes 1572872 | tf_op jit(solution)/shard_map/ppermute | solution.py:546
  5.1 12.9 %collective-permute-start = (bf16[64,4224]{1,0:T(8,128)(2,1)S(1)}, bf16[64,4224]{1,0:T(8,128)(2,1)S(1)}, u32[]{:S(2)}, u32[]{:S(2)}) collective-permute-start(bf16[64,4224]{1,0:T(8,128)(2,1)S(1)} %get-tuple-element.51.tmpl_ref), channel_id=1, source_target_pairs={{0,4},{4,8},{8,12},{12,14},{14,10},{10,6},{6,2},{2,0},{5,1},{9,5},... | collective-permute-start | bytes 1622024 | tf_op jit(solution)/shard_map/ppermute | solution.py:546
  13.4 10.3 %collective-permute-start.6 = (bf16[64,4096]{1,0:T(8,128)(2,1)S(1)}, bf16[64,4096]{1,0:T(8,128)(2,1)S(1)}, u32[]{:S(2)}, u32[]{:S(2)}) collective-permute-start(bf16[64,4096]{1,0:T(8,128)(2,1)S(1)} %collective-permute-done.2.rest_0_), channel_id=1, source_target_pairs={{0,4},{4,8},{8,12},{12,14},{14,10},{10,6},{6,2},{2,0},{5,1},{9,5},... | collective-permute-start | bytes 1572872 | tf_op jit(solution)/shard_map/ppermute | solution.py:546
  15.0 5.1 %copy-start.1 = (s32[8]{0:T(128)S(1)}, s32[8]{0:T(128)}, u32[]{:S(2)}) copy-start(s32[8]{0:T(128)} %rest_7_.1) | copy-start | bytes 100
  15.0 5.1 %copy-start = (s32[64]{0:T(128)S(1)}, s32[64]{0:T(128)}, u32[]{:S(2)}) copy-start(s32[64]{0:T(128)} %param.9) | copy-start | bytes 772
  17.9 7.8 %collective-permute-start.3 = (bf16[64,4096]{1,0:T(8,128)(2,1)S(1)}, bf16[64,4096]{1,0:T(8,128)(2,1)S(1)}, u32[]{:S(2)}, u32[]{:S(2)}) collective-permute-start(bf16[64,4096]{1,0:T(8,128)(2,1)S(1)} %collective-permute-done.2.rest_0_), channel_id=1, source_target_pairs={{0,1},{1,0},{2,3},{3,2},{4,5},{5,4},{6,7},{7,6},{8,9},{9,8},{10,11... | collective-permute-start | bytes 1572872 | tf_op jit(solution)/shard_map/ppermute | solution.py:550
  18.0 13.5 %collective-permute-start.8 = (bf16[64,4224]{1,0:T(8,128)(2,1)S(1)}, bf16[64,4224]{1,0:T(8,128)(2,1)S(1)}, u32[]{:S(2)}, u32[]{:S(2)}) collective-permute-start(bf16[64,4224]{1,0:T(8,128)(2,1)S(1)} %collective-permute-done.rest_0_), channel_id=1, source_target_pairs={{0,1},{1,0},{2,3},{3,2},{4,5},{5,4},{6,7},{7,6},{8,9},{9,8},{10,11... | collective-permute-start | bytes 1622024 | tf_op jit(solution)/shard_map/ppermute | solution.py:550
  18.5 11.0 %collective-permute-start.1 = (bf16[64,4224]{1,0:T(8,128)(2,1)S(1)}, bf16[64,4224]{1,0:T(8,128)(2,1)S(1)}, u32[]{:S(2)}, u32[]{:S(2)}) collective-permute-start(bf16[64,4224]{1,0:T(8,128)(2,1)S(1)} %collective-permute-done.rest_0_), channel_id=1, source_target_pairs={{0,4},{4,8},{8,12},{12,14},{14,10},{10,6},{6,2},{2,0},{5,1},{9,5},... | collective-permute-start | bytes 1622024 | tf_op jit(solution)/shard_map/ppermute | solution.py:546
  23.7 10.3 %collective-permute-start.7 = (bf16[64,4096]{1,0:T(8,128)(2,1)S(1)}, bf16[64,4096]{1,0:T(8,128)(2,1)S(1)}, u32[]{:S(2)}, u32[]{:S(2)}) collective-permute-start(bf16[64,4096]{1,0:T(8,128)(2,1)S(1)} %collective-permute-done.6.rest_0_), channel_id=1, source_target_pairs={{0,1},{1,0},{2,3},{3,2},{4,5},{5,4},{6,7},{7,6},{8,9},{9,8},{10,11... | collective-permute-start | bytes 1572872 | tf_op jit(solution)/shard_map/ppermute | solution.py:550
  23.7 12.3 %collective-permute-start.11 = (bf16[64,4096]{1,0:T(8,128)(2,1)S(1)}, bf16[64,4096]{1,0:T(8,128)(2,1)S(1)}, u32[]{:S(2)}, u32[]{:S(2)}) collective-permute-start(bf16[64,4096]{1,0:T(8,128)(2,1)S(1)} %collective-permute-done.6.rest_0_), channel_id=1, source_target_pairs={{0,4},{4,8},{8,12},{12,14},{14,10},{10,6},{6,2},{2,0},{5,1},{9,5},... | collective-permute-start | bytes 1572872 | tf_op jit(solution)/shard_map/ppermute | solution.py:546
  29.5 8.4 %collective-permute-start.5 = (bf16[64,4224]{1,0:T(8,128)(2,1)S(1)}, bf16[64,4224]{1,0:T(8,128)(2,1)S(1)}, u32[]{:S(2)}, u32[]{:S(2)}) collective-permute-start(bf16[64,4224]{1,0:T(8,128)(2,1)S(1)} %collective-permute-done.1.rest_0_), channel_id=1, source_target_pairs={{0,1},{1,0},{2,3},{3,2},{4,5},{5,4},{6,7},{7,6},{8,9},{9,8},{10,11... | collective-permute-start | bytes 1622024 | tf_op jit(solution)/shard_map/ppermute | solution.py:550
  29.5 11.4 %collective-permute-start.4 = (bf16[64,4224]{1,0:T(8,128)(2,1)S(1)}, bf16[64,4224]{1,0:T(8,128)(2,1)S(1)}, u32[]{:S(2)}, u32[]{:S(2)}) collective-permute-start(bf16[64,4224]{1,0:T(8,128)(2,1)S(1)} %collective-permute-done.1.rest_0_), channel_id=1, source_target_pairs={{0,4},{4,8},{8,12},{12,14},{14,10},{10,6},{6,2},{2,0},{5,1},{9,5},... | collective-permute-start | bytes 1622024 | tf_op jit(solution)/shard_map/ppermute | solution.py:546
  36.0 7.4 %collective-permute-start.12 = (bf16[64,4096]{1,0:T(8,128)(2,1)S(1)}, bf16[64,4096]{1,0:T(8,128)(2,1)S(1)}, u32[]{:S(2)}, u32[]{:S(2)}) collective-permute-start(bf16[64,4096]{1,0:T(8,128)(2,1)S(1)} %collective-permute-done.11.rest_0_), channel_id=1, source_target_pairs={{0,1},{1,0},{2,3},{3,2},{4,5},{5,4},{6,7},{7,6},{8,9},{9,8},{10,11... | collective-permute-start | bytes 1572872 | tf_op jit(solution)/shard_map/ppermute | solution.py:550
  36.3 9.0 %collective-permute-start.14 = (bf16[64,2048]{1,0:T(8,128)(2,1)S(1)}, bf16[64,2048]{1,0:T(8,128)(2,1)S(1)}, u32[]{:S(2)}, u32[]{:S(2)}) collective-permute-start(bf16[64,2048]{1,0:T(8,128)(2,1)S(1)} %constant_dynamic-slice_fusion.1), channel_id=1, source_target_pairs={{0,4},{4,8},{8,12},{12,14},{14,10},{10,6},{6,2},{2,0},{5,1},{9,5},... | collective-permute-start | bytes 786440 | tf_op jit(solution)/shard_map/ppermute | solution.py:546
  40.9 4.7 %collective-permute-start.10 = (bf16[64,4224]{1,0:T(8,128)(2,1)S(1)}, bf16[64,4224]{1,0:T(8,128)(2,1)S(1)}, u32[]{:S(2)}, u32[]{:S(2)}) collective-permute-start(bf16[64,4224]{1,0:T(8,128)(2,1)S(1)} %collective-permute-done.4.rest_0_), channel_id=1, source_target_pairs={{0,1},{1,0},{2,3},{3,2},{4,5},{5,4},{6,7},{7,6},{8,9},{9,8},{10,11... | collective-permute-start | bytes 1622024 | tf_op jit(solution)/shard_map/ppermute | solution.py:550
  41.0 7.0 %collective-permute-start.9 = (bf16[64,2176]{1,0:T(8,128)(2,1)S(1)}, bf16[64,2176]{1,0:T(8,128)(2,1)S(1)}, u32[]{:S(2)}, u32[]{:S(2)}) collective-permute-start(bf16[64,2176]{1,0:T(8,128)(2,1)S(1)} %constant_dynamic-slice_fusion.2), channel_id=1, source_target_pairs={{0,4},{4,8},{8,12},{12,14},{14,10},{10,6},{6,2},{2,0},{5,1},{9,5},... | collective-permute-start | bytes 835592 | tf_op jit(solution)/shard_map/ppermute | solution.py:546
  45.3 3.1 %collective-permute-start.15 = (bf16[64,2048]{1,0:T(8,128)(2,1)S(1)}, bf16[64,2048]{1,0:T(8,128)(2,1)S(1)}, u32[]{:S(2)}, u32[]{:S(2)}) collective-permute-start(bf16[64,2048]{1,0:T(8,128)(2,1)S(1)} %collective-permute-done.14.rest_0_), channel_id=1, source_target_pairs={{0,1},{1,0},{2,3},{3,2},{4,5},{5,4},{6,7},{7,6},{8,9},{9,8},{10,11... | collective-permute-start | bytes 786440 | tf_op jit(solution)/shard_map/ppermute | solution.py:550
  48.0 2.5 %collective-permute-start.13 = (bf16[64,2176]{1,0:T(8,128)(2,1)S(1)}, bf16[64,2176]{1,0:T(8,128)(2,1)S(1)}, u32[]{:S(2)}, u32[]{:S(2)}) collective-permute-start(bf16[64,2176]{1,0:T(8,128)(2,1)S(1)} %collective-permute-done.9.rest_0_), channel_id=1, source_target_pairs={{0,1},{1,0},{2,3},{3,2},{4,5},{5,4},{6,7},{7,6},{8,9},{9,8},{10,11... | collective-permute-start | bytes 835592 | tf_op jit(solution)/shard_map/ppermute | solution.py:550
  55.0 1.3 %collective-permute-start.16 = (f32[4,4,1152]{2,1,0:T(4,128)S(1)}, f32[4,4,1152]{2,1,0:T(4,128)S(1)}, u32[]{:S(2)}, u32[]{:S(2)}) collective-permute-start(f32[4,4,1152]{2,1,0:T(4,128)S(1)} %get-tuple-element.86), channel_id=1, source_target_pairs={{0,1},{1,0},{2,3},{3,2},{4,5},{5,4},{6,7},{7,6},{8,9},{9,8},{10,11... | collective-permute-start | bytes 221192 | tf_op jit(solution)/shard_map/ppermute | solution.py:564
  56.3 4.4 %collective-permute-start.17 = (f32[4,4,1152]{2,1,0:T(4,128)S(1)}, f32[4,4,1152]{2,1,0:T(4,128)S(1)}, u32[]{:S(2)}, u32[]{:S(2)}) collective-permute-start(f32[4,4,1152]{2,1,0:T(4,128)S(1)} %add.15), channel_id=1, source_target_pairs={{0,2},{2,0},{4,6},{6,4},{8,10},{10,8},{12,14},{14,12},{1,3},{3,1},... | collective-permute-start | bytes 221192 | tf_op jit(solution)/shard_map/ppermute | solution.py:565
  59.1 1.6 %collective-permute-start.18 = (f32[4,4,1152]{2,1,0:T(4,128)S(1)}, f32[4,4,1152]{2,1,0:T(4,128)S(1)}, u32[]{:S(2)}, u32[]{:S(2)}) collective-permute-start(f32[4,4,1152]{2,1,0:T(4,128)S(1)} %get-tuple-element.91), channel_id=1, source_target_pairs={{0,1},{1,0},{2,3},{3,2},{4,5},{5,4},{6,7},{7,6},{8,9},{9,8},{10,11... | collective-permute-start | bytes 221192 | tf_op jit(solution)/shard_map/ppermute | solution.py:569
  60.8 4.0 %collective-permute-start.19 = (f32[2,4,1152]{2,1,0:T(4,128)S(1)}, f32[2,4,1152]{2,1,0:T(4,128)S(1)}, u32[]{:S(2)}, u32[]{:S(2)}) collective-permute-start(f32[2,4,1152]{2,1,0:T(4,128)S(1)} %dynamic-slice_bitcast_fusion), channel_id=1, source_target_pairs={{0,4},{2,6},{4,0},{6,2},{8,12},{10,14},{12,8},{14,10},{1,5},{3,7},... | collective-permute-start | bytes 110600 | tf_op jit(solution)/shard_map/ppermute | solution.py:483
  64.8 4.7 %collective-permute-start.20 = (f32[1,4,1152]{2,1,0:T(4,128)S(1)}, f32[1,4,1152]{2,1,0:T(4,128)S(1)}, u32[]{:S(2)}, u32[]{:S(2)}) collective-permute-start(f32[1,4,1152]{2,1,0:T(4,128)S(1)} %constant_dynamic-slice_fusion), channel_id=1, source_target_pairs={{0,8},{2,10},{4,12},{6,14},{8,0},{10,2},{12,4},{14,6},{1,9},{3,11}... | collective-permute-start | bytes 55304 | tf_op jit(solution)/shard_map/ppermute | solution.py:483

commit v19 on v17

--- a/solution.py
+++ b/solution.py
@@ -373,16 +373,24 @@
     core = where_ref[1]
 
     for at, part_ref in enumerate((low_ref, high_ref)):
-        for step in range(quarter // WIDTH):
-            there = pl.ds(step * WIDTH, WIDTH)
-            columns = pl.ds((2 * phase + at) * quarter + step * WIDTH, WIDTH)
+
+        def add(step):
+            there = pl.ds(pl.multiple_of(step * WIDTH, WIDTH), WIDTH)
+            begin = (2 * phase + at) * quarter + step * WIDTH
+            columns = pl.ds(pl.multiple_of(begin, WIDTH), WIDTH)
             if ends:
                 rows = jnp.where(core == at, row_refs[0][:, there], row_refs[1][:, there])
             else:
-                here = pl.ds(at * quarter + step * WIDTH, WIDTH)
+                here = pl.ds(pl.multiple_of(at * quarter + step * WIDTH, WIDTH), WIDTH)
                 rows = jnp.concatenate([ref[:, here] for ref in row_refs], axis=0)
             weighted = weigh(rows, noise_ref[:, columns], energy)
             acc[...] += jnp.dot(weighted, part_ref[there, :], preferred_element_type=jnp.float32)
+
+        if ends and phase == 1:
+            pl.loop(0, quarter // WIDTH)(add)
+        else:
+            for step in range(quarter // WIDTH):
+                add(step)
 
     if phase == 0:
         return

time: 70.2 us -> 70.8 us (level)
  transfers between devices with their start and end apart: 21 -> 21, of which waited for: 7 -> 7; matrix products, arithmetic and copies ran while one was open for 1% -> 1% of each run, Pallas kernels for 42% -> 41%
where the time goes in v19:
time: 70.8 us; the launch traced here: 70.7 us
  Pallas kernels  35.3 us (50%)
  starting transfers between devices  23.9 us (34%)
  waiting for transfers between devices  9.38 us (13%)
  other arithmetic  0.85 us (1%)
  between operations  0.8 us (1%)
    pallas_call x8, Pallas kernels, ring_scores(): pl.pallas_call(functools.partial(ring_kernel, phase, ends, sources), in_s...  20.1 us
    ppermute x8, starting transfers between devices, body(): own = lax.ppermute(message, ('blk', 'cls'), ring)  15.9 us
    pallas_call x3, Pallas kernels, own_scores(): pl.pallas_call(functools.partial(own_kernel, quarters, blocks), in_specs=...  12.6 us
    ppermute x2, starting transfers between devices, scatter_sum(): pieces = keep + lax.ppermute(send, 'blk', swaps)  4.74 us
    ppermute x2, waiting for transfers between devices, scatter_sum(): pieces = keep + lax.ppermute(send, 'blk', swaps)  4.01 us
    ppermute x8, waiting for transfers between devices, body(): own = lax.ppermute(message, ('blk', 'cls'), ring)  2.75 us
    ppermute x1, starting transfers between devices, body(): lax.ppermute(mine + given, 'blk', [(i, i ^ 1) for i in range(blocks)])  1.65 us
    ppermute x1, waiting for transfers between devices, body(): lax.ppermute(mine + given, 'blk', [(i, i ^ 1) for i in range(blocks)])  1.5 us
  transfers between devices with their start and end apart: 21, of which 7 were waited for; matrix products, arithmetic and copies ran while one was open for 1% of the time, Pallas kernels for 41%

profile of v19, /device:TPU:0, one launch (start us, length us, event | category | flops | bytes accessed | tf_op | source)
XLA Modules:
  0.0 70.7 jit_solution(8581692665172223740)
XLA Ops:
  2.1 3.1 %collective-permute-start.2 = (bf16[64,4096]{1,0:T(8,128)(2,1)S(1)}, bf16[64,4096]{1,0:T(8,128)(2,1)S(1)}, u32[]{:S(2)}, u32[]{:S(2)}) collective-permute-start(bf16[64,4096]{1,0:T(8,128)(2,1)S(1)} %get-tuple-element.52.tmpl_ref), channel_id=1, source_target_pairs={{0,4},{4,8},{8,12},{12,14},{14,10},{10,6},{6,2},{2,0},{5,1},{9,5},... | collective-permute-start | bytes 1572872 | tf_op jit(solution)/shard_map/ppermute | solution.py:550
  5.1 1.6 %collective-permute-start = (bf16[64,4224]{1,0:T(8,128)(2,1)S(1)}, bf16[64,4224]{1,0:T(8,128)(2,1)S(1)}, u32[]{:S(2)}, u32[]{:S(2)}) collective-permute-start(bf16[64,4224]{1,0:T(8,128)(2,1)S(1)} %get-tuple-element.51.tmpl_ref), channel_id=1, source_target_pairs={{0,4},{4,8},{8,12},{12,14},{14,10},{10,6},{6,2},{2,0},{5,1},{9,5},... | collective-permute-start | bytes 1622024 | tf_op jit(solution)/shard_map/ppermute | solution.py:550
  6.8 6.5 %shard_map.78 = (s32[16,1024]{1,0:T(8,128)S(1)}, f32[64,1024]{1,0:T(8,128)S(1)}, f32[64,128]{1,0:T(8,128)S(1)}, bf16[2048,1024]{1,0:T(8,128)(2,1)S(1)}, bf16[204...) custom-call(s32[2]{0:T(128)S(1)} %pad_add_fusion.where_ref, ...), custom_call_target="tpu_custom_call" | custom-call | flops 2147483648 | bytes 8388608 | tf_op jit(solution)/shard_map/pallas_call | solution.py:280
  13.4 1.6 %collective-permute-start.6 = (bf16[64,4096]{1,0:T(8,128)(2,1)S(1)}, bf16[64,4096]{1,0:T(8,128)(2,1)S(1)}, u32[]{:S(2)}, u32[]{:S(2)}) collective-permute-start(bf16[64,4096]{1,0:T(8,128)(2,1)S(1)} %collective-permute-done.2.rest_0_), channel_id=1, source_target_pairs={{0,4},{4,8},{8,12},{12,14},{14,10},{10,6},{6,2},{2,0},{5,1},{9,5},... | collective-permute-start | bytes 1572872 | tf_op jit(solution)/shard_map/ppermute | solution.py:550
  15.0 2.9 %shard_map.79 = (f32[64,1024]{1,0:T(8,128)S(1)}, f32[64,128]{1,0:T(8,128)S(1)}, bf16[2048,1024]{1,0:T(8,128)(2,1)S(1)}, bf16[2,1024,1024]{2,1,0:T(8,128)(2,1)S(1)}) custom-call(s32[2]{0:T(128)S(1)} %pad_add_fusion.where_ref, f32[1,8192]{1,0:T(1,128)S(1)} %get-tuple-element.50.noise_ref, bf16[64,4224]{1,0:T(8,128)(2,1)S(1)} %get-tuple-element.51.tmpl_ref, ...), custom_call_target="tpu_custom_call" | custom-call | flops 2147483648 | bytes 8388608 | tf_op jit(solution)/shard_map/pallas_call | solution.py:280
  18.5 1.6 %collective-permute-start.1 = (bf16[64,4224]{1,0:T(8,128)(2,1)S(1)}, bf16[64,4224]{1,0:T(8,128)(2,1)S(1)}, u32[]{:S(2)}, u32[]{:S(2)}) collective-permute-start(bf16[64,4224]{1,0:T(8,128)(2,1)S(1)} %collective-permute-done.rest_0_), channel_id=1, source_target_pairs={{0,4},{4,8},{8,12},{12,14},{14,10},{10,6},{6,2},{2,0},{5,1},{9,5},... | collective-permute-start | bytes 1622024 | tf_op jit(solution)/shard_map/ppermute | solution.py:550
  20.1 3.1 %shard_map.80 = (f32[16,1024]{1,0:T(8,128)S(1)}, bf16[2048,1024]{1,0:T(8,128)(2,1)S(1)}) custom-call(s32[2]{0:T(128)S(1)} %pad_add_fusion.where_ref, f32[1,8192]{1,0:T(1,128)S(1)} %get-tuple-element.50.noise_ref, bf16[64,4224]{1,0:T(8,128)(2,1)S(1)} %get-tuple-element.51.tmpl_ref, bf16[1024,8192]{1,0:T(8,128)(2,1)} %far_ref.5, ...), custom_call_target="tpu_custom_call" | custom-call | flops 2147483648 | bytes 8388608 | tf_op jit(solution)/shard_map/pallas_call | solution.py:280
  23.7 2.1 %collective-permute-start.11 = (bf16[64,4096]{1,0:T(8,128)(2,1)S(1)}, bf16[64,4096]{1,0:T(8,128)(2,1)S(1)}, u32[]{:S(2)}, u32[]{:S(2)}) collective-permute-start(bf16[64,4096]{1,0:T(8,128)(2,1)S(1)} %collective-permute-done.6.rest_0_), channel_id=1, source_target_pairs={{0,4},{4,8},{8,12},{12,14},{14,10},{10,6},{6,2},{2,0},{5,1},{9,5},... | collective-permute-start | bytes 1572872 | tf_op jit(solution)/shard_map/ppermute | solution.py:550
  25.7 2.0 %shard_map.81 = (f32[128,1024]{1,0:T(8,128)S(1)}, f32[128,128]{1,0:T(8,128)S(1)}) custom-call(s32[2]{0:T(128)S(1)} %pad_add_fusion.where_ref, f32[1,8192]{1,0:T(1,128)S(1)} %get-tuple-element.50.noise_ref, bf16[2048,1024]{1,0:T(8,128)(2,1)S(1)} %get-tuple-element.64.low_ref, bf16[2048,1024]{1,0:T(8,128)(2,1)S(1)} %get-tuple-element.65.high_ref, ...), custom_call_target="tpu_custom_call" | custom-call | flops 2147483648 | bytes 8388608 | tf_op jit(solution)/shard_map/pallas_call | solution.py:455
  27.8 1.7 %collective-permute-done.1.rest_0_ = bf16[64,4224]{1,0:T(8,128)(2,1)S(1)} collective-permute-done((bf16[64,4224]{1,0:T(8,128)(2,1)S(1)}, bf16[64,4224]{1,0:T(8,128)(2,1)S(1)}, u32[]{:S(2)}, u32[]{:S(2)}) %collective-permute-start.1) | collective-permute-done | bytes 540704 | tf_op jit(solution)/shard_map/ppermute | solution.py:550
  29.5 2.1 %collective-permute-start.4 = (bf16[64,4224]{1,0:T(8,128)(2,1)S(1)}, bf16[64,4224]{1,0:T(8,128)(2,1)S(1)}, u32[]{:S(2)}, u32[]{:S(2)}) collective-permute-start(bf16[64,4224]{1,0:T(8,128)(2,1)S(1)} %collective-permute-done.1.rest_0_), channel_id=1, source_target_pairs={{0,4},{4,8},{8,12},{12,14},{14,10},{10,6},{6,2},{2,0},{5,1},{9,5},... | collective-permute-start | bytes 1622024 | tf_op jit(solution)/shard_map/ppermute | solution.py:550
  31.5 2.4 %shard_map.83.rest_6_ = f32[16,1024]{1,0:T(8,128)S(1)} custom-call(s32[2]{0:T(128)S(1)} %pad_add_fusion.where_ref, f32[1,8192]{1,0:T(1,128)S(1)} %get-tuple-element.50.noise_ref, bf16[2048,1024]{1,0:T(8,128)(2,1)S(1)} %get-tuple-element.57.low_ref, bf16[2048,1024]{1,0:T(8,128)(2,1)S(1)} %get-tuple-element.62.high_ref, ...), custom_call_target="tpu_custom_call" | custom-call | flops 2147483648 | bytes 8388608 | tf_op jit(solution)/shard_map/pallas_call | solution.py:455
  34.0 2.0 %shard_map.82 = (f32[128,1024]{1,0:T(8,128)S(1)}, f32[128,128]{1,0:T(8,128)S(1)}) custom-call(s32[2]{0:T(128)S(1)} %pad_add_fusion.where_ref, f32[1,8192]{1,0:T(1,128)S(1)} %get-tuple-element.50.noise_ref, bf16[2048,1024]{1,0:T(8,128)(2,1)S(1)} %get-tuple-element.64.low_ref, bf16[2048,1024]{1,0:T(8,128)(2,1)S(1)} %get-tuple-element.65.high_ref, ...), custom_call_target="tpu_custom_call" | custom-call | flops 2147483648 | bytes 8388608 | tf_op jit(solution)/shard_map/pallas_call | solution.py:455
  37.8 2.4 %shard_map.84.rest_6_ = f32[16,1024]{1,0:T(8,128)S(1)} custom-call(s32[2]{0:T(128)S(1)} %pad_add_fusion.where_ref, f32[1,8192]{1,0:T(1,128)S(1)} %get-tuple-element.50.noise_ref, bf16[2048,1024]{1,0:T(8,128)(2,1)S(1)} %get-tuple-element.57.low_ref, bf16[2048,1024]{1,0:T(8,128)(2,1)S(1)} %get-tuple-element.62.high_ref, ...), custom_call_target="tpu_custom_call" | custom-call | flops 2147483648 | bytes 8388608 | tf_op jit(solution)/shard_map/pallas_call | solution.py:455
  41.0 2.3 %collective-permute-start.9 = (bf16[64,2176]{1,0:T(8,128)(2,1)S(1)}, bf16[64,2176]{1,0:T(8,128)(2,1)S(1)}, u32[]{:S(2)}, u32[]{:S(2)}) collective-permute-start(bf16[64,2176]{1,0:T(8,128)(2,1)S(1)} %constant_dynamic-slice_fusion.2), channel_id=1, source_target_pairs={{0,4},{4,8},{8,12},{12,14},{14,10},{10,6},{6,2},{2,0},{5,1},{9,5},... | collective-permute-start | bytes 835592 | tf_op jit(solution)/shard_map/ppermute | solution.py:550
  43.3 2.0 %shard_map.85 = (f32[128,1024]{1,0:T(8,128)S(1)}, f32[128,128]{1,0:T(8,128)S(1)}) custom-call(s32[2]{0:T(128)S(1)} %pad_add_fusion.where_ref, f32[1,8192]{1,0:T(1,128)S(1)} %get-tuple-element.50.noise_ref, bf16[2048,1024]{1,0:T(8,128)(2,1)S(1)} %get-tuple-element.64.low_ref, bf16[2048,1024]{1,0:T(8,128)(2,1)S(1)} %get-tuple-element.65.high_ref, ...), custom_call_target="tpu_custom_call" | custom-call | flops 2147483648 | bytes 8388608 | tf_op jit(solution)/shard_map/pallas_call | solution.py:455
  45.6 2.4 %shard_map.86.rest_6_ = f32[16,1024]{1,0:T(8,128)S(1)} custom-call(s32[2]{0:T(128)S(1)} %pad_add_fusion.where_ref, f32[1,8192]{1,0:T(1,128)S(1)} %get-tuple-element.50.noise_ref, bf16[2048,1024]{1,0:T(8,128)(2,1)S(1)} %get-tuple-element.57.low_ref, bf16[2048,1024]{1,0:T(8,128)(2,1)S(1)} %get-tuple-element.62.high_ref, ...), custom_call_target="tpu_custom_call" | custom-call | flops 2147483648 | bytes 8388608 | tf_op jit(solution)/shard_map/pallas_call | solution.py:455
  48.4 2.1 %shard_map.87 = (f32[64,1024]{1,0:T(8,128)S(1)}, f32[64,128]{1,0:T(8,128)S(1)}) custom-call(s32[2]{0:T(128)S(1)} %pad_add_fusion.where_ref, f32[1,8192]{1,0:T(1,128)S(1)} %get-tuple-element.50.noise_ref, bf16[2048,1024]{1,0:T(8,128)(2,1)S(1)} %get-tuple-element.64.low_ref, bf16[2048,1024]{1,0:T(8,128)(2,1)S(1)} %get-tuple-element.65.high_ref, ...), custom_call_target="tpu_custom_call" | custom-call | flops 2147483648 | bytes 8388608 | tf_op jit(solution)/shard_map/pallas_call | solution.py:455
  50.5 4.7 %shard_map.88 = (f32[1,1024]{1,0:T(1,128)}, f32[4,4,1152]{2,1,0:T(4,128)S(1)}, f32[4,4,1152]{2,1,0:T(4,128)S(1)}, bf16[8,1024]{1,0:T(8,128)(2,1)S(1)}, f32[8,128]{1,0:T(8,128)S(1)}) custom-call(s32[2]{0:T(128)S(1)} %pad_add_fusion.where_ref, f32[1,8192]{1,0:T(1,128)S(1)} %get-tuple-element.50.noise_ref, bf16[2048,1024]{1,0:T(8,128)(2,1)S(1)} %get-tuple-element.57.low_ref, ...), custom_call_target="tpu_custom_call" | custom-call | flops 2147483648 | bytes 8388608 | tf_op jit(solution)/shard_map/pallas_call | solution.py:455
  56.6 1.6 %collective-permute-start.17 = (f32[4,4,1152]{2,1,0:T(4,128)S(1)}, f32[4,4,1152]{2,1,0:T(4,128)S(1)}, u32[]{:S(2)}, u32[]{:S(2)}) collective-permute-start(f32[4,4,1152]{2,1,0:T(4,128)S(1)} %add.15), channel_id=1, source_target_pairs={{0,2},{2,0},{4,6},{6,4},{8,10},{10,8},{12,14},{14,12},{1,3},{3,1},... | collective-permute-start | bytes 221192 | tf_op jit(solution)/shard_map/ppermute | solution.py:569
  61.1 1.9 %collective-permute-start.19 = (f32[2,4,1152]{2,1,0:T(4,128)S(1)}, f32[2,4,1152]{2,1,0:T(4,128)S(1)}, u32[]{:S(2)}, u32[]{:S(2)}) collective-permute-start(f32[2,4,1152]{2,1,0:T(4,128)S(1)} %dynamic-slice_bitcast_fusion), channel_id=1, source_target_pairs={{0,4},{2,6},{4,0},{6,2},{8,12},{10,14},{12,8},{14,10},{1,5},{3,7},... | collective-permute-start | bytes 110600 | tf_op jit(solution)/shard_map/ppermute | solution.py:487
  62.9 2.2 %collective-permute-done.19 = f32[2,4,1152]{2,1,0:T(4,128)S(1)} collective-permute-done((f32[2,4,1152]{2,1,0:T(4,128)S(1)}, f32[2,4,1152]{2,1,0:T(4,128)S(1)}, u32[]{:S(2)}, u32[]{:S(2)}) %collective-permute-start.19) | collective-permute-done | bytes 36896 | tf_op jit(solution)/shard_map/ppermute | solution.py:487
  65.1 2.9 %collective-permute-start.20 = (f32[1,4,1152]{2,1,0:T(4,128)S(1)}, f32[1,4,1152]{2,1,0:T(4,128)S(1)}, u32[]{:S(2)}, u32[]{:S(2)}) collective-permute-start(f32[1,4,1152]{2,1,0:T(4,128)S(1)} %constant_dynamic-slice_fusion), channel_id=1, source_target_pairs={{0,8},{2,10},{4,12},{6,14},{8,0},{10,2},{12,4},{14,6},{1,9},{3,11}... | collective-permute-start | bytes 55304 | tf_op jit(solution)/shard_map/ppermute | solution.py:487
  68.0 1.8 %collective-permute-done.20 = f32[1,4,1152]{2,1,0:T(4,128)S(1)} collective-permute-done((f32[1,4,1152]{2,1,0:T(4,128)S(1)}, f32[1,4,1152]{2,1,0:T(4,128)S(1)}, u32[]{:S(2)}, u32[]{:S(2)}) %collective-permute-start.20) | collective-permute-done | bytes 18464 | tf_op jit(solution)/shard_map/ppermute | solution.py:487
  (48 shorter events, 10.7 us)
Async XLA Ops:
  2.1 11.3 %collective-permute-start.2 = (bf16[64,4096]{1,0:T(8,128)(2,1)S(1)}, bf16[64,4096]{1,0:T(8,128)(2,1)S(1)}, u32[]{:S(2)}, u32[]{:S(2)}) collective-permute-start(bf16[64,4096]{1,0:T(8,128)(2,1)S(1)} %get-tuple-element.52.tmpl_ref), channel_id=1, source_target_pairs={{0,4},{4,8},{8,12},{12,14},{14,10},{10,6},{6,2},{2,0},{5,1},{9,5},... | collective-permute-start | bytes 1572872 | tf_op jit(solution)/shard_map/ppermute | solution.py:550
  5.1 12.9 %collective-permute-start = (bf16[64,4224]{1,0:T(8,128)(2,1)S(1)}, bf16[64,4224]{1,0:T(8,128)(2,1)S(1)}, u32[]{:S(2)}, u32[]{:S(2)}) collective-permute-start(bf16[64,4224]{1,0:T(8,128)(2,1)S(1)} %get-tuple-element.51.tmpl_ref), channel_id=1, source_target_pairs={{0,4},{4,8},{8,12},{12,14},{14,10},{10,6},{6,2},{2,0},{5,1},{9,5},... | collective-permute-start | bytes 1622024 | tf_op jit(solution)/shard_map/ppermute | solution.py:550
  13.4 10.3 %collective-permute-start.6 = (bf16[64,4096]{1,0:T(8,128)(2,1)S(1)}, bf16[64,4096]{1,0:T(8,128)(2,1)S(1)}, u32[]{:S(2)}, u32[]{:S(2)}) collective-permute-start(bf16[64,4096]{1,0:T(8,128)(2,1)S(1)} %collective-permute-done.2.rest_0_), channel_id=1, source_target_pairs={{0,4},{4,8},{8,12},{12,14},{14,10},{10,6},{6,2},{2,0},{5,1},{9,5},... | collective-permute-start | bytes 1572872 | tf_op jit(solution)/shard_map/ppermute | solution.py:550
  15.0 5.1 %copy-start.1 = (s32[8]{0:T(128)S(1)}, s32[8]{0:T(128)}, u32[]{:S(2)}) copy-start(s32[8]{0:T(128)} %rest_7_.1) | copy-start | bytes 100
  15.0 5.1 %copy-start = (s32[64]{0:T(128)S(1)}, s32[64]{0:T(128)}, u32[]{:S(2)}) copy-start(s32[64]{0:T(128)} %param.9) | copy-start | bytes 772
  17.9 7.8 %collective-permute-start.3 = (bf16[64,4096]{1,0:T(8,128)(2,1)S(1)}, bf16[64,4096]{1,0:T(8,128)(2,1)S(1)}, u32[]{:S(2)}, u32[]{:S(2)}) collective-permute-start(bf16[64,4096]{1,0:T(8,128)(2,1)S(1)} %collective-permute-done.2.rest_0_), channel_id=1, source_target_pairs={{0,1},{1,0},{2,3},{3,2},{4,5},{5,4},{6,7},{7,6},{8,9},{9,8},{10,11... | collective-permute-start | bytes 1572872 | tf_op jit(solution)/shard_map/ppermute | solution.py:554
  18.0 13.5 %collective-permute-start.8 = (bf16[64,4224]{1,0:T(8,128)(2,1)S(1)}, bf16[64,4224]{1,0:T(8,128)(2,1)S(1)}, u32[]{:S(2)}, u32[]{:S(2)}) collective-permute-start(bf16[64,4224]{1,0:T(8,128)(2,1)S(1)} %collective-permute-done.rest_0_), channel_id=1, source_target_pairs={{0,1},{1,0},{2,3},{3,2},{4,5},{5,4},{6,7},{7,6},{8,9},{9,8},{10,11... | collective-permute-start | bytes 1622024 | tf_op jit(solution)/shard_map/ppermute | solution.py:554
  18.5 11.0 %collective-permute-start.1 = (bf16[64,4224]{1,0:T(8,128)(2,1)S(1)}, bf16[64,4224]{1,0:T(8,128)(2,1)S(1)}, u32[]{:S(2)}, u32[]{:S(2)}) collective-permute-start(bf16[64,4224]{1,0:T(8,128)(2,1)S(1)} %collective-permute-done.rest_0_), channel_id=1, source_target_pairs={{0,4},{4,8},{8,12},{12,14},{14,10},{10,6},{6,2},{2,0},{5,1},{9,5},... | collective-permute-start | bytes 1622024 | tf_op jit(solution)/shard_map/ppermute | solution.py:550
  23.7 10.3 %collective-permute-start.7 = (bf16[64,4096]{1,0:T(8,128)(2,1)S(1)}, bf16[64,4096]{1,0:T(8,128)(2,1)S(1)}, u32[]{:S(2)}, u32[]{:S(2)}) collective-permute-start(bf16[64,4096]{1,0:T(8,128)(2,1)S(1)} %collective-permute-done.6.rest_0_), channel_id=1, source_target_pairs={{0,1},{1,0},{2,3},{3,2},{4,5},{5,4},{6,7},{7,6},{8,9},{9,8},{10,11... | collective-permute-start | bytes 1572872 | tf_op jit(solution)/shard_map/ppermute | solution.py:554
  23.7 12.3 %collective-permute-start.11 = (bf16[64,4096]{1,0:T(8,128)(2,1)S(1)}, bf16[64,4096]{1,0:T(8,128)(2,1)S(1)}, u32[]{:S(2)}, u32[]{:S(2)}) collective-permute-start(bf16[64,4096]{1,0:T(8,128)(2,1)S(1)} %collective-permute-done.6.rest_0_), channel_id=1, source_target_pairs={{0,4},{4,8},{8,12},{12,14},{14,10},{10,6},{6,2},{2,0},{5,1},{9,5},... | collective-permute-start | bytes 1572872 | tf_op jit(solution)/shard_map/ppermute | solution.py:550
  29.5 8.4 %collective-permute-start.5 = (bf16[64,4224]{1,0:T(8,128)(2,1)S(1)}, bf16[64,4224]{1,0:T(8,128)(2,1)S(1)}, u32[]{:S(2)}, u32[]{:S(2)}) collective-permute-start(bf16[64,4224]{1,0:T(8,128)(2,1)S(1)} %collective-permute-done.1.rest_0_), channel_id=1, source_target_pairs={{0,1},{1,0},{2,3},{3,2},{4,5},{5,4},{6,7},{7,6},{8,9},{9,8},{10,11... | collective-permute-start | bytes 1622024 | tf_op jit(solution)/shard_map/ppermute | solution.py:554
  29.5 11.4 %collective-permute-start.4 = (bf16[64,4224]{1,0:T(8,128)(2,1)S(1)}, bf16[64,4224]{1,0:T(8,128)(2,1)S(1)}, u32[]{:S(2)}, u32[]{:S(2)}) collective-permute-start(bf16[64,4224]{1,0:T(8,128)(2,1)S(1)} %collective-permute-done.1.rest_0_), channel_id=1, source_target_pairs={{0,4},{4,8},{8,12},{12,14},{14,10},{10,6},{6,2},{2,0},{5,1},{9,5},... | collective-permute-start | bytes 1622024 | tf_op jit(solution)/shard_map/ppermute | solution.py:550
  36.0 7.4 %collective-permute-start.12 = (bf16[64,4096]{1,0:T(8,128)(2,1)S(1)}, bf16[64,4096]{1,0:T(8,128)(2,1)S(1)}, u32[]{:S(2)}, u32[]{:S(2)}) collective-permute-start(bf16[64,4096]{1,0:T(8,128)(2,1)S(1)} %collective-permute-done.11.rest_0_), channel_id=1, source_target_pairs={{0,1},{1,0},{2,3},{3,2},{4,5},{5,4},{6,7},{7,6},{8,9},{9,8},{10,11... | collective-permute-start | bytes 1572872 | tf_op jit(solution)/shard_map/ppermute | solution.py:554
  36.3 9.0 %collective-permute-start.14 = (bf16[64,2048]{1,0:T(8,128)(2,1)S(1)}, bf16[64,2048]{1,0:T(8,128)(2,1)S(1)}, u32[]{:S(2)}, u32[]{:S(2)}) collective-permute-start(bf16[64,2048]{1,0:T(8,128)(2,1)S(1)} %constant_dynamic-slice_fusion.1), channel_id=1, source_target_pairs={{0,4},{4,8},{8,12},{12,14},{14,10},{10,6},{6,2},{2,0},{5,1},{9,5},... | collective-permute-start | bytes 786440 | tf_op jit(solution)/shard_map/ppermute | solution.py:550
  40.9 4.7 %collective-permute-start.10 = (bf16[64,4224]{1,0:T(8,128)(2,1)S(1)}, bf16[64,4224]{1,0:T(8,128)(2,1)S(1)}, u32[]{:S(2)}, u32[]{:S(2)}) collective-permute-start(bf16[64,4224]{1,0:T(8,128)(2,1)S(1)} %collective-permute-done.4.rest_0_), channel_id=1, source_target_pairs={{0,1},{1,0},{2,3},{3,2},{4,5},{5,4},{6,7},{7,6},{8,9},{9,8},{10,11... | collective-permute-start | bytes 1622024 | tf_op jit(solution)/shard_map/ppermute | solution.py:554
  41.0 7.0 %collective-permute-start.9 = (bf16[64,2176]{1,0:T(8,128)(2,1)S(1)}, bf16[64,2176]{1,0:T(8,128)(2,1)S(1)}, u32[]{:S(2)}, u32[]{:S(2)}) collective-permute-start(bf16[64,2176]{1,0:T(8,128)(2,1)S(1)} %constant_dynamic-slice_fusion.2), channel_id=1, source_target_pairs={{0,4},{4,8},{8,12},{12,14},{14,10},{10,6},{6,2},{2,0},{5,1},{9,5},... | collective-permute-start | bytes 835592 | tf_op jit(solution)/shard_map/ppermute | solution.py:550
  45.3 3.1 %collective-permute-start.15 = (bf16[64,2048]{1,0:T(8,128)(2,1)S(1)}, bf16[64,2048]{1,0:T(8,128)(2,1)S(1)}, u32[]{:S(2)}, u32[]{:S(2)}) collective-permute-start(bf16[64,2048]{1,0:T(8,128)(2,1)S(1)} %collective-permute-done.14.rest_0_), channel_id=1, source_target_pairs={{0,1},{1,0},{2,3},{3,2},{4,5},{5,4},{6,7},{7,6},{8,9},{9,8},{10,11... | collective-permute-start | bytes 786440 | tf_op jit(solution)/shard_map/ppermute | solution.py:554
  48.0 2.5 %collective-permute-start.13 = (bf16[64,2176]{1,0:T(8,128)(2,1)S(1)}, bf16[64,2176]{1,0:T(8,128)(2,1)S(1)}, u32[]{:S(2)}, u32[]{:S(2)}) collective-permute-start(bf16[64,2176]{1,0:T(8,128)(2,1)S(1)} %collective-permute-done.9.rest_0_), channel_id=1, source_target_pairs={{0,1},{1,0},{2,3},{3,2},{4,5},{5,4},{6,7},{7,6},{8,9},{9,8},{10,11... | collective-permute-start | bytes 835592 | tf_op jit(solution)/shard_map/ppermute | solution.py:554
  55.3 1.3 %collective-permute-start.16 = (f32[4,4,1152]{2,1,0:T(4,128)S(1)}, f32[4,4,1152]{2,1,0:T(4,128)S(1)}, u32[]{:S(2)}, u32[]{:S(2)}) collective-permute-start(f32[4,4,1152]{2,1,0:T(4,128)S(1)} %get-tuple-element.86), channel_id=1, source_target_pairs={{0,1},{1,0},{2,3},{3,2},{4,5},{5,4},{6,7},{7,6},{8,9},{9,8},{10,11... | collective-permute-start | bytes 221192 | tf_op jit(solution)/shard_map/ppermute | solution.py:568
  56.6 4.4 %collective-permute-start.17 = (f32[4,4,1152]{2,1,0:T(4,128)S(1)}, f32[4,4,1152]{2,1,0:T(4,128)S(1)}, u32[]{:S(2)}, u32[]{:S(2)}) collective-permute-start(f32[4,4,1152]{2,1,0:T(4,128)S(1)} %add.15), channel_id=1, source_target_pairs={{0,2},{2,0},{4,6},{6,4},{8,10},{10,8},{12,14},{14,12},{1,3},{3,1},... | collective-permute-start | bytes 221192 | tf_op jit(solution)/shard_map/ppermute | solution.py:569
  59.4 1.6 %collective-permute-start.18 = (f32[4,4,1152]{2,1,0:T(4,128)S(1)}, f32[4,4,1152]{2,1,0:T(4,128)S(1)}, u32[]{:S(2)}, u32[]{:S(2)}) collective-permute-start(f32[4,4,1152]{2,1,0:T(4,128)S(1)} %get-tuple-element.91), channel_id=1, source_target_pairs={{0,1},{1,0},{2,3},{3,2},{4,5},{5,4},{6,7},{7,6},{8,9},{9,8},{10,11... | collective-permute-start | bytes 221192 | tf_op jit(solution)/shard_map/ppermute | solution.py:573
  61.1 4.0 %collective-permute-start.19 = (f32[2,4,1152]{2,1,0:T(4,128)S(1)}, f32[2,4,1152]{2,1,0:T(4,128)S(1)}, u32[]{:S(2)}, u32[]{:S(2)}) collective-permute-start(f32[2,4,1152]{2,1,0:T(4,128)S(1)} %dynamic-slice_bitcast_fusion), channel_id=1, source_target_pairs={{0,4},{2,6},{4,0},{6,2},{8,12},{10,14},{12,8},{14,10},{1,5},{3,7},... | collective-permute-start | bytes 110600 | tf_op jit(solution)/shard_map/ppermute | solution.py:487
  65.1 4.7 %collective-permute-start.20 = (f32[1,4,1152]{2,1,0:T(4,128)S(1)}, f32[1,4,1152]{2,1,0:T(4,128)S(1)}, u32[]{:S(2)}, u32[]{:S(2)}) collective-permute-start(f32[1,4,1152]{2,1,0:T(4,128)S(1)} %constant_dynamic-slice_fusion), channel_id=1, source_target_pairs={{0,8},{2,10},{4,12},{6,14},{8,0},{10,2},{12,4},{14,6},{1,9},{3,11}... | collective-permute-start | bytes 55304 | tf_op jit(solution)/shard_map/ppermute | solution.py:487

commit v20 on v12

--- a/solution.py
+++ b/solution.py
@@ -340,7 +340,11 @@
     )(where, rounded, totals, *(pltpu.with_memory_space_constraint(x, pltpu.VMEM) for x in nears))
 
 
-def ring_kernel(phase, ends, sources, where_ref, noise_ref, low_ref, high_ref, *rest):
+def ring_kernel(phase, ends, sources, *rest):
+    where_ref = None
+    if phase or ends:
+        where_ref, *rest = rest
+    noise_ref, low_ref, high_ref, *rest = rest
     row_refs, rest = rest[: 2 * len(sources)], rest[2 * len(sources) :]
     if phase == 0:
         acc, energy = rest
@@ -358,7 +362,7 @@
         acc[...] = acc_in[...]
         energy[...] = energy_in[...]
     quarter = low_ref.shape[0]
-    core = where_ref[1]
+    core = where_ref[1] if phase or ends else None
 
     for at, part_ref in enumerate((low_ref, high_ref)):
         for step in range(quarter // WIDTH):
@@ -415,6 +419,7 @@
     ]
     scratch = [pltpu.VMEM(array.shape, array.dtype) for array in sums]
     specs = []
+    places = [where] if phase or ends else []
     if phase == 0:
         shapes, scratch = sums, []
     else:
@@ -435,7 +440,7 @@
             shapes = [jax.ShapeDtypeStruct(rest[4].shape, jnp.float32)]
     return pl.pallas_call(
         functools.partial(ring_kernel, phase, ends, sources),
-        in_specs=[in_smem()] + [in_vmem()] * (3 + len(arrays)) + specs,
+        in_specs=[in_smem()] * len(places) + [in_vmem()] * (3 + len(arrays)) + specs,
         out_specs=[in_vmem()] * len(shapes),
         out_shape=shapes,
         scratch_shapes=scratch,
@@ -446,7 +451,7 @@
             transcendentals=0,
         ),
     )(
-        where,
+        *places,
         noise,
         *(pltpu.with_memory_space_constraint(part, pltpu.VMEM) for part in turned),
         *arrays,

time: 70 us -> 70 us (level)
  Pallas kernels: 34.3 us -> 32.7 us
  waiting for transfers between devices: 9.96 us -> 11.1 us
    pallas_call x8, Pallas kernels: 19 us -> 17.4 us  [ring_scores(): pl.pallas_call(functools.partial(ring_kernel, phase, ends, sources), in_s...]
    ppermute x8, waiting for transfers between devices: 3.29 us -> 4.65 us  [body(): own = lax.ppermute(message, ('blk', 'cls'), ring)]
  transfers between devices with their start and end apart: 21 -> 21, of which waited for: 9 -> 10; matrix products, arithmetic and copies ran while one was open for 1% -> 1% of each run, Pallas kernels for 42% -> 40%
where the time goes in v20:
time: 70 us; the launch traced here: 69.8 us
  Pallas kernels  32.7 us (47%)
  starting transfers between devices  24 us (34%)
  waiting for transfers between devices  11.1 us (16%)
  other arithmetic  0.85 us (1%)
  between operations  0.79 us (1%)
    pallas_call x8, Pallas kernels, ring_scores(): pl.pallas_call(functools.partial(ring_kernel, phase, ends, sources), in_s...  17.4 us
    ppermute x8, starting transfers between devices, body(): own = lax.ppermute(message, ('blk', 'cls'), ring)  16.3 us
    pallas_call x3, Pallas kernels, own_scores(): pl.pallas_call(functools.partial(own_kernel, quarters), in_specs=[in_smem...  12.1 us
    ppermute x8, waiting for transfers between devices, body(): own = lax.ppermute(message, ('blk', 'cls'), ring)  4.65 us
    ppermute x2, waiting for transfers between devices, scatter_sum(): pieces = keep + lax.ppermute(send, 'blk', swaps)  4.39 us
    ppermute x2, starting transfers between devices, scatter_sum(): pieces = keep + lax.ppermute(send, 'blk', swaps)  4.36 us
    ppermute x1, starting transfers between devices, body(): lax.ppermute(mine + given, 'blk', [(i, i ^ 1) for i in range(blocks)])  2.09 us
    pallas_call x1, Pallas kernels, rest_sums(): pl.pallas_call(rest_kernel, in_specs=[in_smem()] + [in_vmem()] * (2 + len...  1.74 us
  transfers between devices with their start and end apart: 21, of which 10 were waited for; matrix products, arithmetic and copies ran while one was open for 1% of the time, Pallas kernels for 40%

profile of v20, /device:TPU:0, one launch (start us, length us, event | category | flops | bytes accessed | tf_op | source)
XLA Modules:
  0.0 69.8 jit_solution(16402757602322419019)
XLA Ops:
  2.1 3.1 %collective-permute-start.2 = (bf16[64,4096]{1,0:T(8,128)(2,1)S(1)}, bf16[64,4096]{1,0:T(8,128)(2,1)S(1)}, u32[]{:S(2)}, u32[]{:S(2)}) collective-permute-start(bf16[64,4096]{1,0:T(8,128)(2,1)S(1)} %get-tuple-element.52.tmpl_ref), channel_id=1, source_target_pairs={{0,4},{4,8},{8,12},{12,14},{14,10},{10,6},{6,2},{2,0},{5,1},{9,5},... | collective-permute-start | bytes 1572872 | tf_op jit(solution)/shard_map/ppermute | solution.py:534
  5.1 1.6 %collective-permute-start = (bf16[64,4224]{1,0:T(8,128)(2,1)S(1)}, bf16[64,4224]{1,0:T(8,128)(2,1)S(1)}, u32[]{:S(2)}, u32[]{:S(2)}) collective-permute-start(bf16[64,4224]{1,0:T(8,128)(2,1)S(1)} %get-tuple-element.51.tmpl_ref), channel_id=1, source_target_pairs={{0,4},{4,8},{8,12},{12,14},{14,10},{10,6},{6,2},{2,0},{5,1},{9,5},... | collective-permute-start | bytes 1622024 | tf_op jit(solution)/shard_map/ppermute | solution.py:534
  6.8 6.2 %shard_map.78 = (s32[16,1024]{1,0:T(8,128)S(1)}, f32[64,1024]{1,0:T(8,128)S(1)}, f32[64,128]{1,0:T(8,128)S(1)}, bf16[2048,1024]{1,0:T(8,128)(2,1)S(1)}, bf16[204...) custom-call(s32[2]{0:T(128)S(1)} %pad_add_fusion.where_ref.rest_0_, ...), custom_call_target="tpu_custom_call" | custom-call | flops 2147483648 | bytes 8388608 | tf_op jit(solution)/shard_map/pallas_call | solution.py:267
  13.0 1.6 %collective-permute-start.6 = (bf16[64,4096]{1,0:T(8,128)(2,1)S(1)}, bf16[64,4096]{1,0:T(8,128)(2,1)S(1)}, u32[]{:S(2)}, u32[]{:S(2)}) collective-permute-start(bf16[64,4096]{1,0:T(8,128)(2,1)S(1)} %collective-permute-done.2.rest_3_), channel_id=1, source_target_pairs={{0,4},{4,8},{8,12},{12,14},{14,10},{10,6},{6,2},{2,0},{5,1},{9,5},... | collective-permute-start | bytes 1572872 | tf_op jit(solution)/shard_map/ppermute | solution.py:534
  14.7 2.8 %shard_map.79 = (f32[64,1024]{1,0:T(8,128)S(1)}, f32[64,128]{1,0:T(8,128)S(1)}, bf16[2048,1024]{1,0:T(8,128)(2,1)S(1)}, bf16[4,1024,512]{2,1,0:T(8,128)(2,1)S(1)}) custom-call(s32[2]{0:T(128)S(1)} %pad_add_fusion.where_ref.rest_0_, f32[1,8192]{1,0:T(1,128)S(1)} %get-tuple-element.50.noise_ref.rest_0_.rest_1_, ...), custom_call_target="tpu_custom_call" | custom-call | flops 2147483648 | bytes 8388608 | tf_op jit(solution)/shard_map/pallas_call | solution.py:267
  18.1 2.0 %collective-permute-start.1 = (bf16[64,4224]{1,0:T(8,128)(2,1)S(1)}, bf16[64,4224]{1,0:T(8,128)(2,1)S(1)}, u32[]{:S(2)}, u32[]{:S(2)}) collective-permute-start(bf16[64,4224]{1,0:T(8,128)(2,1)S(1)} %collective-permute-done.rest_4_), channel_id=1, source_target_pairs={{0,4},{4,8},{8,12},{12,14},{14,10},{10,6},{6,2},{2,0},{5,1},{9,5},... | collective-permute-start | bytes 1622024 | tf_op jit(solution)/shard_map/ppermute | solution.py:534
  20.1 3.0 %shard_map.80 = (f32[16,1024]{1,0:T(8,128)S(1)}, bf16[2048,1024]{1,0:T(8,128)(2,1)S(1)}) custom-call(s32[2]{0:T(128)S(1)} %pad_add_fusion.where_ref.rest_0_, f32[1,8192]{1,0:T(1,128)S(1)} %get-tuple-element.50.noise_ref.rest_0_.rest_1_, bf16[64,4224]{1,0:T(8,128)(2,1)S(1)} %get-tuple-element.51.tmpl_ref, bf16[1024,8192]{1,0:T(8,128)(2,1)} %far_ref.5, ...), custom_call_target="tpu_custom_call" | custom-call | flops 2147483648 | bytes 8388608 | tf_op jit(solution)/shard_map/pallas_call | solution.py:267
  23.7 2.1 %collective-permute-start.11 = (bf16[64,4096]{1,0:T(8,128)(2,1)S(1)}, bf16[64,4096]{1,0:T(8,128)(2,1)S(1)}, u32[]{:S(2)}, u32[]{:S(2)}) collective-permute-start(bf16[64,4096]{1,0:T(8,128)(2,1)S(1)} %collective-permute-done.6.rest_3_), channel_id=1, source_target_pairs={{0,4},{4,8},{8,12},{12,14},{14,10},{10,6},{6,2},{2,0},{5,1},{9,5},... | collective-permute-start | bytes 1572872 | tf_op jit(solution)/shard_map/ppermute | solution.py:534
  25.7 1.5 %shard_map.81 = (f32[128,1024]{1,0:T(8,128)S(1)}, f32[128,128]{1,0:T(8,128)S(1)}) custom-call(f32[1,8192]{1,0:T(1,128)S(1)} %get-tuple-element.50.noise_ref.rest_0_.rest_1_, bf16[2048,1024]{1,0:T(8,128)(2,1)S(1)} %get-tuple-element.64.rest_1_.rest_2_, bf16[2048,1024]{1,0:T(8,128)(2,1)S(1)} %get-tuple-element.65.rest_2_.rest_3_, ...), custom_call_target="tpu_custom_call" | custom-call | flops 2147483648 | bytes 8388608 | tf_op jit(solution)/shard_map/pallas_call | solution.py:441
  27.2 2.2 %collective-permute-done.1.rest_4_ = bf16[64,4224]{1,0:T(8,128)(2,1)S(1)} collective-permute-done((bf16[64,4224]{1,0:T(8,128)(2,1)S(1)}, bf16[64,4224]{1,0:T(8,128)(2,1)S(1)}, u32[]{:S(2)}, u32[]{:S(2)}) %collective-permute-start.1) | collective-permute-done | bytes 540704 | tf_op jit(solution)/shard_map/ppermute | solution.py:534
  29.5 2.1 %collective-permute-start.4 = (bf16[64,4224]{1,0:T(8,128)(2,1)S(1)}, bf16[64,4224]{1,0:T(8,128)(2,1)S(1)}, u32[]{:S(2)}, u32[]{:S(2)}) collective-permute-start(bf16[64,4224]{1,0:T(8,128)(2,1)S(1)} %collective-permute-done.1.rest_4_), channel_id=1, source_target_pairs={{0,4},{4,8},{8,12},{12,14},{14,10},{10,6},{6,2},{2,0},{5,1},{9,5},... | collective-permute-start | bytes 1622024 | tf_op jit(solution)/shard_map/ppermute | solution.py:534
  31.5 2.4 %shard_map.83.rest_10_ = f32[16,1024]{1,0:T(8,128)S(1)} custom-call(s32[2]{0:T(128)S(1)} %pad_add_fusion.where_ref.rest_0_, f32[1,8192]{1,0:T(1,128)S(1)} %get-tuple-element.50.noise_ref.rest_0_.rest_1_, bf16[2048,1024]{1,0:T(8,128)(2,1)S(1)} %get-tuple-element.57.rest_2_, bf16[2048,1024]{1,0:T(8,128)(2,1)S(1)} %get-tuple-element.62.rest_3_, ...), custom_call_target="tpu_custom_call" | custom-call | flops 2147483648 | bytes 8388608 | tf_op jit(solution)/shard_map/pallas_call | solution.py:441
  35.8 1.5 %collective-permute-start.14 = (bf16[64,2048]{1,0:T(8,128)(2,1)S(1)}, bf16[64,2048]{1,0:T(8,128)(2,1)S(1)}, u32[]{:S(2)}, u32[]{:S(2)}) collective-permute-start(bf16[64,2048]{1,0:T(8,128)(2,1)S(1)} %constant_dynamic-slice_fusion.1), channel_id=1, source_target_pairs={{0,4},{4,8},{8,12},{12,14},{14,10},{10,6},{6,2},{2,0},{5,1},{9,5},... | collective-permute-start | bytes 786440 | tf_op jit(solution)/shard_map/ppermute | solution.py:534
  37.4 2.4 %shard_map.84.rest_10_ = f32[16,1024]{1,0:T(8,128)S(1)} custom-call(s32[2]{0:T(128)S(1)} %pad_add_fusion.where_ref.rest_0_, f32[1,8192]{1,0:T(1,128)S(1)} %get-tuple-element.50.noise_ref.rest_0_.rest_1_, bf16[2048,1024]{1,0:T(8,128)(2,1)S(1)} %get-tuple-element.57.rest_2_, bf16[2048,1024]{1,0:T(8,128)(2,1)S(1)} %get-tuple-element.62.rest_3_, ...), custom_call_target="tpu_custom_call" | custom-call | flops 2147483648 | bytes 8388608 | tf_op jit(solution)/shard_map/pallas_call | solution.py:441
  41.0 2.3 %collective-permute-start.9 = (bf16[64,2176]{1,0:T(8,128)(2,1)S(1)}, bf16[64,2176]{1,0:T(8,128)(2,1)S(1)}, u32[]{:S(2)}, u32[]{:S(2)}) collective-permute-start(bf16[64,2176]{1,0:T(8,128)(2,1)S(1)} %constant_dynamic-slice_fusion.2), channel_id=1, source_target_pairs={{0,4},{4,8},{8,12},{12,14},{14,10},{10,6},{6,2},{2,0},{5,1},{9,5},... | collective-permute-start | bytes 835592 | tf_op jit(solution)/shard_map/ppermute | solution.py:534
  45.0 2.4 %shard_map.86.rest_10_ = f32[16,1024]{1,0:T(8,128)S(1)} custom-call(s32[2]{0:T(128)S(1)} %pad_add_fusion.where_ref.rest_0_, f32[1,8192]{1,0:T(1,128)S(1)} %get-tuple-element.50.noise_ref.rest_0_.rest_1_, bf16[2048,1024]{1,0:T(8,128)(2,1)S(1)} %get-tuple-element.57.rest_2_, bf16[2048,1024]{1,0:T(8,128)(2,1)S(1)} %get-tuple-element.62.rest_3_, ...), custom_call_target="tpu_custom_call" | custom-call | flops 2147483648 | bytes 8388608 | tf_op jit(solution)/shard_map/pallas_call | solution.py:441
  47.9 2.2 %shard_map.87 = (f32[64,1024]{1,0:T(8,128)S(1)}, f32[64,128]{1,0:T(8,128)S(1)}) custom-call(s32[2]{0:T(128)S(1)} %pad_add_fusion.where_ref.rest_0_, f32[1,8192]{1,0:T(1,128)S(1)} %get-tuple-element.50.noise_ref.rest_0_.rest_1_, bf16[2048,1024]{1,0:T(8,128)(2,1)S(1)} %get-tuple-element.64.rest_1_.rest_2_, ...), custom_call_target="tpu_custom_call" | custom-call | flops 2147483648 | bytes 8388608 | tf_op jit(solution)/shard_map/pallas_call | solution.py:441
  50.0 3.6 %shard_map.88 = (f32[1,1024]{1,0:T(1,128)}, f32[4,4,1152]{2,1,0:T(4,128)S(1)}, f32[4,4,1152]{2,1,0:T(4,128)S(1)}, bf16[8,1024]{1,0:T(8,128)(2,1)S(1)}, f32[8,128]{1,0:T(8,128)S(1)}) custom-call(s32[2]{0:T(128)S(1)} %pad_add_fusion.where_ref.rest_0_, f32[1,8192]{1,0:T(1,128)S(1)} %get-tuple-element.50.noise_ref.rest_0_.rest_1_, ...), custom_call_target="tpu_custom_call" | custom-call | flops 2147483648 | bytes 8388608 | tf_op jit(solution)/shard_map/pallas_call | solution.py:441
  55.1 2.1 %collective-permute-start.17 = (f32[4,4,1152]{2,1,0:T(4,128)S(1)}, f32[4,4,1152]{2,1,0:T(4,128)S(1)}, u32[]{:S(2)}, u32[]{:S(2)}) collective-permute-start(f32[4,4,1152]{2,1,0:T(4,128)S(1)} %add.15), channel_id=1, source_target_pairs={{0,2},{2,0},{4,6},{6,4},{8,10},{10,8},{12,14},{14,12},{1,3},{3,1},... | collective-permute-start | bytes 221192 | tf_op jit(solution)/shard_map/ppermute | solution.py:553
  57.2 1.7 %shard_map.89 = (f32[4,4,1152]{2,1,0:T(4,128)S(1)}, f32[4,4,1152]{2,1,0:T(4,128)S(1)}) custom-call(s32[2]{0:T(128)S(1)} %pad_add_fusion.where_ref.rest_0_, bf16[8,1024]{1,0:T(8,128)(2,1)S(1)} %get-tuple-element.87.rounded_ref, f32[8,128]{1,0:T(8,128)S(1)} %get-tuple-element.88.totals_ref, bf16[8,1024,512]{2,1,0:T(8,128)(2,1)S(1)} %get-tuple-element.83.rest_12_.rest_0_, ...), custom_call_target="tpu_custom_call" | custom-call | flops 1073741824 | bytes 4194304 | tf_op jit(solution)/shard_map/pallas_call | solution.py:329
  60.2 1.7 %collective-permute-start.19 = (f32[2,4,1152]{2,1,0:T(4,128)S(1)}, f32[2,4,1152]{2,1,0:T(4,128)S(1)}, u32[]{:S(2)}, u32[]{:S(2)}) collective-permute-start(f32[2,4,1152]{2,1,0:T(4,128)S(1)} %dynamic-slice_bitcast_fusion), channel_id=1, source_target_pairs={{0,4},{2,6},{4,0},{6,2},{8,12},{10,14},{12,8},{14,10},{1,5},{3,7},... | collective-permute-start | bytes 110600 | tf_op jit(solution)/shard_map/ppermute | solution.py:473
  61.9 2.4 %collective-permute-done.19 = f32[2,4,1152]{2,1,0:T(4,128)S(1)} collective-permute-done((f32[2,4,1152]{2,1,0:T(4,128)S(1)}, f32[2,4,1152]{2,1,0:T(4,128)S(1)}, u32[]{:S(2)}, u32[]{:S(2)}) %collective-permute-start.19) | collective-permute-done | bytes 36896 | tf_op jit(solution)/shard_map/ppermute | solution.py:473
  64.3 2.7 %collective-permute-start.20 = (f32[1,4,1152]{2,1,0:T(4,128)S(1)}, f32[1,4,1152]{2,1,0:T(4,128)S(1)}, u32[]{:S(2)}, u32[]{:S(2)}) collective-permute-start(f32[1,4,1152]{2,1,0:T(4,128)S(1)} %constant_dynamic-slice_fusion), channel_id=1, source_target_pairs={{0,8},{2,10},{4,12},{6,14},{8,0},{10,2},{12,4},{14,6},{1,9},{3,11}... | collective-permute-start | bytes 55304 | tf_op jit(solution)/shard_map/ppermute | solution.py:473
  67.0 2.0 %collective-permute-done.20 = f32[1,4,1152]{2,1,0:T(4,128)S(1)} collective-permute-done((f32[1,4,1152]{2,1,0:T(4,128)S(1)}, f32[1,4,1152]{2,1,0:T(4,128)S(1)}, u32[]{:S(2)}, u32[]{:S(2)}) %collective-permute-start.20) | collective-permute-done | bytes 18464 | tf_op jit(solution)/shard_map/ppermute | solution.py:473
  (48 shorter events, 11.3 us)
Async XLA Ops:
  2.1 11.0 %collective-permute-start.2 = (bf16[64,4096]{1,0:T(8,128)(2,1)S(1)}, bf16[64,4096]{1,0:T(8,128)(2,1)S(1)}, u32[]{:S(2)}, u32[]{:S(2)}) collective-permute-start(bf16[64,4096]{1,0:T(8,128)(2,1)S(1)} %get-tuple-element.52.tmpl_ref), channel_id=1, source_target_pairs={{0,4},{4,8},{8,12},{12,14},{14,10},{10,6},{6,2},{2,0},{5,1},{9,5},... | collective-permute-start | bytes 1572872 | tf_op jit(solution)/shard_map/ppermute | solution.py:534
  5.1 12.9 %collective-permute-start = (bf16[64,4224]{1,0:T(8,128)(2,1)S(1)}, bf16[64,4224]{1,0:T(8,128)(2,1)S(1)}, u32[]{:S(2)}, u32[]{:S(2)}) collective-permute-start(bf16[64,4224]{1,0:T(8,128)(2,1)S(1)} %get-tuple-element.51.tmpl_ref), channel_id=1, source_target_pairs={{0,4},{4,8},{8,12},{12,14},{14,10},{10,6},{6,2},{2,0},{5,1},{9,5},... | collective-permute-start | bytes 1622024 | tf_op jit(solution)/shard_map/ppermute | solution.py:534
  13.0 10.6 %collective-permute-start.6 = (bf16[64,4096]{1,0:T(8,128)(2,1)S(1)}, bf16[64,4096]{1,0:T(8,128)(2,1)S(1)}, u32[]{:S(2)}, u32[]{:S(2)}) collective-permute-start(bf16[64,4096]{1,0:T(8,128)(2,1)S(1)} %collective-permute-done.2.rest_3_), channel_id=1, source_target_pairs={{0,4},{4,8},{8,12},{12,14},{14,10},{10,6},{6,2},{2,0},{5,1},{9,5},... | collective-permute-start | bytes 1572872 | tf_op jit(solution)/shard_map/ppermute | solution.py:534
  14.7 5.5 %copy-start.1 = (s32[8]{0:T(128)S(1)}, s32[8]{0:T(128)}, u32[]{:S(2)}) copy-start(s32[8]{0:T(128)} %rest_11_.1) | copy-start | bytes 100
  14.7 5.5 %copy-start = (s32[64]{0:T(128)S(1)}, s32[64]{0:T(128)}, u32[]{:S(2)}) copy-start(s32[64]{0:T(128)} %param.9) | copy-start | bytes 772
  17.5 8.2 %collective-permute-start.3 = (bf16[64,4096]{1,0:T(8,128)(2,1)S(1)}, bf16[64,4096]{1,0:T(8,128)(2,1)S(1)}, u32[]{:S(2)}, u32[]{:S(2)}) collective-permute-start(bf16[64,4096]{1,0:T(8,128)(2,1)S(1)} %collective-permute-done.2.rest_3_), channel_id=1, source_target_pairs={{0,1},{1,0},{2,3},{3,2},{4,5},{5,4},{6,7},{7,6},{8,9},{9,8},{10,11... | collective-permute-start | bytes 1572872 | tf_op jit(solution)/shard_map/ppermute | solution.py:538
  18.0 13.5 %collective-permute-start.8 = (bf16[64,4224]{1,0:T(8,128)(2,1)S(1)}, bf16[64,4224]{1,0:T(8,128)(2,1)S(1)}, u32[]{:S(2)}, u32[]{:S(2)}) collective-permute-start(bf16[64,4224]{1,0:T(8,128)(2,1)S(1)} %collective-permute-done.rest_4_), channel_id=1, source_target_pairs={{0,1},{1,0},{2,3},{3,2},{4,5},{5,4},{6,7},{7,6},{8,9},{9,8},{10,11... | collective-permute-start | bytes 1622024 | tf_op jit(solution)/shard_map/ppermute | solution.py:538
  18.1 11.3 %collective-permute-start.1 = (bf16[64,4224]{1,0:T(8,128)(2,1)S(1)}, bf16[64,4224]{1,0:T(8,128)(2,1)S(1)}, u32[]{:S(2)}, u32[]{:S(2)}) collective-permute-start(bf16[64,4224]{1,0:T(8,128)(2,1)S(1)} %collective-permute-done.rest_4_), channel_id=1, source_target_pairs={{0,4},{4,8},{8,12},{12,14},{14,10},{10,6},{6,2},{2,0},{5,1},{9,5},... | collective-permute-start | bytes 1622024 | tf_op jit(solution)/shard_map/ppermute | solution.py:534
  23.7 10.3 %collective-permute-start.7 = (bf16[64,4096]{1,0:T(8,128)(2,1)S(1)}, bf16[64,4096]{1,0:T(8,128)(2,1)S(1)}, u32[]{:S(2)}, u32[]{:S(2)}) collective-permute-start(bf16[64,4096]{1,0:T(8,128)(2,1)S(1)} %collective-permute-done.6.rest_3_), channel_id=1, source_target_pairs={{0,1},{1,0},{2,3},{3,2},{4,5},{5,4},{6,7},{7,6},{8,9},{9,8},{10,11... | collective-permute-start | bytes 1572872 | tf_op jit(solution)/shard_map/ppermute | solution.py:538
  23.7 11.8 %collective-permute-start.11 = (bf16[64,4096]{1,0:T(8,128)(2,1)S(1)}, bf16[64,4096]{1,0:T(8,128)(2,1)S(1)}, u32[]{:S(2)}, u32[]{:S(2)}) collective-permute-start(bf16[64,4096]{1,0:T(8,128)(2,1)S(1)} %collective-permute-done.6.rest_3_), channel_id=1, source_target_pairs={{0,4},{4,8},{8,12},{12,14},{14,10},{10,6},{6,2},{2,0},{5,1},{9,5},... | collective-permute-start | bytes 1572872 | tf_op jit(solution)/shard_map/ppermute | solution.py:534
  29.5 7.9 %collective-permute-start.5 = (bf16[64,4224]{1,0:T(8,128)(2,1)S(1)}, bf16[64,4224]{1,0:T(8,128)(2,1)S(1)}, u32[]{:S(2)}, u32[]{:S(2)}) collective-permute-start(bf16[64,4224]{1,0:T(8,128)(2,1)S(1)} %collective-permute-done.1.rest_4_), channel_id=1, source_target_pairs={{0,1},{1,0},{2,3},{3,2},{4,5},{5,4},{6,7},{7,6},{8,9},{9,8},{10,11... | collective-permute-start | bytes 1622024 | tf_op jit(solution)/shard_map/ppermute | solution.py:538
  29.5 11.4 %collective-permute-start.4 = (bf16[64,4224]{1,0:T(8,128)(2,1)S(1)}, bf16[64,4224]{1,0:T(8,128)(2,1)S(1)}, u32[]{:S(2)}, u32[]{:S(2)}) collective-permute-start(bf16[64,4224]{1,0:T(8,128)(2,1)S(1)} %collective-permute-done.1.rest_4_), channel_id=1, source_target_pairs={{0,4},{4,8},{8,12},{12,14},{14,10},{10,6},{6,2},{2,0},{5,1},{9,5},... | collective-permute-start | bytes 1622024 | tf_op jit(solution)/shard_map/ppermute | solution.py:534
  35.4 7.9 %collective-permute-start.12 = (bf16[64,4096]{1,0:T(8,128)(2,1)S(1)}, bf16[64,4096]{1,0:T(8,128)(2,1)S(1)}, u32[]{:S(2)}, u32[]{:S(2)}) collective-permute-start(bf16[64,4096]{1,0:T(8,128)(2,1)S(1)} %collective-permute-done.11.rest_3_), channel_id=1, source_target_pairs={{0,1},{1,0},{2,3},{3,2},{4,5},{5,4},{6,7},{7,6},{8,9},{9,8},{10,11... | collective-permute-start | bytes 1572872 | tf_op jit(solution)/shard_map/ppermute | solution.py:538
  35.8 9.0 %collective-permute-start.14 = (bf16[64,2048]{1,0:T(8,128)(2,1)S(1)}, bf16[64,2048]{1,0:T(8,128)(2,1)S(1)}, u32[]{:S(2)}, u32[]{:S(2)}) collective-permute-start(bf16[64,2048]{1,0:T(8,128)(2,1)S(1)} %constant_dynamic-slice_fusion.1), channel_id=1, source_target_pairs={{0,4},{4,8},{8,12},{12,14},{14,10},{10,6},{6,2},{2,0},{5,1},{9,5},... | collective-permute-start | bytes 786440 | tf_op jit(solution)/shard_map/ppermute | solution.py:534
  40.9 4.2 %collective-permute-start.10 = (bf16[64,4224]{1,0:T(8,128)(2,1)S(1)}, bf16[64,4224]{1,0:T(8,128)(2,1)S(1)}, u32[]{:S(2)}, u32[]{:S(2)}) collective-permute-start(bf16[64,4224]{1,0:T(8,128)(2,1)S(1)} %collective-permute-done.4.rest_4_), channel_id=1, source_target_pairs={{0,1},{1,0},{2,3},{3,2},{4,5},{5,4},{6,7},{7,6},{8,9},{9,8},{10,11... | collective-permute-start | bytes 1622024 | tf_op jit(solution)/shard_map/ppermute | solution.py:538
  41.0 6.8 %collective-permute-start.9 = (bf16[64,2176]{1,0:T(8,128)(2,1)S(1)}, bf16[64,2176]{1,0:T(8,128)(2,1)S(1)}, u32[]{:S(2)}, u32[]{:S(2)}) collective-permute-start(bf16[64,2176]{1,0:T(8,128)(2,1)S(1)} %constant_dynamic-slice_fusion.2), channel_id=1, source_target_pairs={{0,4},{4,8},{8,12},{12,14},{14,10},{10,6},{6,2},{2,0},{5,1},{9,5},... | collective-permute-start | bytes 835592 | tf_op jit(solution)/shard_map/ppermute | solution.py:534
  44.8 3.1 %collective-permute-start.15 = (bf16[64,2048]{1,0:T(8,128)(2,1)S(1)}, bf16[64,2048]{1,0:T(8,128)(2,1)S(1)}, u32[]{:S(2)}, u32[]{:S(2)}) collective-permute-start(bf16[64,2048]{1,0:T(8,128)(2,1)S(1)} %collective-permute-done.14.rest_4_), channel_id=1, source_target_pairs={{0,1},{1,0},{2,3},{3,2},{4,5},{5,4},{6,7},{7,6},{8,9},{9,8},{10,11... | collective-permute-start | bytes 786440 | tf_op jit(solution)/shard_map/ppermute | solution.py:538
  47.8 2.2 %collective-permute-start.13 = (bf16[64,2176]{1,0:T(8,128)(2,1)S(1)}, bf16[64,2176]{1,0:T(8,128)(2,1)S(1)}, u32[]{:S(2)}, u32[]{:S(2)}) collective-permute-start(bf16[64,2176]{1,0:T(8,128)(2,1)S(1)} %collective-permute-done.9.rest_4_), channel_id=1, source_target_pairs={{0,1},{1,0},{2,3},{3,2},{4,5},{5,4},{6,7},{7,6},{8,9},{9,8},{10,11... | collective-permute-start | bytes 835592 | tf_op jit(solution)/shard_map/ppermute | solution.py:538
  53.7 1.4 %collective-permute-start.16 = (f32[4,4,1152]{2,1,0:T(4,128)S(1)}, f32[4,4,1152]{2,1,0:T(4,128)S(1)}, u32[]{:S(2)}, u32[]{:S(2)}) collective-permute-start(f32[4,4,1152]{2,1,0:T(4,128)S(1)} %get-tuple-element.86), channel_id=1, source_target_pairs={{0,1},{1,0},{2,3},{3,2},{4,5},{5,4},{6,7},{7,6},{8,9},{9,8},{10,11... | collective-permute-start | bytes 221192 | tf_op jit(solution)/shard_map/ppermute | solution.py:552
  55.1 4.9 %collective-permute-start.17 = (f32[4,4,1152]{2,1,0:T(4,128)S(1)}, f32[4,4,1152]{2,1,0:T(4,128)S(1)}, u32[]{:S(2)}, u32[]{:S(2)}) collective-permute-start(f32[4,4,1152]{2,1,0:T(4,128)S(1)} %add.15), channel_id=1, source_target_pairs={{0,2},{2,0},{4,6},{6,4},{8,10},{10,8},{12,14},{14,12},{1,3},{3,1},... | collective-permute-start | bytes 221192 | tf_op jit(solution)/shard_map/ppermute | solution.py:553
  58.9 1.3 %collective-permute-start.18 = (f32[4,4,1152]{2,1,0:T(4,128)S(1)}, f32[4,4,1152]{2,1,0:T(4,128)S(1)}, u32[]{:S(2)}, u32[]{:S(2)}) collective-permute-start(f32[4,4,1152]{2,1,0:T(4,128)S(1)} %get-tuple-element.91), channel_id=1, source_target_pairs={{0,1},{1,0},{2,3},{3,2},{4,5},{5,4},{6,7},{7,6},{8,9},{9,8},{10,11... | collective-permute-start | bytes 221192 | tf_op jit(solution)/shard_map/ppermute | solution.py:557
  60.2 4.0 %collective-permute-start.19 = (f32[2,4,1152]{2,1,0:T(4,128)S(1)}, f32[2,4,1152]{2,1,0:T(4,128)S(1)}, u32[]{:S(2)}, u32[]{:S(2)}) collective-permute-start(f32[2,4,1152]{2,1,0:T(4,128)S(1)} %dynamic-slice_bitcast_fusion), channel_id=1, source_target_pairs={{0,4},{2,6},{4,0},{6,2},{8,12},{10,14},{12,8},{14,10},{1,5},{3,7},... | collective-permute-start | bytes 110600 | tf_op jit(solution)/shard_map/ppermute | solution.py:473
  64.3 4.7 %collective-permute-start.20 = (f32[1,4,1152]{2,1,0:T(4,128)S(1)}, f32[1,4,1152]{2,1,0:T(4,128)S(1)}, u32[]{:S(2)}, u32[]{:S(2)}) collective-permute-start(f32[1,4,1152]{2,1,0:T(4,128)S(1)} %constant_dynamic-slice_fusion), channel_id=1, source_target_pairs={{0,8},{2,10},{4,12},{6,14},{8,0},{10,2},{12,4},{14,6},{1,9},{3,11}... | collective-permute-start | bytes 55304 | tf_op jit(solution)/shard_map/ppermute | solution.py:473

commit v21 on v20

--- a/solution.py
+++ b/solution.py
@@ -125,13 +125,13 @@
 
 
 def add_rows(tags, hit, logs_ref, state, acc, energy):
-    classes = logs_ref.shape[0]
-    prior = jnp.zeros_like(tags[:, :1])
-    for tag in range(classes):
-        prior = jnp.where(tags[:, :1] == tag, logs_ref[tag], prior)
+    lane = lax.broadcasted_iota(jnp.int32, tags.shape, 1).astype(jnp.float32)
+    own_lane = tags == lane
+    prior = jnp.sum(jnp.where(own_lane, logs_ref[...], 0.0), axis=1, keepdims=True)
     bias = prior - 0.5 * jnp.sum(energy[...], axis=1, keepdims=True)
     scores = acc[...] + bias
     old_max, old_sum, old_top, weights = state
+    classes = weights.shape[0]
     new_max = jnp.maximum(old_max, jnp.max(scores, axis=0, keepdims=True))
     new_sum = old_sum * jnp.exp(old_max - new_max) + jnp.sum(
         jnp.exp(scores - new_max), axis=0, keepdims=True
@@ -140,8 +140,7 @@
         old_top, jnp.max(jnp.where(hit, scores, LOWEST), axis=0, keepdims=True)
     )
     value = jnp.where(hit, jnp.exp(scores - new_top), 0.0)
-    lane = lax.broadcasted_iota(jnp.int32, tags.shape, 1).astype(jnp.float32)
-    onehot = jnp.transpose(jnp.where(tags == lane, 1.0, 0.0))[:classes, :].astype(jnp.bfloat16)
+    onehot = jnp.transpose(jnp.where(own_lane, 1.0, 0.0))[:classes, :].astype(jnp.bfloat16)
     weights = weights * jnp.exp(old_top - new_top)
     left = value
     for _ in range(3):
@@ -227,12 +226,12 @@
     hit = picked_rows(words_ref, where_ref[0], height)
     lowest = jnp.full((1, acc.shape[1]), LOWEST, jnp.float32)
     none = jnp.zeros((1, acc.shape[1]), jnp.float32)
-    weights = jnp.zeros((logs_ref.shape[0], acc.shape[1]), jnp.float32)
+    weights = jnp.zeros((out_ref.shape[0] - STATE_ROWS, acc.shape[1]), jnp.float32)
     state = (lowest, none, lowest, weights)
     put_state(add_rows(tags, hit, logs_ref, state, acc, energy), out_ref)
 
 
-def own_scores(quarters, where, noise, particles, templates, rest, total=0):
+def own_scores(quarters, where, noise, particles, templates, rest, total=0, classes=0):
     per_device, freqs = particles.shape
     height = templates.shape[0]
     width = freqs // STEPS
@@ -254,9 +253,9 @@
             pltpu.SemaphoreType.DMA((steps, 4)),
         ]
     elif last:
-        rows = STATE_ROWS + rest[2].shape[0]
+        rows = STATE_ROWS + classes
         shapes = [jax.ShapeDtypeStruct((rows, per_device), jnp.float32)] + turned
-        rest_specs = [in_vmem(), in_vmem(), in_smem(), in_vmem(), in_vmem(), in_vmem()]
+        rest_specs = [in_vmem()] * 6
         scratch = [pltpu.VMEM(array.shape, array.dtype) for array in sums]
     else:
         shapes = sums + turned + [raw]
@@ -283,11 +282,10 @@
     _, _, _, weights = state
     classes = weights.shape[0]
     row = lax.broadcasted_iota(jnp.int32, (classes, LANES), 0)
-    counts = jnp.zeros((classes, LANES), jnp.float32)
-    for tag in range(classes):
-        mine = (where_ref[0] == 0) & (where_ref[1] == tag // per_owner)
-        count = jnp.where(mine, counts_ref[tag], 0).astype(jnp.float32)
-        counts = jnp.where(row == tag, count, counts)
+    lane = lax.broadcasted_iota(jnp.int32, (classes, LANES), 1)
+    mine = (lax.div(row, per_owner) == where_ref[1]) & (where_ref[0] == 0)
+    counts = jnp.where(mine & (row == lane), counts_ref[...], 0.0)
+    counts = jnp.broadcast_to(jnp.sum(counts, axis=1, keepdims=True), (classes, LANES))
     weights = weights / jnp.sum(weights, axis=0, keepdims=True)
     totals = jnp.sum(weights, axis=1, keepdims=True) + counts
 
@@ -423,9 +421,9 @@
     if phase == 0:
         shapes, scratch = sums, []
     else:
-        specs = [in_vmem(), in_vmem(), in_smem(), in_vmem(), in_vmem()]
+        specs = [in_vmem()] * 5
         if ends:
-            classes = rest[2].shape[0]
+            classes = rest[4].shape[0] - STATE_ROWS
             shapes = [
                 jax.ShapeDtypeStruct((1, per_device), jnp.float32),
                 piece,
@@ -434,7 +432,7 @@
                 jax.ShapeDtypeStruct((classes, LANES), jnp.float32),
             ]
             nears = [pltpu.with_memory_space_constraint(x, pltpu.VMEM) for x in rest[6:]]
-            specs += [in_smem()] + [in_vmem()] * len(nears)
+            specs += [in_vmem()] * (1 + len(nears))
             rest = (*rest[:6], *nears)
         else:
             shapes = [jax.ShapeDtypeStruct(rest[4].shape, jnp.float32)]
@@ -488,7 +486,9 @@
     swap = [(i, owners - 1 - i) for i in range(owners)]
 
     noise = inv_noise[None, :]
-    logs = jnp.log(class_counts.astype(jnp.float32))
+    counts = jnp.pad(class_counts.astype(jnp.float32), (0, LANES - classes), constant_values=1.0)
+    counts = counts[None, :]
+    logs = jnp.log(counts)
     tags = template_class[None, :]
     *held, near_noise, picks = make_messages(tags, noise, significant, templates)
     where = jnp.stack([block_id, core])
@@ -508,7 +508,7 @@
     *sums, low, raw = own([2], templates=held[1], rest=(*sums, raw))
     nears.append(raw)
     gates.append(sums)
-    state, high = own([3], templates=held[1], rest=(*sums, logs, tags, words, raw))
+    state, high = own([3], templates=held[1], rest=(*sums, logs, tags, words, raw), classes=classes)
     turned.append((low, high))
     gates.append(state)
     width = freqs // blocks
@@ -539,7 +539,7 @@
             arrived.append(own)
             rest = (*sums, logs, words, state) if phase else ()
             if ends and phase:
-                rest += (class_counts, *nears)
+                rest += (counts, *nears)
             sums = ring_scores(
                 phase, tables, where, near_noise, turned[phase], pair, rest, ends, piece
             )

time: 70 us -> 69.9 us (level)
  no operation moved by 1% of the time
where the time goes in v21:
time: 69.9 us; the launch traced here: 69.8 us
  Pallas kernels  32.7 us (47%)
  starting transfers between devices  23.9 us (34%)
  waiting for transfers between devices  11.2 us (16%)
  other arithmetic  0.85 us (1%)
  between operations  0.79 us (1%)
    pallas_call x8, Pallas kernels, ring_scores(): pl.pallas_call(functools.partial(ring_kernel, phase, ends, sources), in_s...  17.4 us
    ppermute x8, starting transfers between devices, body(): own = lax.ppermute(message, ('blk', 'cls'), ring)  16.3 us
    pallas_call x3, Pallas kernels, own_scores(): pl.pallas_call(functools.partial(own_kernel, quarters), in_specs=[in_smem...  12.1 us
    ppermute x8, waiting for transfers between devices, body(): own = lax.ppermute(message, ('blk', 'cls'), ring)  4.66 us
    ppermute x2, waiting for transfers between devices, scatter_sum(): pieces = keep + lax.ppermute(send, 'blk', swaps)  4.39 us
    ppermute x2, starting transfers between devices, scatter_sum(): pieces = keep + lax.ppermute(send, 'blk', swaps)  4.36 us
    ppermute x1, starting transfers between devices, body(): lax.ppermute(mine + given, 'blk', [(i, i ^ 1) for i in range(blocks)])  2.08 us
    pallas_call x1, Pallas kernels, rest_sums(): pl.pallas_call(rest_kernel, in_specs=[in_smem()] + [in_vmem()] * (2 + len...  1.74 us
  transfers between devices with their start and end apart: 21, of which 10 were waited for; matrix products, arithmetic and copies ran while one was open for 1% of the time, Pallas kernels for 40%

profile of v21, /device:TPU:0, one launch (start us, length us, event | category | flops | bytes accessed | tf_op | source)
XLA Modules:
  0.0 69.8 jit_solution(4773152885301682163)
XLA Ops:
  2.1 3.1 %collective-permute-start.2 = (bf16[64,4096]{1,0:T(8,128)(2,1)S(1)}, bf16[64,4096]{1,0:T(8,128)(2,1)S(1)}, u32[]{:S(2)}, u32[]{:S(2)}) collective-permute-start(bf16[64,4096]{1,0:T(8,128)(2,1)S(1)} %get-tuple-element.52.tmpl_ref), channel_id=1, source_target_pairs={{0,4},{4,8},{8,12},{12,14},{14,10},{10,6},{6,2},{2,0},{5,1},{9,5},... | collective-permute-start | bytes 1572872 | tf_op jit(solution)/shard_map/ppermute | solution.py:534
  5.1 1.6 %collective-permute-start = (bf16[64,4224]{1,0:T(8,128)(2,1)S(1)}, bf16[64,4224]{1,0:T(8,128)(2,1)S(1)}, u32[]{:S(2)}, u32[]{:S(2)}) collective-permute-start(bf16[64,4224]{1,0:T(8,128)(2,1)S(1)} %get-tuple-element.51.tmpl_ref), channel_id=1, source_target_pairs={{0,4},{4,8},{8,12},{12,14},{14,10},{10,6},{6,2},{2,0},{5,1},{9,5},... | collective-permute-start | bytes 1622024 | tf_op jit(solution)/shard_map/ppermute | solution.py:534
  6.8 6.2 %shard_map.78 = (s32[16,1024]{1,0:T(8,128)S(1)}, f32[64,1024]{1,0:T(8,128)S(1)}, f32[64,128]{1,0:T(8,128)S(1)}, bf16[2048,1024]{1,0:T(8,128)(2,1)S(1)}, bf16[204...) custom-call(s32[2]{0:T(128)S(1)} %pad_add_fusion.where_ref.rest_0_, ...), custom_call_target="tpu_custom_call" | custom-call | flops 2147483648 | bytes 8388608 | tf_op jit(solution)/shard_map/pallas_call | solution.py:266
  13.0 1.6 %collective-permute-start.6 = (bf16[64,4096]{1,0:T(8,128)(2,1)S(1)}, bf16[64,4096]{1,0:T(8,128)(2,1)S(1)}, u32[]{:S(2)}, u32[]{:S(2)}) collective-permute-start(bf16[64,4096]{1,0:T(8,128)(2,1)S(1)} %collective-permute-done.2.rest_3_), channel_id=1, source_target_pairs={{0,4},{4,8},{8,12},{12,14},{14,10},{10,6},{6,2},{2,0},{5,1},{9,5},... | collective-permute-start | bytes 1572872 | tf_op jit(solution)/shard_map/ppermute | solution.py:534
  14.7 2.8 %shard_map.79 = (f32[64,1024]{1,0:T(8,128)S(1)}, f32[64,128]{1,0:T(8,128)S(1)}, bf16[2048,1024]{1,0:T(8,128)(2,1)S(1)}, bf16[4,1024,512]{2,1,0:T(8,128)(2,1)S(1)}) custom-call(s32[2]{0:T(128)S(1)} %pad_add_fusion.where_ref.rest_0_, f32[1,8192]{1,0:T(1,128)S(1)} %get-tuple-element.50.noise_ref.rest_0_.rest_1_, ...), custom_call_target="tpu_custom_call" | custom-call | flops 2147483648 | bytes 8388608 | tf_op jit(solution)/shard_map/pallas_call | solution.py:266
  18.1 2.0 %collective-permute-start.1 = (bf16[64,4224]{1,0:T(8,128)(2,1)S(1)}, bf16[64,4224]{1,0:T(8,128)(2,1)S(1)}, u32[]{:S(2)}, u32[]{:S(2)}) collective-permute-start(bf16[64,4224]{1,0:T(8,128)(2,1)S(1)} %collective-permute-done.rest_4_), channel_id=1, source_target_pairs={{0,4},{4,8},{8,12},{12,14},{14,10},{10,6},{6,2},{2,0},{5,1},{9,5},... | collective-permute-start | bytes 1622024 | tf_op jit(solution)/shard_map/ppermute | solution.py:534
  20.1 3.0 %shard_map.80 = (f32[16,1024]{1,0:T(8,128)S(1)}, bf16[2048,1024]{1,0:T(8,128)(2,1)S(1)}) custom-call(s32[2]{0:T(128)S(1)} %pad_add_fusion.where_ref.rest_0_, f32[1,8192]{1,0:T(1,128)S(1)} %get-tuple-element.50.noise_ref.rest_0_.rest_1_, bf16[64,4224]{1,0:T(8,128)(2,1)S(1)} %get-tuple-element.51.tmpl_ref, bf16[1024,8192]{1,0:T(8,128)(2,1)} %far_ref.5, ...), custom_call_target="tpu_custom_call" | custom-call | flops 2147483648 | bytes 8388608 | tf_op jit(solution)/shard_map/pallas_call | solution.py:266
  23.7 2.1 %collective-permute-start.11 = (bf16[64,4096]{1,0:T(8,128)(2,1)S(1)}, bf16[64,4096]{1,0:T(8,128)(2,1)S(1)}, u32[]{:S(2)}, u32[]{:S(2)}) collective-permute-start(bf16[64,4096]{1,0:T(8,128)(2,1)S(1)} %collective-permute-done.6.rest_3_), channel_id=1, source_target_pairs={{0,4},{4,8},{8,12},{12,14},{14,10},{10,6},{6,2},{2,0},{5,1},{9,5},... | collective-permute-start | bytes 1572872 | tf_op jit(solution)/shard_map/ppermute | solution.py:534
  27.2 2.2 %collective-permute-done.1.rest_4_ = bf16[64,4224]{1,0:T(8,128)(2,1)S(1)} collective-permute-done((bf16[64,4224]{1,0:T(8,128)(2,1)S(1)}, bf16[64,4224]{1,0:T(8,128)(2,1)S(1)}, u32[]{:S(2)}, u32[]{:S(2)}) %collective-permute-start.1) | collective-permute-done | bytes 540704 | tf_op jit(solution)/shard_map/ppermute | solution.py:534
  29.5 2.1 %collective-permute-start.4 = (bf16[64,4224]{1,0:T(8,128)(2,1)S(1)}, bf16[64,4224]{1,0:T(8,128)(2,1)S(1)}, u32[]{:S(2)}, u32[]{:S(2)}) collective-permute-start(bf16[64,4224]{1,0:T(8,128)(2,1)S(1)} %collective-permute-done.1.rest_4_), channel_id=1, source_target_pairs={{0,4},{4,8},{8,12},{12,14},{14,10},{10,6},{6,2},{2,0},{5,1},{9,5},... | collective-permute-start | bytes 1622024 | tf_op jit(solution)/shard_map/ppermute | solution.py:534
  31.5 2.4 %shard_map.83.rest_10_ = f32[16,1024]{1,0:T(8,128)S(1)} custom-call(s32[2]{0:T(128)S(1)} %pad_add_fusion.where_ref.rest_0_, f32[1,8192]{1,0:T(1,128)S(1)} %get-tuple-element.50.noise_ref.rest_0_.rest_1_, bf16[2048,1024]{1,0:T(8,128)(2,1)S(1)} %get-tuple-element.57.rest_2_, bf16[2048,1024]{1,0:T(8,128)(2,1)S(1)} %get-tuple-element.62.rest_3_, ...), custom_call_target="tpu_custom_call" | custom-call | flops 2147483648 | bytes 8388608 | tf_op jit(solution)/shard_map/pallas_call | solution.py:439
  34.0 1.5 %shard_map.82 = (f32[128,1024]{1,0:T(8,128)S(1)}, f32[128,128]{1,0:T(8,128)S(1)}) custom-call(f32[1,8192]{1,0:T(1,128)S(1)} %get-tuple-element.50.noise_ref.rest_0_.rest_1_, bf16[2048,1024]{1,0:T(8,128)(2,1)S(1)} %get-tuple-element.64.rest_1_.rest_2_, bf16[2048,1024]{1,0:T(8,128)(2,1)S(1)} %get-tuple-element.65.rest_2_.rest_3_, ...), custom_call_target="tpu_custom_call" | custom-call | flops 2147483648 | bytes 8388608 | tf_op jit(solution)/shard_map/pallas_call | solution.py:439
  35.8 1.5 %collective-permute-start.14 = (bf16[64,2048]{1,0:T(8,128)(2,1)S(1)}, bf16[64,2048]{1,0:T(8,128)(2,1)S(1)}, u32[]{:S(2)}, u32[]{:S(2)}) collective-permute-start(bf16[64,2048]{1,0:T(8,128)(2,1)S(1)} %constant_dynamic-slice_fusion.1), channel_id=1, source_target_pairs={{0,4},{4,8},{8,12},{12,14},{14,10},{10,6},{6,2},{2,0},{5,1},{9,5},... | collective-permute-start | bytes 786440 | tf_op jit(solution)/shard_map/ppermute | solution.py:534
  37.4 2.4 %shard_map.84.rest_10_ = f32[16,1024]{1,0:T(8,128)S(1)} custom-call(s32[2]{0:T(128)S(1)} %pad_add_fusion.where_ref.rest_0_, f32[1,8192]{1,0:T(1,128)S(1)} %get-tuple-element.50.noise_ref.rest_0_.rest_1_, bf16[2048,1024]{1,0:T(8,128)(2,1)S(1)} %get-tuple-element.57.rest_2_, bf16[2048,1024]{1,0:T(8,128)(2,1)S(1)} %get-tuple-element.62.rest_3_, ...), custom_call_target="tpu_custom_call" | custom-call | flops 2147483648 | bytes 8388608 | tf_op jit(solution)/shard_map/pallas_call | solution.py:439
  41.0 2.3 %collective-permute-start.9 = (bf16[64,2176]{1,0:T(8,128)(2,1)S(1)}, bf16[64,2176]{1,0:T(8,128)(2,1)S(1)}, u32[]{:S(2)}, u32[]{:S(2)}) collective-permute-start(bf16[64,2176]{1,0:T(8,128)(2,1)S(1)} %constant_dynamic-slice_fusion.2), channel_id=1, source_target_pairs={{0,4},{4,8},{8,12},{12,14},{14,10},{10,6},{6,2},{2,0},{5,1},{9,5},... | collective-permute-start | bytes 835592 | tf_op jit(solution)/shard_map/ppermute | solution.py:534
  45.0 2.4 %shard_map.86.rest_10_ = f32[16,1024]{1,0:T(8,128)S(1)} custom-call(s32[2]{0:T(128)S(1)} %pad_add_fusion.where_ref.rest_0_, f32[1,8192]{1,0:T(1,128)S(1)} %get-tuple-element.50.noise_ref.rest_0_.rest_1_, bf16[2048,1024]{1,0:T(8,128)(2,1)S(1)} %get-tuple-element.57.rest_2_, bf16[2048,1024]{1,0:T(8,128)(2,1)S(1)} %get-tuple-element.62.rest_3_, ...), custom_call_target="tpu_custom_call" | custom-call | flops 2147483648 | bytes 8388608 | tf_op jit(solution)/shard_map/pallas_call | solution.py:439
  47.9 2.1 %shard_map.87 = (f32[64,1024]{1,0:T(8,128)S(1)}, f32[64,128]{1,0:T(8,128)S(1)}) custom-call(s32[2]{0:T(128)S(1)} %pad_add_fusion.where_ref.rest_0_, f32[1,8192]{1,0:T(1,128)S(1)} %get-tuple-element.50.noise_ref.rest_0_.rest_1_, bf16[2048,1024]{1,0:T(8,128)(2,1)S(1)} %get-tuple-element.64.rest_1_.rest_2_, ...), custom_call_target="tpu_custom_call" | custom-call | flops 2147483648 | bytes 8388608 | tf_op jit(solution)/shard_map/pallas_call | solution.py:439
  50.0 3.6 %shard_map.88 = (f32[1,1024]{1,0:T(1,128)}, f32[4,4,1152]{2,1,0:T(4,128)S(1)}, f32[4,4,1152]{2,1,0:T(4,128)S(1)}, bf16[8,1024]{1,0:T(8,128)(2,1)S(1)}, f32[8,128]{1,0:T(8,128)S(1)}) custom-call(s32[2]{0:T(128)S(1)} %pad_add_fusion.where_ref.rest_0_, f32[1,8192]{1,0:T(1,128)S(1)} %get-tuple-element.50.noise_ref.rest_0_.rest_1_, ...), custom_call_target="tpu_custom_call" | custom-call | flops 2147483648 | bytes 8388608 | tf_op jit(solution)/shard_map/pallas_call | solution.py:439
  55.0 2.1 %collective-permute-start.17 = (f32[4,4,1152]{2,1,0:T(4,128)S(1)}, f32[4,4,1152]{2,1,0:T(4,128)S(1)}, u32[]{:S(2)}, u32[]{:S(2)}) collective-permute-start(f32[4,4,1152]{2,1,0:T(4,128)S(1)} %add.17), channel_id=1, source_target_pairs={{0,2},{2,0},{4,6},{6,4},{8,10},{10,8},{12,14},{14,12},{1,3},{3,1},... | collective-permute-start | bytes 221192 | tf_op jit(solution)/shard_map/ppermute | solution.py:553
  57.1 1.7 %shard_map.89 = (f32[4,4,1152]{2,1,0:T(4,128)S(1)}, f32[4,4,1152]{2,1,0:T(4,128)S(1)}) custom-call(s32[2]{0:T(128)S(1)} %pad_add_fusion.where_ref.rest_0_, bf16[8,1024]{1,0:T(8,128)(2,1)S(1)} %get-tuple-element.87.rounded_ref, f32[8,128]{1,0:T(8,128)S(1)} %get-tuple-element.88.totals_ref, bf16[8,1024,512]{2,1,0:T(8,128)(2,1)S(1)} %get-tuple-element.83.rest_12_.rest_0_, ...), custom_call_target="tpu_custom_call" | custom-call | flops 1073741824 | bytes 4194304 | tf_op jit(solution)/shard_map/pallas_call | solution.py:327
  60.2 1.7 %collective-permute-start.19 = (f32[2,4,1152]{2,1,0:T(4,128)S(1)}, f32[2,4,1152]{2,1,0:T(4,128)S(1)}, u32[]{:S(2)}, u32[]{:S(2)}) collective-permute-start(f32[2,4,1152]{2,1,0:T(4,128)S(1)} %dynamic-slice_bitcast_fusion), channel_id=1, source_target_pairs={{0,4},{2,6},{4,0},{6,2},{8,12},{10,14},{12,8},{14,10},{1,5},{3,7},... | collective-permute-start | bytes 110600 | tf_op jit(solution)/shard_map/ppermute | solution.py:471
  61.9 2.4 %collective-permute-done.19 = f32[2,4,1152]{2,1,0:T(4,128)S(1)} collective-permute-done((f32[2,4,1152]{2,1,0:T(4,128)S(1)}, f32[2,4,1152]{2,1,0:T(4,128)S(1)}, u32[]{:S(2)}, u32[]{:S(2)}) %collective-permute-start.19) | collective-permute-done | bytes 36896 | tf_op jit(solution)/shard_map/ppermute | solution.py:471
  64.3 2.7 %collective-permute-start.20 = (f32[1,4,1152]{2,1,0:T(4,128)S(1)}, f32[1,4,1152]{2,1,0:T(4,128)S(1)}, u32[]{:S(2)}, u32[]{:S(2)}) collective-permute-start(f32[1,4,1152]{2,1,0:T(4,128)S(1)} %constant_dynamic-slice_fusion), channel_id=1, source_target_pairs={{0,8},{2,10},{4,12},{6,14},{8,0},{10,2},{12,4},{14,6},{1,9},{3,11}... | collective-permute-start | bytes 55304 | tf_op jit(solution)/shard_map/ppermute | solution.py:471
  66.9 2.0 %collective-permute-done.20 = f32[1,4,1152]{2,1,0:T(4,128)S(1)} collective-permute-done((f32[1,4,1152]{2,1,0:T(4,128)S(1)}, f32[1,4,1152]{2,1,0:T(4,128)S(1)}, u32[]{:S(2)}, u32[]{:S(2)}) %collective-permute-start.20) | collective-permute-done | bytes 18464 | tf_op jit(solution)/shard_map/ppermute | solution.py:471
  (49 shorter events, 11.3 us)
Async XLA Ops:
  2.1 11.0 %collective-permute-start.2 = (bf16[64,4096]{1,0:T(8,128)(2,1)S(1)}, bf16[64,4096]{1,0:T(8,128)(2,1)S(1)}, u32[]{:S(2)}, u32[]{:S(2)}) collective-permute-start(bf16[64,4096]{1,0:T(8,128)(2,1)S(1)} %get-tuple-element.52.tmpl_ref), channel_id=1, source_target_pairs={{0,4},{4,8},{8,12},{12,14},{14,10},{10,6},{6,2},{2,0},{5,1},{9,5},... | collective-permute-start | bytes 1572872 | tf_op jit(solution)/shard_map/ppermute | solution.py:534
  5.1 12.9 %collective-permute-start = (bf16[64,4224]{1,0:T(8,128)(2,1)S(1)}, bf16[64,4224]{1,0:T(8,128)(2,1)S(1)}, u32[]{:S(2)}, u32[]{:S(2)}) collective-permute-start(bf16[64,4224]{1,0:T(8,128)(2,1)S(1)} %get-tuple-element.51.tmpl_ref), channel_id=1, source_target_pairs={{0,4},{4,8},{8,12},{12,14},{14,10},{10,6},{6,2},{2,0},{5,1},{9,5},... | collective-permute-start | bytes 1622024 | tf_op jit(solution)/shard_map/ppermute | solution.py:534
  13.0 10.6 %collective-permute-start.6 = (bf16[64,4096]{1,0:T(8,128)(2,1)S(1)}, bf16[64,4096]{1,0:T(8,128)(2,1)S(1)}, u32[]{:S(2)}, u32[]{:S(2)}) collective-permute-start(bf16[64,4096]{1,0:T(8,128)(2,1)S(1)} %collective-permute-done.2.rest_3_), channel_id=1, source_target_pairs={{0,4},{4,8},{8,12},{12,14},{14,10},{10,6},{6,2},{2,0},{5,1},{9,5},... | collective-permute-start | bytes 1572872 | tf_op jit(solution)/shard_map/ppermute | solution.py:534
  14.7 11.1 %collective-permute-start.3 = (bf16[64,4096]{1,0:T(8,128)(2,1)S(1)}, bf16[64,4096]{1,0:T(8,128)(2,1)S(1)}, u32[]{:S(2)}, u32[]{:S(2)}) collective-permute-start(bf16[64,4096]{1,0:T(8,128)(2,1)S(1)} %collective-permute-done.2.rest_3_), channel_id=1, source_target_pairs={{0,1},{1,0},{2,3},{3,2},{4,5},{5,4},{6,7},{7,6},{8,9},{9,8},{10,11... | collective-permute-start | bytes 1572872 | tf_op jit(solution)/shard_map/ppermute | solution.py:538
  14.7 2.9 %copy-start.1 = (s32[8]{0:T(128)S(1)}, s32[8]{0:T(128)}, u32[]{:S(2)}) copy-start(s32[8]{0:T(128)} %param.10) | copy-start | bytes 100
  14.7 5.5 %copy-start = (s32[64]{0:T(128)S(1)}, s32[64]{0:T(128)}, u32[]{:S(2)}) copy-start(s32[64]{0:T(128)} %param.9) | copy-start | bytes 772
  18.0 13.5 %collective-permute-start.8 = (bf16[64,4224]{1,0:T(8,128)(2,1)S(1)}, bf16[64,4224]{1,0:T(8,128)(2,1)S(1)}, u32[]{:S(2)}, u32[]{:S(2)}) collective-permute-start(bf16[64,4224]{1,0:T(8,128)(2,1)S(1)} %collective-permute-done.rest_4_), channel_id=1, source_target_pairs={{0,1},{1,0},{2,3},{3,2},{4,5},{5,4},{6,7},{7,6},{8,9},{9,8},{10,11... | collective-permute-start | bytes 1622024 | tf_op jit(solution)/shard_map/ppermute | solution.py:538
  18.1 11.3 %collective-permute-start.1 = (bf16[64,4224]{1,0:T(8,128)(2,1)S(1)}, bf16[64,4224]{1,0:T(8,128)(2,1)S(1)}, u32[]{:S(2)}, u32[]{:S(2)}) collective-permute-start(bf16[64,4224]{1,0:T(8,128)(2,1)S(1)} %collective-permute-done.rest_4_), channel_id=1, source_target_pairs={{0,4},{4,8},{8,12},{12,14},{14,10},{10,6},{6,2},{2,0},{5,1},{9,5},... | collective-permute-start | bytes 1622024 | tf_op jit(solution)/shard_map/ppermute | solution.py:534
  23.7 10.3 %collective-permute-start.7 = (bf16[64,4096]{1,0:T(8,128)(2,1)S(1)}, bf16[64,4096]{1,0:T(8,128)(2,1)S(1)}, u32[]{:S(2)}, u32[]{:S(2)}) collective-permute-start(bf16[64,4096]{1,0:T(8,128)(2,1)S(1)} %collective-permute-done.6.rest_3_), channel_id=1, source_target_pairs={{0,1},{1,0},{2,3},{3,2},{4,5},{5,4},{6,7},{7,6},{8,9},{9,8},{10,11... | collective-permute-start | bytes 1572872 | tf_op jit(solution)/shard_map/ppermute | solution.py:538
  23.7 11.8 %collective-permute-start.11 = (bf16[64,4096]{1,0:T(8,128)(2,1)S(1)}, bf16[64,4096]{1,0:T(8,128)(2,1)S(1)}, u32[]{:S(2)}, u32[]{:S(2)}) collective-permute-start(bf16[64,4096]{1,0:T(8,128)(2,1)S(1)} %collective-permute-done.6.rest_3_), channel_id=1, source_target_pairs={{0,4},{4,8},{8,12},{12,14},{14,10},{10,6},{6,2},{2,0},{5,1},{9,5},... | collective-permute-start | bytes 1572872 | tf_op jit(solution)/shard_map/ppermute | solution.py:534
  29.5 7.9 %collective-permute-start.5 = (bf16[64,4224]{1,0:T(8,128)(2,1)S(1)}, bf16[64,4224]{1,0:T(8,128)(2,1)S(1)}, u32[]{:S(2)}, u32[]{:S(2)}) collective-permute-start(bf16[64,4224]{1,0:T(8,128)(2,1)S(1)} %collective-permute-done.1.rest_4_), channel_id=1, source_target_pairs={{0,1},{1,0},{2,3},{3,2},{4,5},{5,4},{6,7},{7,6},{8,9},{9,8},{10,11... | collective-permute-start | bytes 1622024 | tf_op jit(solution)/shard_map/ppermute | solution.py:538
  29.5 11.4 %collective-permute-start.4 = (bf16[64,4224]{1,0:T(8,128)(2,1)S(1)}, bf16[64,4224]{1,0:T(8,128)(2,1)S(1)}, u32[]{:S(2)}, u32[]{:S(2)}) collective-permute-start(bf16[64,4224]{1,0:T(8,128)(2,1)S(1)} %collective-permute-done.1.rest_4_), channel_id=1, source_target_pairs={{0,4},{4,8},{8,12},{12,14},{14,10},{10,6},{6,2},{2,0},{5,1},{9,5},... | collective-permute-start | bytes 1622024 | tf_op jit(solution)/shard_map/ppermute | solution.py:534
  35.4 7.9 %collective-permute-start.12 = (bf16[64,4096]{1,0:T(8,128)(2,1)S(1)}, bf16[64,4096]{1,0:T(8,128)(2,1)S(1)}, u32[]{:S(2)}, u32[]{:S(2)}) collective-permute-start(bf16[64,4096]{1,0:T(8,128)(2,1)S(1)} %collective-permute-done.11.rest_3_), channel_id=1, source_target_pairs={{0,1},{1,0},{2,3},{3,2},{4,5},{5,4},{6,7},{7,6},{8,9},{9,8},{10,11... | collective-permute-start | bytes 1572872 | tf_op jit(solution)/shard_map/ppermute | solution.py:538
  35.8 9.0 %collective-permute-start.14 = (bf16[64,2048]{1,0:T(8,128)(2,1)S(1)}, bf16[64,2048]{1,0:T(8,128)(2,1)S(1)}, u32[]{:S(2)}, u32[]{:S(2)}) collective-permute-start(bf16[64,2048]{1,0:T(8,128)(2,1)S(1)} %constant_dynamic-slice_fusion.1), channel_id=1, source_target_pairs={{0,4},{4,8},{8,12},{12,14},{14,10},{10,6},{6,2},{2,0},{5,1},{9,5},... | collective-permute-start | bytes 786440 | tf_op jit(solution)/shard_map/ppermute | solution.py:534
  40.9 4.2 %collective-permute-start.10 = (bf16[64,4224]{1,0:T(8,128)(2,1)S(1)}, bf16[64,4224]{1,0:T(8,128)(2,1)S(1)}, u32[]{:S(2)}, u32[]{:S(2)}) collective-permute-start(bf16[64,4224]{1,0:T(8,128)(2,1)S(1)} %collective-permute-done.4.rest_4_), channel_id=1, source_target_pairs={{0,1},{1,0},{2,3},{3,2},{4,5},{5,4},{6,7},{7,6},{8,9},{9,8},{10,11... | collective-permute-start | bytes 1622024 | tf_op jit(solution)/shard_map/ppermute | solution.py:538
  41.0 6.8 %collective-permute-start.9 = (bf16[64,2176]{1,0:T(8,128)(2,1)S(1)}, bf16[64,2176]{1,0:T(8,128)(2,1)S(1)}, u32[]{:S(2)}, u32[]{:S(2)}) collective-permute-start(bf16[64,2176]{1,0:T(8,128)(2,1)S(1)} %constant_dynamic-slice_fusion.2), channel_id=1, source_target_pairs={{0,4},{4,8},{8,12},{12,14},{14,10},{10,6},{6,2},{2,0},{5,1},{9,5},... | collective-permute-start | bytes 835592 | tf_op jit(solution)/shard_map/ppermute | solution.py:534
  44.8 3.1 %collective-permute-start.15 = (bf16[64,2048]{1,0:T(8,128)(2,1)S(1)}, bf16[64,2048]{1,0:T(8,128)(2,1)S(1)}, u32[]{:S(2)}, u32[]{:S(2)}) collective-permute-start(bf16[64,2048]{1,0:T(8,128)(2,1)S(1)} %collective-permute-done.14.rest_4_), channel_id=1, source_target_pairs={{0,1},{1,0},{2,3},{3,2},{4,5},{5,4},{6,7},{7,6},{8,9},{9,8},{10,11... | collective-permute-start | bytes 786440 | tf_op jit(solution)/shard_map/ppermute | solution.py:538
  47.8 2.2 %collective-permute-start.13 = (bf16[64,2176]{1,0:T(8,128)(2,1)S(1)}, bf16[64,2176]{1,0:T(8,128)(2,1)S(1)}, u32[]{:S(2)}, u32[]{:S(2)}) collective-permute-start(bf16[64,2176]{1,0:T(8,128)(2,1)S(1)} %collective-permute-done.9.rest_4_), channel_id=1, source_target_pairs={{0,1},{1,0},{2,3},{3,2},{4,5},{5,4},{6,7},{7,6},{8,9},{9,8},{10,11... | collective-permute-start | bytes 835592 | tf_op jit(solution)/shard_map/ppermute | solution.py:538
  53.7 1.4 %collective-permute-start.16 = (f32[4,4,1152]{2,1,0:T(4,128)S(1)}, f32[4,4,1152]{2,1,0:T(4,128)S(1)}, u32[]{:S(2)}, u32[]{:S(2)}) collective-permute-start(f32[4,4,1152]{2,1,0:T(4,128)S(1)} %get-tuple-element.86), channel_id=1, source_target_pairs={{0,1},{1,0},{2,3},{3,2},{4,5},{5,4},{6,7},{7,6},{8,9},{9,8},{10,11... | collective-permute-start | bytes 221192 | tf_op jit(solution)/shard_map/ppermute | solution.py:552
  55.0 4.9 %collective-permute-start.17 = (f32[4,4,1152]{2,1,0:T(4,128)S(1)}, f32[4,4,1152]{2,1,0:T(4,128)S(1)}, u32[]{:S(2)}, u32[]{:S(2)}) collective-permute-start(f32[4,4,1152]{2,1,0:T(4,128)S(1)} %add.17), channel_id=1, source_target_pairs={{0,2},{2,0},{4,6},{6,4},{8,10},{10,8},{12,14},{14,12},{1,3},{3,1},... | collective-permute-start | bytes 221192 | tf_op jit(solution)/shard_map/ppermute | solution.py:553
  58.9 1.3 %collective-permute-start.18 = (f32[4,4,1152]{2,1,0:T(4,128)S(1)}, f32[4,4,1152]{2,1,0:T(4,128)S(1)}, u32[]{:S(2)}, u32[]{:S(2)}) collective-permute-start(f32[4,4,1152]{2,1,0:T(4,128)S(1)} %get-tuple-element.91), channel_id=1, source_target_pairs={{0,1},{1,0},{2,3},{3,2},{4,5},{5,4},{6,7},{7,6},{8,9},{9,8},{10,11... | collective-permute-start | bytes 221192 | tf_op jit(solution)/shard_map/ppermute | solution.py:557
  60.2 4.0 %collective-permute-start.19 = (f32[2,4,1152]{2,1,0:T(4,128)S(1)}, f32[2,4,1152]{2,1,0:T(4,128)S(1)}, u32[]{:S(2)}, u32[]{:S(2)}) collective-permute-start(f32[2,4,1152]{2,1,0:T(4,128)S(1)} %dynamic-slice_bitcast_fusion), channel_id=1, source_target_pairs={{0,4},{2,6},{4,0},{6,2},{8,12},{10,14},{12,8},{14,10},{1,5},{3,7},... | collective-permute-start | bytes 110600 | tf_op jit(solution)/shard_map/ppermute | solution.py:471
  64.3 4.7 %collective-permute-start.20 = (f32[1,4,1152]{2,1,0:T(4,128)S(1)}, f32[1,4,1152]{2,1,0:T(4,128)S(1)}, u32[]{:S(2)}, u32[]{:S(2)}) collective-permute-start(f32[1,4,1152]{2,1,0:T(4,128)S(1)} %constant_dynamic-slice_fusion), channel_id=1, source_target_pairs={{0,8},{2,10},{4,12},{6,14},{8,0},{10,2},{12,4},{14,6},{1,9},{3,11}... | collective-permute-start | bytes 55304 | tf_op jit(solution)/shard_map/ppermute | solution.py:471
